TPU v7x, 32 devices: a whole 2x2x4 slice. The times are simulated.
32 devices in a mesh: pts: 8 (over y, x, core), cen: 4 (over z).
Axes of the slice: x: 2, y: 2, z: 4, core: 2. Of those that a mesh axis runs over, the one named last changes fastest.
Arguments:
- points: bfloat16 [32768, 1024], P('pts'), may hold values from -60 to 60
- fine_assign: int32 [2, 32768], P(None, 'pts'), may hold values from 0 to 2047
- fine_start: float32 [2048, 1024], P('cen'), may hold values from -3 to 3
- coarse_start: float32 [64, 1024], replicated, may hold values from -3 to 3
- coarse_assign: int32 [2048], P('cen'), may hold values from 0 to 63
Outputs:
- fine_centroids: float32 [2048, 1024], P('cen')
- coarse_centroids: float32 [64, 1024], replicated
- gaps: float32 [2, 32768], P(None, 'pts')
All inputs are finite; a program needn't handle non-finite values.
Results may differ from a plain program's by a relative error of at most 0.0028.
Values sent between devices are 32-bit elements; how exact they have to be, the bound alone decides.
No kernel may reach another device: no remote copies, remote signals or barrier semaphores. Data moves between devices by JAX's collectives and lax.ppermute only.
A program may use at most 64 MiB of HBM per device.

v0:
```python
import math

import jax
import jax.numpy as jnp
from jax import lax
from jax.sharding import PartitionSpec as P

NC = 64
PASSES = 2


prior_weight = 4.0


def refine(totals, counts, coarse_cols, coarse_table):
    lookup = jnp.dot(coarse_table, coarse_cols, precision=lax.Precision.HIGHEST)
    fine_next = (totals + prior_weight * lookup) / (counts + prior_weight)[:, None]
    coarse_part = lax.dot_general(
        coarse_table,
        counts[:, None] * fine_next,
        (((0,), (0,)), ((), ())),
        precision=lax.Precision.HIGHEST,
    )
    coarse_weight = jnp.sum(coarse_table * counts[:, None], axis=0)
    return (fine_next, coarse_part, coarse_weight)


def on_device(points, fine_assign, fine_start, coarse_start, coarse_assign):
    width = points.shape[1]
    local_count = fine_start.shape[0]
    offset = lax.axis_index("cen") * local_count
    columns = jnp.arange(local_count, dtype=jnp.int32)
    coarse_table = (coarse_assign[:, None] == jnp.arange(NC, dtype=jnp.int32)[None, :]).astype(
        jnp.float32
    )
    point_values = points.astype(jnp.float32)
    squares = jnp.sum(point_values * point_values, axis=1)
    fine_now = fine_start
    coarse_now = coarse_start
    gap_rows = []
    for pass_index in range(PASSES):
        member = (fine_assign[pass_index] - offset)[:, None] == columns[None, :]
        products = jnp.dot(
            points, fine_now.astype(jnp.bfloat16).T, preferred_element_type=jnp.float32
        )
        energy = jnp.sum(fine_now * fine_now, axis=1)[None, :] - 2.0 * products
        picked_local = jnp.sum(jnp.where(member, energy, 0.0), axis=1)
        nearest_local = jnp.min(energy, axis=1)
        picked = lax.psum(picked_local, "cen")
        nearest = lax.pmin(nearest_local, "cen")
        gap_rows.append((picked - nearest) / math.sqrt(width))
        weights = 1.0 / (1.0 + (squares + picked) / width)
        scaled = (point_values * weights[:, None]).astype(jnp.bfloat16)
        partial_sums = lax.dot_general(
            member.astype(jnp.bfloat16),
            scaled,
            (((0,), (0,)), ((), ())),
            preferred_element_type=jnp.float32,
        )
        partial_weights = jnp.sum(jnp.where(member, weights[:, None], 0.0), axis=0)
        share_width = width // lax.axis_size("pts")
        start = lax.axis_index("pts") * share_width
        shares = lax.psum_scatter(partial_sums, "pts", scatter_dimension=1, tiled=True)
        counts = lax.psum(partial_weights, "pts")
        coarse_cols = lax.dynamic_slice_in_dim(coarse_now, start, share_width, 1)
        fine_share, coarse_part, coarse_weight = refine(shares, counts, coarse_cols, coarse_table)
        coarse_sum, coarse_count = lax.psum((coarse_part, coarse_weight), "cen")
        coarse_share = (coarse_sum + prior_weight * coarse_cols) / (coarse_count + prior_weight)[
            :, None
        ]
        fine_now, coarse_now = (
            lax.all_gather(fine_share, "pts", axis=1, tiled=True),
            lax.all_gather(coarse_share, "pts", axis=1, tiled=True),
        )
    return (fine_now, coarse_now, jnp.stack(gap_rows))


def solution(mesh):
    placed = (P("pts", None), P(None, "pts"), P("cen", None), P(), P("cen"))
    return jax.shard_map(
        on_device,
        mesh=mesh,
        in_specs=placed,
        out_specs=(P("cen", None), P(), P(None, "pts")),
        check_vma=False,
    )
```

profile of v0, /device:TPU:0, one launch (start us, length us, event | category | flops | bytes accessed | tf_op | source)
XLA Modules:
  0.0 271.8 jit_solution(13717750007617004272)
XLA Ops:
  7.2 0.0 copy-start
  7.2 0.0 copy-start.2
  7.2 0.0 reduce-scatter.3.cloned.1.call-start
  7.2 1.9 multiply_reduce_fusion.1
  9.2 5.1 %fusion = f32[4096]{0:T(1024)S(1)} fusion(bf16[4096,1024]{1,0:T(8,128)(2,1)} %param.5), kind=kLoop, calls=%fused_computation.3 | loop fusion | flops 12578816 | bytes 8404992 | tf_op jit(solution)/shard_map/reduce_sum | solution.py:37
  14.3 0.0 copy-done.2
  14.3 0.0 copy-done
  14.3 9.7 %fusion.10 = (f32[4096]{0:T(1024)S(1)}, f32[4096]{0:T(1024)S(1)}) fusion(f32[512]{0:T(512)S(1)} %multiply_reduce_fusion.1, s32[4096]{0:T(1024)S(1)} %bitcast.15, bf16[4096,1024]{1,0:T(8,128)(2,1)} %param.5, f32[512,1024]{1,0:T(8,128)S(1)} %copy-done), kind=kOutput, calls=%fused_computation.19 | convolution fusion | flops 4308066304 | bytes 10536960 | tf_op jit(solution)/shard_map/dot_general | solution.py:43
  24.0 20.4 %psum.56 = f32[4096]{0:T(1024)S(1)} all-reduce(f32[4096]{0:T(1024)S(1)} %get-tuple-element.4), channel_id=1, replica_groups=mesh['pts'=8,'cen'=4] {'cen'}, use_global_device_ids=true, to_apply=%region_3.4 | all-reduce | flops 4096 | bytes 32768 | tf_op jit(solution)/shard_map/psum | solution.py:49
  44.5 0.0 copy-start.3
  44.5 9.4 %fusion.5 = f32[512,1024]{1,0:T(8,128)} fusion(bf16[4096,1024]{1,0:T(8,128)(2,1)} %param.5, f32[4096]{0:T(1024)S(1)} %add_divide_fusion.3, s32[4096]{0:T(1024)S(1)} %bitcast.16), kind=kOutput, calls=%fused_computation.7 | convolution fusion | flops 4309647360 | bytes 10518528 | tf_op jit(solution)/shard_map/dot_general | solution.py:54
  53.8 0.0 reduce-scatter.3.cloned.1.call-update
  53.9 0.0 all-gather.3.cloned.1.call-start
  53.9 1.1 select_reduce_fusion.1
  55.1 11.8 %psum.57 = f32[512]{0:T(512)S(1)} all-reduce(f32[512]{0:T(512)S(1)} %select_reduce_fusion.1), channel_id=1, replica_groups=mesh['pts'=8,'cen'=4] {'pts'}, use_global_device_ids=true, to_apply=%region_6.7 | all-reduce | flops 512 | bytes 4096 | tf_op jit(solution)/shard_map/psum | solution.py:64
  66.9 26.6 %reduce-scatter.3.cloned.1.call-done = f32[512,128]{1,0:T(8,128)} async-done(((f32[512,1024]{1,0:T(8,128)}), f32[512,128]{1,0:T(8,128)}) %reduce-scatter.3.cloned.1.call-update) | async-done | bytes 262160 | tf_op jit(solution)/shard_map/reduce_scatter | solution.py:63
  93.5 0.0 copy-done.3
  93.5 2.1 fusion.17
  95.6 0.0 all-gather.3.cloned.1.call-update
  95.6 0.2 reduce-scatter.5.cloned.1.call-start
  95.8 28.5 %all-gather.3.cloned.1.call-done = f32[512,1024]{1,0:T(8,128)} async-done(((f32[512,128]{1,0:T(8,128)}), f32[512,1024]{1,0:T(8,128)}) %all-gather.3.cloned.1.call-update) | async-done | bytes 2097168 | tf_op jit(solution)/shard_map/all_gather | solution.py:72
  124.3 1.8 multiply_reduce_fusion
  126.1 12.4 %fusion.7 = (f32[4096]{0:T(1024)S(1)}, f32[512,4096]{1,0:T(8,128)}) fusion(f32[512]{0:T(512)S(1)} %multiply_reduce_fusion, s32[4096]{0:T(1024)S(1)} %bitcast.12, bf16[4096,1024]{1,0:T(8,128)(2,1)} %param.5, f32[512,1024]{1,0:T(8,128)} %all-gather.3.cloned.1.call-done), kind=kOutput, calls=%fused_computation.9 | convolution fusion | flops 4305973248 | bytes 18909184 | tf_op jit(solution)/shard_map/dot_general | solution.py:43
  138.5 18.7 %psum.58 = f32[4096]{0:T(1024)S(1)} all-reduce(f32[4096]{0:T(1024)S(1)} %get-tuple-element.17), channel_id=1, replica_groups=mesh['pts'=8,'cen'=4] {'cen'}, use_global_device_ids=true, to_apply=%region_9.10 | all-reduce | flops 4096 | bytes 32768 | tf_op jit(solution)/shard_map/psum | solution.py:49
  157.2 4.6 %fusion.11 = f32[4096]{0:T(1024)S(1)} fusion(f32[512,4096]{1,0:T(8,128)} %get-tuple-element.18, f32[512]{0:T(512)S(1)} %multiply_reduce_fusion), kind=kLoop, calls=%fused_computation.20 | loop fusion | flops 6287360 | bytes 8407040 | tf_op jit(solution)/shard_map/reduce_min | solution.py:48
  161.8 15.9 %all-reduce.2 = (f32[4096]{0:T(1024)S(1)}, f32[4096]{0:T(1024)S(1)}) all-reduce(f32[4096]{0:T(1024)S(1)} %fusion.11, f32[4096]{0:T(1024)S(1)} %get-tuple-element.3), channel_id=1, replica_groups=mesh['pts'=8,'cen'=4] {'cen'}, use_global_device_ids=true, to_apply=%region_22.23 | all-reduce | flops 8192 | bytes 65536 | tf_op jit(solution)/shard_map/pmin | solution.py:50
  177.7 0.0 copy-start.1
  177.7 9.4 %fusion.3 = f32[512,1024]{1,0:T(8,128)} fusion(bf16[4096,1024]{1,0:T(8,128)(2,1)} %param.5, f32[4096]{0:T(1024)S(1)} %get-tuple-element.16, s32[4096]{0:T(1024)S(1)} %bitcast.13), kind=kOutput, calls=%fused_computation.6 | convolution fusion | flops 4309647360 | bytes 10518528 | tf_op jit(solution)/shard_map/dot_general | solution.py:54
  187.1 0.0 reduce-scatter.5.cloned.1.call-update
  187.2 0.0 all-gather.5.cloned.1.call-start
  187.2 0.0 copy-done.1
  187.2 0.3 fusion.24
  187.5 1.1 select_reduce_fusion
  188.7 11.8 %psum.61 = f32[512]{0:T(512)S(1)} all-reduce(f32[512]{0:T(512)S(1)} %select_reduce_fusion), channel_id=1, replica_groups=mesh['pts'=8,'cen'=4] {'pts'}, use_global_device_ids=true, to_apply=%region_15.16 | all-reduce | flops 512 | bytes 4096 | tf_op jit(solution)/shard_map/psum | solution.py:64
  200.5 0.1 select_reduce_fusion.3
  200.6 17.8 %all-reduce.1 = (f32[64,128]{1,0:T(8,128)S(1)}, f32[64]{0:T(128)S(1)}) all-reduce(f32[64,128]{1,0:T(8,128)S(1)} %fusion.24, f32[64]{0:T(128)S(1)} %get-tuple-element.6), channel_id=1, replica_groups=mesh['pts'=8,'cen'=4] {'cen'}, use_global_device_ids=true, to_apply=%region_11.12 | all-reduce | flops 8256 | bytes 66048 | tf_op jit(solution)/shard_map/psum | solution.py:67
  218.4 0.8 add_divide_fusion.1
  219.3 9.8 %all_gather.13 = f32[64,1024]{1,0:T(8,128)S(1)} all-gather(f32[64,128]{1,0:T(8,128)S(1)} %add_divide_fusion.1), channel_id=1, replica_groups=mesh['pts'=8,'cen'=4] {'pts'}, dimensions={1}, use_global_device_ids=true | all-gather | bytes 294912 | tf_op jit(solution)/shard_map/all_gather | solution.py:73
  229.1 0.0 reduce-scatter.5.cloned.1.call-done
  229.1 2.1 fusion.15
  231.1 0.0 all-gather.5.cloned.1.call-update
  231.2 0.6 pad_maximum_fusion
  231.8 1.3 fusion.22
  233.1 17.9 %all-reduce = (f32[64,128]{1,0:T(8,128)S(1)}, f32[64]{0:T(128)S(1)}) all-reduce(f32[64,128]{1,0:T(8,128)S(1)} %fusion.22, f32[64]{0:T(128)S(1)} %get-tuple-element.5), channel_id=1, replica_groups=mesh['pts'=8,'cen'=4] {'cen'}, use_global_device_ids=true, to_apply=%region_16.17 | all-reduce | flops 8256 | bytes 66048 | tf_op jit(solution)/shard_map/psum | solution.py:67
  251.0 0.1 add_divide_fusion
  251.1 10.3 %all_gather.15 = f32[64,1024]{1,0:T(8,128)S(1)} all-gather(f32[64,128]{1,0:T(8,128)S(1)} %add_divide_fusion), channel_id=1, replica_groups=mesh['pts'=8,'cen'=4] {'pts'}, dimensions={1}, use_global_device_ids=true | all-gather | bytes 294912 | tf_op jit(solution)/shard_map/all_gather | solution.py:73
  261.4 0.0 all-gather.5.cloned.1.call-done
  261.4 3.2 %copy.10 = f32[512,1024]{1,0:T(8,128)} copy(f32[512,1024]{1,0:T(8,128)} %all-gather.5.cloned.1.call-done) | data formatting | bytes 4194304
  264.5 0.7 copy.11
  (8 shorter events, 0.1 us)
Async XLA Ops:
  7.2 7.2 %copy-start = (f32[512,1024]{1,0:T(8,128)S(1)}, f32[512,1024]{1,0:T(8,128)}, u32[]{:S(2)}) copy-start(f32[512,1024]{1,0:T(8,128)} %param.7) | copy-start | bytes 6291460
  7.2 7.1 %copy-start.2 = (s32[2,4096]{1,0:T(2,128)S(1)}, s32[2,4096]{1,0:T(2,128)}, u32[]{:S(2)}) copy-start(s32[2,4096]{1,0:T(2,128)} %param.6) | copy-start | bytes 98308
  7.2 86.3 %reduce-scatter.3.cloned.1.call-start = ((), (), s32[]{:S(2)}) async-start(), calls=%async_computation.2 | async-start | bytes 2359296 | tf_op jit(solution)/shard_map/reduce_scatter | solution.py:63
  44.5 49.0 %copy-start.3 = (s32[512]{0:T(512)S(1)}, s32[512]{0:T(512)}, u32[]{:S(2)}) copy-start(s32[512]{0:T(512)} %param.9) | copy-start | bytes 6148
  53.9 70.5 %all-gather.3.cloned.1.call-start = ((), (), s32[]{:S(2)}) async-start(), calls=%async_computation.3 | async-start | bytes 2359296 | tf_op jit(solution)/shard_map/all_gather | solution.py:72
  95.6 133.4 %reduce-scatter.5.cloned.1.call-start = ((), (), s32[]{:S(2)}) async-start(), calls=%async_computation.4 | async-start | bytes 2359296 | tf_op jit(solution)/shard_map/reduce_scatter | solution.py:63
  177.7 9.5 %copy-start.1 = (f32[512,128]{1,0:T(8,128)S(1)}, f32[512,128]{1,0:T(8,128)}, u32[]{:S(2)}) copy-start(f32[512,128]{1,0:T(8,128)} %fusion.17) | copy-start | bytes 786436
  187.2 74.2 %all-gather.5.cloned.1.call-start = ((), (), s32[]{:S(2)}) async-start(), calls=%async_computation.5 | async-start | bytes 2359296 | tf_op jit(solution)/shard_map/all_gather | solution.py:72
Sparse Core Ops, SparseCore 0:
  54.0 39.4 reduce-scatter.2
  96.1 28.1 all-gather.2
  187.3 40.3 reduce-scatter.4
  231.3 27.5 all-gather.4
where the time goes:
time: 272 us
  blocking collectives  134 us (49%)
  waiting for transfers between devices  55.2 us (20%)
  matrix products  46.6 us (17%)
  other arithmetic  17.5 us (6%)
  between operations  13.9 us (5%)
  local copies, waits for them, and re-layouts  3.88 us (1%)
    psum x2, blocking collectives, on_device(): picked = lax.psum(picked_local, 'cen')  39.2 us
    psum x2, blocking collectives, on_device(): coarse_sum, coarse_count = lax.psum((coarse_part, coarse_weight), 'cen')  35.6 us
    all_gather x2, waiting for transfers between devices, on_device(): lax.all_gather(fine_share, 'pts', axis=1, tiled=True)  28.5 us
    reduce_scatter x2, waiting for transfers between devices, on_device(): lax.psum_scatter(partial_sums, 'pts', scatter_dimension=1, tiled=True)  26.6 us
    psum x2, blocking collectives, on_device(): counts = lax.psum(partial_weights, 'pts')  23.6 us
    dot_general x2, matrix products, on_device(): jnp.dot(points, fine_now.astype(jnp.bfloat16).T, preferred_element_type=j...  22.1 us
    all_gather x2, blocking collectives, on_device(): lax.all_gather(coarse_share, 'pts', axis=1, tiled=True)  20.1 us
    dot_general x2, matrix products, on_device(): lax.dot_general(member.astype(jnp.bfloat16), scaled, (((0,), (0,)), ((),...  18.8 us
  transfers between devices with their start and end apart: 4, of which 2 were waited for; matrix products, arithmetic and copies ran while one was open for 2% of the time, Pallas kernels for 0%

commit v1 on v0

--- a/solution.py
+++ b/solution.py
@@ -1,31 +1,35 @@
+import functools
 import math
 
 import jax
 import jax.numpy as jnp
 from jax import lax
+from jax.experimental import pallas as pl
+from jax.experimental.pallas import tpu as pltpu
 from jax.sharding import PartitionSpec as P
 
 NC = 64
 PASSES = 2
-
+FAR = 3.0e38
 
 prior_weight = 4.0
+HIGHEST = lax.Precision.HIGHEST
 
 
 def refine(totals, counts, coarse_cols, coarse_table):
-    lookup = jnp.dot(coarse_table, coarse_cols, precision=lax.Precision.HIGHEST)
+    lookup = jnp.dot(coarse_table, coarse_cols, precision=HIGHEST)
     fine_next = (totals + prior_weight * lookup) / (counts + prior_weight)[:, None]
     coarse_part = lax.dot_general(
         coarse_table,
         counts[:, None] * fine_next,
         (((0,), (0,)), ((), ())),
-        precision=lax.Precision.HIGHEST,
+        precision=HIGHEST,
     )
     coarse_weight = jnp.sum(coarse_table * counts[:, None], axis=0)
     return (fine_next, coarse_part, coarse_weight)
 
 
-def on_device(points, fine_assign, fine_start, coarse_start, coarse_assign):
+def on_device_any(points, fine_assign, fine_start, coarse_start, coarse_assign):
     width = points.shape[1]
     local_count = fine_start.shape[0]
     offset = lax.axis_index("cen") * local_count
@@ -75,8 +79,393 @@
     return (fine_now, coarse_now, jnp.stack(gap_rows))
 
 
+CORE, ACROSS_X, ACROSS_Y = 1, 2, 4
+SLOTS = 4
+TAIL = 8
+
+
+def swap(value, bit, axis="pts"):
+    size = lax.axis_size(axis)
+    return lax.ppermute(value, axis, [(i, i ^ bit) for i in range(size)])
+
+
+def pass_body(info, points, assign, *refs, pass_index, pieces, first, chained, sub):
+    refs = list(refs)
+    fine_refs = [refs.pop(0) for _ in pieces] if pieces else [refs.pop(0)]
+    squares_in = None if first else refs.pop(0)
+    seen_in = refs.pop(0) if chained else None
+    payload, seen = refs.pop(0), refs.pop(0)
+    squares_out = refs.pop(0) if first else None
+    low, norms, sums, tallies = refs
+    step = pl.program_id(0)
+    rows, width = low.shape
+    block_width = width // SLOTS
+    here, base = info[0], info[2]
+
+    @pl.when(step == 0)
+    def _():
+        if pieces:
+            total = jnp.zeros((rows, 1), jnp.float32)
+            parts = {}
+            for (slot, top, height), ref in zip(pieces, fine_refs):
+                block = ref[...]
+                column = pl.multiple_of((here ^ slot) * block_width, block_width)
+                low[top : top + height, pl.ds(column, block_width)] = (-2.0 * block).astype(
+                    jnp.bfloat16
+                )
+                parts.setdefault(slot, []).append(jnp.sum(block * block, axis=1, keepdims=True))
+            for column_parts in parts.values():
+                total = total + (
+                    column_parts[0] if len(column_parts) == 1 else jnp.concatenate(column_parts, 0)
+                )
+            norms[...] = jnp.broadcast_to(total, norms.shape)
+        else:
+            block = fine_refs[0][...]
+            low[...] = (-2.0 * block).astype(jnp.bfloat16)
+            norms[...] = jnp.broadcast_to(
+                jnp.sum(block * block, axis=1, keepdims=True), norms.shape
+            )
+        sums[...] = jnp.zeros_like(sums)
+        tallies[...] = jnp.zeros_like(tallies)
+
+    norm = norms[:, :1]
+    for at in range(0, points.shape[0], sub):
+        span = slice(at, at + sub)
+        tile = points[span, :]
+        energy = norm + lax.dot_general(
+            low[...], tile, (((1,), (1,)), ((), ())), preferred_element_type=jnp.float32
+        )
+        chosen = assign[pass_index : pass_index + 1, span] - base
+        member = lax.broadcasted_iota(jnp.int32, energy.shape, 0) == chosen
+        picked = jnp.sum(jnp.where(member, energy, 0.0), axis=0, keepdims=True)
+        nearest = jnp.min(energy, axis=0, keepdims=True)
+        inside = (chosen >= 0) & (chosen < rows)
+        picked_seen = jnp.where(inside, picked, FAR)
+        if chained:
+            picked_seen = jnp.minimum(picked_seen, seen_in[0:1, span])
+            nearest = jnp.minimum(nearest, seen_in[1:2, span])
+        seen[0:1, span] = picked_seen
+        seen[1:2, span] = nearest
+        if first:
+            folded = jnp.zeros((sub, 128), jnp.float32)
+            for lane in range(0, width, 128):
+                values = tile[:, lane : lane + 128].astype(jnp.float32)
+                folded = folded + values * values
+            squares = lax.dot_general(
+                jnp.ones((8, 128), jnp.float32),
+                folded,
+                (((1,), (1,)), ((), ())),
+                precision=HIGHEST,
+                preferred_element_type=jnp.float32,
+            )[:1]
+            squares_out[0:1, span] = squares
+        else:
+            squares = squares_in[0:1, span]
+        weights = 1.0 / (1.0 + (squares + picked) / width)
+        held = jnp.where(member, weights, 0.0)
+        tally = tallies[...]
+        for lane in range(0, sub, 128):
+            tally = tally + held[:, lane : lane + 128]
+        tallies[...] = tally
+        sums[...] += jnp.dot(
+            held.astype(jnp.bfloat16), tile, preferred_element_type=jnp.float32
+        )
+
+    @pl.when(step == pl.num_programs(0) - 1)
+    def _():
+        for slot in range(SLOTS):
+            column = pl.multiple_of((here ^ slot) * block_width, block_width)
+            payload[slot * rows : (slot + 1) * rows, :] = sums[:, pl.ds(column, block_width)]
+        counts = jnp.sum(tallies[...].T, axis=0, keepdims=True)
+        payload[SLOTS * rows :, :] = jnp.broadcast_to(counts, (TAIL, rows))
+
+
+def run_pass(info, points, fine_assign, fine, squares, seen, *, pass_index, pieces, rows):
+    count, width = points.shape
+    block_width = width // SLOTS
+    tile = min(count, 1024)
+    first = squares is None
+    chained = seen is not None
+    whole = lambda i, info: (0, 0)
+    along = lambda i, info: (0, i)
+    in_specs = [
+        pl.BlockSpec((tile, width), lambda i, info: (i, 0)),
+        pl.BlockSpec((PASSES, tile), along),
+    ]
+    args = [points, fine_assign]
+    if pieces:
+        for (slot, top, height), piece in zip(pieces, fine):
+            in_specs.append(pl.BlockSpec((height, block_width), whole))
+            args.append(piece)
+    else:
+        in_specs.append(pl.BlockSpec((rows, width), lambda i, info: (info[1], 0)))
+        args.append(fine)
+    if not first:
+        in_specs.append(pl.BlockSpec((1, tile), along))
+        args.append(squares)
+    if chained:
+        in_specs.append(pl.BlockSpec((2, tile), along))
+        args.append(seen)
+    out_shape = [
+        jax.ShapeDtypeStruct((SLOTS * rows + TAIL, block_width), jnp.float32),
+        jax.ShapeDtypeStruct((2, count), jnp.float32),
+    ]
+    out_specs = [
+        pl.BlockSpec((SLOTS * rows + TAIL, block_width), whole),
+        pl.BlockSpec((2, tile), along),
+    ]
+    if first:
+        out_shape.append(jax.ShapeDtypeStruct((1, count), jnp.float32))
+        out_specs.append(pl.BlockSpec((1, tile), along))
+    body = functools.partial(
+        pass_body,
+        pass_index=pass_index,
+        pieces=pieces,
+        first=first,
+        chained=chained,
+        sub=min(tile, 512),
+    )
+    return pl.pallas_call(
+        body,
+        out_shape=out_shape,
+        grid_spec=pltpu.PrefetchScalarGridSpec(
+            num_scalar_prefetch=1,
+            grid=(count // tile,),
+            in_specs=in_specs,
+            out_specs=out_specs,
+            scratch_shapes=[
+                pltpu.VMEM((rows, width), jnp.bfloat16),
+                pltpu.VMEM((rows, 128), jnp.float32),
+                pltpu.VMEM((rows, width), jnp.float32),
+                pltpu.VMEM((rows, 128), jnp.float32),
+            ],
+        ),
+        compiler_params=pltpu.CompilerParams(vmem_limit_bytes=40 * 2**20),
+        cost_estimate=pl.CostEstimate(
+            flops=4 * rows * count * width, bytes_accessed=2 * count * width, transcendentals=0
+        ),
+        name=f"energies_and_sums_{pass_index}{int(chained)}",
+    )(info, *args)
+
+
+def refine_body(own, sibling, over_x, over_y, tail, owner, coarse, fine, coarse_part):
+    rows = own.shape[0]
+    totals = own[...] + sibling[...] + over_x[...] + over_y[:rows, :]
+    counts_row = tail[...] + over_y[rows:, :]
+    counts = jnp.broadcast_to(counts_row[:1], (128, rows)).T[:, :1]
+    table = (
+        lax.broadcasted_iota(jnp.int32, (NC, rows), 0) == owner[...]
+    ).astype(jnp.float32)
+    lookup = lax.dot_general(
+        table,
+        coarse[...],
+        (((0,), (0,)), ((), ())),
+        precision=HIGHEST,
+        preferred_element_type=jnp.float32,
+    )
+    new = (totals + prior_weight * lookup) / (counts + prior_weight)
+    fine[...] = new
+    coarse_part[:NC, : new.shape[1]] = jnp.dot(
+        table, counts * new, precision=HIGHEST, preferred_element_type=jnp.float32
+    )
+    weight = jnp.sum(table * counts_row[:1], axis=1, keepdims=True)
+    coarse_part[:NC, new.shape[1] :] = jnp.broadcast_to(weight, (NC, 128))
+
+
+def refine_half(own, sibling, over_x, over_y, tail, owner, coarse):
+    rows, block_width = over_x.shape
+    full = lambda shape: pl.BlockSpec(shape, lambda i: (0, 0))
+    return pl.pallas_call(
+        refine_body,
+        grid=(1,),
+        out_shape=[
+            jax.ShapeDtypeStruct((rows, block_width), jnp.float32),
+            jax.ShapeDtypeStruct((NC, block_width + 128), jnp.float32),
+        ],
+        in_specs=[
+            full((rows, block_width)),
+            full((rows, block_width)),
+            full((rows, block_width)),
+            full((rows + TAIL, block_width)),
+            full((TAIL, block_width)),
+            full((1, rows)),
+            full((NC, block_width)),
+        ],
+        out_specs=[full((rows, block_width)), full((NC, block_width + 128))],
+        compiler_params=pltpu.CompilerParams(vmem_limit_bytes=16 * 2**20),
+        name="refine_half",
+    )(own, sibling, over_x, over_y, tail, owner, coarse)
+
+
+def scatter_sums(own, sibling, rows):
+    mid = rows // 2
+    slot = lambda s: slice(s * rows, (s + 1) * rows)
+    end = slice(SLOTS * rows, SLOTS * rows + TAIL)
+    tail = own[end] + sibling[end]
+    corner = own[slot(3)] + sibling[slot(3)]
+    first_x = swap(jnp.concatenate([corner[:mid], tail], 0), ACROSS_X)
+    first_y = swap(corner[mid:], ACROSS_Y)
+    two = own[slot(2)] + sibling[slot(2)]
+    one = own[slot(1)] + sibling[slot(1)]
+    tail = tail + first_x[mid:]
+    two = jnp.concatenate([two[:mid] + first_x[:mid], two[mid:], tail], 0)
+    one = jnp.concatenate([one[:mid], one[mid:] + first_y], 0)
+    over_y = swap(two, ACROSS_Y)
+    over_x = swap(one, ACROSS_X)
+    return over_x, over_y, tail
+
+
+def gather_half(fine, rows):
+    mid = rows // 2
+    over_x = swap(fine, ACROSS_X)
+    over_y = swap(fine, ACROSS_Y)
+    top = swap(over_y[:mid], ACROSS_X)
+    bottom = swap(over_x[mid:], ACROSS_Y)
+    return [fine, over_x, over_y, top, bottom]
+
+
+def add_everywhere(value):
+    value = value + swap(value, CORE)
+    bit = 1
+    while bit < lax.axis_size("cen"):
+        value = value + swap(value, bit, "cen")
+        bit *= 2
+    return value
+
+
+def place_body(info, *refs, pieces):
+    own = refs[:5]
+    other = refs[5:10]
+    coarse = refs[10:14]
+    fine_out, coarse_out, sems = refs[14:]
+    rows, block_width = own[0].shape
+    here, half = info[0], info[1]
+    copies = []
+    for at, refs_of in ((half, own), (1 - half, other)):
+        for (slot, top, height), ref in zip(pieces, refs_of):
+            row = pl.multiple_of(at * rows + top, 8)
+            column = pl.multiple_of((here ^ slot) * block_width, block_width)
+            copies.append((ref, fine_out.at[pl.ds(row, height), pl.ds(column, block_width)]))
+    for slot, ref in enumerate(coarse):
+        column = pl.multiple_of((here ^ slot) * block_width, block_width)
+        copies.append((ref, coarse_out.at[:, pl.ds(column, block_width)]))
+    started = [
+        pltpu.make_async_copy(source, target, sems.at[i])
+        for i, (source, target) in enumerate(copies)
+    ]
+    for copy in started:
+        copy.start()
+    for copy in started:
+        copy.wait()
+
+
+def place(info, own, other, coarse, pieces):
+    rows, block_width = own[0].shape
+    anywhere = pl.BlockSpec(memory_space=pl.ANY)
+    return pl.pallas_call(
+        functools.partial(place_body, pieces=pieces),
+        out_shape=[
+            jax.ShapeDtypeStruct((2 * rows, SLOTS * block_width), jnp.float32),
+            jax.ShapeDtypeStruct((NC, SLOTS * block_width), jnp.float32),
+        ],
+        grid_spec=pltpu.PrefetchScalarGridSpec(
+            num_scalar_prefetch=1,
+            grid=(1,),
+            in_specs=[anywhere] * 14,
+            out_specs=[anywhere] * 2,
+            scratch_shapes=[pltpu.SemaphoreType.DMA((14,))],
+        ),
+        name="place_blocks",
+    )(info, *own, *other, *coarse)
+
+
+def on_device_paired(points, fine_assign, fine_start, coarse_start, coarse_assign):
+    width = points.shape[1]
+    local_count = fine_start.shape[0]
+    rows = local_count // 2
+    block_width = width // SLOTS
+    offset = lax.axis_index("cen") * local_count
+    me = lax.axis_index("pts")
+    core, here = me & 1, me >> 1
+    pieces = (
+        (0, 0, rows),
+        (1, 0, rows),
+        (2, 0, rows),
+        (3, 0, rows // 2),
+        (3, rows // 2, rows // 2),
+    )
+    owners = coarse_assign.reshape(2, 1, rows)
+    info_of = lambda half: jnp.stack([here, half, offset + half * rows]).astype(jnp.int32)
+    coarse = lax.dynamic_slice_in_dim(coarse_start, here * block_width, block_width, 1)
+
+    seen_rows = []
+    squares = None
+    own = other = None
+    for pass_index in range(PASSES):
+        keep = core if pass_index % 2 == 0 else 1 - core
+        away = 1 - keep
+        call = functools.partial(run_pass, pass_index=pass_index, rows=rows)
+        if pass_index == 0:
+            sent, seen, squares = call(
+                info_of(away), points, fine_assign, fine_start, None, None, pieces=None
+            )
+        else:
+            sent, seen = call(
+                info_of(away), points, fine_assign, own, squares, None, pieces=pieces
+            )
+        sibling = swap(sent, CORE)
+        held, seen = call(
+            info_of(keep),
+            points,
+            fine_assign,
+            fine_start if pass_index == 0 else other,
+            squares,
+            seen,
+            pieces=None if pass_index == 0 else pieces,
+        )
+        seen_rows.append(seen)
+        over_x, over_y, tail = scatter_sums(held, sibling, rows)
+        owner = lax.dynamic_index_in_dim(owners, keep, 0, keepdims=False)
+        fine, coarse_part = refine_half(held, sibling, over_x, over_y, tail, owner, coarse)
+        own = gather_half(fine, rows)
+        other = [swap(piece, CORE) for piece in own]
+        coarse_sum = add_everywhere(coarse_part)
+        coarse = (coarse_sum[:, :block_width] + prior_weight * coarse) / (
+            coarse_sum[:, block_width : block_width + 1] + prior_weight
+        )
+
+    coarse_x = swap(coarse, ACROSS_X)
+    coarse_y = swap(coarse, ACROSS_Y)
+    corner = swap(coarse_y, ACROSS_X)
+    fine_now, coarse_now = place(
+        info_of(keep), own, other, [coarse, coarse_x, coarse_y, corner], pieces
+    )
+
+    seen = jnp.concatenate(seen_rows, 0)
+    others = [swap(seen, bit, "cen") for bit in range(1, lax.axis_size("cen"))]
+    for value in others:
+        seen = jnp.minimum(seen, value)
+    gaps = (seen[0::2] - seen[1::2]) / math.sqrt(width)
+    return (fine_now, coarse_now, gaps)
+
+
 def solution(mesh):
     placed = (P("pts", None), P(None, "pts"), P("cen", None), P(), P("cen"))
+
+    def on_device(points, fine_assign, fine_start, coarse_start, coarse_assign):
+        count, width = points.shape
+        local_count = fine_start.shape[0]
+        centres = mesh.shape["cen"]
+        fits = (
+            mesh.shape["pts"] == 2 * SLOTS
+            and centres & (centres - 1) == 0
+            and width // SLOTS == local_count // 2
+            and (width // SLOTS) % 128 == 0
+            and count % 1024 == 0
+        )
+        plan = on_device_paired if fits else on_device_any
+        return plan(points, fine_assign, fine_start, coarse_start, coarse_assign)
+
     return jax.shard_map(
         on_device,
         mesh=mesh,

time: 272 us -> 219 us (0.81)
  blocking collectives: 134 us -> 0 us
  Pallas kernels: 0 us -> 111 us
  matrix products: 46.6 us -> 0 us
  starting transfers between devices: 0.34 us -> 36.4 us
  other arithmetic: 17.5 us -> 1.88 us
  between operations: 13.9 us -> 1.28 us
  local copies, waits for them, and re-layouts: 3.88 us -> 15.8 us
    pallas_call x0 -> x7, Pallas kernels: none -> 111 us  [the longest x1 73.4 us: place(): pl.pallas_call(functools.partial(place_body, pieces=pieces), out_shape=[j...]
    psum x6 -> x0, blocking collectives: 98.4 us -> none  [the longest x2 39.2 us: on_device(): picked = lax.psum(picked_local, 'cen')]
    ppermute x0 -> x40, waiting for transfers between devices: none -> 52.7 us  [swap(): return lax.ppermute(value, axis, [(i, i ^ bit) for i in range(size)])]
    dot_general x8 -> x0, matrix products: 46.6 us -> none  [the longest x2 22.1 us: on_device(): jnp.dot(points, fine_now.astype(jnp.bfloat16).T, preferred_element_type=j...]
    ppermute x0 -> x40, starting transfers between devices: none -> 36.4 us  [swap(): return lax.ppermute(value, axis, [(i, i ^ bit) for i in range(size)])]
    all_gather x2 -> x0, waiting for transfers between devices: 28.5 us -> none  [on_device(): lax.all_gather(fine_share, 'pts', axis=1, tiled=True)]
    reduce_scatter x2 -> x0, waiting for transfers between devices: 26.6 us -> none  [on_device(): lax.psum_scatter(partial_sums, 'pts', scatter_dimension=1, tiled=True)]
    all_gather x2 -> x0, blocking collectives: 20.1 us -> none  [on_device(): lax.all_gather(coarse_share, 'pts', axis=1, tiled=True)]
  transfers between devices with their start and end apart: 4 -> 40, of which waited for: 2 -> 21; matrix products, arithmetic and copies ran while one was open for 2% -> 1% of each run, Pallas kernels for 0% -> 8%
where the time goes in v1:
time: 219 us
  Pallas kernels  111 us (51%)
  waiting for transfers between devices  52.7 us (24%)
  starting transfers between devices  36.4 us (17%)
  local copies, waits for them, and re-layouts  15.8 us (7%)
    pallas_call x1, Pallas kernels, place(): pl.pallas_call(functools.partial(place_body, pieces=pieces), out_shape=[j...  73.4 us
    ppermute x40, waiting for transfers between devices, swap(): return lax.ppermute(value, axis, [(i, i ^ bit) for i in range(size)])  52.7 us
    ppermute x40, starting transfers between devices, swap(): return lax.ppermute(value, axis, [(i, i ^ bit) for i in range(size)])  36.4 us
    pallas_call x4, Pallas kernels, run_pass(): pl.pallas_call(body, out_shape=out_shape, grid_spec=pltpu.PrefetchScalarG...  35.8 us
    unnamed x48, local copies, waits for them, and re-layouts  15.5 us
  transfers between devices with their start and end apart: 40, of which 21 were waited for; matrix products, arithmetic and copies ran while one was open for 1% of the time, Pallas kernels for 8%

profile of v1, /device:TPU:0, one launch (start us, length us, event | category | flops | bytes accessed | tf_op | source)
XLA Modules:
  0.0 218.9 jit_solution(12107591798427967618)
XLA Ops:
  0.7 3.4 %copy-done.2 = bf16[4096,1024]{1,0:T(8,128)(2,1)S(1)} copy-done((bf16[4096,1024]{1,0:T(8,128)(2,1)S(1)}, bf16[4096,1024]{1,0:T(8,128)(2,1)}, u32[]{:S(2)}) %copy-start.2) | copy-done | bytes 8388632
  4.1 1.6 copy-done.5
  5.7 0.8 copy-done.7
  6.5 10.6 %energies_and_sums_00.1 = (f32[1032,256]{1,0:T(8,128)}, f32[2,4096]{1,0:T(2,128)S(1)}, f32[1,4096]{1,0:T(1,128)S(1)}) custom-call(s32[3]{0:T(128)S(1)} %pad_add_fusion.info, bf16[4096,1024]{1,0:T(8,128)(2,1)S(1)} %copy-done.2, s32[2,4096]{1,0:T(2,128)S(1)} %copy-done.7, f32[512,1024]{1,0:T(8,128)S(1)} %copy-done.5), custom_call_target="tpu_custom_call" | custom-call | flops 4294967296 | bytes 8388608 | tf_op jit(solution)/shard_map/energies_and_sums_00/pallas_call | solution.py:228
  17.0 0.4 collective-permute-start
  17.5 3.4 %copy-done.3 = bf16[4096,1024]{1,0:T(8,128)(2,1)S(1)} copy-done((bf16[4096,1024]{1,0:T(8,128)(2,1)S(1)}, bf16[4096,1024]{1,0:T(8,128)(2,1)}, u32[]{:S(2)}) %copy-start.3) | copy-done | bytes 8388632
  20.9 1.6 copy-done.6
  22.5 8.3 %energies_and_sums_01.1 = (f32[1032,256]{1,0:T(8,128)S(1)}, f32[2,4096]{1,0:T(2,128)S(1)}) custom-call(s32[3]{0:T(128)S(1)} %pad_add_fusion.1.info, bf16[4096,1024]{1,0:T(8,128)(2,1)S(1)} %copy-done.3, s32[2,4096]{1,0:T(2,128)S(1)} %copy-done.8, f32[512,1024]{1,0:T(8,128)S(1)} %copy-done.6, f32[1,4096]{1,0:T(1,128)S(1)} %get-tuple-element.18.refs_1_.refs_5_, ...), custom_call_target="tpu_custom_call" | custom-call | flops 4294967296 | bytes 8388608 | tf_op jit(solution)/shard_map/energies_and_sums_01/pallas_call | solution.py:228
  31.0 2.6 %collective-permute-start.1 = (f32[128,256]{1,0:T(8,128)S(1)}, f32[128,256]{1,0:T(8,128)S(1)}, u32[]{:S(2)}, u32[]{:S(2)}) collective-permute-start(f32[128,256]{1,0:T(8,128)S(1)} %get-tuple-element.48), channel_id=1, source_target_pairs={{0,16},{4,20},{8,24},{12,28},{16,0},{20,4},{24,8},{28,12},{1,17},{... | collective-permute-start | bytes 393224 | tf_op jit(solution)/shard_map/ppermute | solution.py:89
  33.6 1.6 collective-permute-start.3
  35.1 2.6 %collective-permute-done.1 = f32[128,256]{1,0:T(8,128)S(1)} collective-permute-done((f32[128,256]{1,0:T(8,128)S(1)}, f32[128,256]{1,0:T(8,128)S(1)}, u32[]{:S(2)}, u32[]{:S(2)}) %collective-permute-start.1) | collective-permute-done | bytes 131104 | tf_op jit(solution)/shard_map/ppermute | solution.py:89
  37.8 1.7 collective-permute-done.3
  39.9 1.8 collective-permute-start.2
  41.7 5.9 %collective-permute-done.2.over_x = f32[256,256]{1,0:T(8,128)S(1)} collective-permute-done((f32[256,256]{1,0:T(8,128)S(1)}, f32[256,256]{1,0:T(8,128)S(1)}, u32[]{:S(2)}, u32[]{:S(2)}) %collective-permute-start.2) | collective-permute-done | bytes 262176 | tf_op jit(solution)/shard_map/ppermute | solution.py:89
  47.6 0.8 refine_half.2
  48.5 1.5 collective-permute-start.8
  49.9 1.5 collective-permute-start.6
  51.4 3.9 %collective-permute-done.8.refs_2_ = f32[256,256]{1,0:T(8,128)S(1)} collective-permute-done((f32[256,256]{1,0:T(8,128)S(1)}, f32[256,256]{1,0:T(8,128)S(1)}, u32[]{:S(2)}, u32[]{:S(2)}) %collective-permute-start.8) | collective-permute-done | bytes 262176 | tf_op jit(solution)/shard_map/ppermute | solution.py:89
  55.3 1.3 collective-permute-start.10
  56.5 0.4 collective-permute-done.6.refs_1_
  57.0 1.0 collective-permute-start.12
  58.0 2.3 %collective-permute-done.10.refs_3_ = f32[128,256]{1,0:T(8,128)S(1)} collective-permute-done((f32[128,256]{1,0:T(8,128)S(1)}, f32[128,256]{1,0:T(8,128)S(1)}, u32[]{:S(2)}, u32[]{:S(2)}) %collective-permute-start.10) | collective-permute-done | bytes 131104 | tf_op jit(solution)/shard_map/ppermute | solution.py:89
  60.3 1.7 collective-permute-done.12.refs_4_
  62.0 3.4 %copy-done.4 = bf16[4096,1024]{1,0:T(8,128)(2,1)S(1)} copy-done((bf16[4096,1024]{1,0:T(8,128)(2,1)S(1)}, bf16[4096,1024]{1,0:T(8,128)(2,1)}, u32[]{:S(2)}) %copy-start.4) | copy-done | bytes 8388632
  65.4 8.4 %energies_and_sums_10.1 = (f32[1032,256]{1,0:T(8,128)S(1)}, f32[2,4096]{1,0:T(2,128)S(1)}) custom-call(s32[3]{0:T(128)S(1)} %pad_add_fusion.1.info, bf16[4096,1024]{1,0:T(8,128)(2,1)S(1)} %copy-done.4, s32[2,4096]{1,0:T(2,128)S(1)} %copy-done.8, f32[256,256]{1,0:T(8,128)S(1)} %get-tuple-element.22.refs_0_, f32[256,256]{1,0:T(8,128)S(1)} %collective-permute-done.6.refs_1_, ...), custom_call_target="tpu_custom_call" | custom-call | flops 4294967296 | bytes 8388608 | tf_op jit(solution)/shard_map/energies_and_sums_10/pallas_call | solution.py:228
  73.9 0.5 collective-permute-start.19
  74.5 2.2 %collective-permute-done.19 = f32[64,384]{1,0:T(8,128)S(1)} collective-permute-done((f32[64,384]{1,0:T(8,128)S(1)}, f32[64,384]{1,0:T(8,128)S(1)}, u32[]{:S(2)}, u32[]{:S(2)}) %collective-permute-start.19) | collective-permute-done | bytes 98336 | tf_op jit(solution)/shard_map/ppermute | solution.py:89
  76.7 2.1 collective-permute-start.20
  78.8 0.5 collective-permute-start.7
  79.3 2.6 %collective-permute-done.20 = f32[64,384]{1,0:T(8,128)S(1)} collective-permute-done((f32[64,384]{1,0:T(8,128)S(1)}, f32[64,384]{1,0:T(8,128)S(1)}, u32[]{:S(2)}, u32[]{:S(2)}) %collective-permute-start.20) | collective-permute-done | bytes 98336 | tf_op jit(solution)/shard_map/ppermute | solution.py:89
  81.9 2.8 %collective-permute-start.21 = (f32[64,384]{1,0:T(8,128)S(1)}, f32[64,384]{1,0:T(8,128)S(1)}, u32[]{:S(2)}, u32[]{:S(2)}) collective-permute-start(f32[64,384]{1,0:T(8,128)S(1)} %add.112), channel_id=1, source_target_pairs={{0,2},{1,3},{2,0},{3,1},{4,6},{5,7},{6,4},{7,5},{8,10},{9,11},{10,... | collective-permute-start | bytes 294920 | tf_op jit(solution)/shard_map/ppermute | solution.py:89
  84.8 4.6 %collective-permute-done.21 = f32[64,384]{1,0:T(8,128)S(1)} collective-permute-done((f32[64,384]{1,0:T(8,128)S(1)}, f32[64,384]{1,0:T(8,128)S(1)}, u32[]{:S(2)}, u32[]{:S(2)}) %collective-permute-start.21) | collective-permute-done | bytes 98336 | tf_op jit(solution)/shard_map/ppermute | solution.py:89
  89.4 1.3 collective-permute-done.13.refs_4_
  90.7 8.6 %energies_and_sums_11.1 = (f32[1032,256]{1,0:T(8,128)S(1)}, f32[2,4096]{1,0:T(2,128)S(1)}) custom-call(s32[3]{0:T(128)S(1)} %pad_add_fusion.info, bf16[4096,1024]{1,0:T(8,128)(2,1)S(1)} %copy-done.4, s32[2,4096]{1,0:T(2,128)S(1)} %copy-done.8, f32[256,256]{1,0:T(8,128)S(1)} %collective-permute-done.5.refs_0_, f32[256,256]{1,0:T(8,128)S(1)} %collective-permute-done.7.refs_1_, ...), custom_call_target="tpu_custom_call" | custom-call | flops 4294967296 | bytes 8388608 | tf_op jit(solution)/shard_map/energies_and_sums_11/pallas_call | solution.py:228
  99.5 0.4 collective-permute-start.15
  99.9 1.2 collective-permute-start.17
  101.0 4.0 %collective-permute-done.15 = f32[128,256]{1,0:T(8,128)S(1)} collective-permute-done((f32[128,256]{1,0:T(8,128)S(1)}, f32[128,256]{1,0:T(8,128)S(1)}, u32[]{:S(2)}, u32[]{:S(2)}) %collective-permute-start.15) | collective-permute-done | bytes 131104 | tf_op jit(solution)/shard_map/ppermute | solution.py:89
  105.1 1.4 collective-permute-start.16
  106.6 0.6 collective-permute-start.18
  107.4 5.3 %collective-permute-done.16.over_x = f32[256,256]{1,0:T(8,128)S(1)} collective-permute-done((f32[256,256]{1,0:T(8,128)S(1)}, f32[256,256]{1,0:T(8,128)S(1)}, u32[]{:S(2)}, u32[]{:S(2)}) %collective-permute-start.16) | collective-permute-done | bytes 262176 | tf_op jit(solution)/shard_map/ppermute | solution.py:89
  112.7 1.4 collective-permute-done.18.over_y
  114.1 0.8 refine_half.3
  115.1 1.3 collective-permute-done.31
  116.4 0.7 collective-permute-start.32
  117.1 0.6 collective-permute-start.23
  117.7 1.3 collective-permute-start.22
  118.9 2.4 %collective-permute-done.32 = f32[64,384]{1,0:T(8,128)S(1)} collective-permute-done((f32[64,384]{1,0:T(8,128)S(1)}, f32[64,384]{1,0:T(8,128)S(1)}, u32[]{:S(2)}, u32[]{:S(2)}) %collective-permute-start.32) | collective-permute-done | bytes 98336 | tf_op jit(solution)/shard_map/ppermute | solution.py:89
  121.3 2.4 %collective-permute-start.33 = (f32[64,384]{1,0:T(8,128)S(1)}, f32[64,384]{1,0:T(8,128)S(1)}, u32[]{:S(2)}, u32[]{:S(2)}) collective-permute-start(f32[64,384]{1,0:T(8,128)S(1)} %add.117), channel_id=1, source_target_pairs={{0,2},{1,3},{2,0},{3,1},{4,6},{5,7},{6,4},{7,5},{8,10},{9,11},{10,... | collective-permute-start | bytes 294920 | tf_op jit(solution)/shard_map/ppermute | solution.py:89
  123.7 0.7 collective-permute-start.38
  124.4 3.5 %collective-permute-start.39 = (f32[4,4096]{1,0:T(4,128)S(1)}, f32[4,4096]{1,0:T(4,128)S(1)}, u32[]{:S(2)}, u32[]{:S(2)}) collective-permute-start(f32[4,4096]{1,0:T(4,128)S(1)} %pad_maximum_fusion.6), channel_id=1, source_target_pairs={{0,3},{1,2},{2,1},{3,0},{4,7},{5,6},{6,5},{7,4},{8,11},{9,10},{10,... | collective-permute-start | bytes 196616 | tf_op jit(solution)/shard_map/ppermute | solution.py:89
  128.0 4.2 %collective-permute-done.33 = f32[64,384]{1,0:T(8,128)S(1)} collective-permute-done((f32[64,384]{1,0:T(8,128)S(1)}, f32[64,384]{1,0:T(8,128)S(1)}, u32[]{:S(2)}, u32[]{:S(2)}) %collective-permute-start.33) | collective-permute-done | bytes 98336 | tf_op jit(solution)/shard_map/ppermute | solution.py:89
  132.2 0.6 collective-permute-start.24
  133.3 1.0 collective-permute-start.25
  134.3 1.0 collective-permute-start.35
  135.4 1.2 collective-permute-start.34
  137.0 2.0 collective-permute-done.35.refs_12_
  139.0 0.6 collective-permute-done.34.refs_11_
  139.6 1.2 collective-permute-start.36
  140.8 0.5 collective-permute-start.30
  141.3 0.6 subtract_multiply_fusion
  142.0 1.9 collective-permute-done.36.refs_13_
  144.0 0.5 copy-done.21
  144.7 0.7 copy-done.13
  145.4 73.4 %place_blocks.1 = (f32[512,1024]{1,0:T(8,128)}, f32[64,1024]{1,0:T(8,128)}) custom-call(s32[3]{0:T(128)} %copy-done.1, f32[256,256]{1,0:T(8,128)} %copy-done, f32[256,256]{1,0:T(8,128)} %copy-done.10, f32[256,256]{1,0:T(8,128)} %copy-done.9, f32[128,256]{1,0:T(8,128)} %copy-done.15, f32[128,256]{1,0:T(8,128)} %copy-done.16, f32[256,256]{1,0:T(8,128)} %copy-done.11, ...), custom_call_target="tpu_custom_call" | custom-call | tf_op jit(solution)/shard_map/place_blocks/pallas_call | solution.py:365
  (112 shorter events, 3.0 us)
Async XLA Ops:
  0.7 3.4 %copy-start.2 = (bf16[4096,1024]{1,0:T(8,128)(2,1)S(1)}, bf16[4096,1024]{1,0:T(8,128)(2,1)}, u32[]{:S(2)}) copy-start(bf16[4096,1024]{1,0:T(8,128)(2,1)} %points.7) | copy-start | bytes 25165828
  4.1 1.6 copy-start.5
  5.7 0.8 copy-start.7
  6.5 84.2 %copy-start.1 = (s32[3]{0:T(128)}, s32[3]{0:T(128)S(1)}, u32[]{:S(2)}) copy-start(s32[3]{0:T(128)S(1)} %pad_add_fusion.info) | copy-start | bytes 40
  6.5 11.1 %copy-start.8 = (s32[2,4096]{1,0:T(2,128)S(1)}, s32[2,4096]{1,0:T(2,128)}, u32[]{:S(2)}) copy-start(s32[2,4096]{1,0:T(2,128)} %assign.7) | copy-start | bytes 98308
  17.0 13.8 %collective-permute-start = (f32[1032,256]{1,0:T(8,128)}, f32[1032,256]{1,0:T(8,128)S(1)}, u32[]{:S(2)}, u32[]{:S(2)}) collective-permute-start(f32[1032,256]{1,0:T(8,128)} %get-tuple-element.21), channel_id=1, source_target_pairs={{0,4},{4,0},{8,12},{12,8},{16,20},{20,16},{24,28},{28,24},{1,5},{5... | collective-permute-start | bytes 3170312 | tf_op jit(solution)/shard_map/ppermute | solution.py:89
  17.5 3.4 %copy-start.3 = (bf16[4096,1024]{1,0:T(8,128)(2,1)S(1)}, bf16[4096,1024]{1,0:T(8,128)(2,1)}, u32[]{:S(2)}) copy-start(bf16[4096,1024]{1,0:T(8,128)(2,1)} %points.7) | copy-start | bytes 25165828
  20.9 1.6 copy-start.6
  31.0 6.8 %collective-permute-start.1 = (f32[128,256]{1,0:T(8,128)S(1)}, f32[128,256]{1,0:T(8,128)S(1)}, u32[]{:S(2)}, u32[]{:S(2)}) collective-permute-start(f32[128,256]{1,0:T(8,128)S(1)} %get-tuple-element.48), channel_id=1, source_target_pairs={{0,16},{4,20},{8,24},{12,28},{16,0},{20,4},{24,8},{28,12},{1,17},{... | collective-permute-start | bytes 393224 | tf_op jit(solution)/shard_map/ppermute | solution.py:89
  33.6 5.9 %collective-permute-start.3 = (f32[136,256]{1,0:T(8,128)S(1)}, f32[136,256]{1,0:T(8,128)S(1)}, u32[]{:S(2)}, u32[]{:S(2)}) collective-permute-start(f32[136,256]{1,0:T(8,128)S(1)} %pad_maximum_fusion.4), channel_id=1, source_target_pairs={{0,8},{4,12},{8,0},{12,4},{16,24},{20,28},{24,16},{28,20},{1,9},{5... | collective-permute-start | bytes 417800 | tf_op jit(solution)/shard_map/ppermute | solution.py:89
  37.7 3.9 %copy-start.23 = (s32[512]{0:T(512)S(1)}, s32[512]{0:T(512)}, u32[]{:S(2)}) copy-start(s32[512]{0:T(512)} %param.9) | copy-start | bytes 6148
  37.7 3.9 %copy-start.22 = (f32[64,1024]{1,0:T(8,128)S(1)}, f32[64,1024]{1,0:T(8,128)}, u32[]{:S(2)}) copy-start(f32[64,1024]{1,0:T(8,128)} %param.8) | copy-start | bytes 786436
  39.5 8.1 %collective-permute-start.4 = (f32[264,256]{1,0:T(8,128)S(1)}, f32[264,256]{1,0:T(8,128)S(1)}, u32[]{:S(2)}, u32[]{:S(2)}) collective-permute-start(f32[264,256]{1,0:T(8,128)S(1)} %pad_maximum_fusion), channel_id=1, source_target_pairs={{0,16},{4,20},{8,24},{12,28},{16,0},{20,4},{24,8},{28,12},{1,17},{... | collective-permute-start | bytes 811016 | tf_op jit(solution)/shard_map/ppermute | solution.py:89
  39.9 7.7 %collective-permute-start.2 = (f32[256,256]{1,0:T(8,128)S(1)}, f32[256,256]{1,0:T(8,128)S(1)}, u32[]{:S(2)}, u32[]{:S(2)}) collective-permute-start(f32[256,256]{1,0:T(8,128)S(1)} %pad_maximum_fusion.2), channel_id=1, source_target_pairs={{0,8},{4,12},{8,0},{12,4},{16,24},{20,28},{24,16},{28,20},{1,9},{5... | collective-permute-start | bytes 786440 | tf_op jit(solution)/shard_map/ppermute | solution.py:89
  48.5 6.8 %collective-permute-start.8 = (f32[256,256]{1,0:T(8,128)S(1)}, f32[256,256]{1,0:T(8,128)S(1)}, u32[]{:S(2)}, u32[]{:S(2)}) collective-permute-start(f32[256,256]{1,0:T(8,128)S(1)} %get-tuple-element.22.refs_0_), channel_id=1, source_target_pairs={{0,16},{4,20},{8,24},{12,28},{16,0},{20,4},{24,8},{28,12},{1,17},{... | collective-permute-start | bytes 786440 | tf_op jit(solution)/shard_map/ppermute | solution.py:89
  49.9 7.1 %collective-permute-start.6 = (f32[256,256]{1,0:T(8,128)S(1)}, f32[256,256]{1,0:T(8,128)S(1)}, u32[]{:S(2)}, u32[]{:S(2)}) collective-permute-start(f32[256,256]{1,0:T(8,128)S(1)} %get-tuple-element.22.refs_0_), channel_id=1, source_target_pairs={{0,8},{4,12},{8,0},{12,4},{16,24},{20,28},{24,16},{28,20},{1,9},{5... | collective-permute-start | bytes 786440 | tf_op jit(solution)/shard_map/ppermute | solution.py:89
  55.3 5.0 %collective-permute-start.10 = (f32[128,256]{1,0:T(8,128)S(1)}, f32[128,256]{1,0:T(8,128)S(1)}, u32[]{:S(2)}, u32[]{:S(2)}) collective-permute-start(f32[128,256]{1,0:T(8,128)S(1)} %slice.180), channel_id=1, source_target_pairs={{0,8},{4,12},{8,0},{12,4},{16,24},{20,28},{24,16},{28,20},{1,9},{5... | collective-permute-start | bytes 393224 | tf_op jit(solution)/shard_map/ppermute | solution.py:89
  57.0 5.0 %collective-permute-start.12 = (f32[128,256]{1,0:T(8,128)S(1)}, f32[128,256]{1,0:T(8,128)S(1)}, u32[]{:S(2)}, u32[]{:S(2)}) collective-permute-start(f32[128,256]{1,0:T(8,128)S(1)} %slice.181), channel_id=1, source_target_pairs={{0,16},{4,20},{8,24},{12,28},{16,0},{20,4},{24,8},{28,12},{1,17},{... | collective-permute-start | bytes 393224 | tf_op jit(solution)/shard_map/ppermute | solution.py:89
  62.0 3.4 %copy-start.4 = (bf16[4096,1024]{1,0:T(8,128)(2,1)S(1)}, bf16[4096,1024]{1,0:T(8,128)(2,1)}, u32[]{:S(2)}) copy-start(bf16[4096,1024]{1,0:T(8,128)(2,1)} %points.7) | copy-start | bytes 25165828
  73.8 25.4 %collective-permute-start.14 = (f32[1032,256]{1,0:T(8,128)S(1)}, f32[1032,256]{1,0:T(8,128)S(1)}, u32[]{:S(2)}, u32[]{:S(2)}) collective-permute-start(f32[1032,256]{1,0:T(8,128)S(1)} %get-tuple-element.25), channel_id=1, source_target_pairs={{0,4},{4,0},{8,12},{12,8},{16,20},{20,16},{24,28},{28,24},{1,5},{5... | collective-permute-start | bytes 3170312 | tf_op jit(solution)/shard_map/ppermute | solution.py:89
  73.9 2.8 %collective-permute-start.19 = (f32[64,384]{1,0:T(8,128)S(1)}, f32[64,384]{1,0:T(8,128)S(1)}, u32[]{:S(2)}, u32[]{:S(2)}) collective-permute-start(f32[64,384]{1,0:T(8,128)S(1)} %get-tuple-element.26), channel_id=1, source_target_pairs={{0,4},{4,0},{8,12},{12,8},{16,20},{20,16},{24,28},{28,24},{1,5},{5... | collective-permute-start | bytes 294920 | tf_op jit(solution)/shard_map/ppermute | solution.py:89
  74.4 10.4 %collective-permute-start.5 = (f32[256,256]{1,0:T(8,128)S(1)}, f32[256,256]{1,0:T(8,128)S(1)}, u32[]{:S(2)}, u32[]{:S(2)}) collective-permute-start(f32[256,256]{1,0:T(8,128)S(1)} %get-tuple-element.22.refs_0_), channel_id=1, source_target_pairs={{0,4},{4,0},{8,12},{12,8},{16,20},{20,16},{24,28},{28,24},{1,5},{5... | collective-permute-start | bytes 786440 | tf_op jit(solution)/shard_map/ppermute | solution.py:89
  76.7 5.2 %collective-permute-start.20 = (f32[64,384]{1,0:T(8,128)S(1)}, f32[64,384]{1,0:T(8,128)S(1)}, u32[]{:S(2)}, u32[]{:S(2)}) collective-permute-start(f32[64,384]{1,0:T(8,128)S(1)} %add.111), channel_id=1, source_target_pairs={{0,1},{1,0},{2,3},{3,2},{4,5},{5,4},{6,7},{7,6},{8,9},{9,8},{10,11... | collective-permute-start | bytes 294920 | tf_op jit(solution)/shard_map/ppermute | solution.py:89
  78.8 10.5 %collective-permute-start.9 = (f32[256,256]{1,0:T(8,128)S(1)}, f32[256,256]{1,0:T(8,128)S(1)}, u32[]{:S(2)}, u32[]{:S(2)}) collective-permute-start(f32[256,256]{1,0:T(8,128)S(1)} %collective-permute-done.8.refs_2_), channel_id=1, source_target_pairs={{0,4},{4,0},{8,12},{12,8},{16,20},{20,16},{24,28},{28,24},{1,5},{5... | collective-permute-start | bytes 786440 | tf_op jit(solution)/shard_map/ppermute | solution.py:89
  78.8 10.5 %collective-permute-start.7 = (f32[256,256]{1,0:T(8,128)S(1)}, f32[256,256]{1,0:T(8,128)S(1)}, u32[]{:S(2)}, u32[]{:S(2)}) collective-permute-start(f32[256,256]{1,0:T(8,128)S(1)} %collective-permute-done.6.refs_1_), channel_id=1, source_target_pairs={{0,4},{4,0},{8,12},{12,8},{16,20},{20,16},{24,28},{28,24},{1,5},{5... | collective-permute-start | bytes 786440 | tf_op jit(solution)/shard_map/ppermute | solution.py:89
  81.9 7.4 %collective-permute-start.21 = (f32[64,384]{1,0:T(8,128)S(1)}, f32[64,384]{1,0:T(8,128)S(1)}, u32[]{:S(2)}, u32[]{:S(2)}) collective-permute-start(f32[64,384]{1,0:T(8,128)S(1)} %add.112), channel_id=1, source_target_pairs={{0,2},{1,3},{2,0},{3,1},{4,6},{5,7},{6,4},{7,5},{8,10},{9,11},{10,... | collective-permute-start | bytes 294920 | tf_op jit(solution)/shard_map/ppermute | solution.py:89
  84.8 4.6 %collective-permute-start.11 = (f32[128,256]{1,0:T(8,128)S(1)}, f32[128,256]{1,0:T(8,128)S(1)}, u32[]{:S(2)}, u32[]{:S(2)}) collective-permute-start(f32[128,256]{1,0:T(8,128)S(1)} %collective-permute-done.10.refs_3_), channel_id=1, source_target_pairs={{0,4},{4,0},{8,12},{12,8},{16,20},{20,16},{24,28},{28,24},{1,5},{5... | collective-permute-start | bytes 393224 | tf_op jit(solution)/shard_map/ppermute | solution.py:89
  89.3 1.3 collective-permute-start.13
  99.5 5.6 %collective-permute-start.15 = (f32[128,256]{1,0:T(8,128)S(1)}, f32[128,256]{1,0:T(8,128)S(1)}, u32[]{:S(2)}, u32[]{:S(2)}) collective-permute-start(f32[128,256]{1,0:T(8,128)S(1)} %get-tuple-element.42), channel_id=1, source_target_pairs={{0,16},{4,20},{8,24},{12,28},{16,0},{20,4},{24,8},{28,12},{1,17},{... | collective-permute-start | bytes 393224 | tf_op jit(solution)/shard_map/ppermute | solution.py:89
  99.9 6.7 %collective-permute-start.17 = (f32[136,256]{1,0:T(8,128)S(1)}, f32[136,256]{1,0:T(8,128)S(1)}, u32[]{:S(2)}, u32[]{:S(2)}) collective-permute-start(f32[136,256]{1,0:T(8,128)S(1)} %pad_maximum_fusion.5), channel_id=1, source_target_pairs={{0,8},{4,12},{8,0},{12,4},{16,24},{20,28},{24,16},{28,20},{1,9},{5... | collective-permute-start | bytes 417800 | tf_op jit(solution)/shard_map/ppermute | solution.py:89
  105.1 7.6 %collective-permute-start.16 = (f32[256,256]{1,0:T(8,128)S(1)}, f32[256,256]{1,0:T(8,128)S(1)}, u32[]{:S(2)}, u32[]{:S(2)}) collective-permute-start(f32[256,256]{1,0:T(8,128)S(1)} %pad_maximum_fusion.3), channel_id=1, source_target_pairs={{0,8},{4,12},{8,0},{12,4},{16,24},{20,28},{24,16},{28,20},{1,9},{5... | collective-permute-start | bytes 786440 | tf_op jit(solution)/shard_map/ppermute | solution.py:89
  106.6 7.5 %collective-permute-start.18 = (f32[264,256]{1,0:T(8,128)S(1)}, f32[264,256]{1,0:T(8,128)S(1)}, u32[]{:S(2)}, u32[]{:S(2)}) collective-permute-start(f32[264,256]{1,0:T(8,128)S(1)} %pad_maximum_fusion.1), channel_id=1, source_target_pairs={{0,16},{4,20},{8,24},{12,28},{16,0},{20,4},{24,8},{28,12},{1,17},{... | collective-permute-start | bytes 811016 | tf_op jit(solution)/shard_map/ppermute | solution.py:89
  115.0 21.7 %copy-start = (f32[256,256]{1,0:T(8,128)}, f32[256,256]{1,0:T(8,128)S(1)}, u32[]{:S(2)}) copy-start(f32[256,256]{1,0:T(8,128)S(1)} %get-tuple-element.27.refs_0_) | copy-start | bytes 786436
  115.0 1.4 collective-permute-start.31
  116.4 4.9 %collective-permute-start.32 = (f32[64,384]{1,0:T(8,128)S(1)}, f32[64,384]{1,0:T(8,128)S(1)}, u32[]{:S(2)}, u32[]{:S(2)}) collective-permute-start(f32[64,384]{1,0:T(8,128)S(1)} %add.116), channel_id=1, source_target_pairs={{0,1},{1,0},{2,3},{3,2},{4,5},{5,4},{6,7},{7,6},{8,9},{9,8},{10,11... | collective-permute-start | bytes 294920 | tf_op jit(solution)/shard_map/ppermute | solution.py:89
  117.1 10.8 %collective-permute-start.23 = (f32[256,256]{1,0:T(8,128)S(1)}, f32[256,256]{1,0:T(8,128)S(1)}, u32[]{:S(2)}, u32[]{:S(2)}) collective-permute-start(f32[256,256]{1,0:T(8,128)S(1)} %get-tuple-element.27.refs_0_), channel_id=1, source_target_pairs={{0,16},{4,20},{8,24},{12,28},{16,0},{20,4},{24,8},{28,12},{1,17},{... | collective-permute-start | bytes 786440 | tf_op jit(solution)/shard_map/ppermute | solution.py:89
  117.7 10.2 %collective-permute-start.22 = (f32[256,256]{1,0:T(8,128)S(1)}, f32[256,256]{1,0:T(8,128)S(1)}, u32[]{:S(2)}, u32[]{:S(2)}) collective-permute-start(f32[256,256]{1,0:T(8,128)S(1)} %get-tuple-element.27.refs_0_), channel_id=1, source_target_pairs={{0,8},{4,12},{8,0},{12,4},{16,24},{20,28},{24,16},{28,20},{1,9},{5... | collective-permute-start | bytes 786440 | tf_op jit(solution)/shard_map/ppermute | solution.py:89
  121.3 10.9 %collective-permute-start.33 = (f32[64,384]{1,0:T(8,128)S(1)}, f32[64,384]{1,0:T(8,128)S(1)}, u32[]{:S(2)}, u32[]{:S(2)}) collective-permute-start(f32[64,384]{1,0:T(8,128)S(1)} %add.117), channel_id=1, source_target_pairs={{0,2},{1,3},{2,0},{3,1},{4,6},{5,7},{6,4},{7,5},{8,10},{9,11},{10,... | collective-permute-start | bytes 294920 | tf_op jit(solution)/shard_map/ppermute | solution.py:89
  123.7 9.6 %collective-permute-start.38 = (f32[4,4096]{1,0:T(4,128)S(1)}, f32[4,4096]{1,0:T(4,128)S(1)}, u32[]{:S(2)}, u32[]{:S(2)}) collective-permute-start(f32[4,4096]{1,0:T(4,128)S(1)} %pad_maximum_fusion.6), channel_id=1, source_target_pairs={{0,2},{1,3},{2,0},{3,1},{4,6},{5,7},{6,4},{7,5},{8,10},{9,11},{10,... | collective-permute-start | bytes 196616 | tf_op jit(solution)/shard_map/ppermute | solution.py:89
  124.4 9.9 %collective-permute-start.39 = (f32[4,4096]{1,0:T(4,128)S(1)}, f32[4,4096]{1,0:T(4,128)S(1)}, u32[]{:S(2)}, u32[]{:S(2)}) collective-permute-start(f32[4,4096]{1,0:T(4,128)S(1)} %pad_maximum_fusion.6), channel_id=1, source_target_pairs={{0,3},{1,2},{2,1},{3,0},{4,7},{5,6},{6,5},{7,4},{8,11},{9,10},{10,... | collective-permute-start | bytes 196616 | tf_op jit(solution)/shard_map/ppermute | solution.py:89
  127.9 16.1 %copy-start.9 = (f32[256,256]{1,0:T(8,128)}, f32[256,256]{1,0:T(8,128)S(1)}, u32[]{:S(2)}) copy-start(f32[256,256]{1,0:T(8,128)S(1)} %collective-permute-done.23.refs_2_) | copy-start | bytes 786436
  127.9 7.5 %collective-permute-start.37 = (f32[4,4096]{1,0:T(4,128)S(1)}, f32[4,4096]{1,0:T(4,128)S(1)}, u32[]{:S(2)}, u32[]{:S(2)}) collective-permute-start(f32[4,4096]{1,0:T(4,128)S(1)} %pad_maximum_fusion.6), channel_id=1, source_target_pairs={{0,1},{1,0},{2,3},{3,2},{4,5},{5,4},{6,7},{7,6},{8,9},{9,8},{10,11... | collective-permute-start | bytes 196616 | tf_op jit(solution)/shard_map/ppermute | solution.py:89
  127.9 16.0 %copy-start.10 = (f32[256,256]{1,0:T(8,128)}, f32[256,256]{1,0:T(8,128)S(1)}, u32[]{:S(2)}) copy-start(f32[256,256]{1,0:T(8,128)S(1)} %collective-permute-done.22.refs_1_) | copy-start | bytes 786436
  127.9 8.9 %collective-permute-start.26 = (f32[256,256]{1,0:T(8,128)S(1)}, f32[256,256]{1,0:T(8,128)S(1)}, u32[]{:S(2)}, u32[]{:S(2)}) collective-permute-start(f32[256,256]{1,0:T(8,128)S(1)} %get-tuple-element.27.refs_0_), channel_id=1, source_target_pairs={{0,4},{4,0},{8,12},{12,8},{16,20},{20,16},{24,28},{28,24},{1,5},{5... | collective-permute-start | bytes 786440 | tf_op jit(solution)/shard_map/ppermute | solution.py:89
  132.2 8.6 %collective-permute-start.24 = (f32[128,256]{1,0:T(8,128)S(1)}, f32[128,256]{1,0:T(8,128)S(1)}, u32[]{:S(2)}, u32[]{:S(2)}) collective-permute-start(f32[128,256]{1,0:T(8,128)S(1)} %slice.196), channel_id=1, source_target_pairs={{0,8},{4,12},{8,0},{12,4},{16,24},{20,28},{24,16},{28,20},{1,9},{5... | collective-permute-start | bytes 393224 | tf_op jit(solution)/shard_map/ppermute | solution.py:89
  133.0 11.0 %copy-start.14 = (f32[64,256]{1,0:T(8,128)}, f32[64,256]{1,0:T(8,128)S(1)}, u32[]{:S(2)}) copy-start(f32[64,256]{1,0:T(8,128)S(1)} %fusion.refs_10_) | copy-start | bytes 196612
  133.3 7.5 %collective-permute-start.25 = (f32[128,256]{1,0:T(8,128)S(1)}, f32[128,256]{1,0:T(8,128)S(1)}, u32[]{:S(2)}, u32[]{:S(2)}) collective-permute-start(f32[128,256]{1,0:T(8,128)S(1)} %slice.197), channel_id=1, source_target_pairs={{0,16},{4,20},{8,24},{12,28},{16,0},{20,4},{24,8},{28,12},{1,17},{... | collective-permute-start | bytes 393224 | tf_op jit(solution)/shard_map/ppermute | solution.py:89
  134.3 4.7 %collective-permute-start.35 = (f32[64,256]{1,0:T(8,128)S(1)}, f32[64,256]{1,0:T(8,128)S(1)}, u32[]{:S(2)}, u32[]{:S(2)}) collective-permute-start(f32[64,256]{1,0:T(8,128)S(1)} %fusion.refs_10_), channel_id=1, source_target_pairs={{0,16},{4,20},{8,24},{12,28},{16,0},{20,4},{24,8},{28,12},{1,17},{... | collective-permute-start | bytes 196616 | tf_op jit(solution)/shard_map/ppermute | solution.py:89
  135.4 4.3 %collective-permute-start.34 = (f32[64,256]{1,0:T(8,128)S(1)}, f32[64,256]{1,0:T(8,128)S(1)}, u32[]{:S(2)}, u32[]{:S(2)}) collective-permute-start(f32[64,256]{1,0:T(8,128)S(1)} %fusion.refs_10_), channel_id=1, source_target_pairs={{0,8},{4,12},{8,0},{12,4},{16,24},{20,28},{24,16},{28,20},{1,9},{5... | collective-permute-start | bytes 196616 | tf_op jit(solution)/shard_map/ppermute | solution.py:89
  136.9 7.1 %copy-start.11 = (f32[256,256]{1,0:T(8,128)}, f32[256,256]{1,0:T(8,128)S(1)}, u32[]{:S(2)}) copy-start(f32[256,256]{1,0:T(8,128)S(1)} %collective-permute-done.26.refs_5_) | copy-start | bytes 786436
  136.9 7.0 %collective-permute-start.28 = (f32[256,256]{1,0:T(8,128)S(1)}, f32[256,256]{1,0:T(8,128)S(1)}, u32[]{:S(2)}, u32[]{:S(2)}) collective-permute-start(f32[256,256]{1,0:T(8,128)S(1)} %collective-permute-done.23.refs_2_), channel_id=1, source_target_pairs={{0,4},{4,0},{8,12},{12,8},{16,20},{20,16},{24,28},{28,24},{1,5},{5... | collective-permute-start | bytes 786440 | tf_op jit(solution)/shard_map/ppermute | solution.py:89
  139.0 5.0 %copy-start.19 = (f32[64,256]{1,0:T(8,128)}, f32[64,256]{1,0:T(8,128)S(1)}, u32[]{:S(2)}) copy-start(f32[64,256]{1,0:T(8,128)S(1)} %collective-permute-done.35.refs_12_) | copy-start | bytes 196612
  139.0 4.9 %collective-permute-start.27 = (f32[256,256]{1,0:T(8,128)S(1)}, f32[256,256]{1,0:T(8,128)S(1)}, u32[]{:S(2)}, u32[]{:S(2)}) collective-permute-start(f32[256,256]{1,0:T(8,128)S(1)} %collective-permute-done.22.refs_1_), channel_id=1, source_target_pairs={{0,4},{4,0},{8,12},{12,8},{16,20},{20,16},{24,28},{28,24},{1,5},{5... | collective-permute-start | bytes 786440 | tf_op jit(solution)/shard_map/ppermute | solution.py:89
  139.6 4.4 %copy-start.20 = (f32[64,256]{1,0:T(8,128)}, f32[64,256]{1,0:T(8,128)S(1)}, u32[]{:S(2)}) copy-start(f32[64,256]{1,0:T(8,128)S(1)} %collective-permute-done.34.refs_11_) | copy-start | bytes 196612
  139.6 4.3 %collective-permute-start.36 = (f32[64,256]{1,0:T(8,128)S(1)}, f32[64,256]{1,0:T(8,128)S(1)}, u32[]{:S(2)}, u32[]{:S(2)}) collective-permute-start(f32[64,256]{1,0:T(8,128)S(1)} %collective-permute-done.35.refs_12_), channel_id=1, source_target_pairs={{0,8},{4,12},{8,0},{12,4},{16,24},{20,28},{24,16},{28,20},{1,9},{5... | collective-permute-start | bytes 196616 | tf_op jit(solution)/shard_map/ppermute | solution.py:89
  140.8 3.2 %copy-start.15 = (f32[128,256]{1,0:T(8,128)}, f32[128,256]{1,0:T(8,128)S(1)}, u32[]{:S(2)}) copy-start(f32[128,256]{1,0:T(8,128)S(1)} %collective-permute-done.24.refs_3_) | copy-start | bytes 393220
  140.8 3.1 %collective-permute-start.29 = (f32[128,256]{1,0:T(8,128)S(1)}, f32[128,256]{1,0:T(8,128)S(1)}, u32[]{:S(2)}, u32[]{:S(2)}) collective-permute-start(f32[128,256]{1,0:T(8,128)S(1)} %collective-permute-done.24.refs_3_), channel_id=1, source_target_pairs={{0,4},{4,0},{8,12},{12,8},{16,20},{20,16},{24,28},{28,24},{1,5},{5... | collective-permute-start | bytes 393224 | tf_op jit(solution)/shard_map/ppermute | solution.py:89
  140.8 3.2 %copy-start.16 = (f32[128,256]{1,0:T(8,128)}, f32[128,256]{1,0:T(8,128)S(1)}, u32[]{:S(2)}) copy-start(f32[128,256]{1,0:T(8,128)S(1)} %collective-permute-done.25.refs_4_) | copy-start | bytes 393220
  140.8 3.1 %collective-permute-start.30 = (f32[128,256]{1,0:T(8,128)S(1)}, f32[128,256]{1,0:T(8,128)S(1)}, u32[]{:S(2)}, u32[]{:S(2)}) collective-permute-start(f32[128,256]{1,0:T(8,128)S(1)} %collective-permute-done.25.refs_4_), channel_id=1, source_target_pairs={{0,4},{4,0},{8,12},{12,8},{16,20},{20,16},{24,28},{28,24},{1,5},{5... | collective-permute-start | bytes 393224 | tf_op jit(solution)/shard_map/ppermute | solution.py:89
  143.9 0.6 copy-start.21
  143.9 0.7 copy-start.17
  143.9 0.7 copy-start.12
  143.9 0.8 copy-start.18
  144.7 0.7 copy-start.13

commit v2 on v0

--- a/solution.py
+++ b/solution.py
@@ -1,31 +1,35 @@
+import functools
 import math
 
 import jax
 import jax.numpy as jnp
 from jax import lax
+from jax.experimental import pallas as pl
+from jax.experimental.pallas import tpu as pltpu
 from jax.sharding import PartitionSpec as P
 
 NC = 64
 PASSES = 2
-
+FAR = 3.0e38
 
 prior_weight = 4.0
+HIGHEST = lax.Precision.HIGHEST
 
 
 def refine(totals, counts, coarse_cols, coarse_table):
-    lookup = jnp.dot(coarse_table, coarse_cols, precision=lax.Precision.HIGHEST)
+    lookup = jnp.dot(coarse_table, coarse_cols, precision=HIGHEST)
     fine_next = (totals + prior_weight * lookup) / (counts + prior_weight)[:, None]
     coarse_part = lax.dot_general(
         coarse_table,
         counts[:, None] * fine_next,
         (((0,), (0,)), ((), ())),
-        precision=lax.Precision.HIGHEST,
+        precision=HIGHEST,
     )
     coarse_weight = jnp.sum(coarse_table * counts[:, None], axis=0)
     return (fine_next, coarse_part, coarse_weight)
 
 
-def on_device(points, fine_assign, fine_start, coarse_start, coarse_assign):
+def on_device_any(points, fine_assign, fine_start, coarse_start, coarse_assign):
     width = points.shape[1]
     local_count = fine_start.shape[0]
     offset = lax.axis_index("cen") * local_count
@@ -75,8 +79,360 @@
     return (fine_now, coarse_now, jnp.stack(gap_rows))
 
 
+CORE, ACROSS_X, ACROSS_Y = 1, 2, 4
+SLOTS = 4
+TAIL = 8
+
+
+def swap(value, bit, axis="pts"):
+    size = lax.axis_size(axis)
+    return lax.ppermute(value, axis, [(i, i ^ bit) for i in range(size)])
+
+
+def pass_body(info, points, assign, *refs, pass_index, pieces, first, chained, tile):
+    refs = list(refs)
+    fine_refs = [refs.pop(0) for _ in pieces] if pieces else [refs.pop(0)]
+    squares_in = None if first else refs.pop(0)
+    seen_in = refs.pop(0) if chained else None
+    payload, seen = refs.pop(0), refs.pop(0)
+    squares_out = refs.pop(0) if first else None
+    kept, arrived, low, sums, tallies, products, held = refs
+    rows, width = low.shape
+    block_width = width // SLOTS
+    here, base = info[0], info[2]
+    tiles = points.shape[0] // tile
+
+    def span(i):
+        return slice(i * tile, (i + 1) * tile)
+
+    loads = [
+        pltpu.make_async_copy(points.at[span(i)], kept.at[span(i)], arrived.at[i])
+        for i in range(tiles)
+    ]
+    for load in loads:
+        load.start()
+
+    norm = jnp.zeros((rows, 1), jnp.float32)
+    for slot, ref in zip(pieces, fine_refs) if pieces else [(None, fine_refs[0])]:
+        block = ref[...]
+        norm = norm + jnp.sum(block * block, axis=1, keepdims=True)
+        block = (-2.0 * block).astype(jnp.bfloat16)
+        if pieces:
+            column = pl.multiple_of((here ^ slot) * block_width, block_width)
+            low[:, pl.ds(column, block_width)] = block
+        else:
+            low[...] = block
+    sums[...] = jnp.zeros_like(sums)
+    tallies[...] = jnp.zeros_like(tallies)
+
+    def multiply(i):
+        loads[i].wait()
+        products[i % 2] = lax.dot_general(
+            low[...], kept[span(i), :], (((1,), (1,)), ((), ())), preferred_element_type=jnp.float32
+        )
+
+    def weigh(i):
+        energy = norm + products[i % 2]
+        chosen = assign[pass_index : pass_index + 1, span(i)] - base
+        member = lax.broadcasted_iota(jnp.int32, energy.shape, 0) == chosen
+        picked = jnp.sum(jnp.where(member, energy, 0.0), axis=0, keepdims=True)
+        nearest = jnp.min(energy, axis=0, keepdims=True)
+        inside = (chosen >= 0) & (chosen < rows)
+        picked_seen = jnp.where(inside, picked, FAR)
+        if chained:
+            picked_seen = jnp.minimum(picked_seen, seen_in[0:1, span(i)])
+            nearest = jnp.minimum(nearest, seen_in[1:2, span(i)])
+        seen[0:1, span(i)] = picked_seen
+        seen[1:2, span(i)] = nearest
+        if first:
+            folded = jnp.zeros((tile, 128), jnp.float32)
+            for lane in range(0, width, 128):
+                values = kept[span(i), lane : lane + 128].astype(jnp.float32)
+                folded = folded + values * values
+            squares = lax.dot_general(
+                jnp.ones((8, 128), jnp.float32),
+                folded,
+                (((1,), (1,)), ((), ())),
+                precision=HIGHEST,
+                preferred_element_type=jnp.float32,
+            )[:1]
+            squares_out[0:1, span(i)] = squares
+        else:
+            squares = squares_in[0:1, span(i)]
+        weights = 1.0 / (1.0 + (squares + picked) / width)
+        weighted = jnp.where(member, weights, 0.0)
+        tally = tallies[...]
+        for lane in range(0, tile, 128):
+            tally = tally + weighted[:, lane : lane + 128]
+        tallies[...] = tally
+        held[i % 2] = weighted.astype(jnp.bfloat16)
+
+    def collect(i):
+        sums[...] += jnp.dot(held[i % 2], kept[span(i), :], preferred_element_type=jnp.float32)
+
+    multiply(0)
+    for i in range(tiles):
+        if i + 1 < tiles:
+            multiply(i + 1)
+        if i > 0:
+            collect(i - 1)
+        weigh(i)
+    collect(tiles - 1)
+
+    counts = jnp.broadcast_to(jnp.sum(tallies[...].T, axis=0, keepdims=True), (TAIL, rows))
+    for slot in range(SLOTS):
+        column = pl.multiple_of((here ^ slot) * block_width, block_width)
+        top = slot * (rows + TAIL)
+        payload[top : top + rows, :] = sums[:, pl.ds(column, block_width)]
+        payload[top + rows : top + rows + TAIL, :] = counts
+
+
+def run_pass(info, points, fine_assign, fine, squares, seen, *, pass_index, pieces, rows):
+    count, width = points.shape
+    block_width = width // SLOTS
+    tile = 512
+    first = squares is None
+    chained = seen is not None
+    full = lambda *shape: pl.BlockSpec(shape, lambda i, info: (0, 0))
+    in_specs = [pl.BlockSpec(memory_space=pl.ANY), full(PASSES, count)]
+    args = [points, fine_assign]
+    if pieces:
+        in_specs += [full(rows, block_width)] * len(pieces)
+        args += fine
+    else:
+        in_specs.append(pl.BlockSpec((rows, width), lambda i, info: (info[1], 0)))
+        args.append(fine)
+    if not first:
+        in_specs.append(full(1, count))
+        args.append(squares)
+    if chained:
+        in_specs.append(full(2, count))
+        args.append(seen)
+    shapes = [(SLOTS * (rows + TAIL), block_width), (2, count)]
+    if first:
+        shapes.append((1, count))
+    body = functools.partial(
+        pass_body,
+        pass_index=pass_index,
+        pieces=pieces,
+        first=first,
+        chained=chained,
+        tile=tile,
+    )
+    return pl.pallas_call(
+        body,
+        out_shape=[jax.ShapeDtypeStruct(shape, jnp.float32) for shape in shapes],
+        grid_spec=pltpu.PrefetchScalarGridSpec(
+            num_scalar_prefetch=1,
+            grid=(1,),
+            in_specs=in_specs,
+            out_specs=[full(*shape) for shape in shapes],
+            scratch_shapes=[
+                pltpu.VMEM((count, width), jnp.bfloat16),
+                pltpu.SemaphoreType.DMA((count // tile,)),
+                pltpu.VMEM((rows, width), jnp.bfloat16),
+                pltpu.VMEM((rows, width), jnp.float32),
+                pltpu.VMEM((rows, 128), jnp.float32),
+                pltpu.VMEM((2, rows, tile), jnp.float32),
+                pltpu.VMEM((2, rows, tile), jnp.bfloat16),
+            ],
+        ),
+        compiler_params=pltpu.CompilerParams(vmem_limit_bytes=56 * 2**20),
+        cost_estimate=pl.CostEstimate(
+            flops=4 * rows * count * width, bytes_accessed=2 * count * width, transcendentals=0
+        ),
+        name=f"energies_and_sums_{pass_index}{int(chained)}",
+    )(info, *args)
+
+
+def refine_body(own, sibling, over_x, over_y, over_xy, owner, coarse, fine, coarse_part):
+    rows = fine.shape[0]
+    received = own[...] + sibling[...] + over_x[...] + over_y[...] + over_xy[...]
+    totals, counts_row = received[:rows], received[rows:]
+    counts = jnp.broadcast_to(counts_row[:1], (128, rows)).T[:, :1]
+    table = (
+        lax.broadcasted_iota(jnp.int32, (NC, rows), 0) == owner[...]
+    ).astype(jnp.float32)
+    lookup = lax.dot_general(
+        table,
+        coarse[...],
+        (((0,), (0,)), ((), ())),
+        precision=HIGHEST,
+        preferred_element_type=jnp.float32,
+    )
+    new = (totals + prior_weight * lookup) / (counts + prior_weight)
+    fine[...] = new
+    coarse_part[:NC, :] = jnp.dot(
+        table, counts * new, precision=HIGHEST, preferred_element_type=jnp.float32
+    )
+    coarse_part[NC:, :] = jnp.zeros((TAIL, coarse_part.shape[1]), jnp.float32)
+    coarse_part[NC:, :NC] = lax.dot_general(
+        counts_row,
+        table,
+        (((1,), (1,)), ((), ())),
+        precision=HIGHEST,
+        preferred_element_type=jnp.float32,
+    )
+
+
+def refine_half(own, sibling, over_x, over_y, over_xy, owner, coarse):
+    block_width = coarse.shape[1]
+    rows = owner.shape[1]
+    full = lambda *shape: pl.BlockSpec(shape, lambda i: (0, 0))
+    return pl.pallas_call(
+        refine_body,
+        grid=(1,),
+        out_shape=[
+            jax.ShapeDtypeStruct((rows, block_width), jnp.float32),
+            jax.ShapeDtypeStruct((NC + TAIL, block_width), jnp.float32),
+        ],
+        in_specs=[full(rows + TAIL, block_width)] * 5
+        + [full(1, rows), full(NC, block_width)],
+        out_specs=[full(rows, block_width), full(NC + TAIL, block_width)],
+        compiler_params=pltpu.CompilerParams(vmem_limit_bytes=16 * 2**20),
+        name="refine_half",
+    )(own, sibling, over_x, over_y, over_xy, owner, coarse)
+
+
+def spread(value):
+    corner = swap(value, ACROSS_X | ACROSS_Y)
+    return [value, swap(value, ACROSS_X), swap(value, ACROSS_Y), corner]
+
+
+def add_over_cen(value):
+    others = [swap(value, bit, "cen") for bit in range(1, lax.axis_size("cen"))]
+    return functools.reduce(jnp.add, others, value)
+
+
+def place_body(info, *refs):
+    own, other, coarse = refs[:SLOTS], refs[SLOTS : 2 * SLOTS], refs[2 * SLOTS : 3 * SLOTS]
+    fine_out, coarse_out = refs[3 * SLOTS :]
+    block_width = own[0].shape[1]
+    here = info[0]
+
+    def put(pieces, target):
+        for slot, piece in enumerate(pieces):
+            column = pl.multiple_of((here ^ slot) * block_width, block_width)
+            target[:, pl.ds(column, block_width)] = piece[...]
+
+    @pl.when(pl.program_id(0) == 0)
+    def _():
+        put(own, fine_out)
+        put(coarse, coarse_out)
+
+    @pl.when(pl.program_id(0) == 1)
+    def _():
+        put(other, fine_out)
+
+
+def place(info, own, other, coarse):
+    rows, block_width = own[0].shape
+    width = SLOTS * block_width
+    full = lambda *shape: pl.BlockSpec(shape, lambda i, info: (0, 0))
+    return pl.pallas_call(
+        place_body,
+        out_shape=[
+            jax.ShapeDtypeStruct((2 * rows, width), jnp.float32),
+            jax.ShapeDtypeStruct((NC, width), jnp.float32),
+        ],
+        grid_spec=pltpu.PrefetchScalarGridSpec(
+            num_scalar_prefetch=1,
+            grid=(2,),
+            in_specs=[full(rows, block_width)] * (2 * SLOTS) + [full(NC, block_width)] * SLOTS,
+            out_specs=[
+                pl.BlockSpec((rows, width), lambda i, info: (info[1] ^ i, 0)),
+                full(NC, width),
+            ],
+        ),
+        compiler_params=pltpu.CompilerParams(vmem_limit_bytes=24 * 2**20),
+        name="place_blocks",
+    )(info, *own, *other, *coarse)
+
+
+def on_device_paired(points, fine_assign, fine_start, coarse_start, coarse_assign):
+    width = points.shape[1]
+    local_count = fine_start.shape[0]
+    rows = local_count // 2
+    block_width = width // SLOTS
+    offset = lax.axis_index("cen") * local_count
+    me = lax.axis_index("pts")
+    core, here = me & 1, me >> 1
+    owners = coarse_assign.reshape(2, 1, rows)
+    info_of = lambda half: jnp.stack([here, half, offset + half * rows]).astype(jnp.int32)
+    coarse = lax.dynamic_slice_in_dim(coarse_start, here * block_width, block_width, 1)
+    slot_rows = lambda array, slot: array[slot * (rows + TAIL) : (slot + 1) * (rows + TAIL)]
+
+    def renew(coarse, coarse_sum):
+        return (coarse_sum[:NC] + prior_weight * coarse) / (
+            coarse_sum[NC, :NC] + prior_weight
+        )[:, None]
+
+    first_pass = functools.partial(run_pass, pass_index=0, pieces=None, rows=rows)
+    sent, seen, squares = first_pass(
+        info_of(1 - core), points, fine_assign, fine_start, None, None
+    )
+    sibling = swap(sent, CORE)
+    held, seen_first = first_pass(
+        info_of(core), points, fine_assign, fine_start, squares, seen
+    )
+
+    def exchange(held, sibling):
+        outgoing = [slot_rows(held, s) + slot_rows(sibling, s) for s in range(1, SLOTS)]
+        over_xy = swap(outgoing[2], ACROSS_X | ACROSS_Y)
+        return swap(outgoing[0], ACROSS_X), swap(outgoing[1], ACROSS_Y), over_xy
+
+    incoming = exchange(held, sibling)
+    owner = lax.dynamic_index_in_dim(owners, core, 0, keepdims=False)
+    fine, coarse_part = refine_half(held, sibling, *incoming, owner, coarse)
+    own = spread(fine)
+    coarse_part = coarse_part + swap(coarse_part, CORE)
+    other = [swap(piece, CORE) for piece in own]
+
+    second_pass = functools.partial(
+        run_pass, pass_index=1, pieces=tuple(range(SLOTS)), rows=rows
+    )
+    own[0], coarse_part = lax.optimization_barrier((own[0], coarse_part))
+    sent, seen = second_pass(info_of(core), points, fine_assign, own, squares, None)
+    sibling = swap(sent, CORE)
+    held, seen_second = second_pass(
+        info_of(1 - core), points, fine_assign, other, squares, seen
+    )
+    incoming = exchange(held, sibling)
+    coarse = renew(coarse, add_over_cen(coarse_part))
+
+    seen = jnp.concatenate([seen_first, seen_second], 0)
+    others = [swap(seen, bit, "cen") for bit in range(1, lax.axis_size("cen"))]
+    seen = functools.reduce(jnp.minimum, others, seen)
+    gaps = (seen[0::2] - seen[1::2]) / math.sqrt(width)
+
+    owner = lax.dynamic_index_in_dim(owners, 1 - core, 0, keepdims=False)
+    owner, gaps = lax.optimization_barrier((owner, gaps))
+    fine, coarse_part = refine_half(held, sibling, *incoming, owner, coarse)
+    own = spread(fine)
+    coarse_part = coarse_part + swap(coarse_part, CORE)
+    coarse = renew(coarse, add_over_cen(coarse_part))
+    other = [swap(piece, CORE) for piece in own]
+    fine_now, coarse_now = place(info_of(1 - core), own, other, spread(coarse))
+    return (fine_now, coarse_now, gaps)
+
+
 def solution(mesh):
     placed = (P("pts", None), P(None, "pts"), P("cen", None), P(), P("cen"))
+
+    def on_device(points, fine_assign, fine_start, coarse_start, coarse_assign):
+        count, width = points.shape
+        local_count = fine_start.shape[0]
+        centres = mesh.shape["cen"]
+        fits = (
+            mesh.shape["pts"] == 2 * SLOTS
+            and centres & (centres - 1) == 0
+            and width // SLOTS == local_count // 2
+            and (width // SLOTS) % 128 == 0
+            and count % 1024 == 0
+        )
+        plan = on_device_paired if fits else on_device_any
+        return plan(points, fine_assign, fine_start, coarse_start, coarse_assign)
+
     return jax.shard_map(
         on_device,
         mesh=mesh,

time: 272 us -> 157 us (0.58)
  blocking collectives: 134 us -> 0 us
  Pallas kernels: 0 us -> 50.8 us
  matrix products: 46.6 us -> 0 us
  starting transfers between devices: 0.34 us -> 35.1 us
  between operations: 13.9 us -> 0.89 us
  other arithmetic: 17.5 us -> 7.31 us
  waiting for transfers between devices: 55.2 us -> 60.2 us
    psum x6 -> x0, blocking collectives: 98.4 us -> none  [the longest x2 39.2 us: on_device(): picked = lax.psum(picked_local, 'cen')]
    ppermute x0 -> x36, waiting for transfers between devices: none -> 60.2 us  [swap(): return lax.ppermute(value, axis, [(i, i ^ bit) for i in range(size)])]
    pallas_call x0 -> x7, Pallas kernels: none -> 50.8 us  [the longest x4 46.8 us: run_pass(): pl.pallas_call(body, out_shape=[jax.ShapeDtypeStruct(shape, jnp.float32)...]
    dot_general x8 -> x0, matrix products: 46.6 us -> none  [the longest x2 22.1 us: on_device(): jnp.dot(points, fine_now.astype(jnp.bfloat16).T, preferred_element_type=j...]
    ppermute x0 -> x36, starting transfers between devices: none -> 35.1 us  [swap(): return lax.ppermute(value, axis, [(i, i ^ bit) for i in range(size)])]
    all_gather x2 -> x0, waiting for transfers between devices: 28.5 us -> none  [on_device(): lax.all_gather(fine_share, 'pts', axis=1, tiled=True)]
    reduce_scatter x2 -> x0, waiting for transfers between devices: 26.6 us -> none  [on_device(): lax.psum_scatter(partial_sums, 'pts', scatter_dimension=1, tiled=True)]
    all_gather x2 -> x0, blocking collectives: 20.1 us -> none  [on_device(): lax.all_gather(coarse_share, 'pts', axis=1, tiled=True)]
  transfers between devices with their start and end apart: 4 -> 36, of which waited for: 2 -> 20; matrix products, arithmetic and copies ran while one was open for 2% -> 3% of each run, Pallas kernels for 0% -> 21%
where the time goes in v2:
time: 157 us
  waiting for transfers between devices  60.2 us (38%)
  Pallas kernels  50.8 us (32%)
  starting transfers between devices  35.1 us (22%)
  other arithmetic  7.31 us (5%)
  local copies, waits for them, and re-layouts  2.3 us (1%)
    ppermute x36, waiting for transfers between devices, swap(): return lax.ppermute(value, axis, [(i, i ^ bit) for i in range(size)])  60.2 us
    pallas_call x4, Pallas kernels, run_pass(): pl.pallas_call(body, out_shape=[jax.ShapeDtypeStruct(shape, jnp.float32)...  46.8 us
    ppermute x36, starting transfers between devices, swap(): return lax.ppermute(value, axis, [(i, i ^ bit) for i in range(size)])  35.1 us
    add x2, other arithmetic, exchange(): slot_rows(held, s) + slot_rows(sibling, s)  3.33 us
  transfers between devices with their start and end apart: 36, of which 20 were waited for; matrix products, arithmetic and copies ran while one was open for 3% of the time, Pallas kernels for 21%

profile of v2, /device:TPU:0, one launch (start us, length us, event | category | flops | bytes accessed | tf_op | source)
XLA Modules:
  0.0 156.6 jit_solution(13111376436797404116)
XLA Ops:
  0.6 0.7 pad_add_fusion
  1.3 13.2 %energies_and_sums_00.1 = (f32[1056,256]{1,0:T(8,128)}, f32[2,4096]{1,0:T(2,128)}, f32[1,4096]{1,0:T(1,128)}) custom-call(s32[3]{0:T(128)} %get-tuple-element.49.info, bf16[4096,1024]{1,0:T(8,128)(2,1)} %points.7, s32[2,4096]{1,0:T(2,128)} %assign.7, f32[512,1024]{1,0:T(8,128)} %refs_0_.3), custom_call_target="tpu_custom_call" | custom-call | flops 4294967296 | bytes 8388608 | tf_op jit(solution)/shard_map/energies_and_sums_00/pallas_call | solution.py:222
  14.6 0.5 collective-permute-start
  15.1 11.2 %energies_and_sums_01.1 = (f32[1056,256]{1,0:T(8,128)}, f32[2,4096]{1,0:T(2,128)}) custom-call(s32[3]{0:T(128)} %get-tuple-element.50.info, bf16[4096,1024]{1,0:T(8,128)(2,1)} %points.7, s32[2,4096]{1,0:T(2,128)} %assign.7, f32[512,1024]{1,0:T(8,128)} %refs_0_.3, f32[1,4096]{1,0:T(1,128)} %get-tuple-element.22.refs_1_.refs_4_, ...), custom_call_target="tpu_custom_call" | custom-call | flops 4294967296 | bytes 8388608 | tf_op jit(solution)/shard_map/energies_and_sums_01/pallas_call | solution.py:222
  26.3 2.0 %slice_add_fusion.3 = (f32[264,256]{1,0:T(8,128)}, f32[264,256]{1,0:T(8,128)S(1)}, f32[264,256]{1,0:T(8,128)S(1)}) fusion(f32[1056,256]{1,0:T(8,128)S(1)} %collective-permute-done.sibling, f32[1056,256]{1,0:T(8,128)} %get-tuple-element.24.own), kind=kLoop, calls=%fused_computation.3 | loop fusion | flops 202752 | bytes 2433024 | tf_op jit(solution)/shard_map/add | solution.py:380
  28.3 3.5 %collective-permute-start.3 = (f32[264,256]{1,0:T(8,128)}, f32[264,256]{1,0:T(8,128)S(1)}, u32[]{:S(2)}, u32[]{:S(2)}) collective-permute-start(f32[264,256]{1,0:T(8,128)} %get-tuple-element.44), channel_id=1, source_target_pairs={{0,24},{4,28},{8,16},{12,20},{16,8},{20,12},{24,0},{28,4},{1,25},{... | collective-permute-start | bytes 811016 | tf_op jit(solution)/shard_map/ppermute | solution.py:89
  31.8 0.5 collective-permute-start.2
  32.4 0.8 constant_dynamic-slice_fusion.coarse
  33.2 6.2 %collective-permute-done.3.over_xy = f32[264,256]{1,0:T(8,128)S(1)} collective-permute-done((f32[264,256]{1,0:T(8,128)}, f32[264,256]{1,0:T(8,128)S(1)}, u32[]{:S(2)}, u32[]{:S(2)}) %collective-permute-start.3) | collective-permute-done | bytes 270368 | tf_op jit(solution)/shard_map/ppermute | solution.py:89
  39.4 5.6 %collective-permute-done.2.over_y = f32[264,256]{1,0:T(8,128)S(1)} collective-permute-done((f32[264,256]{1,0:T(8,128)S(1)}, f32[264,256]{1,0:T(8,128)S(1)}, u32[]{:S(2)}, u32[]{:S(2)}) %collective-permute-start.2) | collective-permute-done | bytes 270368 | tf_op jit(solution)/shard_map/ppermute | solution.py:89
  44.9 0.3 collective-permute-done.1.over_x
  45.2 1.0 refine_half.2
  46.2 1.3 collective-permute-done.11
  47.5 3.7 %collective-permute-start.21 = (f32[72,256]{1,0:T(8,128)S(1)}, f32[72,256]{1,0:T(8,128)S(1)}, u32[]{:S(2)}, u32[]{:S(2)}) collective-permute-start(f32[72,256]{1,0:T(8,128)S(1)} %add.95), channel_id=1, source_target_pairs={{0,3},{1,2},{2,1},{3,0},{4,7},{5,6},{6,5},{7,4},{8,11},{9,10},{10,... | collective-permute-start | bytes 221192 | tf_op jit(solution)/shard_map/ppermute | solution.py:89
  51.2 0.8 collective-permute-start.19
  52.0 1.4 collective-permute-start.9
  53.4 1.5 collective-permute-start.7
  54.9 0.8 collective-permute-start.5
  55.7 2.0 %collective-permute-done.20 = f32[72,256]{1,0:T(8,128)S(1)} collective-permute-done((f32[72,256]{1,0:T(8,128)S(1)}, f32[72,256]{1,0:T(8,128)S(1)}, u32[]{:S(2)}, u32[]{:S(2)}) %collective-permute-start.20) | collective-permute-done | bytes 73760 | tf_op jit(solution)/shard_map/ppermute | solution.py:89
  57.7 4.4 %collective-permute-done.9.refs_3_ = f32[256,256]{1,0:T(8,128)S(1)} collective-permute-done((f32[256,256]{1,0:T(8,128)S(1)}, f32[256,256]{1,0:T(8,128)S(1)}, u32[]{:S(2)}, u32[]{:S(2)}) %collective-permute-start.9) | collective-permute-done | bytes 262176 | tf_op jit(solution)/shard_map/ppermute | solution.py:89
  62.2 4.0 %collective-permute-done.7.refs_2_ = f32[256,256]{1,0:T(8,128)S(1)} collective-permute-done((f32[256,256]{1,0:T(8,128)S(1)}, f32[256,256]{1,0:T(8,128)S(1)}, u32[]{:S(2)}, u32[]{:S(2)}) %collective-permute-start.7) | collective-permute-done | bytes 262176 | tf_op jit(solution)/shard_map/ppermute | solution.py:89
  66.2 0.5 collective-permute-start.6
  66.7 0.2 copy-done.7
  67.0 11.0 %energies_and_sums_10.1 = (f32[1056,256]{1,0:T(8,128)}, f32[2,4096]{1,0:T(2,128)}) custom-call(s32[3]{0:T(128)} %get-tuple-element.50.info, bf16[4096,1024]{1,0:T(8,128)(2,1)} %points.7, s32[2,4096]{1,0:T(2,128)} %assign.7, f32[256,256]{1,0:T(8,128)} %copy-done.3, f32[256,256]{1,0:T(8,128)} %copy-done.9, f32[256,256]{1,0:T(8,128)} %copy-done.7, ...), custom_call_target="tpu_custom_call" | custom-call | flops 4294967296 | bytes 8388608 | tf_op jit(solution)/shard_map/energies_and_sums_10/pallas_call | solution.py:222
  77.9 0.5 collective-permute-start.12
  78.5 0.6 copy-done.8
  79.3 0.1 copy-done.12
  79.4 11.4 %energies_and_sums_11.1 = (f32[1056,256]{1,0:T(8,128)}, f32[2,4096]{1,0:T(2,128)}) custom-call(s32[3]{0:T(128)} %get-tuple-element.49.info, bf16[4096,1024]{1,0:T(8,128)(2,1)} %points.7, s32[2,4096]{1,0:T(2,128)} %assign.7, f32[256,256]{1,0:T(8,128)} %copy-done.8, f32[256,256]{1,0:T(8,128)} %copy-done.12, f32[256,256]{1,0:T(8,128)} %copy-done.11, ...), custom_call_target="tpu_custom_call" | custom-call | flops 4294967296 | bytes 8388608 | tf_op jit(solution)/shard_map/energies_and_sums_11/pallas_call | solution.py:222
  90.8 0.8 pad_maximum_fusion
  91.6 2.4 %collective-permute-start.17 = (f32[4,4096]{1,0:T(4,128)S(1)}, f32[4,4096]{1,0:T(4,128)S(1)}, u32[]{:S(2)}, u32[]{:S(2)}) collective-permute-start(f32[4,4096]{1,0:T(4,128)S(1)} %pad_maximum_fusion), channel_id=1, source_target_pairs={{0,2},{1,3},{2,0},{3,1},{4,6},{5,7},{6,4},{7,5},{8,10},{9,11},{10,... | collective-permute-start | bytes 196616 | tf_op jit(solution)/shard_map/ppermute | solution.py:89
  93.9 1.5 collective-permute-start.18
  95.4 0.3 collective-permute-start.16
  95.7 0.9 fusion.1.coarse
  96.6 2.9 %collective-permute-done.17 = f32[4,4096]{1,0:T(4,128)S(1)} collective-permute-done((f32[4,4096]{1,0:T(4,128)S(1)}, f32[4,4096]{1,0:T(4,128)S(1)}, u32[]{:S(2)}, u32[]{:S(2)}) %collective-permute-start.17) | collective-permute-done | bytes 65568 | tf_op jit(solution)/shard_map/ppermute | solution.py:89
  99.5 0.8 collective-permute-done.18
  100.3 0.6 collective-permute-done.16
  100.9 0.8 minimum_minimum_fusion
  101.8 0.1 slice.67
  102.0 1.3 slice_add_fusion
  103.3 1.5 collective-permute-start.15
  104.8 1.5 collective-permute-start.14
  106.3 0.6 collective-permute-start.13
  106.9 0.6 subtract_multiply_fusion
  107.5 6.2 %collective-permute-done.15.over_xy = f32[264,256]{1,0:T(8,128)S(1)} collective-permute-done((f32[264,256]{1,0:T(8,128)S(1)}, f32[264,256]{1,0:T(8,128)S(1)}, u32[]{:S(2)}, u32[]{:S(2)}) %collective-permute-start.15) | collective-permute-done | bytes 270368 | tf_op jit(solution)/shard_map/ppermute | solution.py:89
  113.7 4.4 %collective-permute-done.14.over_y = f32[264,256]{1,0:T(8,128)S(1)} collective-permute-done((f32[264,256]{1,0:T(8,128)S(1)}, f32[264,256]{1,0:T(8,128)S(1)}, u32[]{:S(2)}, u32[]{:S(2)}) %collective-permute-start.14) | collective-permute-done | bytes 270368 | tf_op jit(solution)/shard_map/ppermute | solution.py:89
  118.2 1.0 refine_half.3
  119.2 1.3 collective-permute-done.29
  120.5 2.9 %collective-permute-start.32 = (f32[72,256]{1,0:T(8,128)S(1)}, f32[72,256]{1,0:T(8,128)S(1)}, u32[]{:S(2)}, u32[]{:S(2)}) collective-permute-start(f32[72,256]{1,0:T(8,128)S(1)} %add.106), channel_id=1, source_target_pairs={{0,3},{1,2},{2,1},{3,0},{4,7},{5,6},{6,5},{7,4},{8,11},{9,10},{10,... | collective-permute-start | bytes 221192 | tf_op jit(solution)/shard_map/ppermute | solution.py:89
  123.4 1.5 collective-permute-start.30
  124.9 1.5 collective-permute-start.24
  126.4 0.8 collective-permute-done.32
  127.2 1.4 collective-permute-start.23
  128.6 1.8 %collective-permute-done.31 = f32[72,256]{1,0:T(8,128)S(1)} collective-permute-done((f32[72,256]{1,0:T(8,128)S(1)}, f32[72,256]{1,0:T(8,128)S(1)}, u32[]{:S(2)}, u32[]{:S(2)}) %collective-permute-start.31) | collective-permute-done | bytes 73760 | tf_op jit(solution)/shard_map/ppermute | solution.py:89
  130.3 1.5 collective-permute-start.22
  131.8 3.1 %collective-permute-done.24.refs_3_ = f32[256,256]{1,0:T(8,128)S(1)} collective-permute-done((f32[256,256]{1,0:T(8,128)S(1)}, f32[256,256]{1,0:T(8,128)S(1)}, u32[]{:S(2)}, u32[]{:S(2)}) %collective-permute-start.24) | collective-permute-done | bytes 262176 | tf_op jit(solution)/shard_map/ppermute | solution.py:89
  135.0 5.2 %collective-permute-done.23.refs_2_ = f32[256,256]{1,0:T(8,128)S(1)} collective-permute-done((f32[256,256]{1,0:T(8,128)S(1)}, f32[256,256]{1,0:T(8,128)S(1)}, u32[]{:S(2)}, u32[]{:S(2)}) %collective-permute-start.23) | collective-permute-done | bytes 262176 | tf_op jit(solution)/shard_map/ppermute | solution.py:89
  140.2 0.5 collective-permute-start.26
  140.8 1.5 collective-permute-start.35
  142.3 3.7 %collective-permute-done.35.refs_11_ = f32[64,256]{1,0:T(8,128)S(1)} collective-permute-done((f32[64,256]{1,0:T(8,128)S(1)}, f32[64,256]{1,0:T(8,128)S(1)}, u32[]{:S(2)}, u32[]{:S(2)}) %collective-permute-start.35) | collective-permute-done | bytes 65568 | tf_op jit(solution)/shard_map/ppermute | solution.py:89
  146.0 1.4 collective-permute-start.34
  147.4 2.8 %collective-permute-done.34.refs_10_ = f32[64,256]{1,0:T(8,128)S(1)} collective-permute-done((f32[64,256]{1,0:T(8,128)S(1)}, f32[64,256]{1,0:T(8,128)S(1)}, u32[]{:S(2)}, u32[]{:S(2)}) %collective-permute-start.34) | collective-permute-done | bytes 65568 | tf_op jit(solution)/shard_map/ppermute | solution.py:89
  150.3 1.4 collective-permute-start.33
  151.7 2.8 %collective-permute-done.33.refs_9_ = f32[64,256]{1,0:T(8,128)S(1)} collective-permute-done((f32[64,256]{1,0:T(8,128)S(1)}, f32[64,256]{1,0:T(8,128)S(1)}, u32[]{:S(2)}, u32[]{:S(2)}) %collective-permute-start.33) | collective-permute-done | bytes 65568 | tf_op jit(solution)/shard_map/ppermute | solution.py:89
  154.6 2.1 %place_blocks.1 = (f32[512,1024]{1,0:T(8,128)}, f32[64,1024]{1,0:T(8,128)}) custom-call(s32[3]{0:T(128)S(1)} %copy-done.2, f32[256,256]{1,0:T(8,128)S(1)} %get-tuple-element.36.refs_0_, f32[256,256]{1,0:T(8,128)S(1)} %collective-permute-done.22.refs_1_, f32[256,256]{1,0:T(8,128)S(1)} %collective-permute-done.23.refs_2_, ...), custom_call_target="tpu_custom_call" | custom-call | tf_op jit(solution)/shard_map/place_blocks/pallas_call | solution.py:332
  (59 shorter events, 0.7 us)
Async XLA Ops:
  14.6 11.7 %collective-permute-start = (f32[1056,256]{1,0:T(8,128)}, f32[1056,256]{1,0:T(8,128)S(1)}, u32[]{:S(2)}, u32[]{:S(2)}) collective-permute-start(f32[1056,256]{1,0:T(8,128)} %get-tuple-element.25), channel_id=1, source_target_pairs={{0,4},{4,0},{8,12},{12,8},{16,20},{20,16},{24,28},{28,24},{1,5},{5... | collective-permute-start | bytes 3244040 | tf_op jit(solution)/shard_map/ppermute | solution.py:89
  26.3 6.1 %copy-start.5 = (s32[512]{0:T(512)S(1)}, s32[512]{0:T(512)}, u32[]{:S(2)}) copy-start(s32[512]{0:T(512)} %param.9) | copy-start | bytes 6148
  26.3 18.9 %copy-start.1 = (f32[1056,256]{1,0:T(8,128)S(1)}, f32[1056,256]{1,0:T(8,128)}, u32[]{:S(2)}) copy-start(f32[1056,256]{1,0:T(8,128)} %get-tuple-element.24.own) | copy-start | bytes 3244036
  28.3 11.0 %collective-permute-start.3 = (f32[264,256]{1,0:T(8,128)}, f32[264,256]{1,0:T(8,128)S(1)}, u32[]{:S(2)}, u32[]{:S(2)}) collective-permute-start(f32[264,256]{1,0:T(8,128)} %get-tuple-element.44), channel_id=1, source_target_pairs={{0,24},{4,28},{8,16},{12,20},{16,8},{20,12},{24,0},{28,4},{1,25},{... | collective-permute-start | bytes 811016 | tf_op jit(solution)/shard_map/ppermute | solution.py:89
  31.8 13.1 %collective-permute-start.2 = (f32[264,256]{1,0:T(8,128)S(1)}, f32[264,256]{1,0:T(8,128)S(1)}, u32[]{:S(2)}, u32[]{:S(2)}) collective-permute-start(f32[264,256]{1,0:T(8,128)S(1)} %get-tuple-element.45), channel_id=1, source_target_pairs={{0,16},{4,20},{8,24},{12,28},{16,0},{20,4},{24,8},{28,12},{1,17},{... | collective-permute-start | bytes 811016 | tf_op jit(solution)/shard_map/ppermute | solution.py:89
  32.3 12.9 %collective-permute-start.1 = (f32[264,256]{1,0:T(8,128)S(1)}, f32[264,256]{1,0:T(8,128)S(1)}, u32[]{:S(2)}, u32[]{:S(2)}) collective-permute-start(f32[264,256]{1,0:T(8,128)S(1)} %get-tuple-element.46), channel_id=1, source_target_pairs={{0,8},{4,12},{8,0},{12,4},{16,24},{20,28},{24,16},{28,20},{1,9},{5... | collective-permute-start | bytes 811016 | tf_op jit(solution)/shard_map/ppermute | solution.py:89
  46.2 20.4 %copy-start.3 = (f32[256,256]{1,0:T(8,128)}, f32[256,256]{1,0:T(8,128)S(1)}, u32[]{:S(2)}) copy-start(f32[256,256]{1,0:T(8,128)S(1)} %get-tuple-element.28.refs_0_) | copy-start | bytes 786436
  46.2 1.3 collective-permute-start.11
  47.5 7.4 %collective-permute-start.21 = (f32[72,256]{1,0:T(8,128)S(1)}, f32[72,256]{1,0:T(8,128)S(1)}, u32[]{:S(2)}, u32[]{:S(2)}) collective-permute-start(f32[72,256]{1,0:T(8,128)S(1)} %add.95), channel_id=1, source_target_pairs={{0,3},{1,2},{2,1},{3,0},{4,7},{5,6},{6,5},{7,4},{8,11},{9,10},{10,... | collective-permute-start | bytes 221192 | tf_op jit(solution)/shard_map/ppermute | solution.py:89
  51.2 6.5 %collective-permute-start.20 = (f32[72,256]{1,0:T(8,128)S(1)}, f32[72,256]{1,0:T(8,128)S(1)}, u32[]{:S(2)}, u32[]{:S(2)}) collective-permute-start(f32[72,256]{1,0:T(8,128)S(1)} %add.95), channel_id=1, source_target_pairs={{0,2},{1,3},{2,0},{3,1},{4,6},{5,7},{6,4},{7,5},{8,10},{9,11},{10,... | collective-permute-start | bytes 221192 | tf_op jit(solution)/shard_map/ppermute | solution.py:89
  51.2 6.5 %collective-permute-start.19 = (f32[72,256]{1,0:T(8,128)S(1)}, f32[72,256]{1,0:T(8,128)S(1)}, u32[]{:S(2)}, u32[]{:S(2)}) collective-permute-start(f32[72,256]{1,0:T(8,128)S(1)} %add.95), channel_id=1, source_target_pairs={{0,1},{1,0},{2,3},{3,2},{4,5},{5,4},{6,7},{7,6},{8,9},{9,8},{10,11... | collective-permute-start | bytes 221192 | tf_op jit(solution)/shard_map/ppermute | solution.py:89
  52.0 10.2 %collective-permute-start.9 = (f32[256,256]{1,0:T(8,128)S(1)}, f32[256,256]{1,0:T(8,128)S(1)}, u32[]{:S(2)}, u32[]{:S(2)}) collective-permute-start(f32[256,256]{1,0:T(8,128)S(1)} %get-tuple-element.28.refs_0_), channel_id=1, source_target_pairs={{0,24},{4,28},{8,16},{12,20},{16,8},{20,12},{24,0},{28,4},{1,25},{... | collective-permute-start | bytes 786440 | tf_op jit(solution)/shard_map/ppermute | solution.py:89
  53.4 12.7 %collective-permute-start.7 = (f32[256,256]{1,0:T(8,128)S(1)}, f32[256,256]{1,0:T(8,128)S(1)}, u32[]{:S(2)}, u32[]{:S(2)}) collective-permute-start(f32[256,256]{1,0:T(8,128)S(1)} %get-tuple-element.28.refs_0_), channel_id=1, source_target_pairs={{0,16},{4,20},{8,24},{12,28},{16,0},{20,4},{24,8},{28,12},{1,17},{... | collective-permute-start | bytes 786440 | tf_op jit(solution)/shard_map/ppermute | solution.py:89
  54.9 11.3 %collective-permute-start.5 = (f32[256,256]{1,0:T(8,128)S(1)}, f32[256,256]{1,0:T(8,128)S(1)}, u32[]{:S(2)}, u32[]{:S(2)}) collective-permute-start(f32[256,256]{1,0:T(8,128)S(1)} %get-tuple-element.28.refs_0_), channel_id=1, source_target_pairs={{0,8},{4,12},{8,0},{12,4},{16,24},{20,28},{24,16},{28,20},{1,9},{5... | collective-permute-start | bytes 786440 | tf_op jit(solution)/shard_map/ppermute | solution.py:89
  57.7 20.7 %collective-permute-start.4 = (f32[256,256]{1,0:T(8,128)S(1)}, f32[256,256]{1,0:T(8,128)S(1)}, u32[]{:S(2)}, u32[]{:S(2)}) collective-permute-start(f32[256,256]{1,0:T(8,128)S(1)} %get-tuple-element.28.refs_0_), channel_id=1, source_target_pairs={{0,4},{4,0},{8,12},{12,8},{16,20},{20,16},{24,28},{28,24},{1,5},{5... | collective-permute-start | bytes 786440 | tf_op jit(solution)/shard_map/ppermute | solution.py:89
  62.2 4.5 %copy-start.6 = (f32[256,256]{1,0:T(8,128)}, f32[256,256]{1,0:T(8,128)S(1)}, u32[]{:S(2)}) copy-start(f32[256,256]{1,0:T(8,128)S(1)} %collective-permute-done.9.refs_3_) | copy-start | bytes 786436
  62.2 16.3 %collective-permute-start.10 = (f32[256,256]{1,0:T(8,128)S(1)}, f32[256,256]{1,0:T(8,128)S(1)}, u32[]{:S(2)}, u32[]{:S(2)}) collective-permute-start(f32[256,256]{1,0:T(8,128)S(1)} %collective-permute-done.9.refs_3_), channel_id=1, source_target_pairs={{0,4},{4,0},{8,12},{12,8},{16,20},{20,16},{24,28},{28,24},{1,5},{5... | collective-permute-start | bytes 786440 | tf_op jit(solution)/shard_map/ppermute | solution.py:89
  66.2 0.7 copy-start.7
  66.2 12.3 %collective-permute-start.8 = (f32[256,256]{1,0:T(8,128)S(1)}, f32[256,256]{1,0:T(8,128)S(1)}, u32[]{:S(2)}, u32[]{:S(2)}) collective-permute-start(f32[256,256]{1,0:T(8,128)S(1)} %collective-permute-done.7.refs_2_), channel_id=1, source_target_pairs={{0,4},{4,0},{8,12},{12,8},{16,20},{20,16},{24,28},{28,24},{1,5},{5... | collective-permute-start | bytes 786440 | tf_op jit(solution)/shard_map/ppermute | solution.py:89
  66.2 0.8 copy-start.9
  66.2 12.3 %collective-permute-start.6 = (f32[256,256]{1,0:T(8,128)S(1)}, f32[256,256]{1,0:T(8,128)S(1)}, u32[]{:S(2)}, u32[]{:S(2)}) collective-permute-start(f32[256,256]{1,0:T(8,128)S(1)} %collective-permute-done.5.refs_1_), channel_id=1, source_target_pairs={{0,4},{4,0},{8,12},{12,8},{16,20},{20,16},{24,28},{28,24},{1,5},{5... | collective-permute-start | bytes 786440 | tf_op jit(solution)/shard_map/ppermute | solution.py:89
  77.9 24.1 %collective-permute-start.12 = (f32[1056,256]{1,0:T(8,128)}, f32[1056,256]{1,0:T(8,128)S(1)}, u32[]{:S(2)}, u32[]{:S(2)}) collective-permute-start(f32[1056,256]{1,0:T(8,128)} %get-tuple-element.31), channel_id=1, source_target_pairs={{0,4},{4,0},{8,12},{12,8},{16,20},{20,16},{24,28},{28,24},{1,5},{5... | collective-permute-start | bytes 3244040 | tf_op jit(solution)/shard_map/ppermute | solution.py:89
  78.4 0.7 copy-start.8
  78.4 0.8 copy-start.10
  78.5 0.8 copy-start.11
  78.5 0.9 copy-start.12
  79.4 11.4 %copy-start.4 = (f32[2,4096]{1,0:T(2,128)S(1)}, f32[2,4096]{1,0:T(2,128)}, u32[]{:S(2)}) copy-start(f32[2,4096]{1,0:T(2,128)} %get-tuple-element.32) | copy-start | bytes 98308
  91.6 7.9 %collective-permute-start.17 = (f32[4,4096]{1,0:T(4,128)S(1)}, f32[4,4096]{1,0:T(4,128)S(1)}, u32[]{:S(2)}, u32[]{:S(2)}) collective-permute-start(f32[4,4096]{1,0:T(4,128)S(1)} %pad_maximum_fusion), channel_id=1, source_target_pairs={{0,2},{1,3},{2,0},{3,1},{4,6},{5,7},{6,4},{7,5},{8,10},{9,11},{10,... | collective-permute-start | bytes 196616 | tf_op jit(solution)/shard_map/ppermute | solution.py:89
  93.9 6.4 %collective-permute-start.18 = (f32[4,4096]{1,0:T(4,128)S(1)}, f32[4,4096]{1,0:T(4,128)S(1)}, u32[]{:S(2)}, u32[]{:S(2)}) collective-permute-start(f32[4,4096]{1,0:T(4,128)S(1)} %pad_maximum_fusion), channel_id=1, source_target_pairs={{0,3},{1,2},{2,1},{3,0},{4,7},{5,6},{6,5},{7,4},{8,11},{9,10},{10,... | collective-permute-start | bytes 196616 | tf_op jit(solution)/shard_map/ppermute | solution.py:89
  95.4 5.6 %collective-permute-start.16 = (f32[4,4096]{1,0:T(4,128)S(1)}, f32[4,4096]{1,0:T(4,128)S(1)}, u32[]{:S(2)}, u32[]{:S(2)}) collective-permute-start(f32[4,4096]{1,0:T(4,128)S(1)} %pad_maximum_fusion), channel_id=1, source_target_pairs={{0,1},{1,0},{2,3},{3,2},{4,5},{5,4},{6,7},{7,6},{8,9},{9,8},{10,11... | collective-permute-start | bytes 196616 | tf_op jit(solution)/shard_map/ppermute | solution.py:89
  102.0 16.2 %copy-start = (f32[1056,256]{1,0:T(8,128)S(1)}, f32[1056,256]{1,0:T(8,128)}, u32[]{:S(2)}) copy-start(f32[1056,256]{1,0:T(8,128)} %get-tuple-element.30.own) | copy-start | bytes 3244036
  103.3 10.4 %collective-permute-start.15 = (f32[264,256]{1,0:T(8,128)S(1)}, f32[264,256]{1,0:T(8,128)S(1)}, u32[]{:S(2)}, u32[]{:S(2)}) collective-permute-start(f32[264,256]{1,0:T(8,128)S(1)} %get-tuple-element.41), channel_id=1, source_target_pairs={{0,24},{4,28},{8,16},{12,20},{16,8},{20,12},{24,0},{28,4},{1,25},{... | collective-permute-start | bytes 811016 | tf_op jit(solution)/shard_map/ppermute | solution.py:89
  104.8 13.3 %collective-permute-start.14 = (f32[264,256]{1,0:T(8,128)S(1)}, f32[264,256]{1,0:T(8,128)S(1)}, u32[]{:S(2)}, u32[]{:S(2)}) collective-permute-start(f32[264,256]{1,0:T(8,128)S(1)} %get-tuple-element.42), channel_id=1, source_target_pairs={{0,16},{4,20},{8,24},{12,28},{16,0},{20,4},{24,8},{28,12},{1,17},{... | collective-permute-start | bytes 811016 | tf_op jit(solution)/shard_map/ppermute | solution.py:89
  106.3 11.9 %collective-permute-start.13 = (f32[264,256]{1,0:T(8,128)S(1)}, f32[264,256]{1,0:T(8,128)S(1)}, u32[]{:S(2)}, u32[]{:S(2)}) collective-permute-start(f32[264,256]{1,0:T(8,128)S(1)} %get-tuple-element.43), channel_id=1, source_target_pairs={{0,8},{4,12},{8,0},{12,4},{16,24},{20,28},{24,16},{28,20},{1,9},{5... | collective-permute-start | bytes 811016 | tf_op jit(solution)/shard_map/ppermute | solution.py:89
  107.5 47.0 %copy-start.2 = (s32[3]{0:T(128)S(1)}, s32[3]{0:T(128)}, u32[]{:S(2)}) copy-start(s32[3]{0:T(128)} %get-tuple-element.49.info) | copy-start | bytes 40
  119.2 1.3 collective-permute-start.29
  120.5 6.7 %collective-permute-start.32 = (f32[72,256]{1,0:T(8,128)S(1)}, f32[72,256]{1,0:T(8,128)S(1)}, u32[]{:S(2)}, u32[]{:S(2)}) collective-permute-start(f32[72,256]{1,0:T(8,128)S(1)} %add.106), channel_id=1, source_target_pairs={{0,3},{1,2},{2,1},{3,0},{4,7},{5,6},{6,5},{7,4},{8,11},{9,10},{10,... | collective-permute-start | bytes 221192 | tf_op jit(solution)/shard_map/ppermute | solution.py:89
  123.4 7.0 %collective-permute-start.31 = (f32[72,256]{1,0:T(8,128)S(1)}, f32[72,256]{1,0:T(8,128)S(1)}, u32[]{:S(2)}, u32[]{:S(2)}) collective-permute-start(f32[72,256]{1,0:T(8,128)S(1)} %add.106), channel_id=1, source_target_pairs={{0,2},{1,3},{2,0},{3,1},{4,6},{5,7},{6,4},{7,5},{8,10},{9,11},{10,... | collective-permute-start | bytes 221192 | tf_op jit(solution)/shard_map/ppermute | solution.py:89
  123.4 8.4 %collective-permute-start.30 = (f32[72,256]{1,0:T(8,128)S(1)}, f32[72,256]{1,0:T(8,128)S(1)}, u32[]{:S(2)}, u32[]{:S(2)}) collective-permute-start(f32[72,256]{1,0:T(8,128)S(1)} %add.106), channel_id=1, source_target_pairs={{0,1},{1,0},{2,3},{3,2},{4,5},{5,4},{6,7},{7,6},{8,9},{9,8},{10,11... | collective-permute-start | bytes 221192 | tf_op jit(solution)/shard_map/ppermute | solution.py:89
  124.9 29.6 %collective-permute-start.25 = (f32[256,256]{1,0:T(8,128)S(1)}, f32[256,256]{1,0:T(8,128)S(1)}, u32[]{:S(2)}, u32[]{:S(2)}) collective-permute-start(f32[256,256]{1,0:T(8,128)S(1)} %get-tuple-element.36.refs_0_), channel_id=1, source_target_pairs={{0,4},{4,0},{8,12},{12,8},{16,20},{20,16},{24,28},{28,24},{1,5},{5... | collective-permute-start | bytes 786440 | tf_op jit(solution)/shard_map/ppermute | solution.py:89
  124.9 10.0 %collective-permute-start.24 = (f32[256,256]{1,0:T(8,128)S(1)}, f32[256,256]{1,0:T(8,128)S(1)}, u32[]{:S(2)}, u32[]{:S(2)}) collective-permute-start(f32[256,256]{1,0:T(8,128)S(1)} %get-tuple-element.36.refs_0_), channel_id=1, source_target_pairs={{0,24},{4,28},{8,16},{12,20},{16,8},{20,12},{24,0},{28,4},{1,25},{... | collective-permute-start | bytes 786440 | tf_op jit(solution)/shard_map/ppermute | solution.py:89
  127.2 13.0 %collective-permute-start.23 = (f32[256,256]{1,0:T(8,128)S(1)}, f32[256,256]{1,0:T(8,128)S(1)}, u32[]{:S(2)}, u32[]{:S(2)}) collective-permute-start(f32[256,256]{1,0:T(8,128)S(1)} %get-tuple-element.36.refs_0_), channel_id=1, source_target_pairs={{0,16},{4,20},{8,24},{12,28},{16,0},{20,4},{24,8},{28,12},{1,17},{... | collective-permute-start | bytes 786440 | tf_op jit(solution)/shard_map/ppermute | solution.py:89
  130.3 9.8 %collective-permute-start.22 = (f32[256,256]{1,0:T(8,128)S(1)}, f32[256,256]{1,0:T(8,128)S(1)}, u32[]{:S(2)}, u32[]{:S(2)}) collective-permute-start(f32[256,256]{1,0:T(8,128)S(1)} %get-tuple-element.36.refs_0_), channel_id=1, source_target_pairs={{0,8},{4,12},{8,0},{12,4},{16,24},{20,28},{24,16},{28,20},{1,9},{5... | collective-permute-start | bytes 786440 | tf_op jit(solution)/shard_map/ppermute | solution.py:89
  135.0 19.6 %collective-permute-start.28 = (f32[256,256]{1,0:T(8,128)S(1)}, f32[256,256]{1,0:T(8,128)S(1)}, u32[]{:S(2)}, u32[]{:S(2)}) collective-permute-start(f32[256,256]{1,0:T(8,128)S(1)} %collective-permute-done.24.refs_3_), channel_id=1, source_target_pairs={{0,4},{4,0},{8,12},{12,8},{16,20},{20,16},{24,28},{28,24},{1,5},{5... | collective-permute-start | bytes 786440 | tf_op jit(solution)/shard_map/ppermute | solution.py:89
  140.2 14.4 %collective-permute-start.27 = (f32[256,256]{1,0:T(8,128)S(1)}, f32[256,256]{1,0:T(8,128)S(1)}, u32[]{:S(2)}, u32[]{:S(2)}) collective-permute-start(f32[256,256]{1,0:T(8,128)S(1)} %collective-permute-done.23.refs_2_), channel_id=1, source_target_pairs={{0,4},{4,0},{8,12},{12,8},{16,20},{20,16},{24,28},{28,24},{1,5},{5... | collective-permute-start | bytes 786440 | tf_op jit(solution)/shard_map/ppermute | solution.py:89
  140.2 14.4 %collective-permute-start.26 = (f32[256,256]{1,0:T(8,128)S(1)}, f32[256,256]{1,0:T(8,128)S(1)}, u32[]{:S(2)}, u32[]{:S(2)}) collective-permute-start(f32[256,256]{1,0:T(8,128)S(1)} %collective-permute-done.22.refs_1_), channel_id=1, source_target_pairs={{0,4},{4,0},{8,12},{12,8},{16,20},{20,16},{24,28},{28,24},{1,5},{5... | collective-permute-start | bytes 786440 | tf_op jit(solution)/shard_map/ppermute | solution.py:89
  140.8 5.2 %collective-permute-start.35 = (f32[64,256]{1,0:T(8,128)S(1)}, f32[64,256]{1,0:T(8,128)S(1)}, u32[]{:S(2)}, u32[]{:S(2)}) collective-permute-start(f32[64,256]{1,0:T(8,128)S(1)} %fusion.refs_8_), channel_id=1, source_target_pairs={{0,24},{4,28},{8,16},{12,20},{16,8},{20,12},{24,0},{28,4},{1,25},{... | collective-permute-start | bytes 196616 | tf_op jit(solution)/shard_map/ppermute | solution.py:89
  146.0 4.3 %collective-permute-start.34 = (f32[64,256]{1,0:T(8,128)S(1)}, f32[64,256]{1,0:T(8,128)S(1)}, u32[]{:S(2)}, u32[]{:S(2)}) collective-permute-start(f32[64,256]{1,0:T(8,128)S(1)} %fusion.refs_8_), channel_id=1, source_target_pairs={{0,16},{4,20},{8,24},{12,28},{16,0},{20,4},{24,8},{28,12},{1,17},{... | collective-permute-start | bytes 196616 | tf_op jit(solution)/shard_map/ppermute | solution.py:89
  150.3 4.3 %collective-permute-start.33 = (f32[64,256]{1,0:T(8,128)S(1)}, f32[64,256]{1,0:T(8,128)S(1)}, u32[]{:S(2)}, u32[]{:S(2)}) collective-permute-start(f32[64,256]{1,0:T(8,128)S(1)} %fusion.refs_8_), channel_id=1, source_target_pairs={{0,8},{4,12},{8,0},{12,4},{16,24},{20,28},{24,16},{28,20},{1,9},{5... | collective-permute-start | bytes 196616 | tf_op jit(solution)/shard_map/ppermute | solution.py:89

commit v3 on v2

--- a/solution.py
+++ b/solution.py
@@ -91,48 +91,43 @@
 
 def pass_body(info, points, assign, *refs, pass_index, pieces, first, chained, tile):
     refs = list(refs)
-    fine_refs = [refs.pop(0) for _ in pieces] if pieces else [refs.pop(0)]
+    fine_refs = [refs.pop(0) for _ in range(SLOTS if pieces else 1)]
     squares_in = None if first else refs.pop(0)
     seen_in = refs.pop(0) if chained else None
     payload, seen = refs.pop(0), refs.pop(0)
     squares_out = refs.pop(0) if first else None
-    kept, arrived, low, sums, tallies, products, held = refs
+    kept, arrived, low, sums, tallies, even, odd = refs
     rows, width = low.shape
     block_width = width // SLOTS
-    here, base = info[0], info[2]
+    base = info[2]
     tiles = points.shape[0] // tile
 
     def span(i):
-        return slice(i * tile, (i + 1) * tile)
-
-    loads = [
-        pltpu.make_async_copy(points.at[span(i)], kept.at[span(i)], arrived.at[i])
-        for i in range(tiles)
-    ]
-    for load in loads:
-        load.start()
+        return pl.ds(pl.multiple_of(i * tile, tile), tile)
+
+    def load(i):
+        return pltpu.make_async_copy(points.at[span(i)], kept.at[span(i)], arrived.at[i])
+
+    @pl.loop(0, tiles)
+    def _(i):
+        load(i).start()
 
     norm = jnp.zeros((rows, 1), jnp.float32)
-    for slot, ref in zip(pieces, fine_refs) if pieces else [(None, fine_refs[0])]:
+    for slot, ref in enumerate(fine_refs):
         block = ref[...]
         norm = norm + jnp.sum(block * block, axis=1, keepdims=True)
-        block = (-2.0 * block).astype(jnp.bfloat16)
-        if pieces:
-            column = pl.multiple_of((here ^ slot) * block_width, block_width)
-            low[:, pl.ds(column, block_width)] = block
-        else:
-            low[...] = block
+        wide = block.shape[1]
+        low[:, slot * wide : (slot + 1) * wide] = (-2.0 * block).astype(jnp.bfloat16)
     sums[...] = jnp.zeros_like(sums)
     tallies[...] = jnp.zeros_like(tallies)
 
-    def multiply(i):
-        loads[i].wait()
-        products[i % 2] = lax.dot_general(
+    def multiply(i, target):
+        target[...] = lax.dot_general(
             low[...], kept[span(i), :], (((1,), (1,)), ((), ())), preferred_element_type=jnp.float32
         )
 
-    def weigh(i):
-        energy = norm + products[i % 2]
+    def collect(i, products):
+        energy = norm + products[...]
         chosen = assign[pass_index : pass_index + 1, span(i)] - base
         member = lax.broadcasted_iota(jnp.int32, energy.shape, 0) == chosen
         picked = jnp.sum(jnp.where(member, energy, 0.0), axis=0, keepdims=True)
@@ -165,26 +160,31 @@
         for lane in range(0, tile, 128):
             tally = tally + weighted[:, lane : lane + 128]
         tallies[...] = tally
-        held[i % 2] = weighted.astype(jnp.bfloat16)
-
-    def collect(i):
-        sums[...] += jnp.dot(held[i % 2], kept[span(i), :], preferred_element_type=jnp.float32)
-
-    multiply(0)
-    for i in range(tiles):
-        if i + 1 < tiles:
-            multiply(i + 1)
-        if i > 0:
-            collect(i - 1)
-        weigh(i)
-    collect(tiles - 1)
+        sums[...] += jnp.dot(
+            weighted.astype(jnp.bfloat16), kept[span(i), :], preferred_element_type=jnp.float32
+        )
+
+    load(0).wait()
+    multiply(0, even)
+
+    @pl.loop(0, tiles // 2)
+    def _(pair):
+        i = 2 * pair
+        load(i + 1).wait()
+
+        @pl.when(i + 2 < tiles)
+        def _():
+            load(i + 2).wait()
+
+        multiply(i + 1, odd)
+        collect(i, even)
+        multiply(jnp.minimum(i + 2, tiles - 1), even)
+        collect(i + 1, odd)
 
     counts = jnp.broadcast_to(jnp.sum(tallies[...].T, axis=0, keepdims=True), (TAIL, rows))
     for slot in range(SLOTS):
-        column = pl.multiple_of((here ^ slot) * block_width, block_width)
-        top = slot * (rows + TAIL)
-        payload[top : top + rows, :] = sums[:, pl.ds(column, block_width)]
-        payload[top + rows : top + rows + TAIL, :] = counts
+        payload[slot, :rows, :] = sums[:, slot * block_width : (slot + 1) * block_width]
+        payload[slot, rows:, :] = counts
 
 
 def run_pass(info, points, fine_assign, fine, squares, seen, *, pass_index, pieces, rows):
@@ -193,12 +193,15 @@
     tile = 512
     first = squares is None
     chained = seen is not None
-    full = lambda *shape: pl.BlockSpec(shape, lambda i, info: (0, 0))
+    full = lambda *shape: pl.BlockSpec(shape, lambda i, info: (0,) * len(shape))
     in_specs = [pl.BlockSpec(memory_space=pl.ANY), full(PASSES, count)]
     args = [points, fine_assign]
     if pieces:
-        in_specs += [full(rows, block_width)] * len(pieces)
-        args += fine
+        for slot in range(SLOTS):
+            in_specs.append(
+                pl.BlockSpec((None, rows, block_width), lambda i, info, slot=slot: (slot, 0, 0))
+            )
+            args.append(fine)
     else:
         in_specs.append(pl.BlockSpec((rows, width), lambda i, info: (info[1], 0)))
         args.append(fine)
@@ -208,7 +211,7 @@
     if chained:
         in_specs.append(full(2, count))
         args.append(seen)
-    shapes = [(SLOTS * (rows + TAIL), block_width), (2, count)]
+    shapes = [(SLOTS, rows + TAIL, block_width), (2, count)]
     if first:
         shapes.append((1, count))
     body = functools.partial(
@@ -233,8 +236,8 @@
                 pltpu.VMEM((rows, width), jnp.bfloat16),
                 pltpu.VMEM((rows, width), jnp.float32),
                 pltpu.VMEM((rows, 128), jnp.float32),
-                pltpu.VMEM((2, rows, tile), jnp.float32),
-                pltpu.VMEM((2, rows, tile), jnp.bfloat16),
+                pltpu.VMEM((rows, tile), jnp.float32),
+                pltpu.VMEM((rows, tile), jnp.float32),
             ],
         ),
         compiler_params=pltpu.CompilerParams(vmem_limit_bytes=56 * 2**20),
@@ -245,10 +248,10 @@
     )(info, *args)
 
 
-def refine_body(own, sibling, over_x, over_y, over_xy, owner, coarse, fine, coarse_part):
-    rows = fine.shape[0]
-    received = own[...] + sibling[...] + over_x[...] + over_y[...] + over_xy[...]
-    totals, counts_row = received[:rows], received[rows:]
+def refine_body(received, owner, coarse, fine, coarse_part):
+    rows = owner.shape[1]
+    total = (received[0] + received[1]) + (received[2] + received[3])
+    totals, counts_row = total[:rows], total[rows:]
     counts = jnp.broadcast_to(counts_row[:1], (128, rows)).T[:, :1]
     table = (
         lax.broadcasted_iota(jnp.int32, (NC, rows), 0) == owner[...]
@@ -261,7 +264,8 @@
         preferred_element_type=jnp.float32,
     )
     new = (totals + prior_weight * lookup) / (counts + prior_weight)
-    fine[...] = new
+    for slot in range(SLOTS):
+        fine[slot] = new
     coarse_part[:NC, :] = jnp.dot(
         table, counts * new, precision=HIGHEST, preferred_element_type=jnp.float32
     )
@@ -275,28 +279,28 @@
     )
 
 
-def refine_half(own, sibling, over_x, over_y, over_xy, owner, coarse):
+def refine_half(received, owner, coarse):
     block_width = coarse.shape[1]
     rows = owner.shape[1]
-    full = lambda *shape: pl.BlockSpec(shape, lambda i: (0, 0))
+    full = lambda *shape: pl.BlockSpec(shape, lambda i: (0,) * len(shape))
     return pl.pallas_call(
         refine_body,
         grid=(1,),
         out_shape=[
-            jax.ShapeDtypeStruct((rows, block_width), jnp.float32),
+            jax.ShapeDtypeStruct((SLOTS, rows, block_width), jnp.float32),
             jax.ShapeDtypeStruct((NC + TAIL, block_width), jnp.float32),
         ],
-        in_specs=[full(rows + TAIL, block_width)] * 5
-        + [full(1, rows), full(NC, block_width)],
-        out_specs=[full(rows, block_width), full(NC + TAIL, block_width)],
+        in_specs=[full(*received.shape), full(1, rows), full(NC, block_width)],
+        out_specs=[full(SLOTS, rows, block_width), full(NC + TAIL, block_width)],
         compiler_params=pltpu.CompilerParams(vmem_limit_bytes=16 * 2**20),
         name="refine_half",
-    )(own, sibling, over_x, over_y, over_xy, owner, coarse)
-
-
-def spread(value):
-    corner = swap(value, ACROSS_X | ACROSS_Y)
-    return [value, swap(value, ACROSS_X), swap(value, ACROSS_Y), corner]
+    )(received, owner, coarse)
+
+
+def trade(value):
+    size = lax.axis_size("pts")
+    groups = [list(range(core, size, 2)) for core in range(2)]
+    return lax.all_to_all(value, "pts", 0, 0, axis_index_groups=groups)
 
 
 def add_over_cen(value):
@@ -304,16 +308,12 @@
     return functools.reduce(jnp.add, others, value)
 
 
-def place_body(info, *refs):
-    own, other, coarse = refs[:SLOTS], refs[SLOTS : 2 * SLOTS], refs[2 * SLOTS : 3 * SLOTS]
-    fine_out, coarse_out = refs[3 * SLOTS :]
-    block_width = own[0].shape[1]
-    here = info[0]
+def place_body(info, own, other, coarse, fine_out, coarse_out):
+    block_width = own.shape[2]
 
     def put(pieces, target):
-        for slot, piece in enumerate(pieces):
-            column = pl.multiple_of((here ^ slot) * block_width, block_width)
-            target[:, pl.ds(column, block_width)] = piece[...]
+        for slot in range(SLOTS):
+            target[:, slot * block_width : (slot + 1) * block_width] = pieces[slot]
 
     @pl.when(pl.program_id(0) == 0)
     def _():
@@ -326,9 +326,9 @@
 
 
 def place(info, own, other, coarse):
-    rows, block_width = own[0].shape
+    _, rows, block_width = own.shape
     width = SLOTS * block_width
-    full = lambda *shape: pl.BlockSpec(shape, lambda i, info: (0, 0))
+    full = lambda *shape: pl.BlockSpec(shape, lambda i, info: (0,) * len(shape))
     return pl.pallas_call(
         place_body,
         out_shape=[
@@ -338,7 +338,7 @@
         grid_spec=pltpu.PrefetchScalarGridSpec(
             num_scalar_prefetch=1,
             grid=(2,),
-            in_specs=[full(rows, block_width)] * (2 * SLOTS) + [full(NC, block_width)] * SLOTS,
+            in_specs=[full(*own.shape), full(*other.shape), full(*coarse.shape)],
             out_specs=[
                 pl.BlockSpec((rows, width), lambda i, info: (info[1] ^ i, 0)),
                 full(NC, width),
@@ -346,7 +346,7 @@
         ),
         compiler_params=pltpu.CompilerParams(vmem_limit_bytes=24 * 2**20),
         name="place_blocks",
-    )(info, *own, *other, *coarse)
+    )(info, own, other, coarse)
 
 
 def on_device_paired(points, fine_assign, fine_start, coarse_start, coarse_assign):
@@ -360,7 +360,6 @@
     owners = coarse_assign.reshape(2, 1, rows)
     info_of = lambda half: jnp.stack([here, half, offset + half * rows]).astype(jnp.int32)
     coarse = lax.dynamic_slice_in_dim(coarse_start, here * block_width, block_width, 1)
-    slot_rows = lambda array, slot: array[slot * (rows + TAIL) : (slot + 1) * (rows + TAIL)]
 
     def renew(coarse, coarse_sum):
         return (coarse_sum[:NC] + prior_weight * coarse) / (
@@ -376,43 +375,36 @@
         info_of(core), points, fine_assign, fine_start, squares, seen
     )
 
-    def exchange(held, sibling):
-        outgoing = [slot_rows(held, s) + slot_rows(sibling, s) for s in range(1, SLOTS)]
-        over_xy = swap(outgoing[2], ACROSS_X | ACROSS_Y)
-        return swap(outgoing[0], ACROSS_X), swap(outgoing[1], ACROSS_Y), over_xy
-
-    incoming = exchange(held, sibling)
+    received = trade(held + sibling)
     owner = lax.dynamic_index_in_dim(owners, core, 0, keepdims=False)
-    fine, coarse_part = refine_half(held, sibling, *incoming, owner, coarse)
-    own = spread(fine)
+    fine, coarse_part = refine_half(received, owner, coarse)
+    own = trade(fine)
     coarse_part = coarse_part + swap(coarse_part, CORE)
-    other = [swap(piece, CORE) for piece in own]
-
-    second_pass = functools.partial(
-        run_pass, pass_index=1, pieces=tuple(range(SLOTS)), rows=rows
-    )
-    own[0], coarse_part = lax.optimization_barrier((own[0], coarse_part))
+    other = swap(own, CORE)
+
+    second_pass = functools.partial(run_pass, pass_index=1, pieces=True, rows=rows)
+    own, coarse_part = lax.optimization_barrier((own, coarse_part))
     sent, seen = second_pass(info_of(core), points, fine_assign, own, squares, None)
     sibling = swap(sent, CORE)
     held, seen_second = second_pass(
         info_of(1 - core), points, fine_assign, other, squares, seen
     )
-    incoming = exchange(held, sibling)
+    received = trade(held + sibling)
     coarse = renew(coarse, add_over_cen(coarse_part))
+
+    owner = lax.dynamic_index_in_dim(owners, 1 - core, 0, keepdims=False)
+    fine, coarse_part = refine_half(received, owner, coarse)
+    own = trade(fine)
+    coarse_part = coarse_part + swap(coarse_part, CORE)
+    coarse = renew(coarse, add_over_cen(coarse_part))
+    other = swap(own, CORE)
+    coarse = trade(jnp.broadcast_to(coarse, (SLOTS,) + coarse.shape))
+    fine_now, coarse_now = place(info_of(1 - core), own, other, coarse)
 
     seen = jnp.concatenate([seen_first, seen_second], 0)
     others = [swap(seen, bit, "cen") for bit in range(1, lax.axis_size("cen"))]
     seen = functools.reduce(jnp.minimum, others, seen)
     gaps = (seen[0::2] - seen[1::2]) / math.sqrt(width)
-
-    owner = lax.dynamic_index_in_dim(owners, 1 - core, 0, keepdims=False)
-    owner, gaps = lax.optimization_barrier((owner, gaps))
-    fine, coarse_part = refine_half(held, sibling, *incoming, owner, coarse)
-    own = spread(fine)
-    coarse_part = coarse_part + swap(coarse_part, CORE)
-    coarse = renew(coarse, add_over_cen(coarse_part))
-    other = [swap(piece, CORE) for piece in own]
-    fine_now, coarse_now = place(info_of(1 - core), own, other, spread(coarse))
     return (fine_now, coarse_now, gaps)
 
 

time: 157 us -> 150 us (0.955)
  waiting for transfers between devices: 60.2 us -> 52.9 us
  Pallas kernels: 50.8 us -> 53.2 us
  starting transfers between devices: 35.1 us -> 32.7 us
    ppermute x36 -> x15, waiting for transfers between devices: 60.2 us -> 12.6 us  [swap(): return lax.ppermute(value, axis, [(i, i ^ bit) for i in range(size)])]
    all_to_all x0 -> x5, waiting for transfers between devices: none -> 40.3 us  [trade(): return lax.all_to_all(value, 'pts', 0, 0, axis_index_groups=groups)]
    ppermute x36 -> x15, starting transfers between devices: 35.1 us -> 13.9 us  [swap(): return lax.ppermute(value, axis, [(i, i ^ bit) for i in range(size)])]
    all_to_all x0 -> x5, starting transfers between devices: none -> 18.8 us  [trade(): return lax.all_to_all(value, 'pts', 0, 0, axis_index_groups=groups)]
  transfers between devices with their start and end apart: 36 -> 20, of which waited for: 20 -> 10; matrix products, arithmetic and copies ran while one was open for 3% -> 1% of each run, Pallas kernels for 21% -> 23%
where the time goes in v3:
time: 150 us; the launch traced here: 149 us
  Pallas kernels  53.2 us (35%)
  waiting for transfers between devices  52.9 us (35%)
  starting transfers between devices  32.7 us (22%)
  other arithmetic  6.31 us (4%)
  local copies, waits for them, and re-layouts  2.93 us (2%)
    pallas_call x4, Pallas kernels, run_pass(): pl.pallas_call(body, out_shape=[jax.ShapeDtypeStruct(shape, jnp.float32)...  48 us
    all_to_all x5, waiting for transfers between devices, trade(): return lax.all_to_all(value, 'pts', 0, 0, axis_index_groups=groups)  40.3 us
    all_to_all x5, starting transfers between devices, trade(): return lax.all_to_all(value, 'pts', 0, 0, axis_index_groups=groups)  18.8 us
    ppermute x15, starting transfers between devices, swap(): return lax.ppermute(value, axis, [(i, i ^ bit) for i in range(size)])  13.9 us
    ppermute x15, waiting for transfers between devices, swap(): return lax.ppermute(value, axis, [(i, i ^ bit) for i in range(size)])  12.6 us
    add x2, other arithmetic, on_device_paired(): received = trade(held + sibling)  4.71 us
    pallas_call x2, Pallas kernels, refine_half(): pl.pallas_call(refine_body, grid=(1,), out_shape=[jax.ShapeDtypeStruct((S...  3.08 us
  transfers between devices with their start and end apart: 20, of which 10 were waited for; matrix products, arithmetic and copies ran while one was open for 1% of the time, Pallas kernels for 23%

profile of v3, /device:TPU:0, one launch (start us, length us, event | category | flops | bytes accessed | tf_op | source)
XLA Modules:
  0.0 148.9 jit_solution(18118419895845110574)
XLA Ops:
  0.6 0.6 pad_add_fusion
  1.3 14.1 %energies_and_sums_00.1 = (f32[4,264,256]{2,1,0:T(8,128)}, f32[2,4096]{1,0:T(2,128)}, f32[1,4096]{1,0:T(1,128)}) custom-call(s32[3]{0:T(128)} %get-tuple-element.39.info, bf16[4096,1024]{1,0:T(8,128)(2,1)} %points.7, s32[2,4096]{1,0:T(2,128)} %assign.7, f32[512,1024]{1,0:T(8,128)} %refs_0_.3), custom_call_target="tpu_custom_call" | custom-call | flops 4294967296 | bytes 8388608 | tf_op jit(solution)/shard_map/energies_and_sums_00/pallas_call | solution.py:225
  15.4 0.5 collective-permute-start
  15.9 11.3 %energies_and_sums_01.1 = (f32[4,264,256]{2,1,0:T(8,128)}, f32[2,4096]{1,0:T(2,128)}) custom-call(s32[3]{0:T(128)} %get-tuple-element.40.info, bf16[4096,1024]{1,0:T(8,128)(2,1)} %points.7, s32[2,4096]{1,0:T(2,128)} %assign.7, f32[512,1024]{1,0:T(8,128)} %refs_0_.3, f32[1,4096]{1,0:T(1,128)} %get-tuple-element.20.refs_1_.refs_4_, ...), custom_call_target="tpu_custom_call" | custom-call | flops 4294967296 | bytes 8388608 | tf_op jit(solution)/shard_map/energies_and_sums_01/pallas_call | solution.py:225
  27.2 0.0 collective-permute-done
  27.2 2.4 %add.78 = f32[4,264,256]{2,1,0:T(8,128)} add(f32[4,264,256]{2,1,0:T(8,128)} %get-tuple-element.22, f32[4,264,256]{2,1,0:T(8,128)S(1)} %collective-permute-done) | non-fusion elementwise | flops 270336 | bytes 3244032 | tf_op jit(solution)/shard_map/add | solution.py:378
  29.6 4.8 %all-to-all-start = ((f32[4,264,256]{2,1,0:T(8,128)}), f32[4,264,256]{2,1,0:T(8,128)S(1)}, u32[]{:S(2)}, u32[]{:S(2)}) async-start(f32[4,264,256]{2,1,0:T(8,128)} %add.78), calls=%async_computation | async-start | bytes 2162688 | tf_op jit(solution)/shard_map/all_to_all | solution.py:303
  34.4 0.0 copy-done.5
  34.4 0.0 copy-done.4
  34.5 14.6 %all-to-all-done.received = f32[4,264,256]{2,1,0:T(8,128)S(1)} async-done(((f32[4,264,256]{2,1,0:T(8,128)}), f32[4,264,256]{2,1,0:T(8,128)S(1)}, u32[]{:S(2)}, u32[]{:S(2)}) %all-to-all-start) | async-done | bytes 1081376 | tf_op jit(solution)/shard_map/all_to_all | solution.py:303
  49.1 1.5 %refine_half.2 = (f32[4,256,256]{2,1,0:T(8,128)}, f32[72,256]{1,0:T(8,128)S(1)}) custom-call(f32[4,264,256]{2,1,0:T(8,128)S(1)} %all-to-all-done.received, s32[1,256]{1,0:T(1,128)S(1)} %get-tuple-element.38.owner, f32[64,256]{1,0:T(8,128)S(1)} %constant_dynamic-slice_fusion.coarse), custom_call_target="tpu_custom_call" | custom-call | tf_op jit(solution)/shard_map/refine_half/pallas_call | solution.py:286
  50.6 3.5 %all-to-all-start.1 = ((f32[4,256,256]{2,1,0:T(8,128)}), f32[4,256,256]{2,1,0:T(8,128)S(1)}, u32[]{:S(2)}, u32[]{:S(2)}) async-start(f32[4,256,256]{2,1,0:T(8,128)} %get-tuple-element.24), calls=%async_computation.1 | async-start | bytes 2097152 | tf_op jit(solution)/shard_map/all_to_all | solution.py:303
  54.2 0.1 collective-permute-start.2
  54.2 1.3 collective-permute-done.2
  55.5 12.1 %all-to-all-done.1.refs_0_.refs_1_.refs_2_.refs_3_ = f32[4,256,256]{2,1,0:T(8,128)S(1)} async-done(((f32[4,256,256]{2,1,0:T(8,128)}), f32[4,256,256]{2,1,0:T(8,128)S(1)}, u32[]{:S(2)}, u32[]{:S(2)}) %all-to-all-start.1) | async-done | bytes 1048608 | tf_op jit(solution)/shard_map/all_to_all | solution.py:303
  67.6 0.0 collective-permute-start.1
  67.6 1.0 copy-done.1
  68.6 11.3 %energies_and_sums_10.1 = (f32[4,264,256]{2,1,0:T(8,128)}, f32[2,4096]{1,0:T(2,128)}) custom-call(s32[3]{0:T(128)} %get-tuple-element.40.info, bf16[4096,1024]{1,0:T(8,128)(2,1)} %points.7, s32[2,4096]{1,0:T(2,128)} %assign.7, f32[4,256,256]{2,1,0:T(8,128)} %copy-done.1, f32[4,256,256]{2,1,0:T(8,128)} %copy-done.1, f32[4,256,256]{2,1,0:T(8,128)} %copy-done.1, ...), custom_call_target="tpu_custom_call" | custom-call | flops 4294967296 | bytes 8388608 | tf_op jit(solution)/shard_map/energies_and_sums_10/pallas_call | solution.py:225
  79.9 0.1 collective-permute-start.3
  79.9 0.0 collective-permute-done.1.refs_0_.refs_1_.refs_2_.refs_3_
  80.0 0.0 copy-start.6
  80.0 1.0 copy-done.6
  80.9 11.3 %energies_and_sums_11.1 = (f32[4,264,256]{2,1,0:T(8,128)}, f32[2,4096]{1,0:T(2,128)}) custom-call(s32[3]{0:T(128)} %get-tuple-element.39.info, bf16[4096,1024]{1,0:T(8,128)(2,1)} %points.7, s32[2,4096]{1,0:T(2,128)} %assign.7, f32[4,256,256]{2,1,0:T(8,128)} %copy-done.6, f32[4,256,256]{2,1,0:T(8,128)} %copy-done.6, f32[4,256,256]{2,1,0:T(8,128)} %copy-done.6, ...), custom_call_target="tpu_custom_call" | custom-call | flops 4294967296 | bytes 8388608 | tf_op jit(solution)/shard_map/energies_and_sums_11/pallas_call | solution.py:225
  92.2 0.0 collective-permute-done.3
  92.3 2.4 %add.82 = f32[4,264,256]{2,1,0:T(8,128)} add(f32[4,264,256]{2,1,0:T(8,128)} %get-tuple-element.28, f32[4,264,256]{2,1,0:T(8,128)S(1)} %collective-permute-done.3) | non-fusion elementwise | flops 270336 | bytes 3244032 | tf_op jit(solution)/shard_map/add | solution.py:392
  94.6 3.5 %all-to-all-start.2 = ((f32[4,264,256]{2,1,0:T(8,128)}), f32[4,264,256]{2,1,0:T(8,128)S(1)}, u32[]{:S(2)}, u32[]{:S(2)}) async-start(f32[4,264,256]{2,1,0:T(8,128)} %add.82), calls=%async_computation.2 | async-start | bytes 2162688 | tf_op jit(solution)/shard_map/all_to_all | solution.py:303
  98.1 0.0 copy-start.2
  98.2 3.8 %collective-permute-start.6 = (f32[72,256]{1,0:T(8,128)S(1)}, f32[72,256]{1,0:T(8,128)S(1)}, u32[]{:S(2)}, u32[]{:S(2)}) collective-permute-start(f32[72,256]{1,0:T(8,128)S(1)} %add.81), channel_id=1, source_target_pairs={{0,3},{1,2},{2,1},{3,0},{4,7},{5,6},{6,5},{7,4},{8,11},{9,10},{10,... | collective-permute-start | bytes 221192 | tf_op jit(solution)/shard_map/ppermute | solution.py:89
  101.9 0.0 collective-permute-start.5
  101.9 0.7 collective-permute-start.4
  102.6 2.6 %collective-permute-done.6 = f32[72,256]{1,0:T(8,128)S(1)} collective-permute-done((f32[72,256]{1,0:T(8,128)S(1)}, f32[72,256]{1,0:T(8,128)S(1)}, u32[]{:S(2)}, u32[]{:S(2)}) %collective-permute-start.6) | collective-permute-done | bytes 73760 | tf_op jit(solution)/shard_map/ppermute | solution.py:89
  105.2 3.5 %collective-permute-done.5 = f32[72,256]{1,0:T(8,128)S(1)} collective-permute-done((f32[72,256]{1,0:T(8,128)S(1)}, f32[72,256]{1,0:T(8,128)S(1)}, u32[]{:S(2)}, u32[]{:S(2)}) %collective-permute-start.5) | collective-permute-done | bytes 73760 | tf_op jit(solution)/shard_map/ppermute | solution.py:89
  108.8 0.0 collective-permute-done.4
  108.8 0.1 fusion.1.coarse
  108.9 4.1 %all-to-all-done.2.received = f32[4,264,256]{2,1,0:T(8,128)S(1)} async-done(((f32[4,264,256]{2,1,0:T(8,128)}), f32[4,264,256]{2,1,0:T(8,128)S(1)}, u32[]{:S(2)}, u32[]{:S(2)}) %all-to-all-start.2) | async-done | bytes 1081376 | tf_op jit(solution)/shard_map/all_to_all | solution.py:303
  113.0 1.5 %refine_half.3 = (f32[4,256,256]{2,1,0:T(8,128)}, f32[72,256]{1,0:T(8,128)S(1)}) custom-call(f32[4,264,256]{2,1,0:T(8,128)S(1)} %all-to-all-done.2.received, s32[1,256]{1,0:T(1,128)S(1)} %get-tuple-element.37.owner, f32[64,256]{1,0:T(8,128)S(1)} %fusion.1.coarse), custom_call_target="tpu_custom_call" | custom-call | tf_op jit(solution)/shard_map/refine_half/pallas_call | solution.py:286
  114.6 0.0 collective-permute-start.8
  114.6 0.0 copy-done.3
  114.6 2.8 %collective-permute-start.13 = (f32[4,4096]{1,0:T(4,128)S(1)}, f32[4,4096]{1,0:T(4,128)S(1)}, u32[]{:S(2)}, u32[]{:S(2)}) collective-permute-start(f32[4,4096]{1,0:T(4,128)S(1)} %pad_maximum_fusion), channel_id=1, source_target_pairs={{0,2},{1,3},{2,0},{3,1},{4,6},{5,7},{6,4},{7,5},{8,10},{9,11},{10,... | collective-permute-start | bytes 196616 | tf_op jit(solution)/shard_map/ppermute | solution.py:89
  117.4 1.3 collective-permute-start.14
  118.7 0.2 collective-permute-start.12
  119.0 3.5 %all-to-all-start.3 = ((f32[4,256,256]{2,1,0:T(8,128)}), f32[4,256,256]{2,1,0:T(8,128)S(1)}, u32[]{:S(2)}, u32[]{:S(2)}) async-start(f32[4,256,256]{2,1,0:T(8,128)} %get-tuple-element.31), calls=%async_computation.3 | async-start | bytes 2097152 | tf_op jit(solution)/shard_map/all_to_all | solution.py:303
  122.5 0.0 collective-permute-done.8
  122.5 3.0 %collective-permute-start.11 = (f32[72,256]{1,0:T(8,128)S(1)}, f32[72,256]{1,0:T(8,128)S(1)}, u32[]{:S(2)}, u32[]{:S(2)}) collective-permute-start(f32[72,256]{1,0:T(8,128)S(1)} %add.90), channel_id=1, source_target_pairs={{0,3},{1,2},{2,1},{3,0},{4,7},{5,6},{6,5},{7,4},{8,11},{9,10},{10,... | collective-permute-start | bytes 221192 | tf_op jit(solution)/shard_map/ppermute | solution.py:89
  125.5 0.3 collective-permute-start.10
  125.9 0.0 collective-permute-done.13
  125.9 1.1 collective-permute-start.9
  127.0 0.0 collective-permute-done.14
  127.0 0.0 collective-permute-done.12
  127.0 0.1 minimum_minimum_fusion
  127.1 0.1 slice.23
  127.2 0.1 slice.22
  127.3 1.9 %collective-permute-done.11 = f32[72,256]{1,0:T(8,128)S(1)} collective-permute-done((f32[72,256]{1,0:T(8,128)S(1)}, f32[72,256]{1,0:T(8,128)S(1)}, u32[]{:S(2)}, u32[]{:S(2)}) %collective-permute-start.11) | collective-permute-done | bytes 73760 | tf_op jit(solution)/shard_map/ppermute | solution.py:89
  129.2 3.2 %collective-permute-done.10 = f32[72,256]{1,0:T(8,128)S(1)} collective-permute-done((f32[72,256]{1,0:T(8,128)S(1)}, f32[72,256]{1,0:T(8,128)S(1)}, u32[]{:S(2)}, u32[]{:S(2)}) %collective-permute-start.10) | collective-permute-done | bytes 73760 | tf_op jit(solution)/shard_map/ppermute | solution.py:89
  132.5 0.0 collective-permute-done.9
  132.5 4.0 %all-to-all-done.3.own = f32[4,256,256]{2,1,0:T(8,128)S(1)} async-done(((f32[4,256,256]{2,1,0:T(8,128)}), f32[4,256,256]{2,1,0:T(8,128)S(1)}, u32[]{:S(2)}, u32[]{:S(2)}) %all-to-all-start.3) | async-done | bytes 1048608 | tf_op jit(solution)/shard_map/all_to_all | solution.py:303
  136.5 0.0 collective-permute-start.7
  136.5 0.1 fusion
  136.6 0.7 broadcast_in_dim.2
  137.3 3.4 %all-to-all-start.4 = ((f32[4,64,256]{2,1,0:T(8,128)}), f32[4,64,256]{2,1,0:T(8,128)S(1)}, u32[]{:S(2)}, u32[]{:S(2)}) async-start(f32[4,64,256]{2,1,0:T(8,128)} %broadcast_in_dim.2), calls=%async_computation.4 | async-start | bytes 524288 | tf_op jit(solution)/shard_map/all_to_all | solution.py:303
  140.7 0.6 subtract_multiply_fusion
  141.3 5.5 %all-to-all-done.4.coarse = f32[4,64,256]{2,1,0:T(8,128)S(1)} async-done(((f32[4,64,256]{2,1,0:T(8,128)}), f32[4,64,256]{2,1,0:T(8,128)S(1)}, u32[]{:S(2)}, u32[]{:S(2)}) %all-to-all-start.4) | async-done | bytes 262176 | tf_op jit(solution)/shard_map/all_to_all | solution.py:303
  146.8 0.0 collective-permute-done.7.other
  146.8 2.1 %place_blocks.1 = (f32[512,1024]{1,0:T(8,128)}, f32[64,1024]{1,0:T(8,128)}) custom-call(s32[3]{0:T(128)S(1)} %copy-done, f32[4,256,256]{2,1,0:T(8,128)S(1)} %all-to-all-done.3.own, f32[4,256,256]{2,1,0:T(8,128)S(1)} %collective-permute-done.7.other, f32[4,64,256]{2,1,0:T(8,128)S(1)} %all-to-all-done.4.coarse), custom_call_target="tpu_custom_call" | custom-call | tf_op jit(solution)/shard_map/place_blocks/pallas_call | solution.py:332
  (16 shorter events, 0.1 us)
Async XLA Ops:
  15.4 11.9 %collective-permute-start = (f32[4,264,256]{2,1,0:T(8,128)}, f32[4,264,256]{2,1,0:T(8,128)S(1)}, u32[]{:S(2)}, u32[]{:S(2)}) collective-permute-start(f32[4,264,256]{2,1,0:T(8,128)} %get-tuple-element.23), channel_id=1, source_target_pairs={{0,4},{4,0},{8,12},{12,8},{16,20},{20,16},{24,28},{28,24},{1,5},{5... | collective-permute-start | bytes 3244040 | tf_op jit(solution)/shard_map/ppermute | solution.py:89
  29.6 4.9 %copy-start.5 = (s32[512]{0:T(512)S(1)}, s32[512]{0:T(512)}, u32[]{:S(2)}) copy-start(s32[512]{0:T(512)} %param.9) | copy-start | bytes 6148
  29.6 4.9 %copy-start.4 = (f32[64,1024]{1,0:T(8,128)S(1)}, f32[64,1024]{1,0:T(8,128)}, u32[]{:S(2)}) copy-start(f32[64,1024]{1,0:T(8,128)} %param.8) | copy-start | bytes 786436
  29.6 19.5 %all-to-all-start = ((f32[4,264,256]{2,1,0:T(8,128)}), f32[4,264,256]{2,1,0:T(8,128)S(1)}, u32[]{:S(2)}, u32[]{:S(2)}) async-start(f32[4,264,256]{2,1,0:T(8,128)} %add.78), calls=%async_computation | async-start | bytes 2162688 | tf_op jit(solution)/shard_map/all_to_all | solution.py:303
  50.6 17.0 %all-to-all-start.1 = ((f32[4,256,256]{2,1,0:T(8,128)}), f32[4,256,256]{2,1,0:T(8,128)S(1)}, u32[]{:S(2)}, u32[]{:S(2)}) async-start(f32[4,256,256]{2,1,0:T(8,128)} %get-tuple-element.24), calls=%async_computation.1 | async-start | bytes 2097152 | tf_op jit(solution)/shard_map/all_to_all | solution.py:303
  54.2 1.3 collective-permute-start.2
  67.6 1.0 copy-start.1
  67.6 12.3 %collective-permute-start.1 = (f32[4,256,256]{2,1,0:T(8,128)S(1)}, f32[4,256,256]{2,1,0:T(8,128)S(1)}, u32[]{:S(2)}, u32[]{:S(2)}) collective-permute-start(f32[4,256,256]{2,1,0:T(8,128)S(1)} %all-to-all-done.1.refs_0_.refs_1_.refs_2_.refs_3_), channel_id=1, source_target_pairs={{0,4},{4,0},{8,12},{12,8},{16,20},{20,16},{24,28},{28,24},{1,5},{5... | collective-permute-start | bytes 3145736 | tf_op jit(solution)/shard_map/ppermute | solution.py:89
  79.9 12.4 %collective-permute-start.3 = (f32[4,264,256]{2,1,0:T(8,128)}, f32[4,264,256]{2,1,0:T(8,128)S(1)}, u32[]{:S(2)}, u32[]{:S(2)}) collective-permute-start(f32[4,264,256]{2,1,0:T(8,128)} %get-tuple-element.29), channel_id=1, source_target_pairs={{0,4},{4,0},{8,12},{12,8},{16,20},{20,16},{24,28},{28,24},{1,5},{5... | collective-permute-start | bytes 3244040 | tf_op jit(solution)/shard_map/ppermute | solution.py:89
  80.0 1.0 copy-start.6
  94.6 18.4 %all-to-all-start.2 = ((f32[4,264,256]{2,1,0:T(8,128)}), f32[4,264,256]{2,1,0:T(8,128)S(1)}, u32[]{:S(2)}, u32[]{:S(2)}) async-start(f32[4,264,256]{2,1,0:T(8,128)} %add.82), calls=%async_computation.2 | async-start | bytes 2162688 | tf_op jit(solution)/shard_map/all_to_all | solution.py:303
  98.1 16.4 %copy-start.2 = (f32[2,4096]{1,0:T(2,128)S(1)}, f32[2,4096]{1,0:T(2,128)}, u32[]{:S(2)}) copy-start(f32[2,4096]{1,0:T(2,128)} %get-tuple-element.35) | copy-start | bytes 98308
  98.2 16.4 %copy-start.3 = (f32[2,4096]{1,0:T(2,128)S(1)}, f32[2,4096]{1,0:T(2,128)}, u32[]{:S(2)}) copy-start(f32[2,4096]{1,0:T(2,128)} %get-tuple-element.36) | copy-start | bytes 98308
  98.2 7.1 %collective-permute-start.6 = (f32[72,256]{1,0:T(8,128)S(1)}, f32[72,256]{1,0:T(8,128)S(1)}, u32[]{:S(2)}, u32[]{:S(2)}) collective-permute-start(f32[72,256]{1,0:T(8,128)S(1)} %add.81), channel_id=1, source_target_pairs={{0,3},{1,2},{2,1},{3,0},{4,7},{5,6},{6,5},{7,4},{8,11},{9,10},{10,... | collective-permute-start | bytes 221192 | tf_op jit(solution)/shard_map/ppermute | solution.py:89
  101.9 6.8 %collective-permute-start.5 = (f32[72,256]{1,0:T(8,128)S(1)}, f32[72,256]{1,0:T(8,128)S(1)}, u32[]{:S(2)}, u32[]{:S(2)}) collective-permute-start(f32[72,256]{1,0:T(8,128)S(1)} %add.81), channel_id=1, source_target_pairs={{0,2},{1,3},{2,0},{3,1},{4,6},{5,7},{6,4},{7,5},{8,10},{9,11},{10,... | collective-permute-start | bytes 221192 | tf_op jit(solution)/shard_map/ppermute | solution.py:89
  101.9 6.8 %collective-permute-start.4 = (f32[72,256]{1,0:T(8,128)S(1)}, f32[72,256]{1,0:T(8,128)S(1)}, u32[]{:S(2)}, u32[]{:S(2)}) collective-permute-start(f32[72,256]{1,0:T(8,128)S(1)} %add.81), channel_id=1, source_target_pairs={{0,1},{1,0},{2,3},{3,2},{4,5},{5,4},{6,7},{7,6},{8,9},{9,8},{10,11... | collective-permute-start | bytes 221192 | tf_op jit(solution)/shard_map/ppermute | solution.py:89
  114.6 7.9 %collective-permute-start.8 = (f32[72,256]{1,0:T(8,128)S(1)}, f32[72,256]{1,0:T(8,128)S(1)}, u32[]{:S(2)}, u32[]{:S(2)}) collective-permute-start(f32[72,256]{1,0:T(8,128)S(1)} %get-tuple-element.32), channel_id=1, source_target_pairs={{0,4},{4,0},{8,12},{12,8},{16,20},{20,16},{24,28},{28,24},{1,5},{5... | collective-permute-start | bytes 221192 | tf_op jit(solution)/shard_map/ppermute | solution.py:89
  114.6 11.2 %collective-permute-start.13 = (f32[4,4096]{1,0:T(4,128)S(1)}, f32[4,4096]{1,0:T(4,128)S(1)}, u32[]{:S(2)}, u32[]{:S(2)}) collective-permute-start(f32[4,4096]{1,0:T(4,128)S(1)} %pad_maximum_fusion), channel_id=1, source_target_pairs={{0,2},{1,3},{2,0},{3,1},{4,6},{5,7},{6,4},{7,5},{8,10},{9,11},{10,... | collective-permute-start | bytes 196616 | tf_op jit(solution)/shard_map/ppermute | solution.py:89
  117.4 9.6 %collective-permute-start.14 = (f32[4,4096]{1,0:T(4,128)S(1)}, f32[4,4096]{1,0:T(4,128)S(1)}, u32[]{:S(2)}, u32[]{:S(2)}) collective-permute-start(f32[4,4096]{1,0:T(4,128)S(1)} %pad_maximum_fusion), channel_id=1, source_target_pairs={{0,3},{1,2},{2,1},{3,0},{4,7},{5,6},{6,5},{7,4},{8,11},{9,10},{10,... | collective-permute-start | bytes 196616 | tf_op jit(solution)/shard_map/ppermute | solution.py:89
  118.7 8.3 %collective-permute-start.12 = (f32[4,4096]{1,0:T(4,128)S(1)}, f32[4,4096]{1,0:T(4,128)S(1)}, u32[]{:S(2)}, u32[]{:S(2)}) collective-permute-start(f32[4,4096]{1,0:T(4,128)S(1)} %pad_maximum_fusion), channel_id=1, source_target_pairs={{0,1},{1,0},{2,3},{3,2},{4,5},{5,4},{6,7},{7,6},{8,9},{9,8},{10,11... | collective-permute-start | bytes 196616 | tf_op jit(solution)/shard_map/ppermute | solution.py:89
  119.0 17.5 %all-to-all-start.3 = ((f32[4,256,256]{2,1,0:T(8,128)}), f32[4,256,256]{2,1,0:T(8,128)S(1)}, u32[]{:S(2)}, u32[]{:S(2)}) async-start(f32[4,256,256]{2,1,0:T(8,128)} %get-tuple-element.31), calls=%async_computation.3 | async-start | bytes 2097152 | tf_op jit(solution)/shard_map/all_to_all | solution.py:303
  122.5 24.3 %copy-start = (s32[3]{0:T(128)S(1)}, s32[3]{0:T(128)}, u32[]{:S(2)}) copy-start(s32[3]{0:T(128)} %get-tuple-element.39.info) | copy-start | bytes 40
  122.5 6.7 %collective-permute-start.11 = (f32[72,256]{1,0:T(8,128)S(1)}, f32[72,256]{1,0:T(8,128)S(1)}, u32[]{:S(2)}, u32[]{:S(2)}) collective-permute-start(f32[72,256]{1,0:T(8,128)S(1)} %add.90), channel_id=1, source_target_pairs={{0,3},{1,2},{2,1},{3,0},{4,7},{5,6},{6,5},{7,4},{8,11},{9,10},{10,... | collective-permute-start | bytes 221192 | tf_op jit(solution)/shard_map/ppermute | solution.py:89
  125.5 6.9 %collective-permute-start.10 = (f32[72,256]{1,0:T(8,128)S(1)}, f32[72,256]{1,0:T(8,128)S(1)}, u32[]{:S(2)}, u32[]{:S(2)}) collective-permute-start(f32[72,256]{1,0:T(8,128)S(1)} %add.90), channel_id=1, source_target_pairs={{0,2},{1,3},{2,0},{3,1},{4,6},{5,7},{6,4},{7,5},{8,10},{9,11},{10,... | collective-permute-start | bytes 221192 | tf_op jit(solution)/shard_map/ppermute | solution.py:89
  125.9 6.6 %collective-permute-start.9 = (f32[72,256]{1,0:T(8,128)S(1)}, f32[72,256]{1,0:T(8,128)S(1)}, u32[]{:S(2)}, u32[]{:S(2)}) collective-permute-start(f32[72,256]{1,0:T(8,128)S(1)} %add.90), channel_id=1, source_target_pairs={{0,1},{1,0},{2,3},{3,2},{4,5},{5,4},{6,7},{7,6},{8,9},{9,8},{10,11... | collective-permute-start | bytes 221192 | tf_op jit(solution)/shard_map/ppermute | solution.py:89
  136.5 10.4 %collective-permute-start.7 = (f32[4,256,256]{2,1,0:T(8,128)S(1)}, f32[4,256,256]{2,1,0:T(8,128)S(1)}, u32[]{:S(2)}, u32[]{:S(2)}) collective-permute-start(f32[4,256,256]{2,1,0:T(8,128)S(1)} %all-to-all-done.3.own), channel_id=1, source_target_pairs={{0,4},{4,0},{8,12},{12,8},{16,20},{20,16},{24,28},{28,24},{1,5},{5... | collective-permute-start | bytes 3145736 | tf_op jit(solution)/shard_map/ppermute | solution.py:89
  137.3 9.5 %all-to-all-start.4 = ((f32[4,64,256]{2,1,0:T(8,128)}), f32[4,64,256]{2,1,0:T(8,128)S(1)}, u32[]{:S(2)}, u32[]{:S(2)}) async-start(f32[4,64,256]{2,1,0:T(8,128)} %broadcast_in_dim.2), calls=%async_computation.4 | async-start | bytes 524288 | tf_op jit(solution)/shard_map/all_to_all | solution.py:303

commit v4 on v3

v4 whole, which is shorter than its diff:
```python
import functools
import math

import jax
import jax.numpy as jnp
from jax import lax
from jax.experimental import pallas as pl
from jax.experimental.pallas import tpu as pltpu
from jax.sharding import PartitionSpec as P

NC = 64
PASSES = 2
FAR = 3.0e38

prior_weight = 4.0
HIGHEST = lax.Precision.HIGHEST


def refine(totals, counts, coarse_cols, coarse_table):
    lookup = jnp.dot(coarse_table, coarse_cols, precision=HIGHEST)
    fine_next = (totals + prior_weight * lookup) / (counts + prior_weight)[:, None]
    coarse_part = lax.dot_general(
        coarse_table,
        counts[:, None] * fine_next,
        (((0,), (0,)), ((), ())),
        precision=HIGHEST,
    )
    coarse_weight = jnp.sum(coarse_table * counts[:, None], axis=0)
    return (fine_next, coarse_part, coarse_weight)


def on_device_any(points, fine_assign, fine_start, coarse_start, coarse_assign):
    width = points.shape[1]
    local_count = fine_start.shape[0]
    offset = lax.axis_index("cen") * local_count
    columns = jnp.arange(local_count, dtype=jnp.int32)
    coarse_table = (coarse_assign[:, None] == jnp.arange(NC, dtype=jnp.int32)[None, :]).astype(
        jnp.float32
    )
    point_values = points.astype(jnp.float32)
    squares = jnp.sum(point_values * point_values, axis=1)
    fine_now = fine_start
    coarse_now = coarse_start
    gap_rows = []
    for pass_index in range(PASSES):
        member = (fine_assign[pass_index] - offset)[:, None] == columns[None, :]
        products = jnp.dot(
            points, fine_now.astype(jnp.bfloat16).T, preferred_element_type=jnp.float32
        )
        energy = jnp.sum(fine_now * fine_now, axis=1)[None, :] - 2.0 * products
        picked_local = jnp.sum(jnp.where(member, energy, 0.0), axis=1)
        nearest_local = jnp.min(energy, axis=1)
        picked = lax.psum(picked_local, "cen")
        nearest = lax.pmin(nearest_local, "cen")
        gap_rows.append((picked - nearest) / math.sqrt(width))
        weights = 1.0 / (1.0 + (squares + picked) / width)
        scaled = (point_values * weights[:, None]).astype(jnp.bfloat16)
        partial_sums = lax.dot_general(
            member.astype(jnp.bfloat16),
            scaled,
            (((0,), (0,)), ((), ())),
            preferred_element_type=jnp.float32,
        )
        partial_weights = jnp.sum(jnp.where(member, weights[:, None], 0.0), axis=0)
        share_width = width // lax.axis_size("pts")
        start = lax.axis_index("pts") * share_width
        shares = lax.psum_scatter(partial_sums, "pts", scatter_dimension=1, tiled=True)
        counts = lax.psum(partial_weights, "pts")
        coarse_cols = lax.dynamic_slice_in_dim(coarse_now, start, share_width, 1)
        fine_share, coarse_part, coarse_weight = refine(shares, counts, coarse_cols, coarse_table)
        coarse_sum, coarse_count = lax.psum((coarse_part, coarse_weight), "cen")
        coarse_share = (coarse_sum + prior_weight * coarse_cols) / (coarse_count + prior_weight)[
            :, None
        ]
        fine_now, coarse_now = (
            lax.all_gather(fine_share, "pts", axis=1, tiled=True),
            lax.all_gather(coarse_share, "pts", axis=1, tiled=True),
        )
    return (fine_now, coarse_now, jnp.stack(gap_rows))


CORE, ACROSS_X, ACROSS_Y = 1, 2, 4
SLOTS = 4
TAIL = 8


def swap(value, bit, axis="pts"):
    size = lax.axis_size(axis)
    return lax.ppermute(value, axis, [(i, i ^ bit) for i in range(size)])


def full(*shape):
    return pl.BlockSpec(shape, lambda i, info: (0,) * len(shape))


def as_column(row, rows):
    return jnp.broadcast_to(row, (128, rows)).T


def pass_body(info, points, assign, fine, *refs, pass_index, slots, first, chained, tile):
    refs = list(refs)
    squares_in = None if first else refs.pop(0)
    seen_in = refs.pop(0) if chained else None
    payload, seen = refs.pop(0), refs.pop(0)
    squares_out, kept = (refs.pop(0), refs.pop(0)) if first else (None, points)
    low, sums, tallies, even, odd, scaled = refs[:6]
    rows, width = low.shape
    block_width = width // SLOTS
    here, base = info[0], info[2]
    tiles = points.shape[0] // tile

    def span(i):
        return pl.ds(pl.multiple_of(i * tile, tile), tile)

    def column_of(slot):
        return pl.ds(pl.multiple_of((here ^ slot) * block_width, block_width), block_width)

    def load(i):
        return pltpu.make_async_copy(points.at[span(i)], kept.at[span(i)], refs[6].at[i])

    if first:

        @pl.loop(0, tiles)
        def _(i):
            load(i).start()

    if slots:
        norm = jnp.zeros((rows, 1), jnp.float32)
        for slot in range(SLOTS):
            block = fine[slot]
            norm = norm + jnp.sum(block * block, axis=1, keepdims=True)
            low[:, column_of(slot)] = (-2.0 * block).astype(jnp.bfloat16)
    else:
        block = fine[...]
        norm = jnp.sum(block * block, axis=1, keepdims=True)
        low[...] = (-2.0 * block).astype(jnp.bfloat16)
    sums[...] = jnp.zeros_like(sums)
    tallies[...] = jnp.zeros_like(tallies)

    def multiply(i, target):
        target[...] = lax.dot_general(
            low[...], kept[span(i), :], (((1,), (1,)), ((), ())), preferred_element_type=jnp.float32
        )

    def collect(i, products):
        energy = norm + products[...]
        chosen = assign[pass_index : pass_index + 1, span(i)] - base
        member = lax.broadcasted_iota(jnp.int32, energy.shape, 0) == chosen
        picked = jnp.sum(jnp.where(member, energy, 0.0), axis=0, keepdims=True)
        nearest = jnp.min(energy, axis=0, keepdims=True)
        inside = (chosen >= 0) & (chosen < rows)
        picked_seen = jnp.where(inside, picked, FAR)
        if chained:
            picked_seen = jnp.minimum(picked_seen, seen_in[0:1, span(i)])
            nearest = jnp.minimum(nearest, seen_in[1:2, span(i)])
        seen[0:1, span(i)] = picked_seen
        seen[1:2, span(i)] = nearest
        if first:
            folded = jnp.zeros((tile, 128), jnp.float32)
            for lane in range(0, width, 128):
                values = kept[span(i), lane : lane + 128].astype(jnp.float32)
                folded = folded + values * values
            squares = jnp.sum(folded.T, axis=0, keepdims=True)
            squares_out[0:1, span(i)] = squares
        else:
            squares = squares_in[0:1, span(i)]
        weights = 1.0 / (1.0 + (squares + picked) / width)
        weighted = jnp.where(member, weights, 0.0)
        tally = tallies[...]
        for lane in range(0, tile, 128):
            tally = tally + weighted[:, lane : lane + 128]
        tallies[...] = tally
        factor = as_column(weights, tile)
        for lane in range(0, width, 128):
            values = kept[span(i), lane : lane + 128].astype(jnp.float32)
            scaled[:, lane : lane + 128] = (values * factor).astype(jnp.bfloat16)
        sums[...] += jnp.dot(
            member.astype(jnp.float32).astype(jnp.bfloat16),
            scaled[...],
            preferred_element_type=jnp.float32,
        )

    if first:
        load(0).wait()
    multiply(0, even)

    @pl.loop(0, tiles // 2)
    def _(pair):
        i = 2 * pair
        if first:
            load(i + 1).wait()

            @pl.when(i + 2 < tiles)
            def _():
                load(i + 2).wait()

        multiply(i + 1, odd)
        collect(i, even)
        multiply(jnp.minimum(i + 2, tiles - 1), even)
        collect(i + 1, odd)

    counts = jnp.broadcast_to(jnp.sum(tallies[...].T, axis=0, keepdims=True), (TAIL, rows))
    for slot in range(SLOTS):
        payload[slot, :rows, :] = sums[:, column_of(slot)]
        payload[slot, rows:, :] = counts


def run_pass(info, points, fine_assign, fine, squares, seen, *, pass_index, slots, rows):
    count, width = points.shape
    block_width = width // SLOTS
    tile = 512
    first = squares is None
    chained = seen is not None
    whole = pl.BlockSpec(memory_space=pltpu.VMEM)
    in_specs = [pl.BlockSpec(memory_space=pl.ANY) if first else whole, full(PASSES, count)]
    args = [
        pltpu.with_memory_space_constraint(points, pltpu.HBM if first else pltpu.VMEM),
        fine_assign,
    ]
    if slots:
        in_specs.append(full(SLOTS, rows, block_width))
    else:
        in_specs.append(pl.BlockSpec((rows, width), lambda i, info: (info[1], 0)))
    args.append(fine)
    if not first:
        in_specs.append(full(1, count))
        args.append(squares)
    if chained:
        in_specs.append(full(2, count))
        args.append(seen)
    shapes = [(SLOTS, rows + TAIL, block_width), (2, count)] + ([(1, count)] if first else [])
    out_shape = [jax.ShapeDtypeStruct(shape, jnp.float32) for shape in shapes]
    out_specs = [full(*shape) for shape in shapes]
    scratch = [
        pltpu.VMEM((rows, width), jnp.bfloat16),
        pltpu.VMEM((rows, width), jnp.float32),
        pltpu.VMEM((rows, 128), jnp.float32),
        pltpu.VMEM((rows, tile), jnp.float32),
        pltpu.VMEM((rows, tile), jnp.float32),
        pltpu.VMEM((tile, width), jnp.bfloat16),
    ]
    if first:
        out_shape.append(pltpu.VMEM(points.shape, points.dtype))
        out_specs.append(whole)
        scratch.append(pltpu.SemaphoreType.DMA((count // tile,)))
    body = functools.partial(
        pass_body,
        pass_index=pass_index,
        slots=slots,
        first=first,
        chained=chained,
        tile=tile,
    )
    return pl.pallas_call(
        body,
        out_shape=out_shape,
        grid_spec=pltpu.PrefetchScalarGridSpec(
            num_scalar_prefetch=1,
            grid=(1,),
            in_specs=in_specs,
            out_specs=out_specs,
            scratch_shapes=scratch,
        ),
        compiler_params=pltpu.CompilerParams(vmem_limit_bytes=24 * 2**20),
        cost_estimate=pl.CostEstimate(
            flops=4 * rows * count * width, bytes_accessed=2 * count * width, transcendentals=0
        ),
        name=f"energies_and_sums_{pass_index}{int(chained)}",
    )(info, *args)


def refine_body(info, own, sibling, over_x, over_y, over_xy, owner, coarse, fine, part):
    rows = owner.shape[1]
    received = own[...] + sibling[...] + over_x[...] + over_y[...] + over_xy[...]
    totals, counts_row = received[:rows], received[rows:]
    counts = as_column(counts_row[:1], rows)[:, :1]
    table = (
        lax.broadcasted_iota(jnp.int32, (NC, rows), 0) == owner[...]
    ).astype(jnp.float32)
    lookup = lax.dot_general(
        table,
        coarse[...],
        (((0,), (0,)), ((), ())),
        precision=HIGHEST,
        preferred_element_type=jnp.float32,
    )
    new = (totals + prior_weight * lookup) / (counts + prior_weight)
    fine[...] = new
    prior = jnp.where(info[0] == 0, prior_weight, 0.0)
    part[:NC, :] = prior * coarse[...] + jnp.dot(
        table, counts * new, precision=HIGHEST, preferred_element_type=jnp.float32
    )
    part[NC:, :] = jnp.zeros((TAIL, part.shape[1]), jnp.float32)
    part[NC:, :NC] = prior + lax.dot_general(
        counts_row,
        table,
        (((1,), (1,)), ((), ())),
        precision=HIGHEST,
        preferred_element_type=jnp.float32,
    )


def refine_half(info, own, sibling, over_x, over_y, over_xy, owner, coarse):
    block_width = coarse.shape[1]
    rows = owner.shape[1]
    slot = pl.BlockSpec((None, rows + TAIL, block_width), lambda i, info: (0, 0, 0))
    return pl.pallas_call(
        refine_body,
        out_shape=[
            jax.ShapeDtypeStruct((rows, block_width), jnp.float32),
            jax.ShapeDtypeStruct((NC + TAIL, block_width), jnp.float32),
        ],
        grid_spec=pltpu.PrefetchScalarGridSpec(
            num_scalar_prefetch=1,
            grid=(1,),
            in_specs=[slot] * 2
            + [full(rows + TAIL, block_width)] * 3
            + [full(1, rows), full(NC, block_width)],
            out_specs=[full(rows, block_width), full(NC + TAIL, block_width)],
        ),
        compiler_params=pltpu.CompilerParams(vmem_limit_bytes=16 * 2**20),
        name="refine_half",
    )(info, own, sibling, over_x, over_y, over_xy, owner, coarse)


def spread(value):
    corner = swap(value, ACROSS_X | ACROSS_Y)
    return [value, swap(value, ACROSS_X), swap(value, ACROSS_Y), corner]


def over_cen(value, combine):
    others = [swap(value, bit, "cen") for bit in range(1, lax.axis_size("cen"))]
    return functools.reduce(combine, others, value)


def place_body(info, own, other, fine_out, coarse_out):
    block_width = own.shape[2]
    rows = fine_out.shape[0]
    here = info[0]

    def put(pieces):
        for slot in range(SLOTS):
            column = pl.multiple_of((here ^ slot) * block_width, block_width)
            fine_out[:, pl.ds(column, block_width)] = pieces[slot, :rows, :]

    @pl.when(pl.program_id(0) == 0)
    def _():
        put(own)
        weight = own[0, rows + NC : rows + NC + 1, :128] + other[0, rows + NC : rows + NC + 1, :128]
        weight = as_column(weight, 128)[:NC, :1]
        for slot in range(SLOTS):
            column = pl.multiple_of((here ^ slot) * block_width, block_width)
            total = own[slot, rows : rows + NC, :] + other[slot, rows : rows + NC, :]
            coarse_out[:, pl.ds(column, block_width)] = total / weight

    @pl.when(pl.program_id(0) == 1)
    def _():
        put(other)


def place(info, own, other, rows):
    _, _, block_width = own.shape
    width = SLOTS * block_width
    return pl.pallas_call(
        place_body,
        out_shape=[
            jax.ShapeDtypeStruct((2 * rows, width), jnp.float32),
            jax.ShapeDtypeStruct((NC, width), jnp.float32),
        ],
        grid_spec=pltpu.PrefetchScalarGridSpec(
            num_scalar_prefetch=1,
            grid=(2,),
            in_specs=[full(*own.shape), full(*other.shape)],
            out_specs=[
                pl.BlockSpec((rows, width), lambda i, info: (info[1] ^ i, 0)),
                full(NC, width),
            ],
        ),
        compiler_params=pltpu.CompilerParams(vmem_limit_bytes=24 * 2**20),
        name="place_blocks",
    )(info, own, other)


def on_device_paired(points, fine_assign, fine_start, coarse_start, coarse_assign):
    width = points.shape[1]
    local_count = fine_start.shape[0]
    rows = local_count // 2
    block_width = width // SLOTS
    cen = lax.axis_index("cen")
    offset = cen * local_count
    me = lax.axis_index("pts")
    core, here = me & 1, me >> 1
    owners = coarse_assign.reshape(2, 1, rows)
    owner_of = lambda half: lax.dynamic_index_in_dim(owners, half, 0, keepdims=False)
    info_of = lambda half: jnp.stack([here, half, offset + half * rows]).astype(jnp.int32)
    group_place = jnp.stack([cen * 2 + core]).astype(jnp.int32)
    coarse = lax.dynamic_slice_in_dim(coarse_start, here * block_width, block_width, 1)

    def exchange(held, sibling):
        outgoing = [held[s] + sibling[s] for s in range(1, SLOTS)]
        over_xy = swap(outgoing[2], ACROSS_X | ACROSS_Y)
        return swap(outgoing[0], ACROSS_X), swap(outgoing[1], ACROSS_Y), over_xy

    first_pass = functools.partial(run_pass, pass_index=0, slots=False, rows=rows)
    sent, seen, squares, kept = first_pass(
        info_of(1 - core), points, fine_assign, fine_start, None, None
    )
    sibling = swap(sent, CORE)
    held, seen_first = first_pass(
        info_of(core), kept, fine_assign, fine_start, squares, seen
    )
    incoming = exchange(held, sibling)
    fine, part = refine_half(group_place, held, sibling, *incoming, owner_of(core), coarse)
    own = jnp.stack(spread(fine))
    part = part + swap(part, CORE)

    second_pass = functools.partial(run_pass, pass_index=1, slots=True, rows=rows)
    own, part = lax.optimization_barrier((own, part))
    other = swap(own, CORE)
    sent, seen = second_pass(info_of(core), kept, fine_assign, own, squares, None)
    sibling = swap(sent, CORE)
    held, seen_second = second_pass(info_of(1 - core), kept, fine_assign, other, squares, seen)
    incoming = exchange(held, sibling)

    seen = jnp.concatenate([seen_first, seen_second], 0)
    cen_size = lax.axis_size("cen")
    folded = jnp.concatenate([part, seen.reshape(-1, block_width)], 0)
    gathered = [folded] + [swap(folded, bit, "cen") for bit in range(1, cen_size)]
    part = functools.reduce(jnp.add, [each[: NC + TAIL] for each in gathered])
    seen = functools.reduce(jnp.minimum, [each[NC + TAIL :] for each in gathered])
    seen = seen.reshape(2, 2, -1)
    gaps = (seen[:, 0] - seen[:, 1]) / math.sqrt(width)
    coarse = part[:NC] / part[NC, :NC][:, None]

    fine, part = refine_half(
        group_place, held, sibling, *incoming, owner_of(1 - core), coarse
    )
    own = spread(fine)
    parts = spread(over_cen(part, jnp.add))
    own = jnp.stack([jnp.concatenate(pair, 0) for pair in zip(own, parts)])
    other = swap(own, CORE)
    fine_now, coarse_now = place(info_of(1 - core), own, other, rows)
    return (fine_now, coarse_now, gaps)


def solution(mesh):
    placed = (P("pts", None), P(None, "pts"), P("cen", None), P(), P("cen"))

    def on_device(points, fine_assign, fine_start, coarse_start, coarse_assign):
        count, width = points.shape
        local_count = fine_start.shape[0]
        centres = mesh.shape["cen"]
        fits = (
            mesh.shape["pts"] == 2 * SLOTS
            and centres & (centres - 1) == 0
            and width // SLOTS == local_count // 2
            and (width // SLOTS) % 128 == 0
            and count % 1024 == 0
        )
        plan = on_device_paired if fits else on_device_any
        return plan(points, fine_assign, fine_start, coarse_start, coarse_assign)

    return jax.shard_map(
        on_device,
        mesh=mesh,
        in_specs=placed,
        out_specs=(P("cen", None), P(), P(None, "pts")),
        check_vma=False,
    )
```

time: 150 us -> 127 us (0.85)
  Pallas kernels: 53.2 us -> 42.3 us
  waiting for transfers between devices: 52.9 us -> 47.2 us
  starting transfers between devices: 32.7 us -> 28.3 us
  other arithmetic: 6.31 us -> 2.24 us
  local copies, waits for them, and re-layouts: 2.93 us -> 5.93 us
    all_to_all x5 -> x0, waiting for transfers between devices: 40.3 us -> none  [trade(): return lax.all_to_all(value, 'pts', 0, 0, axis_index_groups=groups)]
    ppermute x15 -> x26, waiting for transfers between devices: 12.6 us -> 47.2 us  [swap(): return lax.ppermute(value, axis, [(i, i ^ bit) for i in range(size)])]
    all_to_all x5 -> x0, starting transfers between devices: 18.8 us -> none  [trade(): return lax.all_to_all(value, 'pts', 0, 0, axis_index_groups=groups)]
    ppermute x15 -> x26, starting transfers between devices: 13.9 us -> 28.3 us  [swap(): return lax.ppermute(value, axis, [(i, i ^ bit) for i in range(size)])]
    pallas_call x6, Pallas kernels: 51.1 us -> 40.2 us  [the longest x4 38.2 us: run_pass(): pl.pallas_call(body, out_shape=out_shape, grid_spec=pltpu.PrefetchScalarG...]
    unnamed x14 -> x19, local copies, waits for them, and re-layouts: 1.97 us -> 5.76 us
    add x8 -> x5, other arithmetic: 4.79 us -> 1.09 us  [the longest x2 1.03 us: exchange(): outgoing = [held[s] + sibling[s] for s in range(1, SLOTS)]]
  transfers between devices with their start and end apart: 20 -> 26, of which waited for: 10 -> 13; matrix products, arithmetic and copies ran while one was open for 1% -> 1% of each run, Pallas kernels for 23% -> 21%
where the time goes in v4:
time: 127 us
  waiting for transfers between devices  47.2 us (37%)
  Pallas kernels  42.3 us (33%)
  starting transfers between devices  28.3 us (22%)
  local copies, waits for them, and re-layouts  5.93 us (5%)
  other arithmetic  2.24 us (2%)
    ppermute x26, waiting for transfers between devices, swap(): return lax.ppermute(value, axis, [(i, i ^ bit) for i in range(size)])  47.2 us
    pallas_call x4, Pallas kernels, run_pass(): pl.pallas_call(body, out_shape=out_shape, grid_spec=pltpu.PrefetchScalarG...  38.2 us
    ppermute x26, starting transfers between devices, swap(): return lax.ppermute(value, axis, [(i, i ^ bit) for i in range(size)])  28.3 us
    unnamed x19, local copies, waits for them, and re-layouts  5.76 us
  transfers between devices with their start and end apart: 26, of which 13 were waited for; matrix products, arithmetic and copies ran while one was open for 1% of the time, Pallas kernels for 21%

profile of v4, /device:TPU:0, one launch (start us, length us, event | category | flops | bytes accessed | tf_op | source)
XLA Modules:
  0.0 126.9 jit_solution(15179614017552622366)
XLA Ops:
  0.6 0.0 copy-start
  0.7 0.1 pad_add_fusion
  0.7 1.6 %copy-done.1 = f32[512,1024]{1,0:T(8,128)S(1)} copy-done((f32[512,1024]{1,0:T(8,128)S(1)}, f32[512,1024]{1,0:T(8,128)}, u32[]{:S(2)}) %copy-start.1) | copy-done | bytes 2097176
  2.3 0.8 copy-done.3
  3.1 11.4 %energies_and_sums_00.1 = (f32[4,264,256]{2,1,0:T(8,128)S(1)}, f32[2,4096]{1,0:T(2,128)S(1)}, f32[1,4096]{1,0:T(1,128)S(1)}, bf16[4096,1024]{1,0:T(8,128)(2,1)S(1)}) custom-call(s32[3]{0:T(128)S(1)} %get-tuple-element.49.info, bf16[4096,1024]{1,0:T(8,128)(2,1)} %points.1, s32[2,4096]{1,0:T(2,128)S(1)} %copy-done.3, f32[512,1024]{1,0:T(8,128)S(1)} %copy-done.1), custom_call_target="tpu_custom_call" | custom-call | flops 4294967296 | bytes 8388608 | tf_op jit(solution)/shard_map/energies_and_sums_00/pallas_call | solution.py:254
  14.5 0.5 collective-permute-start
  15.0 8.5 %energies_and_sums_01.1 = (f32[4,264,256]{2,1,0:T(8,128)S(1)}, f32[2,4096]{1,0:T(2,128)S(1)}) custom-call(s32[3]{0:T(128)S(1)} %get-tuple-element.50.info, bf16[4096,1024]{1,0:T(8,128)(2,1)S(1)} %get-tuple-element.21.points, s32[2,4096]{1,0:T(2,128)S(1)} %copy-done.3, f32[512,1024]{1,0:T(8,128)S(1)} %copy-done.2, f32[1,4096]{1,0:T(1,128)S(1)} %get-tuple-element.22.refs_0_, ...), custom_call_target="tpu_custom_call" | custom-call | flops 4294967296 | bytes 8388608 | tf_op jit(solution)/shard_map/energies_and_sums_01/pallas_call | solution.py:254
  23.6 0.0 copy-start.8
  23.6 0.9 fusion.3
  24.5 2.5 %collective-permute-start.1 = (f32[264,256]{1,0:T(8,128)}, f32[264,256]{1,0:T(8,128)S(1)}, u32[]{:S(2)}, u32[]{:S(2)}) collective-permute-start(f32[264,256]{1,0:T(8,128)} %get-tuple-element.44), channel_id=1, source_target_pairs={{0,8},{4,12},{8,0},{12,4},{16,24},{20,28},{24,16},{28,20},{1,9},{5... | collective-permute-start | bytes 811016 | tf_op jit(solution)/shard_map/ppermute | solution.py:89
  27.0 1.5 %collective-permute-start.2 = (f32[264,256]{1,0:T(8,128)}, f32[264,256]{1,0:T(8,128)S(1)}, u32[]{:S(2)}, u32[]{:S(2)}) collective-permute-start(f32[264,256]{1,0:T(8,128)} %get-tuple-element.43), channel_id=1, source_target_pairs={{0,16},{4,20},{8,24},{12,28},{16,0},{20,4},{24,8},{28,12},{1,17},{... | collective-permute-start | bytes 811016 | tf_op jit(solution)/shard_map/ppermute | solution.py:89
  28.6 6.0 %collective-permute-done.1.over_x = f32[264,256]{1,0:T(8,128)S(1)} collective-permute-done((f32[264,256]{1,0:T(8,128)}, f32[264,256]{1,0:T(8,128)S(1)}, u32[]{:S(2)}, u32[]{:S(2)}) %collective-permute-start.1) | collective-permute-done | bytes 270368 | tf_op jit(solution)/shard_map/ppermute | solution.py:89
  34.6 7.0 %collective-permute-done.2.over_y = f32[264,256]{1,0:T(8,128)S(1)} collective-permute-done((f32[264,256]{1,0:T(8,128)}, f32[264,256]{1,0:T(8,128)S(1)}, u32[]{:S(2)}, u32[]{:S(2)}) %collective-permute-start.2) | collective-permute-done | bytes 270368 | tf_op jit(solution)/shard_map/ppermute | solution.py:89
  41.6 0.0 collective-permute-done.3.over_xy
  41.6 1.0 refine_half.2
  42.6 1.2 collective-permute-start.4
  43.8 0.8 collective-permute-start.5
  44.7 1.4 %collective-permute-start.6 = (f32[256,256]{1,0:T(8,128)S(1)}, f32[256,256]{1,0:T(8,128)S(1)}, u32[]{:S(2)}, u32[]{:S(2)}) collective-permute-start(f32[256,256]{1,0:T(8,128)S(1)} %get-tuple-element.26), channel_id=1, source_target_pairs={{0,24},{4,28},{8,16},{12,20},{16,8},{20,12},{24,0},{28,4},{1,25},{... | collective-permute-start | bytes 786440 | tf_op jit(solution)/shard_map/ppermute | solution.py:89
  46.1 0.0 collective-permute-start.7
  46.1 1.3 collective-permute-done.7
  47.4 4.5 %collective-permute-done.4 = f32[256,256]{1,0:T(8,128)S(1)} collective-permute-done((f32[256,256]{1,0:T(8,128)S(1)}, f32[256,256]{1,0:T(8,128)S(1)}, u32[]{:S(2)}, u32[]{:S(2)}) %collective-permute-start.4) | collective-permute-done | bytes 262176 | tf_op jit(solution)/shard_map/ppermute | solution.py:89
  51.8 5.2 %collective-permute-done.5 = f32[256,256]{1,0:T(8,128)S(1)} collective-permute-done((f32[256,256]{1,0:T(8,128)S(1)}, f32[256,256]{1,0:T(8,128)S(1)}, u32[]{:S(2)}, u32[]{:S(2)}) %collective-permute-start.5) | collective-permute-done | bytes 262176 | tf_op jit(solution)/shard_map/ppermute | solution.py:89
  57.1 0.0 collective-permute-done.6
  57.1 0.1 pad_maximum_fusion.1.fine
  57.2 0.1 collective-permute-start.8
  57.3 3.4 %copy-done.6 = bf16[4096,1024]{1,0:T(8,128)(2,1)S(1)} copy-done((bf16[4096,1024]{1,0:T(8,128)(2,1)S(1)}, bf16[4096,1024]{1,0:T(8,128)(2,1)}, u32[]{:S(2)}) %copy-start.6) | copy-done | bytes 8388632
  60.7 9.5 %energies_and_sums_10.1 = (f32[4,264,256]{2,1,0:T(8,128)}, f32[2,4096]{1,0:T(2,128)S(1)}) custom-call(s32[3]{0:T(128)S(1)} %get-tuple-element.50.info, bf16[4096,1024]{1,0:T(8,128)(2,1)S(1)} %copy-done.6, s32[2,4096]{1,0:T(2,128)S(1)} %copy-done.4, f32[4,256,256]{2,1,0:T(8,128)S(1)} %pad_maximum_fusion.1.fine, f32[1,4096]{1,0:T(1,128)S(1)} %get-tuple-element.22.refs_0_), custom_call_target="tpu_custom_call" | custom-call | flops 4294967296 | bytes 8388608 | tf_op jit(solution)/shard_map/energies_and_sums_10/pallas_call | solution.py:254
  70.1 0.5 collective-permute-start.9
  70.7 8.8 %energies_and_sums_11.1 = (f32[4,264,256]{2,1,0:T(8,128)S(1)}, f32[2,4096]{1,0:T(2,128)S(1)}) custom-call(s32[3]{0:T(128)S(1)} %get-tuple-element.49.info, bf16[4096,1024]{1,0:T(8,128)(2,1)S(1)} %copy-done.7, s32[2,4096]{1,0:T(2,128)S(1)} %copy-done.4, f32[4,256,256]{2,1,0:T(8,128)S(1)} %collective-permute-done.8.fine, ...), custom_call_target="tpu_custom_call" | custom-call | flops 4294967296 | bytes 8388608 | tf_op jit(solution)/shard_map/energies_and_sums_11/pallas_call | solution.py:254
  79.5 1.6 %collective-permute-start.13 = (f32[136,256]{1,0:T(8,128)S(1)}, f32[136,256]{1,0:T(8,128)S(1)}, u32[]{:S(2)}, u32[]{:S(2)}) collective-permute-start(f32[136,256]{1,0:T(8,128)S(1)} %constant_dynamic-update-slice_fusion), channel_id=1, source_target_pairs={{0,1},{1,0},{2,3},{3,2},{4,5},{5,4},{6,7},{7,6},{8,9},{9,8},{10,11... | collective-permute-start | bytes 417800 | tf_op jit(solution)/shard_map/ppermute | solution.py:89
  81.2 2.6 %collective-permute-start.14 = (f32[136,256]{1,0:T(8,128)S(1)}, f32[136,256]{1,0:T(8,128)S(1)}, u32[]{:S(2)}, u32[]{:S(2)}) collective-permute-start(f32[136,256]{1,0:T(8,128)S(1)} %constant_dynamic-update-slice_fusion), channel_id=1, source_target_pairs={{0,2},{1,3},{2,0},{3,1},{4,6},{5,7},{6,4},{7,5},{8,10},{9,11},{10,... | collective-permute-start | bytes 417800 | tf_op jit(solution)/shard_map/ppermute | solution.py:89
  83.8 0.2 collective-permute-start.15
  84.0 0.0 collective-permute-done.9.sibling
  84.0 0.1 fusion
  84.1 0.6 collective-permute-start.10
  84.7 1.4 %collective-permute-start.11 = (f32[264,256]{1,0:T(8,128)S(1)}, f32[264,256]{1,0:T(8,128)S(1)}, u32[]{:S(2)}, u32[]{:S(2)}) collective-permute-start(f32[264,256]{1,0:T(8,128)S(1)} %get-tuple-element.40), channel_id=1, source_target_pairs={{0,16},{4,20},{8,24},{12,28},{16,0},{20,4},{24,8},{28,12},{1,17},{... | collective-permute-start | bytes 811016 | tf_op jit(solution)/shard_map/ppermute | solution.py:89
  86.2 1.1 collective-permute-done.13
  87.2 1.4 %collective-permute-start.12 = (f32[264,256]{1,0:T(8,128)S(1)}, f32[264,256]{1,0:T(8,128)S(1)}, u32[]{:S(2)}, u32[]{:S(2)}) collective-permute-start(f32[264,256]{1,0:T(8,128)S(1)} %get-tuple-element.39), channel_id=1, source_target_pairs={{0,24},{4,28},{8,16},{12,20},{16,8},{20,12},{24,0},{28,4},{1,25},{... | collective-permute-start | bytes 811016 | tf_op jit(solution)/shard_map/ppermute | solution.py:89
  88.7 6.0 %collective-permute-done.14 = f32[136,256]{1,0:T(8,128)S(1)} collective-permute-done((f32[136,256]{1,0:T(8,128)S(1)}, f32[136,256]{1,0:T(8,128)S(1)}, u32[]{:S(2)}, u32[]{:S(2)}) %collective-permute-start.14) | collective-permute-done | bytes 139296 | tf_op jit(solution)/shard_map/ppermute | solution.py:89
  94.6 0.0 collective-permute-done.15
  94.7 0.1 slice_divide_fusion.coarse
  94.8 3.1 %collective-permute-done.11.over_y = f32[264,256]{1,0:T(8,128)S(1)} collective-permute-done((f32[264,256]{1,0:T(8,128)S(1)}, f32[264,256]{1,0:T(8,128)S(1)}, u32[]{:S(2)}, u32[]{:S(2)}) %collective-permute-start.11) | collective-permute-done | bytes 270368 | tf_op jit(solution)/shard_map/ppermute | solution.py:89
  97.9 1.0 refine_half.3
  98.9 0.6 collective-permute-start.16
  99.5 3.5 %collective-permute-start.17 = (f32[72,256]{1,0:T(8,128)S(1)}, f32[72,256]{1,0:T(8,128)S(1)}, u32[]{:S(2)}, u32[]{:S(2)}) collective-permute-start(f32[72,256]{1,0:T(8,128)S(1)} %get-tuple-element.36), channel_id=1, source_target_pairs={{0,2},{1,3},{2,0},{3,1},{4,6},{5,7},{6,4},{7,5},{8,10},{9,11},{10,... | collective-permute-start | bytes 221192 | tf_op jit(solution)/shard_map/ppermute | solution.py:89
  103.0 0.3 collective-permute-start.18
  103.4 1.5 %collective-permute-start.19 = (f32[256,256]{1,0:T(8,128)S(1)}, f32[256,256]{1,0:T(8,128)S(1)}, u32[]{:S(2)}, u32[]{:S(2)}) collective-permute-start(f32[256,256]{1,0:T(8,128)S(1)} %get-tuple-element.35), channel_id=1, source_target_pairs={{0,8},{4,12},{8,0},{12,4},{16,24},{20,28},{24,16},{28,20},{1,9},{5... | collective-permute-start | bytes 786440 | tf_op jit(solution)/shard_map/ppermute | solution.py:89
  104.9 0.5 collective-permute-start.21
  105.4 0.0 collective-permute-done.16
  105.4 1.5 %collective-permute-start.23 = (f32[256,256]{1,0:T(8,128)S(1)}, f32[256,256]{1,0:T(8,128)S(1)}, u32[]{:S(2)}, u32[]{:S(2)}) collective-permute-start(f32[256,256]{1,0:T(8,128)S(1)} %get-tuple-element.35), channel_id=1, source_target_pairs={{0,24},{4,28},{8,16},{12,20},{16,8},{20,12},{24,0},{28,4},{1,25},{... | collective-permute-start | bytes 786440 | tf_op jit(solution)/shard_map/ppermute | solution.py:89
  106.9 0.0 collective-permute-done.17
  106.9 2.2 %collective-permute-done.18 = f32[72,256]{1,0:T(8,128)S(1)} collective-permute-done((f32[72,256]{1,0:T(8,128)S(1)}, f32[72,256]{1,0:T(8,128)S(1)}, u32[]{:S(2)}, u32[]{:S(2)}) %collective-permute-start.18) | collective-permute-done | bytes 73760 | tf_op jit(solution)/shard_map/ppermute | solution.py:89
  109.2 1.5 %collective-permute-start.20 = (f32[72,256]{1,0:T(8,128)S(1)}, f32[72,256]{1,0:T(8,128)S(1)}, u32[]{:S(2)}, u32[]{:S(2)}) collective-permute-start(f32[72,256]{1,0:T(8,128)S(1)} %add_add_fusion), channel_id=1, source_target_pairs={{0,8},{4,12},{8,0},{12,4},{16,24},{20,28},{24,16},{28,20},{1,9},{5... | collective-permute-start | bytes 221192 | tf_op jit(solution)/shard_map/ppermute | solution.py:89
  110.7 0.6 collective-permute-start.22
  111.3 4.9 %collective-permute-done.20 = f32[72,256]{1,0:T(8,128)S(1)} collective-permute-done((f32[72,256]{1,0:T(8,128)S(1)}, f32[72,256]{1,0:T(8,128)S(1)}, u32[]{:S(2)}, u32[]{:S(2)}) %collective-permute-start.20) | collective-permute-done | bytes 73760 | tf_op jit(solution)/shard_map/ppermute | solution.py:89
  116.2 1.6 %collective-permute-start.24 = (f32[72,256]{1,0:T(8,128)S(1)}, f32[72,256]{1,0:T(8,128)S(1)}, u32[]{:S(2)}, u32[]{:S(2)}) collective-permute-start(f32[72,256]{1,0:T(8,128)S(1)} %add_add_fusion), channel_id=1, source_target_pairs={{0,24},{4,28},{8,16},{12,20},{16,8},{20,12},{24,0},{28,4},{1,25},{... | collective-permute-start | bytes 221192 | tf_op jit(solution)/shard_map/ppermute | solution.py:89
  117.8 0.2 collective-permute-done.22
  118.1 3.4 %collective-permute-done.24 = f32[72,256]{1,0:T(8,128)S(1)} collective-permute-done((f32[72,256]{1,0:T(8,128)S(1)}, f32[72,256]{1,0:T(8,128)S(1)}, u32[]{:S(2)}, u32[]{:S(2)}) %collective-permute-start.24) | collective-permute-done | bytes 73760 | tf_op jit(solution)/shard_map/ppermute | solution.py:89
  121.5 0.1 pad_maximum_fusion.own
  121.6 0.1 collective-permute-start.25
  121.7 0.1 fusion.8
  121.7 0.7 fusion.7
  122.4 2.3 %collective-permute-done.25.other = f32[4,328,256]{2,1,0:T(8,128)S(1)} collective-permute-done((f32[4,328,256]{2,1,0:T(8,128)S(1)}, f32[4,328,256]{2,1,0:T(8,128)S(1)}, u32[]{:S(2)}, u32[]{:S(2)}) %collective-permute-start.25) | collective-permute-done | bytes 1343520 | tf_op jit(solution)/shard_map/ppermute | solution.py:89
  124.7 2.1 %place_blocks.1 = (f32[512,1024]{1,0:T(8,128)}, f32[64,1024]{1,0:T(8,128)}) custom-call(s32[3]{0:T(128)S(1)} %get-tuple-element.49.info, f32[4,328,256]{2,1,0:T(8,128)S(1)} %pad_maximum_fusion.own, f32[4,328,256]{2,1,0:T(8,128)S(1)} %collective-permute-done.25.other), custom_call_target="tpu_custom_call" | custom-call | tf_op jit(solution)/shard_map/place_blocks/pallas_call | solution.py:364
  (37 shorter events, 0.4 us)
Async XLA Ops:
  0.6 27.9 %copy-start = (f32[64,1024]{1,0:T(8,128)S(1)}, f32[64,1024]{1,0:T(8,128)}, u32[]{:S(2)}) copy-start(f32[64,1024]{1,0:T(8,128)} %param.8) | copy-start | bytes 786436
  0.7 1.6 %copy-start.1 = (f32[512,1024]{1,0:T(8,128)S(1)}, f32[512,1024]{1,0:T(8,128)}, u32[]{:S(2)}) copy-start(f32[512,1024]{1,0:T(8,128)} %fine.3) | copy-start | bytes 6291460
  2.3 0.8 copy-start.3
  3.1 11.9 %copy-start.2 = (f32[512,1024]{1,0:T(8,128)S(1)}, f32[512,1024]{1,0:T(8,128)}, u32[]{:S(2)}) copy-start(f32[512,1024]{1,0:T(8,128)} %fine.3) | copy-start | bytes 6291460
  14.5 9.1 %copy-start.5 = (bf16[4096,1024]{1,0:T(8,128)(2,1)}, bf16[4096,1024]{1,0:T(8,128)(2,1)S(1)}, u32[]{:S(2)}) copy-start(bf16[4096,1024]{1,0:T(8,128)(2,1)S(1)} %get-tuple-element.21.points) | copy-start | bytes 25165828
  14.5 9.1 %collective-permute-start = (f32[4,264,256]{2,1,0:T(8,128)S(1)}, f32[4,264,256]{2,1,0:T(8,128)S(1)}, u32[]{:S(2)}, u32[]{:S(2)}) collective-permute-start(f32[4,264,256]{2,1,0:T(8,128)S(1)} %get-tuple-element.25), channel_id=1, source_target_pairs={{0,4},{4,0},{8,12},{12,8},{16,20},{20,16},{24,28},{28,24},{1,5},{5... | collective-permute-start | bytes 3244040 | tf_op jit(solution)/shard_map/ppermute | solution.py:89
  23.6 5.0 %copy-start.8 = (s32[512]{0:T(512)S(1)}, s32[512]{0:T(512)}, u32[]{:S(2)}) copy-start(s32[512]{0:T(512)} %param.9) | copy-start | bytes 6148
  24.5 10.0 %collective-permute-start.1 = (f32[264,256]{1,0:T(8,128)}, f32[264,256]{1,0:T(8,128)S(1)}, u32[]{:S(2)}, u32[]{:S(2)}) collective-permute-start(f32[264,256]{1,0:T(8,128)} %get-tuple-element.44), channel_id=1, source_target_pairs={{0,8},{4,12},{8,0},{12,4},{16,24},{20,28},{24,16},{28,20},{1,9},{5... | collective-permute-start | bytes 811016 | tf_op jit(solution)/shard_map/ppermute | solution.py:89
  27.0 14.6 %collective-permute-start.2 = (f32[264,256]{1,0:T(8,128)}, f32[264,256]{1,0:T(8,128)S(1)}, u32[]{:S(2)}, u32[]{:S(2)}) collective-permute-start(f32[264,256]{1,0:T(8,128)} %get-tuple-element.43), channel_id=1, source_target_pairs={{0,16},{4,20},{8,24},{12,28},{16,0},{20,4},{24,8},{28,12},{1,17},{... | collective-permute-start | bytes 811016 | tf_op jit(solution)/shard_map/ppermute | solution.py:89
  28.5 13.1 %collective-permute-start.3 = (f32[264,256]{1,0:T(8,128)}, f32[264,256]{1,0:T(8,128)S(1)}, u32[]{:S(2)}, u32[]{:S(2)}) collective-permute-start(f32[264,256]{1,0:T(8,128)} %get-tuple-element.42), channel_id=1, source_target_pairs={{0,24},{4,28},{8,16},{12,20},{16,8},{20,12},{24,0},{28,4},{1,25},{... | collective-permute-start | bytes 811016 | tf_op jit(solution)/shard_map/ppermute | solution.py:89
  42.6 14.7 %copy-start.4 = (s32[2,4096]{1,0:T(2,128)S(1)}, s32[2,4096]{1,0:T(2,128)}, u32[]{:S(2)}) copy-start(s32[2,4096]{1,0:T(2,128)} %assign.7) | copy-start | bytes 98308
  42.6 9.3 %collective-permute-start.4 = (f32[256,256]{1,0:T(8,128)S(1)}, f32[256,256]{1,0:T(8,128)S(1)}, u32[]{:S(2)}, u32[]{:S(2)}) collective-permute-start(f32[256,256]{1,0:T(8,128)S(1)} %get-tuple-element.26), channel_id=1, source_target_pairs={{0,8},{4,12},{8,0},{12,4},{16,24},{20,28},{24,16},{28,20},{1,9},{5... | collective-permute-start | bytes 786440 | tf_op jit(solution)/shard_map/ppermute | solution.py:89
  43.8 13.3 %collective-permute-start.5 = (f32[256,256]{1,0:T(8,128)S(1)}, f32[256,256]{1,0:T(8,128)S(1)}, u32[]{:S(2)}, u32[]{:S(2)}) collective-permute-start(f32[256,256]{1,0:T(8,128)S(1)} %get-tuple-element.26), channel_id=1, source_target_pairs={{0,16},{4,20},{8,24},{12,28},{16,0},{20,4},{24,8},{28,12},{1,17},{... | collective-permute-start | bytes 786440 | tf_op jit(solution)/shard_map/ppermute | solution.py:89
  44.7 12.4 %collective-permute-start.6 = (f32[256,256]{1,0:T(8,128)S(1)}, f32[256,256]{1,0:T(8,128)S(1)}, u32[]{:S(2)}, u32[]{:S(2)}) collective-permute-start(f32[256,256]{1,0:T(8,128)S(1)} %get-tuple-element.26), channel_id=1, source_target_pairs={{0,24},{4,28},{8,16},{12,20},{16,8},{20,12},{24,0},{28,4},{1,25},{... | collective-permute-start | bytes 786440 | tf_op jit(solution)/shard_map/ppermute | solution.py:89
  46.1 1.3 collective-permute-start.7
  57.2 13.5 %collective-permute-start.8 = (f32[4,256,256]{2,1,0:T(8,128)S(1)}, f32[4,256,256]{2,1,0:T(8,128)S(1)}, u32[]{:S(2)}, u32[]{:S(2)}) collective-permute-start(f32[4,256,256]{2,1,0:T(8,128)S(1)} %pad_maximum_fusion.1.fine), channel_id=1, source_target_pairs={{0,4},{4,0},{8,12},{12,8},{16,20},{20,16},{24,28},{28,24},{1,5},{5... | collective-permute-start | bytes 3145736 | tf_op jit(solution)/shard_map/ppermute | solution.py:89
  57.3 3.4 %copy-start.6 = (bf16[4096,1024]{1,0:T(8,128)(2,1)S(1)}, bf16[4096,1024]{1,0:T(8,128)(2,1)}, u32[]{:S(2)}) copy-start(bf16[4096,1024]{1,0:T(8,128)(2,1)} %copy-done.5) | copy-start | bytes 25165828
  60.6 10.0 %copy-start.7 = (bf16[4096,1024]{1,0:T(8,128)(2,1)S(1)}, bf16[4096,1024]{1,0:T(8,128)(2,1)}, u32[]{:S(2)}) copy-start(bf16[4096,1024]{1,0:T(8,128)(2,1)} %copy-done.5) | copy-start | bytes 25165828
  70.1 13.9 %collective-permute-start.9 = (f32[4,264,256]{2,1,0:T(8,128)}, f32[4,264,256]{2,1,0:T(8,128)S(1)}, u32[]{:S(2)}, u32[]{:S(2)}) collective-permute-start(f32[4,264,256]{2,1,0:T(8,128)} %get-tuple-element.31), channel_id=1, source_target_pairs={{0,4},{4,0},{8,12},{12,8},{16,20},{20,16},{24,28},{28,24},{1,5},{5... | collective-permute-start | bytes 3244040 | tf_op jit(solution)/shard_map/ppermute | solution.py:89
  79.5 7.7 %collective-permute-start.13 = (f32[136,256]{1,0:T(8,128)S(1)}, f32[136,256]{1,0:T(8,128)S(1)}, u32[]{:S(2)}, u32[]{:S(2)}) collective-permute-start(f32[136,256]{1,0:T(8,128)S(1)} %constant_dynamic-update-slice_fusion), channel_id=1, source_target_pairs={{0,1},{1,0},{2,3},{3,2},{4,5},{5,4},{6,7},{7,6},{8,9},{9,8},{10,11... | collective-permute-start | bytes 417800 | tf_op jit(solution)/shard_map/ppermute | solution.py:89
  81.2 13.4 %collective-permute-start.14 = (f32[136,256]{1,0:T(8,128)S(1)}, f32[136,256]{1,0:T(8,128)S(1)}, u32[]{:S(2)}, u32[]{:S(2)}) collective-permute-start(f32[136,256]{1,0:T(8,128)S(1)} %constant_dynamic-update-slice_fusion), channel_id=1, source_target_pairs={{0,2},{1,3},{2,0},{3,1},{4,6},{5,7},{6,4},{7,5},{8,10},{9,11},{10,... | collective-permute-start | bytes 417800 | tf_op jit(solution)/shard_map/ppermute | solution.py:89
  83.8 10.9 %collective-permute-start.15 = (f32[136,256]{1,0:T(8,128)S(1)}, f32[136,256]{1,0:T(8,128)S(1)}, u32[]{:S(2)}, u32[]{:S(2)}) collective-permute-start(f32[136,256]{1,0:T(8,128)S(1)} %constant_dynamic-update-slice_fusion), channel_id=1, source_target_pairs={{0,3},{1,2},{2,1},{3,0},{4,7},{5,6},{6,5},{7,4},{8,11},{9,10},{10,... | collective-permute-start | bytes 417800 | tf_op jit(solution)/shard_map/ppermute | solution.py:89
  84.1 10.7 %collective-permute-start.10 = (f32[264,256]{1,0:T(8,128)S(1)}, f32[264,256]{1,0:T(8,128)S(1)}, u32[]{:S(2)}, u32[]{:S(2)}) collective-permute-start(f32[264,256]{1,0:T(8,128)S(1)} %get-tuple-element.41), channel_id=1, source_target_pairs={{0,8},{4,12},{8,0},{12,4},{16,24},{20,28},{24,16},{28,20},{1,9},{5... | collective-permute-start | bytes 811016 | tf_op jit(solution)/shard_map/ppermute | solution.py:89
  84.7 13.1 %collective-permute-start.11 = (f32[264,256]{1,0:T(8,128)S(1)}, f32[264,256]{1,0:T(8,128)S(1)}, u32[]{:S(2)}, u32[]{:S(2)}) collective-permute-start(f32[264,256]{1,0:T(8,128)S(1)} %get-tuple-element.40), channel_id=1, source_target_pairs={{0,16},{4,20},{8,24},{12,28},{16,0},{20,4},{24,8},{28,12},{1,17},{... | collective-permute-start | bytes 811016 | tf_op jit(solution)/shard_map/ppermute | solution.py:89
  87.2 10.7 %collective-permute-start.12 = (f32[264,256]{1,0:T(8,128)S(1)}, f32[264,256]{1,0:T(8,128)S(1)}, u32[]{:S(2)}, u32[]{:S(2)}) collective-permute-start(f32[264,256]{1,0:T(8,128)S(1)} %get-tuple-element.39), channel_id=1, source_target_pairs={{0,24},{4,28},{8,16},{12,20},{16,8},{20,12},{24,0},{28,4},{1,25},{... | collective-permute-start | bytes 811016 | tf_op jit(solution)/shard_map/ppermute | solution.py:89
  98.9 6.5 %collective-permute-start.16 = (f32[72,256]{1,0:T(8,128)S(1)}, f32[72,256]{1,0:T(8,128)S(1)}, u32[]{:S(2)}, u32[]{:S(2)}) collective-permute-start(f32[72,256]{1,0:T(8,128)S(1)} %get-tuple-element.36), channel_id=1, source_target_pairs={{0,1},{1,0},{2,3},{3,2},{4,5},{5,4},{6,7},{7,6},{8,9},{9,8},{10,11... | collective-permute-start | bytes 221192 | tf_op jit(solution)/shard_map/ppermute | solution.py:89
  99.5 7.4 %collective-permute-start.17 = (f32[72,256]{1,0:T(8,128)S(1)}, f32[72,256]{1,0:T(8,128)S(1)}, u32[]{:S(2)}, u32[]{:S(2)}) collective-permute-start(f32[72,256]{1,0:T(8,128)S(1)} %get-tuple-element.36), channel_id=1, source_target_pairs={{0,2},{1,3},{2,0},{3,1},{4,6},{5,7},{6,4},{7,5},{8,10},{9,11},{10,... | collective-permute-start | bytes 221192 | tf_op jit(solution)/shard_map/ppermute | solution.py:89
  103.0 6.2 %collective-permute-start.18 = (f32[72,256]{1,0:T(8,128)S(1)}, f32[72,256]{1,0:T(8,128)S(1)}, u32[]{:S(2)}, u32[]{:S(2)}) collective-permute-start(f32[72,256]{1,0:T(8,128)S(1)} %get-tuple-element.36), channel_id=1, source_target_pairs={{0,3},{1,2},{2,1},{3,0},{4,7},{5,6},{6,5},{7,4},{8,11},{9,10},{10,... | collective-permute-start | bytes 221192 | tf_op jit(solution)/shard_map/ppermute | solution.py:89
  103.4 14.5 %collective-permute-start.19 = (f32[256,256]{1,0:T(8,128)S(1)}, f32[256,256]{1,0:T(8,128)S(1)}, u32[]{:S(2)}, u32[]{:S(2)}) collective-permute-start(f32[256,256]{1,0:T(8,128)S(1)} %get-tuple-element.35), channel_id=1, source_target_pairs={{0,8},{4,12},{8,0},{12,4},{16,24},{20,28},{24,16},{28,20},{1,9},{5... | collective-permute-start | bytes 786440 | tf_op jit(solution)/shard_map/ppermute | solution.py:89
  104.9 13.2 %collective-permute-start.21 = (f32[256,256]{1,0:T(8,128)S(1)}, f32[256,256]{1,0:T(8,128)S(1)}, u32[]{:S(2)}, u32[]{:S(2)}) collective-permute-start(f32[256,256]{1,0:T(8,128)S(1)} %get-tuple-element.35), channel_id=1, source_target_pairs={{0,16},{4,20},{8,24},{12,28},{16,0},{20,4},{24,8},{28,12},{1,17},{... | collective-permute-start | bytes 786440 | tf_op jit(solution)/shard_map/ppermute | solution.py:89
  105.4 16.1 %collective-permute-start.23 = (f32[256,256]{1,0:T(8,128)S(1)}, f32[256,256]{1,0:T(8,128)S(1)}, u32[]{:S(2)}, u32[]{:S(2)}) collective-permute-start(f32[256,256]{1,0:T(8,128)S(1)} %get-tuple-element.35), channel_id=1, source_target_pairs={{0,24},{4,28},{8,16},{12,20},{16,8},{20,12},{24,0},{28,4},{1,25},{... | collective-permute-start | bytes 786440 | tf_op jit(solution)/shard_map/ppermute | solution.py:89
  109.2 7.0 %collective-permute-start.20 = (f32[72,256]{1,0:T(8,128)S(1)}, f32[72,256]{1,0:T(8,128)S(1)}, u32[]{:S(2)}, u32[]{:S(2)}) collective-permute-start(f32[72,256]{1,0:T(8,128)S(1)} %add_add_fusion), channel_id=1, source_target_pairs={{0,8},{4,12},{8,0},{12,4},{16,24},{20,28},{24,16},{28,20},{1,9},{5... | collective-permute-start | bytes 221192 | tf_op jit(solution)/shard_map/ppermute | solution.py:89
  110.7 7.3 %collective-permute-start.22 = (f32[72,256]{1,0:T(8,128)S(1)}, f32[72,256]{1,0:T(8,128)S(1)}, u32[]{:S(2)}, u32[]{:S(2)}) collective-permute-start(f32[72,256]{1,0:T(8,128)S(1)} %add_add_fusion), channel_id=1, source_target_pairs={{0,16},{4,20},{8,24},{12,28},{16,0},{20,4},{24,8},{28,12},{1,17},{... | collective-permute-start | bytes 221192 | tf_op jit(solution)/shard_map/ppermute | solution.py:89
  116.2 5.3 %collective-permute-start.24 = (f32[72,256]{1,0:T(8,128)S(1)}, f32[72,256]{1,0:T(8,128)S(1)}, u32[]{:S(2)}, u32[]{:S(2)}) collective-permute-start(f32[72,256]{1,0:T(8,128)S(1)} %add_add_fusion), channel_id=1, source_target_pairs={{0,24},{4,28},{8,16},{12,20},{16,8},{20,12},{24,0},{28,4},{1,25},{... | collective-permute-start | bytes 221192 | tf_op jit(solution)/shard_map/ppermute | solution.py:89
  121.6 3.1 %collective-permute-start.25 = (f32[4,328,256]{2,1,0:T(8,128)S(1)}, f32[4,328,256]{2,1,0:T(8,128)S(1)}, u32[]{:S(2)}, u32[]{:S(2)}) collective-permute-start(f32[4,328,256]{2,1,0:T(8,128)S(1)} %pad_maximum_fusion.own), channel_id=1, source_target_pairs={{0,4},{4,0},{8,12},{12,8},{16,20},{20,16},{24,28},{28,24},{1,5},{5... | collective-permute-start | bytes 4030472 | tf_op jit(solution)/shard_map/ppermute | solution.py:89

commit v5 on v4

--- a/solution.py
+++ b/solution.py
@@ -97,16 +97,23 @@
     return jnp.broadcast_to(row, (128, rows)).T
 
 
-def pass_body(info, points, assign, fine, *refs, pass_index, slots, first, chained, tile):
+def pass_body(info, points, assign, fine, *refs, pass_index, flip, stream, chained, tile):
     refs = list(refs)
+    initial = pass_index == 0
+    first = initial and stream
     squares_in = None if first else refs.pop(0)
     seen_in = refs.pop(0) if chained else None
     payload, seen = refs.pop(0), refs.pop(0)
-    squares_out, kept = (refs.pop(0), refs.pop(0)) if first else (None, points)
-    low, sums, tallies, even, odd, scaled = refs[:6]
+    squares_out = refs.pop(0) if first else None
+    kept = refs.pop(0) if stream else points
+    low, tallies, even, odd, scaled, table, chosen_in, small_sems = refs[:8]
+    start = refs[8] if initial else None
+    point_sems = refs[-1] if stream else None
     rows, width = low.shape
     block_width = width // SLOTS
-    here, base = info[0], info[2]
+    here = info[0]
+    half = info[1] ^ flip
+    base = info[2] + half * rows
     tiles = points.shape[0] // tile
 
     def span(i):
@@ -116,25 +123,34 @@
         return pl.ds(pl.multiple_of((here ^ slot) * block_width, block_width), block_width)
 
     def load(i):
-        return pltpu.make_async_copy(points.at[span(i)], kept.at[span(i)], refs[6].at[i])
-
-    if first:
-
-        @pl.loop(0, tiles)
+        return pltpu.make_async_copy(points.at[span(i)], kept.at[span(i)], point_sems.at[i])
+
+    load_assign = pltpu.make_async_copy(assign, chosen_in, small_sems.at[0])
+    if initial:
+        load_start = pltpu.make_async_copy(
+            fine.at[pl.ds(pl.multiple_of(half * rows, rows), rows)], start, small_sems.at[1]
+        )
+        load_start.start()
+    if stream:
+        load(0).start()
+    load_assign.start()
+    if stream:
+
+        @pl.loop(1, tiles)
         def _(i):
             load(i).start()
 
-    if slots:
+    if initial:
+        load_start.wait()
+        block = start[...]
+        norm = jnp.sum(block * block, axis=1, keepdims=True)
+        low[...] = (-2.0 * block).astype(jnp.bfloat16)
+    else:
         norm = jnp.zeros((rows, 1), jnp.float32)
         for slot in range(SLOTS):
             block = fine[slot]
             norm = norm + jnp.sum(block * block, axis=1, keepdims=True)
             low[:, column_of(slot)] = (-2.0 * block).astype(jnp.bfloat16)
-    else:
-        block = fine[...]
-        norm = jnp.sum(block * block, axis=1, keepdims=True)
-        low[...] = (-2.0 * block).astype(jnp.bfloat16)
-    sums[...] = jnp.zeros_like(sums)
     tallies[...] = jnp.zeros_like(tallies)
 
     def multiply(i, target):
@@ -142,9 +158,9 @@
             low[...], kept[span(i), :], (((1,), (1,)), ((), ())), preferred_element_type=jnp.float32
         )
 
-    def collect(i, products):
+    def weigh(i, products):
         energy = norm + products[...]
-        chosen = assign[pass_index : pass_index + 1, span(i)] - base
+        chosen = chosen_in[pass_index : pass_index + 1, span(i)] - base
         member = lax.broadcasted_iota(jnp.int32, energy.shape, 0) == chosen
         picked = jnp.sum(jnp.where(member, energy, 0.0), axis=0, keepdims=True)
         nearest = jnp.min(energy, axis=0, keepdims=True)
@@ -173,81 +189,98 @@
         factor = as_column(weights, tile)
         for lane in range(0, width, 128):
             values = kept[span(i), lane : lane + 128].astype(jnp.float32)
-            scaled[:, lane : lane + 128] = (values * factor).astype(jnp.bfloat16)
-        sums[...] += jnp.dot(
-            member.astype(jnp.float32).astype(jnp.bfloat16),
-            scaled[...],
-            preferred_element_type=jnp.float32,
-        )
-
-    if first:
+            scaled[span(i), lane : lane + 128] = (values * factor).astype(jnp.bfloat16)
+        table[:, span(i)] = member.astype(jnp.float32).astype(jnp.bfloat16)
+
+    load_assign.wait()
+    if stream:
         load(0).wait()
     multiply(0, even)
 
-    @pl.loop(0, tiles // 2)
+    @pl.loop(0, tiles // 2 - 1)
     def _(pair):
         i = 2 * pair
-        if first:
+        if stream:
             load(i + 1).wait()
-
-            @pl.when(i + 2 < tiles)
-            def _():
-                load(i + 2).wait()
-
+            load(i + 2).wait()
         multiply(i + 1, odd)
-        collect(i, even)
-        multiply(jnp.minimum(i + 2, tiles - 1), even)
-        collect(i + 1, odd)
+        weigh(i, even)
+        multiply(i + 2, even)
+        weigh(i + 1, odd)
+
+    if stream:
+        load(tiles - 1).wait()
+    multiply(tiles - 1, odd)
+    weigh(tiles - 2, even)
+    weigh(tiles - 1, odd)
 
     counts = jnp.broadcast_to(jnp.sum(tallies[...].T, axis=0, keepdims=True), (TAIL, rows))
+
     for slot in range(SLOTS):
-        payload[slot, :rows, :] = sums[:, column_of(slot)]
+        payload[slot, :rows, :] = jnp.zeros((rows, block_width), jnp.float32)
         payload[slot, rows:, :] = counts
 
-
-def run_pass(info, points, fine_assign, fine, squares, seen, *, pass_index, slots, rows):
+    @pl.loop(0, tiles // 2)
+    def _(i):
+        part = pl.ds(pl.multiple_of(2 * i * tile, 2 * tile), 2 * tile)
+        for slot in range(SLOTS):
+            payload[slot, :rows, :] += jnp.dot(
+                table[:, part], scaled[part, column_of(slot)], preferred_element_type=jnp.float32
+            )
+
+
+def run_pass(info, points, fine_assign, fine, squares, seen, *, pass_index, flip, rows):
     count, width = points.shape
     block_width = width // SLOTS
     tile = 512
-    first = squares is None
+    initial = pass_index == 0
     chained = seen is not None
+    stream = not chained
     whole = pl.BlockSpec(memory_space=pltpu.VMEM)
-    in_specs = [pl.BlockSpec(memory_space=pl.ANY) if first else whole, full(PASSES, count)]
+    anywhere = pl.BlockSpec(memory_space=pl.ANY)
+    in_hbm = lambda value: pltpu.with_memory_space_constraint(value, pltpu.HBM)
+    in_specs = [
+        anywhere if stream else whole,
+        anywhere,
+        anywhere if initial else full(SLOTS, rows, block_width),
+    ]
     args = [
-        pltpu.with_memory_space_constraint(points, pltpu.HBM if first else pltpu.VMEM),
-        fine_assign,
+        in_hbm(points) if stream else pltpu.with_memory_space_constraint(points, pltpu.VMEM),
+        in_hbm(fine_assign),
+        in_hbm(fine) if initial else fine,
     ]
-    if slots:
-        in_specs.append(full(SLOTS, rows, block_width))
-    else:
-        in_specs.append(pl.BlockSpec((rows, width), lambda i, info: (info[1], 0)))
-    args.append(fine)
-    if not first:
+    if squares is not None:
         in_specs.append(full(1, count))
         args.append(squares)
     if chained:
         in_specs.append(full(2, count))
         args.append(seen)
-    shapes = [(SLOTS, rows + TAIL, block_width), (2, count)] + ([(1, count)] if first else [])
+    shapes = [(SLOTS, rows + TAIL, block_width), (2, count)]
+    if squares is None:
+        shapes.append((1, count))
     out_shape = [jax.ShapeDtypeStruct(shape, jnp.float32) for shape in shapes]
     out_specs = [full(*shape) for shape in shapes]
     scratch = [
         pltpu.VMEM((rows, width), jnp.bfloat16),
-        pltpu.VMEM((rows, width), jnp.float32),
         pltpu.VMEM((rows, 128), jnp.float32),
         pltpu.VMEM((rows, tile), jnp.float32),
         pltpu.VMEM((rows, tile), jnp.float32),
-        pltpu.VMEM((tile, width), jnp.bfloat16),
+        pltpu.VMEM((count, width), jnp.bfloat16),
+        pltpu.VMEM((rows, count), jnp.bfloat16),
+        pltpu.VMEM((PASSES, count), jnp.int32),
+        pltpu.SemaphoreType.DMA((2,)),
     ]
-    if first:
+    if initial:
+        scratch.append(pltpu.VMEM((rows, width), jnp.float32))
+    if stream:
         out_shape.append(pltpu.VMEM(points.shape, points.dtype))
         out_specs.append(whole)
         scratch.append(pltpu.SemaphoreType.DMA((count // tile,)))
     body = functools.partial(
         pass_body,
         pass_index=pass_index,
-        slots=slots,
-        first=first,
+        flip=flip,
+        stream=stream,
         chained=chained,
         tile=tile,
     )
@@ -261,7 +294,7 @@
             out_specs=out_specs,
             scratch_shapes=scratch,
         ),
-        compiler_params=pltpu.CompilerParams(vmem_limit_bytes=24 * 2**20),
+        compiler_params=pltpu.CompilerParams(vmem_limit_bytes=28 * 2**20),
         cost_estimate=pl.CostEstimate(
             flops=4 * rows * count * width, bytes_accessed=2 * count * width, transcendentals=0
         ),
@@ -269,10 +302,11 @@
     )(info, *args)
 
 
-def refine_body(info, own, sibling, over_x, over_y, over_xy, owner, coarse, fine, part):
+def refine_body(info, own, sibling, x_top, x_low, y_top, y_low, tail, owner, coarse, *outs):
+    top, low, part = outs
     rows = owner.shape[1]
-    received = own[...] + sibling[...] + over_x[...] + over_y[...] + over_xy[...]
-    totals, counts_row = received[:rows], received[rows:]
+    mid = rows // 2
+    counts_row = tail[...] + y_top[mid:, :]
     counts = as_column(counts_row[:1], rows)[:, :1]
     table = (
         lax.broadcasted_iota(jnp.int32, (NC, rows), 0) == owner[...]
@@ -284,9 +318,13 @@
         precision=HIGHEST,
         preferred_element_type=jnp.float32,
     )
+    totals = own[:rows, :] + sibling[:rows, :] + jnp.concatenate(
+        [x_top[...] + y_top[:mid, :], x_low[...] + y_low[...]], 0
+    )
     new = (totals + prior_weight * lookup) / (counts + prior_weight)
-    fine[...] = new
-    prior = jnp.where(info[0] == 0, prior_weight, 0.0)
+    top[...] = new[:mid]
+    low[...] = new[mid:]
+    prior = jnp.where(info[3] == 0, prior_weight, 0.0)
     part[:NC, :] = prior * coarse[...] + jnp.dot(
         table, counts * new, precision=HIGHEST, preferred_element_type=jnp.float32
     )
@@ -300,27 +338,64 @@
     )
 
 
-def refine_half(info, own, sibling, over_x, over_y, over_xy, owner, coarse):
-    block_width = coarse.shape[1]
-    rows = owner.shape[1]
+def refine_half(info, own, sibling, incoming, owners, coarse, *, flip):
+    _, rows, block_width = own.shape
+    rows -= TAIL
+    mid = rows // 2
     slot = pl.BlockSpec((None, rows + TAIL, block_width), lambda i, info: (0, 0, 0))
+    wide = coarse.shape[1] != block_width
     return pl.pallas_call(
         refine_body,
         out_shape=[
-            jax.ShapeDtypeStruct((rows, block_width), jnp.float32),
+            jax.ShapeDtypeStruct((mid, block_width), jnp.float32),
+            jax.ShapeDtypeStruct((mid, block_width), jnp.float32),
             jax.ShapeDtypeStruct((NC + TAIL, block_width), jnp.float32),
         ],
         grid_spec=pltpu.PrefetchScalarGridSpec(
             num_scalar_prefetch=1,
             grid=(1,),
             in_specs=[slot] * 2
-            + [full(rows + TAIL, block_width)] * 3
-            + [full(1, rows), full(NC, block_width)],
-            out_specs=[full(rows, block_width), full(NC + TAIL, block_width)],
+            + [full(*value.shape) for value in incoming]
+            + [
+                pl.BlockSpec((None, 1, rows), lambda i, info: (info[1] ^ flip, 0, 0)),
+                pl.BlockSpec((NC, block_width), lambda i, info: (0, info[0] if wide else 0)),
+            ],
+            out_specs=[
+                full(mid, block_width),
+                full(mid, block_width),
+                full(NC + TAIL, block_width),
+            ],
         ),
         compiler_params=pltpu.CompilerParams(vmem_limit_bytes=16 * 2**20),
         name="refine_half",
-    )(info, own, sibling, over_x, over_y, over_xy, owner, coarse)
+    )(info, own, sibling, *incoming, owners, coarse)
+
+
+def exchange(held, sibling):
+    rows = held.shape[1] - TAIL
+    mid = rows // 2
+    top, low, tail = slice(0, mid), slice(mid, rows), slice(rows, rows + TAIL)
+    both = lambda slot, part: held[slot, part] + sibling[slot, part]
+    counts = both(0, tail)
+    corner_top = swap(jnp.concatenate([both(3, top), counts], 0), ACROSS_X)
+    corner_low = swap(both(3, low), ACROSS_Y)
+    x_top = swap(both(1, top), ACROSS_X)
+    y_low = swap(both(2, low), ACROSS_Y)
+    counts = counts + corner_top[mid:]
+    y_top = swap(jnp.concatenate([both(2, top) + corner_top[:mid], counts], 0), ACROSS_Y)
+    x_low = swap(both(1, low) + corner_low, ACROSS_X)
+    return x_top, x_low, y_top, y_low, counts
+
+
+def gather_half(top, low):
+    x_low = swap(low, ACROSS_X)
+    y_top = swap(top, ACROSS_Y)
+    x_top = swap(top, ACROSS_X)
+    y_low = swap(low, ACROSS_Y)
+    corner_top = swap(y_top, ACROSS_X)
+    corner_low = swap(x_low, ACROSS_Y)
+    blocks = [(top, low), (x_top, x_low), (y_top, y_low), (corner_top, corner_low)]
+    return [jnp.concatenate(block, 0) for block in blocks]
 
 
 def spread(value):
@@ -333,34 +408,37 @@
     return functools.reduce(combine, others, value)
 
 
-def place_body(info, own, other, fine_out, coarse_out):
-    block_width = own.shape[2]
-    rows = fine_out.shape[0]
+def place_body(info, *refs):
+    own, other = refs[:2], refs[2:4]
+    parts, others_parts, fine_out, coarse_out = refs[4:]
+    block_width = parts.shape[2]
     here = info[0]
+
+    def column_of(slot):
+        return pl.ds(pl.multiple_of((here ^ slot) * block_width, block_width), block_width)
 
     def put(pieces):
         for slot in range(SLOTS):
-            column = pl.multiple_of((here ^ slot) * block_width, block_width)
-            fine_out[:, pl.ds(column, block_width)] = pieces[slot, :rows, :]
+            fine_out[:, column_of(slot)] = pieces[slot // 2][slot % 2]
 
     @pl.when(pl.program_id(0) == 0)
     def _():
         put(own)
-        weight = own[0, rows + NC : rows + NC + 1, :128] + other[0, rows + NC : rows + NC + 1, :128]
+        weight = parts[0, NC : NC + 1, :128] + others_parts[0, NC : NC + 1, :128]
         weight = as_column(weight, 128)[:NC, :1]
         for slot in range(SLOTS):
-            column = pl.multiple_of((here ^ slot) * block_width, block_width)
-            total = own[slot, rows : rows + NC, :] + other[slot, rows : rows + NC, :]
-            coarse_out[:, pl.ds(column, block_width)] = total / weight
+            total = parts[slot, :NC, :] + others_parts[slot, :NC, :]
+            coarse_out[:, column_of(slot)] = total / weight
 
     @pl.when(pl.program_id(0) == 1)
     def _():
         put(other)
 
 
-def place(info, own, other, rows):
-    _, _, block_width = own.shape
+def place(info, own, other, parts, others_parts, *, flip):
+    _, rows, block_width = own[0].shape
     width = SLOTS * block_width
+    args = [*own, *other, parts, others_parts]
     return pl.pallas_call(
         place_body,
         out_shape=[
@@ -370,15 +448,15 @@
         grid_spec=pltpu.PrefetchScalarGridSpec(
             num_scalar_prefetch=1,
             grid=(2,),
-            in_specs=[full(*own.shape), full(*other.shape)],
+            in_specs=[full(*value.shape) for value in args],
             out_specs=[
-                pl.BlockSpec((rows, width), lambda i, info: (info[1] ^ i, 0)),
+                pl.BlockSpec((rows, width), lambda i, info: (info[1] ^ flip ^ i, 0)),
                 full(NC, width),
             ],
         ),
         compiler_params=pltpu.CompilerParams(vmem_limit_bytes=24 * 2**20),
         name="place_blocks",
-    )(info, own, other)
+    )(info, *args)
 
 
 def on_device_paired(points, fine_assign, fine_start, coarse_start, coarse_assign):
@@ -386,60 +464,43 @@
     local_count = fine_start.shape[0]
     rows = local_count // 2
     block_width = width // SLOTS
-    cen = lax.axis_index("cen")
-    offset = cen * local_count
-    me = lax.axis_index("pts")
-    core, here = me & 1, me >> 1
+    cen, me = lax.axis_index("cen"), lax.axis_index("pts")
+    core = me & 1
+    info = jnp.stack([me >> 1, core, cen * local_count, cen * 2 + core]).astype(jnp.int32)
     owners = coarse_assign.reshape(2, 1, rows)
-    owner_of = lambda half: lax.dynamic_index_in_dim(owners, half, 0, keepdims=False)
-    info_of = lambda half: jnp.stack([here, half, offset + half * rows]).astype(jnp.int32)
-    group_place = jnp.stack([cen * 2 + core]).astype(jnp.int32)
-    coarse = lax.dynamic_slice_in_dim(coarse_start, here * block_width, block_width, 1)
-
-    def exchange(held, sibling):
-        outgoing = [held[s] + sibling[s] for s in range(1, SLOTS)]
-        over_xy = swap(outgoing[2], ACROSS_X | ACROSS_Y)
-        return swap(outgoing[0], ACROSS_X), swap(outgoing[1], ACROSS_Y), over_xy
-
-    first_pass = functools.partial(run_pass, pass_index=0, slots=False, rows=rows)
-    sent, seen, squares, kept = first_pass(
-        info_of(1 - core), points, fine_assign, fine_start, None, None
-    )
+
+    call = functools.partial(run_pass, info, pass_index=0, rows=rows)
+    sent, seen, squares, kept = call(points, fine_assign, fine_start, None, None, flip=1)
     sibling = swap(sent, CORE)
-    held, seen_first = first_pass(
-        info_of(core), kept, fine_assign, fine_start, squares, seen
-    )
+    held, seen_first = call(kept, fine_assign, fine_start, squares, seen, flip=0)
     incoming = exchange(held, sibling)
-    fine, part = refine_half(group_place, held, sibling, *incoming, owner_of(core), coarse)
-    own = jnp.stack(spread(fine))
+    top, low, part = refine_half(info, held, sibling, incoming, owners, coarse_start, flip=0)
+    own = jnp.stack(gather_half(top, low))
     part = part + swap(part, CORE)
-
-    second_pass = functools.partial(run_pass, pass_index=1, slots=True, rows=rows)
     own, part = lax.optimization_barrier((own, part))
     other = swap(own, CORE)
-    sent, seen = second_pass(info_of(core), kept, fine_assign, own, squares, None)
+
+    call = functools.partial(run_pass, info, pass_index=1, rows=rows)
+    sent, seen, kept = call(points, fine_assign, own, squares, None, flip=0)
     sibling = swap(sent, CORE)
-    held, seen_second = second_pass(info_of(1 - core), kept, fine_assign, other, squares, seen)
+    held, seen_second = call(kept, fine_assign, other, squares, seen, flip=1)
     incoming = exchange(held, sibling)
 
     seen = jnp.concatenate([seen_first, seen_second], 0)
-    cen_size = lax.axis_size("cen")
     folded = jnp.concatenate([part, seen.reshape(-1, block_width)], 0)
-    gathered = [folded] + [swap(folded, bit, "cen") for bit in range(1, cen_size)]
+    gathered = [folded] + [swap(folded, bit, "cen") for bit in range(1, lax.axis_size("cen"))]
     part = functools.reduce(jnp.add, [each[: NC + TAIL] for each in gathered])
     seen = functools.reduce(jnp.minimum, [each[NC + TAIL :] for each in gathered])
     seen = seen.reshape(2, 2, -1)
     gaps = (seen[:, 0] - seen[:, 1]) / math.sqrt(width)
     coarse = part[:NC] / part[NC, :NC][:, None]
 
-    fine, part = refine_half(
-        group_place, held, sibling, *incoming, owner_of(1 - core), coarse
-    )
-    own = spread(fine)
-    parts = spread(over_cen(part, jnp.add))
-    own = jnp.stack([jnp.concatenate(pair, 0) for pair in zip(own, parts)])
-    other = swap(own, CORE)
-    fine_now, coarse_now = place(info_of(1 - core), own, other, rows)
+    top, low, part = refine_half(info, held, sibling, incoming, owners, coarse, flip=1)
+    own = gather_half(top, low)
+    own = [jnp.stack(own[:2]), jnp.stack(own[2:])]
+    parts = jnp.stack(spread(over_cen(part, jnp.add)))
+    other = [swap(pair, CORE) for pair in own]
+    fine_now, coarse_now = place(info, own, other, parts, swap(parts, CORE), flip=1)
     return (fine_now, coarse_now, gaps)
 
 

time: 127 us -> 132 us (1.039)
  waiting for transfers between devices: 47.2 us -> 33.9 us
  starting transfers between devices: 28.3 us -> 40.8 us
  Pallas kernels: 42.3 us -> 49.8 us
  local copies, waits for them, and re-layouts: 5.93 us -> 1.44 us
  other arithmetic: 2.24 us -> 4.97 us
    ppermute x26 -> x40, waiting for transfers between devices: 47.2 us -> 33.9 us  [swap(): return lax.ppermute(value, axis, [(i, i ^ bit) for i in range(size)])]
    ppermute x26 -> x40, starting transfers between devices: 28.3 us -> 40.8 us  [swap(): return lax.ppermute(value, axis, [(i, i ^ bit) for i in range(size)])]
    pallas_call x4, Pallas kernels: 38.2 us -> 44.6 us  [run_pass(): pl.pallas_call(body, out_shape=out_shape, grid_spec=pltpu.PrefetchScalarG...]
    unnamed x19 -> x9, local copies, waits for them, and re-layouts: 5.76 us -> 0.66 us
  transfers between devices with their start and end apart: 26 -> 40, of which waited for: 13 -> 19; matrix products, arithmetic and copies ran while one was open for 1% -> 5% of each run, Pallas kernels for 21% -> 24%
where the time goes in v5:
time: 132 us
  Pallas kernels  49.8 us (38%)
  starting transfers between devices  40.8 us (31%)
  waiting for transfers between devices  33.9 us (26%)
  other arithmetic  4.97 us (4%)
  local copies, waits for them, and re-layouts  1.44 us (1%)
    pallas_call x4, Pallas kernels, run_pass(): pl.pallas_call(body, out_shape=out_shape, grid_spec=pltpu.PrefetchScalarG...  44.6 us
    ppermute x40, starting transfers between devices, swap(): return lax.ppermute(value, axis, [(i, i ^ bit) for i in range(size)])  40.8 us
    ppermute x40, waiting for transfers between devices, swap(): return lax.ppermute(value, axis, [(i, i ^ bit) for i in range(size)])  33.9 us
    pallas_call x2, Pallas kernels, refine_half(): pl.pallas_call(refine_body, out_shape=[jax.ShapeDtypeStruct((mid, block_w...  3.03 us
  transfers between devices with their start and end apart: 40, of which 19 were waited for; matrix products, arithmetic and copies ran while one was open for 5% of the time, Pallas kernels for 24%

profile of v5, /device:TPU:0, one launch (start us, length us, event | category | flops | bytes accessed | tf_op | source)
XLA Modules:
  0.0 132.0 jit_solution(12647074396817243976)
XLA Ops:
  0.7 12.8 %energies_and_sums_00.1 = (f32[4,264,256]{2,1,0:T(8,128)S(1)}, f32[2,4096]{1,0:T(2,128)S(1)}, f32[1,4096]{1,0:T(1,128)S(1)}, bf16[4096,1024]{1,0:T(8,128)(2,1)S(1)}) custom-call(s32[4]{0:T(128)S(1)} %pad_add_fusion.info, bf16[4096,1024]{1,0:T(8,128)(2,1)} %points.3, s32[2,4096]{1,0:T(2,128)} %assign.7, f32[512,1024]{1,0:T(8,128)} %fine.3), custom_call_target="tpu_custom_call" | custom-call | flops 4294967296 | bytes 8388608 | tf_op jit(solution)/shard_map/energies_and_sums_00/pallas_call | solution.py:287
  13.5 0.5 collective-permute-start
  14.0 10.7 %energies_and_sums_01.1 = (f32[4,264,256]{2,1,0:T(8,128)S(1)}, f32[2,4096]{1,0:T(2,128)S(1)}) custom-call(s32[4]{0:T(128)S(1)} %pad_add_fusion.info, bf16[4096,1024]{1,0:T(8,128)(2,1)S(1)} %get-tuple-element.24.points, s32[2,4096]{1,0:T(2,128)} %assign.7, f32[512,1024]{1,0:T(8,128)} %fine.3, f32[1,4096]{1,0:T(1,128)S(1)} %get-tuple-element.25.refs_0_, ...), custom_call_target="tpu_custom_call" | custom-call | flops 4294967296 | bytes 8388608 | tf_op jit(solution)/shard_map/energies_and_sums_01/pallas_call | solution.py:287
  24.9 2.5 %collective-permute-start.4 = (f32[136,256]{1,0:T(8,128)S(1)}, f32[136,256]{1,0:T(8,128)S(1)}, u32[]{:S(2)}, u32[]{:S(2)}) collective-permute-start(f32[136,256]{1,0:T(8,128)S(1)} %pad_maximum_fusion.4), channel_id=1, source_target_pairs={{0,8},{4,12},{8,0},{12,4},{16,24},{20,28},{24,16},{28,20},{1,9},{5... | collective-permute-start | bytes 417800 | tf_op jit(solution)/shard_map/ppermute | solution.py:89
  27.4 1.5 %collective-permute-start.2 = (f32[128,256]{1,0:T(8,128)S(1)}, f32[128,256]{1,0:T(8,128)S(1)}, u32[]{:S(2)}, u32[]{:S(2)}) collective-permute-start(f32[128,256]{1,0:T(8,128)S(1)} %get-tuple-element.53), channel_id=1, source_target_pairs={{0,16},{4,20},{8,24},{12,28},{16,0},{20,4},{24,8},{28,12},{1,17},{... | collective-permute-start | bytes 393224 | tf_op jit(solution)/shard_map/ppermute | solution.py:89
  28.9 2.8 %collective-permute-done.4 = f32[136,256]{1,0:T(8,128)S(1)} collective-permute-done((f32[136,256]{1,0:T(8,128)S(1)}, f32[136,256]{1,0:T(8,128)S(1)}, u32[]{:S(2)}, u32[]{:S(2)}) %collective-permute-start.4) | collective-permute-done | bytes 139296 | tf_op jit(solution)/shard_map/ppermute | solution.py:89
  31.8 1.3 collective-permute-done.2
  33.1 1.6 %collective-permute-start.5 = (f32[136,256]{1,0:T(8,128)S(1)}, f32[136,256]{1,0:T(8,128)S(1)}, u32[]{:S(2)}, u32[]{:S(2)}) collective-permute-start(f32[136,256]{1,0:T(8,128)S(1)} %pad_maximum_fusion.5), channel_id=1, source_target_pairs={{0,16},{4,20},{8,24},{12,28},{16,0},{20,4},{24,8},{28,12},{1,17},{... | collective-permute-start | bytes 417800 | tf_op jit(solution)/shard_map/ppermute | solution.py:89
  35.2 0.5 collective-permute-start.6
  35.7 1.6 %collective-permute-start.3 = (f32[128,256]{1,0:T(8,128)S(1)}, f32[128,256]{1,0:T(8,128)S(1)}, u32[]{:S(2)}, u32[]{:S(2)}) collective-permute-start(f32[128,256]{1,0:T(8,128)S(1)} %get-tuple-element.56), channel_id=1, source_target_pairs={{0,8},{4,12},{8,0},{12,4},{16,24},{20,28},{24,16},{28,20},{1,9},{5... | collective-permute-start | bytes 393224 | tf_op jit(solution)/shard_map/ppermute | solution.py:89
  37.2 3.4 %collective-permute-done.1.x_top = f32[128,256]{1,0:T(8,128)S(1)} collective-permute-done((f32[128,256]{1,0:T(8,128)S(1)}, f32[128,256]{1,0:T(8,128)S(1)}, u32[]{:S(2)}, u32[]{:S(2)}) %collective-permute-start.1) | collective-permute-done | bytes 131104 | tf_op jit(solution)/shard_map/ppermute | solution.py:89
  41.0 0.9 collective-permute-done.3.x_low
  42.0 1.5 %refine_half.2 = (f32[128,256]{1,0:T(8,128)S(1)}, f32[128,256]{1,0:T(8,128)S(1)}, f32[72,256]{1,0:T(8,128)S(1)}) custom-call(s32[4]{0:T(128)S(1)} %pad_add_fusion.info, f32[4,264,256]{2,1,0:T(8,128)S(1)} %get-tuple-element.27.own, f32[4,264,256]{2,1,0:T(8,128)S(1)} %collective-permute-done.sibling, f32[128,256]{1,0:T(8,128)S(1)} %collective-permute-done.1.x_top, ...), custom_call_target="tpu_custom_call" | custom-call | tf_op jit(solution)/shard_map/refine_half/pallas_call | solution.py:347
  43.5 0.9 collective-permute-start.9
  44.4 0.8 collective-permute-start.8
  45.2 1.2 collective-permute-start.7
  46.4 1.2 collective-permute-start.10
  47.6 1.2 collective-permute-done.13
  48.9 0.6 collective-permute-done.9
  49.5 0.8 collective-permute-start.11
  50.3 1.1 collective-permute-start.12
  51.5 3.0 %collective-permute-done.11 = f32[128,256]{1,0:T(8,128)S(1)} collective-permute-done((f32[128,256]{1,0:T(8,128)S(1)}, f32[128,256]{1,0:T(8,128)S(1)}, u32[]{:S(2)}, u32[]{:S(2)}) %collective-permute-start.11) | collective-permute-done | bytes 131104 | tf_op jit(solution)/shard_map/ppermute | solution.py:89
  54.5 0.7 collective-permute-done.12
  55.5 11.0 %energies_and_sums_10.1 = (f32[4,264,256]{2,1,0:T(8,128)S(1)}, f32[2,4096]{1,0:T(2,128)S(1)}, bf16[4096,1024]{1,0:T(8,128)(2,1)S(1)}) custom-call(s32[4]{0:T(128)S(1)} %pad_add_fusion.info, bf16[4096,1024]{1,0:T(8,128)(2,1)} %points.3, s32[2,4096]{1,0:T(2,128)} %assign.7, f32[4,256,256]{2,1,0:T(8,128)S(1)} %pad_maximum_fusion.fine, ...), custom_call_target="tpu_custom_call" | custom-call | flops 4294967296 | bytes 8388608 | tf_op jit(solution)/shard_map/energies_and_sums_10/pallas_call | solution.py:287
  66.5 0.6 collective-permute-start.15
  67.0 0.6 constant_dynamic-update-slice_fusion.1
  67.7 10.1 %energies_and_sums_11.1 = (f32[4,264,256]{2,1,0:T(8,128)S(1)}, f32[2,4096]{1,0:T(2,128)S(1)}) custom-call(s32[4]{0:T(128)S(1)} %pad_add_fusion.info, bf16[4096,1024]{1,0:T(8,128)(2,1)S(1)} %get-tuple-element.33.points, s32[2,4096]{1,0:T(2,128)} %assign.7, f32[4,256,256]{2,1,0:T(8,128)S(1)} %collective-permute-done.14.fine, ...), custom_call_target="tpu_custom_call" | custom-call | flops 4294967296 | bytes 8388608 | tf_op jit(solution)/shard_map/energies_and_sums_11/pallas_call | solution.py:287
  77.9 0.6 constant_dynamic-update-slice_fusion
  78.5 1.7 %collective-permute-start.22 = (f32[136,256]{1,0:T(8,128)}, f32[136,256]{1,0:T(8,128)S(1)}, u32[]{:S(2)}, u32[]{:S(2)}) collective-permute-start(f32[136,256]{1,0:T(8,128)} %constant_dynamic-update-slice_fusion), channel_id=1, source_target_pairs={{0,1},{1,0},{2,3},{3,2},{4,5},{5,4},{6,7},{7,6},{8,9},{9,8},{10,11... | collective-permute-start | bytes 417800 | tf_op jit(solution)/shard_map/ppermute | solution.py:89
  80.2 2.6 %collective-permute-start.23 = (f32[136,256]{1,0:T(8,128)}, f32[136,256]{1,0:T(8,128)}, u32[]{:S(2)}, u32[]{:S(2)}) collective-permute-start(f32[136,256]{1,0:T(8,128)} %constant_dynamic-update-slice_fusion), channel_id=1, source_target_pairs={{0,2},{1,3},{2,0},{3,1},{4,6},{5,7},{6,4},{7,5},{8,10},{9,11},{10,... | collective-permute-start | bytes 417800 | tf_op jit(solution)/shard_map/ppermute | solution.py:89
  82.9 0.7 fusion
  83.7 1.3 collective-permute-start.19
  85.0 0.8 collective-permute-start.17
  85.7 0.6 collective-permute-done.22
  86.3 1.3 collective-permute-start.16
  87.6 6.4 %collective-permute-done.23 = f32[136,256]{1,0:T(8,128)} collective-permute-done((f32[136,256]{1,0:T(8,128)}, f32[136,256]{1,0:T(8,128)}, u32[]{:S(2)}, u32[]{:S(2)}) %collective-permute-start.23) | collective-permute-done | bytes 139296 | tf_op jit(solution)/shard_map/ppermute | solution.py:89
  94.0 0.9 collective-permute-start.21
  94.9 0.9 slice_minimum_fusion
  95.9 0.9 slice_add_fusion.14
  96.9 1.0 slice_add_fusion.1
  97.9 1.2 collective-permute-start.20
  99.1 1.1 collective-permute-start.18
  100.3 3.7 %collective-permute-done.18.x_low = f32[128,256]{1,0:T(8,128)S(1)} collective-permute-done((f32[128,256]{1,0:T(8,128)S(1)}, f32[128,256]{1,0:T(8,128)S(1)}, u32[]{:S(2)}, u32[]{:S(2)}) %collective-permute-start.18) | collective-permute-done | bytes 131104 | tf_op jit(solution)/shard_map/ppermute | solution.py:89
  104.1 1.5 %refine_half.3 = (f32[128,256]{1,0:T(8,128)S(1)}, f32[128,256]{1,0:T(8,128)S(1)}, f32[72,256]{1,0:T(8,128)S(1)}) custom-call(s32[4]{0:T(128)S(1)} %pad_add_fusion.info, f32[4,264,256]{2,1,0:T(8,128)S(1)} %get-tuple-element.35.own, f32[4,264,256]{2,1,0:T(8,128)S(1)} %collective-permute-done.15.sibling, f32[128,256]{1,0:T(8,128)S(1)} %collective-permute-done.16.x_top, ...), custom_call_target="tpu_custom_call" | custom-call | tf_op jit(solution)/shard_map/refine_half/pallas_call | solution.py:347
  105.6 1.2 collective-permute-start.33
  106.8 1.7 %collective-permute-start.34 = (f32[72,256]{1,0:T(8,128)S(1)}, f32[72,256]{1,0:T(8,128)S(1)}, u32[]{:S(2)}, u32[]{:S(2)}) collective-permute-start(f32[72,256]{1,0:T(8,128)S(1)} %get-tuple-element.42), channel_id=1, source_target_pairs={{0,2},{1,3},{2,0},{3,1},{4,6},{5,7},{6,4},{7,5},{8,10},{9,11},{10,... | collective-permute-start | bytes 221192 | tf_op jit(solution)/shard_map/ppermute | solution.py:89
  108.5 1.4 %collective-permute-start.35 = (f32[72,256]{1,0:T(8,128)S(1)}, f32[72,256]{1,0:T(8,128)S(1)}, u32[]{:S(2)}, u32[]{:S(2)}) collective-permute-start(f32[72,256]{1,0:T(8,128)S(1)} %get-tuple-element.42), channel_id=1, source_target_pairs={{0,3},{1,2},{2,1},{3,0},{4,7},{5,6},{6,5},{7,4},{8,11},{9,10},{10,... | collective-permute-start | bytes 221192 | tf_op jit(solution)/shard_map/ppermute | solution.py:89
  110.0 0.9 collective-permute-start.27
  110.9 1.1 collective-permute-start.28
  112.0 1.1 collective-permute-start.26
  113.2 0.9 collective-permute-start.25
  114.1 0.6 collective-permute-done.35
  114.7 1.2 collective-permute-start.36
  115.9 1.4 %collective-permute-done.26 = f32[128,256]{1,0:T(8,128)S(1)} collective-permute-done((f32[128,256]{1,0:T(8,128)S(1)}, f32[128,256]{1,0:T(8,128)S(1)}, u32[]{:S(2)}, u32[]{:S(2)}) %collective-permute-start.26) | collective-permute-done | bytes 131104 | tf_op jit(solution)/shard_map/ppermute | solution.py:89
  117.3 1.2 collective-permute-start.37
  118.5 1.6 %collective-permute-done.25 = f32[128,256]{1,0:T(8,128)S(1)} collective-permute-done((f32[128,256]{1,0:T(8,128)S(1)}, f32[128,256]{1,0:T(8,128)S(1)}, u32[]{:S(2)}, u32[]{:S(2)}) %collective-permute-start.25) | collective-permute-done | bytes 131104 | tf_op jit(solution)/shard_map/ppermute | solution.py:89
  120.1 1.1 collective-permute-start.38
  121.3 1.5 %collective-permute-start.30 = (f32[128,256]{1,0:T(8,128)S(1)}, f32[128,256]{1,0:T(8,128)S(1)}, u32[]{:S(2)}, u32[]{:S(2)}) collective-permute-start(f32[128,256]{1,0:T(8,128)S(1)} %collective-permute-done.26), channel_id=1, source_target_pairs={{0,16},{4,20},{8,24},{12,28},{16,0},{20,4},{24,8},{28,12},{1,17},{... | collective-permute-start | bytes 393224 | tf_op jit(solution)/shard_map/ppermute | solution.py:89
  122.8 0.9 collective-permute-start.29
  123.9 1.5 %collective-permute-done.38 = f32[72,256]{1,0:T(8,128)S(1)} collective-permute-done((f32[72,256]{1,0:T(8,128)S(1)}, f32[72,256]{1,0:T(8,128)S(1)}, u32[]{:S(2)}, u32[]{:S(2)}) %collective-permute-start.38) | collective-permute-done | bytes 73760 | tf_op jit(solution)/shard_map/ppermute | solution.py:89
  125.5 2.3 %collective-permute-done.29 = f32[128,256]{1,0:T(8,128)S(1)} collective-permute-done((f32[128,256]{1,0:T(8,128)S(1)}, f32[128,256]{1,0:T(8,128)S(1)}, u32[]{:S(2)}, u32[]{:S(2)}) %collective-permute-start.29) | collective-permute-done | bytes 131104 | tf_op jit(solution)/shard_map/ppermute | solution.py:89
  127.9 0.7 fusion.15
  128.6 1.2 collective-permute-done.32.refs_3_
  129.8 2.1 %place_blocks.1 = (f32[512,1024]{1,0:T(8,128)}, f32[64,1024]{1,0:T(8,128)}) custom-call(s32[4]{0:T(128)S(1)} %pad_add_fusion.info, f32[2,256,256]{2,1,0:T(8,128)S(1)} %pad_maximum_fusion.1.refs_0_, f32[2,256,256]{2,1,0:T(8,128)S(1)} %pad_maximum_fusion.2.refs_1_, f32[2,256,256]{2,1,0:T(8,128)S(1)} %collective-permute-done.31.refs_2_, ...), custom_call_target="tpu_custom_call" | custom-call | tf_op jit(solution)/shard_map/place_blocks/pallas_call | solution.py:442
  (69 shorter events, 2.4 us)
Async XLA Ops:
  13.5 11.3 %collective-permute-start = (f32[4,264,256]{2,1,0:T(8,128)S(1)}, f32[4,264,256]{2,1,0:T(8,128)S(1)}, u32[]{:S(2)}, u32[]{:S(2)}) collective-permute-start(f32[4,264,256]{2,1,0:T(8,128)S(1)} %get-tuple-element.28), channel_id=1, source_target_pairs={{0,4},{4,0},{8,12},{12,8},{16,20},{20,16},{24,28},{28,24},{1,5},{5... | collective-permute-start | bytes 3244040 | tf_op jit(solution)/shard_map/ppermute | solution.py:89
  24.9 17.1 %copy-start = (f32[64,1024]{1,0:T(8,128)S(1)}, f32[64,1024]{1,0:T(8,128)}, u32[]{:S(2)}) copy-start(f32[64,1024]{1,0:T(8,128)} %coarse.1) | copy-start | bytes 786436
  24.9 17.1 %copy-start.1 = (s32[512]{0:T(512)S(1)}, s32[512]{0:T(512)}, u32[]{:S(2)}) copy-start(s32[512]{0:T(512)} %param.9) | copy-start | bytes 6148
  24.9 6.8 %collective-permute-start.4 = (f32[136,256]{1,0:T(8,128)S(1)}, f32[136,256]{1,0:T(8,128)S(1)}, u32[]{:S(2)}, u32[]{:S(2)}) collective-permute-start(f32[136,256]{1,0:T(8,128)S(1)} %pad_maximum_fusion.4), channel_id=1, source_target_pairs={{0,8},{4,12},{8,0},{12,4},{16,24},{20,28},{24,16},{28,20},{1,9},{5... | collective-permute-start | bytes 417800 | tf_op jit(solution)/shard_map/ppermute | solution.py:89
  27.4 5.6 %collective-permute-start.2 = (f32[128,256]{1,0:T(8,128)S(1)}, f32[128,256]{1,0:T(8,128)S(1)}, u32[]{:S(2)}, u32[]{:S(2)}) collective-permute-start(f32[128,256]{1,0:T(8,128)S(1)} %get-tuple-element.53), channel_id=1, source_target_pairs={{0,16},{4,20},{8,24},{12,28},{16,0},{20,4},{24,8},{28,12},{1,17},{... | collective-permute-start | bytes 393224 | tf_op jit(solution)/shard_map/ppermute | solution.py:89
  33.1 8.9 %collective-permute-start.5 = (f32[136,256]{1,0:T(8,128)S(1)}, f32[136,256]{1,0:T(8,128)S(1)}, u32[]{:S(2)}, u32[]{:S(2)}) collective-permute-start(f32[136,256]{1,0:T(8,128)S(1)} %pad_maximum_fusion.5), channel_id=1, source_target_pairs={{0,16},{4,20},{8,24},{12,28},{16,0},{20,4},{24,8},{28,12},{1,17},{... | collective-permute-start | bytes 417800 | tf_op jit(solution)/shard_map/ppermute | solution.py:89
  34.7 5.9 %collective-permute-start.1 = (f32[128,256]{1,0:T(8,128)S(1)}, f32[128,256]{1,0:T(8,128)S(1)}, u32[]{:S(2)}, u32[]{:S(2)}) collective-permute-start(f32[128,256]{1,0:T(8,128)S(1)} %get-tuple-element.54), channel_id=1, source_target_pairs={{0,8},{4,12},{8,0},{12,4},{16,24},{20,28},{24,16},{28,20},{1,9},{5... | collective-permute-start | bytes 393224 | tf_op jit(solution)/shard_map/ppermute | solution.py:89
  35.2 5.9 %collective-permute-start.6 = (f32[128,256]{1,0:T(8,128)S(1)}, f32[128,256]{1,0:T(8,128)S(1)}, u32[]{:S(2)}, u32[]{:S(2)}) collective-permute-start(f32[128,256]{1,0:T(8,128)S(1)} %get-tuple-element.51), channel_id=1, source_target_pairs={{0,16},{4,20},{8,24},{12,28},{16,0},{20,4},{24,8},{28,12},{1,17},{... | collective-permute-start | bytes 393224 | tf_op jit(solution)/shard_map/ppermute | solution.py:89
  35.7 6.3 %collective-permute-start.3 = (f32[128,256]{1,0:T(8,128)S(1)}, f32[128,256]{1,0:T(8,128)S(1)}, u32[]{:S(2)}, u32[]{:S(2)}) collective-permute-start(f32[128,256]{1,0:T(8,128)S(1)} %get-tuple-element.56), channel_id=1, source_target_pairs={{0,8},{4,12},{8,0},{12,4},{16,24},{20,28},{24,16},{28,20},{1,9},{5... | collective-permute-start | bytes 393224 | tf_op jit(solution)/shard_map/ppermute | solution.py:89
  43.5 6.0 %collective-permute-start.9 = (f32[128,256]{1,0:T(8,128)S(1)}, f32[128,256]{1,0:T(8,128)S(1)}, u32[]{:S(2)}, u32[]{:S(2)}) collective-permute-start(f32[128,256]{1,0:T(8,128)S(1)} %get-tuple-element.29), channel_id=1, source_target_pairs={{0,16},{4,20},{8,24},{12,28},{16,0},{20,4},{24,8},{28,12},{1,17},{... | collective-permute-start | bytes 393224 | tf_op jit(solution)/shard_map/ppermute | solution.py:89
  44.4 5.9 %collective-permute-start.8 = (f32[128,256]{1,0:T(8,128)S(1)}, f32[128,256]{1,0:T(8,128)S(1)}, u32[]{:S(2)}, u32[]{:S(2)}) collective-permute-start(f32[128,256]{1,0:T(8,128)S(1)} %get-tuple-element.30), channel_id=1, source_target_pairs={{0,8},{4,12},{8,0},{12,4},{16,24},{20,28},{24,16},{28,20},{1,9},{5... | collective-permute-start | bytes 393224 | tf_op jit(solution)/shard_map/ppermute | solution.py:89
  45.2 6.2 %collective-permute-start.7 = (f32[128,256]{1,0:T(8,128)S(1)}, f32[128,256]{1,0:T(8,128)S(1)}, u32[]{:S(2)}, u32[]{:S(2)}) collective-permute-start(f32[128,256]{1,0:T(8,128)S(1)} %get-tuple-element.29), channel_id=1, source_target_pairs={{0,8},{4,12},{8,0},{12,4},{16,24},{20,28},{24,16},{28,20},{1,9},{5... | collective-permute-start | bytes 393224 | tf_op jit(solution)/shard_map/ppermute | solution.py:89
  46.4 5.0 %collective-permute-start.10 = (f32[128,256]{1,0:T(8,128)S(1)}, f32[128,256]{1,0:T(8,128)S(1)}, u32[]{:S(2)}, u32[]{:S(2)}) collective-permute-start(f32[128,256]{1,0:T(8,128)S(1)} %get-tuple-element.30), channel_id=1, source_target_pairs={{0,16},{4,20},{8,24},{12,28},{16,0},{20,4},{24,8},{28,12},{1,17},{... | collective-permute-start | bytes 393224 | tf_op jit(solution)/shard_map/ppermute | solution.py:89
  47.6 1.3 collective-permute-start.13
  48.9 18.2 %copy-start.2 = (f32[72,256]{1,0:T(8,128)}, f32[72,256]{1,0:T(8,128)S(1)}, u32[]{:S(2)}) copy-start(f32[72,256]{1,0:T(8,128)S(1)} %add.144) | copy-start | bytes 221188
  49.5 5.0 %collective-permute-start.11 = (f32[128,256]{1,0:T(8,128)S(1)}, f32[128,256]{1,0:T(8,128)S(1)}, u32[]{:S(2)}, u32[]{:S(2)}) collective-permute-start(f32[128,256]{1,0:T(8,128)S(1)} %collective-permute-done.9), channel_id=1, source_target_pairs={{0,8},{4,12},{8,0},{12,4},{16,24},{20,28},{24,16},{28,20},{1,9},{5... | collective-permute-start | bytes 393224 | tf_op jit(solution)/shard_map/ppermute | solution.py:89
  50.3 5.0 %collective-permute-start.12 = (f32[128,256]{1,0:T(8,128)S(1)}, f32[128,256]{1,0:T(8,128)S(1)}, u32[]{:S(2)}, u32[]{:S(2)}) collective-permute-start(f32[128,256]{1,0:T(8,128)S(1)} %collective-permute-done.8), channel_id=1, source_target_pairs={{0,16},{4,20},{8,24},{12,28},{16,0},{20,4},{24,8},{28,12},{1,17},{... | collective-permute-start | bytes 393224 | tf_op jit(solution)/shard_map/ppermute | solution.py:89
  55.4 12.3 %collective-permute-start.14 = (f32[4,256,256]{2,1,0:T(8,128)S(1)}, f32[4,256,256]{2,1,0:T(8,128)S(1)}, u32[]{:S(2)}, u32[]{:S(2)}) collective-permute-start(f32[4,256,256]{2,1,0:T(8,128)S(1)} %pad_maximum_fusion.fine), channel_id=1, source_target_pairs={{0,4},{4,0},{8,12},{12,8},{16,20},{20,16},{24,28},{28,24},{1,5},{5... | collective-permute-start | bytes 3145736 | tf_op jit(solution)/shard_map/ppermute | solution.py:89
  66.5 16.4 %collective-permute-start.15 = (f32[4,264,256]{2,1,0:T(8,128)S(1)}, f32[4,264,256]{2,1,0:T(8,128)S(1)}, u32[]{:S(2)}, u32[]{:S(2)}) collective-permute-start(f32[4,264,256]{2,1,0:T(8,128)S(1)} %get-tuple-element.36), channel_id=1, source_target_pairs={{0,4},{4,0},{8,12},{12,8},{16,20},{20,16},{24,28},{28,24},{1,5},{5... | collective-permute-start | bytes 3244040 | tf_op jit(solution)/shard_map/ppermute | solution.py:89
  78.5 7.8 %collective-permute-start.22 = (f32[136,256]{1,0:T(8,128)}, f32[136,256]{1,0:T(8,128)S(1)}, u32[]{:S(2)}, u32[]{:S(2)}) collective-permute-start(f32[136,256]{1,0:T(8,128)} %constant_dynamic-update-slice_fusion), channel_id=1, source_target_pairs={{0,1},{1,0},{2,3},{3,2},{4,5},{5,4},{6,7},{7,6},{8,9},{9,8},{10,11... | collective-permute-start | bytes 417800 | tf_op jit(solution)/shard_map/ppermute | solution.py:89
  80.2 13.8 %collective-permute-start.23 = (f32[136,256]{1,0:T(8,128)}, f32[136,256]{1,0:T(8,128)}, u32[]{:S(2)}, u32[]{:S(2)}) collective-permute-start(f32[136,256]{1,0:T(8,128)} %constant_dynamic-update-slice_fusion), channel_id=1, source_target_pairs={{0,2},{1,3},{2,0},{3,1},{4,6},{5,7},{6,4},{7,5},{8,10},{9,11},{10,... | collective-permute-start | bytes 417800 | tf_op jit(solution)/shard_map/ppermute | solution.py:89
  82.8 12.1 %collective-permute-start.24 = (f32[136,256]{1,0:T(8,128)}, f32[136,256]{1,0:T(8,128)}, u32[]{:S(2)}, u32[]{:S(2)}) collective-permute-start(f32[136,256]{1,0:T(8,128)} %constant_dynamic-update-slice_fusion), channel_id=1, source_target_pairs={{0,3},{1,2},{2,1},{3,0},{4,7},{5,6},{6,5},{7,4},{8,11},{9,10},{10,... | collective-permute-start | bytes 417800 | tf_op jit(solution)/shard_map/ppermute | solution.py:89
  82.9 13.0 %copy-start.3 = (f32[72,256]{1,0:T(8,128)S(1)}, f32[72,256]{1,0:T(8,128)}, u32[]{:S(2)}) copy-start(f32[72,256]{1,0:T(8,128)} %copy-done.2) | copy-start | bytes 221188
  83.7 13.2 %collective-permute-start.19 = (f32[136,256]{1,0:T(8,128)S(1)}, f32[136,256]{1,0:T(8,128)S(1)}, u32[]{:S(2)}, u32[]{:S(2)}) collective-permute-start(f32[136,256]{1,0:T(8,128)S(1)} %pad_maximum_fusion.6), channel_id=1, source_target_pairs={{0,8},{4,12},{8,0},{12,4},{16,24},{20,28},{24,16},{28,20},{1,9},{5... | collective-permute-start | bytes 417800 | tf_op jit(solution)/shard_map/ppermute | solution.py:89
  85.0 11.9 %collective-permute-start.17 = (f32[128,256]{1,0:T(8,128)}, f32[128,256]{1,0:T(8,128)}, u32[]{:S(2)}, u32[]{:S(2)}) collective-permute-start(f32[128,256]{1,0:T(8,128)} %get-tuple-element.47), channel_id=1, source_target_pairs={{0,16},{4,20},{8,24},{12,28},{16,0},{20,4},{24,8},{28,12},{1,17},{... | collective-permute-start | bytes 393224 | tf_op jit(solution)/shard_map/ppermute | solution.py:89
  86.3 13.9 %collective-permute-start.16 = (f32[128,256]{1,0:T(8,128)S(1)}, f32[128,256]{1,0:T(8,128)S(1)}, u32[]{:S(2)}, u32[]{:S(2)}) collective-permute-start(f32[128,256]{1,0:T(8,128)S(1)} %get-tuple-element.48), channel_id=1, source_target_pairs={{0,8},{4,12},{8,0},{12,4},{16,24},{20,28},{24,16},{28,20},{1,9},{5... | collective-permute-start | bytes 393224 | tf_op jit(solution)/shard_map/ppermute | solution.py:89
  94.0 6.3 %collective-permute-start.21 = (f32[128,256]{1,0:T(8,128)S(1)}, f32[128,256]{1,0:T(8,128)S(1)}, u32[]{:S(2)}, u32[]{:S(2)}) collective-permute-start(f32[128,256]{1,0:T(8,128)S(1)} %get-tuple-element.45), channel_id=1, source_target_pairs={{0,16},{4,20},{8,24},{12,28},{16,0},{20,4},{24,8},{28,12},{1,17},{... | collective-permute-start | bytes 393224 | tf_op jit(solution)/shard_map/ppermute | solution.py:89
  97.9 6.2 %collective-permute-start.20 = (f32[136,256]{1,0:T(8,128)S(1)}, f32[136,256]{1,0:T(8,128)S(1)}, u32[]{:S(2)}, u32[]{:S(2)}) collective-permute-start(f32[136,256]{1,0:T(8,128)S(1)} %pad_maximum_fusion.7), channel_id=1, source_target_pairs={{0,16},{4,20},{8,24},{12,28},{16,0},{20,4},{24,8},{28,12},{1,17},{... | collective-permute-start | bytes 417800 | tf_op jit(solution)/shard_map/ppermute | solution.py:89
  99.1 5.0 %collective-permute-start.18 = (f32[128,256]{1,0:T(8,128)S(1)}, f32[128,256]{1,0:T(8,128)S(1)}, u32[]{:S(2)}, u32[]{:S(2)}) collective-permute-start(f32[128,256]{1,0:T(8,128)S(1)} %get-tuple-element.50), channel_id=1, source_target_pairs={{0,8},{4,12},{8,0},{12,4},{16,24},{20,28},{24,16},{28,20},{1,9},{5... | collective-permute-start | bytes 393224 | tf_op jit(solution)/shard_map/ppermute | solution.py:89
  105.6 6.4 %collective-permute-start.33 = (f32[72,256]{1,0:T(8,128)S(1)}, f32[72,256]{1,0:T(8,128)S(1)}, u32[]{:S(2)}, u32[]{:S(2)}) collective-permute-start(f32[72,256]{1,0:T(8,128)S(1)} %get-tuple-element.42), channel_id=1, source_target_pairs={{0,1},{1,0},{2,3},{3,2},{4,5},{5,4},{6,7},{7,6},{8,9},{9,8},{10,11... | collective-permute-start | bytes 221192 | tf_op jit(solution)/shard_map/ppermute | solution.py:89
  106.8 6.4 %collective-permute-start.34 = (f32[72,256]{1,0:T(8,128)S(1)}, f32[72,256]{1,0:T(8,128)S(1)}, u32[]{:S(2)}, u32[]{:S(2)}) collective-permute-start(f32[72,256]{1,0:T(8,128)S(1)} %get-tuple-element.42), channel_id=1, source_target_pairs={{0,2},{1,3},{2,0},{3,1},{4,6},{5,7},{6,4},{7,5},{8,10},{9,11},{10,... | collective-permute-start | bytes 221192 | tf_op jit(solution)/shard_map/ppermute | solution.py:89
  108.5 6.2 %collective-permute-start.35 = (f32[72,256]{1,0:T(8,128)S(1)}, f32[72,256]{1,0:T(8,128)S(1)}, u32[]{:S(2)}, u32[]{:S(2)}) collective-permute-start(f32[72,256]{1,0:T(8,128)S(1)} %get-tuple-element.42), channel_id=1, source_target_pairs={{0,3},{1,2},{2,1},{3,0},{4,7},{5,6},{6,5},{7,4},{8,11},{9,10},{10,... | collective-permute-start | bytes 221192 | tf_op jit(solution)/shard_map/ppermute | solution.py:89
  110.0 11.3 %collective-permute-start.27 = (f32[128,256]{1,0:T(8,128)S(1)}, f32[128,256]{1,0:T(8,128)S(1)}, u32[]{:S(2)}, u32[]{:S(2)}) collective-permute-start(f32[128,256]{1,0:T(8,128)S(1)} %get-tuple-element.40), channel_id=1, source_target_pairs={{0,16},{4,20},{8,24},{12,28},{16,0},{20,4},{24,8},{28,12},{1,17},{... | collective-permute-start | bytes 393224 | tf_op jit(solution)/shard_map/ppermute | solution.py:89
  110.9 11.9 %collective-permute-start.28 = (f32[128,256]{1,0:T(8,128)S(1)}, f32[128,256]{1,0:T(8,128)S(1)}, u32[]{:S(2)}, u32[]{:S(2)}) collective-permute-start(f32[128,256]{1,0:T(8,128)S(1)} %get-tuple-element.41), channel_id=1, source_target_pairs={{0,16},{4,20},{8,24},{12,28},{16,0},{20,4},{24,8},{28,12},{1,17},{... | collective-permute-start | bytes 393224 | tf_op jit(solution)/shard_map/ppermute | solution.py:89
  112.0 5.3 %collective-permute-start.26 = (f32[128,256]{1,0:T(8,128)S(1)}, f32[128,256]{1,0:T(8,128)S(1)}, u32[]{:S(2)}, u32[]{:S(2)}) collective-permute-start(f32[128,256]{1,0:T(8,128)S(1)} %get-tuple-element.41), channel_id=1, source_target_pairs={{0,8},{4,12},{8,0},{12,4},{16,24},{20,28},{24,16},{28,20},{1,9},{5... | collective-permute-start | bytes 393224 | tf_op jit(solution)/shard_map/ppermute | solution.py:89
  113.2 6.9 %collective-permute-start.25 = (f32[128,256]{1,0:T(8,128)S(1)}, f32[128,256]{1,0:T(8,128)S(1)}, u32[]{:S(2)}, u32[]{:S(2)}) collective-permute-start(f32[128,256]{1,0:T(8,128)S(1)} %get-tuple-element.40), channel_id=1, source_target_pairs={{0,8},{4,12},{8,0},{12,4},{16,24},{20,28},{24,16},{28,20},{1,9},{5... | collective-permute-start | bytes 393224 | tf_op jit(solution)/shard_map/ppermute | solution.py:89
  114.7 9.1 %collective-permute-start.36 = (f32[72,256]{1,0:T(8,128)S(1)}, f32[72,256]{1,0:T(8,128)S(1)}, u32[]{:S(2)}, u32[]{:S(2)}) collective-permute-start(f32[72,256]{1,0:T(8,128)S(1)} %add_add_fusion), channel_id=1, source_target_pairs={{0,8},{4,12},{8,0},{12,4},{16,24},{20,28},{24,16},{28,20},{1,9},{5... | collective-permute-start | bytes 221192 | tf_op jit(solution)/shard_map/ppermute | solution.py:89
  117.3 6.6 %collective-permute-start.37 = (f32[72,256]{1,0:T(8,128)S(1)}, f32[72,256]{1,0:T(8,128)S(1)}, u32[]{:S(2)}, u32[]{:S(2)}) collective-permute-start(f32[72,256]{1,0:T(8,128)S(1)} %add_add_fusion), channel_id=1, source_target_pairs={{0,16},{4,20},{8,24},{12,28},{16,0},{20,4},{24,8},{28,12},{1,17},{... | collective-permute-start | bytes 221192 | tf_op jit(solution)/shard_map/ppermute | solution.py:89
  120.1 5.3 %collective-permute-start.38 = (f32[72,256]{1,0:T(8,128)S(1)}, f32[72,256]{1,0:T(8,128)S(1)}, u32[]{:S(2)}, u32[]{:S(2)}) collective-permute-start(f32[72,256]{1,0:T(8,128)S(1)} %add_add_fusion), channel_id=1, source_target_pairs={{0,24},{4,28},{8,16},{12,20},{16,8},{20,12},{24,0},{28,4},{1,25},{... | collective-permute-start | bytes 221192 | tf_op jit(solution)/shard_map/ppermute | solution.py:89
  121.3 6.5 %collective-permute-start.30 = (f32[128,256]{1,0:T(8,128)S(1)}, f32[128,256]{1,0:T(8,128)S(1)}, u32[]{:S(2)}, u32[]{:S(2)}) collective-permute-start(f32[128,256]{1,0:T(8,128)S(1)} %collective-permute-done.26), channel_id=1, source_target_pairs={{0,16},{4,20},{8,24},{12,28},{16,0},{20,4},{24,8},{28,12},{1,17},{... | collective-permute-start | bytes 393224 | tf_op jit(solution)/shard_map/ppermute | solution.py:89
  122.8 5.0 %collective-permute-start.29 = (f32[128,256]{1,0:T(8,128)S(1)}, f32[128,256]{1,0:T(8,128)S(1)}, u32[]{:S(2)}, u32[]{:S(2)}) collective-permute-start(f32[128,256]{1,0:T(8,128)S(1)} %collective-permute-done.27), channel_id=1, source_target_pairs={{0,8},{4,12},{8,0},{12,4},{16,24},{20,28},{24,16},{28,20},{1,9},{5... | collective-permute-start | bytes 393224 | tf_op jit(solution)/shard_map/ppermute | solution.py:89
  123.8 4.8 %collective-permute-start.31 = (f32[2,256,256]{2,1,0:T(8,128)S(1)}, f32[2,256,256]{2,1,0:T(8,128)S(1)}, u32[]{:S(2)}, u32[]{:S(2)}) collective-permute-start(f32[2,256,256]{2,1,0:T(8,128)S(1)} %pad_maximum_fusion.1.refs_0_), channel_id=1, source_target_pairs={{0,4},{4,0},{8,12},{12,8},{16,20},{20,16},{24,28},{28,24},{1,5},{5... | collective-permute-start | bytes 1572872 | tf_op jit(solution)/shard_map/ppermute | solution.py:89
  125.4 3.2 %collective-permute-start.39 = (f32[4,72,256]{2,1,0:T(8,128)S(1)}, f32[4,72,256]{2,1,0:T(8,128)S(1)}, u32[]{:S(2)}, u32[]{:S(2)}) collective-permute-start(f32[4,72,256]{2,1,0:T(8,128)S(1)} %pad_maximum_fusion.3.refs_4_), channel_id=1, source_target_pairs={{0,4},{4,0},{8,12},{12,8},{16,20},{20,16},{24,28},{28,24},{1,5},{5... | collective-permute-start | bytes 884744 | tf_op jit(solution)/shard_map/ppermute | solution.py:89
  127.8 2.0 %collective-permute-start.32 = (f32[2,256,256]{2,1,0:T(8,128)S(1)}, f32[2,256,256]{2,1,0:T(8,128)S(1)}, u32[]{:S(2)}, u32[]{:S(2)}) collective-permute-start(f32[2,256,256]{2,1,0:T(8,128)S(1)} %pad_maximum_fusion.2.refs_1_), channel_id=1, source_target_pairs={{0,4},{4,0},{8,12},{12,8},{16,20},{20,16},{24,28},{28,24},{1,5},{5... | collective-permute-start | bytes 1572872 | tf_op jit(solution)/shard_map/ppermute | solution.py:89

commit v6 on v5

--- a/solution.py
+++ b/solution.py
@@ -106,8 +106,9 @@
     payload, seen = refs.pop(0), refs.pop(0)
     squares_out = refs.pop(0) if first else None
     kept = refs.pop(0) if stream else points
-    low, tallies, even, odd, scaled, table, chosen_in, small_sems = refs[:8]
-    start = refs[8] if initial else None
+    low, norms, tallies, sums, chosen_in, small_sems = refs[:6]
+    products, factors, tables, scaleds = refs[6:8], refs[8:10], refs[10:12], refs[12:14]
+    start = refs[14] if initial else None
     point_sems = refs[-1] if stream else None
     rows, width = low.shape
     block_width = width // SLOTS
@@ -151,15 +152,17 @@
             block = fine[slot]
             norm = norm + jnp.sum(block * block, axis=1, keepdims=True)
             low[:, column_of(slot)] = (-2.0 * block).astype(jnp.bfloat16)
+    norms[...] = jnp.broadcast_to(norm, norms.shape)
     tallies[...] = jnp.zeros_like(tallies)
-
-    def multiply(i, target):
-        target[...] = lax.dot_general(
+    sums[...] = jnp.zeros_like(sums)
+
+    def multiply(i, odd):
+        products[odd][...] = lax.dot_general(
             low[...], kept[span(i), :], (((1,), (1,)), ((), ())), preferred_element_type=jnp.float32
         )
 
-    def weigh(i, products):
-        energy = norm + products[...]
+    def weigh(i, odd):
+        energy = products[odd][...] + jnp.concatenate([norms[...]] * (tile // 128), axis=1)
         chosen = chosen_in[pass_index : pass_index + 1, span(i)] - base
         member = lax.broadcasted_iota(jnp.int32, energy.shape, 0) == chosen
         picked = jnp.sum(jnp.where(member, energy, 0.0), axis=0, keepdims=True)
@@ -186,47 +189,47 @@
         for lane in range(0, tile, 128):
             tally = tally + weighted[:, lane : lane + 128]
         tallies[...] = tally
-        factor = as_column(weights, tile)
+        factors[odd][...] = as_column(weights, tile)
+        tables[odd][...] = member.astype(jnp.float32).astype(jnp.bfloat16)
+
+    def collect(i, odd):
+        factor = factors[odd][...]
         for lane in range(0, width, 128):
             values = kept[span(i), lane : lane + 128].astype(jnp.float32)
-            scaled[span(i), lane : lane + 128] = (values * factor).astype(jnp.bfloat16)
-        table[:, span(i)] = member.astype(jnp.float32).astype(jnp.bfloat16)
+            scaleds[odd][:, lane : lane + 128] = (values * factor).astype(jnp.bfloat16)
+        sums[...] += jnp.dot(
+            tables[odd][...], scaleds[odd][...], preferred_element_type=jnp.float32
+        )
 
     load_assign.wait()
     if stream:
         load(0).wait()
-    multiply(0, even)
+        load(1).wait()
+    multiply(0, 0)
+    multiply(1, 1)
+    weigh(0, 0)
 
     @pl.loop(0, tiles // 2 - 1)
     def _(pair):
-        i = 2 * pair
+        i = 2 * pair + 1
         if stream:
             load(i + 1).wait()
             load(i + 2).wait()
-        multiply(i + 1, odd)
-        weigh(i, even)
-        multiply(i + 2, even)
-        weigh(i + 1, odd)
-
-    if stream:
-        load(tiles - 1).wait()
-    multiply(tiles - 1, odd)
-    weigh(tiles - 2, even)
-    weigh(tiles - 1, odd)
+        multiply(i + 1, 0)
+        collect(i - 1, 0)
+        weigh(i, 1)
+        multiply(i + 2, 1)
+        collect(i, 1)
+        weigh(i + 1, 0)
+
+    collect(tiles - 2, 0)
+    weigh(tiles - 1, 1)
+    collect(tiles - 1, 1)
 
     counts = jnp.broadcast_to(jnp.sum(tallies[...].T, axis=0, keepdims=True), (TAIL, rows))
-
     for slot in range(SLOTS):
-        payload[slot, :rows, :] = jnp.zeros((rows, block_width), jnp.float32)
+        payload[slot, :rows, :] = sums[:, column_of(slot)]
         payload[slot, rows:, :] = counts
-
-    @pl.loop(0, tiles // 2)
-    def _(i):
-        part = pl.ds(pl.multiple_of(2 * i * tile, 2 * tile), 2 * tile)
-        for slot in range(SLOTS):
-            payload[slot, :rows, :] += jnp.dot(
-                table[:, part], scaled[part, column_of(slot)], preferred_element_type=jnp.float32
-            )
 
 
 def run_pass(info, points, fine_assign, fine, squares, seen, *, pass_index, flip, rows):
@@ -263,13 +266,18 @@
     scratch = [
         pltpu.VMEM((rows, width), jnp.bfloat16),
         pltpu.VMEM((rows, 128), jnp.float32),
-        pltpu.VMEM((rows, tile), jnp.float32),
-        pltpu.VMEM((rows, tile), jnp.float32),
-        pltpu.VMEM((count, width), jnp.bfloat16),
-        pltpu.VMEM((rows, count), jnp.bfloat16),
+        pltpu.VMEM((rows, 128), jnp.float32),
+        pltpu.VMEM((rows, width), jnp.float32),
         pltpu.VMEM((PASSES, count), jnp.int32),
         pltpu.SemaphoreType.DMA((2,)),
     ]
+    for shape, kind in (
+        ((rows, tile), jnp.float32),
+        ((tile, 128), jnp.float32),
+        ((rows, tile), jnp.bfloat16),
+        ((tile, width), jnp.bfloat16),
+    ):
+        scratch += [pltpu.VMEM(shape, kind)] * 2
     if initial:
         scratch.append(pltpu.VMEM((rows, width), jnp.float32))
     if stream:
@@ -302,11 +310,11 @@
     )(info, *args)
 
 
-def refine_body(info, own, sibling, x_top, x_low, y_top, y_low, tail, owner, coarse, *outs):
+def refine_body(info, own, sibling, over_x, over_y, tail, owner, coarse, *outs):
     top, low, part = outs
     rows = owner.shape[1]
     mid = rows // 2
-    counts_row = tail[...] + y_top[mid:, :]
+    counts_row = tail[...] + over_y[rows:, :]
     counts = as_column(counts_row[:1], rows)[:, :1]
     table = (
         lax.broadcasted_iota(jnp.int32, (NC, rows), 0) == owner[...]
@@ -318,9 +326,7 @@
         precision=HIGHEST,
         preferred_element_type=jnp.float32,
     )
-    totals = own[:rows, :] + sibling[:rows, :] + jnp.concatenate(
-        [x_top[...] + y_top[:mid, :], x_low[...] + y_low[...]], 0
-    )
+    totals = (own[:rows, :] + sibling[:rows, :]) + (over_x[...] + over_y[:rows, :])
     new = (totals + prior_weight * lookup) / (counts + prior_weight)
     top[...] = new[:mid]
     low[...] = new[mid:]
@@ -379,12 +385,12 @@
     counts = both(0, tail)
     corner_top = swap(jnp.concatenate([both(3, top), counts], 0), ACROSS_X)
     corner_low = swap(both(3, low), ACROSS_Y)
-    x_top = swap(both(1, top), ACROSS_X)
-    y_low = swap(both(2, low), ACROSS_Y)
     counts = counts + corner_top[mid:]
-    y_top = swap(jnp.concatenate([both(2, top) + corner_top[:mid], counts], 0), ACROSS_Y)
-    x_low = swap(both(1, low) + corner_low, ACROSS_X)
-    return x_top, x_low, y_top, y_low, counts
+    over_y = swap(
+        jnp.concatenate([both(2, top) + corner_top[:mid], both(2, low), counts], 0), ACROSS_Y
+    )
+    over_x = swap(jnp.concatenate([both(1, top), both(1, low) + corner_low], 0), ACROSS_X)
+    return over_x, over_y, counts
 
 
 def gather_half(top, low):
@@ -486,13 +492,10 @@
     held, seen_second = call(kept, fine_assign, other, squares, seen, flip=1)
     incoming = exchange(held, sibling)
 
-    seen = jnp.concatenate([seen_first, seen_second], 0)
-    folded = jnp.concatenate([part, seen.reshape(-1, block_width)], 0)
+    folded = jnp.concatenate([part, seen_first.reshape(-1, block_width)], 0)
     gathered = [folded] + [swap(folded, bit, "cen") for bit in range(1, lax.axis_size("cen"))]
     part = functools.reduce(jnp.add, [each[: NC + TAIL] for each in gathered])
-    seen = functools.reduce(jnp.minimum, [each[NC + TAIL :] for each in gathered])
-    seen = seen.reshape(2, 2, -1)
-    gaps = (seen[:, 0] - seen[:, 1]) / math.sqrt(width)
+    seen_first = functools.reduce(jnp.minimum, [each[NC + TAIL :] for each in gathered])
     coarse = part[:NC] / part[NC, :NC][:, None]
 
     top, low, part = refine_half(info, held, sibling, incoming, owners, coarse, flip=1)
@@ -501,6 +504,11 @@
     parts = jnp.stack(spread(over_cen(part, jnp.add)))
     other = [swap(pair, CORE) for pair in own]
     fine_now, coarse_now = place(info, own, other, parts, swap(parts, CORE), flip=1)
+
+    seen_first = seen_first.reshape(2, -1)
+    seen_second = over_cen(seen_second, jnp.minimum)
+    gaps = [(seen[0] - seen[1]) / math.sqrt(width) for seen in (seen_first, seen_second)]
+    gaps = jnp.stack(gaps)
     return (fine_now, coarse_now, gaps)
 
 

time: 132 us -> 124 us (0.939)
  Pallas kernels: 49.8 us -> 46.2 us
  other arithmetic: 4.97 us -> 1.66 us
  waiting for transfers between devices: 33.9 us -> 32.5 us
  local copies, waits for them, and re-layouts: 1.44 us -> 0.08 us
    pallas_call x4, Pallas kernels: 44.6 us -> 41 us  [run_pass(): pl.pallas_call(body, out_shape=out_shape, grid_spec=pltpu.PrefetchScalarG...]
    ppermute x40 -> x39, waiting for transfers between devices: 33.9 us -> 32.5 us  [swap(): return lax.ppermute(value, axis, [(i, i ^ bit) for i in range(size)])]
    ppermute x40 -> x39, starting transfers between devices: 40.8 us -> 41.9 us  [swap(): return lax.ppermute(value, axis, [(i, i ^ bit) for i in range(size)])]
  transfers between devices with their start and end apart: 40 -> 39, of which waited for: 19 -> 17; matrix products, arithmetic and copies ran while one was open for 5% -> 1% of each run, Pallas kernels for 24% -> 24%
where the time goes in v6:
time: 124 us; the launch traced here: 123 us
  Pallas kernels  46.2 us (37%)
  starting transfers between devices  41.9 us (34%)
  waiting for transfers between devices  32.5 us (26%)
  other arithmetic  1.66 us (1%)
    ppermute x39, starting transfers between devices, swap(): return lax.ppermute(value, axis, [(i, i ^ bit) for i in range(size)])  41.9 us
    pallas_call x4, Pallas kernels, run_pass(): pl.pallas_call(body, out_shape=out_shape, grid_spec=pltpu.PrefetchScalarG...  41 us
    ppermute x39, waiting for transfers between devices, swap(): return lax.ppermute(value, axis, [(i, i ^ bit) for i in range(size)])  32.5 us
    pallas_call x2, Pallas kernels, refine_half(): pl.pallas_call(refine_body, out_shape=[jax.ShapeDtypeStruct((mid, block_w...  3.03 us
  transfers between devices with their start and end apart: 39, of which 17 were waited for; matrix products, arithmetic and copies ran while one was open for 1% of the time, Pallas kernels for 24%

profile of v6, /device:TPU:0, one launch (start us, length us, event | category | flops | bytes accessed | tf_op | source)
XLA Modules:
  0.0 123.4 jit_solution(2125162975882865181)
XLA Ops:
  0.6 0.1 pad_add_fusion.info
  0.7 11.9 %energies_and_sums_00.1 = (f32[4,264,256]{2,1,0:T(8,128)S(1)}, f32[2,4096]{1,0:T(2,128)S(1)}, f32[1,4096]{1,0:T(1,128)S(1)}, bf16[4096,1024]{1,0:T(8,128)(2,1)S(1)}) custom-call(s32[4]{0:T(128)S(1)} %pad_add_fusion.info, bf16[4096,1024]{1,0:T(8,128)(2,1)} %points.3, s32[2,4096]{1,0:T(2,128)} %assign.7, f32[512,1024]{1,0:T(8,128)} %fine.3), custom_call_target="tpu_custom_call" | custom-call | flops 4294967296 | bytes 8388608 | tf_op jit(solution)/shard_map/energies_and_sums_00/pallas_call | solution.py:295
  12.6 0.5 collective-permute-start
  13.1 9.9 %energies_and_sums_01.1 = (f32[4,264,256]{2,1,0:T(8,128)S(1)}, f32[2,4096]{1,0:T(2,128)S(1)}) custom-call(s32[4]{0:T(128)S(1)} %pad_add_fusion.info, bf16[4096,1024]{1,0:T(8,128)(2,1)S(1)} %get-tuple-element.24.points, s32[2,4096]{1,0:T(2,128)} %assign.7, f32[512,1024]{1,0:T(8,128)} %fine.3, f32[1,4096]{1,0:T(1,128)S(1)} %get-tuple-element.25.refs_0_, ...), custom_call_target="tpu_custom_call" | custom-call | flops 4294967296 | bytes 8388608 | tf_op jit(solution)/shard_map/energies_and_sums_01/pallas_call | solution.py:295
  23.0 0.1 fusion.7
  23.1 2.6 %collective-permute-start.3 = (f32[136,256]{1,0:T(8,128)S(1)}, f32[136,256]{1,0:T(8,128)S(1)}, u32[]{:S(2)}, u32[]{:S(2)}) collective-permute-start(f32[136,256]{1,0:T(8,128)S(1)} %pad_maximum_fusion.8), channel_id=1, source_target_pairs={{0,8},{4,12},{8,0},{12,4},{16,24},{20,28},{24,16},{28,20},{1,9},{5... | collective-permute-start | bytes 417800 | tf_op jit(solution)/shard_map/ppermute | solution.py:89
  25.7 1.5 %collective-permute-start.1 = (f32[128,256]{1,0:T(8,128)S(1)}, f32[128,256]{1,0:T(8,128)S(1)}, u32[]{:S(2)}, u32[]{:S(2)}) collective-permute-start(f32[128,256]{1,0:T(8,128)S(1)} %get-tuple-element.55), channel_id=1, source_target_pairs={{0,16},{4,20},{8,24},{12,28},{16,0},{20,4},{24,8},{28,12},{1,17},{... | collective-permute-start | bytes 393224 | tf_op jit(solution)/shard_map/ppermute | solution.py:89
  27.2 2.8 %collective-permute-done.3 = f32[136,256]{1,0:T(8,128)S(1)} collective-permute-done((f32[136,256]{1,0:T(8,128)S(1)}, f32[136,256]{1,0:T(8,128)S(1)}, u32[]{:S(2)}, u32[]{:S(2)}) %collective-permute-start.3) | collective-permute-done | bytes 139296 | tf_op jit(solution)/shard_map/ppermute | solution.py:89
  30.0 1.3 %collective-permute-done.1 = f32[128,256]{1,0:T(8,128)S(1)} collective-permute-done((f32[128,256]{1,0:T(8,128)S(1)}, f32[128,256]{1,0:T(8,128)S(1)}, u32[]{:S(2)}, u32[]{:S(2)}) %collective-permute-start.1) | collective-permute-done | bytes 131104 | tf_op jit(solution)/shard_map/ppermute | solution.py:89
  31.4 1.6 %collective-permute-start.4 = (f32[264,256]{1,0:T(8,128)S(1)}, f32[264,256]{1,0:T(8,128)S(1)}, u32[]{:S(2)}, u32[]{:S(2)}) collective-permute-start(f32[264,256]{1,0:T(8,128)S(1)} %pad_maximum_fusion.4), channel_id=1, source_target_pairs={{0,16},{4,20},{8,24},{12,28},{16,0},{20,4},{24,8},{28,12},{1,17},{... | collective-permute-start | bytes 811016 | tf_op jit(solution)/shard_map/ppermute | solution.py:89
  33.0 0.6 collective-permute-start.2
  33.6 6.8 %collective-permute-done.2.over_x = f32[256,256]{1,0:T(8,128)S(1)} collective-permute-done((f32[256,256]{1,0:T(8,128)S(1)}, f32[256,256]{1,0:T(8,128)S(1)}, u32[]{:S(2)}, u32[]{:S(2)}) %collective-permute-start.2) | collective-permute-done | bytes 262176 | tf_op jit(solution)/shard_map/ppermute | solution.py:89
  40.4 1.5 %refine_half.2 = (f32[128,256]{1,0:T(8,128)S(1)}, f32[128,256]{1,0:T(8,128)S(1)}, f32[72,256]{1,0:T(8,128)S(1)}) custom-call(s32[4]{0:T(128)S(1)} %pad_add_fusion.info, f32[4,264,256]{2,1,0:T(8,128)S(1)} %get-tuple-element.27.own, f32[4,264,256]{2,1,0:T(8,128)S(1)} %collective-permute-done.sibling, f32[256,256]{1,0:T(8,128)S(1)} %collective-permute-done.2.over_x, ...), custom_call_target="tpu_custom_call" | custom-call | tf_op jit(solution)/shard_map/refine_half/pallas_call | solution.py:353
  41.9 0.5 collective-permute-start.7
  42.4 0.8 collective-permute-start.6
  43.2 1.5 %collective-permute-start.8 = (f32[128,256]{1,0:T(8,128)S(1)}, f32[128,256]{1,0:T(8,128)S(1)}, u32[]{:S(2)}, u32[]{:S(2)}) collective-permute-start(f32[128,256]{1,0:T(8,128)S(1)} %get-tuple-element.30), channel_id=1, source_target_pairs={{0,16},{4,20},{8,24},{12,28},{16,0},{20,4},{24,8},{28,12},{1,17},{... | collective-permute-start | bytes 393224 | tf_op jit(solution)/shard_map/ppermute | solution.py:89
  44.8 1.3 %collective-permute-start.5 = (f32[128,256]{1,0:T(8,128)S(1)}, f32[128,256]{1,0:T(8,128)S(1)}, u32[]{:S(2)}, u32[]{:S(2)}) collective-permute-start(f32[128,256]{1,0:T(8,128)S(1)} %get-tuple-element.29), channel_id=1, source_target_pairs={{0,8},{4,12},{8,0},{12,4},{16,24},{20,28},{24,16},{28,20},{1,9},{5... | collective-permute-start | bytes 393224 | tf_op jit(solution)/shard_map/ppermute | solution.py:89
  46.1 1.2 %collective-permute-done.11 = f32[72,256]{1,0:T(8,128)S(1)} collective-permute-done((f32[72,256]{1,0:T(8,128)S(1)}, f32[72,256]{1,0:T(8,128)S(1)}, u32[]{:S(2)}, u32[]{:S(2)}) %collective-permute-start.11) | collective-permute-done | bytes 73760 | tf_op jit(solution)/shard_map/ppermute | solution.py:89
  47.4 0.8 collective-permute-start.9
  48.2 0.8 collective-permute-start.10
  49.1 0.7 collective-permute-done.5
  49.8 3.2 %collective-permute-done.9 = f32[128,256]{1,0:T(8,128)S(1)} collective-permute-done((f32[128,256]{1,0:T(8,128)S(1)}, f32[128,256]{1,0:T(8,128)S(1)}, u32[]{:S(2)}, u32[]{:S(2)}) %collective-permute-start.9) | collective-permute-done | bytes 131104 | tf_op jit(solution)/shard_map/ppermute | solution.py:89
  53.0 0.5 collective-permute-done.10
  53.5 0.1 pad_maximum_fusion.fine
  53.6 3.7 %collective-permute-start.20 = (f32[104,256]{1,0:T(8,128)S(1)}, f32[104,256]{1,0:T(8,128)S(1)}, u32[]{:S(2)}, u32[]{:S(2)}) collective-permute-start(f32[104,256]{1,0:T(8,128)S(1)} %constant_dynamic-update-slice_fusion), channel_id=1, source_target_pairs={{0,3},{1,2},{2,1},{3,0},{4,7},{5,6},{6,5},{7,4},{8,11},{9,10},{10,... | collective-permute-start | bytes 319496 | tf_op jit(solution)/shard_map/ppermute | solution.py:89
  57.3 0.8 collective-permute-start.18
  58.1 10.1 %energies_and_sums_10.1 = (f32[4,264,256]{2,1,0:T(8,128)S(1)}, f32[2,4096]{1,0:T(2,128)S(1)}, bf16[4096,1024]{1,0:T(8,128)(2,1)S(1)}) custom-call(s32[4]{0:T(128)S(1)} %pad_add_fusion.info, bf16[4096,1024]{1,0:T(8,128)(2,1)} %points.3, s32[2,4096]{1,0:T(2,128)} %assign.7, f32[4,256,256]{2,1,0:T(8,128)S(1)} %pad_maximum_fusion.fine, ...), custom_call_target="tpu_custom_call" | custom-call | flops 4294967296 | bytes 8388608 | tf_op jit(solution)/shard_map/energies_and_sums_10/pallas_call | solution.py:295
  68.3 0.6 collective-permute-start.13
  69.0 0.1 slice_divide_fusion.coarse
  69.1 9.2 %energies_and_sums_11.1 = (f32[4,264,256]{2,1,0:T(8,128)S(1)}, f32[2,4096]{1,0:T(2,128)S(1)}) custom-call(s32[4]{0:T(128)S(1)} %pad_add_fusion.info, bf16[4096,1024]{1,0:T(8,128)(2,1)S(1)} %get-tuple-element.33.points, s32[2,4096]{1,0:T(2,128)} %assign.7, f32[4,256,256]{2,1,0:T(8,128)S(1)} %collective-permute-done.12.fine, ...), custom_call_target="tpu_custom_call" | custom-call | flops 4294967296 | bytes 8388608 | tf_op jit(solution)/shard_map/energies_and_sums_11/pallas_call | solution.py:295
  78.2 3.7 %collective-permute-start.38 = (f32[2,4096]{1,0:T(2,128)S(1)}, f32[2,4096]{1,0:T(2,128)S(1)}, u32[]{:S(2)}, u32[]{:S(2)}) collective-permute-start(f32[2,4096]{1,0:T(2,128)S(1)} %get-tuple-element.44), channel_id=1, source_target_pairs={{0,3},{1,2},{2,1},{3,0},{4,7},{5,6},{6,5},{7,4},{8,11},{9,10},{10,... | collective-permute-start | bytes 98312 | tf_op jit(solution)/shard_map/ppermute | solution.py:89
  81.9 0.8 collective-permute-start.36
  82.7 0.1 fusion
  82.7 0.6 collective-permute-start.14
  83.4 1.3 %collective-permute-start.16 = (f32[136,256]{1,0:T(8,128)S(1)}, f32[136,256]{1,0:T(8,128)S(1)}, u32[]{:S(2)}, u32[]{:S(2)}) collective-permute-start(f32[136,256]{1,0:T(8,128)S(1)} %pad_maximum_fusion.9), channel_id=1, source_target_pairs={{0,8},{4,12},{8,0},{12,4},{16,24},{20,28},{24,16},{28,20},{1,9},{5... | collective-permute-start | bytes 417800 | tf_op jit(solution)/shard_map/ppermute | solution.py:89
  84.7 2.0 %collective-permute-done.37 = f32[2,4096]{1,0:T(2,128)S(1)} collective-permute-done((f32[2,4096]{1,0:T(2,128)S(1)}, f32[2,4096]{1,0:T(2,128)S(1)}, u32[]{:S(2)}, u32[]{:S(2)}) %collective-permute-start.37) | collective-permute-done | bytes 32800 | tf_op jit(solution)/shard_map/ppermute | solution.py:89
  86.7 1.0 collective-permute-done.14
  87.8 0.7 collective-permute-done.16
  88.5 0.1 slice_add_fusion.1
  88.6 1.3 %collective-permute-start.15 = (f32[256,256]{1,0:T(8,128)S(1)}, f32[256,256]{1,0:T(8,128)S(1)}, u32[]{:S(2)}, u32[]{:S(2)}) collective-permute-start(f32[256,256]{1,0:T(8,128)S(1)} %pad_maximum_fusion.7), channel_id=1, source_target_pairs={{0,8},{4,12},{8,0},{12,4},{16,24},{20,28},{24,16},{28,20},{1,9},{5... | collective-permute-start | bytes 786440 | tf_op jit(solution)/shard_map/ppermute | solution.py:89
  89.9 1.6 %collective-permute-start.17 = (f32[264,256]{1,0:T(8,128)S(1)}, f32[264,256]{1,0:T(8,128)S(1)}, u32[]{:S(2)}, u32[]{:S(2)}) collective-permute-start(f32[264,256]{1,0:T(8,128)S(1)} %pad_maximum_fusion.5), channel_id=1, source_target_pairs={{0,16},{4,20},{8,24},{12,28},{16,0},{20,4},{24,8},{28,12},{1,17},{... | collective-permute-start | bytes 811016 | tf_op jit(solution)/shard_map/ppermute | solution.py:89
  91.5 3.5 %collective-permute-done.15.over_x = f32[256,256]{1,0:T(8,128)S(1)} collective-permute-done((f32[256,256]{1,0:T(8,128)S(1)}, f32[256,256]{1,0:T(8,128)S(1)}, u32[]{:S(2)}, u32[]{:S(2)}) %collective-permute-start.15) | collective-permute-done | bytes 262176 | tf_op jit(solution)/shard_map/ppermute | solution.py:89
  95.0 1.4 %collective-permute-done.17.over_y = f32[264,256]{1,0:T(8,128)S(1)} collective-permute-done((f32[264,256]{1,0:T(8,128)S(1)}, f32[264,256]{1,0:T(8,128)S(1)}, u32[]{:S(2)}, u32[]{:S(2)}) %collective-permute-start.17) | collective-permute-done | bytes 270368 | tf_op jit(solution)/shard_map/ppermute | solution.py:89
  96.4 1.5 %refine_half.3 = (f32[128,256]{1,0:T(8,128)S(1)}, f32[128,256]{1,0:T(8,128)S(1)}, f32[72,256]{1,0:T(8,128)S(1)}) custom-call(s32[4]{0:T(128)S(1)} %pad_add_fusion.info, f32[4,264,256]{2,1,0:T(8,128)S(1)} %get-tuple-element.35.own, f32[4,264,256]{2,1,0:T(8,128)S(1)} %collective-permute-done.13.sibling, f32[256,256]{1,0:T(8,128)S(1)} %collective-permute-done.15.over_x, ...), custom_call_target="tpu_custom_call" | custom-call | tf_op jit(solution)/shard_map/refine_half/pallas_call | solution.py:353
  98.0 3.6 %collective-permute-start.31 = (f32[72,256]{1,0:T(8,128)S(1)}, f32[72,256]{1,0:T(8,128)S(1)}, u32[]{:S(2)}, u32[]{:S(2)}) collective-permute-start(f32[72,256]{1,0:T(8,128)S(1)} %get-tuple-element.41), channel_id=1, source_target_pairs={{0,3},{1,2},{2,1},{3,0},{4,7},{5,6},{6,5},{7,4},{8,11},{9,10},{10,... | collective-permute-start | bytes 221192 | tf_op jit(solution)/shard_map/ppermute | solution.py:89
  101.6 0.8 collective-permute-start.29
  102.4 1.5 %collective-permute-start.23 = (f32[128,256]{1,0:T(8,128)S(1)}, f32[128,256]{1,0:T(8,128)S(1)}, u32[]{:S(2)}, u32[]{:S(2)}) collective-permute-start(f32[128,256]{1,0:T(8,128)S(1)} %get-tuple-element.39), channel_id=1, source_target_pairs={{0,16},{4,20},{8,24},{12,28},{16,0},{20,4},{24,8},{28,12},{1,17},{... | collective-permute-start | bytes 393224 | tf_op jit(solution)/shard_map/ppermute | solution.py:89
  103.9 0.8 collective-permute-start.21
  104.7 1.3 %collective-permute-start.24 = (f32[128,256]{1,0:T(8,128)S(1)}, f32[128,256]{1,0:T(8,128)S(1)}, u32[]{:S(2)}, u32[]{:S(2)}) collective-permute-start(f32[128,256]{1,0:T(8,128)S(1)} %get-tuple-element.40), channel_id=1, source_target_pairs={{0,16},{4,20},{8,24},{12,28},{16,0},{20,4},{24,8},{28,12},{1,17},{... | collective-permute-start | bytes 393224 | tf_op jit(solution)/shard_map/ppermute | solution.py:89
  106.0 0.8 collective-permute-done.30
  106.8 0.8 collective-permute-start.22
  107.6 2.3 %collective-permute-start.34 = (f32[72,256]{1,0:T(8,128)S(1)}, f32[72,256]{1,0:T(8,128)S(1)}, u32[]{:S(2)}, u32[]{:S(2)}) collective-permute-start(f32[72,256]{1,0:T(8,128)S(1)} %add_add_fusion), channel_id=1, source_target_pairs={{0,24},{4,28},{8,16},{12,20},{16,8},{20,12},{24,0},{28,4},{1,25},{... | collective-permute-start | bytes 221192 | tf_op jit(solution)/shard_map/ppermute | solution.py:89
  109.9 0.5 collective-permute-start.33
  110.4 1.3 %collective-permute-done.24 = f32[128,256]{1,0:T(8,128)S(1)} collective-permute-done((f32[128,256]{1,0:T(8,128)S(1)}, f32[128,256]{1,0:T(8,128)S(1)}, u32[]{:S(2)}, u32[]{:S(2)}) %collective-permute-start.24) | collective-permute-done | bytes 131104 | tf_op jit(solution)/shard_map/ppermute | solution.py:89
  111.7 1.0 collective-permute-start.32
  112.7 1.1 collective-permute-start.25
  113.8 0.8 collective-permute-start.26
  114.7 3.1 %collective-permute-done.25 = f32[128,256]{1,0:T(8,128)S(1)} collective-permute-done((f32[128,256]{1,0:T(8,128)S(1)}, f32[128,256]{1,0:T(8,128)S(1)}, u32[]{:S(2)}, u32[]{:S(2)}) %collective-permute-start.25) | collective-permute-done | bytes 131104 | tf_op jit(solution)/shard_map/ppermute | solution.py:89
  117.8 1.0 collective-permute-done.26
  118.8 0.1 collective-permute-start.28
  119.0 0.5 collective-permute-start.35
  119.5 0.6 pad_maximum_fusion.10
  120.2 1.1 collective-permute-done.35.refs_5_
  121.2 2.2 %place_blocks.1 = (f32[512,1024]{1,0:T(8,128)}, f32[64,1024]{1,0:T(8,128)}) custom-call(s32[4]{0:T(128)S(1)} %pad_add_fusion.info, f32[2,256,256]{2,1,0:T(8,128)S(1)} %pad_maximum_fusion.1.refs_0_, f32[2,256,256]{2,1,0:T(8,128)S(1)} %pad_maximum_fusion.2.refs_1_, f32[2,256,256]{2,1,0:T(8,128)S(1)} %collective-permute-done.27.refs_2_, ...), custom_call_target="tpu_custom_call" | custom-call | tf_op jit(solution)/shard_map/place_blocks/pallas_call | solution.py:448
  (66 shorter events, 0.7 us)
Async XLA Ops:
  12.6 10.4 %collective-permute-start = (f32[4,264,256]{2,1,0:T(8,128)S(1)}, f32[4,264,256]{2,1,0:T(8,128)S(1)}, u32[]{:S(2)}, u32[]{:S(2)}) collective-permute-start(f32[4,264,256]{2,1,0:T(8,128)S(1)} %get-tuple-element.28), channel_id=1, source_target_pairs={{0,4},{4,0},{8,12},{12,8},{16,20},{20,16},{24,28},{28,24},{1,5},{5... | collective-permute-start | bytes 3244040 | tf_op jit(solution)/shard_map/ppermute | solution.py:89
  23.1 17.3 %copy-start = (f32[64,1024]{1,0:T(8,128)S(1)}, f32[64,1024]{1,0:T(8,128)}, u32[]{:S(2)}) copy-start(f32[64,1024]{1,0:T(8,128)} %coarse.1) | copy-start | bytes 786436
  23.1 17.3 %copy-start.1 = (s32[512]{0:T(512)S(1)}, s32[512]{0:T(512)}, u32[]{:S(2)}) copy-start(s32[512]{0:T(512)} %param.9) | copy-start | bytes 6148
  23.1 6.9 %collective-permute-start.3 = (f32[136,256]{1,0:T(8,128)S(1)}, f32[136,256]{1,0:T(8,128)S(1)}, u32[]{:S(2)}, u32[]{:S(2)}) collective-permute-start(f32[136,256]{1,0:T(8,128)S(1)} %pad_maximum_fusion.8), channel_id=1, source_target_pairs={{0,8},{4,12},{8,0},{12,4},{16,24},{20,28},{24,16},{28,20},{1,9},{5... | collective-permute-start | bytes 417800 | tf_op jit(solution)/shard_map/ppermute | solution.py:89
  25.7 5.6 %collective-permute-start.1 = (f32[128,256]{1,0:T(8,128)S(1)}, f32[128,256]{1,0:T(8,128)S(1)}, u32[]{:S(2)}, u32[]{:S(2)}) collective-permute-start(f32[128,256]{1,0:T(8,128)S(1)} %get-tuple-element.55), channel_id=1, source_target_pairs={{0,16},{4,20},{8,24},{12,28},{16,0},{20,4},{24,8},{28,12},{1,17},{... | collective-permute-start | bytes 393224 | tf_op jit(solution)/shard_map/ppermute | solution.py:89
  31.4 9.0 %collective-permute-start.4 = (f32[264,256]{1,0:T(8,128)S(1)}, f32[264,256]{1,0:T(8,128)S(1)}, u32[]{:S(2)}, u32[]{:S(2)}) collective-permute-start(f32[264,256]{1,0:T(8,128)S(1)} %pad_maximum_fusion.4), channel_id=1, source_target_pairs={{0,16},{4,20},{8,24},{12,28},{16,0},{20,4},{24,8},{28,12},{1,17},{... | collective-permute-start | bytes 811016 | tf_op jit(solution)/shard_map/ppermute | solution.py:89
  33.0 7.4 %collective-permute-start.2 = (f32[256,256]{1,0:T(8,128)S(1)}, f32[256,256]{1,0:T(8,128)S(1)}, u32[]{:S(2)}, u32[]{:S(2)}) collective-permute-start(f32[256,256]{1,0:T(8,128)S(1)} %pad_maximum_fusion.6), channel_id=1, source_target_pairs={{0,8},{4,12},{8,0},{12,4},{16,24},{20,28},{24,16},{28,20},{1,9},{5... | collective-permute-start | bytes 786440 | tf_op jit(solution)/shard_map/ppermute | solution.py:89
  41.9 5.4 %collective-permute-start.7 = (f32[128,256]{1,0:T(8,128)S(1)}, f32[128,256]{1,0:T(8,128)S(1)}, u32[]{:S(2)}, u32[]{:S(2)}) collective-permute-start(f32[128,256]{1,0:T(8,128)S(1)} %get-tuple-element.29), channel_id=1, source_target_pairs={{0,16},{4,20},{8,24},{12,28},{16,0},{20,4},{24,8},{28,12},{1,17},{... | collective-permute-start | bytes 393224 | tf_op jit(solution)/shard_map/ppermute | solution.py:89
  42.4 5.8 %collective-permute-start.6 = (f32[128,256]{1,0:T(8,128)S(1)}, f32[128,256]{1,0:T(8,128)S(1)}, u32[]{:S(2)}, u32[]{:S(2)}) collective-permute-start(f32[128,256]{1,0:T(8,128)S(1)} %get-tuple-element.30), channel_id=1, source_target_pairs={{0,8},{4,12},{8,0},{12,4},{16,24},{20,28},{24,16},{28,20},{1,9},{5... | collective-permute-start | bytes 393224 | tf_op jit(solution)/shard_map/ppermute | solution.py:89
  43.2 5.8 %collective-permute-start.8 = (f32[128,256]{1,0:T(8,128)S(1)}, f32[128,256]{1,0:T(8,128)S(1)}, u32[]{:S(2)}, u32[]{:S(2)}) collective-permute-start(f32[128,256]{1,0:T(8,128)S(1)} %get-tuple-element.30), channel_id=1, source_target_pairs={{0,16},{4,20},{8,24},{12,28},{16,0},{20,4},{24,8},{28,12},{1,17},{... | collective-permute-start | bytes 393224 | tf_op jit(solution)/shard_map/ppermute | solution.py:89
  44.8 5.0 %collective-permute-start.5 = (f32[128,256]{1,0:T(8,128)S(1)}, f32[128,256]{1,0:T(8,128)S(1)}, u32[]{:S(2)}, u32[]{:S(2)}) collective-permute-start(f32[128,256]{1,0:T(8,128)S(1)} %get-tuple-element.29), channel_id=1, source_target_pairs={{0,8},{4,12},{8,0},{12,4},{16,24},{20,28},{24,16},{28,20},{1,9},{5... | collective-permute-start | bytes 393224 | tf_op jit(solution)/shard_map/ppermute | solution.py:89
  46.1 1.3 %collective-permute-start.11 = (f32[72,256]{1,0:T(8,128)S(1)}, f32[72,256]{1,0:T(8,128)S(1)}, u32[]{:S(2)}, u32[]{:S(2)}) collective-permute-start(f32[72,256]{1,0:T(8,128)S(1)} %get-tuple-element.31), channel_id=1, source_target_pairs={{0,4},{4,0},{8,12},{12,8},{16,20},{20,16},{24,28},{28,24},{1,5},{5... | collective-permute-start | bytes 221192 | tf_op jit(solution)/shard_map/ppermute | solution.py:89
  47.4 5.6 %collective-permute-start.9 = (f32[128,256]{1,0:T(8,128)S(1)}, f32[128,256]{1,0:T(8,128)S(1)}, u32[]{:S(2)}, u32[]{:S(2)}) collective-permute-start(f32[128,256]{1,0:T(8,128)S(1)} %collective-permute-done.7), channel_id=1, source_target_pairs={{0,8},{4,12},{8,0},{12,4},{16,24},{20,28},{24,16},{28,20},{1,9},{5... | collective-permute-start | bytes 393224 | tf_op jit(solution)/shard_map/ppermute | solution.py:89
  48.2 5.3 %collective-permute-start.10 = (f32[128,256]{1,0:T(8,128)S(1)}, f32[128,256]{1,0:T(8,128)S(1)}, u32[]{:S(2)}, u32[]{:S(2)}) collective-permute-start(f32[128,256]{1,0:T(8,128)S(1)} %collective-permute-done.6), channel_id=1, source_target_pairs={{0,16},{4,20},{8,24},{12,28},{16,0},{20,4},{24,8},{28,12},{1,17},{... | collective-permute-start | bytes 393224 | tf_op jit(solution)/shard_map/ppermute | solution.py:89
  53.6 15.2 %collective-permute-start.20 = (f32[104,256]{1,0:T(8,128)S(1)}, f32[104,256]{1,0:T(8,128)S(1)}, u32[]{:S(2)}, u32[]{:S(2)}) collective-permute-start(f32[104,256]{1,0:T(8,128)S(1)} %constant_dynamic-update-slice_fusion), channel_id=1, source_target_pairs={{0,3},{1,2},{2,1},{3,0},{4,7},{5,6},{6,5},{7,4},{8,11},{9,10},{10,... | collective-permute-start | bytes 319496 | tf_op jit(solution)/shard_map/ppermute | solution.py:89
  57.3 11.5 %collective-permute-start.19 = (f32[104,256]{1,0:T(8,128)S(1)}, f32[104,256]{1,0:T(8,128)S(1)}, u32[]{:S(2)}, u32[]{:S(2)}) collective-permute-start(f32[104,256]{1,0:T(8,128)S(1)} %constant_dynamic-update-slice_fusion), channel_id=1, source_target_pairs={{0,2},{1,3},{2,0},{3,1},{4,6},{5,7},{6,4},{7,5},{8,10},{9,11},{10,... | collective-permute-start | bytes 319496 | tf_op jit(solution)/shard_map/ppermute | solution.py:89
  57.3 11.5 %collective-permute-start.18 = (f32[104,256]{1,0:T(8,128)S(1)}, f32[104,256]{1,0:T(8,128)S(1)}, u32[]{:S(2)}, u32[]{:S(2)}) collective-permute-start(f32[104,256]{1,0:T(8,128)S(1)} %constant_dynamic-update-slice_fusion), channel_id=1, source_target_pairs={{0,1},{1,0},{2,3},{3,2},{4,5},{5,4},{6,7},{7,6},{8,9},{9,8},{10,11... | collective-permute-start | bytes 319496 | tf_op jit(solution)/shard_map/ppermute | solution.py:89
  58.1 11.0 %collective-permute-start.12 = (f32[4,256,256]{2,1,0:T(8,128)S(1)}, f32[4,256,256]{2,1,0:T(8,128)S(1)}, u32[]{:S(2)}, u32[]{:S(2)}) collective-permute-start(f32[4,256,256]{2,1,0:T(8,128)S(1)} %pad_maximum_fusion.fine), channel_id=1, source_target_pairs={{0,4},{4,0},{8,12},{12,8},{16,20},{20,16},{24,28},{28,24},{1,5},{5... | collective-permute-start | bytes 3145736 | tf_op jit(solution)/shard_map/ppermute | solution.py:89
  68.3 14.4 %collective-permute-start.13 = (f32[4,264,256]{2,1,0:T(8,128)S(1)}, f32[4,264,256]{2,1,0:T(8,128)S(1)}, u32[]{:S(2)}, u32[]{:S(2)}) collective-permute-start(f32[4,264,256]{2,1,0:T(8,128)S(1)} %get-tuple-element.36), channel_id=1, source_target_pairs={{0,4},{4,0},{8,12},{12,8},{16,20},{20,16},{24,28},{28,24},{1,5},{5... | collective-permute-start | bytes 3244040 | tf_op jit(solution)/shard_map/ppermute | solution.py:89
  78.2 6.4 %collective-permute-start.38 = (f32[2,4096]{1,0:T(2,128)S(1)}, f32[2,4096]{1,0:T(2,128)S(1)}, u32[]{:S(2)}, u32[]{:S(2)}) collective-permute-start(f32[2,4096]{1,0:T(2,128)S(1)} %get-tuple-element.44), channel_id=1, source_target_pairs={{0,3},{1,2},{2,1},{3,0},{4,7},{5,6},{6,5},{7,4},{8,11},{9,10},{10,... | collective-permute-start | bytes 98312 | tf_op jit(solution)/shard_map/ppermute | solution.py:89
  81.9 4.8 %collective-permute-start.37 = (f32[2,4096]{1,0:T(2,128)S(1)}, f32[2,4096]{1,0:T(2,128)S(1)}, u32[]{:S(2)}, u32[]{:S(2)}) collective-permute-start(f32[2,4096]{1,0:T(2,128)S(1)} %get-tuple-element.44), channel_id=1, source_target_pairs={{0,2},{1,3},{2,0},{3,1},{4,6},{5,7},{6,4},{7,5},{8,10},{9,11},{10,... | collective-permute-start | bytes 98312 | tf_op jit(solution)/shard_map/ppermute | solution.py:89
  81.9 4.8 %collective-permute-start.36 = (f32[2,4096]{1,0:T(2,128)S(1)}, f32[2,4096]{1,0:T(2,128)S(1)}, u32[]{:S(2)}, u32[]{:S(2)}) collective-permute-start(f32[2,4096]{1,0:T(2,128)S(1)} %get-tuple-element.44), channel_id=1, source_target_pairs={{0,1},{1,0},{2,3},{3,2},{4,5},{5,4},{6,7},{7,6},{8,9},{9,8},{10,11... | collective-permute-start | bytes 98312 | tf_op jit(solution)/shard_map/ppermute | solution.py:89
  82.7 5.0 %collective-permute-start.14 = (f32[128,256]{1,0:T(8,128)S(1)}, f32[128,256]{1,0:T(8,128)S(1)}, u32[]{:S(2)}, u32[]{:S(2)}) collective-permute-start(f32[128,256]{1,0:T(8,128)S(1)} %get-tuple-element.49), channel_id=1, source_target_pairs={{0,16},{4,20},{8,24},{12,28},{16,0},{20,4},{24,8},{28,12},{1,17},{... | collective-permute-start | bytes 393224 | tf_op jit(solution)/shard_map/ppermute | solution.py:89
  83.4 5.1 %collective-permute-start.16 = (f32[136,256]{1,0:T(8,128)S(1)}, f32[136,256]{1,0:T(8,128)S(1)}, u32[]{:S(2)}, u32[]{:S(2)}) collective-permute-start(f32[136,256]{1,0:T(8,128)S(1)} %pad_maximum_fusion.9), channel_id=1, source_target_pairs={{0,8},{4,12},{8,0},{12,4},{16,24},{20,28},{24,16},{28,20},{1,9},{5... | collective-permute-start | bytes 417800 | tf_op jit(solution)/shard_map/ppermute | solution.py:89
  88.6 6.5 %collective-permute-start.15 = (f32[256,256]{1,0:T(8,128)S(1)}, f32[256,256]{1,0:T(8,128)S(1)}, u32[]{:S(2)}, u32[]{:S(2)}) collective-permute-start(f32[256,256]{1,0:T(8,128)S(1)} %pad_maximum_fusion.7), channel_id=1, source_target_pairs={{0,8},{4,12},{8,0},{12,4},{16,24},{20,28},{24,16},{28,20},{1,9},{5... | collective-permute-start | bytes 786440 | tf_op jit(solution)/shard_map/ppermute | solution.py:89
  89.9 6.5 %collective-permute-start.17 = (f32[264,256]{1,0:T(8,128)S(1)}, f32[264,256]{1,0:T(8,128)S(1)}, u32[]{:S(2)}, u32[]{:S(2)}) collective-permute-start(f32[264,256]{1,0:T(8,128)S(1)} %pad_maximum_fusion.5), channel_id=1, source_target_pairs={{0,16},{4,20},{8,24},{12,28},{16,0},{20,4},{24,8},{28,12},{1,17},{... | collective-permute-start | bytes 811016 | tf_op jit(solution)/shard_map/ppermute | solution.py:89
  98.0 6.7 %collective-permute-start.31 = (f32[72,256]{1,0:T(8,128)S(1)}, f32[72,256]{1,0:T(8,128)S(1)}, u32[]{:S(2)}, u32[]{:S(2)}) collective-permute-start(f32[72,256]{1,0:T(8,128)S(1)} %get-tuple-element.41), channel_id=1, source_target_pairs={{0,3},{1,2},{2,1},{3,0},{4,7},{5,6},{6,5},{7,4},{8,11},{9,10},{10,... | collective-permute-start | bytes 221192 | tf_op jit(solution)/shard_map/ppermute | solution.py:89
  101.6 5.3 %collective-permute-start.30 = (f32[72,256]{1,0:T(8,128)S(1)}, f32[72,256]{1,0:T(8,128)S(1)}, u32[]{:S(2)}, u32[]{:S(2)}) collective-permute-start(f32[72,256]{1,0:T(8,128)S(1)} %get-tuple-element.41), channel_id=1, source_target_pairs={{0,2},{1,3},{2,0},{3,1},{4,6},{5,7},{6,4},{7,5},{8,10},{9,11},{10,... | collective-permute-start | bytes 221192 | tf_op jit(solution)/shard_map/ppermute | solution.py:89
  101.6 6.1 %collective-permute-start.29 = (f32[72,256]{1,0:T(8,128)S(1)}, f32[72,256]{1,0:T(8,128)S(1)}, u32[]{:S(2)}, u32[]{:S(2)}) collective-permute-start(f32[72,256]{1,0:T(8,128)S(1)} %get-tuple-element.41), channel_id=1, source_target_pairs={{0,1},{1,0},{2,3},{3,2},{4,5},{5,4},{6,7},{7,6},{8,9},{9,8},{10,11... | collective-permute-start | bytes 221192 | tf_op jit(solution)/shard_map/ppermute | solution.py:89
  102.4 7.5 %collective-permute-start.23 = (f32[128,256]{1,0:T(8,128)S(1)}, f32[128,256]{1,0:T(8,128)S(1)}, u32[]{:S(2)}, u32[]{:S(2)}) collective-permute-start(f32[128,256]{1,0:T(8,128)S(1)} %get-tuple-element.39), channel_id=1, source_target_pairs={{0,16},{4,20},{8,24},{12,28},{16,0},{20,4},{24,8},{28,12},{1,17},{... | collective-permute-start | bytes 393224 | tf_op jit(solution)/shard_map/ppermute | solution.py:89
  103.9 8.8 %collective-permute-start.21 = (f32[128,256]{1,0:T(8,128)S(1)}, f32[128,256]{1,0:T(8,128)S(1)}, u32[]{:S(2)}, u32[]{:S(2)}) collective-permute-start(f32[128,256]{1,0:T(8,128)S(1)} %get-tuple-element.39), channel_id=1, source_target_pairs={{0,8},{4,12},{8,0},{12,4},{16,24},{20,28},{24,16},{28,20},{1,9},{5... | collective-permute-start | bytes 393224 | tf_op jit(solution)/shard_map/ppermute | solution.py:89
  104.7 7.0 %collective-permute-start.24 = (f32[128,256]{1,0:T(8,128)S(1)}, f32[128,256]{1,0:T(8,128)S(1)}, u32[]{:S(2)}, u32[]{:S(2)}) collective-permute-start(f32[128,256]{1,0:T(8,128)S(1)} %get-tuple-element.40), channel_id=1, source_target_pairs={{0,16},{4,20},{8,24},{12,28},{16,0},{20,4},{24,8},{28,12},{1,17},{... | collective-permute-start | bytes 393224 | tf_op jit(solution)/shard_map/ppermute | solution.py:89
  106.8 7.0 %collective-permute-start.22 = (f32[128,256]{1,0:T(8,128)S(1)}, f32[128,256]{1,0:T(8,128)S(1)}, u32[]{:S(2)}, u32[]{:S(2)}) collective-permute-start(f32[128,256]{1,0:T(8,128)S(1)} %get-tuple-element.40), channel_id=1, source_target_pairs={{0,8},{4,12},{8,0},{12,4},{16,24},{20,28},{24,16},{28,20},{1,9},{5... | collective-permute-start | bytes 393224 | tf_op jit(solution)/shard_map/ppermute | solution.py:89
  107.6 11.3 %collective-permute-start.34 = (f32[72,256]{1,0:T(8,128)S(1)}, f32[72,256]{1,0:T(8,128)S(1)}, u32[]{:S(2)}, u32[]{:S(2)}) collective-permute-start(f32[72,256]{1,0:T(8,128)S(1)} %add_add_fusion), channel_id=1, source_target_pairs={{0,24},{4,28},{8,16},{12,20},{16,8},{20,12},{24,0},{28,4},{1,25},{... | collective-permute-start | bytes 221192 | tf_op jit(solution)/shard_map/ppermute | solution.py:89
  109.9 9.0 %collective-permute-start.33 = (f32[72,256]{1,0:T(8,128)S(1)}, f32[72,256]{1,0:T(8,128)S(1)}, u32[]{:S(2)}, u32[]{:S(2)}) collective-permute-start(f32[72,256]{1,0:T(8,128)S(1)} %add_add_fusion), channel_id=1, source_target_pairs={{0,16},{4,20},{8,24},{12,28},{16,0},{20,4},{24,8},{28,12},{1,17},{... | collective-permute-start | bytes 221192 | tf_op jit(solution)/shard_map/ppermute | solution.py:89
  111.7 7.3 %collective-permute-start.32 = (f32[72,256]{1,0:T(8,128)S(1)}, f32[72,256]{1,0:T(8,128)S(1)}, u32[]{:S(2)}, u32[]{:S(2)}) collective-permute-start(f32[72,256]{1,0:T(8,128)S(1)} %add_add_fusion), channel_id=1, source_target_pairs={{0,8},{4,12},{8,0},{12,4},{16,24},{20,28},{24,16},{28,20},{1,9},{5... | collective-permute-start | bytes 221192 | tf_op jit(solution)/shard_map/ppermute | solution.py:89
  112.7 5.0 %collective-permute-start.25 = (f32[128,256]{1,0:T(8,128)S(1)}, f32[128,256]{1,0:T(8,128)S(1)}, u32[]{:S(2)}, u32[]{:S(2)}) collective-permute-start(f32[128,256]{1,0:T(8,128)S(1)} %collective-permute-done.23), channel_id=1, source_target_pairs={{0,8},{4,12},{8,0},{12,4},{16,24},{20,28},{24,16},{28,20},{1,9},{5... | collective-permute-start | bytes 393224 | tf_op jit(solution)/shard_map/ppermute | solution.py:89
  113.8 5.0 %collective-permute-start.26 = (f32[128,256]{1,0:T(8,128)S(1)}, f32[128,256]{1,0:T(8,128)S(1)}, u32[]{:S(2)}, u32[]{:S(2)}) collective-permute-start(f32[128,256]{1,0:T(8,128)S(1)} %collective-permute-done.22), channel_id=1, source_target_pairs={{0,16},{4,20},{8,24},{12,28},{16,0},{20,4},{24,8},{28,12},{1,17},{... | collective-permute-start | bytes 393224 | tf_op jit(solution)/shard_map/ppermute | solution.py:89
  117.8 3.5 %collective-permute-start.27 = (f32[2,256,256]{2,1,0:T(8,128)S(1)}, f32[2,256,256]{2,1,0:T(8,128)S(1)}, u32[]{:S(2)}, u32[]{:S(2)}) collective-permute-start(f32[2,256,256]{2,1,0:T(8,128)S(1)} %pad_maximum_fusion.1.refs_0_), channel_id=1, source_target_pairs={{0,4},{4,0},{8,12},{12,8},{16,20},{20,16},{24,28},{28,24},{1,5},{5... | collective-permute-start | bytes 1572872 | tf_op jit(solution)/shard_map/ppermute | solution.py:89
  118.8 2.4 %collective-permute-start.28 = (f32[2,256,256]{2,1,0:T(8,128)S(1)}, f32[2,256,256]{2,1,0:T(8,128)S(1)}, u32[]{:S(2)}, u32[]{:S(2)}) collective-permute-start(f32[2,256,256]{2,1,0:T(8,128)S(1)} %pad_maximum_fusion.2.refs_1_), channel_id=1, source_target_pairs={{0,4},{4,0},{8,12},{12,8},{16,20},{20,16},{24,28},{28,24},{1,5},{5... | collective-permute-start | bytes 1572872 | tf_op jit(solution)/shard_map/ppermute | solution.py:89
  119.0 2.3 %collective-permute-start.35 = (f32[4,72,256]{2,1,0:T(8,128)S(1)}, f32[4,72,256]{2,1,0:T(8,128)S(1)}, u32[]{:S(2)}, u32[]{:S(2)}) collective-permute-start(f32[4,72,256]{2,1,0:T(8,128)S(1)} %pad_maximum_fusion.3.refs_4_), channel_id=1, source_target_pairs={{0,4},{4,0},{8,12},{12,8},{16,20},{20,16},{24,28},{28,24},{1,5},{5... | collective-permute-start | bytes 884744 | tf_op jit(solution)/shard_map/ppermute | solution.py:89

commit v7 on v5

--- a/solution.py
+++ b/solution.py
@@ -106,9 +106,10 @@
     payload, seen = refs.pop(0), refs.pop(0)
     squares_out = refs.pop(0) if first else None
     kept = refs.pop(0) if stream else points
-    low, tallies, even, odd, scaled, table, chosen_in, small_sems = refs[:8]
-    start = refs[8] if initial else None
-    point_sems = refs[-1] if stream else None
+    low, norms, tallies, sums, places, even, odd, tables = refs[:8]
+    chosen_in = refs[8] if stream else assign
+    small_sems, point_sems = refs[9:11] if stream else (None, None)
+    start = refs[11] if first else fine
     rows, width = low.shape
     block_width = width // SLOTS
     here = info[0]
@@ -125,23 +126,23 @@
     def load(i):
         return pltpu.make_async_copy(points.at[span(i)], kept.at[span(i)], point_sems.at[i])
 
-    load_assign = pltpu.make_async_copy(assign, chosen_in, small_sems.at[0])
-    if initial:
+    if first:
         load_start = pltpu.make_async_copy(
             fine.at[pl.ds(pl.multiple_of(half * rows, rows), rows)], start, small_sems.at[1]
         )
         load_start.start()
     if stream:
         load(0).start()
-    load_assign.start()
-    if stream:
+        load_assign = pltpu.make_async_copy(assign, chosen_in, small_sems.at[0])
+        load_assign.start()
 
         @pl.loop(1, tiles)
         def _(i):
             load(i).start()
 
     if initial:
-        load_start.wait()
+        if first:
+            load_start.wait()
         block = start[...]
         norm = jnp.sum(block * block, axis=1, keepdims=True)
         low[...] = (-2.0 * block).astype(jnp.bfloat16)
@@ -151,15 +152,18 @@
             block = fine[slot]
             norm = norm + jnp.sum(block * block, axis=1, keepdims=True)
             low[:, column_of(slot)] = (-2.0 * block).astype(jnp.bfloat16)
+    norms[...] = jnp.broadcast_to(norm, norms.shape)
     tallies[...] = jnp.zeros_like(tallies)
+    sums[...] = jnp.zeros_like(sums)
+    places[...] = lax.broadcasted_iota(jnp.int32, places.shape, 0).astype(jnp.int16)
 
     def multiply(i, target):
         target[...] = lax.dot_general(
             low[...], kept[span(i), :], (((1,), (1,)), ((), ())), preferred_element_type=jnp.float32
         )
 
-    def weigh(i, products):
-        energy = norm + products[...]
+    def collect(i, products):
+        energy = products[...] + jnp.concatenate([norms[...]] * (tile // 128), axis=1)
         chosen = chosen_in[pass_index : pass_index + 1, span(i)] - base
         member = lax.broadcasted_iota(jnp.int32, energy.shape, 0) == chosen
         picked = jnp.sum(jnp.where(member, energy, 0.0), axis=0, keepdims=True)
@@ -186,14 +190,18 @@
         for lane in range(0, tile, 128):
             tally = tally + weighted[:, lane : lane + 128]
         tallies[...] = tally
-        factor = as_column(weights, tile)
-        for lane in range(0, width, 128):
-            values = kept[span(i), lane : lane + 128].astype(jnp.float32)
-            scaled[span(i), lane : lane + 128] = (values * factor).astype(jnp.bfloat16)
-        table[:, span(i)] = member.astype(jnp.float32).astype(jnp.bfloat16)
-
-    load_assign.wait()
+        high = weights.astype(jnp.bfloat16)
+        rest = (weights - high.astype(jnp.float32)).astype(jnp.bfloat16)
+        narrow = jnp.where(inside, chosen, -1).astype(jnp.int16)
+        member = places[...] == narrow
+        nothing = jnp.zeros((rows, tile), jnp.bfloat16)
+        tables[:rows, :] = jnp.where(member, jnp.broadcast_to(high, nothing.shape), nothing)
+        tables[rows:, :] = jnp.where(member, jnp.broadcast_to(rest, nothing.shape), nothing)
+        both = jnp.dot(tables[...], kept[span(i), :], preferred_element_type=jnp.float32)
+        sums[...] += both[:rows] + both[rows:]
+
     if stream:
+        load_assign.wait()
         load(0).wait()
     multiply(0, even)
 
@@ -204,29 +212,20 @@
             load(i + 1).wait()
             load(i + 2).wait()
         multiply(i + 1, odd)
-        weigh(i, even)
+        collect(i, even)
         multiply(i + 2, even)
-        weigh(i + 1, odd)
+        collect(i + 1, odd)
 
     if stream:
         load(tiles - 1).wait()
     multiply(tiles - 1, odd)
-    weigh(tiles - 2, even)
-    weigh(tiles - 1, odd)
+    collect(tiles - 2, even)
+    collect(tiles - 1, odd)
 
     counts = jnp.broadcast_to(jnp.sum(tallies[...].T, axis=0, keepdims=True), (TAIL, rows))
-
     for slot in range(SLOTS):
-        payload[slot, :rows, :] = jnp.zeros((rows, block_width), jnp.float32)
+        payload[slot, :rows, :] = sums[:, column_of(slot)]
         payload[slot, rows:, :] = counts
-
-    @pl.loop(0, tiles // 2)
-    def _(i):
-        part = pl.ds(pl.multiple_of(2 * i * tile, 2 * tile), 2 * tile)
-        for slot in range(SLOTS):
-            payload[slot, :rows, :] += jnp.dot(
-                table[:, part], scaled[part, column_of(slot)], preferred_element_type=jnp.float32
-            )
 
 
 def run_pass(info, points, fine_assign, fine, squares, seen, *, pass_index, flip, rows):
@@ -239,16 +238,20 @@
     whole = pl.BlockSpec(memory_space=pltpu.VMEM)
     anywhere = pl.BlockSpec(memory_space=pl.ANY)
     in_hbm = lambda value: pltpu.with_memory_space_constraint(value, pltpu.HBM)
-    in_specs = [
-        anywhere if stream else whole,
-        anywhere,
-        anywhere if initial else full(SLOTS, rows, block_width),
-    ]
-    args = [
-        in_hbm(points) if stream else pltpu.with_memory_space_constraint(points, pltpu.VMEM),
-        in_hbm(fine_assign),
-        in_hbm(fine) if initial else fine,
-    ]
+    if stream:
+        in_specs = [anywhere, anywhere]
+        args = [in_hbm(points), in_hbm(fine_assign)]
+    else:
+        in_specs = [whole, full(PASSES, count)]
+        args = [pltpu.with_memory_space_constraint(points, pltpu.VMEM), fine_assign]
+    if not initial:
+        in_specs.append(full(SLOTS, rows, block_width))
+    elif stream:
+        in_specs.append(anywhere)
+        fine = in_hbm(fine)
+    else:
+        in_specs.append(pl.BlockSpec((rows, width), lambda i, info: (info[1] ^ flip, 0)))
+    args.append(fine)
     if squares is not None:
         in_specs.append(full(1, count))
         args.append(squares)
@@ -263,19 +266,23 @@
     scratch = [
         pltpu.VMEM((rows, width), jnp.bfloat16),
         pltpu.VMEM((rows, 128), jnp.float32),
+        pltpu.VMEM((rows, 128), jnp.float32),
+        pltpu.VMEM((rows, width), jnp.float32),
+        pltpu.VMEM((rows, tile), jnp.int16),
         pltpu.VMEM((rows, tile), jnp.float32),
         pltpu.VMEM((rows, tile), jnp.float32),
-        pltpu.VMEM((count, width), jnp.bfloat16),
-        pltpu.VMEM((rows, count), jnp.bfloat16),
-        pltpu.VMEM((PASSES, count), jnp.int32),
-        pltpu.SemaphoreType.DMA((2,)),
+        pltpu.VMEM((2 * rows, tile), jnp.bfloat16),
     ]
-    if initial:
-        scratch.append(pltpu.VMEM((rows, width), jnp.float32))
     if stream:
+        scratch += [
+            pltpu.VMEM((PASSES, count), jnp.int32),
+            pltpu.SemaphoreType.DMA((2,)),
+            pltpu.SemaphoreType.DMA((count // tile,)),
+        ]
+        if initial:
+            scratch.append(pltpu.VMEM((rows, width), jnp.float32))
         out_shape.append(pltpu.VMEM(points.shape, points.dtype))
         out_specs.append(whole)
-        scratch.append(pltpu.SemaphoreType.DMA((count // tile,)))
     body = functools.partial(
         pass_body,
         pass_index=pass_index,
@@ -302,11 +309,11 @@
     )(info, *args)
 
 
-def refine_body(info, own, sibling, x_top, x_low, y_top, y_low, tail, owner, coarse, *outs):
+def refine_body(info, own, sibling, over_x, over_y, tail, owner, coarse, *outs):
     top, low, part = outs
     rows = owner.shape[1]
     mid = rows // 2
-    counts_row = tail[...] + y_top[mid:, :]
+    counts_row = tail[...] + over_y[rows:, :]
     counts = as_column(counts_row[:1], rows)[:, :1]
     table = (
         lax.broadcasted_iota(jnp.int32, (NC, rows), 0) == owner[...]
@@ -318,9 +325,7 @@
         precision=HIGHEST,
         preferred_element_type=jnp.float32,
     )
-    totals = own[:rows, :] + sibling[:rows, :] + jnp.concatenate(
-        [x_top[...] + y_top[:mid, :], x_low[...] + y_low[...]], 0
-    )
+    totals = (own[:rows, :] + sibling[:rows, :]) + (over_x[...] + over_y[:rows, :])
     new = (totals + prior_weight * lookup) / (counts + prior_weight)
     top[...] = new[:mid]
     low[...] = new[mid:]
@@ -379,12 +384,12 @@
     counts = both(0, tail)
     corner_top = swap(jnp.concatenate([both(3, top), counts], 0), ACROSS_X)
     corner_low = swap(both(3, low), ACROSS_Y)
-    x_top = swap(both(1, top), ACROSS_X)
-    y_low = swap(both(2, low), ACROSS_Y)
     counts = counts + corner_top[mid:]
-    y_top = swap(jnp.concatenate([both(2, top) + corner_top[:mid], counts], 0), ACROSS_Y)
-    x_low = swap(both(1, low) + corner_low, ACROSS_X)
-    return x_top, x_low, y_top, y_low, counts
+    over_y = swap(
+        jnp.concatenate([both(2, top) + corner_top[:mid], both(2, low), counts], 0), ACROSS_Y
+    )
+    over_x = swap(jnp.concatenate([both(1, top), both(1, low) + corner_low], 0), ACROSS_X)
+    return over_x, over_y, counts
 
 
 def gather_half(top, low):
@@ -486,12 +491,10 @@
     held, seen_second = call(kept, fine_assign, other, squares, seen, flip=1)
     incoming = exchange(held, sibling)
 
-    seen = jnp.concatenate([seen_first, seen_second], 0)
-    folded = jnp.concatenate([part, seen.reshape(-1, block_width)], 0)
-    gathered = [folded] + [swap(folded, bit, "cen") for bit in range(1, lax.axis_size("cen"))]
-    part = functools.reduce(jnp.add, [each[: NC + TAIL] for each in gathered])
-    seen = functools.reduce(jnp.minimum, [each[NC + TAIL :] for each in gathered])
-    seen = seen.reshape(2, 2, -1)
+    seen = [each.reshape(-1, block_width) for each in (seen_first, seen_second)]
+    gathered = lax.all_gather(jnp.concatenate([part, *seen], 0), "cen")
+    part = jnp.sum(gathered[:, : NC + TAIL], axis=0)
+    seen = jnp.min(gathered[:, NC + TAIL :], axis=0).reshape(2, 2, -1)
     gaps = (seen[:, 0] - seen[:, 1]) / math.sqrt(width)
     coarse = part[:NC] / part[NC, :NC][:, None]
 

time: 132 us -> 144 us (1.091)
  blocking collectives: 0 us -> 16.5 us
  starting transfers between devices: 40.8 us -> 34.4 us
  local copies, waits for them, and re-layouts: 1.44 us -> 7.41 us
  other arithmetic: 4.97 us -> 0.98 us
  waiting for transfers between devices: 33.9 us -> 32.4 us
    all_gather x0 -> x1, blocking collectives: none -> 16.5 us  [on_device_paired(): gathered = lax.all_gather(jnp.concatenate([part, *seen], 0), 'cen')]
    unnamed x9 -> x15, local copies, waits for them, and re-layouts: 0.66 us -> 7.31 us
    ppermute x40 -> x33, starting transfers between devices: 40.8 us -> 34.4 us  [swap(): return lax.ppermute(value, axis, [(i, i ^ bit) for i in range(size)])]
    ppermute x40 -> x33, waiting for transfers between devices: 33.9 us -> 32.4 us  [swap(): return lax.ppermute(value, axis, [(i, i ^ bit) for i in range(size)])]
  transfers between devices with their start and end apart: 40 -> 33, of which waited for: 19 -> 16; matrix products, arithmetic and copies ran while one was open for 5% -> 1% of each run, Pallas kernels for 24% -> 23%
where the time goes in v7:
time: 144 us
  Pallas kernels  51.1 us (35%)
  starting transfers between devices  34.4 us (24%)
  waiting for transfers between devices  32.4 us (22%)
  blocking collectives  16.5 us (11%)
  local copies, waits for them, and re-layouts  7.41 us (5%)
    pallas_call x4, Pallas kernels, run_pass(): pl.pallas_call(body, out_shape=out_shape, grid_spec=pltpu.PrefetchScalarG...  46 us
    ppermute x33, starting transfers between devices, swap(): return lax.ppermute(value, axis, [(i, i ^ bit) for i in range(size)])  34.4 us
    ppermute x33, waiting for transfers between devices, swap(): return lax.ppermute(value, axis, [(i, i ^ bit) for i in range(size)])  32.4 us
    all_gather x1, blocking collectives, on_device_paired(): gathered = lax.all_gather(jnp.concatenate([part, *seen], 0), 'cen')  16.5 us
    unnamed x15, local copies, waits for them, and re-layouts  7.31 us
    pallas_call x2, Pallas kernels, refine_half(): pl.pallas_call(refine_body, out_shape=[jax.ShapeDtypeStruct((mid, block_w...  3 us
  transfers between devices with their start and end apart: 33, of which 16 were waited for; matrix products, arithmetic and copies ran while one was open for 1% of the time, Pallas kernels for 23%

profile of v7, /device:TPU:0, one launch (start us, length us, event | category | flops | bytes accessed | tf_op | source)
XLA Modules:
  0.0 143.8 jit_solution(4723431429084814140)
XLA Ops:
  0.6 0.1 pad_add_fusion.info
  0.7 12.9 %energies_and_sums_00.1 = (f32[4,264,256]{2,1,0:T(8,128)S(1)}, f32[2,4096]{1,0:T(2,128)S(1)}, f32[1,4096]{1,0:T(1,128)S(1)}, bf16[4096,1024]{1,0:T(8,128)(2,1)S(1)}) custom-call(s32[4]{0:T(128)S(1)} %pad_add_fusion.info, bf16[4096,1024]{1,0:T(8,128)(2,1)} %points.3, s32[2,4096]{1,0:T(2,128)} %assign.7, f32[512,1024]{1,0:T(8,128)} %fine.3), custom_call_target="tpu_custom_call" | custom-call | flops 4294967296 | bytes 8388608 | tf_op jit(solution)/shard_map/energies_and_sums_00/pallas_call | solution.py:294
  13.6 0.7 collective-permute-start
  14.3 9.8 %energies_and_sums_01.1 = (f32[4,264,256]{2,1,0:T(8,128)S(1)}, f32[2,4096]{1,0:T(2,128)S(1)}) custom-call(s32[4]{0:T(128)S(1)} %pad_add_fusion.info, bf16[4096,1024]{1,0:T(8,128)(2,1)S(1)} %get-tuple-element.24.points, s32[2,4096]{1,0:T(2,128)S(1)} %copy-done.3, f32[512,1024]{1,0:T(8,128)S(1)} %copy-done.2, f32[1,4096]{1,0:T(1,128)S(1)} %get-tuple-element.25.refs_0_, ...), custom_call_target="tpu_custom_call" | custom-call | flops 4294967296 | bytes 8388608 | tf_op jit(solution)/shard_map/energies_and_sums_01/pallas_call | solution.py:294
  24.1 0.1 fusion.7
  24.2 2.4 %collective-permute-start.3 = (f32[136,256]{1,0:T(8,128)S(1)}, f32[136,256]{1,0:T(8,128)S(1)}, u32[]{:S(2)}, u32[]{:S(2)}) collective-permute-start(f32[136,256]{1,0:T(8,128)S(1)} %pad_maximum_fusion.8), channel_id=1, source_target_pairs={{0,8},{4,12},{8,0},{12,4},{16,24},{20,28},{24,16},{28,20},{1,9},{5... | collective-permute-start | bytes 417800 | tf_op jit(solution)/shard_map/ppermute | solution.py:89
  26.6 1.5 %collective-permute-start.1 = (f32[128,256]{1,0:T(8,128)S(1)}, f32[128,256]{1,0:T(8,128)S(1)}, u32[]{:S(2)}, u32[]{:S(2)}) collective-permute-start(f32[128,256]{1,0:T(8,128)S(1)} %get-tuple-element.55), channel_id=1, source_target_pairs={{0,16},{4,20},{8,24},{12,28},{16,0},{20,4},{24,8},{28,12},{1,17},{... | collective-permute-start | bytes 393224 | tf_op jit(solution)/shard_map/ppermute | solution.py:89
  28.1 2.8 %collective-permute-done.3 = f32[136,256]{1,0:T(8,128)S(1)} collective-permute-done((f32[136,256]{1,0:T(8,128)S(1)}, f32[136,256]{1,0:T(8,128)S(1)}, u32[]{:S(2)}, u32[]{:S(2)}) %collective-permute-start.3) | collective-permute-done | bytes 139296 | tf_op jit(solution)/shard_map/ppermute | solution.py:89
  30.9 1.3 collective-permute-done.1
  32.2 0.1 slice_add_fusion.8
  32.3 1.6 %collective-permute-start.4 = (f32[264,256]{1,0:T(8,128)S(1)}, f32[264,256]{1,0:T(8,128)S(1)}, u32[]{:S(2)}, u32[]{:S(2)}) collective-permute-start(f32[264,256]{1,0:T(8,128)S(1)} %pad_maximum_fusion.4), channel_id=1, source_target_pairs={{0,16},{4,20},{8,24},{12,28},{16,0},{20,4},{24,8},{28,12},{1,17},{... | collective-permute-start | bytes 811016 | tf_op jit(solution)/shard_map/ppermute | solution.py:89
  33.9 0.6 collective-permute-start.2
  34.5 6.8 %collective-permute-done.2.over_x = f32[256,256]{1,0:T(8,128)S(1)} collective-permute-done((f32[256,256]{1,0:T(8,128)S(1)}, f32[256,256]{1,0:T(8,128)S(1)}, u32[]{:S(2)}, u32[]{:S(2)}) %collective-permute-start.2) | collective-permute-done | bytes 262176 | tf_op jit(solution)/shard_map/ppermute | solution.py:89
  41.3 1.5 %refine_half.2 = (f32[128,256]{1,0:T(8,128)S(1)}, f32[128,256]{1,0:T(8,128)S(1)}, f32[72,256]{1,0:T(8,128)S(1)}) custom-call(s32[4]{0:T(128)S(1)} %pad_add_fusion.info, f32[4,264,256]{2,1,0:T(8,128)S(1)} %get-tuple-element.27.own, f32[4,264,256]{2,1,0:T(8,128)S(1)} %collective-permute-done.sibling, f32[256,256]{1,0:T(8,128)S(1)} %collective-permute-done.2.over_x, ...), custom_call_target="tpu_custom_call" | custom-call | tf_op jit(solution)/shard_map/refine_half/pallas_call | solution.py:352
  42.8 0.5 collective-permute-start.7
  43.3 0.8 collective-permute-start.6
  44.1 1.5 %collective-permute-start.8 = (f32[128,256]{1,0:T(8,128)S(1)}, f32[128,256]{1,0:T(8,128)S(1)}, u32[]{:S(2)}, u32[]{:S(2)}) collective-permute-start(f32[128,256]{1,0:T(8,128)S(1)} %get-tuple-element.30), channel_id=1, source_target_pairs={{0,16},{4,20},{8,24},{12,28},{16,0},{20,4},{24,8},{28,12},{1,17},{... | collective-permute-start | bytes 393224 | tf_op jit(solution)/shard_map/ppermute | solution.py:89
  45.6 1.2 collective-permute-start.5
  46.9 1.2 collective-permute-done.11
  48.2 0.9 collective-permute-start.9
  49.0 0.9 collective-permute-start.10
  49.9 0.7 collective-permute-done.5
  50.6 3.2 %collective-permute-done.9 = f32[128,256]{1,0:T(8,128)S(1)} collective-permute-done((f32[128,256]{1,0:T(8,128)S(1)}, f32[128,256]{1,0:T(8,128)S(1)}, u32[]{:S(2)}, u32[]{:S(2)}) %collective-permute-start.9) | collective-permute-done | bytes 131104 | tf_op jit(solution)/shard_map/ppermute | solution.py:89
  53.8 0.5 collective-permute-done.10
  54.3 0.1 pad_maximum_fusion.fine
  54.4 0.1 collective-permute-start.12
  54.5 12.3 %energies_and_sums_10.1 = (f32[4,264,256]{2,1,0:T(8,128)}, f32[2,4096]{1,0:T(2,128)S(1)}, bf16[4096,1024]{1,0:T(8,128)(2,1)S(1)}) custom-call(s32[4]{0:T(128)S(1)} %pad_add_fusion.info, bf16[4096,1024]{1,0:T(8,128)(2,1)} %points.3, s32[2,4096]{1,0:T(2,128)} %assign.7, f32[4,256,256]{2,1,0:T(8,128)S(1)} %pad_maximum_fusion.fine, ...), custom_call_target="tpu_custom_call" | custom-call | flops 4294967296 | bytes 8388608 | tf_op jit(solution)/shard_map/energies_and_sums_10/pallas_call | solution.py:294
  66.8 3.3 %copy-done.5 = bf16[4096,1024]{1,0:T(8,128)(2,1)} copy-done((bf16[4096,1024]{1,0:T(8,128)(2,1)}, bf16[4096,1024]{1,0:T(8,128)(2,1)S(1)}, u32[]{:S(2)}) %copy-start.5) | copy-done | bytes 8388632
  70.1 0.4 collective-permute-start.13
  70.5 3.4 %copy-done.6 = bf16[4096,1024]{1,0:T(8,128)(2,1)S(1)} copy-done((bf16[4096,1024]{1,0:T(8,128)(2,1)S(1)}, bf16[4096,1024]{1,0:T(8,128)(2,1)}, u32[]{:S(2)}) %copy-start.6) | copy-done | bytes 8388632
  73.9 11.1 %energies_and_sums_11.1 = (f32[4,264,256]{2,1,0:T(8,128)S(1)}, f32[2,4096]{1,0:T(2,128)S(1)}) custom-call(s32[4]{0:T(128)S(1)} %pad_add_fusion.info, bf16[4096,1024]{1,0:T(8,128)(2,1)S(1)} %copy-done.6, s32[2,4096]{1,0:T(2,128)S(1)} %copy-done.4, f32[4,256,256]{2,1,0:T(8,128)} %collective-permute-done.12.fine, f32[1,4096]{1,0:T(1,128)S(1)} %get-tuple-element.25.refs_0_, ...), custom_call_target="tpu_custom_call" | custom-call | flops 4294967296 | bytes 8388608 | tf_op jit(solution)/shard_map/energies_and_sums_11/pallas_call | solution.py:294
  85.0 16.5 %all-gather = f32[544,256]{1,0:T(8,128)S(1)} all-gather(f32[136,256]{1,0:T(8,128)S(1)} %pad_maximum_fusion.10), channel_id=2, replica_groups=mesh['pts'=8,'cen'=4] {'cen'}, dimensions={0}, use_global_device_ids=true | all-gather | bytes 696320 | tf_op jit(solution)/shard_map/all_gather | solution.py:495
  101.6 0.1 fusion
  101.6 0.6 collective-permute-start.14
  102.3 1.2 collective-permute-start.16
  103.5 3.1 %collective-permute-done.14 = f32[128,256]{1,0:T(8,128)S(1)} collective-permute-done((f32[128,256]{1,0:T(8,128)S(1)}, f32[128,256]{1,0:T(8,128)S(1)}, u32[]{:S(2)}, u32[]{:S(2)}) %collective-permute-start.14) | collective-permute-done | bytes 131104 | tf_op jit(solution)/shard_map/ppermute | solution.py:89
  106.7 0.8 collective-permute-done.16
  107.5 1.2 collective-permute-start.15
  108.8 1.6 %collective-permute-start.17 = (f32[264,256]{1,0:T(8,128)S(1)}, f32[264,256]{1,0:T(8,128)S(1)}, u32[]{:S(2)}, u32[]{:S(2)}) collective-permute-start(f32[264,256]{1,0:T(8,128)S(1)} %pad_maximum_fusion.5), channel_id=1, source_target_pairs={{0,16},{4,20},{8,24},{12,28},{16,0},{20,4},{24,8},{28,12},{1,17},{... | collective-permute-start | bytes 811016 | tf_op jit(solution)/shard_map/ppermute | solution.py:89
  110.4 0.1 slice_divide_fusion.coarse
  110.5 3.4 %collective-permute-done.15.over_x = f32[256,256]{1,0:T(8,128)S(1)} collective-permute-done((f32[256,256]{1,0:T(8,128)S(1)}, f32[256,256]{1,0:T(8,128)S(1)}, u32[]{:S(2)}, u32[]{:S(2)}) %collective-permute-start.15) | collective-permute-done | bytes 262176 | tf_op jit(solution)/shard_map/ppermute | solution.py:89
  113.9 1.3 collective-permute-done.17.over_y
  115.3 1.5 %refine_half.3 = (f32[128,256]{1,0:T(8,128)S(1)}, f32[128,256]{1,0:T(8,128)S(1)}, f32[72,256]{1,0:T(8,128)S(1)}) custom-call(s32[4]{0:T(128)S(1)} %pad_add_fusion.info, f32[4,264,256]{2,1,0:T(8,128)S(1)} %get-tuple-element.35.own, f32[4,264,256]{2,1,0:T(8,128)S(1)} %collective-permute-done.13.sibling, f32[256,256]{1,0:T(8,128)S(1)} %collective-permute-done.15.over_x, ...), custom_call_target="tpu_custom_call" | custom-call | tf_op jit(solution)/shard_map/refine_half/pallas_call | solution.py:352
  116.8 5.2 %collective-permute-start.28 = (f32[72,256]{1,0:T(8,128)S(1)}, f32[72,256]{1,0:T(8,128)S(1)}, u32[]{:S(2)}, u32[]{:S(2)}) collective-permute-start(f32[72,256]{1,0:T(8,128)S(1)} %get-tuple-element.42), channel_id=1, source_target_pairs={{0,3},{1,2},{2,1},{3,0},{4,7},{5,6},{6,5},{7,4},{8,11},{9,10},{10,... | collective-permute-start | bytes 221192 | tf_op jit(solution)/shard_map/ppermute | solution.py:89
  122.0 0.6 collective-permute-start.26
  122.6 1.5 %collective-permute-start.20 = (f32[128,256]{1,0:T(8,128)S(1)}, f32[128,256]{1,0:T(8,128)S(1)}, u32[]{:S(2)}, u32[]{:S(2)}) collective-permute-start(f32[128,256]{1,0:T(8,128)S(1)} %get-tuple-element.40), channel_id=1, source_target_pairs={{0,16},{4,20},{8,24},{12,28},{16,0},{20,4},{24,8},{28,12},{1,17},{... | collective-permute-start | bytes 393224 | tf_op jit(solution)/shard_map/ppermute | solution.py:89
  124.1 0.8 collective-permute-start.18
  124.9 1.0 collective-permute-start.21
  125.9 1.3 collective-permute-done.27
  127.2 0.9 collective-permute-start.19
  128.1 2.2 %collective-permute-start.31 = (f32[72,256]{1,0:T(8,128)S(1)}, f32[72,256]{1,0:T(8,128)S(1)}, u32[]{:S(2)}, u32[]{:S(2)}) collective-permute-start(f32[72,256]{1,0:T(8,128)S(1)} %add_add_fusion), channel_id=1, source_target_pairs={{0,24},{4,28},{8,16},{12,20},{16,8},{20,12},{24,0},{28,4},{1,25},{... | collective-permute-start | bytes 221192 | tf_op jit(solution)/shard_map/ppermute | solution.py:89
  130.3 0.7 collective-permute-start.30
  131.0 1.2 collective-permute-done.19
  132.2 0.9 collective-permute-start.29
  133.1 1.5 %collective-permute-start.23 = (f32[128,256]{1,0:T(8,128)S(1)}, f32[128,256]{1,0:T(8,128)S(1)}, u32[]{:S(2)}, u32[]{:S(2)}) collective-permute-start(f32[128,256]{1,0:T(8,128)S(1)} %collective-permute-done.19), channel_id=1, source_target_pairs={{0,16},{4,20},{8,24},{12,28},{16,0},{20,4},{24,8},{28,12},{1,17},{... | collective-permute-start | bytes 393224 | tf_op jit(solution)/shard_map/ppermute | solution.py:89
  134.7 1.2 collective-permute-start.22
  135.9 0.1 collective-permute-start.24
  136.0 0.6 collective-permute-done.29
  136.6 0.1 collective-permute-start.32
  136.6 3.0 %collective-permute-done.22 = f32[128,256]{1,0:T(8,128)S(1)} collective-permute-done((f32[128,256]{1,0:T(8,128)S(1)}, f32[128,256]{1,0:T(8,128)S(1)}, u32[]{:S(2)}, u32[]{:S(2)}) %collective-permute-start.22) | collective-permute-done | bytes 131104 | tf_op jit(solution)/shard_map/ppermute | solution.py:89
  139.7 0.1 collective-permute-start.25
  139.8 0.6 copy.10
  140.5 1.2 collective-permute-done.25.refs_3_
  141.7 2.1 %place_blocks.1 = (f32[512,1024]{1,0:T(8,128)}, f32[64,1024]{1,0:T(8,128)}) custom-call(s32[4]{0:T(128)S(1)} %pad_add_fusion.info, f32[2,256,256]{2,1,0:T(8,128)S(1)} %pad_maximum_fusion.1.refs_0_, f32[2,256,256]{2,1,0:T(8,128)S(1)} %pad_maximum_fusion.2.refs_1_, f32[2,256,256]{2,1,0:T(8,128)S(1)} %collective-permute-done.24.refs_2_, ...), custom_call_target="tpu_custom_call" | custom-call | tf_op jit(solution)/shard_map/place_blocks/pallas_call | solution.py:447
  (63 shorter events, 0.7 us)
Async XLA Ops:
  0.7 13.6 %copy-start.2 = (f32[512,1024]{1,0:T(8,128)S(1)}, f32[512,1024]{1,0:T(8,128)}, u32[]{:S(2)}) copy-start(f32[512,1024]{1,0:T(8,128)} %fine.3) | copy-start | bytes 6291460
  0.7 13.6 %copy-start.3 = (s32[2,4096]{1,0:T(2,128)S(1)}, s32[2,4096]{1,0:T(2,128)}, u32[]{:S(2)}) copy-start(s32[2,4096]{1,0:T(2,128)} %assign.7) | copy-start | bytes 98308
  13.6 10.5 %collective-permute-start = (f32[4,264,256]{2,1,0:T(8,128)S(1)}, f32[4,264,256]{2,1,0:T(8,128)S(1)}, u32[]{:S(2)}, u32[]{:S(2)}) collective-permute-start(f32[4,264,256]{2,1,0:T(8,128)S(1)} %get-tuple-element.28), channel_id=1, source_target_pairs={{0,4},{4,0},{8,12},{12,8},{16,20},{20,16},{24,28},{28,24},{1,5},{5... | collective-permute-start | bytes 3244040 | tf_op jit(solution)/shard_map/ppermute | solution.py:89
  24.2 17.1 %copy-start = (f32[64,1024]{1,0:T(8,128)S(1)}, f32[64,1024]{1,0:T(8,128)}, u32[]{:S(2)}) copy-start(f32[64,1024]{1,0:T(8,128)} %coarse.1) | copy-start | bytes 786436
  24.2 17.1 %copy-start.1 = (s32[512]{0:T(512)S(1)}, s32[512]{0:T(512)}, u32[]{:S(2)}) copy-start(s32[512]{0:T(512)} %param.9) | copy-start | bytes 6148
  24.2 6.7 %collective-permute-start.3 = (f32[136,256]{1,0:T(8,128)S(1)}, f32[136,256]{1,0:T(8,128)S(1)}, u32[]{:S(2)}, u32[]{:S(2)}) collective-permute-start(f32[136,256]{1,0:T(8,128)S(1)} %pad_maximum_fusion.8), channel_id=1, source_target_pairs={{0,8},{4,12},{8,0},{12,4},{16,24},{20,28},{24,16},{28,20},{1,9},{5... | collective-permute-start | bytes 417800 | tf_op jit(solution)/shard_map/ppermute | solution.py:89
  26.6 5.6 %collective-permute-start.1 = (f32[128,256]{1,0:T(8,128)S(1)}, f32[128,256]{1,0:T(8,128)S(1)}, u32[]{:S(2)}, u32[]{:S(2)}) collective-permute-start(f32[128,256]{1,0:T(8,128)S(1)} %get-tuple-element.55), channel_id=1, source_target_pairs={{0,16},{4,20},{8,24},{12,28},{16,0},{20,4},{24,8},{28,12},{1,17},{... | collective-permute-start | bytes 393224 | tf_op jit(solution)/shard_map/ppermute | solution.py:89
  32.3 9.0 %collective-permute-start.4 = (f32[264,256]{1,0:T(8,128)S(1)}, f32[264,256]{1,0:T(8,128)S(1)}, u32[]{:S(2)}, u32[]{:S(2)}) collective-permute-start(f32[264,256]{1,0:T(8,128)S(1)} %pad_maximum_fusion.4), channel_id=1, source_target_pairs={{0,16},{4,20},{8,24},{12,28},{16,0},{20,4},{24,8},{28,12},{1,17},{... | collective-permute-start | bytes 811016 | tf_op jit(solution)/shard_map/ppermute | solution.py:89
  33.9 7.4 %collective-permute-start.2 = (f32[256,256]{1,0:T(8,128)S(1)}, f32[256,256]{1,0:T(8,128)S(1)}, u32[]{:S(2)}, u32[]{:S(2)}) collective-permute-start(f32[256,256]{1,0:T(8,128)S(1)} %pad_maximum_fusion.6), channel_id=1, source_target_pairs={{0,8},{4,12},{8,0},{12,4},{16,24},{20,28},{24,16},{28,20},{1,9},{5... | collective-permute-start | bytes 786440 | tf_op jit(solution)/shard_map/ppermute | solution.py:89
  42.8 5.3 %collective-permute-start.7 = (f32[128,256]{1,0:T(8,128)S(1)}, f32[128,256]{1,0:T(8,128)S(1)}, u32[]{:S(2)}, u32[]{:S(2)}) collective-permute-start(f32[128,256]{1,0:T(8,128)S(1)} %get-tuple-element.29), channel_id=1, source_target_pairs={{0,16},{4,20},{8,24},{12,28},{16,0},{20,4},{24,8},{28,12},{1,17},{... | collective-permute-start | bytes 393224 | tf_op jit(solution)/shard_map/ppermute | solution.py:89
  43.3 5.7 %collective-permute-start.6 = (f32[128,256]{1,0:T(8,128)S(1)}, f32[128,256]{1,0:T(8,128)S(1)}, u32[]{:S(2)}, u32[]{:S(2)}) collective-permute-start(f32[128,256]{1,0:T(8,128)S(1)} %get-tuple-element.30), channel_id=1, source_target_pairs={{0,8},{4,12},{8,0},{12,4},{16,24},{20,28},{24,16},{28,20},{1,9},{5... | collective-permute-start | bytes 393224 | tf_op jit(solution)/shard_map/ppermute | solution.py:89
  44.1 5.8 %collective-permute-start.8 = (f32[128,256]{1,0:T(8,128)S(1)}, f32[128,256]{1,0:T(8,128)S(1)}, u32[]{:S(2)}, u32[]{:S(2)}) collective-permute-start(f32[128,256]{1,0:T(8,128)S(1)} %get-tuple-element.30), channel_id=1, source_target_pairs={{0,16},{4,20},{8,24},{12,28},{16,0},{20,4},{24,8},{28,12},{1,17},{... | collective-permute-start | bytes 393224 | tf_op jit(solution)/shard_map/ppermute | solution.py:89
  45.6 5.0 %collective-permute-start.5 = (f32[128,256]{1,0:T(8,128)S(1)}, f32[128,256]{1,0:T(8,128)S(1)}, u32[]{:S(2)}, u32[]{:S(2)}) collective-permute-start(f32[128,256]{1,0:T(8,128)S(1)} %get-tuple-element.29), channel_id=1, source_target_pairs={{0,8},{4,12},{8,0},{12,4},{16,24},{20,28},{24,16},{28,20},{1,9},{5... | collective-permute-start | bytes 393224 | tf_op jit(solution)/shard_map/ppermute | solution.py:89
  46.9 1.3 collective-permute-start.11
  48.2 5.6 %collective-permute-start.9 = (f32[128,256]{1,0:T(8,128)S(1)}, f32[128,256]{1,0:T(8,128)S(1)}, u32[]{:S(2)}, u32[]{:S(2)}) collective-permute-start(f32[128,256]{1,0:T(8,128)S(1)} %collective-permute-done.7), channel_id=1, source_target_pairs={{0,8},{4,12},{8,0},{12,4},{16,24},{20,28},{24,16},{28,20},{1,9},{5... | collective-permute-start | bytes 393224 | tf_op jit(solution)/shard_map/ppermute | solution.py:89
  49.0 5.3 %collective-permute-start.10 = (f32[128,256]{1,0:T(8,128)S(1)}, f32[128,256]{1,0:T(8,128)S(1)}, u32[]{:S(2)}, u32[]{:S(2)}) collective-permute-start(f32[128,256]{1,0:T(8,128)S(1)} %collective-permute-done.6), channel_id=1, source_target_pairs={{0,16},{4,20},{8,24},{12,28},{16,0},{20,4},{24,8},{28,12},{1,17},{... | collective-permute-start | bytes 393224 | tf_op jit(solution)/shard_map/ppermute | solution.py:89
  54.4 16.1 %copy-start.4 = (s32[2,4096]{1,0:T(2,128)S(1)}, s32[2,4096]{1,0:T(2,128)}, u32[]{:S(2)}) copy-start(s32[2,4096]{1,0:T(2,128)} %assign.7) | copy-start | bytes 98308
  54.4 16.1 %collective-permute-start.12 = (f32[4,256,256]{2,1,0:T(8,128)S(1)}, f32[4,256,256]{2,1,0:T(8,128)}, u32[]{:S(2)}, u32[]{:S(2)}) collective-permute-start(f32[4,256,256]{2,1,0:T(8,128)S(1)} %pad_maximum_fusion.fine), channel_id=1, source_target_pairs={{0,4},{4,0},{8,12},{12,8},{16,20},{20,16},{24,28},{28,24},{1,5},{5... | collective-permute-start | bytes 3145736 | tf_op jit(solution)/shard_map/ppermute | solution.py:89
  66.8 3.3 %copy-start.5 = (bf16[4096,1024]{1,0:T(8,128)(2,1)}, bf16[4096,1024]{1,0:T(8,128)(2,1)S(1)}, u32[]{:S(2)}) copy-start(bf16[4096,1024]{1,0:T(8,128)(2,1)S(1)} %get-tuple-element.33.points) | copy-start | bytes 25165828
  70.1 31.5 %collective-permute-start.13 = (f32[4,264,256]{2,1,0:T(8,128)}, f32[4,264,256]{2,1,0:T(8,128)S(1)}, u32[]{:S(2)}, u32[]{:S(2)}) collective-permute-start(f32[4,264,256]{2,1,0:T(8,128)} %get-tuple-element.36), channel_id=1, source_target_pairs={{0,4},{4,0},{8,12},{12,8},{16,20},{20,16},{24,28},{28,24},{1,5},{5... | collective-permute-start | bytes 3244040 | tf_op jit(solution)/shard_map/ppermute | solution.py:89
  70.5 3.4 %copy-start.6 = (bf16[4096,1024]{1,0:T(8,128)(2,1)S(1)}, bf16[4096,1024]{1,0:T(8,128)(2,1)}, u32[]{:S(2)}) copy-start(bf16[4096,1024]{1,0:T(8,128)(2,1)} %copy-done.5) | copy-start | bytes 25165828
  101.6 5.0 %collective-permute-start.14 = (f32[128,256]{1,0:T(8,128)S(1)}, f32[128,256]{1,0:T(8,128)S(1)}, u32[]{:S(2)}, u32[]{:S(2)}) collective-permute-start(f32[128,256]{1,0:T(8,128)S(1)} %get-tuple-element.49), channel_id=1, source_target_pairs={{0,16},{4,20},{8,24},{12,28},{16,0},{20,4},{24,8},{28,12},{1,17},{... | collective-permute-start | bytes 393224 | tf_op jit(solution)/shard_map/ppermute | solution.py:89
  102.3 5.1 %collective-permute-start.16 = (f32[136,256]{1,0:T(8,128)S(1)}, f32[136,256]{1,0:T(8,128)S(1)}, u32[]{:S(2)}, u32[]{:S(2)}) collective-permute-start(f32[136,256]{1,0:T(8,128)S(1)} %pad_maximum_fusion.9), channel_id=1, source_target_pairs={{0,8},{4,12},{8,0},{12,4},{16,24},{20,28},{24,16},{28,20},{1,9},{5... | collective-permute-start | bytes 417800 | tf_op jit(solution)/shard_map/ppermute | solution.py:89
  107.5 6.4 %collective-permute-start.15 = (f32[256,256]{1,0:T(8,128)S(1)}, f32[256,256]{1,0:T(8,128)S(1)}, u32[]{:S(2)}, u32[]{:S(2)}) collective-permute-start(f32[256,256]{1,0:T(8,128)S(1)} %pad_maximum_fusion.7), channel_id=1, source_target_pairs={{0,8},{4,12},{8,0},{12,4},{16,24},{20,28},{24,16},{28,20},{1,9},{5... | collective-permute-start | bytes 786440 | tf_op jit(solution)/shard_map/ppermute | solution.py:89
  108.8 6.5 %collective-permute-start.17 = (f32[264,256]{1,0:T(8,128)S(1)}, f32[264,256]{1,0:T(8,128)S(1)}, u32[]{:S(2)}, u32[]{:S(2)}) collective-permute-start(f32[264,256]{1,0:T(8,128)S(1)} %pad_maximum_fusion.5), channel_id=1, source_target_pairs={{0,16},{4,20},{8,24},{12,28},{16,0},{20,4},{24,8},{28,12},{1,17},{... | collective-permute-start | bytes 811016 | tf_op jit(solution)/shard_map/ppermute | solution.py:89
  116.8 8.2 %collective-permute-start.28 = (f32[72,256]{1,0:T(8,128)S(1)}, f32[72,256]{1,0:T(8,128)S(1)}, u32[]{:S(2)}, u32[]{:S(2)}) collective-permute-start(f32[72,256]{1,0:T(8,128)S(1)} %get-tuple-element.42), channel_id=1, source_target_pairs={{0,3},{1,2},{2,1},{3,0},{4,7},{5,6},{6,5},{7,4},{8,11},{9,10},{10,... | collective-permute-start | bytes 221192 | tf_op jit(solution)/shard_map/ppermute | solution.py:89
  122.0 5.3 %collective-permute-start.27 = (f32[72,256]{1,0:T(8,128)S(1)}, f32[72,256]{1,0:T(8,128)S(1)}, u32[]{:S(2)}, u32[]{:S(2)}) collective-permute-start(f32[72,256]{1,0:T(8,128)S(1)} %get-tuple-element.42), channel_id=1, source_target_pairs={{0,2},{1,3},{2,0},{3,1},{4,6},{5,7},{6,4},{7,5},{8,10},{9,11},{10,... | collective-permute-start | bytes 221192 | tf_op jit(solution)/shard_map/ppermute | solution.py:89
  122.0 6.1 %collective-permute-start.26 = (f32[72,256]{1,0:T(8,128)S(1)}, f32[72,256]{1,0:T(8,128)S(1)}, u32[]{:S(2)}, u32[]{:S(2)}) collective-permute-start(f32[72,256]{1,0:T(8,128)S(1)} %get-tuple-element.42), channel_id=1, source_target_pairs={{0,1},{1,0},{2,3},{3,2},{4,5},{5,4},{6,7},{7,6},{8,9},{9,8},{10,11... | collective-permute-start | bytes 221192 | tf_op jit(solution)/shard_map/ppermute | solution.py:89
  122.6 10.5 %collective-permute-start.20 = (f32[128,256]{1,0:T(8,128)S(1)}, f32[128,256]{1,0:T(8,128)S(1)}, u32[]{:S(2)}, u32[]{:S(2)}) collective-permute-start(f32[128,256]{1,0:T(8,128)S(1)} %get-tuple-element.40), channel_id=1, source_target_pairs={{0,16},{4,20},{8,24},{12,28},{16,0},{20,4},{24,8},{28,12},{1,17},{... | collective-permute-start | bytes 393224 | tf_op jit(solution)/shard_map/ppermute | solution.py:89
  124.1 6.2 %collective-permute-start.18 = (f32[128,256]{1,0:T(8,128)S(1)}, f32[128,256]{1,0:T(8,128)S(1)}, u32[]{:S(2)}, u32[]{:S(2)}) collective-permute-start(f32[128,256]{1,0:T(8,128)S(1)} %get-tuple-element.40), channel_id=1, source_target_pairs={{0,8},{4,12},{8,0},{12,4},{16,24},{20,28},{24,16},{28,20},{1,9},{5... | collective-permute-start | bytes 393224 | tf_op jit(solution)/shard_map/ppermute | solution.py:89
  124.9 9.7 %collective-permute-start.21 = (f32[128,256]{1,0:T(8,128)S(1)}, f32[128,256]{1,0:T(8,128)S(1)}, u32[]{:S(2)}, u32[]{:S(2)}) collective-permute-start(f32[128,256]{1,0:T(8,128)S(1)} %get-tuple-element.41), channel_id=1, source_target_pairs={{0,16},{4,20},{8,24},{12,28},{16,0},{20,4},{24,8},{28,12},{1,17},{... | collective-permute-start | bytes 393224 | tf_op jit(solution)/shard_map/ppermute | solution.py:89
  127.2 5.0 %collective-permute-start.19 = (f32[128,256]{1,0:T(8,128)S(1)}, f32[128,256]{1,0:T(8,128)S(1)}, u32[]{:S(2)}, u32[]{:S(2)}) collective-permute-start(f32[128,256]{1,0:T(8,128)S(1)} %get-tuple-element.41), channel_id=1, source_target_pairs={{0,8},{4,12},{8,0},{12,4},{16,24},{20,28},{24,16},{28,20},{1,9},{5... | collective-permute-start | bytes 393224 | tf_op jit(solution)/shard_map/ppermute | solution.py:89
  128.1 7.8 %collective-permute-start.31 = (f32[72,256]{1,0:T(8,128)S(1)}, f32[72,256]{1,0:T(8,128)S(1)}, u32[]{:S(2)}, u32[]{:S(2)}) collective-permute-start(f32[72,256]{1,0:T(8,128)S(1)} %add_add_fusion), channel_id=1, source_target_pairs={{0,24},{4,28},{8,16},{12,20},{16,8},{20,12},{24,0},{28,4},{1,25},{... | collective-permute-start | bytes 221192 | tf_op jit(solution)/shard_map/ppermute | solution.py:89
  130.3 5.7 %collective-permute-start.30 = (f32[72,256]{1,0:T(8,128)S(1)}, f32[72,256]{1,0:T(8,128)S(1)}, u32[]{:S(2)}, u32[]{:S(2)}) collective-permute-start(f32[72,256]{1,0:T(8,128)S(1)} %add_add_fusion), channel_id=1, source_target_pairs={{0,16},{4,20},{8,24},{12,28},{16,0},{20,4},{24,8},{28,12},{1,17},{... | collective-permute-start | bytes 221192 | tf_op jit(solution)/shard_map/ppermute | solution.py:89
  132.2 4.4 %collective-permute-start.29 = (f32[72,256]{1,0:T(8,128)S(1)}, f32[72,256]{1,0:T(8,128)S(1)}, u32[]{:S(2)}, u32[]{:S(2)}) collective-permute-start(f32[72,256]{1,0:T(8,128)S(1)} %add_add_fusion), channel_id=1, source_target_pairs={{0,8},{4,12},{8,0},{12,4},{16,24},{20,28},{24,16},{28,20},{1,9},{5... | collective-permute-start | bytes 221192 | tf_op jit(solution)/shard_map/ppermute | solution.py:89
  133.1 6.5 %collective-permute-start.23 = (f32[128,256]{1,0:T(8,128)S(1)}, f32[128,256]{1,0:T(8,128)S(1)}, u32[]{:S(2)}, u32[]{:S(2)}) collective-permute-start(f32[128,256]{1,0:T(8,128)S(1)} %collective-permute-done.19), channel_id=1, source_target_pairs={{0,16},{4,20},{8,24},{12,28},{16,0},{20,4},{24,8},{28,12},{1,17},{... | collective-permute-start | bytes 393224 | tf_op jit(solution)/shard_map/ppermute | solution.py:89
  134.7 5.0 %collective-permute-start.22 = (f32[128,256]{1,0:T(8,128)S(1)}, f32[128,256]{1,0:T(8,128)S(1)}, u32[]{:S(2)}, u32[]{:S(2)}) collective-permute-start(f32[128,256]{1,0:T(8,128)S(1)} %collective-permute-done.20), channel_id=1, source_target_pairs={{0,8},{4,12},{8,0},{12,4},{16,24},{20,28},{24,16},{28,20},{1,9},{5... | collective-permute-start | bytes 393224 | tf_op jit(solution)/shard_map/ppermute | solution.py:89
  135.9 4.6 %collective-permute-start.24 = (f32[2,256,256]{2,1,0:T(8,128)S(1)}, f32[2,256,256]{2,1,0:T(8,128)S(1)}, u32[]{:S(2)}, u32[]{:S(2)}) collective-permute-start(f32[2,256,256]{2,1,0:T(8,128)S(1)} %pad_maximum_fusion.1.refs_0_), channel_id=1, source_target_pairs={{0,4},{4,0},{8,12},{12,8},{16,20},{20,16},{24,28},{28,24},{1,5},{5... | collective-permute-start | bytes 1572872 | tf_op jit(solution)/shard_map/ppermute | solution.py:89
  136.6 3.9 %collective-permute-start.32 = (f32[4,72,256]{2,1,0:T(8,128)S(1)}, f32[4,72,256]{2,1,0:T(8,128)S(1)}, u32[]{:S(2)}, u32[]{:S(2)}) collective-permute-start(f32[4,72,256]{2,1,0:T(8,128)S(1)} %pad_maximum_fusion.3.refs_4_), channel_id=1, source_target_pairs={{0,4},{4,0},{8,12},{12,8},{16,20},{20,16},{24,28},{28,24},{1,5},{5... | collective-permute-start | bytes 884744 | tf_op jit(solution)/shard_map/ppermute | solution.py:89
  139.7 2.0 %collective-permute-start.25 = (f32[2,256,256]{2,1,0:T(8,128)S(1)}, f32[2,256,256]{2,1,0:T(8,128)S(1)}, u32[]{:S(2)}, u32[]{:S(2)}) collective-permute-start(f32[2,256,256]{2,1,0:T(8,128)S(1)} %pad_maximum_fusion.2.refs_1_), channel_id=1, source_target_pairs={{0,4},{4,0},{8,12},{12,8},{16,20},{20,16},{24,28},{28,24},{1,5},{5... | collective-permute-start | bytes 1572872 | tf_op jit(solution)/shard_map/ppermute | solution.py:89

commit v8 on v7

--- a/solution.py
+++ b/solution.py
@@ -106,11 +106,11 @@
     payload, seen = refs.pop(0), refs.pop(0)
     squares_out = refs.pop(0) if first else None
     kept = refs.pop(0) if stream else points
-    low, norms, tallies, sums, places, even, odd, tables = refs[:8]
-    chosen_in = refs[8] if stream else assign
-    small_sems, point_sems = refs[9:11] if stream else (None, None)
-    start = refs[11] if first else fine
-    rows, width = low.shape
+    low, norms, tallies, sums, even, odd, scaled = refs[:7]
+    chosen_in = refs[7] if stream else assign
+    small_sems, point_sems = refs[8:10] if stream else (None, None)
+    start = refs[10] if first else fine
+    width, rows = low.shape
     block_width = width // SLOTS
     here = info[0]
     half = info[1] ^ flip
@@ -145,22 +145,21 @@
             load_start.wait()
         block = start[...]
         norm = jnp.sum(block * block, axis=1, keepdims=True)
-        low[...] = (-2.0 * block).astype(jnp.bfloat16)
+        low[...] = (-2.0 * block).T.astype(jnp.bfloat16)
     else:
         norm = jnp.zeros((rows, 1), jnp.float32)
         for slot in range(SLOTS):
             block = fine[slot]
             norm = norm + jnp.sum(block * block, axis=1, keepdims=True)
-            low[:, column_of(slot)] = (-2.0 * block).astype(jnp.bfloat16)
+            low[column_of(slot), :] = (-2.0 * block).T.astype(jnp.bfloat16)
     norms[...] = jnp.broadcast_to(norm, norms.shape)
     tallies[...] = jnp.zeros_like(tallies)
     sums[...] = jnp.zeros_like(sums)
-    places[...] = lax.broadcasted_iota(jnp.int32, places.shape, 0).astype(jnp.int16)
 
     def multiply(i, target):
-        target[...] = lax.dot_general(
-            low[...], kept[span(i), :], (((1,), (1,)), ((), ())), preferred_element_type=jnp.float32
-        )
+        target[...] = jnp.dot(
+            kept[span(i), :], low[...], preferred_element_type=jnp.float32
+        ).T
 
     def collect(i, products):
         energy = products[...] + jnp.concatenate([norms[...]] * (tile // 128), axis=1)
@@ -190,15 +189,15 @@
         for lane in range(0, tile, 128):
             tally = tally + weighted[:, lane : lane + 128]
         tallies[...] = tally
-        high = weights.astype(jnp.bfloat16)
-        rest = (weights - high.astype(jnp.float32)).astype(jnp.bfloat16)
-        narrow = jnp.where(inside, chosen, -1).astype(jnp.int16)
-        member = places[...] == narrow
-        nothing = jnp.zeros((rows, tile), jnp.bfloat16)
-        tables[:rows, :] = jnp.where(member, jnp.broadcast_to(high, nothing.shape), nothing)
-        tables[rows:, :] = jnp.where(member, jnp.broadcast_to(rest, nothing.shape), nothing)
-        both = jnp.dot(tables[...], kept[span(i), :], preferred_element_type=jnp.float32)
-        sums[...] += both[:rows] + both[rows:]
+        factor = as_column(weights, tile)
+        for lane in range(0, width, 128):
+            values = kept[span(i), lane : lane + 128].astype(jnp.float32)
+            scaled[:, lane : lane + 128] = (values * factor).astype(jnp.bfloat16)
+        sums[...] += jnp.dot(
+            member.astype(jnp.float32).astype(jnp.bfloat16),
+            scaled[...],
+            preferred_element_type=jnp.float32,
+        )
 
     if stream:
         load_assign.wait()
@@ -264,14 +263,13 @@
     out_shape = [jax.ShapeDtypeStruct(shape, jnp.float32) for shape in shapes]
     out_specs = [full(*shape) for shape in shapes]
     scratch = [
-        pltpu.VMEM((rows, width), jnp.bfloat16),
+        pltpu.VMEM((width, rows), jnp.bfloat16),
         pltpu.VMEM((rows, 128), jnp.float32),
         pltpu.VMEM((rows, 128), jnp.float32),
         pltpu.VMEM((rows, width), jnp.float32),
-        pltpu.VMEM((rows, tile), jnp.int16),
         pltpu.VMEM((rows, tile), jnp.float32),
         pltpu.VMEM((rows, tile), jnp.float32),
-        pltpu.VMEM((2 * rows, tile), jnp.bfloat16),
+        pltpu.VMEM((tile, width), jnp.bfloat16),
     ]
     if stream:
         scratch += [
@@ -301,7 +299,7 @@
             out_specs=out_specs,
             scratch_shapes=scratch,
         ),
-        compiler_params=pltpu.CompilerParams(vmem_limit_bytes=28 * 2**20),
+        compiler_params=pltpu.CompilerParams(vmem_limit_bytes=18 * 2**20),
         cost_estimate=pl.CostEstimate(
             flops=4 * rows * count * width, bytes_accessed=2 * count * width, transcendentals=0
         ),
@@ -376,7 +374,7 @@
     )(info, own, sibling, *incoming, owners, coarse)
 
 
-def exchange(held, sibling):
+def exchange(held, sibling, later):
     rows = held.shape[1] - TAIL
     mid = rows // 2
     top, low, tail = slice(0, mid), slice(mid, rows), slice(rows, rows + TAIL)
@@ -385,22 +383,31 @@
     corner_top = swap(jnp.concatenate([both(3, top), counts], 0), ACROSS_X)
     corner_low = swap(both(3, low), ACROSS_Y)
     counts = counts + corner_top[mid:]
-    over_y = swap(
-        jnp.concatenate([both(2, top) + corner_top[:mid], both(2, low), counts], 0), ACROSS_Y
-    )
-    over_x = swap(jnp.concatenate([both(1, top), both(1, low) + corner_low], 0), ACROSS_X)
-    return over_x, over_y, counts
-
-
-def gather_half(top, low):
+    to_y = jnp.concatenate([both(2, top) + corner_top[:mid], both(2, low), counts], 0)
+    to_x = jnp.concatenate([both(1, top), both(1, low) + corner_low], 0)
+    to_y, to_x, later = lax.optimization_barrier((to_y, to_x, later))
+    return (swap(to_x, ACROSS_X), swap(to_y, ACROSS_Y), counts), later
+
+
+def gather_half(top, low, later):
     x_low = swap(low, ACROSS_X)
     y_top = swap(top, ACROSS_Y)
     x_top = swap(top, ACROSS_X)
     y_low = swap(low, ACROSS_Y)
+    x_low, y_top, later = lax.optimization_barrier((x_low, y_top, later))
     corner_top = swap(y_top, ACROSS_X)
     corner_low = swap(x_low, ACROSS_Y)
     blocks = [(top, low), (x_top, x_low), (y_top, y_low), (corner_top, corner_low)]
-    return [jnp.concatenate(block, 0) for block in blocks]
+    return [jnp.concatenate(block, 0) for block in blocks], later
+
+
+def gather_last(top, low):
+    mid = top.shape[0]
+    block = jnp.concatenate([top, low], 0)
+    over_x, over_y = swap(block, ACROSS_X), swap(block, ACROSS_Y)
+    corner_top = swap(over_y[:mid], ACROSS_X)
+    corner_low = swap(over_x[mid:], ACROSS_Y)
+    return jnp.stack([block, over_x, over_y]), jnp.concatenate([corner_top, corner_low], 0)
 
 
 def spread(value):
@@ -408,42 +415,51 @@
     return [value, swap(value, ACROSS_X), swap(value, ACROSS_Y), corner]
 
 
-def over_cen(value, combine):
-    others = [swap(value, bit, "cen") for bit in range(1, lax.axis_size("cen"))]
-    return functools.reduce(combine, others, value)
-
-
-def place_body(info, *refs):
-    own, other = refs[:2], refs[2:4]
-    parts, others_parts, fine_out, coarse_out = refs[4:]
-    block_width = parts.shape[2]
+def over_cen(value, combine, bits=None):
+    for bit in range(lax.axis_size("cen").bit_length() - 1) if bits is None else bits:
+        value = combine(value, swap(value, 1 << bit, "cen"))
+    return value
+
+
+def fold(first, second):
+    cut = NC + TAIL
+    return jnp.concatenate(
+        [first[:cut] + second[:cut], jnp.minimum(first[cut:], second[cut:])], 0
+    )
+
+
+def place_body(info, own, other, last, last_other, fine_out, coarse_out):
+    _, rows, block_width = own.shape
     here = info[0]
 
     def column_of(slot):
         return pl.ds(pl.multiple_of((here ^ slot) * block_width, block_width), block_width)
 
-    def put(pieces):
-        for slot in range(SLOTS):
-            fine_out[:, column_of(slot)] = pieces[slot // 2][slot % 2]
+    def put(pieces, corner):
+        for slot in range(SLOTS - 1):
+            fine_out[:, column_of(slot)] = pieces[slot]
+        fine_out[:, column_of(SLOTS - 1)] = corner[:rows, :]
 
     @pl.when(pl.program_id(0) == 0)
     def _():
-        put(own)
-        weight = parts[0, NC : NC + 1, :128] + others_parts[0, NC : NC + 1, :128]
-        weight = as_column(weight, 128)[:NC, :1]
+        put(own, last)
+        part = lambda slot, start, size: (
+            last[pl.ds(rows + slot * (NC + TAIL) + start, size), :]
+            + last_other[pl.ds(rows + slot * (NC + TAIL) + start, size), :]
+        )
+        weight = as_column(part(0, NC, TAIL)[:1, :128], 128)[:NC, :1]
         for slot in range(SLOTS):
-            total = parts[slot, :NC, :] + others_parts[slot, :NC, :]
-            coarse_out[:, column_of(slot)] = total / weight
+            coarse_out[:, column_of(slot)] = part(slot, 0, NC) / weight
 
     @pl.when(pl.program_id(0) == 1)
     def _():
-        put(other)
-
-
-def place(info, own, other, parts, others_parts, *, flip):
-    _, rows, block_width = own[0].shape
+        put(other, last_other)
+
+
+def place(info, own, other, last, last_other, *, flip):
+    _, rows, block_width = own.shape
     width = SLOTS * block_width
-    args = [*own, *other, parts, others_parts]
+    args = [own, other, last, last_other]
     return pl.pallas_call(
         place_body,
         out_shape=[
@@ -478,33 +494,36 @@
     sent, seen, squares, kept = call(points, fine_assign, fine_start, None, None, flip=1)
     sibling = swap(sent, CORE)
     held, seen_first = call(kept, fine_assign, fine_start, squares, seen, flip=0)
-    incoming = exchange(held, sibling)
+    incoming, _ = exchange(held, sibling, ())
     top, low, part = refine_half(info, held, sibling, incoming, owners, coarse_start, flip=0)
-    own = jnp.stack(gather_half(top, low))
     part = part + swap(part, CORE)
-    own, part = lax.optimization_barrier((own, part))
+    seen_first = seen_first.reshape(-1, block_width)
+    own, folded = gather_half(top, low, jnp.concatenate([part, seen_first], 0))
+    bits = range(lax.axis_size("cen").bit_length() - 1)
+    folded = over_cen(folded, fold, bits[:1])
+    own, folded = lax.optimization_barrier((jnp.stack(own), folded))
     other = swap(own, CORE)
 
     call = functools.partial(run_pass, info, pass_index=1, rows=rows)
     sent, seen, kept = call(points, fine_assign, own, squares, None, flip=0)
     sibling = swap(sent, CORE)
     held, seen_second = call(kept, fine_assign, other, squares, seen, flip=1)
-    incoming = exchange(held, sibling)
-
-    seen = [each.reshape(-1, block_width) for each in (seen_first, seen_second)]
-    gathered = lax.all_gather(jnp.concatenate([part, *seen], 0), "cen")
-    part = jnp.sum(gathered[:, : NC + TAIL], axis=0)
-    seen = jnp.min(gathered[:, NC + TAIL :], axis=0).reshape(2, 2, -1)
-    gaps = (seen[:, 0] - seen[:, 1]) / math.sqrt(width)
+
+    folded = over_cen(folded, fold, bits[1:])
+    part, seen_first = folded[: NC + TAIL], folded[NC + TAIL :]
     coarse = part[:NC] / part[NC, :NC][:, None]
 
+    incoming, seen_second = exchange(held, sibling, seen_second)
+    seen_second = over_cen(seen_second, jnp.minimum)
+    seen_second, coarse = lax.optimization_barrier((seen_second, coarse))
     top, low, part = refine_half(info, held, sibling, incoming, owners, coarse, flip=1)
-    own = gather_half(top, low)
-    own = [jnp.stack(own[:2]), jnp.stack(own[2:])]
-    parts = jnp.stack(spread(over_cen(part, jnp.add)))
-    other = [swap(pair, CORE) for pair in own]
-    fine_now, coarse_now = place(info, own, other, parts, swap(parts, CORE), flip=1)
-    return (fine_now, coarse_now, gaps)
+    own, corner = gather_last(top, low)
+    parts = spread(over_cen(part, jnp.add))
+    last = jnp.concatenate([corner, *parts], 0)
+    fine_now, coarse_now = place(info, own, swap(own, CORE), last, swap(last, CORE), flip=1)
+
+    gaps = [(seen[0] - seen[1]) for seen in (seen_first.reshape(2, -1), seen_second)]
+    return (fine_now, coarse_now, jnp.stack(gaps) / math.sqrt(width))
 
 
 def solution(mesh):

time: 144 us -> 128 us (0.89)
  blocking collectives: 16.5 us -> 0 us
  waiting for transfers between devices: 32.4 us -> 45.4 us
  local copies, waits for them, and re-layouts: 7.41 us -> 0.15 us
  starting transfers between devices: 34.4 us -> 30.9 us
  Pallas kernels: 51.1 us -> 48.2 us
    all_gather x1 -> x0, blocking collectives: 16.5 us -> none  [on_device_paired(): gathered = lax.all_gather(jnp.concatenate([part, *seen], 0), 'cen')]
    ppermute x33, waiting for transfers between devices: 32.4 us -> 45.4 us  [swap(): return lax.ppermute(value, axis, [(i, i ^ bit) for i in range(size)])]
    unnamed x15 -> x16, local copies, waits for them, and re-layouts: 7.31 us -> 0.09 us
    ppermute x33, starting transfers between devices: 34.4 us -> 30.9 us  [swap(): return lax.ppermute(value, axis, [(i, i ^ bit) for i in range(size)])]
    pallas_call x4, Pallas kernels: 46 us -> 43 us  [run_pass(): pl.pallas_call(body, out_shape=out_shape, grid_spec=pltpu.PrefetchScalarG...]
  transfers between devices with their start and end apart: 33 -> 33, of which waited for: 16 -> 18; matrix products, arithmetic and copies ran while one was open for 1% -> 1% of each run, Pallas kernels for 23% -> 24%
where the time goes in v8:
time: 128 us
  Pallas kernels  48.2 us (38%)
  waiting for transfers between devices  45.4 us (35%)
  starting transfers between devices  30.9 us (24%)
  other arithmetic  2.23 us (2%)
    ppermute x33, waiting for transfers between devices, swap(): return lax.ppermute(value, axis, [(i, i ^ bit) for i in range(size)])  45.4 us
    pallas_call x4, Pallas kernels, run_pass(): pl.pallas_call(body, out_shape=out_shape, grid_spec=pltpu.PrefetchScalarG...  43 us
    ppermute x33, starting transfers between devices, swap(): return lax.ppermute(value, axis, [(i, i ^ bit) for i in range(size)])  30.9 us
    pallas_call x2, Pallas kernels, refine_half(): pl.pallas_call(refine_body, out_shape=[jax.ShapeDtypeStruct((mid, block_w...  3.04 us
  transfers between devices with their start and end apart: 33, of which 18 were waited for; matrix products, arithmetic and copies ran while one was open for 1% of the time, Pallas kernels for 24%

profile of v8, /device:TPU:0, one launch (start us, length us, event | category | flops | bytes accessed | tf_op | source)
XLA Modules:
  0.0 127.9 jit_solution(5945990868231536183)
XLA Ops:
  0.6 0.1 pad_add_fusion.info
  0.7 12.3 %energies_and_sums_00.1 = (f32[4,264,256]{2,1,0:T(8,128)S(1)}, f32[2,4096]{1,0:T(2,128)S(1)}, f32[1,4096]{1,0:T(1,128)S(1)}, bf16[4096,1024]{1,0:T(8,128)(2,1)S(1)}) custom-call(s32[4]{0:T(128)S(1)} %pad_add_fusion.info, bf16[4096,1024]{1,0:T(8,128)(2,1)} %points.3, s32[2,4096]{1,0:T(2,128)} %assign.7, f32[512,1024]{1,0:T(8,128)} %fine.3), custom_call_target="tpu_custom_call" | custom-call | flops 4294967296 | bytes 8388608 | tf_op jit(solution)/shard_map/energies_and_sums_00/pallas_call | solution.py:292
  13.0 0.9 collective-permute-start
  13.9 9.8 %energies_and_sums_01.1 = (f32[4,264,256]{2,1,0:T(8,128)S(1)}, f32[2,4096]{1,0:T(2,128)S(1)}) custom-call(s32[4]{0:T(128)S(1)} %pad_add_fusion.info, bf16[4096,1024]{1,0:T(8,128)(2,1)S(1)} %get-tuple-element.34.points, s32[2,4096]{1,0:T(2,128)S(1)} %copy-done.3, f32[512,1024]{1,0:T(8,128)S(1)} %copy-done.2, f32[1,4096]{1,0:T(1,128)S(1)} %get-tuple-element.35.refs_0_, ...), custom_call_target="tpu_custom_call" | custom-call | flops 4294967296 | bytes 8388608 | tf_op jit(solution)/shard_map/energies_and_sums_01/pallas_call | solution.py:292
  23.7 0.1 fusion.10
  23.8 2.4 %collective-permute-start.1 = (f32[136,256]{1,0:T(8,128)S(1)}, f32[136,256]{1,0:T(8,128)S(1)}, u32[]{:S(2)}, u32[]{:S(2)}) collective-permute-start(f32[136,256]{1,0:T(8,128)S(1)} %pad_maximum_fusion.6), channel_id=1, source_target_pairs={{0,8},{4,12},{8,0},{12,4},{16,24},{20,28},{24,16},{28,20},{1,9},{5... | collective-permute-start | bytes 417800 | tf_op jit(solution)/shard_map/ppermute | solution.py:89
  26.2 1.5 %collective-permute-start.2 = (f32[128,256]{1,0:T(8,128)S(1)}, f32[128,256]{1,0:T(8,128)S(1)}, u32[]{:S(2)}, u32[]{:S(2)}) collective-permute-start(f32[128,256]{1,0:T(8,128)S(1)} %get-tuple-element.74), channel_id=1, source_target_pairs={{0,16},{4,20},{8,24},{12,28},{16,0},{20,4},{24,8},{28,12},{1,17},{... | collective-permute-start | bytes 393224 | tf_op jit(solution)/shard_map/ppermute | solution.py:89
  27.7 3.9 %collective-permute-done.2 = f32[128,256]{1,0:T(8,128)S(1)} collective-permute-done((f32[128,256]{1,0:T(8,128)S(1)}, f32[128,256]{1,0:T(8,128)S(1)}, u32[]{:S(2)}, u32[]{:S(2)}) %collective-permute-start.2) | collective-permute-done | bytes 131104 | tf_op jit(solution)/shard_map/ppermute | solution.py:89
  31.6 0.1 fusion.9
  31.7 0.7 pad_maximum_fusion.4
  32.4 1.6 %collective-permute-start.4 = (f32[264,256]{1,0:T(8,128)S(1)}, f32[264,256]{1,0:T(8,128)S(1)}, u32[]{:S(2)}, u32[]{:S(2)}) collective-permute-start(f32[264,256]{1,0:T(8,128)S(1)} %pad_maximum_fusion.2), channel_id=1, source_target_pairs={{0,16},{4,20},{8,24},{12,28},{16,0},{20,4},{24,8},{28,12},{1,17},{... | collective-permute-start | bytes 811016 | tf_op jit(solution)/shard_map/ppermute | solution.py:89
  34.0 0.5 collective-permute-start.3
  34.6 6.8 %collective-permute-done.3.over_x = f32[256,256]{1,0:T(8,128)S(1)} collective-permute-done((f32[256,256]{1,0:T(8,128)}, f32[256,256]{1,0:T(8,128)S(1)}, u32[]{:S(2)}, u32[]{:S(2)}) %collective-permute-start.3) | collective-permute-done | bytes 262176 | tf_op jit(solution)/shard_map/ppermute | solution.py:89
  41.4 1.5 %refine_half.2 = (f32[128,256]{1,0:T(8,128)S(1)}, f32[128,256]{1,0:T(8,128)S(1)}, f32[72,256]{1,0:T(8,128)S(1)}) custom-call(s32[4]{0:T(128)S(1)} %pad_add_fusion.info, f32[4,264,256]{2,1,0:T(8,128)S(1)} %get-tuple-element.37.own, f32[4,264,256]{2,1,0:T(8,128)S(1)} %collective-permute-done.sibling, f32[256,256]{1,0:T(8,128)S(1)} %collective-permute-done.3.over_x, ...), custom_call_target="tpu_custom_call" | custom-call | tf_op jit(solution)/shard_map/refine_half/pallas_call | solution.py:350
  42.9 0.5 collective-permute-start.7
  43.4 0.8 collective-permute-start.5
  44.2 1.5 %collective-permute-start.9 = (f32[128,256]{1,0:T(8,128)S(1)}, f32[128,256]{1,0:T(8,128)S(1)}, u32[]{:S(2)}, u32[]{:S(2)}) collective-permute-start(f32[128,256]{1,0:T(8,128)S(1)} %get-tuple-element.42), channel_id=1, source_target_pairs={{0,16},{4,20},{8,24},{12,28},{16,0},{20,4},{24,8},{28,12},{1,17},{... | collective-permute-start | bytes 393224 | tf_op jit(solution)/shard_map/ppermute | solution.py:89
  45.7 1.3 collective-permute-start.6
  47.0 1.2 collective-permute-done.8
  48.2 2.4 %collective-permute-done.6 = f32[128,256]{1,0:T(8,128)S(1)} collective-permute-done((f32[128,256]{1,0:T(8,128)S(1)}, f32[128,256]{1,0:T(8,128)S(1)}, u32[]{:S(2)}, u32[]{:S(2)}) %collective-permute-start.6) | collective-permute-done | bytes 131104 | tf_op jit(solution)/shard_map/ppermute | solution.py:89
  50.6 1.6 %collective-permute-start.12 = (f32[104,256]{1,0:T(8,128)S(1)}, f32[104,256]{1,0:T(8,128)S(1)}, u32[]{:S(2)}, u32[]{:S(2)}) collective-permute-start(f32[104,256]{1,0:T(8,128)S(1)} %pad_maximum_fusion.8), channel_id=1, source_target_pairs={{0,1},{1,0},{2,3},{3,2},{4,5},{5,4},{6,7},{7,6},{8,9},{9,8},{10,11... | collective-permute-start | bytes 319496 | tf_op jit(solution)/shard_map/ppermute | solution.py:89
  52.2 0.6 collective-permute-start.11
  52.9 1.1 collective-permute-start.10
  54.0 1.3 %collective-permute-done.12 = f32[104,256]{1,0:T(8,128)S(1)} collective-permute-done((f32[104,256]{1,0:T(8,128)S(1)}, f32[104,256]{1,0:T(8,128)S(1)}, u32[]{:S(2)}, u32[]{:S(2)}) %collective-permute-start.12) | collective-permute-done | bytes 106528 | tf_op jit(solution)/shard_map/ppermute | solution.py:89
  55.4 1.8 %collective-permute-done.11 = f32[128,256]{1,0:T(8,128)S(1)} collective-permute-done((f32[128,256]{1,0:T(8,128)S(1)}, f32[128,256]{1,0:T(8,128)S(1)}, u32[]{:S(2)}, u32[]{:S(2)}) %collective-permute-start.11) | collective-permute-done | bytes 131104 | tf_op jit(solution)/shard_map/ppermute | solution.py:89
  57.2 0.6 collective-permute-done.10
  57.8 0.1 pad_maximum_fusion.fine
  57.9 0.1 collective-permute-start.13
  58.0 11.2 %energies_and_sums_10.1 = (f32[4,264,256]{2,1,0:T(8,128)S(1)}, f32[2,4096]{1,0:T(2,128)S(1)}, bf16[4096,1024]{1,0:T(8,128)(2,1)S(1)}) custom-call(s32[4]{0:T(128)S(1)} %pad_add_fusion.info, bf16[4096,1024]{1,0:T(8,128)(2,1)} %points.3, s32[2,4096]{1,0:T(2,128)} %assign.7, f32[4,256,256]{2,1,0:T(8,128)S(1)} %pad_maximum_fusion.fine, ...), custom_call_target="tpu_custom_call" | custom-call | flops 4294967296 | bytes 8388608 | tf_op jit(solution)/shard_map/energies_and_sums_10/pallas_call | solution.py:292
  69.2 0.5 collective-permute-start.14
  69.7 2.6 %collective-permute-start.21 = (f32[104,256]{1,0:T(8,128)S(1)}, f32[104,256]{1,0:T(8,128)S(1)}, u32[]{:S(2)}, u32[]{:S(2)}) collective-permute-start(f32[104,256]{1,0:T(8,128)S(1)} %pad_maximum_fusion.9), channel_id=1, source_target_pairs={{0,2},{1,3},{2,0},{3,1},{4,6},{5,7},{6,4},{7,5},{8,10},{9,11},{10,... | collective-permute-start | bytes 319496 | tf_op jit(solution)/shard_map/ppermute | solution.py:89
  72.3 9.8 %energies_and_sums_11.1 = (f32[4,264,256]{2,1,0:T(8,128)S(1)}, f32[2,4096]{1,0:T(2,128)S(1)}) custom-call(s32[4]{0:T(128)S(1)} %pad_add_fusion.info, bf16[4096,1024]{1,0:T(8,128)(2,1)S(1)} %get-tuple-element.49.points, s32[2,4096]{1,0:T(2,128)S(1)} %copy-done.4, f32[4,256,256]{2,1,0:T(8,128)S(1)} %collective-permute-done.13.fine, ...), custom_call_target="tpu_custom_call" | custom-call | flops 4294967296 | bytes 8388608 | tf_op jit(solution)/shard_map/energies_and_sums_11/pallas_call | solution.py:292
  82.2 0.1 fusion.3
  82.2 1.5 %collective-permute-start.16 = (f32[128,256]{1,0:T(8,128)S(1)}, f32[128,256]{1,0:T(8,128)S(1)}, u32[]{:S(2)}, u32[]{:S(2)}) collective-permute-start(f32[128,256]{1,0:T(8,128)S(1)} %get-tuple-element.68), channel_id=1, source_target_pairs={{0,16},{4,20},{8,24},{12,28},{16,0},{20,4},{24,8},{28,12},{1,17},{... | collective-permute-start | bytes 393224 | tf_op jit(solution)/shard_map/ppermute | solution.py:89
  83.7 1.3 %collective-permute-start.15 = (f32[136,256]{1,0:T(8,128)S(1)}, f32[136,256]{1,0:T(8,128)S(1)}, u32[]{:S(2)}, u32[]{:S(2)}) collective-permute-start(f32[136,256]{1,0:T(8,128)S(1)} %pad_maximum_fusion.7), channel_id=1, source_target_pairs={{0,8},{4,12},{8,0},{12,4},{16,24},{20,28},{24,16},{28,20},{1,9},{5... | collective-permute-start | bytes 417800 | tf_op jit(solution)/shard_map/ppermute | solution.py:89
  85.0 2.4 %collective-permute-done.16 = f32[128,256]{1,0:T(8,128)S(1)} collective-permute-done((f32[128,256]{1,0:T(8,128)S(1)}, f32[128,256]{1,0:T(8,128)S(1)}, u32[]{:S(2)}, u32[]{:S(2)}) %collective-permute-start.16) | collective-permute-done | bytes 131104 | tf_op jit(solution)/shard_map/ppermute | solution.py:89
  87.5 1.4 %collective-permute-done.15 = f32[136,256]{1,0:T(8,128)S(1)} collective-permute-done((f32[136,256]{1,0:T(8,128)S(1)}, f32[136,256]{1,0:T(8,128)S(1)}, u32[]{:S(2)}, u32[]{:S(2)}) %collective-permute-start.15) | collective-permute-done | bytes 139296 | tf_op jit(solution)/shard_map/ppermute | solution.py:89
  89.0 0.5 collective-permute-start.19
  89.5 1.3 collective-permute-start.17
  90.7 0.5 collective-permute-start.18
  91.3 1.7 %collective-permute-done.19 = f32[2,4096]{1,0:T(2,128)S(1)} collective-permute-done((f32[2,4096]{1,0:T(2,128)S(1)}, f32[2,4096]{1,0:T(2,128)S(1)}, u32[]{:S(2)}, u32[]{:S(2)}) %collective-permute-start.19) | collective-permute-done | bytes 32800 | tf_op jit(solution)/shard_map/ppermute | solution.py:89
  93.0 0.4 collective-permute-start.20
  93.4 0.1 slice_divide_fusion.coarse
  93.5 4.6 %collective-permute-done.20 = f32[2,4096]{1,0:T(2,128)S(1)} collective-permute-done((f32[2,4096]{1,0:T(2,128)S(1)}, f32[2,4096]{1,0:T(2,128)S(1)}, u32[]{:S(2)}, u32[]{:S(2)}) %collective-permute-start.20) | collective-permute-done | bytes 32800 | tf_op jit(solution)/shard_map/ppermute | solution.py:89
  98.1 1.5 %refine_half.3 = (f32[128,256]{1,0:T(8,128)S(1)}, f32[128,256]{1,0:T(8,128)S(1)}, f32[72,256]{1,0:T(8,128)S(1)}) custom-call(s32[4]{0:T(128)S(1)} %pad_add_fusion.info, f32[4,264,256]{2,1,0:T(8,128)S(1)} %get-tuple-element.51.own, f32[4,264,256]{2,1,0:T(8,128)S(1)} %collective-permute-done.14.sibling, f32[256,256]{1,0:T(8,128)S(1)} %collective-permute-done.17.over_x, ...), custom_call_target="tpu_custom_call" | custom-call | tf_op jit(solution)/shard_map/refine_half/pallas_call | solution.py:350
  99.7 0.8 collective-permute-start.23
  100.5 1.0 collective-permute-start.22
  101.5 0.3 collective-permute-start.27
  101.8 5.3 %collective-permute-done.23 = f32[256,256]{1,0:T(8,128)S(1)} collective-permute-done((f32[256,256]{1,0:T(8,128)S(1)}, f32[256,256]{1,0:T(8,128)S(1)}, u32[]{:S(2)}, u32[]{:S(2)}) %collective-permute-start.23) | collective-permute-done | bytes 262176 | tf_op jit(solution)/shard_map/ppermute | solution.py:89
  107.2 1.7 %collective-permute-start.25 = (f32[128,256]{1,0:T(8,128)S(1)}, f32[128,256]{1,0:T(8,128)S(1)}, u32[]{:S(2)}, u32[]{:S(2)}) collective-permute-start(f32[128,256]{1,0:T(8,128)S(1)} %slice.217), channel_id=1, source_target_pairs={{0,8},{4,12},{8,0},{12,4},{16,24},{20,28},{24,16},{28,20},{1,9},{5... | collective-permute-start | bytes 393224 | tf_op jit(solution)/shard_map/ppermute | solution.py:89
  108.9 0.1 collective-permute-start.26
  109.1 0.2 collective-permute-start.28
  109.2 3.4 %collective-permute-done.25 = f32[128,256]{1,0:T(8,128)S(1)} collective-permute-done((f32[128,256]{1,0:T(8,128)S(1)}, f32[128,256]{1,0:T(8,128)S(1)}, u32[]{:S(2)}, u32[]{:S(2)}) %collective-permute-start.25) | collective-permute-done | bytes 131104 | tf_op jit(solution)/shard_map/ppermute | solution.py:89
  112.6 1.4 %collective-permute-done.26 = f32[128,256]{1,0:T(8,128)S(1)} collective-permute-done((f32[128,256]{1,0:T(8,128)S(1)}, f32[128,256]{1,0:T(8,128)S(1)}, u32[]{:S(2)}, u32[]{:S(2)}) %collective-permute-start.26) | collective-permute-done | bytes 131104 | tf_op jit(solution)/shard_map/ppermute | solution.py:89
  114.0 0.4 collective-permute-done.28
  114.4 2.0 %collective-permute-start.29 = (f32[72,256]{1,0:T(8,128)S(1)}, f32[72,256]{1,0:T(8,128)S(1)}, u32[]{:S(2)}, u32[]{:S(2)}) collective-permute-start(f32[72,256]{1,0:T(8,128)S(1)} %get-tuple-element.66), channel_id=1, source_target_pairs={{0,8},{4,12},{8,0},{12,4},{16,24},{20,28},{24,16},{28,20},{1,9},{5... | collective-permute-start | bytes 221192 | tf_op jit(solution)/shard_map/ppermute | solution.py:89
  116.5 0.1 collective-permute-start.24
  116.6 1.7 %collective-permute-start.31 = (f32[72,256]{1,0:T(8,128)S(1)}, f32[72,256]{1,0:T(8,128)S(1)}, u32[]{:S(2)}, u32[]{:S(2)}) collective-permute-start(f32[72,256]{1,0:T(8,128)S(1)} %get-tuple-element.66), channel_id=1, source_target_pairs={{0,24},{4,28},{8,16},{12,20},{16,8},{20,12},{24,0},{28,4},{1,25},{... | collective-permute-start | bytes 221192 | tf_op jit(solution)/shard_map/ppermute | solution.py:89
  118.3 0.5 collective-permute-done.29
  118.8 4.9 %collective-permute-done.30 = f32[72,256]{1,0:T(8,128)S(1)} collective-permute-done((f32[72,256]{1,0:T(8,128)S(1)}, f32[72,256]{1,0:T(8,128)S(1)}, u32[]{:S(2)}, u32[]{:S(2)}) %collective-permute-start.30) | collective-permute-done | bytes 73760 | tf_op jit(solution)/shard_map/ppermute | solution.py:89
  123.8 0.1 collective-permute-start.32
  123.9 0.7 maximum_multiply_fusion
  124.5 1.2 collective-permute-done.32.last_other
  125.8 2.1 %place_blocks.1 = (f32[512,1024]{1,0:T(8,128)}, f32[64,1024]{1,0:T(8,128)}) custom-call(s32[4]{0:T(128)S(1)} %pad_add_fusion.info, f32[3,256,256]{2,1,0:T(8,128)S(1)} %pad_maximum_fusion.1.own, f32[3,256,256]{2,1,0:T(8,128)S(1)} %collective-permute-done.24.other, f32[544,256]{1,0:T(8,128)S(1)} %constant_dynamic-update-slice_fusion.2.last, ...), custom_call_target="tpu_custom_call" | custom-call | tf_op jit(solution)/shard_map/place_blocks/pallas_call | solution.py:463
  (67 shorter events, 0.6 us)
Async XLA Ops:
  0.7 13.2 %copy-start.2 = (f32[512,1024]{1,0:T(8,128)S(1)}, f32[512,1024]{1,0:T(8,128)}, u32[]{:S(2)}) copy-start(f32[512,1024]{1,0:T(8,128)} %fine.3) | copy-start | bytes 6291460
  0.7 13.2 %copy-start.3 = (s32[2,4096]{1,0:T(2,128)S(1)}, s32[2,4096]{1,0:T(2,128)}, u32[]{:S(2)}) copy-start(s32[2,4096]{1,0:T(2,128)} %assign.7) | copy-start | bytes 98308
  13.0 10.7 %collective-permute-start = (f32[4,264,256]{2,1,0:T(8,128)S(1)}, f32[4,264,256]{2,1,0:T(8,128)S(1)}, u32[]{:S(2)}, u32[]{:S(2)}) collective-permute-start(f32[4,264,256]{2,1,0:T(8,128)S(1)} %get-tuple-element.38), channel_id=1, source_target_pairs={{0,4},{4,0},{8,12},{12,8},{16,20},{20,16},{24,28},{28,24},{1,5},{5... | collective-permute-start | bytes 3244040 | tf_op jit(solution)/shard_map/ppermute | solution.py:89
  23.8 7.8 %collective-permute-start.1 = (f32[136,256]{1,0:T(8,128)S(1)}, f32[136,256]{1,0:T(8,128)S(1)}, u32[]{:S(2)}, u32[]{:S(2)}) collective-permute-start(f32[136,256]{1,0:T(8,128)S(1)} %pad_maximum_fusion.6), channel_id=1, source_target_pairs={{0,8},{4,12},{8,0},{12,4},{16,24},{20,28},{24,16},{28,20},{1,9},{5... | collective-permute-start | bytes 417800 | tf_op jit(solution)/shard_map/ppermute | solution.py:89
  26.2 15.2 %copy-start = (f32[64,1024]{1,0:T(8,128)S(1)}, f32[64,1024]{1,0:T(8,128)}, u32[]{:S(2)}) copy-start(f32[64,1024]{1,0:T(8,128)} %coarse.1) | copy-start | bytes 786436
  26.2 15.2 %copy-start.1 = (s32[512]{0:T(512)S(1)}, s32[512]{0:T(512)}, u32[]{:S(2)}) copy-start(s32[512]{0:T(512)} %param.9) | copy-start | bytes 6148
  26.2 5.4 %collective-permute-start.2 = (f32[128,256]{1,0:T(8,128)S(1)}, f32[128,256]{1,0:T(8,128)S(1)}, u32[]{:S(2)}, u32[]{:S(2)}) collective-permute-start(f32[128,256]{1,0:T(8,128)S(1)} %get-tuple-element.74), channel_id=1, source_target_pairs={{0,16},{4,20},{8,24},{12,28},{16,0},{20,4},{24,8},{28,12},{1,17},{... | collective-permute-start | bytes 393224 | tf_op jit(solution)/shard_map/ppermute | solution.py:89
  32.4 8.9 %collective-permute-start.4 = (f32[264,256]{1,0:T(8,128)S(1)}, f32[264,256]{1,0:T(8,128)S(1)}, u32[]{:S(2)}, u32[]{:S(2)}) collective-permute-start(f32[264,256]{1,0:T(8,128)S(1)} %pad_maximum_fusion.2), channel_id=1, source_target_pairs={{0,16},{4,20},{8,24},{12,28},{16,0},{20,4},{24,8},{28,12},{1,17},{... | collective-permute-start | bytes 811016 | tf_op jit(solution)/shard_map/ppermute | solution.py:89
  34.0 7.3 %collective-permute-start.3 = (f32[256,256]{1,0:T(8,128)}, f32[256,256]{1,0:T(8,128)S(1)}, u32[]{:S(2)}, u32[]{:S(2)}) collective-permute-start(f32[256,256]{1,0:T(8,128)} %pad_maximum_fusion.4), channel_id=1, source_target_pairs={{0,8},{4,12},{8,0},{12,4},{16,24},{20,28},{24,16},{28,20},{1,9},{5... | collective-permute-start | bytes 786440 | tf_op jit(solution)/shard_map/ppermute | solution.py:89
  42.9 5.4 %collective-permute-start.7 = (f32[128,256]{1,0:T(8,128)S(1)}, f32[128,256]{1,0:T(8,128)S(1)}, u32[]{:S(2)}, u32[]{:S(2)}) collective-permute-start(f32[128,256]{1,0:T(8,128)S(1)} %get-tuple-element.41), channel_id=1, source_target_pairs={{0,16},{4,20},{8,24},{12,28},{16,0},{20,4},{24,8},{28,12},{1,17},{... | collective-permute-start | bytes 393224 | tf_op jit(solution)/shard_map/ppermute | solution.py:89
  43.4 10.6 %collective-permute-start.5 = (f32[128,256]{1,0:T(8,128)S(1)}, f32[128,256]{1,0:T(8,128)S(1)}, u32[]{:S(2)}, u32[]{:S(2)}) collective-permute-start(f32[128,256]{1,0:T(8,128)S(1)} %get-tuple-element.41), channel_id=1, source_target_pairs={{0,8},{4,12},{8,0},{12,4},{16,24},{20,28},{24,16},{28,20},{1,9},{5... | collective-permute-start | bytes 393224 | tf_op jit(solution)/shard_map/ppermute | solution.py:89
  44.2 9.9 %collective-permute-start.9 = (f32[128,256]{1,0:T(8,128)S(1)}, f32[128,256]{1,0:T(8,128)S(1)}, u32[]{:S(2)}, u32[]{:S(2)}) collective-permute-start(f32[128,256]{1,0:T(8,128)S(1)} %get-tuple-element.42), channel_id=1, source_target_pairs={{0,16},{4,20},{8,24},{12,28},{16,0},{20,4},{24,8},{28,12},{1,17},{... | collective-permute-start | bytes 393224 | tf_op jit(solution)/shard_map/ppermute | solution.py:89
  45.7 5.0 %collective-permute-start.6 = (f32[128,256]{1,0:T(8,128)S(1)}, f32[128,256]{1,0:T(8,128)S(1)}, u32[]{:S(2)}, u32[]{:S(2)}) collective-permute-start(f32[128,256]{1,0:T(8,128)S(1)} %get-tuple-element.42), channel_id=1, source_target_pairs={{0,8},{4,12},{8,0},{12,4},{16,24},{20,28},{24,16},{28,20},{1,9},{5... | collective-permute-start | bytes 393224 | tf_op jit(solution)/shard_map/ppermute | solution.py:89
  46.9 1.3 collective-permute-start.8
  50.6 4.7 %collective-permute-start.12 = (f32[104,256]{1,0:T(8,128)S(1)}, f32[104,256]{1,0:T(8,128)S(1)}, u32[]{:S(2)}, u32[]{:S(2)}) collective-permute-start(f32[104,256]{1,0:T(8,128)S(1)} %pad_maximum_fusion.8), channel_id=1, source_target_pairs={{0,1},{1,0},{2,3},{3,2},{4,5},{5,4},{6,7},{7,6},{8,9},{9,8},{10,11... | collective-permute-start | bytes 319496 | tf_op jit(solution)/shard_map/ppermute | solution.py:89
  52.2 5.0 %collective-permute-start.11 = (f32[128,256]{1,0:T(8,128)S(1)}, f32[128,256]{1,0:T(8,128)S(1)}, u32[]{:S(2)}, u32[]{:S(2)}) collective-permute-start(f32[128,256]{1,0:T(8,128)S(1)} %collective-permute-done.6), channel_id=1, source_target_pairs={{0,16},{4,20},{8,24},{12,28},{16,0},{20,4},{24,8},{28,12},{1,17},{... | collective-permute-start | bytes 393224 | tf_op jit(solution)/shard_map/ppermute | solution.py:89
  52.9 5.0 %collective-permute-start.10 = (f32[128,256]{1,0:T(8,128)S(1)}, f32[128,256]{1,0:T(8,128)S(1)}, u32[]{:S(2)}, u32[]{:S(2)}) collective-permute-start(f32[128,256]{1,0:T(8,128)S(1)} %collective-permute-done.7), channel_id=1, source_target_pairs={{0,8},{4,12},{8,0},{12,4},{16,24},{20,28},{24,16},{28,20},{1,9},{5... | collective-permute-start | bytes 393224 | tf_op jit(solution)/shard_map/ppermute | solution.py:89
  57.9 14.4 %copy-start.4 = (s32[2,4096]{1,0:T(2,128)S(1)}, s32[2,4096]{1,0:T(2,128)}, u32[]{:S(2)}) copy-start(s32[2,4096]{1,0:T(2,128)} %assign.7) | copy-start | bytes 98308
  57.9 14.4 %collective-permute-start.13 = (f32[4,256,256]{2,1,0:T(8,128)S(1)}, f32[4,256,256]{2,1,0:T(8,128)S(1)}, u32[]{:S(2)}, u32[]{:S(2)}) collective-permute-start(f32[4,256,256]{2,1,0:T(8,128)S(1)} %pad_maximum_fusion.fine), channel_id=1, source_target_pairs={{0,4},{4,0},{8,12},{12,8},{16,20},{20,16},{24,28},{28,24},{1,5},{5... | collective-permute-start | bytes 3145736 | tf_op jit(solution)/shard_map/ppermute | solution.py:89
  69.2 13.0 %collective-permute-start.14 = (f32[4,264,256]{2,1,0:T(8,128)S(1)}, f32[4,264,256]{2,1,0:T(8,128)S(1)}, u32[]{:S(2)}, u32[]{:S(2)}) collective-permute-start(f32[4,264,256]{2,1,0:T(8,128)S(1)} %get-tuple-element.52), channel_id=1, source_target_pairs={{0,4},{4,0},{8,12},{12,8},{16,20},{20,16},{24,28},{28,24},{1,5},{5... | collective-permute-start | bytes 3244040 | tf_op jit(solution)/shard_map/ppermute | solution.py:89
  69.7 15.3 %collective-permute-start.21 = (f32[104,256]{1,0:T(8,128)S(1)}, f32[104,256]{1,0:T(8,128)S(1)}, u32[]{:S(2)}, u32[]{:S(2)}) collective-permute-start(f32[104,256]{1,0:T(8,128)S(1)} %pad_maximum_fusion.9), channel_id=1, source_target_pairs={{0,2},{1,3},{2,0},{3,1},{4,6},{5,7},{6,4},{7,5},{8,10},{9,11},{10,... | collective-permute-start | bytes 319496 | tf_op jit(solution)/shard_map/ppermute | solution.py:89
  82.2 5.3 %collective-permute-start.16 = (f32[128,256]{1,0:T(8,128)S(1)}, f32[128,256]{1,0:T(8,128)S(1)}, u32[]{:S(2)}, u32[]{:S(2)}) collective-permute-start(f32[128,256]{1,0:T(8,128)S(1)} %get-tuple-element.68), channel_id=1, source_target_pairs={{0,16},{4,20},{8,24},{12,28},{16,0},{20,4},{24,8},{28,12},{1,17},{... | collective-permute-start | bytes 393224 | tf_op jit(solution)/shard_map/ppermute | solution.py:89
  83.7 5.2 %collective-permute-start.15 = (f32[136,256]{1,0:T(8,128)S(1)}, f32[136,256]{1,0:T(8,128)S(1)}, u32[]{:S(2)}, u32[]{:S(2)}) collective-permute-start(f32[136,256]{1,0:T(8,128)S(1)} %pad_maximum_fusion.7), channel_id=1, source_target_pairs={{0,8},{4,12},{8,0},{12,4},{16,24},{20,28},{24,16},{28,20},{1,9},{5... | collective-permute-start | bytes 417800 | tf_op jit(solution)/shard_map/ppermute | solution.py:89
  89.0 4.0 %collective-permute-start.19 = (f32[2,4096]{1,0:T(2,128)S(1)}, f32[2,4096]{1,0:T(2,128)S(1)}, u32[]{:S(2)}, u32[]{:S(2)}) collective-permute-start(f32[2,4096]{1,0:T(2,128)S(1)} %get-tuple-element.56), channel_id=1, source_target_pairs={{0,1},{1,0},{2,3},{3,2},{4,5},{5,4},{6,7},{7,6},{8,9},{9,8},{10,11... | collective-permute-start | bytes 98312 | tf_op jit(solution)/shard_map/ppermute | solution.py:89
  89.5 8.6 %collective-permute-start.17 = (f32[256,256]{1,0:T(8,128)S(1)}, f32[256,256]{1,0:T(8,128)S(1)}, u32[]{:S(2)}, u32[]{:S(2)}) collective-permute-start(f32[256,256]{1,0:T(8,128)S(1)} %pad_maximum_fusion.5), channel_id=1, source_target_pairs={{0,8},{4,12},{8,0},{12,4},{16,24},{20,28},{24,16},{28,20},{1,9},{5... | collective-permute-start | bytes 786440 | tf_op jit(solution)/shard_map/ppermute | solution.py:89
  90.7 7.4 %collective-permute-start.18 = (f32[264,256]{1,0:T(8,128)S(1)}, f32[264,256]{1,0:T(8,128)S(1)}, u32[]{:S(2)}, u32[]{:S(2)}) collective-permute-start(f32[264,256]{1,0:T(8,128)S(1)} %pad_maximum_fusion.3), channel_id=1, source_target_pairs={{0,16},{4,20},{8,24},{12,28},{16,0},{20,4},{24,8},{28,12},{1,17},{... | collective-permute-start | bytes 811016 | tf_op jit(solution)/shard_map/ppermute | solution.py:89
  93.0 5.1 %collective-permute-start.20 = (f32[2,4096]{1,0:T(2,128)S(1)}, f32[2,4096]{1,0:T(2,128)S(1)}, u32[]{:S(2)}, u32[]{:S(2)}) collective-permute-start(f32[2,4096]{1,0:T(2,128)S(1)} %min.13), channel_id=1, source_target_pairs={{0,2},{1,3},{2,0},{3,1},{4,6},{5,7},{6,4},{7,5},{8,10},{9,11},{10,... | collective-permute-start | bytes 98312 | tf_op jit(solution)/shard_map/ppermute | solution.py:89
  99.7 7.5 %collective-permute-start.23 = (f32[256,256]{1,0:T(8,128)S(1)}, f32[256,256]{1,0:T(8,128)S(1)}, u32[]{:S(2)}, u32[]{:S(2)}) collective-permute-start(f32[256,256]{1,0:T(8,128)S(1)} %constant_dynamic-update-slice_fusion), channel_id=1, source_target_pairs={{0,16},{4,20},{8,24},{12,28},{16,0},{20,4},{24,8},{28,12},{1,17},{... | collective-permute-start | bytes 786440 | tf_op jit(solution)/shard_map/ppermute | solution.py:89
  100.5 8.4 %collective-permute-start.22 = (f32[256,256]{1,0:T(8,128)S(1)}, f32[256,256]{1,0:T(8,128)S(1)}, u32[]{:S(2)}, u32[]{:S(2)}) collective-permute-start(f32[256,256]{1,0:T(8,128)S(1)} %constant_dynamic-update-slice_fusion), channel_id=1, source_target_pairs={{0,8},{4,12},{8,0},{12,4},{16,24},{20,28},{24,16},{28,20},{1,9},{5... | collective-permute-start | bytes 786440 | tf_op jit(solution)/shard_map/ppermute | solution.py:89
  101.5 7.5 %collective-permute-start.27 = (f32[72,256]{1,0:T(8,128)S(1)}, f32[72,256]{1,0:T(8,128)S(1)}, u32[]{:S(2)}, u32[]{:S(2)}) collective-permute-start(f32[72,256]{1,0:T(8,128)S(1)} %get-tuple-element.61), channel_id=1, source_target_pairs={{0,1},{1,0},{2,3},{3,2},{4,5},{5,4},{6,7},{7,6},{8,9},{9,8},{10,11... | collective-permute-start | bytes 221192 | tf_op jit(solution)/shard_map/ppermute | solution.py:89
  107.2 5.4 %collective-permute-start.25 = (f32[128,256]{1,0:T(8,128)S(1)}, f32[128,256]{1,0:T(8,128)S(1)}, u32[]{:S(2)}, u32[]{:S(2)}) collective-permute-start(f32[128,256]{1,0:T(8,128)S(1)} %slice.217), channel_id=1, source_target_pairs={{0,8},{4,12},{8,0},{12,4},{16,24},{20,28},{24,16},{28,20},{1,9},{5... | collective-permute-start | bytes 393224 | tf_op jit(solution)/shard_map/ppermute | solution.py:89
  108.9 5.0 %collective-permute-start.26 = (f32[128,256]{1,0:T(8,128)S(1)}, f32[128,256]{1,0:T(8,128)S(1)}, u32[]{:S(2)}, u32[]{:S(2)}) collective-permute-start(f32[128,256]{1,0:T(8,128)S(1)} %slice.218), channel_id=1, source_target_pairs={{0,16},{4,20},{8,24},{12,28},{16,0},{20,4},{24,8},{28,12},{1,17},{... | collective-permute-start | bytes 393224 | tf_op jit(solution)/shard_map/ppermute | solution.py:89
  109.1 5.3 %collective-permute-start.28 = (f32[72,256]{1,0:T(8,128)S(1)}, f32[72,256]{1,0:T(8,128)S(1)}, u32[]{:S(2)}, u32[]{:S(2)}) collective-permute-start(f32[72,256]{1,0:T(8,128)S(1)} %add.158), channel_id=1, source_target_pairs={{0,2},{1,3},{2,0},{3,1},{4,6},{5,7},{6,4},{7,5},{8,10},{9,11},{10,... | collective-permute-start | bytes 221192 | tf_op jit(solution)/shard_map/ppermute | solution.py:89
  114.4 4.4 %collective-permute-start.29 = (f32[72,256]{1,0:T(8,128)S(1)}, f32[72,256]{1,0:T(8,128)S(1)}, u32[]{:S(2)}, u32[]{:S(2)}) collective-permute-start(f32[72,256]{1,0:T(8,128)S(1)} %get-tuple-element.66), channel_id=1, source_target_pairs={{0,8},{4,12},{8,0},{12,4},{16,24},{20,28},{24,16},{28,20},{1,9},{5... | collective-permute-start | bytes 221192 | tf_op jit(solution)/shard_map/ppermute | solution.py:89
  116.5 9.3 %collective-permute-start.24 = (f32[3,256,256]{2,1,0:T(8,128)S(1)}, f32[3,256,256]{2,1,0:T(8,128)S(1)}, u32[]{:S(2)}, u32[]{:S(2)}) collective-permute-start(f32[3,256,256]{2,1,0:T(8,128)S(1)} %pad_maximum_fusion.1.own), channel_id=1, source_target_pairs={{0,4},{4,0},{8,12},{12,8},{16,20},{20,16},{24,28},{28,24},{1,5},{5... | collective-permute-start | bytes 2359304 | tf_op jit(solution)/shard_map/ppermute | solution.py:89
  116.6 7.2 %collective-permute-start.31 = (f32[72,256]{1,0:T(8,128)S(1)}, f32[72,256]{1,0:T(8,128)S(1)}, u32[]{:S(2)}, u32[]{:S(2)}) collective-permute-start(f32[72,256]{1,0:T(8,128)S(1)} %get-tuple-element.66), channel_id=1, source_target_pairs={{0,24},{4,28},{8,16},{12,20},{16,8},{20,12},{24,0},{28,4},{1,25},{... | collective-permute-start | bytes 221192 | tf_op jit(solution)/shard_map/ppermute | solution.py:89
  118.3 5.5 %collective-permute-start.30 = (f32[72,256]{1,0:T(8,128)S(1)}, f32[72,256]{1,0:T(8,128)S(1)}, u32[]{:S(2)}, u32[]{:S(2)}) collective-permute-start(f32[72,256]{1,0:T(8,128)S(1)} %get-tuple-element.66), channel_id=1, source_target_pairs={{0,16},{4,20},{8,24},{12,28},{16,0},{20,4},{24,8},{28,12},{1,17},{... | collective-permute-start | bytes 221192 | tf_op jit(solution)/shard_map/ppermute | solution.py:89
  123.8 2.0 %collective-permute-start.32 = (f32[544,256]{1,0:T(8,128)S(1)}, f32[544,256]{1,0:T(8,128)S(1)}, u32[]{:S(2)}, u32[]{:S(2)}) collective-permute-start(f32[544,256]{1,0:T(8,128)S(1)} %constant_dynamic-update-slice_fusion.2.last), channel_id=1, source_target_pairs={{0,4},{4,0},{8,12},{12,8},{16,20},{20,16},{24,28},{28,24},{1,5},{5... | collective-permute-start | bytes 1671176 | tf_op jit(solution)/shard_map/ppermute | solution.py:89

commit v9 on v8

--- a/solution.py
+++ b/solution.py
@@ -89,6 +89,21 @@
     return lax.ppermute(value, axis, [(i, i ^ bit) for i in range(size)])
 
 
+def swap_first(value):
+    pairs = [(i, i ^ (ACROSS_Y if i & CORE else ACROSS_X)) for i in range(lax.axis_size("pts"))]
+    return lax.ppermute(value, "pts", pairs)
+
+
+def swap_second(value):
+    pairs = [(i, i ^ (ACROSS_X if i & CORE else ACROSS_Y)) for i in range(lax.axis_size("pts"))]
+    return lax.ppermute(value, "pts", pairs)
+
+
+def block_of(info, slot, core):
+    crossed = (slot >> 1) | ((slot & 1) << 1)
+    return info[0] ^ (slot + core * (crossed - slot))
+
+
 def full(*shape):
     return pl.BlockSpec(shape, lambda i, info: (0,) * len(shape))
 
@@ -110,9 +125,8 @@
     chosen_in = refs[7] if stream else assign
     small_sems, point_sems = refs[8:10] if stream else (None, None)
     start = refs[10] if first else fine
-    width, rows = low.shape
+    rows, width = low.shape
     block_width = width // SLOTS
-    here = info[0]
     half = info[1] ^ flip
     base = info[2] + half * rows
     tiles = points.shape[0] // tile
@@ -120,8 +134,9 @@
     def span(i):
         return pl.ds(pl.multiple_of(i * tile, tile), tile)
 
-    def column_of(slot):
-        return pl.ds(pl.multiple_of((here ^ slot) * block_width, block_width), block_width)
+    def column_of(slot, core):
+        start = block_of(info, slot, core) * block_width
+        return pl.ds(pl.multiple_of(start, block_width), block_width)
 
     def load(i):
         return pltpu.make_async_copy(points.at[span(i)], kept.at[span(i)], point_sems.at[i])
@@ -145,21 +160,21 @@
             load_start.wait()
         block = start[...]
         norm = jnp.sum(block * block, axis=1, keepdims=True)
-        low[...] = (-2.0 * block).T.astype(jnp.bfloat16)
+        low[...] = (-2.0 * block).astype(jnp.bfloat16)
     else:
         norm = jnp.zeros((rows, 1), jnp.float32)
         for slot in range(SLOTS):
             block = fine[slot]
             norm = norm + jnp.sum(block * block, axis=1, keepdims=True)
-            low[column_of(slot), :] = (-2.0 * block).T.astype(jnp.bfloat16)
+            low[:, column_of(slot, info[1] ^ chained)] = (-2.0 * block).astype(jnp.bfloat16)
     norms[...] = jnp.broadcast_to(norm, norms.shape)
     tallies[...] = jnp.zeros_like(tallies)
     sums[...] = jnp.zeros_like(sums)
 
     def multiply(i, target):
-        target[...] = jnp.dot(
-            kept[span(i), :], low[...], preferred_element_type=jnp.float32
-        ).T
+        target[...] = lax.dot_general(
+            low[...], kept[span(i), :], (((1,), (1,)), ((), ())), preferred_element_type=jnp.float32
+        )
 
     def collect(i, products):
         energy = products[...] + jnp.concatenate([norms[...]] * (tile // 128), axis=1)
@@ -223,7 +238,7 @@
 
     counts = jnp.broadcast_to(jnp.sum(tallies[...].T, axis=0, keepdims=True), (TAIL, rows))
     for slot in range(SLOTS):
-        payload[slot, :rows, :] = sums[:, column_of(slot)]
+        payload[slot, :rows, :] = sums[:, column_of(slot, info[1] ^ (not chained))]
         payload[slot, rows:, :] = counts
 
 
@@ -263,7 +278,7 @@
     out_shape = [jax.ShapeDtypeStruct(shape, jnp.float32) for shape in shapes]
     out_specs = [full(*shape) for shape in shapes]
     scratch = [
-        pltpu.VMEM((width, rows), jnp.bfloat16),
+        pltpu.VMEM((rows, width), jnp.bfloat16),
         pltpu.VMEM((rows, 128), jnp.float32),
         pltpu.VMEM((rows, 128), jnp.float32),
         pltpu.VMEM((rows, width), jnp.float32),
@@ -307,11 +322,10 @@
     )(info, *args)
 
 
-def refine_body(info, own, sibling, over_x, over_y, tail, owner, coarse, *outs):
-    top, low, part = outs
+def refine_body(info, own, sibling, first, second, owner, coarse, fine, part):
     rows = owner.shape[1]
-    mid = rows // 2
-    counts_row = tail[...] + over_y[rows:, :]
+    total = (own[...] + sibling[...]) + (first[...] + second[...])
+    totals, counts_row = total[:rows], total[rows:]
     counts = as_column(counts_row[:1], rows)[:, :1]
     table = (
         lax.broadcasted_iota(jnp.int32, (NC, rows), 0) == owner[...]
@@ -323,10 +337,8 @@
         precision=HIGHEST,
         preferred_element_type=jnp.float32,
     )
-    totals = (own[:rows, :] + sibling[:rows, :]) + (over_x[...] + over_y[:rows, :])
     new = (totals + prior_weight * lookup) / (counts + prior_weight)
-    top[...] = new[:mid]
-    low[...] = new[mid:]
+    fine[...] = new
     prior = jnp.where(info[3] == 0, prior_weight, 0.0)
     part[:NC, :] = prior * coarse[...] + jnp.dot(
         table, counts * new, precision=HIGHEST, preferred_element_type=jnp.float32
@@ -341,78 +353,39 @@
     )
 
 
-def refine_half(info, own, sibling, incoming, owners, coarse, *, flip):
+def refine_half(info, own, sibling, first, second, owners, coarse, *, flip):
     _, rows, block_width = own.shape
     rows -= TAIL
-    mid = rows // 2
     slot = pl.BlockSpec((None, rows + TAIL, block_width), lambda i, info: (0, 0, 0))
     wide = coarse.shape[1] != block_width
     return pl.pallas_call(
         refine_body,
         out_shape=[
-            jax.ShapeDtypeStruct((mid, block_width), jnp.float32),
-            jax.ShapeDtypeStruct((mid, block_width), jnp.float32),
+            jax.ShapeDtypeStruct((rows, block_width), jnp.float32),
             jax.ShapeDtypeStruct((NC + TAIL, block_width), jnp.float32),
         ],
         grid_spec=pltpu.PrefetchScalarGridSpec(
             num_scalar_prefetch=1,
             grid=(1,),
-            in_specs=[slot] * 2
-            + [full(*value.shape) for value in incoming]
-            + [
+            in_specs=[
+                slot,
+                slot,
+                slot,
+                full(*second.shape),
                 pl.BlockSpec((None, 1, rows), lambda i, info: (info[1] ^ flip, 0, 0)),
                 pl.BlockSpec((NC, block_width), lambda i, info: (0, info[0] if wide else 0)),
             ],
-            out_specs=[
-                full(mid, block_width),
-                full(mid, block_width),
-                full(NC + TAIL, block_width),
-            ],
+            out_specs=[full(rows, block_width), full(NC + TAIL, block_width)],
         ),
         compiler_params=pltpu.CompilerParams(vmem_limit_bytes=16 * 2**20),
         name="refine_half",
-    )(info, own, sibling, *incoming, owners, coarse)
-
-
-def exchange(held, sibling, later):
-    rows = held.shape[1] - TAIL
-    mid = rows // 2
-    top, low, tail = slice(0, mid), slice(mid, rows), slice(rows, rows + TAIL)
-    both = lambda slot, part: held[slot, part] + sibling[slot, part]
-    counts = both(0, tail)
-    corner_top = swap(jnp.concatenate([both(3, top), counts], 0), ACROSS_X)
-    corner_low = swap(both(3, low), ACROSS_Y)
-    counts = counts + corner_top[mid:]
-    to_y = jnp.concatenate([both(2, top) + corner_top[:mid], both(2, low), counts], 0)
-    to_x = jnp.concatenate([both(1, top), both(1, low) + corner_low], 0)
-    to_y, to_x, later = lax.optimization_barrier((to_y, to_x, later))
-    return (swap(to_x, ACROSS_X), swap(to_y, ACROSS_Y), counts), later
-
-
-def gather_half(top, low, later):
-    x_low = swap(low, ACROSS_X)
-    y_top = swap(top, ACROSS_Y)
-    x_top = swap(top, ACROSS_X)
-    y_low = swap(low, ACROSS_Y)
-    x_low, y_top, later = lax.optimization_barrier((x_low, y_top, later))
-    corner_top = swap(y_top, ACROSS_X)
-    corner_low = swap(x_low, ACROSS_Y)
-    blocks = [(top, low), (x_top, x_low), (y_top, y_low), (corner_top, corner_low)]
-    return [jnp.concatenate(block, 0) for block in blocks], later
-
-
-def gather_last(top, low):
-    mid = top.shape[0]
-    block = jnp.concatenate([top, low], 0)
-    over_x, over_y = swap(block, ACROSS_X), swap(block, ACROSS_Y)
-    corner_top = swap(over_y[:mid], ACROSS_X)
-    corner_low = swap(over_x[mid:], ACROSS_Y)
-    return jnp.stack([block, over_x, over_y]), jnp.concatenate([corner_top, corner_low], 0)
-
-
-def spread(value):
-    corner = swap(value, ACROSS_X | ACROSS_Y)
-    return [value, swap(value, ACROSS_X), swap(value, ACROSS_Y), corner]
+    )(info, own, sibling, first, second, owners, coarse)
+
+
+def exchange(held, sibling):
+    first = swap_first(held[1::2] + sibling[1::2])
+    second = swap_second(held[2] + sibling[2] + first[1])
+    return first, second
 
 
 def over_cen(value, combine, bits=None):
@@ -430,30 +403,32 @@
 
 def place_body(info, own, other, last, last_other, fine_out, coarse_out):
     _, rows, block_width = own.shape
-    here = info[0]
-
-    def column_of(slot):
-        return pl.ds(pl.multiple_of((here ^ slot) * block_width, block_width), block_width)
-
-    def put(pieces, corner):
-        for slot in range(SLOTS - 1):
-            fine_out[:, column_of(slot)] = pieces[slot]
-        fine_out[:, column_of(SLOTS - 1)] = corner[:rows, :]
+
+    def column_of(slot, core):
+        start = block_of(info, slot, core) * block_width
+        return pl.ds(pl.multiple_of(start, block_width), block_width)
+
+    def put(near, far, core):
+        for slot in range(SLOTS):
+            block = far[slot // 2, :rows, :] if slot % 2 else near[slot // 2]
+            fine_out[:, column_of(slot, core)] = block
 
     @pl.when(pl.program_id(0) == 0)
     def _():
-        put(own, last)
-        part = lambda slot, start, size: (
-            last[pl.ds(rows + slot * (NC + TAIL) + start, size), :]
-            + last_other[pl.ds(rows + slot * (NC + TAIL) + start, size), :]
-        )
-        weight = as_column(part(0, NC, TAIL)[:1, :128], 128)[:NC, :1]
-        for slot in range(SLOTS):
-            coarse_out[:, column_of(slot)] = part(slot, 0, NC) / weight
+        put(own, last, info[1])
+        def part(source, slot, start, size):
+            top = rows + (0 if slot % 2 else NC + TAIL) + start
+            return source[slot // 2, top : top + size, :]
+
+        weight = part(last, 0, NC, TAIL) + part(last_other, 0, NC, TAIL)
+        weight = as_column(weight[:1, :128], 128)[:NC, :1]
+        for slot, crossed in enumerate((0, 2, 1, 3)):
+            total = part(last, slot, 0, NC) + part(last_other, crossed, 0, NC)
+            coarse_out[:, column_of(slot, info[1])] = total / weight
 
     @pl.when(pl.program_id(0) == 1)
     def _():
-        put(other, last_other)
+        put(other, last_other, 1 - info[1])
 
 
 def place(info, own, other, last, last_other, *, flip):
@@ -494,33 +469,38 @@
     sent, seen, squares, kept = call(points, fine_assign, fine_start, None, None, flip=1)
     sibling = swap(sent, CORE)
     held, seen_first = call(kept, fine_assign, fine_start, squares, seen, flip=0)
-    incoming, _ = exchange(held, sibling, ())
-    top, low, part = refine_half(info, held, sibling, incoming, owners, coarse_start, flip=0)
+    first, second = exchange(held, sibling)
+    fine, part = refine_half(
+        info, held, sibling, first, second, owners, coarse_start, flip=0
+    )
     part = part + swap(part, CORE)
-    seen_first = seen_first.reshape(-1, block_width)
-    own, folded = gather_half(top, low, jnp.concatenate([part, seen_first], 0))
+    near = jnp.stack([fine, swap_second(fine)])
+    far = swap_first(near)
     bits = range(lax.axis_size("cen").bit_length() - 1)
+    folded = jnp.concatenate([part, seen_first.reshape(-1, block_width)], 0)
     folded = over_cen(folded, fold, bits[:1])
-    own, folded = lax.optimization_barrier((jnp.stack(own), folded))
+    own = jnp.stack([near[0], far[0], near[1], far[1]])
+    own, folded = lax.optimization_barrier((own, folded))
     other = swap(own, CORE)
 
     call = functools.partial(run_pass, info, pass_index=1, rows=rows)
     sent, seen, kept = call(points, fine_assign, own, squares, None, flip=0)
     sibling = swap(sent, CORE)
     held, seen_second = call(kept, fine_assign, other, squares, seen, flip=1)
+    first, second = exchange(held, sibling)
 
     folded = over_cen(folded, fold, bits[1:])
     part, seen_first = folded[: NC + TAIL], folded[NC + TAIL :]
     coarse = part[:NC] / part[NC, :NC][:, None]
-
-    incoming, seen_second = exchange(held, sibling, seen_second)
     seen_second = over_cen(seen_second, jnp.minimum)
-    seen_second, coarse = lax.optimization_barrier((seen_second, coarse))
-    top, low, part = refine_half(info, held, sibling, incoming, owners, coarse, flip=1)
-    own, corner = gather_last(top, low)
-    parts = spread(over_cen(part, jnp.add))
-    last = jnp.concatenate([corner, *parts], 0)
-    fine_now, coarse_now = place(info, own, swap(own, CORE), last, swap(last, CORE), flip=1)
+
+    fine, part = refine_half(info, held, sibling, first, second, owners, coarse, flip=1)
+    near = jnp.stack([fine, swap_second(fine)])
+    far = swap_first(near)
+    part = over_cen(part, jnp.add)
+    parts = jnp.stack([part, swap_second(part)])
+    last = jnp.concatenate([far, swap_first(parts), parts], 1)
+    fine_now, coarse_now = place(info, near, swap(near, CORE), last, swap(last, CORE), flip=1)
 
     gaps = [(seen[0] - seen[1]) for seen in (seen_first.reshape(2, -1), seen_second)]
     return (fine_now, coarse_now, jnp.stack(gaps) / math.sqrt(width))

time: 128 us -> 120 us (0.938)
  Pallas kernels: 48.2 us -> 43.3 us
  waiting for transfers between devices: 45.4 us -> 40.7 us
  starting transfers between devices: 30.9 us -> 33.3 us
    ppermute x33 -> x12, waiting for transfers between devices: 45.4 us -> 12 us  [swap(): return lax.ppermute(value, axis, [(i, i ^ bit) for i in range(size)])]
    ppermute x0 -> x10, waiting for transfers between devices: none -> 28.7 us  [the longest x5 17.9 us: swap_first(): return lax.ppermute(value, 'pts', pairs)]
    ppermute x0 -> x10, starting transfers between devices: none -> 19.3 us  [the longest x5 11.5 us: swap_first(): return lax.ppermute(value, 'pts', pairs)]
    ppermute x33 -> x12, starting transfers between devices: 30.9 us -> 14 us  [swap(): return lax.ppermute(value, axis, [(i, i ^ bit) for i in range(size)])]
    pallas_call x4, Pallas kernels: 43 us -> 38.2 us  [run_pass(): pl.pallas_call(body, out_shape=out_shape, grid_spec=pltpu.PrefetchScalarG...]
  transfers between devices with their start and end apart: 33 -> 22, of which waited for: 18 -> 11; matrix products, arithmetic and copies ran while one was open for 1% -> 1% of each run, Pallas kernels for 24% -> 22%
where the time goes in v9:
time: 120 us
  Pallas kernels  43.3 us (36%)
  waiting for transfers between devices  40.7 us (34%)
  starting transfers between devices  33.3 us (28%)
  other arithmetic  1.43 us (1%)
    pallas_call x4, Pallas kernels, run_pass(): pl.pallas_call(body, out_shape=out_shape, grid_spec=pltpu.PrefetchScalarG...  38.2 us
    ppermute x5, waiting for transfers between devices, swap_first(): return lax.ppermute(value, 'pts', pairs)  17.9 us
    ppermute x12, starting transfers between devices, swap(): return lax.ppermute(value, axis, [(i, i ^ bit) for i in range(size)])  14 us
    ppermute x12, waiting for transfers between devices, swap(): return lax.ppermute(value, axis, [(i, i ^ bit) for i in range(size)])  12 us
    ppermute x5, starting transfers between devices, swap_first(): return lax.ppermute(value, 'pts', pairs)  11.5 us
    ppermute x5, waiting for transfers between devices, swap_second(): return lax.ppermute(value, 'pts', pairs)  10.7 us
    ppermute x5, starting transfers between devices, swap_second(): return lax.ppermute(value, 'pts', pairs)  7.84 us
    pallas_call x2, Pallas kernels, refine_half(): pl.pallas_call(refine_body, out_shape=[jax.ShapeDtypeStruct((rows, block_...  3.01 us
  transfers between devices with their start and end apart: 22, of which 11 were waited for; matrix products, arithmetic and copies ran while one was open for 1% of the time, Pallas kernels for 22%

profile of v9, /device:TPU:0, one launch (start us, length us, event | category | flops | bytes accessed | tf_op | source)
XLA Modules:
  0.0 119.8 jit_solution(2271842186016672464)
XLA Ops:
  0.6 0.1 pad_add_fusion.info
  0.7 11.6 %energies_and_sums_00.1 = (f32[4,264,256]{2,1,0:T(8,128)S(1)}, f32[2,4096]{1,0:T(2,128)S(1)}, f32[1,4096]{1,0:T(1,128)S(1)}, bf16[4096,1024]{1,0:T(8,128)(2,1)S(1)}) custom-call(s32[4]{0:T(128)S(1)} %pad_add_fusion.info, bf16[4096,1024]{1,0:T(8,128)(2,1)} %points.3, s32[2,4096]{1,0:T(2,128)} %assign.7, f32[512,1024]{1,0:T(8,128)} %fine.3), custom_call_target="tpu_custom_call" | custom-call | flops 4294967296 | bytes 8388608 | tf_op jit(solution)/shard_map/energies_and_sums_00/pallas_call | solution.py:307
  12.3 0.8 collective-permute-start
  13.1 0.0 copy-done.2
  13.1 8.3 %energies_and_sums_01.1 = (f32[4,264,256]{2,1,0:T(8,128)S(1)}, f32[2,4096]{1,0:T(2,128)S(1)}) custom-call(s32[4]{0:T(128)S(1)} %pad_add_fusion.info, bf16[4096,1024]{1,0:T(8,128)(2,1)S(1)} %get-tuple-element.22.points, s32[2,4096]{1,0:T(2,128)S(1)} %copy-done.3, f32[512,1024]{1,0:T(8,128)S(1)} %copy-done.2, f32[1,4096]{1,0:T(1,128)S(1)} %get-tuple-element.23.refs_0_, ...), custom_call_target="tpu_custom_call" | custom-call | flops 4294967296 | bytes 8388608 | tf_op jit(solution)/shard_map/energies_and_sums_01/pallas_call | solution.py:307
  21.4 0.0 collective-permute-done.sibling
  21.4 0.0 copy-start
  21.4 0.0 copy-start.1
  21.4 0.1 slice_add_fusion.1
  21.5 2.4 %collective-permute-start.1 = (f32[2,264,256]{2,1,0:T(8,128)S(1)}, f32[2,264,256]{2,1,0:T(8,128)S(1)}, u32[]{:S(2)}, u32[]{:S(2)}) collective-permute-start(f32[2,264,256]{2,1,0:T(8,128)S(1)} %slice_add_fusion.1), channel_id=1, source_target_pairs={{0,8},{4,20},{8,0},{12,28},{16,24},{20,4},{24,16},{28,12},{1,9},{5... | collective-permute-start | bytes 1622024 | tf_op jit(solution)/shard_map/ppermute | solution.py:94
  23.9 7.3 %collective-permute-done.1.first = f32[2,264,256]{2,1,0:T(8,128)S(1)} collective-permute-done((f32[2,264,256]{2,1,0:T(8,128)S(1)}, f32[2,264,256]{2,1,0:T(8,128)S(1)}, u32[]{:S(2)}, u32[]{:S(2)}) %collective-permute-start.1) | collective-permute-done | bytes 540704 | tf_op jit(solution)/shard_map/ppermute | solution.py:94
  31.2 0.1 fusion.1
  31.3 2.1 %collective-permute-start.2 = (f32[264,256]{1,0:T(8,128)S(1)}, f32[264,256]{1,0:T(8,128)S(1)}, u32[]{:S(2)}, u32[]{:S(2)}) collective-permute-start(f32[264,256]{1,0:T(8,128)S(1)} %fusion.1), channel_id=1, source_target_pairs={{0,16},{4,12},{8,24},{12,4},{16,0},{20,28},{24,8},{28,20},{1,17},{... | collective-permute-start | bytes 811016 | tf_op jit(solution)/shard_map/ppermute | solution.py:99
  33.4 4.4 %collective-permute-done.2.second = f32[264,256]{1,0:T(8,128)S(1)} collective-permute-done((f32[264,256]{1,0:T(8,128)S(1)}, f32[264,256]{1,0:T(8,128)S(1)}, u32[]{:S(2)}, u32[]{:S(2)}) %collective-permute-start.2) | collective-permute-done | bytes 270368 | tf_op jit(solution)/shard_map/ppermute | solution.py:99
  37.9 1.5 %refine_half.2 = (f32[256,256]{1,0:T(8,128)S(1)}, f32[72,256]{1,0:T(8,128)S(1)}) custom-call(s32[4]{0:T(128)S(1)} %pad_add_fusion.info, f32[4,264,256]{2,1,0:T(8,128)S(1)} %get-tuple-element.25.own, f32[4,264,256]{2,1,0:T(8,128)S(1)} %collective-permute-done.sibling, f32[2,264,256]{2,1,0:T(8,128)S(1)} %collective-permute-done.1.first, ...), custom_call_target="tpu_custom_call" | custom-call | tf_op jit(solution)/shard_map/refine_half/pallas_call | solution.py:361
  39.3 2.0 %collective-permute-start.3 = (f32[256,256]{1,0:T(8,128)S(1)}, f32[256,256]{1,0:T(8,128)S(1)}, u32[]{:S(2)}, u32[]{:S(2)}) collective-permute-start(f32[256,256]{1,0:T(8,128)S(1)} %get-tuple-element.27), channel_id=1, source_target_pairs={{0,16},{4,12},{8,24},{12,4},{16,0},{20,28},{24,8},{28,20},{1,17},{... | collective-permute-start | bytes 786440 | tf_op jit(solution)/shard_map/ppermute | solution.py:99
  41.4 0.0 collective-permute-start.5
  41.4 1.2 %collective-permute-done.5 = f32[72,256]{1,0:T(8,128)S(1)} collective-permute-done((f32[72,256]{1,0:T(8,128)S(1)}, f32[72,256]{1,0:T(8,128)S(1)}, u32[]{:S(2)}, u32[]{:S(2)}) %collective-permute-start.5) | collective-permute-done | bytes 73760 | tf_op jit(solution)/shard_map/ppermute | solution.py:89
  42.7 1.6 %collective-permute-start.6 = (f32[104,256]{1,0:T(8,128)S(1)}, f32[104,256]{1,0:T(8,128)S(1)}, u32[]{:S(2)}, u32[]{:S(2)}) collective-permute-start(f32[104,256]{1,0:T(8,128)S(1)} %pad_maximum_fusion.4), channel_id=1, source_target_pairs={{0,1},{1,0},{2,3},{3,2},{4,5},{5,4},{6,7},{7,6},{8,9},{9,8},{10,11... | collective-permute-start | bytes 319496 | tf_op jit(solution)/shard_map/ppermute | solution.py:89
  44.3 1.4 %collective-permute-done.3 = f32[256,256]{1,0:T(8,128)S(1)} collective-permute-done((f32[256,256]{1,0:T(8,128)S(1)}, f32[256,256]{1,0:T(8,128)S(1)}, u32[]{:S(2)}, u32[]{:S(2)}) %collective-permute-start.3) | collective-permute-done | bytes 262176 | tf_op jit(solution)/shard_map/ppermute | solution.py:99
  45.8 2.0 %collective-permute-start.4 = (f32[2,256,256]{2,1,0:T(8,128)S(1)}, f32[2,256,256]{2,1,0:T(8,128)S(1)}, u32[]{:S(2)}, u32[]{:S(2)}) collective-permute-start(f32[2,256,256]{2,1,0:T(8,128)S(1)} %pad_maximum_fusion.1), channel_id=1, source_target_pairs={{0,8},{4,20},{8,0},{12,28},{16,24},{20,4},{24,16},{28,12},{1,9},{5... | collective-permute-start | bytes 1572872 | tf_op jit(solution)/shard_map/ppermute | solution.py:94
  47.8 0.0 collective-permute-done.6
  47.9 7.2 %collective-permute-done.4 = f32[2,256,256]{2,1,0:T(8,128)S(1)} collective-permute-done((f32[2,256,256]{2,1,0:T(8,128)S(1)}, f32[2,256,256]{2,1,0:T(8,128)S(1)}, u32[]{:S(2)}, u32[]{:S(2)}) %collective-permute-start.4) | collective-permute-done | bytes 524320 | tf_op jit(solution)/shard_map/ppermute | solution.py:94
  55.1 0.1 pad_maximum_fusion.fine
  55.1 0.0 copy-start.4
  55.1 0.1 collective-permute-start.7
  55.2 10.0 %energies_and_sums_10.1 = (f32[4,264,256]{2,1,0:T(8,128)S(1)}, f32[2,4096]{1,0:T(2,128)S(1)}, bf16[4096,1024]{1,0:T(8,128)(2,1)S(1)}) custom-call(s32[4]{0:T(128)S(1)} %pad_add_fusion.info, bf16[4096,1024]{1,0:T(8,128)(2,1)} %points.3, s32[2,4096]{1,0:T(2,128)} %assign.7, f32[4,256,256]{2,1,0:T(8,128)S(1)} %pad_maximum_fusion.fine, ...), custom_call_target="tpu_custom_call" | custom-call | flops 4294967296 | bytes 8388608 | tf_op jit(solution)/shard_map/energies_and_sums_10/pallas_call | solution.py:307
  65.2 0.5 collective-permute-start.8
  65.7 0.0 collective-permute-done.7.fine
  65.7 8.3 %energies_and_sums_11.1 = (f32[4,264,256]{2,1,0:T(8,128)S(1)}, f32[2,4096]{1,0:T(2,128)S(1)}) custom-call(s32[4]{0:T(128)S(1)} %pad_add_fusion.info, bf16[4096,1024]{1,0:T(8,128)(2,1)S(1)} %get-tuple-element.31.points, s32[2,4096]{1,0:T(2,128)S(1)} %copy-done.4, f32[4,256,256]{2,1,0:T(8,128)S(1)} %collective-permute-done.7.fine, ...), custom_call_target="tpu_custom_call" | custom-call | flops 4294967296 | bytes 8388608 | tf_op jit(solution)/shard_map/energies_and_sums_11/pallas_call | solution.py:307
  74.1 0.0 collective-permute-done.8.sibling
  74.1 0.1 slice_add_fusion
  74.2 2.0 %collective-permute-start.9 = (f32[2,264,256]{2,1,0:T(8,128)S(1)}, f32[2,264,256]{2,1,0:T(8,128)S(1)}, u32[]{:S(2)}, u32[]{:S(2)}) collective-permute-start(f32[2,264,256]{2,1,0:T(8,128)S(1)} %slice_add_fusion), channel_id=1, source_target_pairs={{0,8},{4,20},{8,0},{12,28},{16,24},{20,4},{24,16},{28,12},{1,9},{5... | collective-permute-start | bytes 1622024 | tf_op jit(solution)/shard_map/ppermute | solution.py:94
  76.2 2.6 %collective-permute-start.11 = (f32[104,256]{1,0:T(8,128)S(1)}, f32[104,256]{1,0:T(8,128)S(1)}, u32[]{:S(2)}, u32[]{:S(2)}) collective-permute-start(f32[104,256]{1,0:T(8,128)S(1)} %pad_maximum_fusion.5), channel_id=1, source_target_pairs={{0,2},{1,3},{2,0},{3,1},{4,6},{5,7},{6,4},{7,5},{8,10},{9,11},{10,... | collective-permute-start | bytes 319496 | tf_op jit(solution)/shard_map/ppermute | solution.py:89
  78.8 5.3 %collective-permute-done.11 = f32[104,256]{1,0:T(8,128)S(1)} collective-permute-done((f32[104,256]{1,0:T(8,128)S(1)}, f32[104,256]{1,0:T(8,128)S(1)}, u32[]{:S(2)}, u32[]{:S(2)}) %collective-permute-start.11) | collective-permute-done | bytes 106528 | tf_op jit(solution)/shard_map/ppermute | solution.py:89
  84.1 0.0 collective-permute-done.9.first
  84.1 0.1 fusion
  84.2 1.6 %collective-permute-start.10 = (f32[264,256]{1,0:T(8,128)S(1)}, f32[264,256]{1,0:T(8,128)S(1)}, u32[]{:S(2)}, u32[]{:S(2)}) collective-permute-start(f32[264,256]{1,0:T(8,128)S(1)} %fusion), channel_id=1, source_target_pairs={{0,16},{4,12},{8,24},{12,4},{16,0},{20,28},{24,8},{28,20},{1,17},{... | collective-permute-start | bytes 811016 | tf_op jit(solution)/shard_map/ppermute | solution.py:99
  85.7 0.1 slice_divide_fusion.coarse
  85.8 4.9 %collective-permute-done.10.second = f32[264,256]{1,0:T(8,128)S(1)} collective-permute-done((f32[264,256]{1,0:T(8,128)S(1)}, f32[264,256]{1,0:T(8,128)S(1)}, u32[]{:S(2)}, u32[]{:S(2)}) %collective-permute-start.10) | collective-permute-done | bytes 270368 | tf_op jit(solution)/shard_map/ppermute | solution.py:99
  90.7 1.5 %refine_half.3 = (f32[256,256]{1,0:T(8,128)S(1)}, f32[72,256]{1,0:T(8,128)S(1)}) custom-call(s32[4]{0:T(128)S(1)} %pad_add_fusion.info, f32[4,264,256]{2,1,0:T(8,128)S(1)} %get-tuple-element.33.own, f32[4,264,256]{2,1,0:T(8,128)S(1)} %collective-permute-done.8.sibling, f32[2,264,256]{2,1,0:T(8,128)S(1)} %collective-permute-done.9.first, ...), custom_call_target="tpu_custom_call" | custom-call | tf_op jit(solution)/shard_map/refine_half/pallas_call | solution.py:361
  92.2 1.5 %collective-permute-start.12 = (f32[256,256]{1,0:T(8,128)S(1)}, f32[256,256]{1,0:T(8,128)S(1)}, u32[]{:S(2)}, u32[]{:S(2)}) collective-permute-start(f32[256,256]{1,0:T(8,128)S(1)} %get-tuple-element.36), channel_id=1, source_target_pairs={{0,16},{4,12},{8,24},{12,4},{16,0},{20,28},{24,8},{28,20},{1,17},{... | collective-permute-start | bytes 786440 | tf_op jit(solution)/shard_map/ppermute | solution.py:99
  93.7 1.6 %collective-permute-start.15 = (f32[72,256]{1,0:T(8,128)S(1)}, f32[72,256]{1,0:T(8,128)S(1)}, u32[]{:S(2)}, u32[]{:S(2)}) collective-permute-start(f32[72,256]{1,0:T(8,128)S(1)} %get-tuple-element.37), channel_id=1, source_target_pairs={{0,1},{1,0},{2,3},{3,2},{4,5},{5,4},{6,7},{7,6},{8,9},{9,8},{10,11... | collective-permute-start | bytes 221192 | tf_op jit(solution)/shard_map/ppermute | solution.py:89
  95.3 2.8 %collective-permute-done.15 = f32[72,256]{1,0:T(8,128)S(1)} collective-permute-done((f32[72,256]{1,0:T(8,128)S(1)}, f32[72,256]{1,0:T(8,128)S(1)}, u32[]{:S(2)}, u32[]{:S(2)}) %collective-permute-start.15) | collective-permute-done | bytes 73760 | tf_op jit(solution)/shard_map/ppermute | solution.py:89
  98.1 2.6 %collective-permute-start.16 = (f32[72,256]{1,0:T(8,128)S(1)}, f32[72,256]{1,0:T(8,128)S(1)}, u32[]{:S(2)}, u32[]{:S(2)}) collective-permute-start(f32[72,256]{1,0:T(8,128)S(1)} %add.56), channel_id=1, source_target_pairs={{0,2},{1,3},{2,0},{3,1},{4,6},{5,7},{6,4},{7,5},{8,10},{9,11},{10,... | collective-permute-start | bytes 221192 | tf_op jit(solution)/shard_map/ppermute | solution.py:89
  100.7 1.6 %collective-permute-start.20 = (f32[2,4096]{1,0:T(2,128)S(1)}, f32[2,4096]{1,0:T(2,128)S(1)}, u32[]{:S(2)}, u32[]{:S(2)}) collective-permute-start(f32[2,4096]{1,0:T(2,128)S(1)} %get-tuple-element.40), channel_id=1, source_target_pairs={{0,1},{1,0},{2,3},{3,2},{4,5},{5,4},{6,7},{7,6},{8,9},{9,8},{10,11... | collective-permute-start | bytes 98312 | tf_op jit(solution)/shard_map/ppermute | solution.py:89
  102.3 1.1 collective-permute-done.16
  103.4 0.6 collective-permute-start.17
  104.0 0.0 collective-permute-done.12
  104.0 2.4 %collective-permute-start.14 = (f32[2,256,256]{2,1,0:T(8,128)S(1)}, f32[2,256,256]{2,1,0:T(8,128)S(1)}, u32[]{:S(2)}, u32[]{:S(2)}) collective-permute-start(f32[2,256,256]{2,1,0:T(8,128)S(1)} %pad_maximum_fusion.2.own), channel_id=1, source_target_pairs={{0,8},{4,20},{8,0},{12,28},{16,24},{20,4},{24,16},{28,12},{1,9},{5... | collective-permute-start | bytes 1572872 | tf_op jit(solution)/shard_map/ppermute | solution.py:94
  106.4 0.0 collective-permute-done.20
  106.5 2.4 %collective-permute-start.21 = (f32[2,4096]{1,0:T(2,128)S(1)}, f32[2,4096]{1,0:T(2,128)S(1)}, u32[]{:S(2)}, u32[]{:S(2)}) collective-permute-start(f32[2,4096]{1,0:T(2,128)S(1)} %min.14), channel_id=1, source_target_pairs={{0,2},{1,3},{2,0},{3,1},{4,6},{5,7},{6,4},{7,5},{8,10},{9,11},{10,... | collective-permute-start | bytes 98312 | tf_op jit(solution)/shard_map/ppermute | solution.py:89
  108.9 0.0 collective-permute-done.17
  108.9 2.7 %collective-permute-start.18 = (f32[2,72,256]{2,1,0:T(8,128)S(1)}, f32[2,72,256]{2,1,0:T(8,128)S(1)}, u32[]{:S(2)}, u32[]{:S(2)}) collective-permute-start(f32[2,72,256]{2,1,0:T(8,128)S(1)} %pad_maximum_fusion.3), channel_id=1, source_target_pairs={{0,8},{4,20},{8,0},{12,28},{16,24},{20,4},{24,16},{28,12},{1,9},{5... | collective-permute-start | bytes 442376 | tf_op jit(solution)/shard_map/ppermute | solution.py:94
  111.6 0.0 collective-permute-done.21
  111.6 0.1 collective-permute-start.13
  111.7 3.4 %collective-permute-done.18 = f32[2,72,256]{2,1,0:T(8,128)S(1)} collective-permute-done((f32[2,72,256]{2,1,0:T(8,128)S(1)}, f32[2,72,256]{2,1,0:T(8,128)S(1)}, u32[]{:S(2)}, u32[]{:S(2)}) %collective-permute-start.18) | collective-permute-done | bytes 147488 | tf_op jit(solution)/shard_map/ppermute | solution.py:94
  115.2 0.0 collective-permute-done.14
  115.2 0.1 maximum_maximum_fusion.last
  115.2 0.1 collective-permute-start.19
  115.3 0.7 maximum_multiply_fusion
  116.0 0.0 collective-permute-done.13.other
  116.0 1.6 %collective-permute-done.19.last_other = f32[2,400,256]{2,1,0:T(8,128)S(1)} collective-permute-done((f32[2,400,256]{2,1,0:T(8,128)S(1)}, f32[2,400,256]{2,1,0:T(8,128)S(1)}, u32[]{:S(2)}, u32[]{:S(2)}) %collective-permute-start.19) | collective-permute-done | bytes 819232 | tf_op jit(solution)/shard_map/ppermute | solution.py:89
  117.6 2.2 %place_blocks.1 = (f32[512,1024]{1,0:T(8,128)}, f32[64,1024]{1,0:T(8,128)}) custom-call(s32[4]{0:T(128)S(1)} %pad_add_fusion.info, f32[2,256,256]{2,1,0:T(8,128)S(1)} %pad_maximum_fusion.2.own, f32[2,256,256]{2,1,0:T(8,128)S(1)} %collective-permute-done.13.other, f32[2,400,256]{2,1,0:T(8,128)S(1)} %maximum_maximum_fusion.last, ...), custom_call_target="tpu_custom_call" | custom-call | tf_op jit(solution)/shard_map/place_blocks/pallas_call | solution.py:438
  (26 shorter events, 0.3 us)
Async XLA Ops:
  0.7 12.4 %copy-start.2 = (f32[512,1024]{1,0:T(8,128)S(1)}, f32[512,1024]{1,0:T(8,128)}, u32[]{:S(2)}) copy-start(f32[512,1024]{1,0:T(8,128)} %fine.3) | copy-start | bytes 6291460
  0.7 12.4 %copy-start.3 = (s32[2,4096]{1,0:T(2,128)S(1)}, s32[2,4096]{1,0:T(2,128)}, u32[]{:S(2)}) copy-start(s32[2,4096]{1,0:T(2,128)} %assign.7) | copy-start | bytes 98308
  12.3 9.1 %collective-permute-start = (f32[4,264,256]{2,1,0:T(8,128)S(1)}, f32[4,264,256]{2,1,0:T(8,128)S(1)}, u32[]{:S(2)}, u32[]{:S(2)}) collective-permute-start(f32[4,264,256]{2,1,0:T(8,128)S(1)} %get-tuple-element.26), channel_id=1, source_target_pairs={{0,4},{4,0},{8,12},{12,8},{16,20},{20,16},{24,28},{28,24},{1,5},{5... | collective-permute-start | bytes 3244040 | tf_op jit(solution)/shard_map/ppermute | solution.py:89
  21.4 16.4 %copy-start = (f32[64,1024]{1,0:T(8,128)S(1)}, f32[64,1024]{1,0:T(8,128)}, u32[]{:S(2)}) copy-start(f32[64,1024]{1,0:T(8,128)} %coarse.1) | copy-start | bytes 786436
  21.4 16.4 %copy-start.1 = (s32[512]{0:T(512)S(1)}, s32[512]{0:T(512)}, u32[]{:S(2)}) copy-start(s32[512]{0:T(512)} %param.9) | copy-start | bytes 6148
  21.5 9.7 %collective-permute-start.1 = (f32[2,264,256]{2,1,0:T(8,128)S(1)}, f32[2,264,256]{2,1,0:T(8,128)S(1)}, u32[]{:S(2)}, u32[]{:S(2)}) collective-permute-start(f32[2,264,256]{2,1,0:T(8,128)S(1)} %slice_add_fusion.1), channel_id=1, source_target_pairs={{0,8},{4,20},{8,0},{12,28},{16,24},{20,4},{24,16},{28,12},{1,9},{5... | collective-permute-start | bytes 1622024 | tf_op jit(solution)/shard_map/ppermute | solution.py:94
  31.3 6.6 %collective-permute-start.2 = (f32[264,256]{1,0:T(8,128)S(1)}, f32[264,256]{1,0:T(8,128)S(1)}, u32[]{:S(2)}, u32[]{:S(2)}) collective-permute-start(f32[264,256]{1,0:T(8,128)S(1)} %fusion.1), channel_id=1, source_target_pairs={{0,16},{4,12},{8,24},{12,4},{16,0},{20,28},{24,8},{28,20},{1,17},{... | collective-permute-start | bytes 811016 | tf_op jit(solution)/shard_map/ppermute | solution.py:99
  39.3 6.4 %collective-permute-start.3 = (f32[256,256]{1,0:T(8,128)S(1)}, f32[256,256]{1,0:T(8,128)S(1)}, u32[]{:S(2)}, u32[]{:S(2)}) collective-permute-start(f32[256,256]{1,0:T(8,128)S(1)} %get-tuple-element.27), channel_id=1, source_target_pairs={{0,16},{4,12},{8,24},{12,4},{16,0},{20,28},{24,8},{28,20},{1,17},{... | collective-permute-start | bytes 786440 | tf_op jit(solution)/shard_map/ppermute | solution.py:99
  41.4 1.3 %collective-permute-start.5 = (f32[72,256]{1,0:T(8,128)S(1)}, f32[72,256]{1,0:T(8,128)S(1)}, u32[]{:S(2)}, u32[]{:S(2)}) collective-permute-start(f32[72,256]{1,0:T(8,128)S(1)} %get-tuple-element.28), channel_id=1, source_target_pairs={{0,4},{4,0},{8,12},{12,8},{16,20},{20,16},{24,28},{28,24},{1,5},{5... | collective-permute-start | bytes 221192 | tf_op jit(solution)/shard_map/ppermute | solution.py:89
  42.7 5.1 %collective-permute-start.6 = (f32[104,256]{1,0:T(8,128)S(1)}, f32[104,256]{1,0:T(8,128)S(1)}, u32[]{:S(2)}, u32[]{:S(2)}) collective-permute-start(f32[104,256]{1,0:T(8,128)S(1)} %pad_maximum_fusion.4), channel_id=1, source_target_pairs={{0,1},{1,0},{2,3},{3,2},{4,5},{5,4},{6,7},{7,6},{8,9},{9,8},{10,11... | collective-permute-start | bytes 319496 | tf_op jit(solution)/shard_map/ppermute | solution.py:89
  45.8 9.2 %collective-permute-start.4 = (f32[2,256,256]{2,1,0:T(8,128)S(1)}, f32[2,256,256]{2,1,0:T(8,128)S(1)}, u32[]{:S(2)}, u32[]{:S(2)}) collective-permute-start(f32[2,256,256]{2,1,0:T(8,128)S(1)} %pad_maximum_fusion.1), channel_id=1, source_target_pairs={{0,8},{4,20},{8,0},{12,28},{16,24},{20,4},{24,16},{28,12},{1,9},{5... | collective-permute-start | bytes 1572872 | tf_op jit(solution)/shard_map/ppermute | solution.py:94
  55.1 10.6 %copy-start.4 = (s32[2,4096]{1,0:T(2,128)S(1)}, s32[2,4096]{1,0:T(2,128)}, u32[]{:S(2)}) copy-start(s32[2,4096]{1,0:T(2,128)} %assign.7) | copy-start | bytes 98308
  55.1 10.6 %collective-permute-start.7 = (f32[4,256,256]{2,1,0:T(8,128)S(1)}, f32[4,256,256]{2,1,0:T(8,128)S(1)}, u32[]{:S(2)}, u32[]{:S(2)}) collective-permute-start(f32[4,256,256]{2,1,0:T(8,128)S(1)} %pad_maximum_fusion.fine), channel_id=1, source_target_pairs={{0,4},{4,0},{8,12},{12,8},{16,20},{20,16},{24,28},{28,24},{1,5},{5... | collective-permute-start | bytes 3145736 | tf_op jit(solution)/shard_map/ppermute | solution.py:89
  65.2 8.9 %collective-permute-start.8 = (f32[4,264,256]{2,1,0:T(8,128)S(1)}, f32[4,264,256]{2,1,0:T(8,128)S(1)}, u32[]{:S(2)}, u32[]{:S(2)}) collective-permute-start(f32[4,264,256]{2,1,0:T(8,128)S(1)} %get-tuple-element.34), channel_id=1, source_target_pairs={{0,4},{4,0},{8,12},{12,8},{16,20},{20,16},{24,28},{28,24},{1,5},{5... | collective-permute-start | bytes 3244040 | tf_op jit(solution)/shard_map/ppermute | solution.py:89
  74.2 9.9 %collective-permute-start.9 = (f32[2,264,256]{2,1,0:T(8,128)S(1)}, f32[2,264,256]{2,1,0:T(8,128)S(1)}, u32[]{:S(2)}, u32[]{:S(2)}) collective-permute-start(f32[2,264,256]{2,1,0:T(8,128)S(1)} %slice_add_fusion), channel_id=1, source_target_pairs={{0,8},{4,20},{8,0},{12,28},{16,24},{20,4},{24,16},{28,12},{1,9},{5... | collective-permute-start | bytes 1622024 | tf_op jit(solution)/shard_map/ppermute | solution.py:94
  76.2 7.9 %collective-permute-start.11 = (f32[104,256]{1,0:T(8,128)S(1)}, f32[104,256]{1,0:T(8,128)S(1)}, u32[]{:S(2)}, u32[]{:S(2)}) collective-permute-start(f32[104,256]{1,0:T(8,128)S(1)} %pad_maximum_fusion.5), channel_id=1, source_target_pairs={{0,2},{1,3},{2,0},{3,1},{4,6},{5,7},{6,4},{7,5},{8,10},{9,11},{10,... | collective-permute-start | bytes 319496 | tf_op jit(solution)/shard_map/ppermute | solution.py:89
  84.2 6.5 %collective-permute-start.10 = (f32[264,256]{1,0:T(8,128)S(1)}, f32[264,256]{1,0:T(8,128)S(1)}, u32[]{:S(2)}, u32[]{:S(2)}) collective-permute-start(f32[264,256]{1,0:T(8,128)S(1)} %fusion), channel_id=1, source_target_pairs={{0,16},{4,12},{8,24},{12,4},{16,0},{20,28},{24,8},{28,20},{1,17},{... | collective-permute-start | bytes 811016 | tf_op jit(solution)/shard_map/ppermute | solution.py:99
  92.2 11.8 %collective-permute-start.12 = (f32[256,256]{1,0:T(8,128)S(1)}, f32[256,256]{1,0:T(8,128)S(1)}, u32[]{:S(2)}, u32[]{:S(2)}) collective-permute-start(f32[256,256]{1,0:T(8,128)S(1)} %get-tuple-element.36), channel_id=1, source_target_pairs={{0,16},{4,12},{8,24},{12,4},{16,0},{20,28},{24,8},{28,20},{1,17},{... | collective-permute-start | bytes 786440 | tf_op jit(solution)/shard_map/ppermute | solution.py:99
  93.7 4.4 %collective-permute-start.15 = (f32[72,256]{1,0:T(8,128)S(1)}, f32[72,256]{1,0:T(8,128)S(1)}, u32[]{:S(2)}, u32[]{:S(2)}) collective-permute-start(f32[72,256]{1,0:T(8,128)S(1)} %get-tuple-element.37), channel_id=1, source_target_pairs={{0,1},{1,0},{2,3},{3,2},{4,5},{5,4},{6,7},{7,6},{8,9},{9,8},{10,11... | collective-permute-start | bytes 221192 | tf_op jit(solution)/shard_map/ppermute | solution.py:89
  98.1 5.3 %collective-permute-start.16 = (f32[72,256]{1,0:T(8,128)S(1)}, f32[72,256]{1,0:T(8,128)S(1)}, u32[]{:S(2)}, u32[]{:S(2)}) collective-permute-start(f32[72,256]{1,0:T(8,128)S(1)} %add.56), channel_id=1, source_target_pairs={{0,2},{1,3},{2,0},{3,1},{4,6},{5,7},{6,4},{7,5},{8,10},{9,11},{10,... | collective-permute-start | bytes 221192 | tf_op jit(solution)/shard_map/ppermute | solution.py:89
  100.7 5.7 %collective-permute-start.20 = (f32[2,4096]{1,0:T(2,128)S(1)}, f32[2,4096]{1,0:T(2,128)S(1)}, u32[]{:S(2)}, u32[]{:S(2)}) collective-permute-start(f32[2,4096]{1,0:T(2,128)S(1)} %get-tuple-element.40), channel_id=1, source_target_pairs={{0,1},{1,0},{2,3},{3,2},{4,5},{5,4},{6,7},{7,6},{8,9},{9,8},{10,11... | collective-permute-start | bytes 98312 | tf_op jit(solution)/shard_map/ppermute | solution.py:89
  103.4 5.4 %collective-permute-start.17 = (f32[72,256]{1,0:T(8,128)S(1)}, f32[72,256]{1,0:T(8,128)S(1)}, u32[]{:S(2)}, u32[]{:S(2)}) collective-permute-start(f32[72,256]{1,0:T(8,128)S(1)} %add.57), channel_id=1, source_target_pairs={{0,16},{4,12},{8,24},{12,4},{16,0},{20,28},{24,8},{28,20},{1,17},{... | collective-permute-start | bytes 221192 | tf_op jit(solution)/shard_map/ppermute | solution.py:99
  104.0 11.1 %collective-permute-start.14 = (f32[2,256,256]{2,1,0:T(8,128)S(1)}, f32[2,256,256]{2,1,0:T(8,128)S(1)}, u32[]{:S(2)}, u32[]{:S(2)}) collective-permute-start(f32[2,256,256]{2,1,0:T(8,128)S(1)} %pad_maximum_fusion.2.own), channel_id=1, source_target_pairs={{0,8},{4,20},{8,0},{12,28},{16,24},{20,4},{24,16},{28,12},{1,9},{5... | collective-permute-start | bytes 1572872 | tf_op jit(solution)/shard_map/ppermute | solution.py:94
  106.5 5.1 %collective-permute-start.21 = (f32[2,4096]{1,0:T(2,128)S(1)}, f32[2,4096]{1,0:T(2,128)S(1)}, u32[]{:S(2)}, u32[]{:S(2)}) collective-permute-start(f32[2,4096]{1,0:T(2,128)S(1)} %min.14), channel_id=1, source_target_pairs={{0,2},{1,3},{2,0},{3,1},{4,6},{5,7},{6,4},{7,5},{8,10},{9,11},{10,... | collective-permute-start | bytes 98312 | tf_op jit(solution)/shard_map/ppermute | solution.py:89
  108.9 6.3 %collective-permute-start.18 = (f32[2,72,256]{2,1,0:T(8,128)S(1)}, f32[2,72,256]{2,1,0:T(8,128)S(1)}, u32[]{:S(2)}, u32[]{:S(2)}) collective-permute-start(f32[2,72,256]{2,1,0:T(8,128)S(1)} %pad_maximum_fusion.3), channel_id=1, source_target_pairs={{0,8},{4,20},{8,0},{12,28},{16,24},{20,4},{24,16},{28,12},{1,9},{5... | collective-permute-start | bytes 442376 | tf_op jit(solution)/shard_map/ppermute | solution.py:94
  111.6 4.4 %collective-permute-start.13 = (f32[2,256,256]{2,1,0:T(8,128)S(1)}, f32[2,256,256]{2,1,0:T(8,128)S(1)}, u32[]{:S(2)}, u32[]{:S(2)}) collective-permute-start(f32[2,256,256]{2,1,0:T(8,128)S(1)} %pad_maximum_fusion.2.own), channel_id=1, source_target_pairs={{0,4},{4,0},{8,12},{12,8},{16,20},{20,16},{24,28},{28,24},{1,5},{5... | collective-permute-start | bytes 1572872 | tf_op jit(solution)/shard_map/ppermute | solution.py:89
  115.2 2.4 %collective-permute-start.19 = (f32[2,400,256]{2,1,0:T(8,128)S(1)}, f32[2,400,256]{2,1,0:T(8,128)S(1)}, u32[]{:S(2)}, u32[]{:S(2)}) collective-permute-start(f32[2,400,256]{2,1,0:T(8,128)S(1)} %maximum_maximum_fusion.last), channel_id=1, source_target_pairs={{0,4},{4,0},{8,12},{12,8},{16,20},{20,16},{24,28},{28,24},{1,5},{5... | collective-permute-start | bytes 2457608 | tf_op jit(solution)/shard_map/ppermute | solution.py:89

commit v10 on v9

--- a/solution.py
+++ b/solution.py
@@ -126,6 +126,7 @@
     small_sems, point_sems = refs[8:10] if stream else (None, None)
     start = refs[10] if first else fine
     rows, width = low.shape
+    mid = rows // 2
     block_width = width // SLOTS
     half = info[1] ^ flip
     base = info[2] + half * rows
@@ -166,7 +167,7 @@
         for slot in range(SLOTS):
             block = fine[slot]
             norm = norm + jnp.sum(block * block, axis=1, keepdims=True)
-            low[:, column_of(slot, info[1] ^ chained)] = (-2.0 * block).astype(jnp.bfloat16)
+            low[:, column_of(slot, 0)] = (-2.0 * block).astype(jnp.bfloat16)
     norms[...] = jnp.broadcast_to(norm, norms.shape)
     tallies[...] = jnp.zeros_like(tallies)
     sums[...] = jnp.zeros_like(sums)
@@ -238,8 +239,10 @@
 
     counts = jnp.broadcast_to(jnp.sum(tallies[...].T, axis=0, keepdims=True), (TAIL, rows))
     for slot in range(SLOTS):
-        payload[slot, :rows, :] = sums[:, column_of(slot, info[1] ^ (not chained))]
-        payload[slot, rows:, :] = counts
+        columns = column_of(slot, info[1] ^ (not chained))
+        payload[slot, :mid, :] = sums[:mid, columns]
+        payload[slot, mid : mid + TAIL, :] = counts
+        payload[slot, mid + TAIL :, :] = sums[mid:, columns]
 
 
 def run_pass(info, points, fine_assign, fine, squares, seen, *, pass_index, flip, rows):
@@ -322,10 +325,14 @@
     )(info, *args)
 
 
-def refine_body(info, own, sibling, first, second, owner, coarse, fine, part):
+def refine_body(info, own, sibling, *refs):
+    first_top, first_low, second_top, second_low, owner, coarse, top, low, part = refs
     rows = owner.shape[1]
-    total = (own[...] + sibling[...]) + (first[...] + second[...])
-    totals, counts_row = total[:rows], total[rows:]
+    mid = rows // 2
+    total = own[...] + sibling[...]
+    head = total[: mid + TAIL] + (first_top[...] + second_top[...])
+    rest = total[mid + TAIL :] + (first_low[...] + second_low[...])
+    totals, counts_row = jnp.concatenate([head[:mid], rest], 0), head[mid:]
     counts = as_column(counts_row[:1], rows)[:, :1]
     table = (
         lax.broadcasted_iota(jnp.int32, (NC, rows), 0) == owner[...]
@@ -338,7 +345,8 @@
         preferred_element_type=jnp.float32,
     )
     new = (totals + prior_weight * lookup) / (counts + prior_weight)
-    fine[...] = new
+    top[...] = new[:mid]
+    low[...] = new[mid:]
     prior = jnp.where(info[3] == 0, prior_weight, 0.0)
     part[:NC, :] = prior * coarse[...] + jnp.dot(
         table, counts * new, precision=HIGHEST, preferred_element_type=jnp.float32
@@ -353,39 +361,64 @@
     )
 
 
-def refine_half(info, own, sibling, first, second, owners, coarse, *, flip):
+def refine_half(info, own, sibling, incoming, owners, coarse, *, flip):
     _, rows, block_width = own.shape
     rows -= TAIL
-    slot = pl.BlockSpec((None, rows + TAIL, block_width), lambda i, info: (0, 0, 0))
+    mid = rows // 2
+    leading = lambda size: pl.BlockSpec((None, size, block_width), lambda i, info: (0, 0, 0))
     wide = coarse.shape[1] != block_width
     return pl.pallas_call(
         refine_body,
         out_shape=[
-            jax.ShapeDtypeStruct((rows, block_width), jnp.float32),
+            jax.ShapeDtypeStruct((mid, block_width), jnp.float32),
+            jax.ShapeDtypeStruct((mid, block_width), jnp.float32),
             jax.ShapeDtypeStruct((NC + TAIL, block_width), jnp.float32),
         ],
         grid_spec=pltpu.PrefetchScalarGridSpec(
             num_scalar_prefetch=1,
             grid=(1,),
             in_specs=[
-                slot,
-                slot,
-                slot,
-                full(*second.shape),
+                leading(rows + TAIL),
+                leading(rows + TAIL),
+                leading(mid + TAIL),
+                leading(mid),
+                full(mid + TAIL, block_width),
+                full(mid, block_width),
                 pl.BlockSpec((None, 1, rows), lambda i, info: (info[1] ^ flip, 0, 0)),
                 pl.BlockSpec((NC, block_width), lambda i, info: (0, info[0] if wide else 0)),
             ],
-            out_specs=[full(rows, block_width), full(NC + TAIL, block_width)],
+            out_specs=[
+                full(mid, block_width),
+                full(mid, block_width),
+                full(NC + TAIL, block_width),
+            ],
         ),
         compiler_params=pltpu.CompilerParams(vmem_limit_bytes=16 * 2**20),
         name="refine_half",
-    )(info, own, sibling, first, second, owners, coarse)
-
-
-def exchange(held, sibling):
-    first = swap_first(held[1::2] + sibling[1::2])
-    second = swap_second(held[2] + sibling[2] + first[1])
-    return first, second
+    )(info, own, sibling, *incoming, owners, coarse)
+
+
+def exchange(held, sibling, later=()):
+    cut = (held.shape[1] - TAIL) // 2 + TAIL
+    chunks = slice(0, cut), slice(cut, None)
+    first = [swap_first(held[1::2, rows] + sibling[1::2, rows]) for rows in chunks]
+    first[0], later = lax.optimization_barrier((first[0], later))
+    second = [
+        swap_second(held[2, rows] + sibling[2, rows] + arrived[1])
+        for rows, arrived in zip(chunks, first)
+    ]
+    return [*first, *second], later
+
+
+def gather_half(top, low):
+    x_low = swap(low, ACROSS_X)
+    y_top = swap(top, ACROSS_Y)
+    x_top = swap(top, ACROSS_X)
+    y_low = swap(low, ACROSS_Y)
+    corner_top = swap(y_top, ACROSS_X)
+    corner_low = swap(x_low, ACROSS_Y)
+    blocks = [(top, low), (x_top, x_low), (y_top, y_low), (corner_top, corner_low)]
+    return [jnp.concatenate(block, 0) for block in blocks]
 
 
 def over_cen(value, combine, bits=None):
@@ -416,8 +449,9 @@
     @pl.when(pl.program_id(0) == 0)
     def _():
         put(own, last, info[1])
+
         def part(source, slot, start, size):
-            top = rows + (0 if slot % 2 else NC + TAIL) + start
+            top = rows + (slot % 2) * (NC + TAIL) + start
             return source[slot // 2, top : top + size, :]
 
         weight = part(last, 0, NC, TAIL) + part(last_other, 0, NC, TAIL)
@@ -469,17 +503,15 @@
     sent, seen, squares, kept = call(points, fine_assign, fine_start, None, None, flip=1)
     sibling = swap(sent, CORE)
     held, seen_first = call(kept, fine_assign, fine_start, squares, seen, flip=0)
-    first, second = exchange(held, sibling)
-    fine, part = refine_half(
-        info, held, sibling, first, second, owners, coarse_start, flip=0
+    incoming, _ = exchange(held, sibling)
+    top, low, part = refine_half(
+        info, held, sibling, incoming, owners, coarse_start, flip=0
     )
     part = part + swap(part, CORE)
-    near = jnp.stack([fine, swap_second(fine)])
-    far = swap_first(near)
+    own = jnp.stack(gather_half(top, low))
     bits = range(lax.axis_size("cen").bit_length() - 1)
     folded = jnp.concatenate([part, seen_first.reshape(-1, block_width)], 0)
     folded = over_cen(folded, fold, bits[:1])
-    own = jnp.stack([near[0], far[0], near[1], far[1]])
     own, folded = lax.optimization_barrier((own, folded))
     other = swap(own, CORE)
 
@@ -487,23 +519,28 @@
     sent, seen, kept = call(points, fine_assign, own, squares, None, flip=0)
     sibling = swap(sent, CORE)
     held, seen_second = call(kept, fine_assign, other, squares, seen, flip=1)
-    first, second = exchange(held, sibling)
+    incoming, folded = exchange(held, sibling, folded)
 
     folded = over_cen(folded, fold, bits[1:])
     part, seen_first = folded[: NC + TAIL], folded[NC + TAIL :]
     coarse = part[:NC] / part[NC, :NC][:, None]
-    seen_second = over_cen(seen_second, jnp.minimum)
-
-    fine, part = refine_half(info, held, sibling, first, second, owners, coarse, flip=1)
-    near = jnp.stack([fine, swap_second(fine)])
+
+    top, low, part = refine_half(info, held, sibling, incoming, owners, coarse, flip=1)
+    fine = jnp.concatenate([top, low], 0)
+    folded = jnp.concatenate([part, seen_second.reshape(-1, block_width)], 0)
+    folded = over_cen(folded, fold, bits[:1])
+    over_second, folded = lax.optimization_barrier((swap_second(fine), folded))
+    near = jnp.stack([fine, over_second])
     far = swap_first(near)
-    part = over_cen(part, jnp.add)
+    folded = over_cen(folded, fold, bits[1:])
+    part, seen_second = folded[: NC + TAIL], folded[NC + TAIL :]
     parts = jnp.stack([part, swap_second(part)])
-    last = jnp.concatenate([far, swap_first(parts), parts], 1)
+    last = jnp.concatenate([far, parts, swap_first(parts)], 1)
     fine_now, coarse_now = place(info, near, swap(near, CORE), last, swap(last, CORE), flip=1)
 
-    gaps = [(seen[0] - seen[1]) for seen in (seen_first.reshape(2, -1), seen_second)]
-    return (fine_now, coarse_now, jnp.stack(gaps) / math.sqrt(width))
+    seen = [each.reshape(2, -1) for each in (seen_first, seen_second)]
+    gaps = jnp.stack([each[0] - each[1] for each in seen]) / math.sqrt(width)
+    return (fine_now, coarse_now, gaps)
 
 
 def solution(mesh):

time: 120 us -> 121 us (level)
    ppermute x5 -> x6, starting transfers between devices: 11.5 us -> 6.47 us  [swap_first(): return lax.ppermute(value, 'pts', pairs)]
    ppermute x5 -> x6, starting transfers between devices: 7.84 us -> 11 us  [swap_second(): return lax.ppermute(value, 'pts', pairs)]
    ppermute x12 -> x16, starting transfers between devices: 14 us -> 16.4 us  [swap(): return lax.ppermute(value, axis, [(i, i ^ bit) for i in range(size)])]
    ppermute x5 -> x6, waiting for transfers between devices: 17.9 us -> 15.8 us  [swap_first(): return lax.ppermute(value, 'pts', pairs)]
    ppermute x12 -> x16, waiting for transfers between devices: 12 us -> 13.2 us  [swap(): return lax.ppermute(value, axis, [(i, i ^ bit) for i in range(size)])]
    ppermute x5 -> x6, waiting for transfers between devices: 10.7 us -> 11.2 us  [swap_second(): return lax.ppermute(value, 'pts', pairs)]
  transfers between devices with their start and end apart: 22 -> 28, of which waited for: 11 -> 17; matrix products, arithmetic and copies ran while one was open for 1% -> 2% of each run, Pallas kernels for 22% -> 22%
where the time goes in v10:
time: 121 us
  Pallas kernels  43.3 us (36%)
  waiting for transfers between devices  40.3 us (33%)
  starting transfers between devices  33.9 us (28%)
  other arithmetic  2.09 us (2%)
    pallas_call x4, Pallas kernels, run_pass(): pl.pallas_call(body, out_shape=out_shape, grid_spec=pltpu.PrefetchScalarG...  38.2 us
    ppermute x16, starting transfers between devices, swap(): return lax.ppermute(value, axis, [(i, i ^ bit) for i in range(size)])  16.4 us
    ppermute x6, waiting for transfers between devices, swap_first(): return lax.ppermute(value, 'pts', pairs)  15.8 us
    ppermute x16, waiting for transfers between devices, swap(): return lax.ppermute(value, axis, [(i, i ^ bit) for i in range(size)])  13.2 us
    ppermute x6, waiting for transfers between devices, swap_second(): return lax.ppermute(value, 'pts', pairs)  11.2 us
    ppermute x6, starting transfers between devices, swap_second(): return lax.ppermute(value, 'pts', pairs)  11 us
    ppermute x6, starting transfers between devices, swap_first(): return lax.ppermute(value, 'pts', pairs)  6.47 us
    pallas_call x2, Pallas kernels, refine_half(): pl.pallas_call(refine_body, out_shape=[jax.ShapeDtypeStruct((mid, block_w...  3 us
  transfers between devices with their start and end apart: 28, of which 17 were waited for; matrix products, arithmetic and copies ran while one was open for 2% of the time, Pallas kernels for 22%

profile of v10, /device:TPU:0, one launch (start us, length us, event | category | flops | bytes accessed | tf_op | source)
XLA Modules:
  0.0 120.7 jit_solution(12298951345711259157)
XLA Ops:
  0.6 0.1 pad_add_fusion.info
  0.7 11.6 %energies_and_sums_00.1 = (f32[4,264,256]{2,1,0:T(8,128)S(1)}, f32[2,4096]{1,0:T(2,128)S(1)}, f32[1,4096]{1,0:T(1,128)S(1)}, bf16[4096,1024]{1,0:T(8,128)(2,1)S(1)}) custom-call(s32[4]{0:T(128)S(1)} %pad_add_fusion.info, bf16[4096,1024]{1,0:T(8,128)(2,1)} %points.3, s32[2,4096]{1,0:T(2,128)} %assign.7, f32[512,1024]{1,0:T(8,128)} %fine.3), custom_call_target="tpu_custom_call" | custom-call | flops 4294967296 | bytes 8388608 | tf_op jit(solution)/shard_map/energies_and_sums_00/pallas_call | solution.py:310
  12.3 0.8 collective-permute-start
  13.1 8.3 %energies_and_sums_01.1 = (f32[4,264,256]{2,1,0:T(8,128)S(1)}, f32[2,4096]{1,0:T(2,128)S(1)}) custom-call(s32[4]{0:T(128)S(1)} %pad_add_fusion.info, bf16[4096,1024]{1,0:T(8,128)(2,1)S(1)} %get-tuple-element.28.points, s32[2,4096]{1,0:T(2,128)S(1)} %copy-done.3, f32[512,1024]{1,0:T(8,128)S(1)} %copy-done.2, f32[1,4096]{1,0:T(1,128)S(1)} %get-tuple-element.29.refs_0_, ...), custom_call_target="tpu_custom_call" | custom-call | flops 4294967296 | bytes 8388608 | tf_op jit(solution)/shard_map/energies_and_sums_01/pallas_call | solution.py:310
  21.5 0.0 copy-start
  21.5 0.0 copy-start.1
  21.5 2.4 %collective-permute-start.1 = (f32[2,136,256]{2,1,0:T(8,128)S(1)}, f32[2,136,256]{2,1,0:T(8,128)S(1)}, u32[]{:S(2)}, u32[]{:S(2)}) collective-permute-start(f32[2,136,256]{2,1,0:T(8,128)S(1)} %slice_add_fusion.1), channel_id=1, source_target_pairs={{0,8},{4,20},{8,0},{12,28},{16,24},{20,4},{24,16},{28,12},{1,9},{5... | collective-permute-start | bytes 835592 | tf_op jit(solution)/shard_map/ppermute | solution.py:94
  23.9 0.1 collective-permute-start.2
  24.0 4.4 %collective-permute-done.1.refs_0_ = f32[2,136,256]{2,1,0:T(8,128)S(1)} collective-permute-done((f32[2,136,256]{2,1,0:T(8,128)S(1)}, f32[2,136,256]{2,1,0:T(8,128)S(1)}, u32[]{:S(2)}, u32[]{:S(2)}) %collective-permute-start.1) | collective-permute-done | bytes 278560 | tf_op jit(solution)/shard_map/ppermute | solution.py:94
  28.4 2.1 %collective-permute-start.3 = (f32[136,256]{1,0:T(8,128)S(1)}, f32[136,256]{1,0:T(8,128)S(1)}, u32[]{:S(2)}, u32[]{:S(2)}) collective-permute-start(f32[136,256]{1,0:T(8,128)S(1)} %fusion.2), channel_id=1, source_target_pairs={{0,16},{4,12},{8,24},{12,4},{16,0},{20,28},{24,8},{28,20},{1,17},{... | collective-permute-start | bytes 417800 | tf_op jit(solution)/shard_map/ppermute | solution.py:99
  30.5 0.8 collective-permute-done.2.refs_1_
  31.3 0.7 fusion.4
  32.0 2.4 %collective-permute-start.4 = (f32[128,256]{1,0:T(8,128)}, f32[128,256]{1,0:T(8,128)S(1)}, u32[]{:S(2)}, u32[]{:S(2)}) collective-permute-start(f32[128,256]{1,0:T(8,128)} %fusion.4), channel_id=1, source_target_pairs={{0,16},{4,12},{8,24},{12,4},{16,0},{20,28},{24,8},{28,20},{1,17},{... | collective-permute-start | bytes 393224 | tf_op jit(solution)/shard_map/ppermute | solution.py:99
  34.4 3.1 %collective-permute-done.4.refs_3_ = f32[128,256]{1,0:T(8,128)S(1)} collective-permute-done((f32[128,256]{1,0:T(8,128)}, f32[128,256]{1,0:T(8,128)S(1)}, u32[]{:S(2)}, u32[]{:S(2)}) %collective-permute-start.4) | collective-permute-done | bytes 131104 | tf_op jit(solution)/shard_map/ppermute | solution.py:99
  37.6 0.0 collective-permute-done.3.refs_2_
  37.6 1.5 %refine_half.2 = (f32[128,256]{1,0:T(8,128)S(1)}, f32[128,256]{1,0:T(8,128)S(1)}, f32[72,256]{1,0:T(8,128)S(1)}) custom-call(s32[4]{0:T(128)S(1)} %pad_add_fusion.info, f32[4,264,256]{2,1,0:T(8,128)S(1)} %get-tuple-element.31.own, f32[4,264,256]{2,1,0:T(8,128)S(1)} %collective-permute-done.sibling, f32[2,136,256]{2,1,0:T(8,128)S(1)} %collective-permute-done.1.refs_0_, ...), custom_call_target="tpu_custom_call" | custom-call | tf_op jit(solution)/shard_map/refine_half/pallas_call | solution.py:370
  39.1 2.0 %collective-permute-start.7 = (f32[128,256]{1,0:T(8,128)S(1)}, f32[128,256]{1,0:T(8,128)S(1)}, u32[]{:S(2)}, u32[]{:S(2)}) collective-permute-start(f32[128,256]{1,0:T(8,128)S(1)} %get-tuple-element.33), channel_id=1, source_target_pairs={{0,16},{4,20},{8,24},{12,28},{16,0},{20,4},{24,8},{28,12},{1,17},{... | collective-permute-start | bytes 393224 | tf_op jit(solution)/shard_map/ppermute | solution.py:89
  41.1 1.5 %collective-permute-start.5 = (f32[128,256]{1,0:T(8,128)S(1)}, f32[128,256]{1,0:T(8,128)S(1)}, u32[]{:S(2)}, u32[]{:S(2)}) collective-permute-start(f32[128,256]{1,0:T(8,128)S(1)} %get-tuple-element.33), channel_id=1, source_target_pairs={{0,8},{4,12},{8,0},{12,4},{16,24},{20,28},{24,16},{28,20},{1,9},{5... | collective-permute-start | bytes 393224 | tf_op jit(solution)/shard_map/ppermute | solution.py:89
  42.6 0.5 collective-permute-start.8
  43.1 0.1 collective-permute-start.6
  43.2 0.0 collective-permute-start.11
  43.2 1.2 %collective-permute-done.11 = f32[72,256]{1,0:T(8,128)S(1)} collective-permute-done((f32[72,256]{1,0:T(8,128)S(1)}, f32[72,256]{1,0:T(8,128)S(1)}, u32[]{:S(2)}, u32[]{:S(2)}) %collective-permute-start.11) | collective-permute-done | bytes 73760 | tf_op jit(solution)/shard_map/ppermute | solution.py:89
  44.5 2.1 %collective-permute-start.12 = (f32[104,256]{1,0:T(8,128)S(1)}, f32[104,256]{1,0:T(8,128)S(1)}, u32[]{:S(2)}, u32[]{:S(2)}) collective-permute-start(f32[104,256]{1,0:T(8,128)S(1)} %pad_maximum_fusion.4), channel_id=1, source_target_pairs={{0,1},{1,0},{2,3},{3,2},{4,5},{5,4},{6,7},{7,6},{8,9},{9,8},{10,11... | collective-permute-start | bytes 319496 | tf_op jit(solution)/shard_map/ppermute | solution.py:89
  46.6 0.0 collective-permute-done.7
  46.6 1.5 %collective-permute-start.9 = (f32[128,256]{1,0:T(8,128)S(1)}, f32[128,256]{1,0:T(8,128)S(1)}, u32[]{:S(2)}, u32[]{:S(2)}) collective-permute-start(f32[128,256]{1,0:T(8,128)S(1)} %collective-permute-done.7), channel_id=1, source_target_pairs={{0,8},{4,12},{8,0},{12,4},{16,24},{20,28},{24,16},{28,20},{1,9},{5... | collective-permute-start | bytes 393224 | tf_op jit(solution)/shard_map/ppermute | solution.py:89
  48.1 1.5 %collective-permute-start.10 = (f32[128,256]{1,0:T(8,128)S(1)}, f32[128,256]{1,0:T(8,128)S(1)}, u32[]{:S(2)}, u32[]{:S(2)}) collective-permute-start(f32[128,256]{1,0:T(8,128)S(1)} %collective-permute-done.6), channel_id=1, source_target_pairs={{0,16},{4,20},{8,24},{12,28},{16,0},{20,4},{24,8},{28,12},{1,17},{... | collective-permute-start | bytes 393224 | tf_op jit(solution)/shard_map/ppermute | solution.py:89
  49.6 0.0 collective-permute-done.8
  49.7 0.2 collective-permute-done.12
  49.9 1.9 %collective-permute-done.9 = f32[128,256]{1,0:T(8,128)S(1)} collective-permute-done((f32[128,256]{1,0:T(8,128)S(1)}, f32[128,256]{1,0:T(8,128)S(1)}, u32[]{:S(2)}, u32[]{:S(2)}) %collective-permute-start.9) | collective-permute-done | bytes 131104 | tf_op jit(solution)/shard_map/ppermute | solution.py:89
  51.9 1.2 collective-permute-done.10
  53.1 0.1 pad_maximum_fusion.fine
  53.2 0.0 copy-start.4
  53.2 0.1 collective-permute-start.13
  53.3 10.0 %energies_and_sums_10.1 = (f32[4,264,256]{2,1,0:T(8,128)S(1)}, f32[2,4096]{1,0:T(2,128)S(1)}, bf16[4096,1024]{1,0:T(8,128)(2,1)S(1)}) custom-call(s32[4]{0:T(128)S(1)} %pad_add_fusion.info, bf16[4096,1024]{1,0:T(8,128)(2,1)} %points.3, s32[2,4096]{1,0:T(2,128)} %assign.7, f32[4,256,256]{2,1,0:T(8,128)S(1)} %pad_maximum_fusion.fine, ...), custom_call_target="tpu_custom_call" | custom-call | flops 4294967296 | bytes 8388608 | tf_op jit(solution)/shard_map/energies_and_sums_10/pallas_call | solution.py:310
  63.2 0.4 collective-permute-start.14
  63.6 8.3 %energies_and_sums_11.1 = (f32[4,264,256]{2,1,0:T(8,128)S(1)}, f32[2,4096]{1,0:T(2,128)S(1)}) custom-call(s32[4]{0:T(128)S(1)} %pad_add_fusion.info, bf16[4096,1024]{1,0:T(8,128)(2,1)S(1)} %get-tuple-element.38.points, s32[2,4096]{1,0:T(2,128)S(1)} %copy-done.4, f32[4,256,256]{2,1,0:T(8,128)S(1)} %collective-permute-done.13.fine, ...), custom_call_target="tpu_custom_call" | custom-call | flops 4294967296 | bytes 8388608 | tf_op jit(solution)/shard_map/energies_and_sums_11/pallas_call | solution.py:310
  72.0 0.9 collective-permute-start.16
  73.0 1.2 %collective-permute-start.15 = (f32[2,136,256]{2,1,0:T(8,128)S(1)}, f32[2,136,256]{2,1,0:T(8,128)S(1)}, u32[]{:S(2)}, u32[]{:S(2)}) collective-permute-start(f32[2,136,256]{2,1,0:T(8,128)S(1)} %slice_add_fusion), channel_id=1, source_target_pairs={{0,8},{4,20},{8,0},{12,28},{16,24},{20,4},{24,16},{28,12},{1,9},{5... | collective-permute-start | bytes 835592 | tf_op jit(solution)/shard_map/ppermute | solution.py:94
  74.3 4.2 %collective-permute-done.16.refs_1_ = f32[2,128,256]{2,1,0:T(8,128)S(1)} collective-permute-done((f32[2,128,256]{2,1,0:T(8,128)S(1)}, f32[2,128,256]{2,1,0:T(8,128)S(1)}, u32[]{:S(2)}, u32[]{:S(2)}) %collective-permute-start.16) | collective-permute-done | bytes 262176 | tf_op jit(solution)/shard_map/ppermute | solution.py:94
  78.5 1.6 %collective-permute-start.18 = (f32[128,256]{1,0:T(8,128)S(1)}, f32[128,256]{1,0:T(8,128)S(1)}, u32[]{:S(2)}, u32[]{:S(2)}) collective-permute-start(f32[128,256]{1,0:T(8,128)S(1)} %fusion.3), channel_id=1, source_target_pairs={{0,16},{4,12},{8,24},{12,4},{16,0},{20,28},{24,8},{28,20},{1,17},{... | collective-permute-start | bytes 393224 | tf_op jit(solution)/shard_map/ppermute | solution.py:99
  80.1 2.2 %collective-permute-done.15.refs_0_ = f32[2,136,256]{2,1,0:T(8,128)S(1)} collective-permute-done((f32[2,136,256]{2,1,0:T(8,128)S(1)}, f32[2,136,256]{2,1,0:T(8,128)S(1)}, u32[]{:S(2)}, u32[]{:S(2)}) %collective-permute-start.15) | collective-permute-done | bytes 278560 | tf_op jit(solution)/shard_map/ppermute | solution.py:94
  82.3 2.6 %collective-permute-start.19 = (f32[104,256]{1,0:T(8,128)S(1)}, f32[104,256]{1,0:T(8,128)S(1)}, u32[]{:S(2)}, u32[]{:S(2)}) collective-permute-start(f32[104,256]{1,0:T(8,128)S(1)} %pad_maximum_fusion.5), channel_id=1, source_target_pairs={{0,2},{1,3},{2,0},{3,1},{4,6},{5,7},{6,4},{7,5},{8,10},{9,11},{10,... | collective-permute-start | bytes 319496 | tf_op jit(solution)/shard_map/ppermute | solution.py:89
  84.9 1.6 %collective-permute-start.17 = (f32[136,256]{1,0:T(8,128)S(1)}, f32[136,256]{1,0:T(8,128)S(1)}, u32[]{:S(2)}, u32[]{:S(2)}) collective-permute-start(f32[136,256]{1,0:T(8,128)S(1)} %fusion.1), channel_id=1, source_target_pairs={{0,16},{4,12},{8,24},{12,4},{16,0},{20,28},{24,8},{28,20},{1,17},{... | collective-permute-start | bytes 417800 | tf_op jit(solution)/shard_map/ppermute | solution.py:99
  86.5 1.4 %collective-permute-done.19 = f32[104,256]{1,0:T(8,128)S(1)} collective-permute-done((f32[104,256]{1,0:T(8,128)S(1)}, f32[104,256]{1,0:T(8,128)S(1)}, u32[]{:S(2)}, u32[]{:S(2)}) %collective-permute-start.19) | collective-permute-done | bytes 106528 | tf_op jit(solution)/shard_map/ppermute | solution.py:89
  88.0 0.1 slice_divide_fusion.refs_5_
  88.1 2.0 %collective-permute-done.17.refs_2_ = f32[136,256]{1,0:T(8,128)S(1)} collective-permute-done((f32[136,256]{1,0:T(8,128)S(1)}, f32[136,256]{1,0:T(8,128)S(1)}, u32[]{:S(2)}, u32[]{:S(2)}) %collective-permute-start.17) | collective-permute-done | bytes 139296 | tf_op jit(solution)/shard_map/ppermute | solution.py:99
  90.1 1.5 %refine_half.3 = (f32[128,256]{1,0:T(8,128)S(1)}, f32[128,256]{1,0:T(8,128)S(1)}, f32[72,256]{1,0:T(8,128)S(1)}) custom-call(s32[4]{0:T(128)S(1)} %pad_add_fusion.info, f32[4,264,256]{2,1,0:T(8,128)S(1)} %get-tuple-element.40.own, f32[4,264,256]{2,1,0:T(8,128)S(1)} %collective-permute-done.14.sibling, f32[2,136,256]{2,1,0:T(8,128)S(1)} %collective-permute-done.15.refs_0_, ...), custom_call_target="tpu_custom_call" | custom-call | tf_op jit(solution)/shard_map/refine_half/pallas_call | solution.py:370
  91.6 1.7 %collective-permute-start.21 = (f32[104,256]{1,0:T(8,128)S(1)}, f32[104,256]{1,0:T(8,128)S(1)}, u32[]{:S(2)}, u32[]{:S(2)}) collective-permute-start(f32[104,256]{1,0:T(8,128)S(1)} %pad_maximum_fusion.6), channel_id=1, source_target_pairs={{0,1},{1,0},{2,3},{3,2},{4,5},{5,4},{6,7},{7,6},{8,9},{9,8},{10,11... | collective-permute-start | bytes 319496 | tf_op jit(solution)/shard_map/ppermute | solution.py:89
  93.3 1.7 %collective-permute-start.20 = (f32[256,256]{1,0:T(8,128)S(1)}, f32[256,256]{1,0:T(8,128)S(1)}, u32[]{:S(2)}, u32[]{:S(2)}) collective-permute-start(f32[256,256]{1,0:T(8,128)S(1)} %constant_dynamic-update-slice_fusion), channel_id=1, source_target_pairs={{0,16},{4,12},{8,24},{12,4},{16,0},{20,28},{24,8},{28,20},{1,17},{... | collective-permute-start | bytes 786440 | tf_op jit(solution)/shard_map/ppermute | solution.py:99
  94.9 1.4 %collective-permute-done.21 = f32[104,256]{1,0:T(8,128)S(1)} collective-permute-done((f32[104,256]{1,0:T(8,128)S(1)}, f32[104,256]{1,0:T(8,128)S(1)}, u32[]{:S(2)}, u32[]{:S(2)}) %collective-permute-start.21) | collective-permute-done | bytes 106528 | tf_op jit(solution)/shard_map/ppermute | solution.py:89
  96.4 3.3 %collective-permute-done.20 = f32[256,256]{1,0:T(8,128)S(1)} collective-permute-done((f32[256,256]{1,0:T(8,128)S(1)}, f32[256,256]{1,0:T(8,128)S(1)}, u32[]{:S(2)}, u32[]{:S(2)}) %collective-permute-start.20) | collective-permute-done | bytes 262176 | tf_op jit(solution)/shard_map/ppermute | solution.py:99
  99.7 1.6 %collective-permute-start.24 = (f32[104,256]{1,0:T(8,128)S(1)}, f32[104,256]{1,0:T(8,128)S(1)}, u32[]{:S(2)}, u32[]{:S(2)}) collective-permute-start(f32[104,256]{1,0:T(8,128)S(1)} %pad_maximum_fusion.7), channel_id=1, source_target_pairs={{0,2},{1,3},{2,0},{3,1},{4,6},{5,7},{6,4},{7,5},{8,10},{9,11},{10,... | collective-permute-start | bytes 319496 | tf_op jit(solution)/shard_map/ppermute | solution.py:89
  101.3 0.9 collective-permute-start.23
  102.3 4.2 %collective-permute-done.24 = f32[104,256]{1,0:T(8,128)S(1)} collective-permute-done((f32[104,256]{1,0:T(8,128)S(1)}, f32[104,256]{1,0:T(8,128)S(1)}, u32[]{:S(2)}, u32[]{:S(2)}) %collective-permute-start.24) | collective-permute-done | bytes 106528 | tf_op jit(solution)/shard_map/ppermute | solution.py:89
  106.5 1.6 %collective-permute-start.25 = (f32[72,256]{1,0:T(8,128)S(1)}, f32[72,256]{1,0:T(8,128)S(1)}, u32[]{:S(2)}, u32[]{:S(2)}) collective-permute-start(f32[72,256]{1,0:T(8,128)S(1)} %slice_add_fusion.11), channel_id=1, source_target_pairs={{0,16},{4,12},{8,24},{12,4},{16,0},{20,28},{24,8},{28,20},{1,17},{... | collective-permute-start | bytes 221192 | tf_op jit(solution)/shard_map/ppermute | solution.py:99
  108.1 2.8 %collective-permute-done.25 = f32[72,256]{1,0:T(8,128)S(1)} collective-permute-done((f32[72,256]{1,0:T(8,128)S(1)}, f32[72,256]{1,0:T(8,128)S(1)}, u32[]{:S(2)}, u32[]{:S(2)}) %collective-permute-start.25) | collective-permute-done | bytes 73760 | tf_op jit(solution)/shard_map/ppermute | solution.py:99
  110.9 0.9 collective-permute-start.26
  111.8 0.1 collective-permute-start.22
  111.9 4.2 %collective-permute-done.26 = f32[2,72,256]{2,1,0:T(8,128)S(1)} collective-permute-done((f32[2,72,256]{2,1,0:T(8,128)S(1)}, f32[2,72,256]{2,1,0:T(8,128)S(1)}, u32[]{:S(2)}, u32[]{:S(2)}) %collective-permute-start.26) | collective-permute-done | bytes 147488 | tf_op jit(solution)/shard_map/ppermute | solution.py:94
  116.1 0.1 pad_maximum_fusion.1.last
  116.2 0.1 collective-permute-start.27
  116.3 0.7 maximum_multiply_fusion
  117.0 1.6 %collective-permute-done.27.last_other = f32[2,400,256]{2,1,0:T(8,128)S(1)} collective-permute-done((f32[2,400,256]{2,1,0:T(8,128)S(1)}, f32[2,400,256]{2,1,0:T(8,128)S(1)}, u32[]{:S(2)}, u32[]{:S(2)}) %collective-permute-start.27) | collective-permute-done | bytes 819232 | tf_op jit(solution)/shard_map/ppermute | solution.py:89
  118.6 2.2 %place_blocks.1 = (f32[512,1024]{1,0:T(8,128)}, f32[64,1024]{1,0:T(8,128)}) custom-call(s32[4]{0:T(128)S(1)} %pad_add_fusion.info, f32[2,256,256]{2,1,0:T(8,128)S(1)} %pad_maximum_fusion.2.own, f32[2,256,256]{2,1,0:T(8,128)S(1)} %collective-permute-done.22.other, f32[2,400,256]{2,1,0:T(8,128)S(1)} %pad_maximum_fusion.1.last, ...), custom_call_target="tpu_custom_call" | custom-call | tf_op jit(solution)/shard_map/place_blocks/pallas_call | solution.py:472
  (50 shorter events, 0.6 us)
Async XLA Ops:
  0.7 12.4 %copy-start.2 = (f32[512,1024]{1,0:T(8,128)S(1)}, f32[512,1024]{1,0:T(8,128)}, u32[]{:S(2)}) copy-start(f32[512,1024]{1,0:T(8,128)} %fine.3) | copy-start | bytes 6291460
  0.7 12.4 %copy-start.3 = (s32[2,4096]{1,0:T(2,128)S(1)}, s32[2,4096]{1,0:T(2,128)}, u32[]{:S(2)}) copy-start(s32[2,4096]{1,0:T(2,128)} %assign.7) | copy-start | bytes 98308
  12.3 9.1 %collective-permute-start = (f32[4,264,256]{2,1,0:T(8,128)S(1)}, f32[4,264,256]{2,1,0:T(8,128)S(1)}, u32[]{:S(2)}, u32[]{:S(2)}) collective-permute-start(f32[4,264,256]{2,1,0:T(8,128)S(1)} %get-tuple-element.32), channel_id=1, source_target_pairs={{0,4},{4,0},{8,12},{12,8},{16,20},{20,16},{24,28},{28,24},{1,5},{5... | collective-permute-start | bytes 3244040 | tf_op jit(solution)/shard_map/ppermute | solution.py:89
  21.5 16.1 %copy-start = (f32[64,1024]{1,0:T(8,128)S(1)}, f32[64,1024]{1,0:T(8,128)}, u32[]{:S(2)}) copy-start(f32[64,1024]{1,0:T(8,128)} %refs_5_.1) | copy-start | bytes 786436
  21.5 16.1 %copy-start.1 = (s32[512]{0:T(512)S(1)}, s32[512]{0:T(512)}, u32[]{:S(2)}) copy-start(s32[512]{0:T(512)} %param.9) | copy-start | bytes 6148
  21.5 6.9 %collective-permute-start.1 = (f32[2,136,256]{2,1,0:T(8,128)S(1)}, f32[2,136,256]{2,1,0:T(8,128)S(1)}, u32[]{:S(2)}, u32[]{:S(2)}) collective-permute-start(f32[2,136,256]{2,1,0:T(8,128)S(1)} %slice_add_fusion.1), channel_id=1, source_target_pairs={{0,8},{4,20},{8,0},{12,28},{16,24},{20,4},{24,16},{28,12},{1,9},{5... | collective-permute-start | bytes 835592 | tf_op jit(solution)/shard_map/ppermute | solution.py:94
  23.9 7.5 %collective-permute-start.2 = (f32[2,128,256]{2,1,0:T(8,128)S(1)}, f32[2,128,256]{2,1,0:T(8,128)S(1)}, u32[]{:S(2)}, u32[]{:S(2)}) collective-permute-start(f32[2,128,256]{2,1,0:T(8,128)S(1)} %slice_add_fusion.3), channel_id=1, source_target_pairs={{0,8},{4,20},{8,0},{12,28},{16,24},{20,4},{24,16},{28,12},{1,9},{5... | collective-permute-start | bytes 786440 | tf_op jit(solution)/shard_map/ppermute | solution.py:94
  28.4 9.2 %collective-permute-start.3 = (f32[136,256]{1,0:T(8,128)S(1)}, f32[136,256]{1,0:T(8,128)S(1)}, u32[]{:S(2)}, u32[]{:S(2)}) collective-permute-start(f32[136,256]{1,0:T(8,128)S(1)} %fusion.2), channel_id=1, source_target_pairs={{0,16},{4,12},{8,24},{12,4},{16,0},{20,28},{24,8},{28,20},{1,17},{... | collective-permute-start | bytes 417800 | tf_op jit(solution)/shard_map/ppermute | solution.py:99
  32.0 5.5 %collective-permute-start.4 = (f32[128,256]{1,0:T(8,128)}, f32[128,256]{1,0:T(8,128)S(1)}, u32[]{:S(2)}, u32[]{:S(2)}) collective-permute-start(f32[128,256]{1,0:T(8,128)} %fusion.4), channel_id=1, source_target_pairs={{0,16},{4,12},{8,24},{12,4},{16,0},{20,28},{24,8},{28,20},{1,17},{... | collective-permute-start | bytes 393224 | tf_op jit(solution)/shard_map/ppermute | solution.py:99
  39.1 7.5 %collective-permute-start.7 = (f32[128,256]{1,0:T(8,128)S(1)}, f32[128,256]{1,0:T(8,128)S(1)}, u32[]{:S(2)}, u32[]{:S(2)}) collective-permute-start(f32[128,256]{1,0:T(8,128)S(1)} %get-tuple-element.33), channel_id=1, source_target_pairs={{0,16},{4,20},{8,24},{12,28},{16,0},{20,4},{24,8},{28,12},{1,17},{... | collective-permute-start | bytes 393224 | tf_op jit(solution)/shard_map/ppermute | solution.py:89
  41.1 8.5 %collective-permute-start.5 = (f32[128,256]{1,0:T(8,128)S(1)}, f32[128,256]{1,0:T(8,128)S(1)}, u32[]{:S(2)}, u32[]{:S(2)}) collective-permute-start(f32[128,256]{1,0:T(8,128)S(1)} %get-tuple-element.33), channel_id=1, source_target_pairs={{0,8},{4,12},{8,0},{12,4},{16,24},{20,28},{24,16},{28,20},{1,9},{5... | collective-permute-start | bytes 393224 | tf_op jit(solution)/shard_map/ppermute | solution.py:89
  42.6 7.0 %collective-permute-start.8 = (f32[128,256]{1,0:T(8,128)S(1)}, f32[128,256]{1,0:T(8,128)S(1)}, u32[]{:S(2)}, u32[]{:S(2)}) collective-permute-start(f32[128,256]{1,0:T(8,128)S(1)} %get-tuple-element.34), channel_id=1, source_target_pairs={{0,16},{4,20},{8,24},{12,28},{16,0},{20,4},{24,8},{28,12},{1,17},{... | collective-permute-start | bytes 393224 | tf_op jit(solution)/shard_map/ppermute | solution.py:89
  43.1 5.0 %collective-permute-start.6 = (f32[128,256]{1,0:T(8,128)S(1)}, f32[128,256]{1,0:T(8,128)S(1)}, u32[]{:S(2)}, u32[]{:S(2)}) collective-permute-start(f32[128,256]{1,0:T(8,128)S(1)} %get-tuple-element.34), channel_id=1, source_target_pairs={{0,8},{4,12},{8,0},{12,4},{16,24},{20,28},{24,16},{28,20},{1,9},{5... | collective-permute-start | bytes 393224 | tf_op jit(solution)/shard_map/ppermute | solution.py:89
  43.2 1.3 %collective-permute-start.11 = (f32[72,256]{1,0:T(8,128)S(1)}, f32[72,256]{1,0:T(8,128)S(1)}, u32[]{:S(2)}, u32[]{:S(2)}) collective-permute-start(f32[72,256]{1,0:T(8,128)S(1)} %get-tuple-element.35), channel_id=1, source_target_pairs={{0,4},{4,0},{8,12},{12,8},{16,20},{20,16},{24,28},{28,24},{1,5},{5... | collective-permute-start | bytes 221192 | tf_op jit(solution)/shard_map/ppermute | solution.py:89
  44.5 5.4 %collective-permute-start.12 = (f32[104,256]{1,0:T(8,128)S(1)}, f32[104,256]{1,0:T(8,128)S(1)}, u32[]{:S(2)}, u32[]{:S(2)}) collective-permute-start(f32[104,256]{1,0:T(8,128)S(1)} %pad_maximum_fusion.4), channel_id=1, source_target_pairs={{0,1},{1,0},{2,3},{3,2},{4,5},{5,4},{6,7},{7,6},{8,9},{9,8},{10,11... | collective-permute-start | bytes 319496 | tf_op jit(solution)/shard_map/ppermute | solution.py:89
  46.6 5.3 %collective-permute-start.9 = (f32[128,256]{1,0:T(8,128)S(1)}, f32[128,256]{1,0:T(8,128)S(1)}, u32[]{:S(2)}, u32[]{:S(2)}) collective-permute-start(f32[128,256]{1,0:T(8,128)S(1)} %collective-permute-done.7), channel_id=1, source_target_pairs={{0,8},{4,12},{8,0},{12,4},{16,24},{20,28},{24,16},{28,20},{1,9},{5... | collective-permute-start | bytes 393224 | tf_op jit(solution)/shard_map/ppermute | solution.py:89
  48.1 5.0 %collective-permute-start.10 = (f32[128,256]{1,0:T(8,128)S(1)}, f32[128,256]{1,0:T(8,128)S(1)}, u32[]{:S(2)}, u32[]{:S(2)}) collective-permute-start(f32[128,256]{1,0:T(8,128)S(1)} %collective-permute-done.6), channel_id=1, source_target_pairs={{0,16},{4,20},{8,24},{12,28},{16,0},{20,4},{24,8},{28,12},{1,17},{... | collective-permute-start | bytes 393224 | tf_op jit(solution)/shard_map/ppermute | solution.py:89
  53.2 10.4 %copy-start.4 = (s32[2,4096]{1,0:T(2,128)S(1)}, s32[2,4096]{1,0:T(2,128)}, u32[]{:S(2)}) copy-start(s32[2,4096]{1,0:T(2,128)} %assign.7) | copy-start | bytes 98308
  53.2 10.4 %collective-permute-start.13 = (f32[4,256,256]{2,1,0:T(8,128)S(1)}, f32[4,256,256]{2,1,0:T(8,128)S(1)}, u32[]{:S(2)}, u32[]{:S(2)}) collective-permute-start(f32[4,256,256]{2,1,0:T(8,128)S(1)} %pad_maximum_fusion.fine), channel_id=1, source_target_pairs={{0,4},{4,0},{8,12},{12,8},{16,20},{20,16},{24,28},{28,24},{1,5},{5... | collective-permute-start | bytes 3145736 | tf_op jit(solution)/shard_map/ppermute | solution.py:89
  63.2 8.7 %collective-permute-start.14 = (f32[4,264,256]{2,1,0:T(8,128)S(1)}, f32[4,264,256]{2,1,0:T(8,128)S(1)}, u32[]{:S(2)}, u32[]{:S(2)}) collective-permute-start(f32[4,264,256]{2,1,0:T(8,128)S(1)} %get-tuple-element.41), channel_id=1, source_target_pairs={{0,4},{4,0},{8,12},{12,8},{16,20},{20,16},{24,28},{28,24},{1,5},{5... | collective-permute-start | bytes 3244040 | tf_op jit(solution)/shard_map/ppermute | solution.py:89
  72.0 6.4 %collective-permute-start.16 = (f32[2,128,256]{2,1,0:T(8,128)S(1)}, f32[2,128,256]{2,1,0:T(8,128)S(1)}, u32[]{:S(2)}, u32[]{:S(2)}) collective-permute-start(f32[2,128,256]{2,1,0:T(8,128)S(1)} %slice_add_fusion.2), channel_id=1, source_target_pairs={{0,8},{4,20},{8,0},{12,28},{16,24},{20,4},{24,16},{28,12},{1,9},{5... | collective-permute-start | bytes 786440 | tf_op jit(solution)/shard_map/ppermute | solution.py:94
  73.0 9.3 %collective-permute-start.15 = (f32[2,136,256]{2,1,0:T(8,128)S(1)}, f32[2,136,256]{2,1,0:T(8,128)S(1)}, u32[]{:S(2)}, u32[]{:S(2)}) collective-permute-start(f32[2,136,256]{2,1,0:T(8,128)S(1)} %slice_add_fusion), channel_id=1, source_target_pairs={{0,8},{4,20},{8,0},{12,28},{16,24},{20,4},{24,16},{28,12},{1,9},{5... | collective-permute-start | bytes 835592 | tf_op jit(solution)/shard_map/ppermute | solution.py:94
  78.5 9.5 %collective-permute-start.18 = (f32[128,256]{1,0:T(8,128)S(1)}, f32[128,256]{1,0:T(8,128)S(1)}, u32[]{:S(2)}, u32[]{:S(2)}) collective-permute-start(f32[128,256]{1,0:T(8,128)S(1)} %fusion.3), channel_id=1, source_target_pairs={{0,16},{4,12},{8,24},{12,4},{16,0},{20,28},{24,8},{28,20},{1,17},{... | collective-permute-start | bytes 393224 | tf_op jit(solution)/shard_map/ppermute | solution.py:99
  82.3 5.6 %collective-permute-start.19 = (f32[104,256]{1,0:T(8,128)S(1)}, f32[104,256]{1,0:T(8,128)S(1)}, u32[]{:S(2)}, u32[]{:S(2)}) collective-permute-start(f32[104,256]{1,0:T(8,128)S(1)} %pad_maximum_fusion.5), channel_id=1, source_target_pairs={{0,2},{1,3},{2,0},{3,1},{4,6},{5,7},{6,4},{7,5},{8,10},{9,11},{10,... | collective-permute-start | bytes 319496 | tf_op jit(solution)/shard_map/ppermute | solution.py:89
  84.9 5.1 %collective-permute-start.17 = (f32[136,256]{1,0:T(8,128)S(1)}, f32[136,256]{1,0:T(8,128)S(1)}, u32[]{:S(2)}, u32[]{:S(2)}) collective-permute-start(f32[136,256]{1,0:T(8,128)S(1)} %fusion.1), channel_id=1, source_target_pairs={{0,16},{4,12},{8,24},{12,4},{16,0},{20,28},{24,8},{28,20},{1,17},{... | collective-permute-start | bytes 417800 | tf_op jit(solution)/shard_map/ppermute | solution.py:99
  91.6 4.8 %collective-permute-start.21 = (f32[104,256]{1,0:T(8,128)S(1)}, f32[104,256]{1,0:T(8,128)S(1)}, u32[]{:S(2)}, u32[]{:S(2)}) collective-permute-start(f32[104,256]{1,0:T(8,128)S(1)} %pad_maximum_fusion.6), channel_id=1, source_target_pairs={{0,1},{1,0},{2,3},{3,2},{4,5},{5,4},{6,7},{7,6},{8,9},{9,8},{10,11... | collective-permute-start | bytes 319496 | tf_op jit(solution)/shard_map/ppermute | solution.py:89
  93.3 6.4 %collective-permute-start.20 = (f32[256,256]{1,0:T(8,128)S(1)}, f32[256,256]{1,0:T(8,128)S(1)}, u32[]{:S(2)}, u32[]{:S(2)}) collective-permute-start(f32[256,256]{1,0:T(8,128)S(1)} %constant_dynamic-update-slice_fusion), channel_id=1, source_target_pairs={{0,16},{4,12},{8,24},{12,4},{16,0},{20,28},{24,8},{28,20},{1,17},{... | collective-permute-start | bytes 786440 | tf_op jit(solution)/shard_map/ppermute | solution.py:99
  99.7 6.7 %collective-permute-start.24 = (f32[104,256]{1,0:T(8,128)S(1)}, f32[104,256]{1,0:T(8,128)S(1)}, u32[]{:S(2)}, u32[]{:S(2)}) collective-permute-start(f32[104,256]{1,0:T(8,128)S(1)} %pad_maximum_fusion.7), channel_id=1, source_target_pairs={{0,2},{1,3},{2,0},{3,1},{4,6},{5,7},{6,4},{7,5},{8,10},{9,11},{10,... | collective-permute-start | bytes 319496 | tf_op jit(solution)/shard_map/ppermute | solution.py:89
  101.3 14.8 %collective-permute-start.23 = (f32[2,256,256]{2,1,0:T(8,128)S(1)}, f32[2,256,256]{2,1,0:T(8,128)S(1)}, u32[]{:S(2)}, u32[]{:S(2)}) collective-permute-start(f32[2,256,256]{2,1,0:T(8,128)S(1)} %pad_maximum_fusion.2.own), channel_id=1, source_target_pairs={{0,8},{4,20},{8,0},{12,28},{16,24},{20,4},{24,16},{28,12},{1,9},{5... | collective-permute-start | bytes 1572872 | tf_op jit(solution)/shard_map/ppermute | solution.py:94
  106.5 4.4 %collective-permute-start.25 = (f32[72,256]{1,0:T(8,128)S(1)}, f32[72,256]{1,0:T(8,128)S(1)}, u32[]{:S(2)}, u32[]{:S(2)}) collective-permute-start(f32[72,256]{1,0:T(8,128)S(1)} %slice_add_fusion.11), channel_id=1, source_target_pairs={{0,16},{4,12},{8,24},{12,4},{16,0},{20,28},{24,8},{28,20},{1,17},{... | collective-permute-start | bytes 221192 | tf_op jit(solution)/shard_map/ppermute | solution.py:99
  110.9 5.2 %collective-permute-start.26 = (f32[2,72,256]{2,1,0:T(8,128)S(1)}, f32[2,72,256]{2,1,0:T(8,128)S(1)}, u32[]{:S(2)}, u32[]{:S(2)}) collective-permute-start(f32[2,72,256]{2,1,0:T(8,128)S(1)} %pad_maximum_fusion.3), channel_id=1, source_target_pairs={{0,8},{4,20},{8,0},{12,28},{16,24},{20,4},{24,16},{28,12},{1,9},{5... | collective-permute-start | bytes 442376 | tf_op jit(solution)/shard_map/ppermute | solution.py:94
  111.8 5.1 %collective-permute-start.22 = (f32[2,256,256]{2,1,0:T(8,128)S(1)}, f32[2,256,256]{2,1,0:T(8,128)S(1)}, u32[]{:S(2)}, u32[]{:S(2)}) collective-permute-start(f32[2,256,256]{2,1,0:T(8,128)S(1)} %pad_maximum_fusion.2.own), channel_id=1, source_target_pairs={{0,4},{4,0},{8,12},{12,8},{16,20},{20,16},{24,28},{28,24},{1,5},{5... | collective-permute-start | bytes 1572872 | tf_op jit(solution)/shard_map/ppermute | solution.py:89
  116.2 2.4 %collective-permute-start.27 = (f32[2,400,256]{2,1,0:T(8,128)S(1)}, f32[2,400,256]{2,1,0:T(8,128)S(1)}, u32[]{:S(2)}, u32[]{:S(2)}) collective-permute-start(f32[2,400,256]{2,1,0:T(8,128)S(1)} %pad_maximum_fusion.1.last), channel_id=1, source_target_pairs={{0,4},{4,0},{8,12},{12,8},{16,20},{20,16},{24,28},{28,24},{1,5},{5... | collective-permute-start | bytes 2457608 | tf_op jit(solution)/shard_map/ppermute | solution.py:89

commit v11 on v10

--- a/solution.py
+++ b/solution.py
@@ -104,8 +104,17 @@
     return info[0] ^ (slot + core * (crossed - slot))
 
 
-def full(*shape):
-    return pl.BlockSpec(shape, lambda i, info: (0,) * len(shape))
+HERE = pl.BlockSpec(memory_space=pltpu.VMEM)
+AWAY = pl.BlockSpec(memory_space=pl.ANY)
+SCALARS = pl.BlockSpec(memory_space=pltpu.SMEM)
+
+
+def near_by(value):
+    return pltpu.with_memory_space_constraint(value, pltpu.VMEM)
+
+
+def far_off(value):
+    return pltpu.with_memory_space_constraint(value, pltpu.HBM)
 
 
 def as_column(row, rows):
@@ -124,7 +133,7 @@
     low, norms, tallies, sums, even, odd, scaled = refs[:7]
     chosen_in = refs[7] if stream else assign
     small_sems, point_sems = refs[8:10] if stream else (None, None)
-    start = refs[10] if first else fine
+    start = refs[10] if first else None
     rows, width = low.shape
     mid = rows // 2
     block_width = width // SLOTS
@@ -159,7 +168,9 @@
     if initial:
         if first:
             load_start.wait()
-        block = start[...]
+            block = start[...]
+        else:
+            block = fine[pl.ds(pl.multiple_of(half * rows, rows), rows), :]
         norm = jnp.sum(block * block, axis=1, keepdims=True)
         low[...] = (-2.0 * block).astype(jnp.bfloat16)
     else:
@@ -252,34 +263,20 @@
     initial = pass_index == 0
     chained = seen is not None
     stream = not chained
-    whole = pl.BlockSpec(memory_space=pltpu.VMEM)
-    anywhere = pl.BlockSpec(memory_space=pl.ANY)
-    in_hbm = lambda value: pltpu.with_memory_space_constraint(value, pltpu.HBM)
     if stream:
-        in_specs = [anywhere, anywhere]
-        args = [in_hbm(points), in_hbm(fine_assign)]
+        in_specs = [AWAY, AWAY, AWAY if initial else HERE]
+        args = [far_off(points), far_off(fine_assign), far_off(fine) if initial else near_by(fine)]
     else:
-        in_specs = [whole, full(PASSES, count)]
-        args = [pltpu.with_memory_space_constraint(points, pltpu.VMEM), fine_assign]
-    if not initial:
-        in_specs.append(full(SLOTS, rows, block_width))
-    elif stream:
-        in_specs.append(anywhere)
-        fine = in_hbm(fine)
-    else:
-        in_specs.append(pl.BlockSpec((rows, width), lambda i, info: (info[1] ^ flip, 0)))
-    args.append(fine)
-    if squares is not None:
-        in_specs.append(full(1, count))
-        args.append(squares)
-    if chained:
-        in_specs.append(full(2, count))
-        args.append(seen)
+        in_specs = [HERE] * 3
+        args = [near_by(points), near_by(fine_assign), near_by(fine)]
+    for value in (squares, seen):
+        if value is not None:
+            in_specs.append(HERE)
+            args.append(near_by(value))
     shapes = [(SLOTS, rows + TAIL, block_width), (2, count)]
     if squares is None:
         shapes.append((1, count))
-    out_shape = [jax.ShapeDtypeStruct(shape, jnp.float32) for shape in shapes]
-    out_specs = [full(*shape) for shape in shapes]
+    out_shape = [pltpu.VMEM(shape, jnp.float32) for shape in shapes]
     scratch = [
         pltpu.VMEM((rows, width), jnp.bfloat16),
         pltpu.VMEM((rows, 128), jnp.float32),
@@ -298,7 +295,6 @@
         if initial:
             scratch.append(pltpu.VMEM((rows, width), jnp.float32))
         out_shape.append(pltpu.VMEM(points.shape, points.dtype))
-        out_specs.append(whole)
     body = functools.partial(
         pass_body,
         pass_index=pass_index,
@@ -310,14 +306,10 @@
     return pl.pallas_call(
         body,
         out_shape=out_shape,
-        grid_spec=pltpu.PrefetchScalarGridSpec(
-            num_scalar_prefetch=1,
-            grid=(1,),
-            in_specs=in_specs,
-            out_specs=out_specs,
-            scratch_shapes=scratch,
-        ),
-        compiler_params=pltpu.CompilerParams(vmem_limit_bytes=18 * 2**20),
+        in_specs=[SCALARS, *in_specs],
+        out_specs=[HERE] * len(out_shape),
+        scratch_shapes=scratch,
+        compiler_params=pltpu.CompilerParams(vmem_limit_bytes=16 * 2**20),
         cost_estimate=pl.CostEstimate(
             flops=4 * rows * count * width, bytes_accessed=2 * count * width, transcendentals=0
         ),
@@ -325,21 +317,28 @@
     )(info, *args)
 
 
-def refine_body(info, own, sibling, *refs):
-    first_top, first_low, second_top, second_low, owner, coarse, top, low, part = refs
-    rows = owner.shape[1]
+def refine_body(info, own, sibling, *refs, flip):
+    first_top, first_low, second_top, second_low, owners, coarse_in, top, low, part = refs
+    rows = owners.shape[2]
     mid = rows // 2
-    total = own[...] + sibling[...]
-    head = total[: mid + TAIL] + (first_top[...] + second_top[...])
-    rest = total[mid + TAIL :] + (first_low[...] + second_low[...])
+    block_width = part.shape[1]
+    owner = owners[info[1] ^ flip]
+    if coarse_in.shape[1] == block_width:
+        coarse = coarse_in[...]
+    else:
+        coarse = coarse_in[:, pl.ds(pl.multiple_of(info[0] * block_width, block_width), block_width)]
+    head = own[0, : mid + TAIL, :] + sibling[0, : mid + TAIL, :]
+    rest = own[0, mid + TAIL :, :] + sibling[0, mid + TAIL :, :]
+    head = head + (first_top[0] + second_top[...])
+    rest = rest + (first_low[0] + second_low[...])
     totals, counts_row = jnp.concatenate([head[:mid], rest], 0), head[mid:]
     counts = as_column(counts_row[:1], rows)[:, :1]
     table = (
-        lax.broadcasted_iota(jnp.int32, (NC, rows), 0) == owner[...]
+        lax.broadcasted_iota(jnp.int32, (NC, rows), 0) == owner
     ).astype(jnp.float32)
     lookup = lax.dot_general(
         table,
-        coarse[...],
+        coarse,
         (((0,), (0,)), ((), ())),
         precision=HIGHEST,
         preferred_element_type=jnp.float32,
@@ -348,7 +347,7 @@
     top[...] = new[:mid]
     low[...] = new[mid:]
     prior = jnp.where(info[3] == 0, prior_weight, 0.0)
-    part[:NC, :] = prior * coarse[...] + jnp.dot(
+    part[:NC, :] = prior * coarse + jnp.dot(
         table, counts * new, precision=HIGHEST, preferred_element_type=jnp.float32
     )
     part[NC:, :] = jnp.zeros((TAIL, part.shape[1]), jnp.float32)
@@ -363,51 +362,28 @@
 
 def refine_half(info, own, sibling, incoming, owners, coarse, *, flip):
     _, rows, block_width = own.shape
-    rows -= TAIL
-    mid = rows // 2
-    leading = lambda size: pl.BlockSpec((None, size, block_width), lambda i, info: (0, 0, 0))
-    wide = coarse.shape[1] != block_width
+    mid = (rows - TAIL) // 2
+    args = [near_by(value) for value in (own, sibling, *incoming, owners, coarse)]
+    shapes = [(mid, block_width), (mid, block_width), (NC + TAIL, block_width)]
     return pl.pallas_call(
-        refine_body,
-        out_shape=[
-            jax.ShapeDtypeStruct((mid, block_width), jnp.float32),
-            jax.ShapeDtypeStruct((mid, block_width), jnp.float32),
-            jax.ShapeDtypeStruct((NC + TAIL, block_width), jnp.float32),
-        ],
-        grid_spec=pltpu.PrefetchScalarGridSpec(
-            num_scalar_prefetch=1,
-            grid=(1,),
-            in_specs=[
-                leading(rows + TAIL),
-                leading(rows + TAIL),
-                leading(mid + TAIL),
-                leading(mid),
-                full(mid + TAIL, block_width),
-                full(mid, block_width),
-                pl.BlockSpec((None, 1, rows), lambda i, info: (info[1] ^ flip, 0, 0)),
-                pl.BlockSpec((NC, block_width), lambda i, info: (0, info[0] if wide else 0)),
-            ],
-            out_specs=[
-                full(mid, block_width),
-                full(mid, block_width),
-                full(NC + TAIL, block_width),
-            ],
-        ),
-        compiler_params=pltpu.CompilerParams(vmem_limit_bytes=16 * 2**20),
+        functools.partial(refine_body, flip=flip),
+        out_shape=[pltpu.VMEM(shape, jnp.float32) for shape in shapes],
+        in_specs=[SCALARS] + [HERE] * len(args),
+        out_specs=[HERE] * len(shapes),
+        compiler_params=pltpu.CompilerParams(vmem_limit_bytes=8 * 2**20),
         name="refine_half",
-    )(info, own, sibling, *incoming, owners, coarse)
-
-
-def exchange(held, sibling, later=()):
+    )(info, *args)
+
+
+def exchange(held, sibling):
     cut = (held.shape[1] - TAIL) // 2 + TAIL
     chunks = slice(0, cut), slice(cut, None)
     first = [swap_first(held[1::2, rows] + sibling[1::2, rows]) for rows in chunks]
-    first[0], later = lax.optimization_barrier((first[0], later))
     second = [
         swap_second(held[2, rows] + sibling[2, rows] + arrived[1])
         for rows, arrived in zip(chunks, first)
     ]
-    return [*first, *second], later
+    return [*first, *second]
 
 
 def gather_half(top, low):
@@ -421,6 +397,11 @@
     return [jnp.concatenate(block, 0) for block in blocks]
 
 
+def spread(value):
+    corner = swap(value, ACROSS_X | ACROSS_Y)
+    return [value, swap(value, ACROSS_X), swap(value, ACROSS_Y), corner]
+
+
 def over_cen(value, combine, bits=None):
     for bit in range(lax.axis_size("cen").bit_length() - 1) if bits is None else bits:
         value = combine(value, swap(value, 1 << bit, "cen"))
@@ -434,57 +415,60 @@
     )
 
 
-def place_body(info, own, other, last, last_other, fine_out, coarse_out):
-    _, rows, block_width = own.shape
+def place_body(info, *refs, flip):
+    own, other = refs[:3], refs[3:6]
+    fine_out, coarse_out, fine_held, coarse_held, sems = refs[6:]
+    block_width = coarse_out.shape[1] // SLOTS
+    rows = fine_out.shape[0] // 2
+    half = info[1] ^ flip
 
     def column_of(slot, core):
         start = block_of(info, slot, core) * block_width
         return pl.ds(pl.multiple_of(start, block_width), block_width)
 
-    def put(near, far, core):
+    def put(at, near, far, core):
         for slot in range(SLOTS):
-            block = far[slot // 2, :rows, :] if slot % 2 else near[slot // 2]
-            fine_out[:, column_of(slot, core)] = block
-
-    @pl.when(pl.program_id(0) == 0)
-    def _():
-        put(own, last, info[1])
-
-        def part(source, slot, start, size):
-            top = rows + (slot % 2) * (NC + TAIL) + start
-            return source[slot // 2, top : top + size, :]
-
-        weight = part(last, 0, NC, TAIL) + part(last_other, 0, NC, TAIL)
-        weight = as_column(weight[:1, :128], 128)[:NC, :1]
-        for slot, crossed in enumerate((0, 2, 1, 3)):
-            total = part(last, slot, 0, NC) + part(last_other, crossed, 0, NC)
-            coarse_out[:, column_of(slot, info[1])] = total / weight
-
-    @pl.when(pl.program_id(0) == 1)
-    def _():
-        put(other, last_other, 1 - info[1])
-
-
-def place(info, own, other, last, last_other, *, flip):
-    _, rows, block_width = own.shape
+            fine_held[at, :, column_of(slot, core)] = (far if slot % 2 else near)[slot // 2]
+
+    def send(at, half):
+        span = pl.ds(pl.multiple_of(half * rows, rows), rows)
+        return pltpu.make_async_copy(fine_held.at[at], fine_out.at[span], sems.at[at])
+
+    put(0, *own[:2], info[1])
+    send(0, half).start()
+    put(1, *other[:2], 1 - info[1])
+    send(1, 1 - half).start()
+    parts, others = own[2], other[2]
+    weight = parts[0, NC:, :128] + others[0, NC:, :128]
+    weight = as_column(weight[:1], 128)[:NC, :1]
+    for slot in range(SLOTS):
+        total = parts[slot, :NC, :] + others[slot, :NC, :]
+        coarse_held[:, column_of(slot, 0)] = total / weight
+    send_coarse = pltpu.make_async_copy(coarse_held, coarse_out, sems.at[2])
+    send_coarse.start()
+    send(0, half).wait()
+    send(1, 1 - half).wait()
+    send_coarse.wait()
+
+
+def place(info, own, other, *, flip):
+    _, rows, block_width = own[0].shape
     width = SLOTS * block_width
-    args = [own, other, last, last_other]
+    args = [near_by(value) for value in (*own, *other)]
     return pl.pallas_call(
-        place_body,
+        functools.partial(place_body, flip=flip),
         out_shape=[
             jax.ShapeDtypeStruct((2 * rows, width), jnp.float32),
             jax.ShapeDtypeStruct((NC, width), jnp.float32),
         ],
-        grid_spec=pltpu.PrefetchScalarGridSpec(
-            num_scalar_prefetch=1,
-            grid=(2,),
-            in_specs=[full(*value.shape) for value in args],
-            out_specs=[
-                pl.BlockSpec((rows, width), lambda i, info: (info[1] ^ flip ^ i, 0)),
-                full(NC, width),
-            ],
-        ),
-        compiler_params=pltpu.CompilerParams(vmem_limit_bytes=24 * 2**20),
+        in_specs=[SCALARS] + [HERE] * len(args),
+        out_specs=[AWAY, AWAY],
+        scratch_shapes=[
+            pltpu.VMEM((2, rows, width), jnp.float32),
+            pltpu.VMEM((NC, width), jnp.float32),
+            pltpu.SemaphoreType.DMA((3,)),
+        ],
+        compiler_params=pltpu.CompilerParams(vmem_limit_bytes=8 * 2**20),
         name="place_blocks",
     )(info, *args)
 
@@ -503,40 +487,41 @@
     sent, seen, squares, kept = call(points, fine_assign, fine_start, None, None, flip=1)
     sibling = swap(sent, CORE)
     held, seen_first = call(kept, fine_assign, fine_start, squares, seen, flip=0)
-    incoming, _ = exchange(held, sibling)
+    incoming = exchange(held, sibling)
     top, low, part = refine_half(
         info, held, sibling, incoming, owners, coarse_start, flip=0
     )
-    part = part + swap(part, CORE)
     own = jnp.stack(gather_half(top, low))
-    bits = range(lax.axis_size("cen").bit_length() - 1)
     folded = jnp.concatenate([part, seen_first.reshape(-1, block_width)], 0)
-    folded = over_cen(folded, fold, bits[:1])
-    own, folded = lax.optimization_barrier((own, folded))
+    paired = swap(folded, 1, "cen")
     other = swap(own, CORE)
 
     call = functools.partial(run_pass, info, pass_index=1, rows=rows)
     sent, seen, kept = call(points, fine_assign, own, squares, None, flip=0)
+    sent, paired = lax.optimization_barrier((sent, paired))
     sibling = swap(sent, CORE)
+    folded = fold(folded, paired)
+    paired = [swap(folded, bit, "cen") for bit in (2,) if bit < lax.axis_size("cen")]
     held, seen_second = call(kept, fine_assign, other, squares, seen, flip=1)
-    incoming, folded = exchange(held, sibling, folded)
-
-    folded = over_cen(folded, fold, bits[1:])
+    held, paired = lax.optimization_barrier((held, paired))
+    incoming = exchange(held, sibling)
+    folded = functools.reduce(fold, paired, folded)
+    folded = over_cen(folded, fold, range(2, lax.axis_size("cen").bit_length() - 1))
     part, seen_first = folded[: NC + TAIL], folded[NC + TAIL :]
+    part = part + swap(part, CORE)
     coarse = part[:NC] / part[NC, :NC][:, None]
 
     top, low, part = refine_half(info, held, sibling, incoming, owners, coarse, flip=1)
     fine = jnp.concatenate([top, low], 0)
+    over_first, over_second = lax.optimization_barrier((swap_first(fine), swap_second(fine)))
+    near = jnp.stack([fine, over_second])
+    far = jnp.stack([over_first, swap_first(over_second)])
     folded = jnp.concatenate([part, seen_second.reshape(-1, block_width)], 0)
-    folded = over_cen(folded, fold, bits[:1])
-    over_second, folded = lax.optimization_barrier((swap_second(fine), folded))
-    near = jnp.stack([fine, over_second])
-    far = swap_first(near)
-    folded = over_cen(folded, fold, bits[1:])
+    folded = over_cen(folded, fold)
     part, seen_second = folded[: NC + TAIL], folded[NC + TAIL :]
-    parts = jnp.stack([part, swap_second(part)])
-    last = jnp.concatenate([far, parts, swap_first(parts)], 1)
-    fine_now, coarse_now = place(info, near, swap(near, CORE), last, swap(last, CORE), flip=1)
+    parts = jnp.stack(spread(part))
+    blocks = [near, far, parts]
+    fine_now, coarse_now = place(info, blocks, [swap(block, CORE) for block in blocks], flip=1)
 
     seen = [each.reshape(2, -1) for each in (seen_first, seen_second)]
     gaps = jnp.stack([each[0] - each[1] for each in seen]) / math.sqrt(width)

time: 121 us -> 120 us (level)
  starting transfers between devices: 33.9 us -> 32.2 us
    ppermute x6 -> x5, waiting for transfers between devices: 11.2 us -> 7.59 us  [swap_second(): return lax.ppermute(value, 'pts', pairs)]
    ppermute x6 -> x5, starting transfers between devices: 11 us -> 7.55 us  [swap_second(): return lax.ppermute(value, 'pts', pairs)]
    ppermute x16 -> x20, waiting for transfers between devices: 13.2 us -> 16.4 us  [swap(): return lax.ppermute(value, axis, [(i, i ^ bit) for i in range(size)])]
    ppermute x16 -> x20, starting transfers between devices: 16.4 us -> 18.1 us  [swap(): return lax.ppermute(value, axis, [(i, i ^ bit) for i in range(size)])]
  transfers between devices with their start and end apart: 28 -> 31, of which waited for: 17 -> 14; matrix products, arithmetic and copies ran while one was open for 2% -> 2% of each run, Pallas kernels for 22% -> 22%
where the time goes in v11:
time: 120 us
  Pallas kernels  43.1 us (36%)
  waiting for transfers between devices  40.8 us (34%)
  starting transfers between devices  32.2 us (27%)
  other arithmetic  2.34 us (2%)
    pallas_call x4, Pallas kernels, run_pass(): pl.pallas_call(body, out_shape=out_shape, in_specs=[SCALARS, *in_specs],...  38 us
    ppermute x20, starting transfers between devices, swap(): return lax.ppermute(value, axis, [(i, i ^ bit) for i in range(size)])  18.1 us
    ppermute x6, waiting for transfers between devices, swap_first(): return lax.ppermute(value, 'pts', pairs)  16.8 us
    ppermute x20, waiting for transfers between devices, swap(): return lax.ppermute(value, axis, [(i, i ^ bit) for i in range(size)])  16.4 us
    ppermute x5, waiting for transfers between devices, swap_second(): return lax.ppermute(value, 'pts', pairs)  7.59 us
    ppermute x5, starting transfers between devices, swap_second(): return lax.ppermute(value, 'pts', pairs)  7.55 us
    ppermute x6, starting transfers between devices, swap_first(): return lax.ppermute(value, 'pts', pairs)  6.51 us
    pallas_call x2, Pallas kernels, refine_half(): pl.pallas_call(functools.partial(refine_body, flip=flip), out_shape=[pltp...  3.01 us
  transfers between devices with their start and end apart: 31, of which 14 were waited for; matrix products, arithmetic and copies ran while one was open for 2% of the time, Pallas kernels for 22%

profile of v11, /device:TPU:0, one launch (start us, length us, event | category | flops | bytes accessed | tf_op | source)
XLA Modules:
  0.0 119.8 jit_solution(2784261814799255018)
XLA Ops:
  0.6 0.1 pad_add_fusion.info
  0.7 11.6 %energies_and_sums_00.1 = (f32[4,264,256]{2,1,0:T(8,128)S(1)}, f32[2,4096]{1,0:T(2,128)S(1)}, f32[1,4096]{1,0:T(1,128)S(1)}, bf16[4096,1024]{1,0:T(8,128)(2,1)S(1)}) custom-call(s32[4]{0:T(128)S(1)} %pad_add_fusion.info, bf16[4096,1024]{1,0:T(8,128)(2,1)} %points.3, s32[2,4096]{1,0:T(2,128)} %assign.7, f32[512,1024]{1,0:T(8,128)} %fine.3), custom_call_target="tpu_custom_call" | custom-call | flops 4294967296 | bytes 8388608 | tf_op jit(solution)/shard_map/energies_and_sums_00/pallas_call | solution.py:306
  12.3 0.8 collective-permute-start
  13.1 8.3 %energies_and_sums_01.1 = (f32[4,264,256]{2,1,0:T(8,128)S(1)}, f32[2,4096]{1,0:T(2,128)S(1)}) custom-call(s32[4]{0:T(128)S(1)} %pad_add_fusion.info, bf16[4096,1024]{1,0:T(8,128)(2,1)S(1)} %get-tuple-element.28.points, s32[2,4096]{1,0:T(2,128)S(1)} %copy-done.3, f32[512,1024]{1,0:T(8,128)S(1)} %copy-done.2, f32[1,4096]{1,0:T(1,128)S(1)} %get-tuple-element.29.refs_0_, ...), custom_call_target="tpu_custom_call" | custom-call | flops 4294967296 | bytes 8388608 | tf_op jit(solution)/shard_map/energies_and_sums_01/pallas_call | solution.py:306
  21.4 0.0 collective-permute-done.sibling
  21.5 0.0 copy-start
  21.5 0.0 copy-start.1
  21.5 2.4 %collective-permute-start.1 = (f32[2,136,256]{2,1,0:T(8,128)S(1)}, f32[2,136,256]{2,1,0:T(8,128)S(1)}, u32[]{:S(2)}, u32[]{:S(2)}) collective-permute-start(f32[2,136,256]{2,1,0:T(8,128)S(1)} %slice_add_fusion.1), channel_id=1, source_target_pairs={{0,8},{4,20},{8,0},{12,28},{16,24},{20,4},{24,16},{28,12},{1,9},{5... | collective-permute-start | bytes 835592 | tf_op jit(solution)/shard_map/ppermute | solution.py:94
  23.9 0.1 collective-permute-start.2
  24.0 4.4 %collective-permute-done.1.refs_0_ = f32[2,136,256]{2,1,0:T(8,128)S(1)} collective-permute-done((f32[2,136,256]{2,1,0:T(8,128)S(1)}, f32[2,136,256]{2,1,0:T(8,128)S(1)}, u32[]{:S(2)}, u32[]{:S(2)}) %collective-permute-start.1) | collective-permute-done | bytes 278560 | tf_op jit(solution)/shard_map/ppermute | solution.py:94
  28.4 2.1 %collective-permute-start.3 = (f32[136,256]{1,0:T(8,128)S(1)}, f32[136,256]{1,0:T(8,128)S(1)}, u32[]{:S(2)}, u32[]{:S(2)}) collective-permute-start(f32[136,256]{1,0:T(8,128)S(1)} %fusion.1), channel_id=1, source_target_pairs={{0,16},{4,12},{8,24},{12,4},{16,0},{20,28},{24,8},{28,20},{1,17},{... | collective-permute-start | bytes 417800 | tf_op jit(solution)/shard_map/ppermute | solution.py:99
  30.5 0.8 collective-permute-done.2.refs_1_
  31.4 2.4 %collective-permute-start.4 = (f32[128,256]{1,0:T(8,128)S(1)}, f32[128,256]{1,0:T(8,128)S(1)}, u32[]{:S(2)}, u32[]{:S(2)}) collective-permute-start(f32[128,256]{1,0:T(8,128)S(1)} %fusion.3), channel_id=1, source_target_pairs={{0,16},{4,12},{8,24},{12,4},{16,0},{20,28},{24,8},{28,20},{1,17},{... | collective-permute-start | bytes 393224 | tf_op jit(solution)/shard_map/ppermute | solution.py:99
  33.8 2.9 %collective-permute-done.4.refs_3_ = f32[128,256]{1,0:T(8,128)S(1)} collective-permute-done((f32[128,256]{1,0:T(8,128)S(1)}, f32[128,256]{1,0:T(8,128)S(1)}, u32[]{:S(2)}, u32[]{:S(2)}) %collective-permute-start.4) | collective-permute-done | bytes 131104 | tf_op jit(solution)/shard_map/ppermute | solution.py:99
  36.8 1.5 %refine_half.2 = (f32[128,256]{1,0:T(8,128)S(1)}, f32[128,256]{1,0:T(8,128)S(1)}, f32[72,256]{1,0:T(8,128)S(1)}) custom-call(s32[4]{0:T(128)S(1)} %pad_add_fusion.info, f32[4,264,256]{2,1,0:T(8,128)S(1)} %get-tuple-element.31.own, f32[4,264,256]{2,1,0:T(8,128)S(1)} %collective-permute-done.sibling, f32[2,136,256]{2,1,0:T(8,128)S(1)} %collective-permute-done.1.refs_0_, ...), custom_call_target="tpu_custom_call" | custom-call | tf_op jit(solution)/shard_map/refine_half/pallas_call | solution.py:368
  38.3 2.0 %collective-permute-start.6 = (f32[128,256]{1,0:T(8,128)S(1)}, f32[128,256]{1,0:T(8,128)S(1)}, u32[]{:S(2)}, u32[]{:S(2)}) collective-permute-start(f32[128,256]{1,0:T(8,128)S(1)} %get-tuple-element.34), channel_id=1, source_target_pairs={{0,8},{4,12},{8,0},{12,4},{16,24},{20,28},{24,16},{28,20},{1,9},{5... | collective-permute-start | bytes 393224 | tf_op jit(solution)/shard_map/ppermute | solution.py:89
  40.3 1.5 %collective-permute-start.7 = (f32[128,256]{1,0:T(8,128)S(1)}, f32[128,256]{1,0:T(8,128)S(1)}, u32[]{:S(2)}, u32[]{:S(2)}) collective-permute-start(f32[128,256]{1,0:T(8,128)S(1)} %get-tuple-element.33), channel_id=1, source_target_pairs={{0,16},{4,20},{8,24},{12,28},{16,0},{20,4},{24,8},{28,12},{1,17},{... | collective-permute-start | bytes 393224 | tf_op jit(solution)/shard_map/ppermute | solution.py:89
  41.8 0.5 collective-permute-start.8
  42.4 0.1 collective-permute-start.5
  42.5 1.9 %collective-permute-done.6 = f32[128,256]{1,0:T(8,128)S(1)} collective-permute-done((f32[128,256]{1,0:T(8,128)S(1)}, f32[128,256]{1,0:T(8,128)S(1)}, u32[]{:S(2)}, u32[]{:S(2)}) %collective-permute-start.6) | collective-permute-done | bytes 131104 | tf_op jit(solution)/shard_map/ppermute | solution.py:89
  44.4 2.3 %collective-permute-start.10 = (f32[128,256]{1,0:T(8,128)S(1)}, f32[128,256]{1,0:T(8,128)S(1)}, u32[]{:S(2)}, u32[]{:S(2)}) collective-permute-start(f32[128,256]{1,0:T(8,128)S(1)} %collective-permute-done.6), channel_id=1, source_target_pairs={{0,16},{4,20},{8,24},{12,28},{16,0},{20,4},{24,8},{28,12},{1,17},{... | collective-permute-start | bytes 393224 | tf_op jit(solution)/shard_map/ppermute | solution.py:89
  46.7 0.0 collective-permute-done.7
  46.7 0.8 collective-permute-start.9
  47.5 0.0 collective-permute-done.8
  47.6 0.0 collective-permute-done.5
  47.6 2.0 %collective-permute-done.10 = f32[128,256]{1,0:T(8,128)S(1)} collective-permute-done((f32[128,256]{1,0:T(8,128)S(1)}, f32[128,256]{1,0:T(8,128)S(1)}, u32[]{:S(2)}, u32[]{:S(2)}) %collective-permute-start.10) | collective-permute-done | bytes 131104 | tf_op jit(solution)/shard_map/ppermute | solution.py:89
  49.6 2.0 %collective-permute-done.9 = f32[128,256]{1,0:T(8,128)S(1)} collective-permute-done((f32[128,256]{1,0:T(8,128)S(1)}, f32[128,256]{1,0:T(8,128)S(1)}, u32[]{:S(2)}, u32[]{:S(2)}) %collective-permute-start.9) | collective-permute-done | bytes 131104 | tf_op jit(solution)/shard_map/ppermute | solution.py:89
  51.7 0.1 pad_maximum_fusion.fine
  51.8 0.1 collective-permute-start.11
  51.9 0.0 copy-start.4
  51.9 1.6 %collective-permute-start.12 = (f32[104,256]{1,0:T(8,128)S(1)}, f32[104,256]{1,0:T(8,128)S(1)}, u32[]{:S(2)}, u32[]{:S(2)}) collective-permute-start(f32[104,256]{1,0:T(8,128)S(1)} %pad_maximum_fusion.4), channel_id=1, source_target_pairs={{0,1},{1,0},{2,3},{3,2},{4,5},{5,4},{6,7},{7,6},{8,9},{9,8},{10,11... | collective-permute-start | bytes 319496 | tf_op jit(solution)/shard_map/ppermute | solution.py:89
  53.5 9.8 %energies_and_sums_10.1 = (f32[4,264,256]{2,1,0:T(8,128)S(1)}, f32[2,4096]{1,0:T(2,128)S(1)}, bf16[4096,1024]{1,0:T(8,128)(2,1)S(1)}) custom-call(s32[4]{0:T(128)S(1)} %pad_add_fusion.info, bf16[4096,1024]{1,0:T(8,128)(2,1)} %points.3, s32[2,4096]{1,0:T(2,128)} %assign.7, f32[4,256,256]{2,1,0:T(8,128)S(1)} %pad_maximum_fusion.fine, ...), custom_call_target="tpu_custom_call" | custom-call | flops 4294967296 | bytes 8388608 | tf_op jit(solution)/shard_map/energies_and_sums_10/pallas_call | solution.py:306
  63.3 0.0 collective-permute-done.12
  63.4 2.7 %collective-permute-start.13 = (f32[104,256]{1,0:T(8,128)S(1)}, f32[104,256]{1,0:T(8,128)S(1)}, u32[]{:S(2)}, u32[]{:S(2)}) collective-permute-start(f32[104,256]{1,0:T(8,128)S(1)} %pad_maximum_fusion.5), channel_id=1, source_target_pairs={{0,2},{1,3},{2,0},{3,1},{4,6},{5,7},{6,4},{7,5},{8,10},{9,11},{10,... | collective-permute-start | bytes 319496 | tf_op jit(solution)/shard_map/ppermute | solution.py:89
  66.1 8.3 %energies_and_sums_11.1 = (f32[4,264,256]{2,1,0:T(8,128)S(1)}, f32[2,4096]{1,0:T(2,128)S(1)}) custom-call(s32[4]{0:T(128)S(1)} %pad_add_fusion.info, bf16[4096,1024]{1,0:T(8,128)(2,1)S(1)} %get-tuple-element.35.points, s32[2,4096]{1,0:T(2,128)S(1)} %copy-done.4, f32[4,256,256]{2,1,0:T(8,128)S(1)} %collective-permute-done.11.fine, ...), custom_call_target="tpu_custom_call" | custom-call | flops 4294967296 | bytes 8388608 | tf_op jit(solution)/shard_map/energies_and_sums_11/pallas_call | solution.py:306
  74.4 0.6 collective-permute-start.19
  75.2 0.8 collective-permute-start.16
  76.0 1.3 %collective-permute-start.15 = (f32[2,136,256]{2,1,0:T(8,128)S(1)}, f32[2,136,256]{2,1,0:T(8,128)S(1)}, u32[]{:S(2)}, u32[]{:S(2)}) collective-permute-start(f32[2,136,256]{2,1,0:T(8,128)S(1)} %slice_add_fusion), channel_id=1, source_target_pairs={{0,8},{4,20},{8,0},{12,28},{16,24},{20,4},{24,16},{28,12},{1,9},{5... | collective-permute-start | bytes 835592 | tf_op jit(solution)/shard_map/ppermute | solution.py:94
  77.4 0.9 add.89
  78.3 3.3 %collective-permute-done.16.refs_1_ = f32[2,128,256]{2,1,0:T(8,128)S(1)} collective-permute-done((f32[2,128,256]{2,1,0:T(8,128)S(1)}, f32[2,128,256]{2,1,0:T(8,128)S(1)}, u32[]{:S(2)}, u32[]{:S(2)}) %collective-permute-start.16) | collective-permute-done | bytes 262176 | tf_op jit(solution)/shard_map/ppermute | solution.py:94
  81.6 1.0 collective-permute-start.18
  82.6 3.0 %collective-permute-done.15.refs_0_ = f32[2,136,256]{2,1,0:T(8,128)S(1)} collective-permute-done((f32[2,136,256]{2,1,0:T(8,128)S(1)}, f32[2,136,256]{2,1,0:T(8,128)S(1)}, u32[]{:S(2)}, u32[]{:S(2)}) %collective-permute-start.15) | collective-permute-done | bytes 278560 | tf_op jit(solution)/shard_map/ppermute | solution.py:94
  85.7 1.0 collective-permute-start.17
  86.7 0.1 slice_divide_fusion.refs_5_
  86.8 4.0 %collective-permute-done.17.refs_2_ = f32[136,256]{1,0:T(8,128)S(1)} collective-permute-done((f32[136,256]{1,0:T(8,128)S(1)}, f32[136,256]{1,0:T(8,128)S(1)}, u32[]{:S(2)}, u32[]{:S(2)}) %collective-permute-start.17) | collective-permute-done | bytes 139296 | tf_op jit(solution)/shard_map/ppermute | solution.py:99
  90.8 1.5 %refine_half.3 = (f32[128,256]{1,0:T(8,128)S(1)}, f32[128,256]{1,0:T(8,128)S(1)}, f32[72,256]{1,0:T(8,128)S(1)}) custom-call(s32[4]{0:T(128)S(1)} %pad_add_fusion.info, f32[4,264,256]{2,1,0:T(8,128)S(1)} %get-tuple-element.42.own, f32[4,264,256]{2,1,0:T(8,128)S(1)} %collective-permute-done.14.sibling, f32[2,136,256]{2,1,0:T(8,128)S(1)} %collective-permute-done.15.refs_0_, ...), custom_call_target="tpu_custom_call" | custom-call | tf_op jit(solution)/shard_map/refine_half/pallas_call | solution.py:368
  92.3 0.5 collective-permute-start.23
  92.8 4.8 %collective-permute-done.23 = f32[104,256]{1,0:T(8,128)S(1)} collective-permute-done((f32[104,256]{1,0:T(8,128)S(1)}, f32[104,256]{1,0:T(8,128)S(1)}, u32[]{:S(2)}, u32[]{:S(2)}) %collective-permute-start.23) | collective-permute-done | bytes 106528 | tf_op jit(solution)/shard_map/ppermute | solution.py:89
  97.7 0.4 collective-permute-start.24
  98.0 0.9 collective-permute-start.20
  98.9 1.0 collective-permute-start.21
  99.9 4.6 %collective-permute-done.24 = f32[104,256]{1,0:T(8,128)S(1)} collective-permute-done((f32[104,256]{1,0:T(8,128)S(1)}, f32[104,256]{1,0:T(8,128)S(1)}, u32[]{:S(2)}, u32[]{:S(2)}) %collective-permute-start.24) | collective-permute-done | bytes 106528 | tf_op jit(solution)/shard_map/ppermute | solution.py:89
  104.5 1.3 %collective-permute-start.27 = (f32[72,256]{1,0:T(8,128)S(1)}, f32[72,256]{1,0:T(8,128)S(1)}, u32[]{:S(2)}, u32[]{:S(2)}) collective-permute-start(f32[72,256]{1,0:T(8,128)S(1)} %slice_add_fusion.12), channel_id=1, source_target_pairs={{0,24},{4,28},{8,16},{12,20},{16,8},{20,12},{24,0},{28,4},{1,25},{... | collective-permute-start | bytes 221192 | tf_op jit(solution)/shard_map/ppermute | solution.py:89
  105.8 1.0 collective-permute-start.26
  106.8 1.2 %collective-permute-start.25 = (f32[72,256]{1,0:T(8,128)S(1)}, f32[72,256]{1,0:T(8,128)S(1)}, u32[]{:S(2)}, u32[]{:S(2)}) collective-permute-start(f32[72,256]{1,0:T(8,128)S(1)} %slice_add_fusion.12), channel_id=1, source_target_pairs={{0,8},{4,12},{8,0},{12,4},{16,24},{20,28},{24,16},{28,20},{1,9},{5... | collective-permute-start | bytes 221192 | tf_op jit(solution)/shard_map/ppermute | solution.py:89
  108.0 0.6 collective-permute-done.21
  108.7 1.0 collective-permute-start.22
  109.7 0.1 collective-permute-start.28
  109.8 5.2 %collective-permute-done.22 = f32[256,256]{1,0:T(8,128)S(1)} collective-permute-done((f32[256,256]{1,0:T(8,128)S(1)}, f32[256,256]{1,0:T(8,128)S(1)}, u32[]{:S(2)}, u32[]{:S(2)}) %collective-permute-start.22) | collective-permute-done | bytes 262176 | tf_op jit(solution)/shard_map/ppermute | solution.py:94
  115.1 0.1 collective-permute-start.29
  115.2 0.5 collective-permute-start.30
  115.8 0.6 maximum_multiply_fusion
  116.4 1.1 collective-permute-done.30.refs_5_
  117.5 2.1 %place_blocks.1 = (f32[512,1024]{1,0:T(8,128)}, f32[64,1024]{1,0:T(8,128)}) custom-call(s32[4]{0:T(128)S(1)} %pad_add_fusion.info, f32[2,256,256]{2,1,0:T(8,128)S(1)} %pad_maximum_fusion.1.refs_0_, f32[2,256,256]{2,1,0:T(8,128)S(1)} %pad_maximum_fusion.2.refs_1_, f32[4,72,256]{2,1,0:T(8,128)S(1)} %pad_maximum_fusion.3.refs_2_, ...), custom_call_target="tpu_custom_call" | custom-call | tf_op jit(solution)/shard_map/place_blocks/pallas_call | solution.py:458
  (56 shorter events, 0.7 us)
Async XLA Ops:
  0.7 12.4 %copy-start.2 = (f32[512,1024]{1,0:T(8,128)S(1)}, f32[512,1024]{1,0:T(8,128)}, u32[]{:S(2)}) copy-start(f32[512,1024]{1,0:T(8,128)} %fine.3) | copy-start | bytes 6291460
  0.7 12.4 %copy-start.3 = (s32[2,4096]{1,0:T(2,128)S(1)}, s32[2,4096]{1,0:T(2,128)}, u32[]{:S(2)}) copy-start(s32[2,4096]{1,0:T(2,128)} %assign.7) | copy-start | bytes 98308
  12.3 9.1 %collective-permute-start = (f32[4,264,256]{2,1,0:T(8,128)S(1)}, f32[4,264,256]{2,1,0:T(8,128)S(1)}, u32[]{:S(2)}, u32[]{:S(2)}) collective-permute-start(f32[4,264,256]{2,1,0:T(8,128)S(1)} %get-tuple-element.32), channel_id=1, source_target_pairs={{0,4},{4,0},{8,12},{12,8},{16,20},{20,16},{24,28},{28,24},{1,5},{5... | collective-permute-start | bytes 3244040 | tf_op jit(solution)/shard_map/ppermute | solution.py:89
  21.5 15.3 %copy-start = (f32[64,1024]{1,0:T(8,128)S(1)}, f32[64,1024]{1,0:T(8,128)}, u32[]{:S(2)}) copy-start(f32[64,1024]{1,0:T(8,128)} %refs_5_.1) | copy-start | bytes 786436
  21.5 15.3 %copy-start.1 = (s32[512]{0:T(512)S(1)}, s32[512]{0:T(512)}, u32[]{:S(2)}) copy-start(s32[512]{0:T(512)} %param.9) | copy-start | bytes 6148
  21.5 6.9 %collective-permute-start.1 = (f32[2,136,256]{2,1,0:T(8,128)S(1)}, f32[2,136,256]{2,1,0:T(8,128)S(1)}, u32[]{:S(2)}, u32[]{:S(2)}) collective-permute-start(f32[2,136,256]{2,1,0:T(8,128)S(1)} %slice_add_fusion.1), channel_id=1, source_target_pairs={{0,8},{4,20},{8,0},{12,28},{16,24},{20,4},{24,16},{28,12},{1,9},{5... | collective-permute-start | bytes 835592 | tf_op jit(solution)/shard_map/ppermute | solution.py:94
  23.9 7.5 %collective-permute-start.2 = (f32[2,128,256]{2,1,0:T(8,128)S(1)}, f32[2,128,256]{2,1,0:T(8,128)S(1)}, u32[]{:S(2)}, u32[]{:S(2)}) collective-permute-start(f32[2,128,256]{2,1,0:T(8,128)S(1)} %slice_add_fusion.3), channel_id=1, source_target_pairs={{0,8},{4,20},{8,0},{12,28},{16,24},{20,4},{24,16},{28,12},{1,9},{5... | collective-permute-start | bytes 786440 | tf_op jit(solution)/shard_map/ppermute | solution.py:94
  28.4 8.3 %collective-permute-start.3 = (f32[136,256]{1,0:T(8,128)S(1)}, f32[136,256]{1,0:T(8,128)S(1)}, u32[]{:S(2)}, u32[]{:S(2)}) collective-permute-start(f32[136,256]{1,0:T(8,128)S(1)} %fusion.1), channel_id=1, source_target_pairs={{0,16},{4,12},{8,24},{12,4},{16,0},{20,28},{24,8},{28,20},{1,17},{... | collective-permute-start | bytes 417800 | tf_op jit(solution)/shard_map/ppermute | solution.py:99
  31.4 5.4 %collective-permute-start.4 = (f32[128,256]{1,0:T(8,128)S(1)}, f32[128,256]{1,0:T(8,128)S(1)}, u32[]{:S(2)}, u32[]{:S(2)}) collective-permute-start(f32[128,256]{1,0:T(8,128)S(1)} %fusion.3), channel_id=1, source_target_pairs={{0,16},{4,12},{8,24},{12,4},{16,0},{20,28},{24,8},{28,20},{1,17},{... | collective-permute-start | bytes 393224 | tf_op jit(solution)/shard_map/ppermute | solution.py:99
  38.3 6.1 %collective-permute-start.6 = (f32[128,256]{1,0:T(8,128)S(1)}, f32[128,256]{1,0:T(8,128)S(1)}, u32[]{:S(2)}, u32[]{:S(2)}) collective-permute-start(f32[128,256]{1,0:T(8,128)S(1)} %get-tuple-element.34), channel_id=1, source_target_pairs={{0,8},{4,12},{8,0},{12,4},{16,24},{20,28},{24,16},{28,20},{1,9},{5... | collective-permute-start | bytes 393224 | tf_op jit(solution)/shard_map/ppermute | solution.py:89
  40.3 6.4 %collective-permute-start.7 = (f32[128,256]{1,0:T(8,128)S(1)}, f32[128,256]{1,0:T(8,128)S(1)}, u32[]{:S(2)}, u32[]{:S(2)}) collective-permute-start(f32[128,256]{1,0:T(8,128)S(1)} %get-tuple-element.33), channel_id=1, source_target_pairs={{0,16},{4,20},{8,24},{12,28},{16,0},{20,4},{24,8},{28,12},{1,17},{... | collective-permute-start | bytes 393224 | tf_op jit(solution)/shard_map/ppermute | solution.py:89
  41.8 5.7 %collective-permute-start.8 = (f32[128,256]{1,0:T(8,128)S(1)}, f32[128,256]{1,0:T(8,128)S(1)}, u32[]{:S(2)}, u32[]{:S(2)}) collective-permute-start(f32[128,256]{1,0:T(8,128)S(1)} %get-tuple-element.34), channel_id=1, source_target_pairs={{0,16},{4,20},{8,24},{12,28},{16,0},{20,4},{24,8},{28,12},{1,17},{... | collective-permute-start | bytes 393224 | tf_op jit(solution)/shard_map/ppermute | solution.py:89
  42.4 5.2 %collective-permute-start.5 = (f32[128,256]{1,0:T(8,128)S(1)}, f32[128,256]{1,0:T(8,128)S(1)}, u32[]{:S(2)}, u32[]{:S(2)}) collective-permute-start(f32[128,256]{1,0:T(8,128)S(1)} %get-tuple-element.33), channel_id=1, source_target_pairs={{0,8},{4,12},{8,0},{12,4},{16,24},{20,28},{24,16},{28,20},{1,9},{5... | collective-permute-start | bytes 393224 | tf_op jit(solution)/shard_map/ppermute | solution.py:89
  44.4 5.2 %collective-permute-start.10 = (f32[128,256]{1,0:T(8,128)S(1)}, f32[128,256]{1,0:T(8,128)S(1)}, u32[]{:S(2)}, u32[]{:S(2)}) collective-permute-start(f32[128,256]{1,0:T(8,128)S(1)} %collective-permute-done.6), channel_id=1, source_target_pairs={{0,16},{4,20},{8,24},{12,28},{16,0},{20,4},{24,8},{28,12},{1,17},{... | collective-permute-start | bytes 393224 | tf_op jit(solution)/shard_map/ppermute | solution.py:89
  46.7 5.0 %collective-permute-start.9 = (f32[128,256]{1,0:T(8,128)S(1)}, f32[128,256]{1,0:T(8,128)S(1)}, u32[]{:S(2)}, u32[]{:S(2)}) collective-permute-start(f32[128,256]{1,0:T(8,128)S(1)} %collective-permute-done.7), channel_id=1, source_target_pairs={{0,8},{4,12},{8,0},{12,4},{16,24},{20,28},{24,16},{28,20},{1,9},{5... | collective-permute-start | bytes 393224 | tf_op jit(solution)/shard_map/ppermute | solution.py:89
  51.8 14.3 %collective-permute-start.11 = (f32[4,256,256]{2,1,0:T(8,128)S(1)}, f32[4,256,256]{2,1,0:T(8,128)S(1)}, u32[]{:S(2)}, u32[]{:S(2)}) collective-permute-start(f32[4,256,256]{2,1,0:T(8,128)S(1)} %pad_maximum_fusion.fine), channel_id=1, source_target_pairs={{0,4},{4,0},{8,12},{12,8},{16,20},{20,16},{24,28},{28,24},{1,5},{5... | collective-permute-start | bytes 3145736 | tf_op jit(solution)/shard_map/ppermute | solution.py:89
  51.9 14.2 %copy-start.4 = (s32[2,4096]{1,0:T(2,128)S(1)}, s32[2,4096]{1,0:T(2,128)}, u32[]{:S(2)}) copy-start(s32[2,4096]{1,0:T(2,128)} %assign.7) | copy-start | bytes 98308
  51.9 11.4 %collective-permute-start.12 = (f32[104,256]{1,0:T(8,128)S(1)}, f32[104,256]{1,0:T(8,128)S(1)}, u32[]{:S(2)}, u32[]{:S(2)}) collective-permute-start(f32[104,256]{1,0:T(8,128)S(1)} %pad_maximum_fusion.4), channel_id=1, source_target_pairs={{0,1},{1,0},{2,3},{3,2},{4,5},{5,4},{6,7},{7,6},{8,9},{9,8},{10,11... | collective-permute-start | bytes 319496 | tf_op jit(solution)/shard_map/ppermute | solution.py:89
  63.4 11.1 %collective-permute-start.13 = (f32[104,256]{1,0:T(8,128)S(1)}, f32[104,256]{1,0:T(8,128)S(1)}, u32[]{:S(2)}, u32[]{:S(2)}) collective-permute-start(f32[104,256]{1,0:T(8,128)S(1)} %pad_maximum_fusion.5), channel_id=1, source_target_pairs={{0,2},{1,3},{2,0},{3,1},{4,6},{5,7},{6,4},{7,5},{8,10},{9,11},{10,... | collective-permute-start | bytes 319496 | tf_op jit(solution)/shard_map/ppermute | solution.py:89
  66.1 9.0 %collective-permute-start.14 = (f32[4,264,256]{2,1,0:T(8,128)S(1)}, f32[4,264,256]{2,1,0:T(8,128)S(1)}, u32[]{:S(2)}, u32[]{:S(2)}) collective-permute-start(f32[4,264,256]{2,1,0:T(8,128)S(1)} %get-tuple-element.43), channel_id=1, source_target_pairs={{0,4},{4,0},{8,12},{12,8},{16,20},{20,16},{24,28},{28,24},{1,5},{5... | collective-permute-start | bytes 3244040 | tf_op jit(solution)/shard_map/ppermute | solution.py:89
  74.4 2.9 %collective-permute-start.19 = (f32[72,256]{1,0:T(8,128)S(1)}, f32[72,256]{1,0:T(8,128)}, u32[]{:S(2)}, u32[]{:S(2)}) collective-permute-start(f32[72,256]{1,0:T(8,128)S(1)} %slice_add_fusion.14), channel_id=1, source_target_pairs={{0,4},{4,0},{8,12},{12,8},{16,20},{20,16},{24,28},{28,24},{1,5},{5... | collective-permute-start | bytes 221192 | tf_op jit(solution)/shard_map/ppermute | solution.py:89
  75.2 6.4 %collective-permute-start.16 = (f32[2,128,256]{2,1,0:T(8,128)S(1)}, f32[2,128,256]{2,1,0:T(8,128)S(1)}, u32[]{:S(2)}, u32[]{:S(2)}) collective-permute-start(f32[2,128,256]{2,1,0:T(8,128)S(1)} %slice_add_fusion.2), channel_id=1, source_target_pairs={{0,8},{4,20},{8,0},{12,28},{16,24},{20,4},{24,16},{28,12},{1,9},{5... | collective-permute-start | bytes 786440 | tf_op jit(solution)/shard_map/ppermute | solution.py:94
  76.0 9.6 %collective-permute-start.15 = (f32[2,136,256]{2,1,0:T(8,128)S(1)}, f32[2,136,256]{2,1,0:T(8,128)S(1)}, u32[]{:S(2)}, u32[]{:S(2)}) collective-permute-start(f32[2,136,256]{2,1,0:T(8,128)S(1)} %slice_add_fusion), channel_id=1, source_target_pairs={{0,8},{4,20},{8,0},{12,28},{16,24},{20,4},{24,16},{28,12},{1,9},{5... | collective-permute-start | bytes 835592 | tf_op jit(solution)/shard_map/ppermute | solution.py:94
  81.6 5.2 %collective-permute-start.18 = (f32[128,256]{1,0:T(8,128)S(1)}, f32[128,256]{1,0:T(8,128)S(1)}, u32[]{:S(2)}, u32[]{:S(2)}) collective-permute-start(f32[128,256]{1,0:T(8,128)S(1)} %fusion.2), channel_id=1, source_target_pairs={{0,16},{4,12},{8,24},{12,4},{16,0},{20,28},{24,8},{28,20},{1,17},{... | collective-permute-start | bytes 393224 | tf_op jit(solution)/shard_map/ppermute | solution.py:99
  85.7 5.1 %collective-permute-start.17 = (f32[136,256]{1,0:T(8,128)S(1)}, f32[136,256]{1,0:T(8,128)S(1)}, u32[]{:S(2)}, u32[]{:S(2)}) collective-permute-start(f32[136,256]{1,0:T(8,128)S(1)} %fusion), channel_id=1, source_target_pairs={{0,16},{4,12},{8,24},{12,4},{16,0},{20,28},{24,8},{28,20},{1,17},{... | collective-permute-start | bytes 417800 | tf_op jit(solution)/shard_map/ppermute | solution.py:99
  92.3 5.3 %collective-permute-start.23 = (f32[104,256]{1,0:T(8,128)S(1)}, f32[104,256]{1,0:T(8,128)S(1)}, u32[]{:S(2)}, u32[]{:S(2)}) collective-permute-start(f32[104,256]{1,0:T(8,128)S(1)} %pad_maximum_fusion.6), channel_id=1, source_target_pairs={{0,1},{1,0},{2,3},{3,2},{4,5},{5,4},{6,7},{7,6},{8,9},{9,8},{10,11... | collective-permute-start | bytes 319496 | tf_op jit(solution)/shard_map/ppermute | solution.py:89
  97.7 6.8 %collective-permute-start.24 = (f32[104,256]{1,0:T(8,128)S(1)}, f32[104,256]{1,0:T(8,128)S(1)}, u32[]{:S(2)}, u32[]{:S(2)}) collective-permute-start(f32[104,256]{1,0:T(8,128)S(1)} %pad_maximum_fusion.7), channel_id=1, source_target_pairs={{0,2},{1,3},{2,0},{3,1},{4,6},{5,7},{6,4},{7,5},{8,10},{9,11},{10,... | collective-permute-start | bytes 319496 | tf_op jit(solution)/shard_map/ppermute | solution.py:89
  98.0 10.0 %collective-permute-start.20 = (f32[256,256]{1,0:T(8,128)S(1)}, f32[256,256]{1,0:T(8,128)S(1)}, u32[]{:S(2)}, u32[]{:S(2)}) collective-permute-start(f32[256,256]{1,0:T(8,128)S(1)} %constant_dynamic-update-slice_fusion), channel_id=1, source_target_pairs={{0,8},{4,20},{8,0},{12,28},{16,24},{20,4},{24,16},{28,12},{1,9},{5... | collective-permute-start | bytes 786440 | tf_op jit(solution)/shard_map/ppermute | solution.py:94
  98.9 9.8 %collective-permute-start.21 = (f32[256,256]{1,0:T(8,128)S(1)}, f32[256,256]{1,0:T(8,128)S(1)}, u32[]{:S(2)}, u32[]{:S(2)}) collective-permute-start(f32[256,256]{1,0:T(8,128)S(1)} %constant_dynamic-update-slice_fusion), channel_id=1, source_target_pairs={{0,16},{4,12},{8,24},{12,4},{16,0},{20,28},{24,8},{28,20},{1,17},{... | collective-permute-start | bytes 786440 | tf_op jit(solution)/shard_map/ppermute | solution.py:99
  104.5 10.7 %collective-permute-start.27 = (f32[72,256]{1,0:T(8,128)S(1)}, f32[72,256]{1,0:T(8,128)S(1)}, u32[]{:S(2)}, u32[]{:S(2)}) collective-permute-start(f32[72,256]{1,0:T(8,128)S(1)} %slice_add_fusion.12), channel_id=1, source_target_pairs={{0,24},{4,28},{8,16},{12,20},{16,8},{20,12},{24,0},{28,4},{1,25},{... | collective-permute-start | bytes 221192 | tf_op jit(solution)/shard_map/ppermute | solution.py:89
  105.8 9.4 %collective-permute-start.26 = (f32[72,256]{1,0:T(8,128)S(1)}, f32[72,256]{1,0:T(8,128)S(1)}, u32[]{:S(2)}, u32[]{:S(2)}) collective-permute-start(f32[72,256]{1,0:T(8,128)S(1)} %slice_add_fusion.12), channel_id=1, source_target_pairs={{0,16},{4,20},{8,24},{12,28},{16,0},{20,4},{24,8},{28,12},{1,17},{... | collective-permute-start | bytes 221192 | tf_op jit(solution)/shard_map/ppermute | solution.py:89
  106.8 8.4 %collective-permute-start.25 = (f32[72,256]{1,0:T(8,128)S(1)}, f32[72,256]{1,0:T(8,128)S(1)}, u32[]{:S(2)}, u32[]{:S(2)}) collective-permute-start(f32[72,256]{1,0:T(8,128)S(1)} %slice_add_fusion.12), channel_id=1, source_target_pairs={{0,8},{4,12},{8,0},{12,4},{16,24},{20,28},{24,16},{28,20},{1,9},{5... | collective-permute-start | bytes 221192 | tf_op jit(solution)/shard_map/ppermute | solution.py:89
  108.7 6.4 %collective-permute-start.22 = (f32[256,256]{1,0:T(8,128)S(1)}, f32[256,256]{1,0:T(8,128)S(1)}, u32[]{:S(2)}, u32[]{:S(2)}) collective-permute-start(f32[256,256]{1,0:T(8,128)S(1)} %collective-permute-done.21), channel_id=1, source_target_pairs={{0,8},{4,20},{8,0},{12,28},{16,24},{20,4},{24,16},{28,12},{1,9},{5... | collective-permute-start | bytes 786440 | tf_op jit(solution)/shard_map/ppermute | solution.py:94
  109.7 7.7 %collective-permute-start.28 = (f32[2,256,256]{2,1,0:T(8,128)S(1)}, f32[2,256,256]{2,1,0:T(8,128)S(1)}, u32[]{:S(2)}, u32[]{:S(2)}) collective-permute-start(f32[2,256,256]{2,1,0:T(8,128)S(1)} %pad_maximum_fusion.1.refs_0_), channel_id=1, source_target_pairs={{0,4},{4,0},{8,12},{12,8},{16,20},{20,16},{24,28},{28,24},{1,5},{5... | collective-permute-start | bytes 1572872 | tf_op jit(solution)/shard_map/ppermute | solution.py:89
  115.1 2.4 %collective-permute-start.29 = (f32[2,256,256]{2,1,0:T(8,128)S(1)}, f32[2,256,256]{2,1,0:T(8,128)S(1)}, u32[]{:S(2)}, u32[]{:S(2)}) collective-permute-start(f32[2,256,256]{2,1,0:T(8,128)S(1)} %pad_maximum_fusion.2.refs_1_), channel_id=1, source_target_pairs={{0,4},{4,0},{8,12},{12,8},{16,20},{20,16},{24,28},{28,24},{1,5},{5... | collective-permute-start | bytes 1572872 | tf_op jit(solution)/shard_map/ppermute | solution.py:89
  115.2 2.3 %collective-permute-start.30 = (f32[4,72,256]{2,1,0:T(8,128)S(1)}, f32[4,72,256]{2,1,0:T(8,128)S(1)}, u32[]{:S(2)}, u32[]{:S(2)}) collective-permute-start(f32[4,72,256]{2,1,0:T(8,128)S(1)} %pad_maximum_fusion.3.refs_2_), channel_id=1, source_target_pairs={{0,4},{4,0},{8,12},{12,8},{16,20},{20,16},{24,28},{28,24},{1,5},{5... | collective-permute-start | bytes 884744 | tf_op jit(solution)/shard_map/ppermute | solution.py:89

commit v12 on v11

--- a/solution.py
+++ b/solution.py
@@ -121,65 +121,65 @@
     return jnp.broadcast_to(row, (128, rows)).T
 
 
-def pass_body(info, points, assign, fine, *refs, pass_index, flip, stream, chained, tile):
+def pass_body(info, points, assign, *refs, pass_index, first, tile):
     refs = list(refs)
-    initial = pass_index == 0
-    first = initial and stream
+    fine = [refs.pop(0) for _ in range(1 if first else 6)]
     squares_in = None if first else refs.pop(0)
-    seen_in = refs.pop(0) if chained else None
-    payload, seen = refs.pop(0), refs.pop(0)
+    held, sent_near, sent_far, seen = refs[:4]
+    refs = refs[4:]
     squares_out = refs.pop(0) if first else None
-    kept = refs.pop(0) if stream else points
-    low, norms, tallies, sums, even, odd, scaled = refs[:7]
-    chosen_in = refs[7] if stream else assign
-    small_sems, point_sems = refs[8:10] if stream else (None, None)
-    start = refs[10] if first else None
+    kept, low, norms, tallies, sums, even, odd, scaled, chosen_in, small_sems, point_sems = refs[:11]
+    start = refs[11] if first else None
     rows, width = low.shape
-    mid = rows // 2
+    half_rows = rows // 2
+    mid = half_rows // 2
     block_width = width // SLOTS
-    half = info[1] ^ flip
-    base = info[2] + half * rows
+    core = info[1]
     tiles = points.shape[0] // tile
+    halves = [slice(0, half_rows), slice(half_rows, rows)]
+    bases = [info[2] + half * half_rows for half in (core, 1 - core)]
 
     def span(i):
         return pl.ds(pl.multiple_of(i * tile, tile), tile)
 
     def column_of(slot, core):
-        start = block_of(info, slot, core) * block_width
-        return pl.ds(pl.multiple_of(start, block_width), block_width)
+        at = block_of(info, slot, core) * block_width
+        return pl.ds(pl.multiple_of(at, block_width), block_width)
 
     def load(i):
         return pltpu.make_async_copy(points.at[span(i)], kept.at[span(i)], point_sems.at[i])
 
+    load_starts = []
     if first:
-        load_start = pltpu.make_async_copy(
-            fine.at[pl.ds(pl.multiple_of(half * rows, rows), rows)], start, small_sems.at[1]
-        )
-        load_start.start()
-    if stream:
-        load(0).start()
-        load_assign = pltpu.make_async_copy(assign, chosen_in, small_sems.at[0])
-        load_assign.start()
-
-        @pl.loop(1, tiles)
-        def _(i):
-            load(i).start()
-
-    if initial:
+        for at, half in enumerate((core, 1 - core)):
+            rows_of = pl.ds(pl.multiple_of(half * half_rows, half_rows), half_rows)
+            load_starts.append(
+                pltpu.make_async_copy(fine[0].at[rows_of], start.at[halves[at]], small_sems.at[at])
+            )
+    for copy in load_starts:
+        copy.start()
+    load(0).start()
+    load_assign = pltpu.make_async_copy(assign, chosen_in, small_sems.at[2])
+    load_assign.start()
+
+    @pl.loop(1, tiles)
+    def _(i):
+        load(i).start()
+
+    for at, part in enumerate(halves):
         if first:
-            load_start.wait()
-            block = start[...]
+            load_starts[at].wait()
+            block = start[part, :]
+            norm = jnp.sum(block * block, axis=1, keepdims=True)
+            low[part, :] = (-2.0 * block).astype(jnp.bfloat16)
         else:
-            block = fine[pl.ds(pl.multiple_of(half * rows, rows), rows), :]
-        norm = jnp.sum(block * block, axis=1, keepdims=True)
-        low[...] = (-2.0 * block).astype(jnp.bfloat16)
-    else:
-        norm = jnp.zeros((rows, 1), jnp.float32)
-        for slot in range(SLOTS):
-            block = fine[slot]
-            norm = norm + jnp.sum(block * block, axis=1, keepdims=True)
-            low[:, column_of(slot, 0)] = (-2.0 * block).astype(jnp.bfloat16)
-    norms[...] = jnp.broadcast_to(norm, norms.shape)
+            near, sides, corner = fine[3 * at : 3 * at + 3]
+            norm = jnp.zeros((half_rows, 1), jnp.float32)
+            for slot in range(SLOTS):
+                block = (near, sides.at[0], sides.at[1], corner)[slot][...]
+                norm = norm + jnp.sum(block * block, axis=1, keepdims=True)
+                low[part, column_of(slot, 0)] = (-2.0 * block).astype(jnp.bfloat16)
+        norms[part, :] = jnp.broadcast_to(norm, (half_rows, 128))
     tallies[...] = jnp.zeros_like(tallies)
     sums[...] = jnp.zeros_like(sums)
 
@@ -189,17 +189,17 @@
         )
 
     def collect(i, products):
-        energy = products[...] + jnp.concatenate([norms[...]] * (tile // 128), axis=1)
-        chosen = chosen_in[pass_index : pass_index + 1, span(i)] - base
-        member = lax.broadcasted_iota(jnp.int32, energy.shape, 0) == chosen
-        picked = jnp.sum(jnp.where(member, energy, 0.0), axis=0, keepdims=True)
-        nearest = jnp.min(energy, axis=0, keepdims=True)
-        inside = (chosen >= 0) & (chosen < rows)
-        picked_seen = jnp.where(inside, picked, FAR)
-        if chained:
-            picked_seen = jnp.minimum(picked_seen, seen_in[0:1, span(i)])
-            nearest = jnp.minimum(nearest, seen_in[1:2, span(i)])
-        seen[0:1, span(i)] = picked_seen
+        everyone = chosen_in[pass_index : pass_index + 1, span(i)]
+        members, picked, nearest, inside = [], 0.0, FAR, False
+        for part, base in zip(halves, bases):
+            energy = products[part, :] + jnp.concatenate([norms[part, :]] * (tile // 128), axis=1)
+            chosen = everyone - base
+            member = lax.broadcasted_iota(jnp.int32, energy.shape, 0) == chosen
+            members.append(member)
+            picked = picked + jnp.sum(jnp.where(member, energy, 0.0), axis=0, keepdims=True)
+            nearest = jnp.minimum(nearest, jnp.min(energy, axis=0, keepdims=True))
+            inside = inside | ((chosen >= 0) & (chosen < half_rows))
+        seen[0:1, span(i)] = jnp.where(inside, picked, FAR)
         seen[1:2, span(i)] = nearest
         if first:
             folded = jnp.zeros((tile, 128), jnp.float32)
@@ -211,73 +211,68 @@
         else:
             squares = squares_in[0:1, span(i)]
         weights = 1.0 / (1.0 + (squares + picked) / width)
-        weighted = jnp.where(member, weights, 0.0)
-        tally = tallies[...]
-        for lane in range(0, tile, 128):
-            tally = tally + weighted[:, lane : lane + 128]
-        tallies[...] = tally
+        for part, member in zip(halves, members):
+            weighted = jnp.where(member, weights, 0.0)
+            tally = tallies[part, :]
+            for lane in range(0, tile, 128):
+                tally = tally + weighted[:, lane : lane + 128]
+            tallies[part, :] = tally
         factor = as_column(weights, tile)
         for lane in range(0, width, 128):
             values = kept[span(i), lane : lane + 128].astype(jnp.float32)
             scaled[:, lane : lane + 128] = (values * factor).astype(jnp.bfloat16)
+        member = jnp.concatenate([each.astype(jnp.float32) for each in members], 0)
         sums[...] += jnp.dot(
-            member.astype(jnp.float32).astype(jnp.bfloat16),
-            scaled[...],
-            preferred_element_type=jnp.float32,
+            member.astype(jnp.bfloat16), scaled[...], preferred_element_type=jnp.float32
         )
 
-    if stream:
-        load_assign.wait()
-        load(0).wait()
+    load_assign.wait()
+    load(0).wait()
     multiply(0, even)
 
     @pl.loop(0, tiles // 2 - 1)
     def _(pair):
         i = 2 * pair
-        if stream:
-            load(i + 1).wait()
-            load(i + 2).wait()
+        load(i + 1).wait()
+        load(i + 2).wait()
         multiply(i + 1, odd)
         collect(i, even)
         multiply(i + 2, even)
         collect(i + 1, odd)
 
-    if stream:
-        load(tiles - 1).wait()
+    load(tiles - 1).wait()
     multiply(tiles - 1, odd)
     collect(tiles - 2, even)
     collect(tiles - 1, odd)
 
-    counts = jnp.broadcast_to(jnp.sum(tallies[...].T, axis=0, keepdims=True), (TAIL, rows))
-    for slot in range(SLOTS):
-        columns = column_of(slot, info[1] ^ (not chained))
-        payload[slot, :mid, :] = sums[:mid, columns]
-        payload[slot, mid : mid + TAIL, :] = counts
-        payload[slot, mid + TAIL :, :] = sums[mid:, columns]
-
-
-def run_pass(info, points, fine_assign, fine, squares, seen, *, pass_index, flip, rows):
+    for at, part in enumerate(halves):
+        counts = jnp.sum(tallies[part, :].T, axis=0, keepdims=True)
+        counts = jnp.broadcast_to(counts, (TAIL, half_rows))
+        for slot in range(SLOTS):
+            columns = column_of(slot, core ^ at)
+            target = held.at[slot] if at == 0 else sent_far.at[slot - 1] if slot else sent_near
+            target[:mid, :] = sums[part, columns][:mid]
+            target[mid : mid + TAIL, :] = counts
+            target[mid + TAIL :, :] = sums[part, columns][mid:]
+
+
+def run_pass(info, points, fine_assign, fine, squares, *, pass_index, rows):
     count, width = points.shape
-    block_width = width // SLOTS
+    half_rows = rows // 2
+    block = (half_rows + TAIL, width // SLOTS)
     tile = 512
-    initial = pass_index == 0
-    chained = seen is not None
-    stream = not chained
-    if stream:
-        in_specs = [AWAY, AWAY, AWAY if initial else HERE]
-        args = [far_off(points), far_off(fine_assign), far_off(fine) if initial else near_by(fine)]
+    first = squares is None
+    args = [far_off(points), far_off(fine_assign)]
+    in_specs = [AWAY, AWAY]
+    if first:
+        args.append(far_off(fine))
+        in_specs.append(AWAY)
     else:
-        in_specs = [HERE] * 3
-        args = [near_by(points), near_by(fine_assign), near_by(fine)]
-    for value in (squares, seen):
-        if value is not None:
-            in_specs.append(HERE)
-            args.append(near_by(value))
-    shapes = [(SLOTS, rows + TAIL, block_width), (2, count)]
-    if squares is None:
-        shapes.append((1, count))
-    out_shape = [pltpu.VMEM(shape, jnp.float32) for shape in shapes]
+        args += [near_by(value) for value in (*fine, squares)]
+        in_specs += [HERE] * (len(fine) + 1)
+    shapes = [(SLOTS, *block), block, (SLOTS - 1, *block), (2, count)]
     scratch = [
+        pltpu.VMEM((count, width), jnp.bfloat16),
         pltpu.VMEM((rows, width), jnp.bfloat16),
         pltpu.VMEM((rows, 128), jnp.float32),
         pltpu.VMEM((rows, 128), jnp.float32),
@@ -285,50 +280,39 @@
         pltpu.VMEM((rows, tile), jnp.float32),
         pltpu.VMEM((rows, tile), jnp.float32),
         pltpu.VMEM((tile, width), jnp.bfloat16),
+        pltpu.VMEM((PASSES, count), jnp.int32),
+        pltpu.SemaphoreType.DMA((3,)),
+        pltpu.SemaphoreType.DMA((count // tile,)),
     ]
-    if stream:
-        scratch += [
-            pltpu.VMEM((PASSES, count), jnp.int32),
-            pltpu.SemaphoreType.DMA((2,)),
-            pltpu.SemaphoreType.DMA((count // tile,)),
-        ]
-        if initial:
-            scratch.append(pltpu.VMEM((rows, width), jnp.float32))
-        out_shape.append(pltpu.VMEM(points.shape, points.dtype))
-    body = functools.partial(
-        pass_body,
-        pass_index=pass_index,
-        flip=flip,
-        stream=stream,
-        chained=chained,
-        tile=tile,
-    )
+    if first:
+        shapes.append((1, count))
+        scratch.append(pltpu.VMEM((rows, width), jnp.float32))
     return pl.pallas_call(
-        body,
-        out_shape=out_shape,
+        functools.partial(pass_body, pass_index=pass_index, first=first, tile=tile),
+        out_shape=[pltpu.VMEM(shape, jnp.float32) for shape in shapes],
         in_specs=[SCALARS, *in_specs],
-        out_specs=[HERE] * len(out_shape),
+        out_specs=[HERE] * len(shapes),
         scratch_shapes=scratch,
-        compiler_params=pltpu.CompilerParams(vmem_limit_bytes=16 * 2**20),
+        compiler_params=pltpu.CompilerParams(vmem_limit_bytes=28 * 2**20),
         cost_estimate=pl.CostEstimate(
             flops=4 * rows * count * width, bytes_accessed=2 * count * width, transcendentals=0
         ),
-        name=f"energies_and_sums_{pass_index}{int(chained)}",
+        name=f"energies_and_sums_{pass_index}",
     )(info, *args)
 
 
-def refine_body(info, own, sibling, *refs, flip):
+def refine_body(info, own, sibling, *refs):
     first_top, first_low, second_top, second_low, owners, coarse_in, top, low, part = refs
     rows = owners.shape[2]
     mid = rows // 2
     block_width = part.shape[1]
-    owner = owners[info[1] ^ flip]
+    owner = owners[info[1]]
     if coarse_in.shape[1] == block_width:
         coarse = coarse_in[...]
     else:
         coarse = coarse_in[:, pl.ds(pl.multiple_of(info[0] * block_width, block_width), block_width)]
-    head = own[0, : mid + TAIL, :] + sibling[0, : mid + TAIL, :]
-    rest = own[0, mid + TAIL :, :] + sibling[0, mid + TAIL :, :]
+    head = own[0, : mid + TAIL, :] + sibling[: mid + TAIL, :]
+    rest = own[0, mid + TAIL :, :] + sibling[mid + TAIL :, :]
     head = head + (first_top[0] + second_top[...])
     rest = rest + (first_low[0] + second_low[...])
     totals, counts_row = jnp.concatenate([head[:mid], rest], 0), head[mid:]
@@ -360,13 +344,13 @@
     )
 
 
-def refine_half(info, own, sibling, incoming, owners, coarse, *, flip):
+def refine_half(info, own, sibling, incoming, owners, coarse):
     _, rows, block_width = own.shape
     mid = (rows - TAIL) // 2
     args = [near_by(value) for value in (own, sibling, *incoming, owners, coarse)]
     shapes = [(mid, block_width), (mid, block_width), (NC + TAIL, block_width)]
     return pl.pallas_call(
-        functools.partial(refine_body, flip=flip),
+        refine_body,
         out_shape=[pltpu.VMEM(shape, jnp.float32) for shape in shapes],
         in_specs=[SCALARS] + [HERE] * len(args),
         out_specs=[HERE] * len(shapes),
@@ -378,9 +362,9 @@
 def exchange(held, sibling):
     cut = (held.shape[1] - TAIL) // 2 + TAIL
     chunks = slice(0, cut), slice(cut, None)
-    first = [swap_first(held[1::2, rows] + sibling[1::2, rows]) for rows in chunks]
+    first = [swap_first(held[1::2, rows] + sibling[::2, rows]) for rows in chunks]
     second = [
-        swap_second(held[2, rows] + sibling[2, rows] + arrived[1])
+        swap_second(held[2, rows] + sibling[1, rows] + arrived[1])
         for rows, arrived in zip(chunks, first)
     ]
     return [*first, *second]
@@ -393,8 +377,10 @@
     y_low = swap(low, ACROSS_Y)
     corner_top = swap(y_top, ACROSS_X)
     corner_low = swap(x_low, ACROSS_Y)
-    blocks = [(top, low), (x_top, x_low), (y_top, y_low), (corner_top, corner_low)]
-    return [jnp.concatenate(block, 0) for block in blocks]
+    near = jnp.concatenate([top, low], 0)
+    sides = jnp.stack([jnp.concatenate(pair, 0) for pair in ((x_top, x_low), (y_top, y_low))])
+    own = [near, sides, jnp.concatenate([corner_top, corner_low], 0)]
+    return [*own, *[swap(block, CORE) for block in own]]
 
 
 def spread(value):
@@ -415,12 +401,12 @@
     )
 
 
-def place_body(info, *refs, flip):
+def place_body(info, *refs):
     own, other = refs[:3], refs[3:6]
     fine_out, coarse_out, fine_held, coarse_held, sems = refs[6:]
     block_width = coarse_out.shape[1] // SLOTS
     rows = fine_out.shape[0] // 2
-    half = info[1] ^ flip
+    half = info[1]
 
     def column_of(slot, core):
         start = block_of(info, slot, core) * block_width
@@ -451,12 +437,12 @@
     send_coarse.wait()
 
 
-def place(info, own, other, *, flip):
+def place(info, own, other):
     _, rows, block_width = own[0].shape
     width = SLOTS * block_width
     args = [near_by(value) for value in (*own, *other)]
     return pl.pallas_call(
-        functools.partial(place_body, flip=flip),
+        place_body,
         out_shape=[
             jax.ShapeDtypeStruct((2 * rows, width), jnp.float32),
             jax.ShapeDtypeStruct((NC, width), jnp.float32),
@@ -483,35 +469,29 @@
     info = jnp.stack([me >> 1, core, cen * local_count, cen * 2 + core]).astype(jnp.int32)
     owners = coarse_assign.reshape(2, 1, rows)
 
-    call = functools.partial(run_pass, info, pass_index=0, rows=rows)
-    sent, seen, squares, kept = call(points, fine_assign, fine_start, None, None, flip=1)
-    sibling = swap(sent, CORE)
-    held, seen_first = call(kept, fine_assign, fine_start, squares, seen, flip=0)
-    incoming = exchange(held, sibling)
-    top, low, part = refine_half(
-        info, held, sibling, incoming, owners, coarse_start, flip=0
-    )
-    own = jnp.stack(gather_half(top, low))
+    held, sent_near, sent_far, seen_first, squares = run_pass(
+        info, points, fine_assign, fine_start, None, pass_index=0, rows=local_count
+    )
+    sibling_far, sibling_near = swap(sent_far, CORE), swap(sent_near, CORE)
+    incoming = exchange(held, sibling_far)
+    top, low, part = refine_half(info, held, sibling_near, incoming, owners, coarse_start)
+    blocks = gather_half(top, low)
     folded = jnp.concatenate([part, seen_first.reshape(-1, block_width)], 0)
     paired = swap(folded, 1, "cen")
-    other = swap(own, CORE)
-
-    call = functools.partial(run_pass, info, pass_index=1, rows=rows)
-    sent, seen, kept = call(points, fine_assign, own, squares, None, flip=0)
-    sent, paired = lax.optimization_barrier((sent, paired))
-    sibling = swap(sent, CORE)
-    folded = fold(folded, paired)
-    paired = [swap(folded, bit, "cen") for bit in (2,) if bit < lax.axis_size("cen")]
-    held, seen_second = call(kept, fine_assign, other, squares, seen, flip=1)
-    held, paired = lax.optimization_barrier((held, paired))
-    incoming = exchange(held, sibling)
-    folded = functools.reduce(fold, paired, folded)
-    folded = over_cen(folded, fold, range(2, lax.axis_size("cen").bit_length() - 1))
+
+    held, sent_near, sent_far, seen_second = run_pass(
+        info, points, fine_assign, blocks, squares, pass_index=1, rows=local_count
+    )
+    sent_far, paired = lax.optimization_barrier((sent_far, paired))
+    sibling_far, sibling_near = swap(sent_far, CORE), swap(sent_near, CORE)
+    incoming = exchange(held, sibling_far)
+    bits = range(1, lax.axis_size("cen").bit_length() - 1)
+    folded = over_cen(fold(folded, paired), fold, bits)
     part, seen_first = folded[: NC + TAIL], folded[NC + TAIL :]
     part = part + swap(part, CORE)
     coarse = part[:NC] / part[NC, :NC][:, None]
 
-    top, low, part = refine_half(info, held, sibling, incoming, owners, coarse, flip=1)
+    top, low, part = refine_half(info, held, sibling_near, incoming, owners, coarse)
     fine = jnp.concatenate([top, low], 0)
     over_first, over_second = lax.optimization_barrier((swap_first(fine), swap_second(fine)))
     near = jnp.stack([fine, over_second])
@@ -521,7 +501,7 @@
     part, seen_second = folded[: NC + TAIL], folded[NC + TAIL :]
     parts = jnp.stack(spread(part))
     blocks = [near, far, parts]
-    fine_now, coarse_now = place(info, blocks, [swap(block, CORE) for block in blocks], flip=1)
+    fine_now, coarse_now = place(info, blocks, [swap(block, CORE) for block in blocks])
 
     seen = [each.reshape(2, -1) for each in (seen_first, seen_second)]
     gaps = jnp.stack([each[0] - each[1] for each in seen]) / math.sqrt(width)

time: 120 us -> 130 us (1.083)
  waiting for transfers between devices: 40.8 us -> 47 us
  Pallas kernels: 43.1 us -> 37.4 us
  starting transfers between devices: 32.2 us -> 37.8 us
  local copies, waits for them, and re-layouts: 0.15 us -> 5.32 us
    ppermute x20 -> x24, waiting for transfers between devices: 16.4 us -> 23.2 us  [swap(): return lax.ppermute(value, axis, [(i, i ^ bit) for i in range(size)])]
    pallas_call x7 -> x5, Pallas kernels: 43.1 us -> 37.4 us  [the longest x2 32.3 us: run_pass(): pl.pallas_call(functools.partial(pass_body, pass_index=pass_index, first=...]
    unnamed x13 -> x21, local copies, waits for them, and re-layouts: 0.07 us -> 5.23 us
    ppermute x6, starting transfers between devices: 6.51 us -> 8.93 us  [swap_first(): return lax.ppermute(value, 'pts', pairs)]
    ppermute x5, starting transfers between devices: 7.55 us -> 9.29 us  [swap_second(): return lax.ppermute(value, 'pts', pairs)]
    ppermute x20 -> x24, starting transfers between devices: 18.1 us -> 19.6 us  [swap(): return lax.ppermute(value, axis, [(i, i ^ bit) for i in range(size)])]
  transfers between devices with their start and end apart: 31 -> 35, of which waited for: 14 -> 18; matrix products, arithmetic and copies ran while one was open for 2% -> 1% of each run, Pallas kernels for 22% -> 12%
where the time goes in v12:
time: 130 us
  waiting for transfers between devices  47 us (36%)
  starting transfers between devices  37.8 us (29%)
  Pallas kernels  37.4 us (29%)
  local copies, waits for them, and re-layouts  5.32 us (4%)
  other arithmetic  1.37 us (1%)
    pallas_call x2, Pallas kernels, run_pass(): pl.pallas_call(functools.partial(pass_body, pass_index=pass_index, first=...  32.3 us
    ppermute x24, waiting for transfers between devices, swap(): return lax.ppermute(value, axis, [(i, i ^ bit) for i in range(size)])  23.2 us
    ppermute x24, starting transfers between devices, swap(): return lax.ppermute(value, axis, [(i, i ^ bit) for i in range(size)])  19.6 us
    ppermute x6, waiting for transfers between devices, swap_first(): return lax.ppermute(value, 'pts', pairs)  16.2 us
    ppermute x5, starting transfers between devices, swap_second(): return lax.ppermute(value, 'pts', pairs)  9.29 us
    ppermute x6, starting transfers between devices, swap_first(): return lax.ppermute(value, 'pts', pairs)  8.93 us
    ppermute x5, waiting for transfers between devices, swap_second(): return lax.ppermute(value, 'pts', pairs)  7.6 us
    unnamed x21, local copies, waits for them, and re-layouts  5.23 us
  transfers between devices with their start and end apart: 35, of which 18 were waited for; matrix products, arithmetic and copies ran while one was open for 1% of the time, Pallas kernels for 12%

profile of v12, /device:TPU:0, one launch (start us, length us, event | category | flops | bytes accessed | tf_op | source)
XLA Modules:
  0.0 130.1 jit_solution(15984214318339105767)
XLA Ops:
  0.6 0.1 pad_add_fusion.info
  0.7 16.9 %energies_and_sums_0.1 = (f32[4,264,256]{2,1,0:T(8,128)S(1)}, f32[264,256]{1,0:T(8,128)S(1)}, f32[3,264,256]{2,1,0:T(8,128)S(1)}, f32[2,4096]{1,0:T(2,128)S(1)}, f32[1,4096]{1,0:T(1,128)S(1)}) custom-call(s32[4]{0:T(128)S(1)} %pad_add_fusion.info, bf16[4096,1024]{1,0:T(8,128)(2,1)} %points.3, s32[2,4096]{1,0:T(2,128)} %assign.3, f32[512,1024]{1,0:T(8,128)} %refs_0_.1), custom_call_target="tpu_custom_call" | custom-call | flops 8589934592 | bytes 8388608 | tf_op jit(solution)/shard_map/energies_and_sums_0/pallas_call | solution.py:290
  17.6 0.5 collective-permute-start.1
  18.2 1.9 %collective-permute-done.1 = f32[3,264,256]{2,1,0:T(8,128)S(1)} collective-permute-done((f32[3,264,256]{2,1,0:T(8,128)S(1)}, f32[3,264,256]{2,1,0:T(8,128)S(1)}, u32[]{:S(2)}, u32[]{:S(2)}) %collective-permute-start.1) | collective-permute-done | bytes 811040 | tf_op jit(solution)/shard_map/ppermute | solution.py:89
  20.2 2.9 %collective-permute-start.2 = (f32[2,136,256]{2,1,0:T(8,128)S(1)}, f32[2,136,256]{2,1,0:T(8,128)S(1)}, u32[]{:S(2)}, u32[]{:S(2)}) collective-permute-start(f32[2,136,256]{2,1,0:T(8,128)S(1)} %slice_add_fusion.1), channel_id=1, source_target_pairs={{0,8},{4,20},{8,0},{12,28},{16,24},{20,4},{24,16},{28,12},{1,9},{5... | collective-permute-start | bytes 835592 | tf_op jit(solution)/shard_map/ppermute | solution.py:94
  23.1 0.1 collective-permute-start.3
  23.3 4.3 %collective-permute-done.2.refs_0_ = f32[2,136,256]{2,1,0:T(8,128)S(1)} collective-permute-done((f32[2,136,256]{2,1,0:T(8,128)S(1)}, f32[2,136,256]{2,1,0:T(8,128)S(1)}, u32[]{:S(2)}, u32[]{:S(2)}) %collective-permute-start.2) | collective-permute-done | bytes 278560 | tf_op jit(solution)/shard_map/ppermute | solution.py:94
  27.7 2.1 %collective-permute-start.4 = (f32[136,256]{1,0:T(8,128)S(1)}, f32[136,256]{1,0:T(8,128)S(1)}, u32[]{:S(2)}, u32[]{:S(2)}) collective-permute-start(f32[136,256]{1,0:T(8,128)S(1)} %fusion.1), channel_id=1, source_target_pairs={{0,16},{4,12},{8,24},{12,4},{16,0},{20,28},{24,8},{28,20},{1,17},{... | collective-permute-start | bytes 417800 | tf_op jit(solution)/shard_map/ppermute | solution.py:99
  29.8 1.1 collective-permute-done.3.refs_1_
  30.9 2.4 %collective-permute-start.5 = (f32[128,256]{1,0:T(8,128)S(1)}, f32[128,256]{1,0:T(8,128)S(1)}, u32[]{:S(2)}, u32[]{:S(2)}) collective-permute-start(f32[128,256]{1,0:T(8,128)S(1)} %fusion.3), channel_id=1, source_target_pairs={{0,16},{4,12},{8,24},{12,4},{16,0},{20,28},{24,8},{28,20},{1,17},{... | collective-permute-start | bytes 393224 | tf_op jit(solution)/shard_map/ppermute | solution.py:99
  33.3 2.9 %collective-permute-done.5.refs_3_ = f32[128,256]{1,0:T(8,128)S(1)} collective-permute-done((f32[128,256]{1,0:T(8,128)S(1)}, f32[128,256]{1,0:T(8,128)S(1)}, u32[]{:S(2)}, u32[]{:S(2)}) %collective-permute-start.5) | collective-permute-done | bytes 131104 | tf_op jit(solution)/shard_map/ppermute | solution.py:99
  36.3 1.5 %refine_half.2 = (f32[128,256]{1,0:T(8,128)S(1)}, f32[128,256]{1,0:T(8,128)S(1)}, f32[72,256]{1,0:T(8,128)S(1)}) custom-call(s32[4]{0:T(128)S(1)} %pad_add_fusion.info, f32[4,264,256]{2,1,0:T(8,128)S(1)} %get-tuple-element.24.own, f32[264,256]{1,0:T(8,128)S(1)} %collective-permute-done.sibling, f32[2,136,256]{2,1,0:T(8,128)S(1)} %collective-permute-done.2.refs_0_, ...), custom_call_target="tpu_custom_call" | custom-call | tf_op jit(solution)/shard_map/refine_half/pallas_call | solution.py:352
  37.8 2.0 %collective-permute-start.8 = (f32[128,256]{1,0:T(8,128)S(1)}, f32[128,256]{1,0:T(8,128)S(1)}, u32[]{:S(2)}, u32[]{:S(2)}) collective-permute-start(f32[128,256]{1,0:T(8,128)S(1)} %get-tuple-element.27), channel_id=1, source_target_pairs={{0,16},{4,20},{8,24},{12,28},{16,0},{20,4},{24,8},{28,12},{1,17},{... | collective-permute-start | bytes 393224 | tf_op jit(solution)/shard_map/ppermute | solution.py:89
  39.9 1.9 %collective-permute-start.6 = (f32[128,256]{1,0:T(8,128)S(1)}, f32[128,256]{1,0:T(8,128)S(1)}, u32[]{:S(2)}, u32[]{:S(2)}) collective-permute-start(f32[128,256]{1,0:T(8,128)S(1)} %get-tuple-element.27), channel_id=1, source_target_pairs={{0,8},{4,12},{8,0},{12,4},{16,24},{20,28},{24,16},{28,20},{1,9},{5... | collective-permute-start | bytes 393224 | tf_op jit(solution)/shard_map/ppermute | solution.py:89
  41.9 0.1 collective-permute-start.7
  42.0 0.8 collective-permute-done.8
  42.8 2.0 %collective-permute-start.10 = (f32[128,256]{1,0:T(8,128)S(1)}, f32[128,256]{1,0:T(8,128)S(1)}, u32[]{:S(2)}, u32[]{:S(2)}) collective-permute-start(f32[128,256]{1,0:T(8,128)S(1)} %collective-permute-done.8), channel_id=1, source_target_pairs={{0,8},{4,12},{8,0},{12,4},{16,24},{20,28},{24,16},{28,20},{1,9},{5... | collective-permute-start | bytes 393224 | tf_op jit(solution)/shard_map/ppermute | solution.py:89
  44.8 0.4 collective-permute-done.6
  45.2 1.6 %collective-permute-done.7 = f32[128,256]{1,0:T(8,128)S(1)} collective-permute-done((f32[128,256]{1,0:T(8,128)S(1)}, f32[128,256]{1,0:T(8,128)S(1)}, u32[]{:S(2)}, u32[]{:S(2)}) %collective-permute-start.7) | collective-permute-done | bytes 131104 | tf_op jit(solution)/shard_map/ppermute | solution.py:89
  46.9 0.1 collective-permute-start.13
  47.0 1.6 %collective-permute-start.11 = (f32[128,256]{1,0:T(8,128)S(1)}, f32[128,256]{1,0:T(8,128)S(1)}, u32[]{:S(2)}, u32[]{:S(2)}) collective-permute-start(f32[128,256]{1,0:T(8,128)S(1)} %collective-permute-done.7), channel_id=1, source_target_pairs={{0,16},{4,20},{8,24},{12,28},{16,0},{20,4},{24,8},{28,12},{1,17},{... | collective-permute-start | bytes 393224 | tf_op jit(solution)/shard_map/ppermute | solution.py:89
  48.6 0.2 collective-permute-start.12
  48.8 4.1 %collective-permute-done.11 = f32[128,256]{1,0:T(8,128)S(1)} collective-permute-done((f32[128,256]{1,0:T(8,128)S(1)}, f32[128,256]{1,0:T(8,128)S(1)}, u32[]{:S(2)}, u32[]{:S(2)}) %collective-permute-start.11) | collective-permute-done | bytes 131104 | tf_op jit(solution)/shard_map/ppermute | solution.py:89
  52.9 0.1 collective-permute-start.14
  53.0 1.6 %collective-permute-start.16 = (f32[104,256]{1,0:T(8,128)S(1)}, f32[104,256]{1,0:T(8,128)S(1)}, u32[]{:S(2)}, u32[]{:S(2)}) collective-permute-start(f32[104,256]{1,0:T(8,128)S(1)} %pad_maximum_fusion.4), channel_id=1, source_target_pairs={{0,1},{1,0},{2,3},{3,2},{4,5},{5,4},{6,7},{7,6},{8,9},{9,8},{10,11... | collective-permute-start | bytes 319496 | tf_op jit(solution)/shard_map/ppermute | solution.py:89
  54.7 0.7 copy-done.4
  55.4 0.7 copy-done.6
  56.1 0.8 copy-done.2
  56.9 1.0 copy-done.3
  57.9 0.9 copy-done.5
  58.9 0.9 copy-done.7
  59.8 15.4 %energies_and_sums_1.1 = (f32[4,264,256]{2,1,0:T(8,128)S(1)}, f32[264,256]{1,0:T(8,128)S(1)}, f32[3,264,256]{2,1,0:T(8,128)S(1)}, f32[2,4096]{1,0:T(2,128)S(1)}) custom-call(s32[4]{0:T(128)S(1)} %pad_add_fusion.info, bf16[4096,1024]{1,0:T(8,128)(2,1)} %points.3, s32[2,4096]{1,0:T(2,128)} %assign.3, f32[256,256]{1,0:T(8,128)S(1)} %constant_dynamic-update-slice_fusion.refs_0_, ...), custom_call_target="tpu_custom_call" | custom-call | flops 8589934592 | bytes 8388608 | tf_op jit(solution)/shard_map/energies_and_sums_1/pallas_call | solution.py:290
  75.3 0.3 collective-permute-start.17
  75.6 2.7 %collective-permute-start.22 = (f32[104,256]{1,0:T(8,128)S(1)}, f32[104,256]{1,0:T(8,128)S(1)}, u32[]{:S(2)}, u32[]{:S(2)}) collective-permute-start(f32[104,256]{1,0:T(8,128)S(1)} %pad_maximum_fusion.5), channel_id=1, source_target_pairs={{0,2},{1,3},{2,0},{3,1},{4,6},{5,7},{6,4},{7,5},{8,10},{9,11},{10,... | collective-permute-start | bytes 319496 | tf_op jit(solution)/shard_map/ppermute | solution.py:89
  78.3 0.1 collective-permute-start.15
  78.3 5.6 %collective-permute-done.22 = f32[104,256]{1,0:T(8,128)S(1)} collective-permute-done((f32[104,256]{1,0:T(8,128)S(1)}, f32[104,256]{1,0:T(8,128)S(1)}, u32[]{:S(2)}, u32[]{:S(2)}) %collective-permute-start.22) | collective-permute-done | bytes 106528 | tf_op jit(solution)/shard_map/ppermute | solution.py:89
  84.0 0.1 collective-permute-start.23
  84.1 1.2 collective-permute-done.23
  85.4 1.5 %collective-permute-start.19 = (f32[2,128,256]{2,1,0:T(8,128)S(1)}, f32[2,128,256]{2,1,0:T(8,128)S(1)}, u32[]{:S(2)}, u32[]{:S(2)}) collective-permute-start(f32[2,128,256]{2,1,0:T(8,128)S(1)} %slice_add_fusion.2), channel_id=1, source_target_pairs={{0,8},{4,20},{8,0},{12,28},{16,24},{20,4},{24,16},{28,12},{1,9},{5... | collective-permute-start | bytes 786440 | tf_op jit(solution)/shard_map/ppermute | solution.py:94
  86.9 0.6 collective-permute-start.18
  87.6 4.2 %collective-permute-done.19.refs_1_ = f32[2,128,256]{2,1,0:T(8,128)S(1)} collective-permute-done((f32[2,128,256]{2,1,0:T(8,128)S(1)}, f32[2,128,256]{2,1,0:T(8,128)S(1)}, u32[]{:S(2)}, u32[]{:S(2)}) %collective-permute-start.19) | collective-permute-done | bytes 262176 | tf_op jit(solution)/shard_map/ppermute | solution.py:94
  91.9 1.6 %collective-permute-start.21 = (f32[128,256]{1,0:T(8,128)S(1)}, f32[128,256]{1,0:T(8,128)S(1)}, u32[]{:S(2)}, u32[]{:S(2)}) collective-permute-start(f32[128,256]{1,0:T(8,128)S(1)} %fusion.2), channel_id=1, source_target_pairs={{0,16},{4,12},{8,24},{12,4},{16,0},{20,28},{24,8},{28,20},{1,17},{... | collective-permute-start | bytes 393224 | tf_op jit(solution)/shard_map/ppermute | solution.py:99
  93.4 2.3 %collective-permute-done.18.refs_0_ = f32[2,136,256]{2,1,0:T(8,128)S(1)} collective-permute-done((f32[2,136,256]{2,1,0:T(8,128)S(1)}, f32[2,136,256]{2,1,0:T(8,128)S(1)}, u32[]{:S(2)}, u32[]{:S(2)}) %collective-permute-start.18) | collective-permute-done | bytes 278560 | tf_op jit(solution)/shard_map/ppermute | solution.py:94
  95.8 1.6 %collective-permute-start.20 = (f32[136,256]{1,0:T(8,128)S(1)}, f32[136,256]{1,0:T(8,128)S(1)}, u32[]{:S(2)}, u32[]{:S(2)}) collective-permute-start(f32[136,256]{1,0:T(8,128)S(1)} %fusion), channel_id=1, source_target_pairs={{0,16},{4,12},{8,24},{12,4},{16,0},{20,28},{24,8},{28,20},{1,17},{... | collective-permute-start | bytes 417800 | tf_op jit(solution)/shard_map/ppermute | solution.py:99
  97.4 0.1 slice_divide_fusion.refs_5_
  97.5 3.4 %collective-permute-done.20.refs_2_ = f32[136,256]{1,0:T(8,128)S(1)} collective-permute-done((f32[136,256]{1,0:T(8,128)S(1)}, f32[136,256]{1,0:T(8,128)S(1)}, u32[]{:S(2)}, u32[]{:S(2)}) %collective-permute-start.20) | collective-permute-done | bytes 139296 | tf_op jit(solution)/shard_map/ppermute | solution.py:99
  100.9 1.5 %refine_half.3 = (f32[128,256]{1,0:T(8,128)S(1)}, f32[128,256]{1,0:T(8,128)S(1)}, f32[72,256]{1,0:T(8,128)S(1)}) custom-call(s32[4]{0:T(128)S(1)} %pad_add_fusion.info, f32[4,264,256]{2,1,0:T(8,128)S(1)} %get-tuple-element.30.own, f32[264,256]{1,0:T(8,128)S(1)} %collective-permute-done.15.sibling, f32[2,136,256]{2,1,0:T(8,128)S(1)} %collective-permute-done.18.refs_0_, ...), custom_call_target="tpu_custom_call" | custom-call | tf_op jit(solution)/shard_map/refine_half/pallas_call | solution.py:352
  102.4 0.1 collective-permute-start.27
  102.5 5.1 %collective-permute-done.27 = f32[104,256]{1,0:T(8,128)S(1)} collective-permute-done((f32[104,256]{1,0:T(8,128)S(1)}, f32[104,256]{1,0:T(8,128)S(1)}, u32[]{:S(2)}, u32[]{:S(2)}) %collective-permute-start.27) | collective-permute-done | bytes 106528 | tf_op jit(solution)/shard_map/ppermute | solution.py:89
  107.7 1.9 %collective-permute-start.28 = (f32[104,256]{1,0:T(8,128)S(1)}, f32[104,256]{1,0:T(8,128)S(1)}, u32[]{:S(2)}, u32[]{:S(2)}) collective-permute-start(f32[104,256]{1,0:T(8,128)S(1)} %pad_maximum_fusion.7), channel_id=1, source_target_pairs={{0,2},{1,3},{2,0},{3,1},{4,6},{5,7},{6,4},{7,5},{8,10},{9,11},{10,... | collective-permute-start | bytes 319496 | tf_op jit(solution)/shard_map/ppermute | solution.py:89
  109.5 1.6 %collective-permute-start.25 = (f32[256,256]{1,0:T(8,128)S(1)}, f32[256,256]{1,0:T(8,128)S(1)}, u32[]{:S(2)}, u32[]{:S(2)}) collective-permute-start(f32[256,256]{1,0:T(8,128)S(1)} %constant_dynamic-update-slice_fusion.4), channel_id=1, source_target_pairs={{0,16},{4,12},{8,24},{12,4},{16,0},{20,28},{24,8},{28,20},{1,17},{... | collective-permute-start | bytes 786440 | tf_op jit(solution)/shard_map/ppermute | solution.py:99
  111.1 1.4 %collective-permute-start.24 = (f32[256,256]{1,0:T(8,128)S(1)}, f32[256,256]{1,0:T(8,128)S(1)}, u32[]{:S(2)}, u32[]{:S(2)}) collective-permute-start(f32[256,256]{1,0:T(8,128)S(1)} %constant_dynamic-update-slice_fusion.4), channel_id=1, source_target_pairs={{0,8},{4,20},{8,0},{12,28},{16,24},{20,4},{24,16},{28,12},{1,9},{5... | collective-permute-start | bytes 786440 | tf_op jit(solution)/shard_map/ppermute | solution.py:94
  112.6 1.3 %collective-permute-done.28 = f32[104,256]{1,0:T(8,128)S(1)} collective-permute-done((f32[104,256]{1,0:T(8,128)S(1)}, f32[104,256]{1,0:T(8,128)S(1)}, u32[]{:S(2)}, u32[]{:S(2)}) %collective-permute-start.28) | collective-permute-done | bytes 106528 | tf_op jit(solution)/shard_map/ppermute | solution.py:89
  113.9 2.5 %collective-permute-start.31 = (f32[72,256]{1,0:T(8,128)S(1)}, f32[72,256]{1,0:T(8,128)S(1)}, u32[]{:S(2)}, u32[]{:S(2)}) collective-permute-start(f32[72,256]{1,0:T(8,128)S(1)} %slice_add_fusion.12), channel_id=1, source_target_pairs={{0,24},{4,28},{8,16},{12,20},{16,8},{20,12},{24,0},{28,4},{1,25},{... | collective-permute-start | bytes 221192 | tf_op jit(solution)/shard_map/ppermute | solution.py:89
  116.4 0.5 collective-permute-start.30
  116.9 0.6 collective-permute-start.29
  117.5 1.2 collective-permute-done.25
  118.7 2.3 %collective-permute-start.26 = (f32[256,256]{1,0:T(8,128)S(1)}, f32[256,256]{1,0:T(8,128)S(1)}, u32[]{:S(2)}, u32[]{:S(2)}) collective-permute-start(f32[256,256]{1,0:T(8,128)S(1)} %collective-permute-done.25), channel_id=1, source_target_pairs={{0,8},{4,20},{8,0},{12,28},{16,24},{20,4},{24,16},{28,12},{1,9},{5... | collective-permute-start | bytes 786440 | tf_op jit(solution)/shard_map/ppermute | solution.py:94
  121.1 0.1 collective-permute-start.32
  121.2 4.2 %collective-permute-done.26 = f32[256,256]{1,0:T(8,128)S(1)} collective-permute-done((f32[256,256]{1,0:T(8,128)S(1)}, f32[256,256]{1,0:T(8,128)S(1)}, u32[]{:S(2)}, u32[]{:S(2)}) %collective-permute-start.26) | collective-permute-done | bytes 262176 | tf_op jit(solution)/shard_map/ppermute | solution.py:94
  125.6 0.5 collective-permute-start.34
  126.1 0.6 maximum_multiply_fusion
  126.7 1.1 collective-permute-done.34.refs_5_
  127.8 2.1 %place_blocks.1 = (f32[512,1024]{1,0:T(8,128)}, f32[64,1024]{1,0:T(8,128)}) custom-call(s32[4]{0:T(128)S(1)} %pad_add_fusion.info, f32[2,256,256]{2,1,0:T(8,128)S(1)} %pad_maximum_fusion.1.refs_0_, f32[2,256,256]{2,1,0:T(8,128)S(1)} %pad_maximum_fusion.2.refs_1_, f32[4,72,256]{2,1,0:T(8,128)S(1)} %pad_maximum_fusion.3.refs_2_, ...), custom_call_target="tpu_custom_call" | custom-call | tf_op jit(solution)/shard_map/place_blocks/pallas_call | solution.py:444
  (70 shorter events, 1.0 us)
Async XLA Ops:
  17.6 2.5 %collective-permute-start.1 = (f32[3,264,256]{2,1,0:T(8,128)S(1)}, f32[3,264,256]{2,1,0:T(8,128)S(1)}, u32[]{:S(2)}, u32[]{:S(2)}) collective-permute-start(f32[3,264,256]{2,1,0:T(8,128)S(1)} %get-tuple-element.26), channel_id=1, source_target_pairs={{0,4},{4,0},{8,12},{12,8},{16,20},{20,16},{24,28},{28,24},{1,5},{5... | collective-permute-start | bytes 2433032 | tf_op jit(solution)/shard_map/ppermute | solution.py:89
  20.2 16.1 %copy-start = (f32[64,1024]{1,0:T(8,128)S(1)}, f32[64,1024]{1,0:T(8,128)}, u32[]{:S(2)}) copy-start(f32[64,1024]{1,0:T(8,128)} %refs_5_.1) | copy-start | bytes 786436
  20.2 16.1 %copy-start.1 = (s32[512]{0:T(512)S(1)}, s32[512]{0:T(512)}, u32[]{:S(2)}) copy-start(s32[512]{0:T(512)} %param.9) | copy-start | bytes 6148
  20.2 7.5 %collective-permute-start.2 = (f32[2,136,256]{2,1,0:T(8,128)S(1)}, f32[2,136,256]{2,1,0:T(8,128)S(1)}, u32[]{:S(2)}, u32[]{:S(2)}) collective-permute-start(f32[2,136,256]{2,1,0:T(8,128)S(1)} %slice_add_fusion.1), channel_id=1, source_target_pairs={{0,8},{4,20},{8,0},{12,28},{16,24},{20,4},{24,16},{28,12},{1,9},{5... | collective-permute-start | bytes 835592 | tf_op jit(solution)/shard_map/ppermute | solution.py:94
  23.1 7.8 %collective-permute-start.3 = (f32[2,128,256]{2,1,0:T(8,128)S(1)}, f32[2,128,256]{2,1,0:T(8,128)S(1)}, u32[]{:S(2)}, u32[]{:S(2)}) collective-permute-start(f32[2,128,256]{2,1,0:T(8,128)S(1)} %slice_add_fusion.3), channel_id=1, source_target_pairs={{0,8},{4,20},{8,0},{12,28},{16,24},{20,4},{24,16},{28,12},{1,9},{5... | collective-permute-start | bytes 786440 | tf_op jit(solution)/shard_map/ppermute | solution.py:94
  23.2 10.1 %collective-permute-start = (f32[264,256]{1,0:T(8,128)S(1)}, f32[264,256]{1,0:T(8,128)S(1)}, u32[]{:S(2)}, u32[]{:S(2)}) collective-permute-start(f32[264,256]{1,0:T(8,128)S(1)} %get-tuple-element.25), channel_id=1, source_target_pairs={{0,4},{4,0},{8,12},{12,8},{16,20},{20,16},{24,28},{28,24},{1,5},{5... | collective-permute-start | bytes 811016 | tf_op jit(solution)/shard_map/ppermute | solution.py:89
  27.7 8.6 %collective-permute-start.4 = (f32[136,256]{1,0:T(8,128)S(1)}, f32[136,256]{1,0:T(8,128)S(1)}, u32[]{:S(2)}, u32[]{:S(2)}) collective-permute-start(f32[136,256]{1,0:T(8,128)S(1)} %fusion.1), channel_id=1, source_target_pairs={{0,16},{4,12},{8,24},{12,4},{16,0},{20,28},{24,8},{28,20},{1,17},{... | collective-permute-start | bytes 417800 | tf_op jit(solution)/shard_map/ppermute | solution.py:99
  30.9 5.3 %collective-permute-start.5 = (f32[128,256]{1,0:T(8,128)S(1)}, f32[128,256]{1,0:T(8,128)S(1)}, u32[]{:S(2)}, u32[]{:S(2)}) collective-permute-start(f32[128,256]{1,0:T(8,128)S(1)} %fusion.3), channel_id=1, source_target_pairs={{0,16},{4,12},{8,24},{12,4},{16,0},{20,28},{24,8},{28,20},{1,17},{... | collective-permute-start | bytes 393224 | tf_op jit(solution)/shard_map/ppermute | solution.py:99
  37.8 5.0 %collective-permute-start.8 = (f32[128,256]{1,0:T(8,128)S(1)}, f32[128,256]{1,0:T(8,128)S(1)}, u32[]{:S(2)}, u32[]{:S(2)}) collective-permute-start(f32[128,256]{1,0:T(8,128)S(1)} %get-tuple-element.27), channel_id=1, source_target_pairs={{0,16},{4,20},{8,24},{12,28},{16,0},{20,4},{24,8},{28,12},{1,17},{... | collective-permute-start | bytes 393224 | tf_op jit(solution)/shard_map/ppermute | solution.py:89
  39.8 5.0 %collective-permute-start.9 = (f32[128,256]{1,0:T(8,128)S(1)}, f32[128,256]{1,0:T(8,128)S(1)}, u32[]{:S(2)}, u32[]{:S(2)}) collective-permute-start(f32[128,256]{1,0:T(8,128)S(1)} %get-tuple-element.28), channel_id=1, source_target_pairs={{0,16},{4,20},{8,24},{12,28},{16,0},{20,4},{24,8},{28,12},{1,17},{... | collective-permute-start | bytes 393224 | tf_op jit(solution)/shard_map/ppermute | solution.py:89
  39.9 5.3 %collective-permute-start.6 = (f32[128,256]{1,0:T(8,128)S(1)}, f32[128,256]{1,0:T(8,128)S(1)}, u32[]{:S(2)}, u32[]{:S(2)}) collective-permute-start(f32[128,256]{1,0:T(8,128)S(1)} %get-tuple-element.27), channel_id=1, source_target_pairs={{0,8},{4,12},{8,0},{12,4},{16,24},{20,28},{24,16},{28,20},{1,9},{5... | collective-permute-start | bytes 393224 | tf_op jit(solution)/shard_map/ppermute | solution.py:89
  41.9 5.0 %collective-permute-start.7 = (f32[128,256]{1,0:T(8,128)S(1)}, f32[128,256]{1,0:T(8,128)S(1)}, u32[]{:S(2)}, u32[]{:S(2)}) collective-permute-start(f32[128,256]{1,0:T(8,128)S(1)} %get-tuple-element.28), channel_id=1, source_target_pairs={{0,8},{4,12},{8,0},{12,4},{16,24},{20,28},{24,16},{28,20},{1,9},{5... | collective-permute-start | bytes 393224 | tf_op jit(solution)/shard_map/ppermute | solution.py:89
  42.8 6.0 %collective-permute-start.10 = (f32[128,256]{1,0:T(8,128)S(1)}, f32[128,256]{1,0:T(8,128)S(1)}, u32[]{:S(2)}, u32[]{:S(2)}) collective-permute-start(f32[128,256]{1,0:T(8,128)S(1)} %collective-permute-done.8), channel_id=1, source_target_pairs={{0,8},{4,12},{8,0},{12,4},{16,24},{20,28},{24,16},{28,20},{1,9},{5... | collective-permute-start | bytes 393224 | tf_op jit(solution)/shard_map/ppermute | solution.py:89
  46.9 9.2 %collective-permute-start.13 = (f32[2,256,256]{2,1,0:T(8,128)S(1)}, f32[2,256,256]{2,1,0:T(8,128)S(1)}, u32[]{:S(2)}, u32[]{:S(2)}) collective-permute-start(f32[2,256,256]{2,1,0:T(8,128)S(1)} %pad_maximum_fusion.refs_1_), channel_id=1, source_target_pairs={{0,4},{4,0},{8,12},{12,8},{16,20},{20,16},{24,28},{28,24},{1,5},{5... | collective-permute-start | bytes 1572872 | tf_op jit(solution)/shard_map/ppermute | solution.py:89
  47.0 5.9 %collective-permute-start.11 = (f32[128,256]{1,0:T(8,128)S(1)}, f32[128,256]{1,0:T(8,128)S(1)}, u32[]{:S(2)}, u32[]{:S(2)}) collective-permute-start(f32[128,256]{1,0:T(8,128)S(1)} %collective-permute-done.7), channel_id=1, source_target_pairs={{0,16},{4,20},{8,24},{12,28},{16,0},{20,4},{24,8},{28,12},{1,17},{... | collective-permute-start | bytes 393224 | tf_op jit(solution)/shard_map/ppermute | solution.py:89
  48.6 6.1 %collective-permute-start.12 = (f32[256,256]{1,0:T(8,128)S(1)}, f32[256,256]{1,0:T(8,128)S(1)}, u32[]{:S(2)}, u32[]{:S(2)}) collective-permute-start(f32[256,256]{1,0:T(8,128)S(1)} %constant_dynamic-update-slice_fusion.refs_0_), channel_id=1, source_target_pairs={{0,4},{4,0},{8,12},{12,8},{16,20},{20,16},{24,28},{28,24},{1,5},{5... | collective-permute-start | bytes 786440 | tf_op jit(solution)/shard_map/ppermute | solution.py:89
  52.9 2.5 %collective-permute-start.14 = (f32[256,256]{1,0:T(8,128)S(1)}, f32[256,256]{1,0:T(8,128)S(1)}, u32[]{:S(2)}, u32[]{:S(2)}) collective-permute-start(f32[256,256]{1,0:T(8,128)S(1)} %constant_dynamic-update-slice_fusion.2.refs_2_), channel_id=1, source_target_pairs={{0,4},{4,0},{8,12},{12,8},{16,20},{20,16},{24,28},{28,24},{1,5},{5... | collective-permute-start | bytes 786440 | tf_op jit(solution)/shard_map/ppermute | solution.py:89
  53.0 22.2 %collective-permute-start.16 = (f32[104,256]{1,0:T(8,128)S(1)}, f32[104,256]{1,0:T(8,128)S(1)}, u32[]{:S(2)}, u32[]{:S(2)}) collective-permute-start(f32[104,256]{1,0:T(8,128)S(1)} %pad_maximum_fusion.4), channel_id=1, source_target_pairs={{0,1},{1,0},{2,3},{3,2},{4,5},{5,4},{6,7},{7,6},{8,9},{9,8},{10,11... | collective-permute-start | bytes 319496 | tf_op jit(solution)/shard_map/ppermute | solution.py:89
  54.7 0.7 copy-start.4
  55.4 0.7 copy-start.6
  56.1 0.8 copy-start.2
  56.9 1.0 copy-start.3
  57.9 0.9 copy-start.5
  58.9 0.9 copy-start.7
  75.3 10.1 %collective-permute-start.17 = (f32[3,264,256]{2,1,0:T(8,128)S(1)}, f32[3,264,256]{2,1,0:T(8,128)S(1)}, u32[]{:S(2)}, u32[]{:S(2)}) collective-permute-start(f32[3,264,256]{2,1,0:T(8,128)S(1)} %get-tuple-element.35), channel_id=1, source_target_pairs={{0,4},{4,0},{8,12},{12,8},{16,20},{20,16},{24,28},{28,24},{1,5},{5... | collective-permute-start | bytes 2433032 | tf_op jit(solution)/shard_map/ppermute | solution.py:89
  75.6 8.4 %collective-permute-start.22 = (f32[104,256]{1,0:T(8,128)S(1)}, f32[104,256]{1,0:T(8,128)S(1)}, u32[]{:S(2)}, u32[]{:S(2)}) collective-permute-start(f32[104,256]{1,0:T(8,128)S(1)} %pad_maximum_fusion.5), channel_id=1, source_target_pairs={{0,2},{1,3},{2,0},{3,1},{4,6},{5,7},{6,4},{7,5},{8,10},{9,11},{10,... | collective-permute-start | bytes 319496 | tf_op jit(solution)/shard_map/ppermute | solution.py:89
  78.3 19.2 %collective-permute-start.15 = (f32[264,256]{1,0:T(8,128)S(1)}, f32[264,256]{1,0:T(8,128)S(1)}, u32[]{:S(2)}, u32[]{:S(2)}) collective-permute-start(f32[264,256]{1,0:T(8,128)S(1)} %get-tuple-element.31), channel_id=1, source_target_pairs={{0,4},{4,0},{8,12},{12,8},{16,20},{20,16},{24,28},{28,24},{1,5},{5... | collective-permute-start | bytes 811016 | tf_op jit(solution)/shard_map/ppermute | solution.py:89
  84.0 1.3 %collective-permute-start.23 = (f32[72,256]{1,0:T(8,128)S(1)}, f32[72,256]{1,0:T(8,128)S(1)}, u32[]{:S(2)}, u32[]{:S(2)}) collective-permute-start(f32[72,256]{1,0:T(8,128)S(1)} %slice_add_fusion.14), channel_id=1, source_target_pairs={{0,4},{4,0},{8,12},{12,8},{16,20},{20,16},{24,28},{28,24},{1,5},{5... | collective-permute-start | bytes 221192 | tf_op jit(solution)/shard_map/ppermute | solution.py:89
  85.4 6.4 %collective-permute-start.19 = (f32[2,128,256]{2,1,0:T(8,128)S(1)}, f32[2,128,256]{2,1,0:T(8,128)S(1)}, u32[]{:S(2)}, u32[]{:S(2)}) collective-permute-start(f32[2,128,256]{2,1,0:T(8,128)S(1)} %slice_add_fusion.2), channel_id=1, source_target_pairs={{0,8},{4,20},{8,0},{12,28},{16,24},{20,4},{24,16},{28,12},{1,9},{5... | collective-permute-start | bytes 786440 | tf_op jit(solution)/shard_map/ppermute | solution.py:94
  86.9 8.8 %collective-permute-start.18 = (f32[2,136,256]{2,1,0:T(8,128)S(1)}, f32[2,136,256]{2,1,0:T(8,128)S(1)}, u32[]{:S(2)}, u32[]{:S(2)}) collective-permute-start(f32[2,136,256]{2,1,0:T(8,128)S(1)} %slice_add_fusion), channel_id=1, source_target_pairs={{0,8},{4,20},{8,0},{12,28},{16,24},{20,4},{24,16},{28,12},{1,9},{5... | collective-permute-start | bytes 835592 | tf_op jit(solution)/shard_map/ppermute | solution.py:94
  91.9 5.6 %collective-permute-start.21 = (f32[128,256]{1,0:T(8,128)S(1)}, f32[128,256]{1,0:T(8,128)S(1)}, u32[]{:S(2)}, u32[]{:S(2)}) collective-permute-start(f32[128,256]{1,0:T(8,128)S(1)} %fusion.2), channel_id=1, source_target_pairs={{0,16},{4,12},{8,24},{12,4},{16,0},{20,28},{24,8},{28,20},{1,17},{... | collective-permute-start | bytes 393224 | tf_op jit(solution)/shard_map/ppermute | solution.py:99
  95.8 5.1 %collective-permute-start.20 = (f32[136,256]{1,0:T(8,128)S(1)}, f32[136,256]{1,0:T(8,128)S(1)}, u32[]{:S(2)}, u32[]{:S(2)}) collective-permute-start(f32[136,256]{1,0:T(8,128)S(1)} %fusion), channel_id=1, source_target_pairs={{0,16},{4,12},{8,24},{12,4},{16,0},{20,28},{24,8},{28,20},{1,17},{... | collective-permute-start | bytes 417800 | tf_op jit(solution)/shard_map/ppermute | solution.py:99
  102.4 5.2 %collective-permute-start.27 = (f32[104,256]{1,0:T(8,128)S(1)}, f32[104,256]{1,0:T(8,128)S(1)}, u32[]{:S(2)}, u32[]{:S(2)}) collective-permute-start(f32[104,256]{1,0:T(8,128)S(1)} %pad_maximum_fusion.6), channel_id=1, source_target_pairs={{0,1},{1,0},{2,3},{3,2},{4,5},{5,4},{6,7},{7,6},{8,9},{9,8},{10,11... | collective-permute-start | bytes 319496 | tf_op jit(solution)/shard_map/ppermute | solution.py:89
  107.7 6.2 %collective-permute-start.28 = (f32[104,256]{1,0:T(8,128)S(1)}, f32[104,256]{1,0:T(8,128)S(1)}, u32[]{:S(2)}, u32[]{:S(2)}) collective-permute-start(f32[104,256]{1,0:T(8,128)S(1)} %pad_maximum_fusion.7), channel_id=1, source_target_pairs={{0,2},{1,3},{2,0},{3,1},{4,6},{5,7},{6,4},{7,5},{8,10},{9,11},{10,... | collective-permute-start | bytes 319496 | tf_op jit(solution)/shard_map/ppermute | solution.py:89
  109.5 9.2 %collective-permute-start.25 = (f32[256,256]{1,0:T(8,128)S(1)}, f32[256,256]{1,0:T(8,128)S(1)}, u32[]{:S(2)}, u32[]{:S(2)}) collective-permute-start(f32[256,256]{1,0:T(8,128)S(1)} %constant_dynamic-update-slice_fusion.4), channel_id=1, source_target_pairs={{0,16},{4,12},{8,24},{12,4},{16,0},{20,28},{24,8},{28,20},{1,17},{... | collective-permute-start | bytes 786440 | tf_op jit(solution)/shard_map/ppermute | solution.py:99
  111.1 7.6 %collective-permute-start.24 = (f32[256,256]{1,0:T(8,128)S(1)}, f32[256,256]{1,0:T(8,128)S(1)}, u32[]{:S(2)}, u32[]{:S(2)}) collective-permute-start(f32[256,256]{1,0:T(8,128)S(1)} %constant_dynamic-update-slice_fusion.4), channel_id=1, source_target_pairs={{0,8},{4,20},{8,0},{12,28},{16,24},{20,4},{24,16},{28,12},{1,9},{5... | collective-permute-start | bytes 786440 | tf_op jit(solution)/shard_map/ppermute | solution.py:94
  113.9 11.6 %collective-permute-start.31 = (f32[72,256]{1,0:T(8,128)S(1)}, f32[72,256]{1,0:T(8,128)S(1)}, u32[]{:S(2)}, u32[]{:S(2)}) collective-permute-start(f32[72,256]{1,0:T(8,128)S(1)} %slice_add_fusion.12), channel_id=1, source_target_pairs={{0,24},{4,28},{8,16},{12,20},{16,8},{20,12},{24,0},{28,4},{1,25},{... | collective-permute-start | bytes 221192 | tf_op jit(solution)/shard_map/ppermute | solution.py:89
  116.4 9.1 %collective-permute-start.30 = (f32[72,256]{1,0:T(8,128)S(1)}, f32[72,256]{1,0:T(8,128)S(1)}, u32[]{:S(2)}, u32[]{:S(2)}) collective-permute-start(f32[72,256]{1,0:T(8,128)S(1)} %slice_add_fusion.12), channel_id=1, source_target_pairs={{0,16},{4,20},{8,24},{12,28},{16,0},{20,4},{24,8},{28,12},{1,17},{... | collective-permute-start | bytes 221192 | tf_op jit(solution)/shard_map/ppermute | solution.py:89
  116.9 8.6 %collective-permute-start.29 = (f32[72,256]{1,0:T(8,128)S(1)}, f32[72,256]{1,0:T(8,128)S(1)}, u32[]{:S(2)}, u32[]{:S(2)}) collective-permute-start(f32[72,256]{1,0:T(8,128)S(1)} %slice_add_fusion.12), channel_id=1, source_target_pairs={{0,8},{4,12},{8,0},{12,4},{16,24},{20,28},{24,16},{28,20},{1,9},{5... | collective-permute-start | bytes 221192 | tf_op jit(solution)/shard_map/ppermute | solution.py:89
  118.7 6.7 %collective-permute-start.26 = (f32[256,256]{1,0:T(8,128)S(1)}, f32[256,256]{1,0:T(8,128)S(1)}, u32[]{:S(2)}, u32[]{:S(2)}) collective-permute-start(f32[256,256]{1,0:T(8,128)S(1)} %collective-permute-done.25), channel_id=1, source_target_pairs={{0,8},{4,20},{8,0},{12,28},{16,24},{20,4},{24,16},{28,12},{1,9},{5... | collective-permute-start | bytes 786440 | tf_op jit(solution)/shard_map/ppermute | solution.py:94
  121.1 6.7 %collective-permute-start.32 = (f32[2,256,256]{2,1,0:T(8,128)S(1)}, f32[2,256,256]{2,1,0:T(8,128)S(1)}, u32[]{:S(2)}, u32[]{:S(2)}) collective-permute-start(f32[2,256,256]{2,1,0:T(8,128)S(1)} %pad_maximum_fusion.1.refs_0_), channel_id=1, source_target_pairs={{0,4},{4,0},{8,12},{12,8},{16,20},{20,16},{24,28},{28,24},{1,5},{5... | collective-permute-start | bytes 1572872 | tf_op jit(solution)/shard_map/ppermute | solution.py:89
  125.4 2.4 %collective-permute-start.33 = (f32[2,256,256]{2,1,0:T(8,128)S(1)}, f32[2,256,256]{2,1,0:T(8,128)S(1)}, u32[]{:S(2)}, u32[]{:S(2)}) collective-permute-start(f32[2,256,256]{2,1,0:T(8,128)S(1)} %pad_maximum_fusion.2.refs_1_), channel_id=1, source_target_pairs={{0,4},{4,0},{8,12},{12,8},{16,20},{20,16},{24,28},{28,24},{1,5},{5... | collective-permute-start | bytes 1572872 | tf_op jit(solution)/shard_map/ppermute | solution.py:89
  125.6 2.3 %collective-permute-start.34 = (f32[4,72,256]{2,1,0:T(8,128)S(1)}, f32[4,72,256]{2,1,0:T(8,128)S(1)}, u32[]{:S(2)}, u32[]{:S(2)}) collective-permute-start(f32[4,72,256]{2,1,0:T(8,128)S(1)} %pad_maximum_fusion.3.refs_2_), channel_id=1, source_target_pairs={{0,4},{4,0},{8,12},{12,8},{16,20},{20,16},{24,28},{28,24},{1,5},{5... | collective-permute-start | bytes 884744 | tf_op jit(solution)/shard_map/ppermute | solution.py:89

commit v13 on v11

--- a/solution.py
+++ b/solution.py
@@ -259,7 +259,7 @@
 def run_pass(info, points, fine_assign, fine, squares, seen, *, pass_index, flip, rows):
     count, width = points.shape
     block_width = width // SLOTS
-    tile = 512
+    tile = 1024
     initial = pass_index == 0
     chained = seen is not None
     stream = not chained
@@ -309,7 +309,7 @@
         in_specs=[SCALARS, *in_specs],
         out_specs=[HERE] * len(out_shape),
         scratch_shapes=scratch,
-        compiler_params=pltpu.CompilerParams(vmem_limit_bytes=16 * 2**20),
+        compiler_params=pltpu.CompilerParams(vmem_limit_bytes=20 * 2**20),
         cost_estimate=pl.CostEstimate(
             flops=4 * rows * count * width, bytes_accessed=2 * count * width, transcendentals=0
         ),
@@ -386,15 +386,16 @@
     return [*first, *second]
 
 
-def gather_half(top, low):
+def gather_half(top, low, later=()):
     x_low = swap(low, ACROSS_X)
     y_top = swap(top, ACROSS_Y)
+    x_low, y_top, later = lax.optimization_barrier((x_low, y_top, later))
+    corner_top = swap(y_top, ACROSS_X)
+    corner_low = swap(x_low, ACROSS_Y)
     x_top = swap(top, ACROSS_X)
     y_low = swap(low, ACROSS_Y)
-    corner_top = swap(y_top, ACROSS_X)
-    corner_low = swap(x_low, ACROSS_Y)
     blocks = [(top, low), (x_top, x_low), (y_top, y_low), (corner_top, corner_low)]
-    return [jnp.concatenate(block, 0) for block in blocks]
+    return [jnp.concatenate(block, 0) for block in blocks], later
 
 
 def spread(value):
@@ -426,17 +427,17 @@
         start = block_of(info, slot, core) * block_width
         return pl.ds(pl.multiple_of(start, block_width), block_width)
 
-    def put(at, near, far, core):
+    def put(at, near, far):
         for slot in range(SLOTS):
-            fine_held[at, :, column_of(slot, core)] = (far if slot % 2 else near)[slot // 2]
+            fine_held[at, :, column_of(slot, 0)] = (near, far)[slot // 2][slot % 2]
 
     def send(at, half):
         span = pl.ds(pl.multiple_of(half * rows, rows), rows)
         return pltpu.make_async_copy(fine_held.at[at], fine_out.at[span], sems.at[at])
 
-    put(0, *own[:2], info[1])
+    put(0, *own[:2])
     send(0, half).start()
-    put(1, *other[:2], 1 - info[1])
+    put(1, *other[:2])
     send(1, 1 - half).start()
     parts, others = own[2], other[2]
     weight = parts[0, NC:, :128] + others[0, NC:, :128]
@@ -491,7 +492,7 @@
     top, low, part = refine_half(
         info, held, sibling, incoming, owners, coarse_start, flip=0
     )
-    own = jnp.stack(gather_half(top, low))
+    own = jnp.stack(gather_half(top, low)[0])
     folded = jnp.concatenate([part, seen_first.reshape(-1, block_width)], 0)
     paired = swap(folded, 1, "cen")
     other = swap(own, CORE)
@@ -501,26 +502,22 @@
     sent, paired = lax.optimization_barrier((sent, paired))
     sibling = swap(sent, CORE)
     folded = fold(folded, paired)
-    paired = [swap(folded, bit, "cen") for bit in (2,) if bit < lax.axis_size("cen")]
     held, seen_second = call(kept, fine_assign, other, squares, seen, flip=1)
-    held, paired = lax.optimization_barrier((held, paired))
+    held, folded = lax.optimization_barrier((held, folded))
     incoming = exchange(held, sibling)
-    folded = functools.reduce(fold, paired, folded)
-    folded = over_cen(folded, fold, range(2, lax.axis_size("cen").bit_length() - 1))
+    bits = range(lax.axis_size("cen").bit_length() - 1)
+    folded = over_cen(folded, fold, bits[1:])
     part, seen_first = folded[: NC + TAIL], folded[NC + TAIL :]
     part = part + swap(part, CORE)
     coarse = part[:NC] / part[NC, :NC][:, None]
 
     top, low, part = refine_half(info, held, sibling, incoming, owners, coarse, flip=1)
-    fine = jnp.concatenate([top, low], 0)
-    over_first, over_second = lax.optimization_barrier((swap_first(fine), swap_second(fine)))
-    near = jnp.stack([fine, over_second])
-    far = jnp.stack([over_first, swap_first(over_second)])
     folded = jnp.concatenate([part, seen_second.reshape(-1, block_width)], 0)
-    folded = over_cen(folded, fold)
+    folded = over_cen(folded, fold, bits[:1])
+    own, folded = gather_half(top, low, folded)
+    folded = over_cen(folded, fold, bits[1:])
     part, seen_second = folded[: NC + TAIL], folded[NC + TAIL :]
-    parts = jnp.stack(spread(part))
-    blocks = [near, far, parts]
+    blocks = [jnp.stack(own[:2]), jnp.stack(own[2:]), jnp.stack(spread(part))]
     fine_now, coarse_now = place(info, blocks, [swap(block, CORE) for block in blocks], flip=1)
 
     seen = [each.reshape(2, -1) for each in (seen_first, seen_second)]

time: 120 us -> 120 us (level)
  waiting for transfers between devices: 40.8 us -> 34.3 us
  starting transfers between devices: 32.2 us -> 38.2 us
    ppermute x6 -> x4, waiting for transfers between devices: 16.8 us -> 5.6 us  [swap_first(): return lax.ppermute(value, 'pts', pairs)]
    ppermute x20 -> x26, starting transfers between devices: 18.1 us -> 24.9 us  [swap(): return lax.ppermute(value, axis, [(i, i ^ bit) for i in range(size)])]
    ppermute x20 -> x26, waiting for transfers between devices: 16.4 us -> 22.5 us  [swap(): return lax.ppermute(value, axis, [(i, i ^ bit) for i in range(size)])]
    ppermute x6 -> x4, starting transfers between devices: 6.51 us -> 4.7 us  [swap_first(): return lax.ppermute(value, 'pts', pairs)]
    ppermute x5 -> x4, waiting for transfers between devices: 7.59 us -> 6.23 us  [swap_second(): return lax.ppermute(value, 'pts', pairs)]
    ppermute x5 -> x4, starting transfers between devices: 7.55 us -> 8.52 us  [swap_second(): return lax.ppermute(value, 'pts', pairs)]
  transfers between devices with their start and end apart: 31 -> 34, of which waited for: 14 -> 16; matrix products, arithmetic and copies ran while one was open for 2% -> 2% of each run, Pallas kernels for 22% -> 22%
where the time goes in v13:
time: 120 us
  Pallas kernels  44 us (37%)
  starting transfers between devices  38.2 us (32%)
  waiting for transfers between devices  34.3 us (29%)
  other arithmetic  2.17 us (2%)
  between operations  1.22 us (1%)
    pallas_call x4, Pallas kernels, run_pass(): pl.pallas_call(body, out_shape=out_shape, in_specs=[SCALARS, *in_specs],...  38.9 us
    ppermute x26, starting transfers between devices, swap(): return lax.ppermute(value, axis, [(i, i ^ bit) for i in range(size)])  24.9 us
    ppermute x26, waiting for transfers between devices, swap(): return lax.ppermute(value, axis, [(i, i ^ bit) for i in range(size)])  22.5 us
    ppermute x4, starting transfers between devices, swap_second(): return lax.ppermute(value, 'pts', pairs)  8.52 us
    ppermute x4, waiting for transfers between devices, swap_second(): return lax.ppermute(value, 'pts', pairs)  6.23 us
    ppermute x4, waiting for transfers between devices, swap_first(): return lax.ppermute(value, 'pts', pairs)  5.6 us
    ppermute x4, starting transfers between devices, swap_first(): return lax.ppermute(value, 'pts', pairs)  4.7 us
    pallas_call x2, Pallas kernels, refine_half(): pl.pallas_call(functools.partial(refine_body, flip=flip), out_shape=[pltp...  3 us
  transfers between devices with their start and end apart: 34, of which 16 were waited for; matrix products, arithmetic and copies ran while one was open for 2% of the time, Pallas kernels for 22%

profile of v13, /device:TPU:0, one launch (start us, length us, event | category | flops | bytes accessed | tf_op | source)
XLA Modules:
  0.0 120.0 jit_solution(10561412148633757464)
XLA Ops:
  0.6 0.1 pad_add_fusion.info
  0.7 12.3 %energies_and_sums_00.1 = (f32[4,264,256]{2,1,0:T(8,128)S(1)}, f32[2,4096]{1,0:T(2,128)S(1)}, f32[1,4096]{1,0:T(1,128)S(1)}, bf16[4096,1024]{1,0:T(8,128)(2,1)S(1)}) custom-call(s32[4]{0:T(128)S(1)} %pad_add_fusion.info, bf16[4096,1024]{1,0:T(8,128)(2,1)} %points.3, s32[2,4096]{1,0:T(2,128)} %assign.7, f32[512,1024]{1,0:T(8,128)} %fine.3), custom_call_target="tpu_custom_call" | custom-call | flops 4294967296 | bytes 8388608 | tf_op jit(solution)/shard_map/energies_and_sums_00/pallas_call | solution.py:306
  13.0 0.6 collective-permute-start
  13.6 7.6 %energies_and_sums_01.1 = (f32[4,264,256]{2,1,0:T(8,128)S(1)}, f32[2,4096]{1,0:T(2,128)S(1)}) custom-call(s32[4]{0:T(128)S(1)} %pad_add_fusion.info, bf16[4096,1024]{1,0:T(8,128)(2,1)S(1)} %get-tuple-element.31.points, s32[2,4096]{1,0:T(2,128)S(1)} %copy-done.3, f32[512,1024]{1,0:T(8,128)S(1)} %copy-done.2, f32[1,4096]{1,0:T(1,128)S(1)} %get-tuple-element.32.refs_0_, ...), custom_call_target="tpu_custom_call" | custom-call | flops 4294967296 | bytes 8388608 | tf_op jit(solution)/shard_map/energies_and_sums_01/pallas_call | solution.py:306
  21.3 0.0 copy-start
  21.3 0.0 copy-start.1
  21.3 2.5 %collective-permute-start.1 = (f32[2,136,256]{2,1,0:T(8,128)S(1)}, f32[2,136,256]{2,1,0:T(8,128)S(1)}, u32[]{:S(2)}, u32[]{:S(2)}) collective-permute-start(f32[2,136,256]{2,1,0:T(8,128)S(1)} %slice_add_fusion.1), channel_id=1, source_target_pairs={{0,8},{4,20},{8,0},{12,28},{16,24},{20,4},{24,16},{28,12},{1,9},{5... | collective-permute-start | bytes 835592 | tf_op jit(solution)/shard_map/ppermute | solution.py:94
  23.8 0.1 collective-permute-start.2
  23.9 4.4 %collective-permute-done.1.refs_0_ = f32[2,136,256]{2,1,0:T(8,128)S(1)} collective-permute-done((f32[2,136,256]{2,1,0:T(8,128)S(1)}, f32[2,136,256]{2,1,0:T(8,128)S(1)}, u32[]{:S(2)}, u32[]{:S(2)}) %collective-permute-start.1) | collective-permute-done | bytes 278560 | tf_op jit(solution)/shard_map/ppermute | solution.py:94
  28.3 2.1 %collective-permute-start.3 = (f32[136,256]{1,0:T(8,128)S(1)}, f32[136,256]{1,0:T(8,128)S(1)}, u32[]{:S(2)}, u32[]{:S(2)}) collective-permute-start(f32[136,256]{1,0:T(8,128)S(1)} %fusion.1), channel_id=1, source_target_pairs={{0,16},{4,12},{8,24},{12,4},{16,0},{20,28},{24,8},{28,20},{1,17},{... | collective-permute-start | bytes 417800 | tf_op jit(solution)/shard_map/ppermute | solution.py:99
  30.5 0.8 collective-permute-done.2.refs_1_
  31.2 0.7 fusion.3
  31.9 2.4 %collective-permute-start.4 = (f32[128,256]{1,0:T(8,128)}, f32[128,256]{1,0:T(8,128)S(1)}, u32[]{:S(2)}, u32[]{:S(2)}) collective-permute-start(f32[128,256]{1,0:T(8,128)} %fusion.3), channel_id=1, source_target_pairs={{0,16},{4,12},{8,24},{12,4},{16,0},{20,28},{24,8},{28,20},{1,17},{... | collective-permute-start | bytes 393224 | tf_op jit(solution)/shard_map/ppermute | solution.py:99
  34.3 3.1 %collective-permute-done.4.refs_3_ = f32[128,256]{1,0:T(8,128)S(1)} collective-permute-done((f32[128,256]{1,0:T(8,128)}, f32[128,256]{1,0:T(8,128)S(1)}, u32[]{:S(2)}, u32[]{:S(2)}) %collective-permute-start.4) | collective-permute-done | bytes 131104 | tf_op jit(solution)/shard_map/ppermute | solution.py:99
  37.5 1.5 %refine_half.2 = (f32[128,256]{1,0:T(8,128)S(1)}, f32[128,256]{1,0:T(8,128)S(1)}, f32[72,256]{1,0:T(8,128)S(1)}) custom-call(s32[4]{0:T(128)S(1)} %pad_add_fusion.info, f32[4,264,256]{2,1,0:T(8,128)S(1)} %get-tuple-element.34.own, f32[4,264,256]{2,1,0:T(8,128)S(1)} %collective-permute-done.sibling, f32[2,136,256]{2,1,0:T(8,128)S(1)} %collective-permute-done.1.refs_0_, ...), custom_call_target="tpu_custom_call" | custom-call | tf_op jit(solution)/shard_map/refine_half/pallas_call | solution.py:368
  39.0 2.0 %collective-permute-start.7 = (f32[128,256]{1,0:T(8,128)S(1)}, f32[128,256]{1,0:T(8,128)S(1)}, u32[]{:S(2)}, u32[]{:S(2)}) collective-permute-start(f32[128,256]{1,0:T(8,128)S(1)} %get-tuple-element.36), channel_id=1, source_target_pairs={{0,16},{4,20},{8,24},{12,28},{16,0},{20,4},{24,8},{28,12},{1,17},{... | collective-permute-start | bytes 393224 | tf_op jit(solution)/shard_map/ppermute | solution.py:89
  41.0 1.5 %collective-permute-start.5 = (f32[128,256]{1,0:T(8,128)S(1)}, f32[128,256]{1,0:T(8,128)S(1)}, u32[]{:S(2)}, u32[]{:S(2)}) collective-permute-start(f32[128,256]{1,0:T(8,128)S(1)} %get-tuple-element.36), channel_id=1, source_target_pairs={{0,8},{4,12},{8,0},{12,4},{16,24},{20,28},{24,16},{28,20},{1,9},{5... | collective-permute-start | bytes 393224 | tf_op jit(solution)/shard_map/ppermute | solution.py:89
  42.5 0.5 collective-permute-start.6
  43.0 0.1 collective-permute-start.8
  43.2 2.1 %collective-permute-start.12 = (f32[104,256]{1,0:T(8,128)S(1)}, f32[104,256]{1,0:T(8,128)S(1)}, u32[]{:S(2)}, u32[]{:S(2)}) collective-permute-start(f32[104,256]{1,0:T(8,128)S(1)} %pad_maximum_fusion.4), channel_id=1, source_target_pairs={{0,1},{1,0},{2,3},{3,2},{4,5},{5,4},{6,7},{7,6},{8,9},{9,8},{10,11... | collective-permute-start | bytes 319496 | tf_op jit(solution)/shard_map/ppermute | solution.py:89
  45.3 2.7 %collective-permute-done.6 = f32[128,256]{1,0:T(8,128)S(1)} collective-permute-done((f32[128,256]{1,0:T(8,128)S(1)}, f32[128,256]{1,0:T(8,128)S(1)}, u32[]{:S(2)}, u32[]{:S(2)}) %collective-permute-start.6) | collective-permute-done | bytes 131104 | tf_op jit(solution)/shard_map/ppermute | solution.py:89
  48.0 1.3 %collective-permute-start.9 = (f32[128,256]{1,0:T(8,128)S(1)}, f32[128,256]{1,0:T(8,128)S(1)}, u32[]{:S(2)}, u32[]{:S(2)}) collective-permute-start(f32[128,256]{1,0:T(8,128)S(1)} %collective-permute-done.7), channel_id=1, source_target_pairs={{0,8},{4,12},{8,0},{12,4},{16,24},{20,28},{24,16},{28,20},{1,9},{5... | collective-permute-start | bytes 393224 | tf_op jit(solution)/shard_map/ppermute | solution.py:89
  49.4 3.6 %collective-permute-done.10 = f32[128,256]{1,0:T(8,128)S(1)} collective-permute-done((f32[128,256]{1,0:T(8,128)S(1)}, f32[128,256]{1,0:T(8,128)S(1)}, u32[]{:S(2)}, u32[]{:S(2)}) %collective-permute-start.10) | collective-permute-done | bytes 131104 | tf_op jit(solution)/shard_map/ppermute | solution.py:89
  53.0 0.1 pad_maximum_fusion.fine
  53.1 0.0 copy-start.4
  53.1 0.1 collective-permute-start.11
  53.2 11.2 %energies_and_sums_10.1 = (f32[4,264,256]{2,1,0:T(8,128)}, f32[2,4096]{1,0:T(2,128)S(1)}, bf16[4096,1024]{1,0:T(8,128)(2,1)S(1)}) custom-call(s32[4]{0:T(128)S(1)} %pad_add_fusion.info, bf16[4096,1024]{1,0:T(8,128)(2,1)} %points.3, s32[2,4096]{1,0:T(2,128)} %assign.7, f32[4,256,256]{2,1,0:T(8,128)S(1)} %pad_maximum_fusion.fine, ...), custom_call_target="tpu_custom_call" | custom-call | flops 4294967296 | bytes 8388608 | tf_op jit(solution)/shard_map/energies_and_sums_10/pallas_call | solution.py:306
  64.4 0.6 collective-permute-start.13
  65.1 7.8 %energies_and_sums_11.1 = (f32[4,264,256]{2,1,0:T(8,128)S(1)}, f32[2,4096]{1,0:T(2,128)S(1)}) custom-call(s32[4]{0:T(128)S(1)} %pad_add_fusion.info, bf16[4096,1024]{1,0:T(8,128)(2,1)S(1)} %get-tuple-element.40.points, s32[2,4096]{1,0:T(2,128)S(1)} %copy-done.4, f32[4,256,256]{2,1,0:T(8,128)S(1)} %collective-permute-done.11.fine, ...), custom_call_target="tpu_custom_call" | custom-call | flops 4294967296 | bytes 8388608 | tf_op jit(solution)/shard_map/energies_and_sums_11/pallas_call | solution.py:306
  72.8 2.6 %collective-permute-start.18 = (f32[104,256]{1,0:T(8,128)S(1)}, f32[104,256]{1,0:T(8,128)S(1)}, u32[]{:S(2)}, u32[]{:S(2)}) collective-permute-start(f32[104,256]{1,0:T(8,128)S(1)} %pad_maximum_fusion.5), channel_id=1, source_target_pairs={{0,2},{1,3},{2,0},{3,1},{4,6},{5,7},{6,4},{7,5},{8,10},{9,11},{10,... | collective-permute-start | bytes 319496 | tf_op jit(solution)/shard_map/ppermute | solution.py:89
  75.5 1.5 %collective-permute-start.15 = (f32[2,128,256]{2,1,0:T(8,128)S(1)}, f32[2,128,256]{2,1,0:T(8,128)S(1)}, u32[]{:S(2)}, u32[]{:S(2)}) collective-permute-start(f32[2,128,256]{2,1,0:T(8,128)S(1)} %slice_add_fusion.2), channel_id=1, source_target_pairs={{0,8},{4,20},{8,0},{12,28},{16,24},{20,4},{24,16},{28,12},{1,9},{5... | collective-permute-start | bytes 786440 | tf_op jit(solution)/shard_map/ppermute | solution.py:94
  77.0 0.7 collective-permute-start.14
  77.7 3.3 %collective-permute-done.18 = f32[104,256]{1,0:T(8,128)S(1)} collective-permute-done((f32[104,256]{1,0:T(8,128)S(1)}, f32[104,256]{1,0:T(8,128)S(1)}, u32[]{:S(2)}, u32[]{:S(2)}) %collective-permute-start.18) | collective-permute-done | bytes 106528 | tf_op jit(solution)/shard_map/ppermute | solution.py:89
  81.0 0.1 collective-permute-start.19
  81.1 1.2 collective-permute-done.19
  82.4 2.1 %collective-permute-start.17 = (f32[128,256]{1,0:T(8,128)S(1)}, f32[128,256]{1,0:T(8,128)S(1)}, u32[]{:S(2)}, u32[]{:S(2)}) collective-permute-start(f32[128,256]{1,0:T(8,128)S(1)} %fusion.2), channel_id=1, source_target_pairs={{0,16},{4,12},{8,24},{12,4},{16,0},{20,28},{24,8},{28,20},{1,17},{... | collective-permute-start | bytes 393224 | tf_op jit(solution)/shard_map/ppermute | solution.py:99
  84.5 0.4 collective-permute-done.14.refs_0_
  84.9 1.9 %collective-permute-start.16 = (f32[136,256]{1,0:T(8,128)S(1)}, f32[136,256]{1,0:T(8,128)S(1)}, u32[]{:S(2)}, u32[]{:S(2)}) collective-permute-start(f32[136,256]{1,0:T(8,128)S(1)} %fusion), channel_id=1, source_target_pairs={{0,16},{4,12},{8,24},{12,4},{16,0},{20,28},{24,8},{28,20},{1,17},{... | collective-permute-start | bytes 417800 | tf_op jit(solution)/shard_map/ppermute | solution.py:99
  86.9 0.1 slice_divide_fusion.refs_5_
  87.0 0.5 collective-permute-done.17.refs_3_
  87.4 2.6 %collective-permute-done.16.refs_2_ = f32[136,256]{1,0:T(8,128)S(1)} collective-permute-done((f32[136,256]{1,0:T(8,128)S(1)}, f32[136,256]{1,0:T(8,128)S(1)}, u32[]{:S(2)}, u32[]{:S(2)}) %collective-permute-start.16) | collective-permute-done | bytes 139296 | tf_op jit(solution)/shard_map/ppermute | solution.py:99
  90.1 1.5 %refine_half.3 = (f32[128,256]{1,0:T(8,128)S(1)}, f32[128,256]{1,0:T(8,128)S(1)}, f32[72,256]{1,0:T(8,128)S(1)}) custom-call(s32[4]{0:T(128)S(1)} %pad_add_fusion.info, f32[4,264,256]{2,1,0:T(8,128)S(1)} %get-tuple-element.47.own, f32[4,264,256]{2,1,0:T(8,128)S(1)} %collective-permute-done.13.sibling, f32[2,136,256]{2,1,0:T(8,128)S(1)} %collective-permute-done.14.refs_0_, ...), custom_call_target="tpu_custom_call" | custom-call | tf_op jit(solution)/shard_map/refine_half/pallas_call | solution.py:368
  91.6 1.4 %collective-permute-start.21 = (f32[128,256]{1,0:T(8,128)S(1)}, f32[128,256]{1,0:T(8,128)S(1)}, u32[]{:S(2)}, u32[]{:S(2)}) collective-permute-start(f32[128,256]{1,0:T(8,128)S(1)} %get-tuple-element.51), channel_id=1, source_target_pairs={{0,8},{4,12},{8,0},{12,4},{16,24},{20,28},{24,16},{28,20},{1,9},{5... | collective-permute-start | bytes 393224 | tf_op jit(solution)/shard_map/ppermute | solution.py:89
  93.0 1.7 %collective-permute-start.24 = (f32[128,256]{1,0:T(8,128)S(1)}, f32[128,256]{1,0:T(8,128)S(1)}, u32[]{:S(2)}, u32[]{:S(2)}) collective-permute-start(f32[128,256]{1,0:T(8,128)S(1)} %get-tuple-element.51), channel_id=1, source_target_pairs={{0,16},{4,20},{8,24},{12,28},{16,0},{20,4},{24,8},{28,12},{1,17},{... | collective-permute-start | bytes 393224 | tf_op jit(solution)/shard_map/ppermute | solution.py:89
  94.7 0.3 collective-permute-start.22
  95.0 0.6 collective-permute-start.20
  95.7 2.2 %collective-permute-start.23 = (f32[104,256]{1,0:T(8,128)S(1)}, f32[104,256]{1,0:T(8,128)S(1)}, u32[]{:S(2)}, u32[]{:S(2)}) collective-permute-start(f32[104,256]{1,0:T(8,128)S(1)} %pad_maximum_fusion.6), channel_id=1, source_target_pairs={{0,1},{1,0},{2,3},{3,2},{4,5},{5,4},{6,7},{7,6},{8,9},{9,8},{10,11... | collective-permute-start | bytes 319496 | tf_op jit(solution)/shard_map/ppermute | solution.py:89
  97.9 3.8 %collective-permute-done.23 = f32[104,256]{1,0:T(8,128)S(1)} collective-permute-done((f32[104,256]{1,0:T(8,128)S(1)}, f32[104,256]{1,0:T(8,128)S(1)}, u32[]{:S(2)}, u32[]{:S(2)}) %collective-permute-start.23) | collective-permute-done | bytes 106528 | tf_op jit(solution)/shard_map/ppermute | solution.py:89
  101.8 0.2 collective-permute-start.27
  102.0 1.4 %collective-permute-start.25 = (f32[128,256]{1,0:T(8,128)S(1)}, f32[128,256]{1,0:T(8,128)S(1)}, u32[]{:S(2)}, u32[]{:S(2)}) collective-permute-start(f32[128,256]{1,0:T(8,128)S(1)} %collective-permute-done.22), channel_id=1, source_target_pairs={{0,8},{4,12},{8,0},{12,4},{16,24},{20,28},{24,16},{28,20},{1,9},{5... | collective-permute-start | bytes 393224 | tf_op jit(solution)/shard_map/ppermute | solution.py:89
  103.4 1.7 %collective-permute-start.26 = (f32[128,256]{1,0:T(8,128)S(1)}, f32[128,256]{1,0:T(8,128)S(1)}, u32[]{:S(2)}, u32[]{:S(2)}) collective-permute-start(f32[128,256]{1,0:T(8,128)S(1)} %collective-permute-done.21), channel_id=1, source_target_pairs={{0,16},{4,20},{8,24},{12,28},{16,0},{20,4},{24,8},{28,12},{1,17},{... | collective-permute-start | bytes 393224 | tf_op jit(solution)/shard_map/ppermute | solution.py:89
  105.1 0.1 collective-permute-start.31
  105.2 2.2 %collective-permute-done.27 = f32[104,256]{1,0:T(8,128)S(1)} collective-permute-done((f32[104,256]{1,0:T(8,128)S(1)}, f32[104,256]{1,0:T(8,128)S(1)}, u32[]{:S(2)}, u32[]{:S(2)}) %collective-permute-start.27) | collective-permute-done | bytes 106528 | tf_op jit(solution)/shard_map/ppermute | solution.py:89
  107.4 1.5 %collective-permute-start.28 = (f32[72,256]{1,0:T(8,128)S(1)}, f32[72,256]{1,0:T(8,128)S(1)}, u32[]{:S(2)}, u32[]{:S(2)}) collective-permute-start(f32[72,256]{1,0:T(8,128)S(1)} %slice_add_fusion.12), channel_id=1, source_target_pairs={{0,8},{4,12},{8,0},{12,4},{16,24},{20,28},{24,16},{28,20},{1,9},{5... | collective-permute-start | bytes 221192 | tf_op jit(solution)/shard_map/ppermute | solution.py:89
  109.0 1.7 %collective-permute-start.29 = (f32[72,256]{1,0:T(8,128)S(1)}, f32[72,256]{1,0:T(8,128)S(1)}, u32[]{:S(2)}, u32[]{:S(2)}) collective-permute-start(f32[72,256]{1,0:T(8,128)S(1)} %slice_add_fusion.12), channel_id=1, source_target_pairs={{0,16},{4,20},{8,24},{12,28},{16,0},{20,4},{24,8},{28,12},{1,17},{... | collective-permute-start | bytes 221192 | tf_op jit(solution)/shard_map/ppermute | solution.py:89
  110.7 0.4 collective-permute-start.30
  111.2 0.1 collective-permute-start.32
  111.3 0.6 collective-permute-done.28
  111.9 1.5 %collective-permute-done.29 = f32[72,256]{1,0:T(8,128)S(1)} collective-permute-done((f32[72,256]{1,0:T(8,128)S(1)}, f32[72,256]{1,0:T(8,128)S(1)}, u32[]{:S(2)}, u32[]{:S(2)}) %collective-permute-start.29) | collective-permute-done | bytes 73760 | tf_op jit(solution)/shard_map/ppermute | solution.py:89
  113.3 2.7 %collective-permute-done.30 = f32[72,256]{1,0:T(8,128)S(1)} collective-permute-done((f32[72,256]{1,0:T(8,128)S(1)}, f32[72,256]{1,0:T(8,128)S(1)}, u32[]{:S(2)}, u32[]{:S(2)}) %collective-permute-start.30) | collective-permute-done | bytes 73760 | tf_op jit(solution)/shard_map/ppermute | solution.py:89
  116.0 0.1 collective-permute-start.33
  116.1 0.7 maximum_multiply_fusion
  116.8 0.9 collective-permute-done.33.refs_5_
  117.7 2.1 %place_blocks.1 = (f32[512,1024]{1,0:T(8,128)}, f32[64,1024]{1,0:T(8,128)}) custom-call(s32[4]{0:T(128)S(1)} %pad_add_fusion.info, f32[2,256,256]{2,1,0:T(8,128)S(1)} %pad_maximum_fusion.1.refs_0_, f32[2,256,256]{2,1,0:T(8,128)S(1)} %pad_maximum_fusion.2.refs_1_, f32[4,72,256]{2,1,0:T(8,128)S(1)} %pad_maximum_fusion.3.refs_2_, ...), custom_call_target="tpu_custom_call" | custom-call | tf_op jit(solution)/shard_map/place_blocks/pallas_call | solution.py:459
  (64 shorter events, 0.8 us)
Async XLA Ops:
  0.7 12.9 %copy-start.2 = (f32[512,1024]{1,0:T(8,128)S(1)}, f32[512,1024]{1,0:T(8,128)}, u32[]{:S(2)}) copy-start(f32[512,1024]{1,0:T(8,128)} %fine.3) | copy-start | bytes 6291460
  0.7 12.9 %copy-start.3 = (s32[2,4096]{1,0:T(2,128)S(1)}, s32[2,4096]{1,0:T(2,128)}, u32[]{:S(2)}) copy-start(s32[2,4096]{1,0:T(2,128)} %assign.7) | copy-start | bytes 98308
  13.0 8.2 %collective-permute-start = (f32[4,264,256]{2,1,0:T(8,128)S(1)}, f32[4,264,256]{2,1,0:T(8,128)S(1)}, u32[]{:S(2)}, u32[]{:S(2)}) collective-permute-start(f32[4,264,256]{2,1,0:T(8,128)S(1)} %get-tuple-element.35), channel_id=1, source_target_pairs={{0,4},{4,0},{8,12},{12,8},{16,20},{20,16},{24,28},{28,24},{1,5},{5... | collective-permute-start | bytes 3244040 | tf_op jit(solution)/shard_map/ppermute | solution.py:89
  21.3 16.2 %copy-start = (f32[64,1024]{1,0:T(8,128)S(1)}, f32[64,1024]{1,0:T(8,128)}, u32[]{:S(2)}) copy-start(f32[64,1024]{1,0:T(8,128)} %refs_5_.1) | copy-start | bytes 786436
  21.3 16.1 %copy-start.1 = (s32[512]{0:T(512)S(1)}, s32[512]{0:T(512)}, u32[]{:S(2)}) copy-start(s32[512]{0:T(512)} %param.9) | copy-start | bytes 6148
  21.3 7.0 %collective-permute-start.1 = (f32[2,136,256]{2,1,0:T(8,128)S(1)}, f32[2,136,256]{2,1,0:T(8,128)S(1)}, u32[]{:S(2)}, u32[]{:S(2)}) collective-permute-start(f32[2,136,256]{2,1,0:T(8,128)S(1)} %slice_add_fusion.1), channel_id=1, source_target_pairs={{0,8},{4,20},{8,0},{12,28},{16,24},{20,4},{24,16},{28,12},{1,9},{5... | collective-permute-start | bytes 835592 | tf_op jit(solution)/shard_map/ppermute | solution.py:94
  23.8 7.4 %collective-permute-start.2 = (f32[2,128,256]{2,1,0:T(8,128)S(1)}, f32[2,128,256]{2,1,0:T(8,128)S(1)}, u32[]{:S(2)}, u32[]{:S(2)}) collective-permute-start(f32[2,128,256]{2,1,0:T(8,128)S(1)} %slice_add_fusion.3), channel_id=1, source_target_pairs={{0,8},{4,20},{8,0},{12,28},{16,24},{20,4},{24,16},{28,12},{1,9},{5... | collective-permute-start | bytes 786440 | tf_op jit(solution)/shard_map/ppermute | solution.py:94
  28.3 9.1 %collective-permute-start.3 = (f32[136,256]{1,0:T(8,128)S(1)}, f32[136,256]{1,0:T(8,128)S(1)}, u32[]{:S(2)}, u32[]{:S(2)}) collective-permute-start(f32[136,256]{1,0:T(8,128)S(1)} %fusion.1), channel_id=1, source_target_pairs={{0,16},{4,12},{8,24},{12,4},{16,0},{20,28},{24,8},{28,20},{1,17},{... | collective-permute-start | bytes 417800 | tf_op jit(solution)/shard_map/ppermute | solution.py:99
  31.9 5.5 %collective-permute-start.4 = (f32[128,256]{1,0:T(8,128)}, f32[128,256]{1,0:T(8,128)S(1)}, u32[]{:S(2)}, u32[]{:S(2)}) collective-permute-start(f32[128,256]{1,0:T(8,128)} %fusion.3), channel_id=1, source_target_pairs={{0,16},{4,12},{8,24},{12,4},{16,0},{20,28},{24,8},{28,20},{1,17},{... | collective-permute-start | bytes 393224 | tf_op jit(solution)/shard_map/ppermute | solution.py:99
  39.0 9.1 %collective-permute-start.7 = (f32[128,256]{1,0:T(8,128)S(1)}, f32[128,256]{1,0:T(8,128)S(1)}, u32[]{:S(2)}, u32[]{:S(2)}) collective-permute-start(f32[128,256]{1,0:T(8,128)S(1)} %get-tuple-element.36), channel_id=1, source_target_pairs={{0,16},{4,20},{8,24},{12,28},{16,0},{20,4},{24,8},{28,12},{1,17},{... | collective-permute-start | bytes 393224 | tf_op jit(solution)/shard_map/ppermute | solution.py:89
  41.0 8.4 %collective-permute-start.5 = (f32[128,256]{1,0:T(8,128)S(1)}, f32[128,256]{1,0:T(8,128)S(1)}, u32[]{:S(2)}, u32[]{:S(2)}) collective-permute-start(f32[128,256]{1,0:T(8,128)S(1)} %get-tuple-element.36), channel_id=1, source_target_pairs={{0,8},{4,12},{8,0},{12,4},{16,24},{20,28},{24,16},{28,20},{1,9},{5... | collective-permute-start | bytes 393224 | tf_op jit(solution)/shard_map/ppermute | solution.py:89
  42.5 5.5 %collective-permute-start.6 = (f32[128,256]{1,0:T(8,128)S(1)}, f32[128,256]{1,0:T(8,128)S(1)}, u32[]{:S(2)}, u32[]{:S(2)}) collective-permute-start(f32[128,256]{1,0:T(8,128)S(1)} %get-tuple-element.37), channel_id=1, source_target_pairs={{0,8},{4,12},{8,0},{12,4},{16,24},{20,28},{24,16},{28,20},{1,9},{5... | collective-permute-start | bytes 393224 | tf_op jit(solution)/shard_map/ppermute | solution.py:89
  43.0 6.3 %collective-permute-start.8 = (f32[128,256]{1,0:T(8,128)S(1)}, f32[128,256]{1,0:T(8,128)S(1)}, u32[]{:S(2)}, u32[]{:S(2)}) collective-permute-start(f32[128,256]{1,0:T(8,128)S(1)} %get-tuple-element.37), channel_id=1, source_target_pairs={{0,16},{4,20},{8,24},{12,28},{16,0},{20,4},{24,8},{28,12},{1,17},{... | collective-permute-start | bytes 393224 | tf_op jit(solution)/shard_map/ppermute | solution.py:89
  43.2 21.3 %collective-permute-start.12 = (f32[104,256]{1,0:T(8,128)S(1)}, f32[104,256]{1,0:T(8,128)S(1)}, u32[]{:S(2)}, u32[]{:S(2)}) collective-permute-start(f32[104,256]{1,0:T(8,128)S(1)} %pad_maximum_fusion.4), channel_id=1, source_target_pairs={{0,1},{1,0},{2,3},{3,2},{4,5},{5,4},{6,7},{7,6},{8,9},{9,8},{10,11... | collective-permute-start | bytes 319496 | tf_op jit(solution)/shard_map/ppermute | solution.py:89
  48.0 5.0 %collective-permute-start.10 = (f32[128,256]{1,0:T(8,128)S(1)}, f32[128,256]{1,0:T(8,128)S(1)}, u32[]{:S(2)}, u32[]{:S(2)}) collective-permute-start(f32[128,256]{1,0:T(8,128)S(1)} %collective-permute-done.6), channel_id=1, source_target_pairs={{0,16},{4,20},{8,24},{12,28},{16,0},{20,4},{24,8},{28,12},{1,17},{... | collective-permute-start | bytes 393224 | tf_op jit(solution)/shard_map/ppermute | solution.py:89
  48.0 5.0 %collective-permute-start.9 = (f32[128,256]{1,0:T(8,128)S(1)}, f32[128,256]{1,0:T(8,128)S(1)}, u32[]{:S(2)}, u32[]{:S(2)}) collective-permute-start(f32[128,256]{1,0:T(8,128)S(1)} %collective-permute-done.7), channel_id=1, source_target_pairs={{0,8},{4,12},{8,0},{12,4},{16,24},{20,28},{24,16},{28,20},{1,9},{5... | collective-permute-start | bytes 393224 | tf_op jit(solution)/shard_map/ppermute | solution.py:89
  53.1 12.0 %copy-start.4 = (s32[2,4096]{1,0:T(2,128)S(1)}, s32[2,4096]{1,0:T(2,128)}, u32[]{:S(2)}) copy-start(s32[2,4096]{1,0:T(2,128)} %assign.7) | copy-start | bytes 98308
  53.1 11.9 %collective-permute-start.11 = (f32[4,256,256]{2,1,0:T(8,128)S(1)}, f32[4,256,256]{2,1,0:T(8,128)S(1)}, u32[]{:S(2)}, u32[]{:S(2)}) collective-permute-start(f32[4,256,256]{2,1,0:T(8,128)S(1)} %pad_maximum_fusion.fine), channel_id=1, source_target_pairs={{0,4},{4,0},{8,12},{12,8},{16,20},{20,16},{24,28},{28,24},{1,5},{5... | collective-permute-start | bytes 3145736 | tf_op jit(solution)/shard_map/ppermute | solution.py:89
  64.4 11.0 %collective-permute-start.13 = (f32[4,264,256]{2,1,0:T(8,128)}, f32[4,264,256]{2,1,0:T(8,128)S(1)}, u32[]{:S(2)}, u32[]{:S(2)}) collective-permute-start(f32[4,264,256]{2,1,0:T(8,128)} %get-tuple-element.48), channel_id=1, source_target_pairs={{0,4},{4,0},{8,12},{12,8},{16,20},{20,16},{24,28},{28,24},{1,5},{5... | collective-permute-start | bytes 3244040 | tf_op jit(solution)/shard_map/ppermute | solution.py:89
  72.8 8.2 %collective-permute-start.18 = (f32[104,256]{1,0:T(8,128)S(1)}, f32[104,256]{1,0:T(8,128)S(1)}, u32[]{:S(2)}, u32[]{:S(2)}) collective-permute-start(f32[104,256]{1,0:T(8,128)S(1)} %pad_maximum_fusion.5), channel_id=1, source_target_pairs={{0,2},{1,3},{2,0},{3,1},{4,6},{5,7},{6,4},{7,5},{8,10},{9,11},{10,... | collective-permute-start | bytes 319496 | tf_op jit(solution)/shard_map/ppermute | solution.py:89
  75.5 6.9 %collective-permute-start.15 = (f32[2,128,256]{2,1,0:T(8,128)S(1)}, f32[2,128,256]{2,1,0:T(8,128)S(1)}, u32[]{:S(2)}, u32[]{:S(2)}) collective-permute-start(f32[2,128,256]{2,1,0:T(8,128)S(1)} %slice_add_fusion.2), channel_id=1, source_target_pairs={{0,8},{4,20},{8,0},{12,28},{16,24},{20,4},{24,16},{28,12},{1,9},{5... | collective-permute-start | bytes 786440 | tf_op jit(solution)/shard_map/ppermute | solution.py:94
  77.0 7.9 %collective-permute-start.14 = (f32[2,136,256]{2,1,0:T(8,128)S(1)}, f32[2,136,256]{2,1,0:T(8,128)S(1)}, u32[]{:S(2)}, u32[]{:S(2)}) collective-permute-start(f32[2,136,256]{2,1,0:T(8,128)S(1)} %slice_add_fusion), channel_id=1, source_target_pairs={{0,8},{4,20},{8,0},{12,28},{16,24},{20,4},{24,16},{28,12},{1,9},{5... | collective-permute-start | bytes 835592 | tf_op jit(solution)/shard_map/ppermute | solution.py:94
  81.0 1.3 %collective-permute-start.19 = (f32[72,256]{1,0:T(8,128)S(1)}, f32[72,256]{1,0:T(8,128)S(1)}, u32[]{:S(2)}, u32[]{:S(2)}) collective-permute-start(f32[72,256]{1,0:T(8,128)S(1)} %slice_add_fusion.14), channel_id=1, source_target_pairs={{0,4},{4,0},{8,12},{12,8},{16,20},{20,16},{24,28},{28,24},{1,5},{5... | collective-permute-start | bytes 221192 | tf_op jit(solution)/shard_map/ppermute | solution.py:89
  82.4 5.0 %collective-permute-start.17 = (f32[128,256]{1,0:T(8,128)S(1)}, f32[128,256]{1,0:T(8,128)S(1)}, u32[]{:S(2)}, u32[]{:S(2)}) collective-permute-start(f32[128,256]{1,0:T(8,128)S(1)} %fusion.2), channel_id=1, source_target_pairs={{0,16},{4,12},{8,24},{12,4},{16,0},{20,28},{24,8},{28,20},{1,17},{... | collective-permute-start | bytes 393224 | tf_op jit(solution)/shard_map/ppermute | solution.py:99
  84.9 5.1 %collective-permute-start.16 = (f32[136,256]{1,0:T(8,128)S(1)}, f32[136,256]{1,0:T(8,128)S(1)}, u32[]{:S(2)}, u32[]{:S(2)}) collective-permute-start(f32[136,256]{1,0:T(8,128)S(1)} %fusion), channel_id=1, source_target_pairs={{0,16},{4,12},{8,24},{12,4},{16,0},{20,28},{24,8},{28,20},{1,17},{... | collective-permute-start | bytes 417800 | tf_op jit(solution)/shard_map/ppermute | solution.py:99
  91.6 10.2 %collective-permute-start.21 = (f32[128,256]{1,0:T(8,128)S(1)}, f32[128,256]{1,0:T(8,128)S(1)}, u32[]{:S(2)}, u32[]{:S(2)}) collective-permute-start(f32[128,256]{1,0:T(8,128)S(1)} %get-tuple-element.51), channel_id=1, source_target_pairs={{0,8},{4,12},{8,0},{12,4},{16,24},{20,28},{24,16},{28,20},{1,9},{5... | collective-permute-start | bytes 393224 | tf_op jit(solution)/shard_map/ppermute | solution.py:89
  93.0 12.2 %collective-permute-start.24 = (f32[128,256]{1,0:T(8,128)S(1)}, f32[128,256]{1,0:T(8,128)S(1)}, u32[]{:S(2)}, u32[]{:S(2)}) collective-permute-start(f32[128,256]{1,0:T(8,128)S(1)} %get-tuple-element.51), channel_id=1, source_target_pairs={{0,16},{4,20},{8,24},{12,28},{16,0},{20,4},{24,8},{28,12},{1,17},{... | collective-permute-start | bytes 393224 | tf_op jit(solution)/shard_map/ppermute | solution.py:89
  94.7 7.0 %collective-permute-start.22 = (f32[128,256]{1,0:T(8,128)S(1)}, f32[128,256]{1,0:T(8,128)S(1)}, u32[]{:S(2)}, u32[]{:S(2)}) collective-permute-start(f32[128,256]{1,0:T(8,128)S(1)} %get-tuple-element.50), channel_id=1, source_target_pairs={{0,16},{4,20},{8,24},{12,28},{16,0},{20,4},{24,8},{28,12},{1,17},{... | collective-permute-start | bytes 393224 | tf_op jit(solution)/shard_map/ppermute | solution.py:89
  95.0 10.0 %collective-permute-start.20 = (f32[128,256]{1,0:T(8,128)S(1)}, f32[128,256]{1,0:T(8,128)S(1)}, u32[]{:S(2)}, u32[]{:S(2)}) collective-permute-start(f32[128,256]{1,0:T(8,128)S(1)} %get-tuple-element.50), channel_id=1, source_target_pairs={{0,8},{4,12},{8,0},{12,4},{16,24},{20,28},{24,16},{28,20},{1,9},{5... | collective-permute-start | bytes 393224 | tf_op jit(solution)/shard_map/ppermute | solution.py:89
  95.7 6.0 %collective-permute-start.23 = (f32[104,256]{1,0:T(8,128)S(1)}, f32[104,256]{1,0:T(8,128)S(1)}, u32[]{:S(2)}, u32[]{:S(2)}) collective-permute-start(f32[104,256]{1,0:T(8,128)S(1)} %pad_maximum_fusion.6), channel_id=1, source_target_pairs={{0,1},{1,0},{2,3},{3,2},{4,5},{5,4},{6,7},{7,6},{8,9},{9,8},{10,11... | collective-permute-start | bytes 319496 | tf_op jit(solution)/shard_map/ppermute | solution.py:89
  101.8 5.7 %collective-permute-start.27 = (f32[104,256]{1,0:T(8,128)S(1)}, f32[104,256]{1,0:T(8,128)S(1)}, u32[]{:S(2)}, u32[]{:S(2)}) collective-permute-start(f32[104,256]{1,0:T(8,128)S(1)} %pad_maximum_fusion.7), channel_id=1, source_target_pairs={{0,2},{1,3},{2,0},{3,1},{4,6},{5,7},{6,4},{7,5},{8,10},{9,11},{10,... | collective-permute-start | bytes 319496 | tf_op jit(solution)/shard_map/ppermute | solution.py:89
  102.0 8.7 %collective-permute-start.25 = (f32[128,256]{1,0:T(8,128)S(1)}, f32[128,256]{1,0:T(8,128)S(1)}, u32[]{:S(2)}, u32[]{:S(2)}) collective-permute-start(f32[128,256]{1,0:T(8,128)S(1)} %collective-permute-done.22), channel_id=1, source_target_pairs={{0,8},{4,12},{8,0},{12,4},{16,24},{20,28},{24,16},{28,20},{1,9},{5... | collective-permute-start | bytes 393224 | tf_op jit(solution)/shard_map/ppermute | solution.py:89
  103.4 7.8 %collective-permute-start.26 = (f32[128,256]{1,0:T(8,128)S(1)}, f32[128,256]{1,0:T(8,128)S(1)}, u32[]{:S(2)}, u32[]{:S(2)}) collective-permute-start(f32[128,256]{1,0:T(8,128)S(1)} %collective-permute-done.21), channel_id=1, source_target_pairs={{0,16},{4,20},{8,24},{12,28},{16,0},{20,4},{24,8},{28,12},{1,17},{... | collective-permute-start | bytes 393224 | tf_op jit(solution)/shard_map/ppermute | solution.py:89
  105.1 12.6 %collective-permute-start.31 = (f32[2,256,256]{2,1,0:T(8,128)S(1)}, f32[2,256,256]{2,1,0:T(8,128)S(1)}, u32[]{:S(2)}, u32[]{:S(2)}) collective-permute-start(f32[2,256,256]{2,1,0:T(8,128)S(1)} %pad_maximum_fusion.1.refs_0_), channel_id=1, source_target_pairs={{0,4},{4,0},{8,12},{12,8},{16,20},{20,16},{24,28},{28,24},{1,5},{5... | collective-permute-start | bytes 1572872 | tf_op jit(solution)/shard_map/ppermute | solution.py:89
  107.4 4.4 %collective-permute-start.28 = (f32[72,256]{1,0:T(8,128)S(1)}, f32[72,256]{1,0:T(8,128)S(1)}, u32[]{:S(2)}, u32[]{:S(2)}) collective-permute-start(f32[72,256]{1,0:T(8,128)S(1)} %slice_add_fusion.12), channel_id=1, source_target_pairs={{0,8},{4,12},{8,0},{12,4},{16,24},{20,28},{24,16},{28,20},{1,9},{5... | collective-permute-start | bytes 221192 | tf_op jit(solution)/shard_map/ppermute | solution.py:89
  109.0 4.4 %collective-permute-start.29 = (f32[72,256]{1,0:T(8,128)S(1)}, f32[72,256]{1,0:T(8,128)S(1)}, u32[]{:S(2)}, u32[]{:S(2)}) collective-permute-start(f32[72,256]{1,0:T(8,128)S(1)} %slice_add_fusion.12), channel_id=1, source_target_pairs={{0,16},{4,20},{8,24},{12,28},{16,0},{20,4},{24,8},{28,12},{1,17},{... | collective-permute-start | bytes 221192 | tf_op jit(solution)/shard_map/ppermute | solution.py:89
  110.7 5.3 %collective-permute-start.30 = (f32[72,256]{1,0:T(8,128)S(1)}, f32[72,256]{1,0:T(8,128)S(1)}, u32[]{:S(2)}, u32[]{:S(2)}) collective-permute-start(f32[72,256]{1,0:T(8,128)S(1)} %slice_add_fusion.12), channel_id=1, source_target_pairs={{0,24},{4,28},{8,16},{12,20},{16,8},{20,12},{24,0},{28,4},{1,25},{... | collective-permute-start | bytes 221192 | tf_op jit(solution)/shard_map/ppermute | solution.py:89
  111.2 6.5 %collective-permute-start.32 = (f32[2,256,256]{2,1,0:T(8,128)S(1)}, f32[2,256,256]{2,1,0:T(8,128)S(1)}, u32[]{:S(2)}, u32[]{:S(2)}) collective-permute-start(f32[2,256,256]{2,1,0:T(8,128)S(1)} %pad_maximum_fusion.2.refs_1_), channel_id=1, source_target_pairs={{0,4},{4,0},{8,12},{12,8},{16,20},{20,16},{24,28},{28,24},{1,5},{5... | collective-permute-start | bytes 1572872 | tf_op jit(solution)/shard_map/ppermute | solution.py:89
  116.0 1.6 %collective-permute-start.33 = (f32[4,72,256]{2,1,0:T(8,128)S(1)}, f32[4,72,256]{2,1,0:T(8,128)S(1)}, u32[]{:S(2)}, u32[]{:S(2)}) collective-permute-start(f32[4,72,256]{2,1,0:T(8,128)S(1)} %pad_maximum_fusion.3.refs_2_), channel_id=1, source_target_pairs={{0,4},{4,0},{8,12},{12,8},{16,20},{20,16},{24,28},{28,24},{1,5},{5... | collective-permute-start | bytes 884744 | tf_op jit(solution)/shard_map/ppermute | solution.py:89

commit v14 on v13

--- a/solution.py
+++ b/solution.py
@@ -161,10 +161,6 @@
         load_assign = pltpu.make_async_copy(assign, chosen_in, small_sems.at[0])
         load_assign.start()
 
-        @pl.loop(1, tiles)
-        def _(i):
-            load(i).start()
-
     if initial:
         if first:
             load_start.wait()
@@ -174,11 +170,13 @@
         norm = jnp.sum(block * block, axis=1, keepdims=True)
         low[...] = (-2.0 * block).astype(jnp.bfloat16)
     else:
-        norm = jnp.zeros((rows, 1), jnp.float32)
-        for slot in range(SLOTS):
-            block = fine[slot]
-            norm = norm + jnp.sum(block * block, axis=1, keepdims=True)
-            low[:, column_of(slot, 0)] = (-2.0 * block).astype(jnp.bfloat16)
+        norm = [jnp.zeros((mid, 1), jnp.float32)] * 2
+        for piece, (slot, is_low) in enumerate(PIECES):
+            block = fine[piece]
+            norm[is_low] = norm[is_low] + jnp.sum(block * block, axis=1, keepdims=True)
+            part = slice(is_low * mid, (is_low + 1) * mid)
+            low[part, column_of(slot, 0)] = (-2.0 * block).astype(jnp.bfloat16)
+        norm = jnp.concatenate(norm, 0)
     norms[...] = jnp.broadcast_to(norm, norms.shape)
     tallies[...] = jnp.zeros_like(tallies)
     sums[...] = jnp.zeros_like(sums)
@@ -226,24 +224,28 @@
             preferred_element_type=jnp.float32,
         )
 
+    def arrive(i, more):
+        if stream:
+            load(i).wait()
+            if more:
+                load(i + 1).start()
+
     if stream:
         load_assign.wait()
-        load(0).wait()
+    arrive(0, True)
     multiply(0, even)
 
     @pl.loop(0, tiles // 2 - 1)
     def _(pair):
         i = 2 * pair
-        if stream:
-            load(i + 1).wait()
-            load(i + 2).wait()
+        arrive(i + 1, True)
         multiply(i + 1, odd)
         collect(i, even)
+        arrive(i + 2, True)
         multiply(i + 2, even)
         collect(i + 1, odd)
 
-    if stream:
-        load(tiles - 1).wait()
+    arrive(tiles - 1, False)
     multiply(tiles - 1, odd)
     collect(tiles - 2, even)
     collect(tiles - 1, odd)
@@ -375,27 +377,33 @@
     )(info, *args)
 
 
-def exchange(held, sibling):
+def exchange(held, sibling, later=()):
     cut = (held.shape[1] - TAIL) // 2 + TAIL
     chunks = slice(0, cut), slice(cut, None)
-    first = [swap_first(held[1::2, rows] + sibling[1::2, rows]) for rows in chunks]
+    first = [held[1::2, rows] + sibling[1::2, rows] for rows in chunks]
+    first, later = lax.optimization_barrier((first, later))
+    first = [swap_first(chunk) for chunk in first]
     second = [
         swap_second(held[2, rows] + sibling[2, rows] + arrived[1])
         for rows, arrived in zip(chunks, first)
     ]
-    return [*first, *second]
-
-
-def gather_half(top, low, later=()):
+    return [*first, *second], later
+
+
+PIECES = ((1, 1), (2, 0), (3, 0), (3, 1), (1, 0), (2, 1), (0, 0), (0, 1))
+
+
+def gather_half(top, low, later=None):
     x_low = swap(low, ACROSS_X)
     y_top = swap(top, ACROSS_Y)
-    x_low, y_top, later = lax.optimization_barrier((x_low, y_top, later))
+    again = top, low
+    if later is not None:
+        x_low, y_top, again, later = lax.optimization_barrier((x_low, y_top, again, later))
+    x_top = swap(again[0], ACROSS_X)
+    y_low = swap(again[1], ACROSS_Y)
     corner_top = swap(y_top, ACROSS_X)
     corner_low = swap(x_low, ACROSS_Y)
-    x_top = swap(top, ACROSS_X)
-    y_low = swap(low, ACROSS_Y)
-    blocks = [(top, low), (x_top, x_low), (y_top, y_low), (corner_top, corner_low)]
-    return [jnp.concatenate(block, 0) for block in blocks], later
+    return [x_low, y_top, corner_top, corner_low, x_top, y_low, top, low], later
 
 
 def spread(value):
@@ -421,15 +429,17 @@
     fine_out, coarse_out, fine_held, coarse_held, sems = refs[6:]
     block_width = coarse_out.shape[1] // SLOTS
     rows = fine_out.shape[0] // 2
+    mid = rows // 2
     half = info[1] ^ flip
 
     def column_of(slot, core):
         start = block_of(info, slot, core) * block_width
         return pl.ds(pl.multiple_of(start, block_width), block_width)
 
-    def put(at, near, far):
-        for slot in range(SLOTS):
-            fine_held[at, :, column_of(slot, 0)] = (near, far)[slot // 2][slot % 2]
+    def put(at, *groups):
+        for piece, (slot, is_low) in enumerate(PIECES):
+            part = slice(is_low * mid, (is_low + 1) * mid)
+            fine_held[at, part, column_of(slot, 0)] = groups[piece // SLOTS][piece % SLOTS]
 
     def send(at, half):
         span = pl.ds(pl.multiple_of(half * rows, rows), rows)
@@ -453,8 +463,8 @@
 
 
 def place(info, own, other, *, flip):
-    _, rows, block_width = own[0].shape
-    width = SLOTS * block_width
+    _, mid, block_width = own[0].shape
+    rows, width = 2 * mid, SLOTS * block_width
     args = [near_by(value) for value in (*own, *other)]
     return pl.pallas_call(
         functools.partial(place_body, flip=flip),
@@ -488,7 +498,7 @@
     sent, seen, squares, kept = call(points, fine_assign, fine_start, None, None, flip=1)
     sibling = swap(sent, CORE)
     held, seen_first = call(kept, fine_assign, fine_start, squares, seen, flip=0)
-    incoming = exchange(held, sibling)
+    incoming, _ = exchange(held, sibling)
     top, low, part = refine_half(
         info, held, sibling, incoming, owners, coarse_start, flip=0
     )
@@ -502,22 +512,25 @@
     sent, paired = lax.optimization_barrier((sent, paired))
     sibling = swap(sent, CORE)
     folded = fold(folded, paired)
+    part = folded[: NC + TAIL]
+    others_part = swap(part, CORE)
     held, seen_second = call(kept, fine_assign, other, squares, seen, flip=1)
-    held, folded = lax.optimization_barrier((held, folded))
-    incoming = exchange(held, sibling)
+    held, others_part = lax.optimization_barrier((held, others_part))
+    folded = jnp.concatenate([part + others_part, folded[NC + TAIL :]], 0)
+    incoming, folded = exchange(held, sibling, folded)
     bits = range(lax.axis_size("cen").bit_length() - 1)
     folded = over_cen(folded, fold, bits[1:])
     part, seen_first = folded[: NC + TAIL], folded[NC + TAIL :]
-    part = part + swap(part, CORE)
     coarse = part[:NC] / part[NC, :NC][:, None]
 
     top, low, part = refine_half(info, held, sibling, incoming, owners, coarse, flip=1)
     folded = jnp.concatenate([part, seen_second.reshape(-1, block_width)], 0)
+    top, low, folded = lax.optimization_barrier((top, low, folded))
     folded = over_cen(folded, fold, bits[:1])
     own, folded = gather_half(top, low, folded)
     folded = over_cen(folded, fold, bits[1:])
     part, seen_second = folded[: NC + TAIL], folded[NC + TAIL :]
-    blocks = [jnp.stack(own[:2]), jnp.stack(own[2:]), jnp.stack(spread(part))]
+    blocks = [jnp.stack(own[:4]), jnp.stack(own[4:]), jnp.stack(spread(part))]
     fine_now, coarse_now = place(info, blocks, [swap(block, CORE) for block in blocks], flip=1)
 
     seen = [each.reshape(2, -1) for each in (seen_first, seen_second)]
@@ -537,7 +550,7 @@
             and centres & (centres - 1) == 0
             and width // SLOTS == local_count // 2
             and (width // SLOTS) % 128 == 0
-            and count % 1024 == 0
+            and count % 2048 == 0
         )
         plan = on_device_paired if fits else on_device_any
         return plan(points, fine_assign, fine_start, coarse_start, coarse_assign)

time: 120 us -> 119 us (level)
  starting transfers between devices: 38.2 us -> 33.3 us
  waiting for transfers between devices: 34.3 us -> 38.6 us
    ppermute x4, waiting for transfers between devices: 5.6 us -> 9.11 us  [swap_first(): return lax.ppermute(value, 'pts', pairs)]
    ppermute x26, starting transfers between devices: 24.9 us -> 21.9 us  [swap(): return lax.ppermute(value, axis, [(i, i ^ bit) for i in range(size)])]
    ppermute x4, starting transfers between devices: 8.52 us -> 6.64 us  [swap_second(): return lax.ppermute(value, 'pts', pairs)]
  transfers between devices with their start and end apart: 34 -> 34, of which waited for: 16 -> 18; matrix products, arithmetic and copies ran while one was open for 2% -> 1% of each run, Pallas kernels for 22% -> 22%
where the time goes in v14:
time: 119 us
  Pallas kernels  44 us (37%)
  waiting for transfers between devices  38.6 us (32%)
  starting transfers between devices  33.3 us (28%)
  other arithmetic  1.32 us (1%)
  between operations  1.21 us (1%)
    pallas_call x4, Pallas kernels, run_pass(): pl.pallas_call(body, out_shape=out_shape, in_specs=[SCALARS, *in_specs],...  38.8 us
    ppermute x26, waiting for transfers between devices, swap(): return lax.ppermute(value, axis, [(i, i ^ bit) for i in range(size)])  22.2 us
    ppermute x26, starting transfers between devices, swap(): return lax.ppermute(value, axis, [(i, i ^ bit) for i in range(size)])  21.9 us
    ppermute x4, waiting for transfers between devices, swap_first(): return lax.ppermute(value, 'pts', pairs)  9.11 us
    ppermute x4, waiting for transfers between devices, swap_second(): return lax.ppermute(value, 'pts', pairs)  7.34 us
    ppermute x4, starting transfers between devices, swap_second(): return lax.ppermute(value, 'pts', pairs)  6.64 us
    ppermute x4, starting transfers between devices, swap_first(): return lax.ppermute(value, 'pts', pairs)  4.76 us
    pallas_call x2, Pallas kernels, refine_half(): pl.pallas_call(functools.partial(refine_body, flip=flip), out_shape=[pltp...  3.02 us
  transfers between devices with their start and end apart: 34, of which 18 were waited for; matrix products, arithmetic and copies ran while one was open for 1% of the time, Pallas kernels for 22%

profile of v14, /device:TPU:0, one launch (start us, length us, event | category | flops | bytes accessed | tf_op | source)
XLA Modules:
  0.0 118.7 jit_solution(16000737371787529256)
XLA Ops:
  0.6 0.1 pad_add_fusion.info
  0.7 12.5 %energies_and_sums_00.1 = (f32[4,264,256]{2,1,0:T(8,128)S(1)}, f32[2,4096]{1,0:T(2,128)S(1)}, f32[1,4096]{1,0:T(1,128)S(1)}, bf16[4096,1024]{1,0:T(8,128)(2,1)S(1)}) custom-call(s32[4]{0:T(128)S(1)} %pad_add_fusion.info, bf16[4096,1024]{1,0:T(8,128)(2,1)} %points.3, s32[2,4096]{1,0:T(2,128)} %assign.7, f32[512,1024]{1,0:T(8,128)} %fine.3), custom_call_target="tpu_custom_call" | custom-call | flops 4294967296 | bytes 8388608 | tf_op jit(solution)/shard_map/energies_and_sums_00/pallas_call | solution.py:308
  13.2 0.5 collective-permute-start
  13.8 7.6 %energies_and_sums_01.1 = (f32[4,264,256]{2,1,0:T(8,128)S(1)}, f32[2,4096]{1,0:T(2,128)S(1)}) custom-call(s32[4]{0:T(128)S(1)} %pad_add_fusion.info, bf16[4096,1024]{1,0:T(8,128)(2,1)S(1)} %get-tuple-element.39.points, s32[2,4096]{1,0:T(2,128)S(1)} %copy-done.3, f32[512,1024]{1,0:T(8,128)S(1)} %copy-done.2, f32[1,4096]{1,0:T(1,128)S(1)} %get-tuple-element.40.refs_0_, ...), custom_call_target="tpu_custom_call" | custom-call | flops 4294967296 | bytes 8388608 | tf_op jit(solution)/shard_map/energies_and_sums_01/pallas_call | solution.py:308
  21.4 0.0 copy-start
  21.4 0.0 copy-start.1
  21.5 2.6 %collective-permute-start.1 = (f32[2,136,256]{2,1,0:T(8,128)S(1)}, f32[2,136,256]{2,1,0:T(8,128)S(1)}, u32[]{:S(2)}, u32[]{:S(2)}) collective-permute-start(f32[2,136,256]{2,1,0:T(8,128)S(1)} %slice_add_fusion.1), channel_id=1, source_target_pairs={{0,8},{4,20},{8,0},{12,28},{16,24},{20,4},{24,16},{28,12},{1,9},{5... | collective-permute-start | bytes 835592 | tf_op jit(solution)/shard_map/ppermute | solution.py:94
  24.1 0.1 collective-permute-start.2
  24.2 4.4 %collective-permute-done.1.refs_0_ = f32[2,136,256]{2,1,0:T(8,128)S(1)} collective-permute-done((f32[2,136,256]{2,1,0:T(8,128)S(1)}, f32[2,136,256]{2,1,0:T(8,128)S(1)}, u32[]{:S(2)}, u32[]{:S(2)}) %collective-permute-start.1) | collective-permute-done | bytes 278560 | tf_op jit(solution)/shard_map/ppermute | solution.py:94
  28.6 2.1 %collective-permute-start.3 = (f32[136,256]{1,0:T(8,128)S(1)}, f32[136,256]{1,0:T(8,128)S(1)}, u32[]{:S(2)}, u32[]{:S(2)}) collective-permute-start(f32[136,256]{1,0:T(8,128)S(1)} %fusion.1), channel_id=1, source_target_pairs={{0,16},{4,12},{8,24},{12,4},{16,0},{20,28},{24,8},{28,20},{1,17},{... | collective-permute-start | bytes 417800 | tf_op jit(solution)/shard_map/ppermute | solution.py:99
  30.7 0.8 collective-permute-done.2.refs_1_
  31.6 2.4 %collective-permute-start.4 = (f32[128,256]{1,0:T(8,128)S(1)}, f32[128,256]{1,0:T(8,128)S(1)}, u32[]{:S(2)}, u32[]{:S(2)}) collective-permute-start(f32[128,256]{1,0:T(8,128)S(1)} %fusion.3), channel_id=1, source_target_pairs={{0,16},{4,12},{8,24},{12,4},{16,0},{20,28},{24,8},{28,20},{1,17},{... | collective-permute-start | bytes 393224 | tf_op jit(solution)/shard_map/ppermute | solution.py:99
  34.0 2.9 %collective-permute-done.4.refs_3_ = f32[128,256]{1,0:T(8,128)S(1)} collective-permute-done((f32[128,256]{1,0:T(8,128)S(1)}, f32[128,256]{1,0:T(8,128)S(1)}, u32[]{:S(2)}, u32[]{:S(2)}) %collective-permute-start.4) | collective-permute-done | bytes 131104 | tf_op jit(solution)/shard_map/ppermute | solution.py:99
  36.9 1.5 %refine_half.2 = (f32[128,256]{1,0:T(8,128)S(1)}, f32[128,256]{1,0:T(8,128)S(1)}, f32[72,256]{1,0:T(8,128)S(1)}) custom-call(s32[4]{0:T(128)S(1)} %pad_add_fusion.info, f32[4,264,256]{2,1,0:T(8,128)S(1)} %get-tuple-element.42.own, f32[4,264,256]{2,1,0:T(8,128)S(1)} %collective-permute-done.sibling, f32[2,136,256]{2,1,0:T(8,128)S(1)} %collective-permute-done.1.refs_0_, ...), custom_call_target="tpu_custom_call" | custom-call | tf_op jit(solution)/shard_map/refine_half/pallas_call | solution.py:370
  38.4 2.0 %collective-permute-start.5 = (f32[128,256]{1,0:T(8,128)S(1)}, f32[128,256]{1,0:T(8,128)S(1)}, u32[]{:S(2)}, u32[]{:S(2)}) collective-permute-start(f32[128,256]{1,0:T(8,128)S(1)} %get-tuple-element.46), channel_id=1, source_target_pairs={{0,8},{4,12},{8,0},{12,4},{16,24},{20,28},{24,16},{28,20},{1,9},{5... | collective-permute-start | bytes 393224 | tf_op jit(solution)/shard_map/ppermute | solution.py:89
  40.5 1.6 %collective-permute-start.6 = (f32[128,256]{1,0:T(8,128)S(1)}, f32[128,256]{1,0:T(8,128)S(1)}, u32[]{:S(2)}, u32[]{:S(2)}) collective-permute-start(f32[128,256]{1,0:T(8,128)S(1)} %get-tuple-element.47), channel_id=1, source_target_pairs={{0,16},{4,20},{8,24},{12,28},{16,0},{20,4},{24,8},{28,12},{1,17},{... | collective-permute-start | bytes 393224 | tf_op jit(solution)/shard_map/ppermute | solution.py:89
  42.1 0.5 collective-permute-start.9
  42.6 0.1 collective-permute-start.10
  42.7 2.0 %collective-permute-done.5 = f32[128,256]{1,0:T(8,128)S(1)} collective-permute-done((f32[128,256]{1,0:T(8,128)S(1)}, f32[128,256]{1,0:T(8,128)S(1)}, u32[]{:S(2)}, u32[]{:S(2)}) %collective-permute-start.5) | collective-permute-done | bytes 131104 | tf_op jit(solution)/shard_map/ppermute | solution.py:89
  44.7 0.8 collective-permute-start.8
  45.5 1.1 collective-permute-done.6
  46.6 0.5 collective-permute-start.7
  47.1 4.5 %collective-permute-done.7 = f32[128,256]{1,0:T(8,128)S(1)} collective-permute-done((f32[128,256]{1,0:T(8,128)S(1)}, f32[128,256]{1,0:T(8,128)S(1)}, u32[]{:S(2)}, u32[]{:S(2)}) %collective-permute-start.7) | collective-permute-done | bytes 131104 | tf_op jit(solution)/shard_map/ppermute | solution.py:89
  51.7 0.1 collective-permute-start.11
  51.8 0.0 copy-start.4
  51.8 1.6 %collective-permute-start.12 = (f32[104,256]{1,0:T(8,128)S(1)}, f32[104,256]{1,0:T(8,128)S(1)}, u32[]{:S(2)}, u32[]{:S(2)}) collective-permute-start(f32[104,256]{1,0:T(8,128)S(1)} %pad_maximum_fusion.3), channel_id=1, source_target_pairs={{0,1},{1,0},{2,3},{3,2},{4,5},{5,4},{6,7},{7,6},{8,9},{9,8},{10,11... | collective-permute-start | bytes 319496 | tf_op jit(solution)/shard_map/ppermute | solution.py:89
  53.5 11.0 %energies_and_sums_10.1 = (f32[4,264,256]{2,1,0:T(8,128)S(1)}, f32[2,4096]{1,0:T(2,128)S(1)}, bf16[4096,1024]{1,0:T(8,128)(2,1)S(1)}) custom-call(s32[4]{0:T(128)S(1)} %pad_add_fusion.info, bf16[4096,1024]{1,0:T(8,128)(2,1)} %points.3, s32[2,4096]{1,0:T(2,128)} %assign.7, f32[8,128,256]{2,1,0:T(8,128)S(1)} %bitcast_dynamic-update-slice_fusion.fine, ...), custom_call_target="tpu_custom_call" | custom-call | flops 4294967296 | bytes 8388608 | tf_op jit(solution)/shard_map/energies_and_sums_10/pallas_call | solution.py:308
  64.5 0.3 collective-permute-start.14
  64.8 0.3 collective-permute-start.13
  65.1 7.8 %energies_and_sums_11.1 = (f32[4,264,256]{2,1,0:T(8,128)S(1)}, f32[2,4096]{1,0:T(2,128)S(1)}) custom-call(s32[4]{0:T(128)S(1)} %pad_add_fusion.info, bf16[4096,1024]{1,0:T(8,128)(2,1)S(1)} %get-tuple-element.48.points, s32[2,4096]{1,0:T(2,128)S(1)} %copy-done.4, f32[8,128,256]{2,1,0:T(8,128)S(1)} %collective-permute-done.11.fine, ...), custom_call_target="tpu_custom_call" | custom-call | flops 4294967296 | bytes 8388608 | tf_op jit(solution)/shard_map/energies_and_sums_11/pallas_call | solution.py:308
  73.1 2.7 %collective-permute-start.19 = (f32[104,256]{1,0:T(8,128)S(1)}, f32[104,256]{1,0:T(8,128)S(1)}, u32[]{:S(2)}, u32[]{:S(2)}) collective-permute-start(f32[104,256]{1,0:T(8,128)S(1)} %pad_maximum_fusion.4), channel_id=1, source_target_pairs={{0,2},{1,3},{2,0},{3,1},{4,6},{5,7},{6,4},{7,5},{8,10},{9,11},{10,... | collective-permute-start | bytes 319496 | tf_op jit(solution)/shard_map/ppermute | solution.py:89
  75.8 0.8 collective-permute-start.15
  76.6 1.2 %collective-permute-start.16 = (f32[2,128,256]{2,1,0:T(8,128)S(1)}, f32[2,128,256]{2,1,0:T(8,128)S(1)}, u32[]{:S(2)}, u32[]{:S(2)}) collective-permute-start(f32[2,128,256]{2,1,0:T(8,128)S(1)} %slice_add_fusion.2), channel_id=1, source_target_pairs={{0,8},{4,20},{8,0},{12,28},{16,24},{20,4},{24,16},{28,12},{1,9},{5... | collective-permute-start | bytes 786440 | tf_op jit(solution)/shard_map/ppermute | solution.py:94
  77.9 3.4 %collective-permute-done.19 = f32[104,256]{1,0:T(8,128)S(1)} collective-permute-done((f32[104,256]{1,0:T(8,128)S(1)}, f32[104,256]{1,0:T(8,128)S(1)}, u32[]{:S(2)}, u32[]{:S(2)}) %collective-permute-start.19) | collective-permute-done | bytes 106528 | tf_op jit(solution)/shard_map/ppermute | solution.py:89
  81.3 3.9 %collective-permute-done.16.refs_1_ = f32[2,128,256]{2,1,0:T(8,128)S(1)} collective-permute-done((f32[2,128,256]{2,1,0:T(8,128)S(1)}, f32[2,128,256]{2,1,0:T(8,128)S(1)}, u32[]{:S(2)}, u32[]{:S(2)}) %collective-permute-start.16) | collective-permute-done | bytes 262176 | tf_op jit(solution)/shard_map/ppermute | solution.py:94
  85.2 1.5 %collective-permute-start.18 = (f32[128,256]{1,0:T(8,128)S(1)}, f32[128,256]{1,0:T(8,128)S(1)}, u32[]{:S(2)}, u32[]{:S(2)}) collective-permute-start(f32[128,256]{1,0:T(8,128)S(1)} %fusion.2), channel_id=1, source_target_pairs={{0,16},{4,12},{8,24},{12,4},{16,0},{20,28},{24,8},{28,20},{1,17},{... | collective-permute-start | bytes 393224 | tf_op jit(solution)/shard_map/ppermute | solution.py:99
  86.8 0.6 collective-permute-start.17
  87.4 0.1 slice_divide_fusion.refs_5_
  87.5 2.7 %collective-permute-done.18.refs_3_ = f32[128,256]{1,0:T(8,128)S(1)} collective-permute-done((f32[128,256]{1,0:T(8,128)S(1)}, f32[128,256]{1,0:T(8,128)S(1)}, u32[]{:S(2)}, u32[]{:S(2)}) %collective-permute-start.18) | collective-permute-done | bytes 131104 | tf_op jit(solution)/shard_map/ppermute | solution.py:99
  90.3 1.6 %collective-permute-done.17.refs_2_ = f32[136,256]{1,0:T(8,128)S(1)} collective-permute-done((f32[136,256]{1,0:T(8,128)S(1)}, f32[136,256]{1,0:T(8,128)S(1)}, u32[]{:S(2)}, u32[]{:S(2)}) %collective-permute-start.17) | collective-permute-done | bytes 139296 | tf_op jit(solution)/shard_map/ppermute | solution.py:99
  91.9 1.5 %refine_half.3 = (f32[128,256]{1,0:T(8,128)S(1)}, f32[128,256]{1,0:T(8,128)S(1)}, f32[72,256]{1,0:T(8,128)S(1)}) custom-call(s32[4]{0:T(128)S(1)} %pad_add_fusion.info, f32[4,264,256]{2,1,0:T(8,128)S(1)} %get-tuple-element.55.own, f32[4,264,256]{2,1,0:T(8,128)S(1)} %collective-permute-done.14.sibling, f32[2,136,256]{2,1,0:T(8,128)S(1)} %collective-permute-done.15.refs_0_, ...), custom_call_target="tpu_custom_call" | custom-call | tf_op jit(solution)/shard_map/refine_half/pallas_call | solution.py:370
  93.4 0.5 collective-permute-start.22
  94.0 0.6 collective-permute-start.20
  94.6 1.3 %collective-permute-start.21 = (f32[128,256]{1,0:T(8,128)S(1)}, f32[128,256]{1,0:T(8,128)S(1)}, u32[]{:S(2)}, u32[]{:S(2)}) collective-permute-start(f32[128,256]{1,0:T(8,128)S(1)} %get-tuple-element.70), channel_id=1, source_target_pairs={{0,16},{4,20},{8,24},{12,28},{16,0},{20,4},{24,8},{28,12},{1,17},{... | collective-permute-start | bytes 393224 | tf_op jit(solution)/shard_map/ppermute | solution.py:89
  95.9 2.3 %collective-permute-done.22 = f32[104,256]{1,0:T(8,128)S(1)} collective-permute-done((f32[104,256]{1,0:T(8,128)S(1)}, f32[104,256]{1,0:T(8,128)S(1)}, u32[]{:S(2)}, u32[]{:S(2)}) %collective-permute-start.22) | collective-permute-done | bytes 106528 | tf_op jit(solution)/shard_map/ppermute | solution.py:89
  98.3 0.7 collective-permute-done.20
  99.0 1.4 %collective-permute-done.21 = f32[128,256]{1,0:T(8,128)S(1)} collective-permute-done((f32[128,256]{1,0:T(8,128)S(1)}, f32[128,256]{1,0:T(8,128)S(1)}, u32[]{:S(2)}, u32[]{:S(2)}) %collective-permute-start.21) | collective-permute-done | bytes 131104 | tf_op jit(solution)/shard_map/ppermute | solution.py:89
  100.4 1.3 %collective-permute-start.24 = (f32[128,256]{1,0:T(8,128)S(1)}, f32[128,256]{1,0:T(8,128)S(1)}, u32[]{:S(2)}, u32[]{:S(2)}) collective-permute-start(f32[128,256]{1,0:T(8,128)S(1)} %collective-permute-done.20), channel_id=1, source_target_pairs={{0,16},{4,20},{8,24},{12,28},{16,0},{20,4},{24,8},{28,12},{1,17},{... | collective-permute-start | bytes 393224 | tf_op jit(solution)/shard_map/ppermute | solution.py:89
  101.8 1.5 %collective-permute-start.23 = (f32[128,256]{1,0:T(8,128)S(1)}, f32[128,256]{1,0:T(8,128)S(1)}, u32[]{:S(2)}, u32[]{:S(2)}) collective-permute-start(f32[128,256]{1,0:T(8,128)S(1)} %collective-permute-done.21), channel_id=1, source_target_pairs={{0,8},{4,12},{8,0},{12,4},{16,24},{20,28},{24,16},{28,20},{1,9},{5... | collective-permute-start | bytes 393224 | tf_op jit(solution)/shard_map/ppermute | solution.py:89
  103.2 0.9 collective-permute-start.26
  104.1 0.5 collective-permute-start.25
  104.5 2.6 %collective-permute-done.27 = f32[104,256]{1,0:T(8,128)S(1)} collective-permute-done((f32[104,256]{1,0:T(8,128)S(1)}, f32[104,256]{1,0:T(8,128)S(1)}, u32[]{:S(2)}, u32[]{:S(2)}) %collective-permute-start.27) | collective-permute-done | bytes 106528 | tf_op jit(solution)/shard_map/ppermute | solution.py:89
  107.2 2.2 %collective-permute-start.30 = (f32[72,256]{1,0:T(8,128)S(1)}, f32[72,256]{1,0:T(8,128)S(1)}, u32[]{:S(2)}, u32[]{:S(2)}) collective-permute-start(f32[72,256]{1,0:T(8,128)S(1)} %slice_add_fusion.12), channel_id=1, source_target_pairs={{0,24},{4,28},{8,16},{12,20},{16,8},{20,12},{24,0},{28,4},{1,25},{... | collective-permute-start | bytes 221192 | tf_op jit(solution)/shard_map/ppermute | solution.py:89
  109.4 0.9 collective-permute-start.29
  110.4 0.5 collective-permute-start.28
  110.9 0.1 collective-permute-start.31
  111.0 0.6 collective-permute-start.32
  111.6 0.9 collective-permute-done.30
  112.5 1.4 %collective-permute-done.29 = f32[72,256]{1,0:T(8,128)S(1)} collective-permute-done((f32[72,256]{1,0:T(8,128)S(1)}, f32[72,256]{1,0:T(8,128)S(1)}, u32[]{:S(2)}, u32[]{:S(2)}) %collective-permute-start.29) | collective-permute-done | bytes 73760 | tf_op jit(solution)/shard_map/ppermute | solution.py:89
  113.8 0.9 collective-permute-done.28
  114.8 0.1 collective-permute-start.33
  114.8 0.7 maximum_multiply_fusion
  115.5 0.9 collective-permute-done.33.refs_5_
  116.4 2.1 %place_blocks.1 = (f32[512,1024]{1,0:T(8,128)}, f32[64,1024]{1,0:T(8,128)}) custom-call(s32[4]{0:T(128)S(1)} %pad_add_fusion.info, f32[4,128,256]{2,1,0:T(8,128)S(1)} %pad_maximum_fusion.refs_0_, f32[4,128,256]{2,1,0:T(8,128)S(1)} %pad_maximum_fusion.1.refs_1_, f32[4,72,256]{2,1,0:T(8,128)S(1)} %pad_maximum_fusion.2.refs_2_, ...), custom_call_target="tpu_custom_call" | custom-call | tf_op jit(solution)/shard_map/place_blocks/pallas_call | solution.py:469
  (63 shorter events, 0.8 us)
Async XLA Ops:
  0.7 13.0 %copy-start.2 = (f32[512,1024]{1,0:T(8,128)S(1)}, f32[512,1024]{1,0:T(8,128)}, u32[]{:S(2)}) copy-start(f32[512,1024]{1,0:T(8,128)} %fine.3) | copy-start | bytes 6291460
  0.7 13.0 %copy-start.3 = (s32[2,4096]{1,0:T(2,128)S(1)}, s32[2,4096]{1,0:T(2,128)}, u32[]{:S(2)}) copy-start(s32[2,4096]{1,0:T(2,128)} %assign.7) | copy-start | bytes 98308
  13.2 8.1 %collective-permute-start = (f32[4,264,256]{2,1,0:T(8,128)S(1)}, f32[4,264,256]{2,1,0:T(8,128)S(1)}, u32[]{:S(2)}, u32[]{:S(2)}) collective-permute-start(f32[4,264,256]{2,1,0:T(8,128)S(1)} %get-tuple-element.43), channel_id=1, source_target_pairs={{0,4},{4,0},{8,12},{12,8},{16,20},{20,16},{24,28},{28,24},{1,5},{5... | collective-permute-start | bytes 3244040 | tf_op jit(solution)/shard_map/ppermute | solution.py:89
  21.4 15.5 %copy-start = (f32[64,1024]{1,0:T(8,128)S(1)}, f32[64,1024]{1,0:T(8,128)}, u32[]{:S(2)}) copy-start(f32[64,1024]{1,0:T(8,128)} %refs_5_.1) | copy-start | bytes 786436
  21.4 15.5 %copy-start.1 = (s32[512]{0:T(512)S(1)}, s32[512]{0:T(512)}, u32[]{:S(2)}) copy-start(s32[512]{0:T(512)} %param.9) | copy-start | bytes 6148
  21.5 7.1 %collective-permute-start.1 = (f32[2,136,256]{2,1,0:T(8,128)S(1)}, f32[2,136,256]{2,1,0:T(8,128)S(1)}, u32[]{:S(2)}, u32[]{:S(2)}) collective-permute-start(f32[2,136,256]{2,1,0:T(8,128)S(1)} %slice_add_fusion.1), channel_id=1, source_target_pairs={{0,8},{4,20},{8,0},{12,28},{16,24},{20,4},{24,16},{28,12},{1,9},{5... | collective-permute-start | bytes 835592 | tf_op jit(solution)/shard_map/ppermute | solution.py:94
  24.1 7.5 %collective-permute-start.2 = (f32[2,128,256]{2,1,0:T(8,128)S(1)}, f32[2,128,256]{2,1,0:T(8,128)S(1)}, u32[]{:S(2)}, u32[]{:S(2)}) collective-permute-start(f32[2,128,256]{2,1,0:T(8,128)S(1)} %slice_add_fusion.3), channel_id=1, source_target_pairs={{0,8},{4,20},{8,0},{12,28},{16,24},{20,4},{24,16},{28,12},{1,9},{5... | collective-permute-start | bytes 786440 | tf_op jit(solution)/shard_map/ppermute | solution.py:94
  28.6 8.3 %collective-permute-start.3 = (f32[136,256]{1,0:T(8,128)S(1)}, f32[136,256]{1,0:T(8,128)S(1)}, u32[]{:S(2)}, u32[]{:S(2)}) collective-permute-start(f32[136,256]{1,0:T(8,128)S(1)} %fusion.1), channel_id=1, source_target_pairs={{0,16},{4,12},{8,24},{12,4},{16,0},{20,28},{24,8},{28,20},{1,17},{... | collective-permute-start | bytes 417800 | tf_op jit(solution)/shard_map/ppermute | solution.py:99
  31.6 5.3 %collective-permute-start.4 = (f32[128,256]{1,0:T(8,128)S(1)}, f32[128,256]{1,0:T(8,128)S(1)}, u32[]{:S(2)}, u32[]{:S(2)}) collective-permute-start(f32[128,256]{1,0:T(8,128)S(1)} %fusion.3), channel_id=1, source_target_pairs={{0,16},{4,12},{8,24},{12,4},{16,0},{20,28},{24,8},{28,20},{1,17},{... | collective-permute-start | bytes 393224 | tf_op jit(solution)/shard_map/ppermute | solution.py:99
  38.4 6.2 %collective-permute-start.5 = (f32[128,256]{1,0:T(8,128)S(1)}, f32[128,256]{1,0:T(8,128)S(1)}, u32[]{:S(2)}, u32[]{:S(2)}) collective-permute-start(f32[128,256]{1,0:T(8,128)S(1)} %get-tuple-element.46), channel_id=1, source_target_pairs={{0,8},{4,12},{8,0},{12,4},{16,24},{20,28},{24,16},{28,20},{1,9},{5... | collective-permute-start | bytes 393224 | tf_op jit(solution)/shard_map/ppermute | solution.py:89
  40.5 6.1 %collective-permute-start.6 = (f32[128,256]{1,0:T(8,128)S(1)}, f32[128,256]{1,0:T(8,128)S(1)}, u32[]{:S(2)}, u32[]{:S(2)}) collective-permute-start(f32[128,256]{1,0:T(8,128)S(1)} %get-tuple-element.47), channel_id=1, source_target_pairs={{0,16},{4,20},{8,24},{12,28},{16,0},{20,4},{24,8},{28,12},{1,17},{... | collective-permute-start | bytes 393224 | tf_op jit(solution)/shard_map/ppermute | solution.py:89
  42.1 9.6 %collective-permute-start.9 = (f32[128,256]{1,0:T(8,128)S(1)}, f32[128,256]{1,0:T(8,128)S(1)}, u32[]{:S(2)}, u32[]{:S(2)}) collective-permute-start(f32[128,256]{1,0:T(8,128)S(1)} %get-tuple-element.47), channel_id=1, source_target_pairs={{0,8},{4,12},{8,0},{12,4},{16,24},{20,28},{24,16},{28,20},{1,9},{5... | collective-permute-start | bytes 393224 | tf_op jit(solution)/shard_map/ppermute | solution.py:89
  42.6 9.1 %collective-permute-start.10 = (f32[128,256]{1,0:T(8,128)S(1)}, f32[128,256]{1,0:T(8,128)S(1)}, u32[]{:S(2)}, u32[]{:S(2)}) collective-permute-start(f32[128,256]{1,0:T(8,128)S(1)} %get-tuple-element.46), channel_id=1, source_target_pairs={{0,16},{4,20},{8,24},{12,28},{16,0},{20,4},{24,8},{28,12},{1,17},{... | collective-permute-start | bytes 393224 | tf_op jit(solution)/shard_map/ppermute | solution.py:89
  44.7 7.0 %collective-permute-start.8 = (f32[128,256]{1,0:T(8,128)S(1)}, f32[128,256]{1,0:T(8,128)S(1)}, u32[]{:S(2)}, u32[]{:S(2)}) collective-permute-start(f32[128,256]{1,0:T(8,128)S(1)} %collective-permute-done.5), channel_id=1, source_target_pairs={{0,16},{4,20},{8,24},{12,28},{16,0},{20,4},{24,8},{28,12},{1,17},{... | collective-permute-start | bytes 393224 | tf_op jit(solution)/shard_map/ppermute | solution.py:89
  46.6 5.0 %collective-permute-start.7 = (f32[128,256]{1,0:T(8,128)S(1)}, f32[128,256]{1,0:T(8,128)S(1)}, u32[]{:S(2)}, u32[]{:S(2)}) collective-permute-start(f32[128,256]{1,0:T(8,128)S(1)} %collective-permute-done.6), channel_id=1, source_target_pairs={{0,8},{4,12},{8,0},{12,4},{16,24},{20,28},{24,16},{28,20},{1,9},{5... | collective-permute-start | bytes 393224 | tf_op jit(solution)/shard_map/ppermute | solution.py:89
  51.7 13.4 %collective-permute-start.11 = (f32[8,128,256]{2,1,0:T(8,128)S(1)}, f32[8,128,256]{2,1,0:T(8,128)S(1)}, u32[]{:S(2)}, u32[]{:S(2)}) collective-permute-start(f32[8,128,256]{2,1,0:T(8,128)S(1)} %bitcast_dynamic-update-slice_fusion.fine), channel_id=1, source_target_pairs={{0,4},{4,0},{8,12},{12,8},{16,20},{20,16},{24,28},{28,24},{1,5},{5... | collective-permute-start | bytes 3145736 | tf_op jit(solution)/shard_map/ppermute | solution.py:89
  51.8 13.3 %copy-start.4 = (s32[2,4096]{1,0:T(2,128)S(1)}, s32[2,4096]{1,0:T(2,128)}, u32[]{:S(2)}) copy-start(s32[2,4096]{1,0:T(2,128)} %assign.7) | copy-start | bytes 98308
  51.8 12.6 %collective-permute-start.12 = (f32[104,256]{1,0:T(8,128)S(1)}, f32[104,256]{1,0:T(8,128)S(1)}, u32[]{:S(2)}, u32[]{:S(2)}) collective-permute-start(f32[104,256]{1,0:T(8,128)S(1)} %pad_maximum_fusion.3), channel_id=1, source_target_pairs={{0,1},{1,0},{2,3},{3,2},{4,5},{5,4},{6,7},{7,6},{8,9},{9,8},{10,11... | collective-permute-start | bytes 319496 | tf_op jit(solution)/shard_map/ppermute | solution.py:89
  64.5 8.5 %collective-permute-start.14 = (f32[4,264,256]{2,1,0:T(8,128)S(1)}, f32[4,264,256]{2,1,0:T(8,128)S(1)}, u32[]{:S(2)}, u32[]{:S(2)}) collective-permute-start(f32[4,264,256]{2,1,0:T(8,128)S(1)} %get-tuple-element.56), channel_id=1, source_target_pairs={{0,4},{4,0},{8,12},{12,8},{16,20},{20,16},{24,28},{28,24},{1,5},{5... | collective-permute-start | bytes 3244040 | tf_op jit(solution)/shard_map/ppermute | solution.py:89
  64.8 8.2 %collective-permute-start.13 = (f32[72,256]{1,0:T(8,128)S(1)}, f32[72,256]{1,0:T(8,128)S(1)}, u32[]{:S(2)}, u32[]{:S(2)}) collective-permute-start(f32[72,256]{1,0:T(8,128)S(1)} %slice_add_fusion.15), channel_id=1, source_target_pairs={{0,4},{4,0},{8,12},{12,8},{16,20},{20,16},{24,28},{28,24},{1,5},{5... | collective-permute-start | bytes 221192 | tf_op jit(solution)/shard_map/ppermute | solution.py:89
  73.1 8.2 %collective-permute-start.19 = (f32[104,256]{1,0:T(8,128)S(1)}, f32[104,256]{1,0:T(8,128)S(1)}, u32[]{:S(2)}, u32[]{:S(2)}) collective-permute-start(f32[104,256]{1,0:T(8,128)S(1)} %pad_maximum_fusion.4), channel_id=1, source_target_pairs={{0,2},{1,3},{2,0},{3,1},{4,6},{5,7},{6,4},{7,5},{8,10},{9,11},{10,... | collective-permute-start | bytes 319496 | tf_op jit(solution)/shard_map/ppermute | solution.py:89
  75.8 11.0 %collective-permute-start.15 = (f32[2,136,256]{2,1,0:T(8,128)S(1)}, f32[2,136,256]{2,1,0:T(8,128)S(1)}, u32[]{:S(2)}, u32[]{:S(2)}) collective-permute-start(f32[2,136,256]{2,1,0:T(8,128)S(1)} %slice_add_fusion), channel_id=1, source_target_pairs={{0,8},{4,20},{8,0},{12,28},{16,24},{20,4},{24,16},{28,12},{1,9},{5... | collective-permute-start | bytes 835592 | tf_op jit(solution)/shard_map/ppermute | solution.py:94
  76.6 8.6 %collective-permute-start.16 = (f32[2,128,256]{2,1,0:T(8,128)S(1)}, f32[2,128,256]{2,1,0:T(8,128)S(1)}, u32[]{:S(2)}, u32[]{:S(2)}) collective-permute-start(f32[2,128,256]{2,1,0:T(8,128)S(1)} %slice_add_fusion.2), channel_id=1, source_target_pairs={{0,8},{4,20},{8,0},{12,28},{16,24},{20,4},{24,16},{28,12},{1,9},{5... | collective-permute-start | bytes 786440 | tf_op jit(solution)/shard_map/ppermute | solution.py:94
  85.2 5.0 %collective-permute-start.18 = (f32[128,256]{1,0:T(8,128)S(1)}, f32[128,256]{1,0:T(8,128)S(1)}, u32[]{:S(2)}, u32[]{:S(2)}) collective-permute-start(f32[128,256]{1,0:T(8,128)S(1)} %fusion.2), channel_id=1, source_target_pairs={{0,16},{4,12},{8,24},{12,4},{16,0},{20,28},{24,8},{28,20},{1,17},{... | collective-permute-start | bytes 393224 | tf_op jit(solution)/shard_map/ppermute | solution.py:99
  86.8 5.1 %collective-permute-start.17 = (f32[136,256]{1,0:T(8,128)S(1)}, f32[136,256]{1,0:T(8,128)S(1)}, u32[]{:S(2)}, u32[]{:S(2)}) collective-permute-start(f32[136,256]{1,0:T(8,128)S(1)} %fusion), channel_id=1, source_target_pairs={{0,16},{4,12},{8,24},{12,4},{16,0},{20,28},{24,8},{28,20},{1,17},{... | collective-permute-start | bytes 417800 | tf_op jit(solution)/shard_map/ppermute | solution.py:99
  93.4 4.8 %collective-permute-start.22 = (f32[104,256]{1,0:T(8,128)S(1)}, f32[104,256]{1,0:T(8,128)S(1)}, u32[]{:S(2)}, u32[]{:S(2)}) collective-permute-start(f32[104,256]{1,0:T(8,128)S(1)} %pad_maximum_fusion.5), channel_id=1, source_target_pairs={{0,1},{1,0},{2,3},{3,2},{4,5},{5,4},{6,7},{7,6},{8,9},{9,8},{10,11... | collective-permute-start | bytes 319496 | tf_op jit(solution)/shard_map/ppermute | solution.py:89
  94.0 5.0 %collective-permute-start.20 = (f32[128,256]{1,0:T(8,128)S(1)}, f32[128,256]{1,0:T(8,128)S(1)}, u32[]{:S(2)}, u32[]{:S(2)}) collective-permute-start(f32[128,256]{1,0:T(8,128)S(1)} %get-tuple-element.71), channel_id=1, source_target_pairs={{0,8},{4,12},{8,0},{12,4},{16,24},{20,28},{24,16},{28,20},{1,9},{5... | collective-permute-start | bytes 393224 | tf_op jit(solution)/shard_map/ppermute | solution.py:89
  94.6 5.8 %collective-permute-start.21 = (f32[128,256]{1,0:T(8,128)S(1)}, f32[128,256]{1,0:T(8,128)S(1)}, u32[]{:S(2)}, u32[]{:S(2)}) collective-permute-start(f32[128,256]{1,0:T(8,128)S(1)} %get-tuple-element.70), channel_id=1, source_target_pairs={{0,16},{4,20},{8,24},{12,28},{16,0},{20,4},{24,8},{28,12},{1,17},{... | collective-permute-start | bytes 393224 | tf_op jit(solution)/shard_map/ppermute | solution.py:89
  100.4 6.7 %collective-permute-start.27 = (f32[104,256]{1,0:T(8,128)S(1)}, f32[104,256]{1,0:T(8,128)S(1)}, u32[]{:S(2)}, u32[]{:S(2)}) collective-permute-start(f32[104,256]{1,0:T(8,128)S(1)} %pad_maximum_fusion.6), channel_id=1, source_target_pairs={{0,2},{1,3},{2,0},{3,1},{4,6},{5,7},{6,4},{7,5},{8,10},{9,11},{10,... | collective-permute-start | bytes 319496 | tf_op jit(solution)/shard_map/ppermute | solution.py:89
  100.4 9.0 %collective-permute-start.24 = (f32[128,256]{1,0:T(8,128)S(1)}, f32[128,256]{1,0:T(8,128)S(1)}, u32[]{:S(2)}, u32[]{:S(2)}) collective-permute-start(f32[128,256]{1,0:T(8,128)S(1)} %collective-permute-done.20), channel_id=1, source_target_pairs={{0,16},{4,20},{8,24},{12,28},{16,0},{20,4},{24,8},{28,12},{1,17},{... | collective-permute-start | bytes 393224 | tf_op jit(solution)/shard_map/ppermute | solution.py:89
  101.8 8.6 %collective-permute-start.23 = (f32[128,256]{1,0:T(8,128)S(1)}, f32[128,256]{1,0:T(8,128)S(1)}, u32[]{:S(2)}, u32[]{:S(2)}) collective-permute-start(f32[128,256]{1,0:T(8,128)S(1)} %collective-permute-done.21), channel_id=1, source_target_pairs={{0,8},{4,12},{8,0},{12,4},{16,24},{20,28},{24,16},{28,20},{1,9},{5... | collective-permute-start | bytes 393224 | tf_op jit(solution)/shard_map/ppermute | solution.py:89
  103.2 7.6 %collective-permute-start.26 = (f32[128,256]{1,0:T(8,128)S(1)}, f32[128,256]{1,0:T(8,128)S(1)}, u32[]{:S(2)}, u32[]{:S(2)}) collective-permute-start(f32[128,256]{1,0:T(8,128)S(1)} %get-tuple-element.71), channel_id=1, source_target_pairs={{0,16},{4,20},{8,24},{12,28},{16,0},{20,4},{24,8},{28,12},{1,17},{... | collective-permute-start | bytes 393224 | tf_op jit(solution)/shard_map/ppermute | solution.py:89
  104.1 6.9 %collective-permute-start.25 = (f32[128,256]{1,0:T(8,128)S(1)}, f32[128,256]{1,0:T(8,128)S(1)}, u32[]{:S(2)}, u32[]{:S(2)}) collective-permute-start(f32[128,256]{1,0:T(8,128)S(1)} %get-tuple-element.70), channel_id=1, source_target_pairs={{0,8},{4,12},{8,0},{12,4},{16,24},{20,28},{24,16},{28,20},{1,9},{5... | collective-permute-start | bytes 393224 | tf_op jit(solution)/shard_map/ppermute | solution.py:89
  107.2 5.3 %collective-permute-start.30 = (f32[72,256]{1,0:T(8,128)S(1)}, f32[72,256]{1,0:T(8,128)S(1)}, u32[]{:S(2)}, u32[]{:S(2)}) collective-permute-start(f32[72,256]{1,0:T(8,128)S(1)} %slice_add_fusion.12), channel_id=1, source_target_pairs={{0,24},{4,28},{8,16},{12,20},{16,8},{20,12},{24,0},{28,4},{1,25},{... | collective-permute-start | bytes 221192 | tf_op jit(solution)/shard_map/ppermute | solution.py:89
  109.4 4.4 %collective-permute-start.29 = (f32[72,256]{1,0:T(8,128)S(1)}, f32[72,256]{1,0:T(8,128)S(1)}, u32[]{:S(2)}, u32[]{:S(2)}) collective-permute-start(f32[72,256]{1,0:T(8,128)S(1)} %slice_add_fusion.12), channel_id=1, source_target_pairs={{0,16},{4,20},{8,24},{12,28},{16,0},{20,4},{24,8},{28,12},{1,17},{... | collective-permute-start | bytes 221192 | tf_op jit(solution)/shard_map/ppermute | solution.py:89
  110.4 4.4 %collective-permute-start.28 = (f32[72,256]{1,0:T(8,128)S(1)}, f32[72,256]{1,0:T(8,128)S(1)}, u32[]{:S(2)}, u32[]{:S(2)}) collective-permute-start(f32[72,256]{1,0:T(8,128)S(1)} %slice_add_fusion.12), channel_id=1, source_target_pairs={{0,8},{4,12},{8,0},{12,4},{16,24},{20,28},{24,16},{28,20},{1,9},{5... | collective-permute-start | bytes 221192 | tf_op jit(solution)/shard_map/ppermute | solution.py:89
  110.9 5.5 %collective-permute-start.31 = (f32[4,128,256]{2,1,0:T(8,128)S(1)}, f32[4,128,256]{2,1,0:T(8,128)S(1)}, u32[]{:S(2)}, u32[]{:S(2)}) collective-permute-start(f32[4,128,256]{2,1,0:T(8,128)S(1)} %pad_maximum_fusion.refs_0_), channel_id=1, source_target_pairs={{0,4},{4,0},{8,12},{12,8},{16,20},{20,16},{24,28},{28,24},{1,5},{5... | collective-permute-start | bytes 1572872 | tf_op jit(solution)/shard_map/ppermute | solution.py:89
  111.0 5.4 %collective-permute-start.32 = (f32[4,128,256]{2,1,0:T(8,128)S(1)}, f32[4,128,256]{2,1,0:T(8,128)S(1)}, u32[]{:S(2)}, u32[]{:S(2)}) collective-permute-start(f32[4,128,256]{2,1,0:T(8,128)S(1)} %pad_maximum_fusion.1.refs_1_), channel_id=1, source_target_pairs={{0,4},{4,0},{8,12},{12,8},{16,20},{20,16},{24,28},{28,24},{1,5},{5... | collective-permute-start | bytes 1572872 | tf_op jit(solution)/shard_map/ppermute | solution.py:89
  114.8 1.6 %collective-permute-start.33 = (f32[4,72,256]{2,1,0:T(8,128)S(1)}, f32[4,72,256]{2,1,0:T(8,128)S(1)}, u32[]{:S(2)}, u32[]{:S(2)}) collective-permute-start(f32[4,72,256]{2,1,0:T(8,128)S(1)} %pad_maximum_fusion.2.refs_2_), channel_id=1, source_target_pairs={{0,4},{4,0},{8,12},{12,8},{16,20},{20,16},{24,28},{28,24},{1,5},{5... | collective-permute-start | bytes 884744 | tf_op jit(solution)/shard_map/ppermute | solution.py:89

commit v15 on v14

--- a/solution.py
+++ b/solution.py
@@ -124,7 +124,7 @@
 def pass_body(info, points, assign, fine, *refs, pass_index, flip, stream, chained, tile):
     refs = list(refs)
     initial = pass_index == 0
-    first = initial and stream
+    first = stream
     squares_in = None if first else refs.pop(0)
     seen_in = refs.pop(0) if chained else None
     payload, seen = refs.pop(0), refs.pop(0)
@@ -148,8 +148,9 @@
         start = block_of(info, slot, core) * block_width
         return pl.ds(pl.multiple_of(start, block_width), block_width)
 
-    def load(i):
-        return pltpu.make_async_copy(points.at[span(i)], kept.at[span(i)], point_sems.at[i])
+    def load(i, half):
+        part = pl.ds(pl.multiple_of(i * tile + half * (tile // 2), tile // 2), tile // 2)
+        return pltpu.make_async_copy(points.at[part], kept.at[part], point_sems.at[2 * i + half])
 
     if first:
         load_start = pltpu.make_async_copy(
@@ -157,7 +158,8 @@
         )
         load_start.start()
     if stream:
-        load(0).start()
+        load(0, 0).start()
+        load(0, 1).start()
         load_assign = pltpu.make_async_copy(assign, chosen_in, small_sems.at[0])
         load_assign.start()
 
@@ -225,10 +227,11 @@
         )
 
     def arrive(i, more):
-        if stream:
-            load(i).wait()
-            if more:
-                load(i + 1).start()
+        for half in range(2):
+            if stream:
+                load(i, half).wait()
+                if more:
+                    load(i + 1, half).start()
 
     if stream:
         load_assign.wait()
@@ -258,16 +261,46 @@
         payload[slot, mid + TAIL :, :] = sums[mid:, columns]
 
 
+def fetch_body(points, *refs):
+    *_, kept, sems = refs
+    share = points.shape[0] // sems.shape[0]
+    copies = [
+        pltpu.make_async_copy(
+            points.at[i * share : (i + 1) * share], kept.at[i * share : (i + 1) * share], sems.at[i]
+        )
+        for i in range(sems.shape[0])
+    ]
+    for copy in copies:
+        copy.start()
+    for copy in copies:
+        copy.wait()
+
+
+def fetch(points, after):
+    return pl.pallas_call(
+        fetch_body,
+        out_shape=pltpu.VMEM(points.shape, points.dtype),
+        in_specs=[AWAY] + [HERE] * len(after),
+        out_specs=HERE,
+        scratch_shapes=[pltpu.SemaphoreType.DMA((8,))],
+        compiler_params=pltpu.CompilerParams(vmem_limit_bytes=2 * 2**20),
+        cost_estimate=pl.CostEstimate(
+            flops=0, bytes_accessed=4 * points.size, transcendentals=0
+        ),
+        name="fetch_points",
+    )(far_off(points), *[near_by(value) for value in after])
+
+
 def run_pass(info, points, fine_assign, fine, squares, seen, *, pass_index, flip, rows):
     count, width = points.shape
     block_width = width // SLOTS
     tile = 1024
     initial = pass_index == 0
     chained = seen is not None
-    stream = not chained
+    stream = squares is None
     if stream:
-        in_specs = [AWAY, AWAY, AWAY if initial else HERE]
-        args = [far_off(points), far_off(fine_assign), far_off(fine) if initial else near_by(fine)]
+        in_specs = [AWAY] * 3
+        args = [far_off(points), far_off(fine_assign), far_off(fine)]
     else:
         in_specs = [HERE] * 3
         args = [near_by(points), near_by(fine_assign), near_by(fine)]
@@ -292,7 +325,7 @@
         scratch += [
             pltpu.VMEM((PASSES, count), jnp.int32),
             pltpu.SemaphoreType.DMA((2,)),
-            pltpu.SemaphoreType.DMA((count // tile,)),
+            pltpu.SemaphoreType.DMA((2 * count // tile,)),
         ]
         if initial:
             scratch.append(pltpu.VMEM((rows, width), jnp.float32))
@@ -320,15 +353,17 @@
 
 
 def refine_body(info, own, sibling, *refs, flip):
-    first_top, first_low, second_top, second_low, owners, coarse_in, top, low, part = refs
+    first_top, first_low, second_top, second_low, owners, *coarse_in, top, low, part = refs
     rows = owners.shape[2]
     mid = rows // 2
     block_width = part.shape[1]
     owner = owners[info[1] ^ flip]
-    if coarse_in.shape[1] == block_width:
-        coarse = coarse_in[...]
+    if len(coarse_in) == 1:
+        column = pl.multiple_of(info[0] * block_width, block_width)
+        coarse = coarse_in[0][:, pl.ds(column, block_width)]
     else:
-        coarse = coarse_in[:, pl.ds(pl.multiple_of(info[0] * block_width, block_width), block_width)]
+        sums = coarse_in[0][: NC + TAIL, :] + coarse_in[1][: NC + TAIL, :]
+        coarse = sums[:NC] / as_column(sums[NC : NC + 1, :128], 128)[:NC, :1]
     head = own[0, : mid + TAIL, :] + sibling[0, : mid + TAIL, :]
     rest = own[0, mid + TAIL :, :] + sibling[0, mid + TAIL :, :]
     head = head + (first_top[0] + second_top[...])
@@ -365,7 +400,7 @@
 def refine_half(info, own, sibling, incoming, owners, coarse, *, flip):
     _, rows, block_width = own.shape
     mid = (rows - TAIL) // 2
-    args = [near_by(value) for value in (own, sibling, *incoming, owners, coarse)]
+    args = [near_by(value) for value in (own, sibling, *incoming, owners, *coarse)]
     shapes = [(mid, block_width), (mid, block_width), (NC + TAIL, block_width)]
     return pl.pallas_call(
         functools.partial(refine_body, flip=flip),
@@ -377,33 +412,36 @@
     )(info, *args)
 
 
-def exchange(held, sibling, later=()):
+def exchange(held, sibling, folded=None):
     cut = (held.shape[1] - TAIL) // 2 + TAIL
     chunks = slice(0, cut), slice(cut, None)
     first = [held[1::2, rows] + sibling[1::2, rows] for rows in chunks]
-    first, later = lax.optimization_barrier((first, later))
+    first, folded = lax.optimization_barrier((first, folded))
     first = [swap_first(chunk) for chunk in first]
+    if folded is not None:
+        folded = swap(folded, lax.axis_size("cen") // 2, "cen")
+        first[1], folded = lax.optimization_barrier((first[1], folded))
     second = [
         swap_second(held[2, rows] + sibling[2, rows] + arrived[1])
         for rows, arrived in zip(chunks, first)
     ]
-    return [*first, *second], later
+    return [*first, *second], folded
 
 
 PIECES = ((1, 1), (2, 0), (3, 0), (3, 1), (1, 0), (2, 1), (0, 0), (0, 1))
 
 
-def gather_half(top, low, later=None):
+def gather_half(top, low, later=False):
     x_low = swap(low, ACROSS_X)
     y_top = swap(top, ACROSS_Y)
     again = top, low
-    if later is not None:
-        x_low, y_top, again, later = lax.optimization_barrier((x_low, y_top, again, later))
+    if later:
+        x_low, y_top, again = lax.optimization_barrier((x_low, y_top, again))
     x_top = swap(again[0], ACROSS_X)
     y_low = swap(again[1], ACROSS_Y)
     corner_top = swap(y_top, ACROSS_X)
     corner_low = swap(x_low, ACROSS_Y)
-    return [x_low, y_top, corner_top, corner_low, x_top, y_low, top, low], later
+    return [x_low, y_top, corner_top, corner_low, x_top, y_low, top, low]
 
 
 def spread(value):
@@ -425,41 +463,22 @@
 
 
 def place_body(info, *refs, flip):
-    own, other = refs[:3], refs[3:6]
-    fine_out, coarse_out, fine_held, coarse_held, sems = refs[6:]
-    block_width = coarse_out.shape[1] // SLOTS
+    fine_out, held, sems = refs[4:]
     rows = fine_out.shape[0] // 2
     mid = rows // 2
-    half = info[1] ^ flip
-
-    def column_of(slot, core):
-        start = block_of(info, slot, core) * block_width
-        return pl.ds(pl.multiple_of(start, block_width), block_width)
-
-    def put(at, *groups):
+    block_width = fine_out.shape[1] // SLOTS
+    sends = []
+    for at in range(2):
         for piece, (slot, is_low) in enumerate(PIECES):
-            part = slice(is_low * mid, (is_low + 1) * mid)
-            fine_held[at, part, column_of(slot, 0)] = groups[piece // SLOTS][piece % SLOTS]
-
-    def send(at, half):
+            block = refs[2 * at + piece // SLOTS][piece % SLOTS]
+            column = pl.multiple_of(block_of(info, slot, 0) * block_width, block_width)
+            held[at, is_low * mid : (is_low + 1) * mid, pl.ds(column, block_width)] = block
+        half = info[1] ^ flip ^ at
         span = pl.ds(pl.multiple_of(half * rows, rows), rows)
-        return pltpu.make_async_copy(fine_held.at[at], fine_out.at[span], sems.at[at])
-
-    put(0, *own[:2])
-    send(0, half).start()
-    put(1, *other[:2])
-    send(1, 1 - half).start()
-    parts, others = own[2], other[2]
-    weight = parts[0, NC:, :128] + others[0, NC:, :128]
-    weight = as_column(weight[:1], 128)[:NC, :1]
-    for slot in range(SLOTS):
-        total = parts[slot, :NC, :] + others[slot, :NC, :]
-        coarse_held[:, column_of(slot, 0)] = total / weight
-    send_coarse = pltpu.make_async_copy(coarse_held, coarse_out, sems.at[2])
-    send_coarse.start()
-    send(0, half).wait()
-    send(1, 1 - half).wait()
-    send_coarse.wait()
+        sends.append(pltpu.make_async_copy(held.at[at], fine_out.at[span], sems.at[at]))
+        sends[at].start()
+    for send in sends:
+        send.wait()
 
 
 def place(info, own, other, *, flip):
@@ -468,20 +487,37 @@
     args = [near_by(value) for value in (*own, *other)]
     return pl.pallas_call(
         functools.partial(place_body, flip=flip),
-        out_shape=[
-            jax.ShapeDtypeStruct((2 * rows, width), jnp.float32),
-            jax.ShapeDtypeStruct((NC, width), jnp.float32),
-        ],
+        out_shape=jax.ShapeDtypeStruct((2 * rows, width), jnp.float32),
         in_specs=[SCALARS] + [HERE] * len(args),
-        out_specs=[AWAY, AWAY],
+        out_specs=AWAY,
         scratch_shapes=[
             pltpu.VMEM((2, rows, width), jnp.float32),
-            pltpu.VMEM((NC, width), jnp.float32),
-            pltpu.SemaphoreType.DMA((3,)),
+            pltpu.SemaphoreType.DMA((2,)),
         ],
         compiler_params=pltpu.CompilerParams(vmem_limit_bytes=8 * 2**20),
-        name="place_blocks",
+        name="place_fine",
     )(info, *args)
+
+
+def place_coarse_body(info, parts, others, after, coarse_out):
+    block_width = parts.shape[2]
+    weight = parts[0, NC:, :128] + others[0, NC:, :128]
+    weight = as_column(weight[:1], 128)[:NC, :1]
+    for slot in range(SLOTS):
+        total = parts[slot, :NC, :] + others[slot, :NC, :]
+        column = pl.multiple_of(block_of(info, slot, 0) * block_width, block_width)
+        coarse_out[:, pl.ds(column, block_width)] = total / weight
+
+
+def place_coarse(info, parts, others, after):
+    return pl.pallas_call(
+        place_coarse_body,
+        out_shape=jax.ShapeDtypeStruct((NC, SLOTS * parts.shape[2]), jnp.float32),
+        in_specs=[SCALARS, HERE, HERE, AWAY],
+        out_specs=HERE,
+        compiler_params=pltpu.CompilerParams(vmem_limit_bytes=4 * 2**20),
+        name="place_coarse",
+    )(info, near_by(parts), near_by(others), far_off(after))
 
 
 def on_device_paired(points, fine_assign, fine_start, coarse_start, coarse_assign):
@@ -500,38 +536,41 @@
     held, seen_first = call(kept, fine_assign, fine_start, squares, seen, flip=0)
     incoming, _ = exchange(held, sibling)
     top, low, part = refine_half(
-        info, held, sibling, incoming, owners, coarse_start, flip=0
-    )
-    own = jnp.stack(gather_half(top, low)[0])
+        info, held, sibling, incoming, owners, [coarse_start], flip=0
+    )
+    own = gather_half(top, low)
+    own, kept = lax.optimization_barrier((own, fetch(points, own[:2])))
+    own = jnp.stack(own)
+    bits = range(lax.axis_size("cen").bit_length() - 1)
     folded = jnp.concatenate([part, seen_first.reshape(-1, block_width)], 0)
-    paired = swap(folded, 1, "cen")
+    folded = over_cen(folded, fold, bits[:1])
+    own, folded = lax.optimization_barrier((own, folded))
     other = swap(own, CORE)
 
     call = functools.partial(run_pass, info, pass_index=1, rows=rows)
-    sent, seen, kept = call(points, fine_assign, own, squares, None, flip=0)
-    sent, paired = lax.optimization_barrier((sent, paired))
+    sent, seen = call(kept, fine_assign, own, squares, None, flip=0)
     sibling = swap(sent, CORE)
-    folded = fold(folded, paired)
     part = folded[: NC + TAIL]
     others_part = swap(part, CORE)
     held, seen_second = call(kept, fine_assign, other, squares, seen, flip=1)
     held, others_part = lax.optimization_barrier((held, others_part))
     folded = jnp.concatenate([part + others_part, folded[NC + TAIL :]], 0)
-    incoming, folded = exchange(held, sibling, folded)
-    bits = range(lax.axis_size("cen").bit_length() - 1)
-    folded = over_cen(folded, fold, bits[1:])
-    part, seen_first = folded[: NC + TAIL], folded[NC + TAIL :]
-    coarse = part[:NC] / part[NC, :NC][:, None]
-
-    top, low, part = refine_half(info, held, sibling, incoming, owners, coarse, flip=1)
+    folded = over_cen(folded, fold, bits[1:-1])
+    incoming, paired = exchange(held, sibling, folded)
+    seen_first = jnp.minimum(folded[NC + TAIL :], paired[NC + TAIL :])
+
+    top, low, part = refine_half(
+        info, held, sibling, incoming, owners, [folded, paired], flip=1
+    )
     folded = jnp.concatenate([part, seen_second.reshape(-1, block_width)], 0)
     top, low, folded = lax.optimization_barrier((top, low, folded))
-    folded = over_cen(folded, fold, bits[:1])
-    own, folded = gather_half(top, low, folded)
-    folded = over_cen(folded, fold, bits[1:])
+    own = gather_half(top, low, True)
+    folded = over_cen(folded, fold)
     part, seen_second = folded[: NC + TAIL], folded[NC + TAIL :]
-    blocks = [jnp.stack(own[:4]), jnp.stack(own[4:]), jnp.stack(spread(part))]
-    fine_now, coarse_now = place(info, blocks, [swap(block, CORE) for block in blocks], flip=1)
+    own = [jnp.stack(own[:4]), jnp.stack(own[4:])]
+    fine_now = place(info, own, [swap(group, CORE) for group in own], flip=1)
+    parts = jnp.stack(spread(part))
+    coarse_now = place_coarse(info, parts, swap(parts, CORE), fine_now)
 
     seen = [each.reshape(2, -1) for each in (seen_first, seen_second)]
     gaps = jnp.stack([each[0] - each[1] for each in seen]) / math.sqrt(width)
@@ -548,6 +587,7 @@
         fits = (
             mesh.shape["pts"] == 2 * SLOTS
             and centres & (centres - 1) == 0
+            and centres >= 4
             and width // SLOTS == local_count // 2
             and (width // SLOTS) % 128 == 0
             and count % 2048 == 0

time: 119 us -> 116 us (0.975)
  waiting for transfers between devices: 38.6 us -> 28.9 us
  starting transfers between devices: 33.3 us -> 37.1 us
  other arithmetic: 1.32 us -> 3.17 us
    ppermute x26, waiting for transfers between devices: 22.2 us -> 16.2 us  [swap(): return lax.ppermute(value, axis, [(i, i ^ bit) for i in range(size)])]
    pallas_call x1 -> x3, Pallas kernels: 2.1 us -> 6.85 us  [the longest x1 3.48 us: fetch(): pl.pallas_call(fetch_body, out_shape=pltpu.VMEM(points.shape, points.dtyp...]
    ppermute x26, starting transfers between devices: 21.9 us -> 25.9 us  [swap(): return lax.ppermute(value, axis, [(i, i ^ bit) for i in range(size)])]
    ppermute x4, waiting for transfers between devices: 9.11 us -> 5.21 us  [swap_first(): return lax.ppermute(value, 'pts', pairs)]
    pallas_call x4, Pallas kernels: 38.8 us -> 35.2 us  [run_pass(): pl.pallas_call(body, out_shape=out_shape, in_specs=[SCALARS, *in_specs],...]
    add x4, other arithmetic: 0.13 us -> 2.07 us  [exchange(): held[2, rows] + sibling[2, rows] + arrived[1]]
  transfers between devices with their start and end apart: 34 -> 34, of which waited for: 18 -> 12; matrix products, arithmetic and copies ran while one was open for 1% -> 2% of each run, Pallas kernels for 22% -> 25%
where the time goes in v15:
time: 116 us
  Pallas kernels  45.1 us (39%)
  starting transfers between devices  37.1 us (32%)
  waiting for transfers between devices  28.9 us (25%)
  other arithmetic  3.17 us (3%)
    pallas_call x4, Pallas kernels, run_pass(): pl.pallas_call(body, out_shape=out_shape, in_specs=[SCALARS, *in_specs],...  35.2 us
    ppermute x26, starting transfers between devices, swap(): return lax.ppermute(value, axis, [(i, i ^ bit) for i in range(size)])  25.9 us
    ppermute x26, waiting for transfers between devices, swap(): return lax.ppermute(value, axis, [(i, i ^ bit) for i in range(size)])  16.2 us
    ppermute x4, waiting for transfers between devices, swap_second(): return lax.ppermute(value, 'pts', pairs)  7.45 us
    ppermute x4, starting transfers between devices, swap_second(): return lax.ppermute(value, 'pts', pairs)  6.54 us
    ppermute x4, waiting for transfers between devices, swap_first(): return lax.ppermute(value, 'pts', pairs)  5.21 us
    ppermute x4, starting transfers between devices, swap_first(): return lax.ppermute(value, 'pts', pairs)  4.71 us
    pallas_call x1, Pallas kernels, fetch(): pl.pallas_call(fetch_body, out_shape=pltpu.VMEM(points.shape, points.dtyp...  3.48 us
  transfers between devices with their start and end apart: 34, of which 12 were waited for; matrix products, arithmetic and copies ran while one was open for 2% of the time, Pallas kernels for 25%

profile of v15, /device:TPU:0, one launch (start us, length us, event | category | flops | bytes accessed | tf_op | source)
XLA Modules:
  0.0 115.6 jit_solution(16362722597851556037)
XLA Ops:
  0.6 0.1 pad_add_fusion.info
  0.7 12.2 %energies_and_sums_00.1 = (f32[4,264,256]{2,1,0:T(8,128)S(1)}, f32[2,4096]{1,0:T(2,128)S(1)}, f32[1,4096]{1,0:T(1,128)S(1)}, bf16[4096,1024]{1,0:T(8,128)(2,1)S(1)}) custom-call(s32[4]{0:T(128)S(1)} %pad_add_fusion.info, bf16[4096,1024]{1,0:T(8,128)(2,1)} %points.3, s32[2,4096]{1,0:T(2,128)} %assign.7, f32[512,1024]{1,0:T(8,128)} %fine.3), custom_call_target="tpu_custom_call" | custom-call | flops 4294967296 | bytes 8388608 | tf_op jit(solution)/shard_map/energies_and_sums_00/pallas_call | solution.py:341
  12.9 0.6 collective-permute-start
  13.5 7.6 %energies_and_sums_01.1 = (f32[4,264,256]{2,1,0:T(8,128)S(1)}, f32[2,4096]{1,0:T(2,128)S(1)}) custom-call(s32[4]{0:T(128)S(1)} %pad_add_fusion.info, bf16[4096,1024]{1,0:T(8,128)(2,1)S(1)} %get-tuple-element.46.points, s32[2,4096]{1,0:T(2,128)S(1)} %copy-done.3, f32[512,1024]{1,0:T(8,128)S(1)} %copy-done.2, f32[1,4096]{1,0:T(1,128)S(1)} %get-tuple-element.47.refs_0_, ...), custom_call_target="tpu_custom_call" | custom-call | flops 4294967296 | bytes 8388608 | tf_op jit(solution)/shard_map/energies_and_sums_01/pallas_call | solution.py:341
  21.2 0.0 copy-start
  21.2 0.0 copy-start.1
  21.3 2.5 %collective-permute-start.1 = (f32[2,136,256]{2,1,0:T(8,128)S(1)}, f32[2,136,256]{2,1,0:T(8,128)S(1)}, u32[]{:S(2)}, u32[]{:S(2)}) collective-permute-start(f32[2,136,256]{2,1,0:T(8,128)S(1)} %slice_add_fusion.1), channel_id=1, source_target_pairs={{0,8},{4,20},{8,0},{12,28},{16,24},{20,4},{24,16},{28,12},{1,9},{5... | collective-permute-start | bytes 835592 | tf_op jit(solution)/shard_map/ppermute | solution.py:94
  23.8 0.1 collective-permute-start.2
  23.8 4.4 %collective-permute-done.1.refs_0_ = f32[2,136,256]{2,1,0:T(8,128)S(1)} collective-permute-done((f32[2,136,256]{2,1,0:T(8,128)S(1)}, f32[2,136,256]{2,1,0:T(8,128)S(1)}, u32[]{:S(2)}, u32[]{:S(2)}) %collective-permute-start.1) | collective-permute-done | bytes 278560 | tf_op jit(solution)/shard_map/ppermute | solution.py:94
  28.3 2.1 %collective-permute-start.3 = (f32[136,256]{1,0:T(8,128)S(1)}, f32[136,256]{1,0:T(8,128)S(1)}, u32[]{:S(2)}, u32[]{:S(2)}) collective-permute-start(f32[136,256]{1,0:T(8,128)S(1)} %fusion.1), channel_id=1, source_target_pairs={{0,16},{4,12},{8,24},{12,4},{16,0},{20,28},{24,8},{28,20},{1,17},{... | collective-permute-start | bytes 417800 | tf_op jit(solution)/shard_map/ppermute | solution.py:99
  30.4 0.8 collective-permute-done.2.refs_1_
  31.2 0.7 fusion.4
  31.9 2.4 %collective-permute-start.4 = (f32[128,256]{1,0:T(8,128)}, f32[128,256]{1,0:T(8,128)S(1)}, u32[]{:S(2)}, u32[]{:S(2)}) collective-permute-start(f32[128,256]{1,0:T(8,128)} %fusion.4), channel_id=1, source_target_pairs={{0,16},{4,12},{8,24},{12,4},{16,0},{20,28},{24,8},{28,20},{1,17},{... | collective-permute-start | bytes 393224 | tf_op jit(solution)/shard_map/ppermute | solution.py:99
  34.3 3.1 %collective-permute-done.4.refs_3_ = f32[128,256]{1,0:T(8,128)S(1)} collective-permute-done((f32[128,256]{1,0:T(8,128)}, f32[128,256]{1,0:T(8,128)S(1)}, u32[]{:S(2)}, u32[]{:S(2)}) %collective-permute-start.4) | collective-permute-done | bytes 131104 | tf_op jit(solution)/shard_map/ppermute | solution.py:99
  37.4 1.5 %refine_half.2 = (f32[128,256]{1,0:T(8,128)S(1)}, f32[128,256]{1,0:T(8,128)S(1)}, f32[72,256]{1,0:T(8,128)S(1)}) custom-call(s32[4]{0:T(128)S(1)} %pad_add_fusion.info, f32[4,264,256]{2,1,0:T(8,128)S(1)} %get-tuple-element.49.own, f32[4,264,256]{2,1,0:T(8,128)S(1)} %collective-permute-done.sibling, f32[2,136,256]{2,1,0:T(8,128)S(1)} %collective-permute-done.1.refs_0_, ...), custom_call_target="tpu_custom_call" | custom-call | tf_op jit(solution)/shard_map/refine_half/pallas_call | solution.py:405
  39.0 2.1 %collective-permute-start.11 = (f32[104,256]{1,0:T(8,128)S(1)}, f32[104,256]{1,0:T(8,128)S(1)}, u32[]{:S(2)}, u32[]{:S(2)}) collective-permute-start(f32[104,256]{1,0:T(8,128)S(1)} %pad_maximum_fusion.3), channel_id=1, source_target_pairs={{0,1},{1,0},{2,3},{3,2},{4,5},{5,4},{6,7},{7,6},{8,9},{9,8},{10,11... | collective-permute-start | bytes 319496 | tf_op jit(solution)/shard_map/ppermute | solution.py:89
  41.1 1.5 %collective-permute-start.5 = (f32[128,256]{1,0:T(8,128)S(1)}, f32[128,256]{1,0:T(8,128)S(1)}, u32[]{:S(2)}, u32[]{:S(2)}) collective-permute-start(f32[128,256]{1,0:T(8,128)S(1)} %get-tuple-element.63), channel_id=1, source_target_pairs={{0,8},{4,12},{8,0},{12,4},{16,24},{20,28},{24,16},{28,20},{1,9},{5... | collective-permute-start | bytes 393224 | tf_op jit(solution)/shard_map/ppermute | solution.py:89
  42.6 1.5 %collective-permute-start.10 = (f32[128,256]{1,0:T(8,128)S(1)}, f32[128,256]{1,0:T(8,128)S(1)}, u32[]{:S(2)}, u32[]{:S(2)}) collective-permute-start(f32[128,256]{1,0:T(8,128)S(1)} %get-tuple-element.63), channel_id=1, source_target_pairs={{0,16},{4,20},{8,24},{12,28},{16,0},{20,4},{24,8},{28,12},{1,17},{... | collective-permute-start | bytes 393224 | tf_op jit(solution)/shard_map/ppermute | solution.py:89
  44.1 0.5 collective-permute-start.6
  44.6 0.5 collective-permute-start.9
  45.1 4.9 %collective-permute-done.6.refs_1_ = f32[128,256]{1,0:T(8,128)S(1)} collective-permute-done((f32[128,256]{1,0:T(8,128)S(1)}, f32[128,256]{1,0:T(8,128)S(1)}, u32[]{:S(2)}, u32[]{:S(2)}) %collective-permute-start.6) | collective-permute-done | bytes 131104 | tf_op jit(solution)/shard_map/ppermute | solution.py:89
  50.0 1.1 collective-permute-start.8
  51.2 3.5 %fetch_points.1.points = bf16[4096,1024]{1,0:T(8,128)(2,1)S(1)} custom-call(bf16[4096,1024]{1,0:T(8,128)(2,1)} %points.3, f32[128,256]{1,0:T(8,128)S(1)} %collective-permute-done.5.refs_0_, f32[128,256]{1,0:T(8,128)S(1)} %collective-permute-done.6.refs_1_), custom_call_target="tpu_custom_call" | custom-call | bytes 16777216 | tf_op jit(solution)/shard_map/fetch_points/pallas_call | solution.py:280
  54.7 0.0 collective-permute-done.10
  54.7 0.3 collective-permute-done.7
  55.0 0.0 collective-permute-done.8
  55.2 0.1 collective-permute-start.12
  55.2 7.6 %energies_and_sums_10.1 = (f32[4,264,256]{2,1,0:T(8,128)S(1)}, f32[2,4096]{1,0:T(2,128)S(1)}) custom-call(s32[4]{0:T(128)S(1)} %pad_add_fusion.info, bf16[4096,1024]{1,0:T(8,128)(2,1)S(1)} %fetch_points.1.points, s32[2,4096]{1,0:T(2,128)S(1)} %copy-done.3, f32[8,128,256]{2,1,0:T(8,128)S(1)} %bitcast_dynamic-update-slice_fusion.fine, ...), custom_call_target="tpu_custom_call" | custom-call | flops 4294967296 | bytes 8388608 | tf_op jit(solution)/shard_map/energies_and_sums_10/pallas_call | solution.py:341
  62.8 0.6 collective-permute-start.14
  63.4 0.1 collective-permute-start.13
  63.5 0.0 collective-permute-done.12.fine
  63.5 7.8 %energies_and_sums_11.1 = (f32[4,264,256]{2,1,0:T(8,128)S(1)}, f32[2,4096]{1,0:T(2,128)S(1)}) custom-call(s32[4]{0:T(128)S(1)} %pad_add_fusion.info, bf16[4096,1024]{1,0:T(8,128)(2,1)S(1)} %fetch_points.1.points, s32[2,4096]{1,0:T(2,128)S(1)} %copy-done.3, f32[8,128,256]{2,1,0:T(8,128)S(1)} %collective-permute-done.12.fine, ...), custom_call_target="tpu_custom_call" | custom-call | flops 4294967296 | bytes 8388608 | tf_op jit(solution)/shard_map/energies_and_sums_11/pallas_call | solution.py:341
  71.4 2.1 %collective-permute-start.15 = (f32[2,136,256]{2,1,0:T(8,128)S(1)}, f32[2,136,256]{2,1,0:T(8,128)S(1)}, u32[]{:S(2)}, u32[]{:S(2)}) collective-permute-start(f32[2,136,256]{2,1,0:T(8,128)S(1)} %slice_add_fusion), channel_id=1, source_target_pairs={{0,8},{4,20},{8,0},{12,28},{16,24},{20,4},{24,16},{28,12},{1,9},{5... | collective-permute-start | bytes 835592 | tf_op jit(solution)/shard_map/ppermute | solution.py:94
  73.5 0.1 collective-permute-start.16
  73.6 2.6 %collective-permute-start.17 = (f32[104,256]{1,0:T(8,128)S(1)}, f32[104,256]{1,0:T(8,128)S(1)}, u32[]{:S(2)}, u32[]{:S(2)}) collective-permute-start(f32[104,256]{1,0:T(8,128)S(1)} %pad_maximum_fusion.5.refs_5_), channel_id=1, source_target_pairs={{0,2},{1,3},{2,0},{3,1},{4,6},{5,7},{6,4},{7,5},{8,10},{9,11},{10,... | collective-permute-start | bytes 319496 | tf_op jit(solution)/shard_map/ppermute | solution.py:89
  76.2 5.0 %collective-permute-done.17.refs_6_ = f32[104,256]{1,0:T(8,128)S(1)} collective-permute-done((f32[104,256]{1,0:T(8,128)S(1)}, f32[104,256]{1,0:T(8,128)S(1)}, u32[]{:S(2)}, u32[]{:S(2)}) %collective-permute-start.17) | collective-permute-done | bytes 106528 | tf_op jit(solution)/shard_map/ppermute | solution.py:89
  81.2 0.7 fusion
  81.9 1.2 %collective-permute-start.18 = (f32[136,256]{1,0:T(8,128)}, f32[136,256]{1,0:T(8,128)S(1)}, u32[]{:S(2)}, u32[]{:S(2)}) collective-permute-start(f32[136,256]{1,0:T(8,128)} %fusion), channel_id=1, source_target_pairs={{0,16},{4,12},{8,24},{12,4},{16,0},{20,28},{24,8},{28,20},{1,17},{... | collective-permute-start | bytes 417800 | tf_op jit(solution)/shard_map/ppermute | solution.py:99
  83.1 0.7 fusion.3
  83.7 0.8 collective-permute-start.19
  84.6 4.3 %collective-permute-done.19.refs_3_ = f32[128,256]{1,0:T(8,128)S(1)} collective-permute-done((f32[128,256]{1,0:T(8,128)}, f32[128,256]{1,0:T(8,128)S(1)}, u32[]{:S(2)}, u32[]{:S(2)}) %collective-permute-start.19) | collective-permute-done | bytes 131104 | tf_op jit(solution)/shard_map/ppermute | solution.py:99
  88.9 1.6 %refine_half.3 = (f32[128,256]{1,0:T(8,128)S(1)}, f32[128,256]{1,0:T(8,128)S(1)}, f32[72,256]{1,0:T(8,128)S(1)}) custom-call(s32[4]{0:T(128)S(1)} %pad_add_fusion.info, f32[4,264,256]{2,1,0:T(8,128)S(1)} %get-tuple-element.70.own, f32[4,264,256]{2,1,0:T(8,128)S(1)} %collective-permute-done.14.sibling, f32[2,136,256]{2,1,0:T(8,128)S(1)} %collective-permute-done.15.refs_0_, ...), custom_call_target="tpu_custom_call" | custom-call | tf_op jit(solution)/shard_map/refine_half/pallas_call | solution.py:405
  90.5 0.1 collective-permute-start.28
  90.6 1.9 %collective-permute-start.20 = (f32[128,256]{1,0:T(8,128)S(1)}, f32[128,256]{1,0:T(8,128)S(1)}, u32[]{:S(2)}, u32[]{:S(2)}) collective-permute-start(f32[128,256]{1,0:T(8,128)S(1)} %get-tuple-element.87), channel_id=1, source_target_pairs={{0,8},{4,12},{8,0},{12,4},{16,24},{20,28},{24,16},{28,20},{1,9},{5... | collective-permute-start | bytes 393224 | tf_op jit(solution)/shard_map/ppermute | solution.py:89
  92.6 1.0 collective-permute-start.21
  93.6 1.7 %collective-permute-done.28 = f32[104,256]{1,0:T(8,128)S(1)} collective-permute-done((f32[104,256]{1,0:T(8,128)S(1)}, f32[104,256]{1,0:T(8,128)S(1)}, u32[]{:S(2)}, u32[]{:S(2)}) %collective-permute-start.28) | collective-permute-done | bytes 106528 | tf_op jit(solution)/shard_map/ppermute | solution.py:89
  95.4 2.2 %collective-permute-start.29 = (f32[104,256]{1,0:T(8,128)S(1)}, f32[104,256]{1,0:T(8,128)S(1)}, u32[]{:S(2)}, u32[]{:S(2)}) collective-permute-start(f32[104,256]{1,0:T(8,128)S(1)} %pad_maximum_fusion.7), channel_id=1, source_target_pairs={{0,2},{1,3},{2,0},{3,1},{4,6},{5,7},{6,4},{7,5},{8,10},{9,11},{10,... | collective-permute-start | bytes 319496 | tf_op jit(solution)/shard_map/ppermute | solution.py:89
  97.7 2.8 %collective-permute-start.24 = (f32[128,256]{1,0:T(8,128)S(1)}, f32[128,256]{1,0:T(8,128)S(1)}, u32[]{:S(2)}, u32[]{:S(2)}) collective-permute-start(f32[128,256]{1,0:T(8,128)S(1)} %get-tuple-element.86), channel_id=1, source_target_pairs={{0,8},{4,12},{8,0},{12,4},{16,24},{20,28},{24,16},{28,20},{1,9},{5... | collective-permute-start | bytes 393224 | tf_op jit(solution)/shard_map/ppermute | solution.py:89
  100.4 0.8 collective-permute-start.25
  101.2 0.1 collective-permute-start.22
  101.3 1.2 %collective-permute-start.23 = (f32[128,256]{1,0:T(8,128)S(1)}, f32[128,256]{1,0:T(8,128)S(1)}, u32[]{:S(2)}, u32[]{:S(2)}) collective-permute-start(f32[128,256]{1,0:T(8,128)S(1)} %collective-permute-done.20), channel_id=1, source_target_pairs={{0,16},{4,20},{8,24},{12,28},{16,0},{20,4},{24,8},{28,12},{1,17},{... | collective-permute-start | bytes 393224 | tf_op jit(solution)/shard_map/ppermute | solution.py:89
  102.6 2.0 %collective-permute-start.30 = (f32[72,256]{1,0:T(8,128)S(1)}, f32[72,256]{1,0:T(8,128)S(1)}, u32[]{:S(2)}, u32[]{:S(2)}) collective-permute-start(f32[72,256]{1,0:T(8,128)S(1)} %slice_add_fusion.11), channel_id=1, source_target_pairs={{0,8},{4,12},{8,0},{12,4},{16,24},{20,28},{24,16},{28,20},{1,9},{5... | collective-permute-start | bytes 221192 | tf_op jit(solution)/shard_map/ppermute | solution.py:89
  104.7 0.8 collective-permute-start.31
  105.4 0.8 collective-permute-done.25
  106.2 1.5 %collective-permute-start.32 = (f32[72,256]{1,0:T(8,128)S(1)}, f32[72,256]{1,0:T(8,128)S(1)}, u32[]{:S(2)}, u32[]{:S(2)}) collective-permute-start(f32[72,256]{1,0:T(8,128)S(1)} %slice_add_fusion.11), channel_id=1, source_target_pairs={{0,24},{4,28},{8,16},{12,20},{16,8},{20,12},{24,0},{28,4},{1,25},{... | collective-permute-start | bytes 221192 | tf_op jit(solution)/shard_map/ppermute | solution.py:89
  107.7 0.1 collective-permute-start.27
  107.8 0.6 collective-permute-done.23
  108.4 0.1 collective-permute-start.26
  108.5 0.7 collective-permute-done.31
  109.2 2.3 %collective-permute-done.32 = f32[72,256]{1,0:T(8,128)S(1)} collective-permute-done((f32[72,256]{1,0:T(8,128)S(1)}, f32[72,256]{1,0:T(8,128)S(1)}, u32[]{:S(2)}, u32[]{:S(2)}) %collective-permute-start.32) | collective-permute-done | bytes 73760 | tf_op jit(solution)/shard_map/ppermute | solution.py:89
  111.5 0.1 collective-permute-start.33
  111.6 0.7 maximum_multiply_fusion
  112.2 2.0 %place_fine.1.after = f32[512,1024]{1,0:T(8,128)} custom-call(s32[4]{0:T(128)S(1)} %pad_add_fusion.info, f32[4,128,256]{2,1,0:T(8,128)S(1)} %pad_maximum_fusion.refs_0_, f32[4,128,256]{2,1,0:T(8,128)S(1)} %pad_maximum_fusion.1.refs_1_, f32[4,128,256]{2,1,0:T(8,128)S(1)} %collective-permute-done.26.refs_2_, f32[4,128,256]{2,1,0:T(8,128)S(1)} %collective-permute-done.27.refs_3_), custom_call_target="tpu_custom_call" | custom-call | tf_op jit(solution)/shard_map/place_fine/pallas_call | solution.py:488
  114.2 1.4 %place_coarse.1 = f32[64,1024]{1,0:T(8,128)} custom-call(s32[4]{0:T(128)S(1)} %pad_add_fusion.info, f32[4,72,256]{2,1,0:T(8,128)S(1)} %pad_maximum_fusion.2.parts, f32[4,72,256]{2,1,0:T(8,128)S(1)} %collective-permute-done.33.others, f32[512,1024]{1,0:T(8,128)} %place_fine.1.after), custom_call_target="tpu_custom_call" | custom-call | tf_op jit(solution)/shard_map/place_coarse/pallas_call | solution.py:513
  (63 shorter events, 0.7 us)
Async XLA Ops:
  0.7 12.8 %copy-start.2 = (f32[512,1024]{1,0:T(8,128)S(1)}, f32[512,1024]{1,0:T(8,128)}, u32[]{:S(2)}) copy-start(f32[512,1024]{1,0:T(8,128)} %fine.3) | copy-start | bytes 6291460
  0.7 12.8 %copy-start.3 = (s32[2,4096]{1,0:T(2,128)S(1)}, s32[2,4096]{1,0:T(2,128)}, u32[]{:S(2)}) copy-start(s32[2,4096]{1,0:T(2,128)} %assign.7) | copy-start | bytes 98308
  12.9 8.2 %collective-permute-start = (f32[4,264,256]{2,1,0:T(8,128)S(1)}, f32[4,264,256]{2,1,0:T(8,128)S(1)}, u32[]{:S(2)}, u32[]{:S(2)}) collective-permute-start(f32[4,264,256]{2,1,0:T(8,128)S(1)} %get-tuple-element.50), channel_id=1, source_target_pairs={{0,4},{4,0},{8,12},{12,8},{16,20},{20,16},{24,28},{28,24},{1,5},{5... | collective-permute-start | bytes 3244040 | tf_op jit(solution)/shard_map/ppermute | solution.py:89
  21.2 16.2 %copy-start = (f32[64,1024]{1,0:T(8,128)S(1)}, f32[64,1024]{1,0:T(8,128)}, u32[]{:S(2)}) copy-start(f32[64,1024]{1,0:T(8,128)} %refs_5_.1) | copy-start | bytes 786436
  21.2 16.2 %copy-start.1 = (s32[512]{0:T(512)S(1)}, s32[512]{0:T(512)}, u32[]{:S(2)}) copy-start(s32[512]{0:T(512)} %param.9) | copy-start | bytes 6148
  21.3 7.0 %collective-permute-start.1 = (f32[2,136,256]{2,1,0:T(8,128)S(1)}, f32[2,136,256]{2,1,0:T(8,128)S(1)}, u32[]{:S(2)}, u32[]{:S(2)}) collective-permute-start(f32[2,136,256]{2,1,0:T(8,128)S(1)} %slice_add_fusion.1), channel_id=1, source_target_pairs={{0,8},{4,20},{8,0},{12,28},{16,24},{20,4},{24,16},{28,12},{1,9},{5... | collective-permute-start | bytes 835592 | tf_op jit(solution)/shard_map/ppermute | solution.py:94
  23.8 7.4 %collective-permute-start.2 = (f32[2,128,256]{2,1,0:T(8,128)S(1)}, f32[2,128,256]{2,1,0:T(8,128)S(1)}, u32[]{:S(2)}, u32[]{:S(2)}) collective-permute-start(f32[2,128,256]{2,1,0:T(8,128)S(1)} %slice_add_fusion.3), channel_id=1, source_target_pairs={{0,8},{4,20},{8,0},{12,28},{16,24},{20,4},{24,16},{28,12},{1,9},{5... | collective-permute-start | bytes 786440 | tf_op jit(solution)/shard_map/ppermute | solution.py:94
  28.3 9.1 %collective-permute-start.3 = (f32[136,256]{1,0:T(8,128)S(1)}, f32[136,256]{1,0:T(8,128)S(1)}, u32[]{:S(2)}, u32[]{:S(2)}) collective-permute-start(f32[136,256]{1,0:T(8,128)S(1)} %fusion.1), channel_id=1, source_target_pairs={{0,16},{4,12},{8,24},{12,4},{16,0},{20,28},{24,8},{28,20},{1,17},{... | collective-permute-start | bytes 417800 | tf_op jit(solution)/shard_map/ppermute | solution.py:99
  31.9 5.5 %collective-permute-start.4 = (f32[128,256]{1,0:T(8,128)}, f32[128,256]{1,0:T(8,128)S(1)}, u32[]{:S(2)}, u32[]{:S(2)}) collective-permute-start(f32[128,256]{1,0:T(8,128)} %fusion.4), channel_id=1, source_target_pairs={{0,16},{4,12},{8,24},{12,4},{16,0},{20,28},{24,8},{28,20},{1,17},{... | collective-permute-start | bytes 393224 | tf_op jit(solution)/shard_map/ppermute | solution.py:99
  39.0 6.2 %collective-permute-start.11 = (f32[104,256]{1,0:T(8,128)S(1)}, f32[104,256]{1,0:T(8,128)S(1)}, u32[]{:S(2)}, u32[]{:S(2)}) collective-permute-start(f32[104,256]{1,0:T(8,128)S(1)} %pad_maximum_fusion.3), channel_id=1, source_target_pairs={{0,1},{1,0},{2,3},{3,2},{4,5},{5,4},{6,7},{7,6},{8,9},{9,8},{10,11... | collective-permute-start | bytes 319496 | tf_op jit(solution)/shard_map/ppermute | solution.py:89
  41.1 9.0 %collective-permute-start.5 = (f32[128,256]{1,0:T(8,128)S(1)}, f32[128,256]{1,0:T(8,128)S(1)}, u32[]{:S(2)}, u32[]{:S(2)}) collective-permute-start(f32[128,256]{1,0:T(8,128)S(1)} %get-tuple-element.63), channel_id=1, source_target_pairs={{0,8},{4,12},{8,0},{12,4},{16,24},{20,28},{24,16},{28,20},{1,9},{5... | collective-permute-start | bytes 393224 | tf_op jit(solution)/shard_map/ppermute | solution.py:89
  42.6 12.1 %collective-permute-start.10 = (f32[128,256]{1,0:T(8,128)S(1)}, f32[128,256]{1,0:T(8,128)S(1)}, u32[]{:S(2)}, u32[]{:S(2)}) collective-permute-start(f32[128,256]{1,0:T(8,128)S(1)} %get-tuple-element.63), channel_id=1, source_target_pairs={{0,16},{4,20},{8,24},{12,28},{16,0},{20,4},{24,8},{28,12},{1,17},{... | collective-permute-start | bytes 393224 | tf_op jit(solution)/shard_map/ppermute | solution.py:89
  44.1 5.9 %collective-permute-start.6 = (f32[128,256]{1,0:T(8,128)S(1)}, f32[128,256]{1,0:T(8,128)S(1)}, u32[]{:S(2)}, u32[]{:S(2)}) collective-permute-start(f32[128,256]{1,0:T(8,128)S(1)} %get-tuple-element.62), channel_id=1, source_target_pairs={{0,16},{4,20},{8,24},{12,28},{16,0},{20,4},{24,8},{28,12},{1,17},{... | collective-permute-start | bytes 393224 | tf_op jit(solution)/shard_map/ppermute | solution.py:89
  44.6 10.1 %collective-permute-start.9 = (f32[128,256]{1,0:T(8,128)S(1)}, f32[128,256]{1,0:T(8,128)S(1)}, u32[]{:S(2)}, u32[]{:S(2)}) collective-permute-start(f32[128,256]{1,0:T(8,128)S(1)} %get-tuple-element.62), channel_id=1, source_target_pairs={{0,8},{4,12},{8,0},{12,4},{16,24},{20,28},{24,16},{28,20},{1,9},{5... | collective-permute-start | bytes 393224 | tf_op jit(solution)/shard_map/ppermute | solution.py:89
  50.0 5.0 %collective-permute-start.7 = (f32[128,256]{1,0:T(8,128)S(1)}, f32[128,256]{1,0:T(8,128)S(1)}, u32[]{:S(2)}, u32[]{:S(2)}) collective-permute-start(f32[128,256]{1,0:T(8,128)S(1)} %collective-permute-done.6.refs_1_), channel_id=1, source_target_pairs={{0,8},{4,12},{8,0},{12,4},{16,24},{20,28},{24,16},{28,20},{1,9},{5... | collective-permute-start | bytes 393224 | tf_op jit(solution)/shard_map/ppermute | solution.py:89
  50.0 5.0 %collective-permute-start.8 = (f32[128,256]{1,0:T(8,128)S(1)}, f32[128,256]{1,0:T(8,128)S(1)}, u32[]{:S(2)}, u32[]{:S(2)}) collective-permute-start(f32[128,256]{1,0:T(8,128)S(1)} %collective-permute-done.5.refs_0_), channel_id=1, source_target_pairs={{0,16},{4,20},{8,24},{12,28},{16,0},{20,4},{24,8},{28,12},{1,17},{... | collective-permute-start | bytes 393224 | tf_op jit(solution)/shard_map/ppermute | solution.py:89
  55.2 8.3 %collective-permute-start.12 = (f32[8,128,256]{2,1,0:T(8,128)S(1)}, f32[8,128,256]{2,1,0:T(8,128)S(1)}, u32[]{:S(2)}, u32[]{:S(2)}) collective-permute-start(f32[8,128,256]{2,1,0:T(8,128)S(1)} %bitcast_dynamic-update-slice_fusion.fine), channel_id=1, source_target_pairs={{0,4},{4,0},{8,12},{12,8},{16,20},{20,16},{24,28},{28,24},{1,5},{5... | collective-permute-start | bytes 3145736 | tf_op jit(solution)/shard_map/ppermute | solution.py:89
  62.8 8.5 %collective-permute-start.14 = (f32[4,264,256]{2,1,0:T(8,128)S(1)}, f32[4,264,256]{2,1,0:T(8,128)S(1)}, u32[]{:S(2)}, u32[]{:S(2)}) collective-permute-start(f32[4,264,256]{2,1,0:T(8,128)S(1)} %get-tuple-element.71), channel_id=1, source_target_pairs={{0,4},{4,0},{8,12},{12,8},{16,20},{20,16},{24,28},{28,24},{1,5},{5... | collective-permute-start | bytes 3244040 | tf_op jit(solution)/shard_map/ppermute | solution.py:89
  63.4 7.9 %collective-permute-start.13 = (f32[72,256]{1,0:T(8,128)S(1)}, f32[72,256]{1,0:T(8,128)S(1)}, u32[]{:S(2)}, u32[]{:S(2)}) collective-permute-start(f32[72,256]{1,0:T(8,128)S(1)} %slice.121), channel_id=1, source_target_pairs={{0,4},{4,0},{8,12},{12,8},{16,20},{20,16},{24,28},{28,24},{1,5},{5... | collective-permute-start | bytes 221192 | tf_op jit(solution)/shard_map/ppermute | solution.py:89
  71.4 9.8 %collective-permute-start.15 = (f32[2,136,256]{2,1,0:T(8,128)S(1)}, f32[2,136,256]{2,1,0:T(8,128)S(1)}, u32[]{:S(2)}, u32[]{:S(2)}) collective-permute-start(f32[2,136,256]{2,1,0:T(8,128)S(1)} %slice_add_fusion), channel_id=1, source_target_pairs={{0,8},{4,20},{8,0},{12,28},{16,24},{20,4},{24,16},{28,12},{1,9},{5... | collective-permute-start | bytes 835592 | tf_op jit(solution)/shard_map/ppermute | solution.py:94
  73.5 7.7 %collective-permute-start.16 = (f32[2,128,256]{2,1,0:T(8,128)S(1)}, f32[2,128,256]{2,1,0:T(8,128)S(1)}, u32[]{:S(2)}, u32[]{:S(2)}) collective-permute-start(f32[2,128,256]{2,1,0:T(8,128)S(1)} %slice_add_fusion.2), channel_id=1, source_target_pairs={{0,8},{4,20},{8,0},{12,28},{16,24},{20,4},{24,16},{28,12},{1,9},{5... | collective-permute-start | bytes 786440 | tf_op jit(solution)/shard_map/ppermute | solution.py:94
  73.6 7.6 %collective-permute-start.17 = (f32[104,256]{1,0:T(8,128)S(1)}, f32[104,256]{1,0:T(8,128)S(1)}, u32[]{:S(2)}, u32[]{:S(2)}) collective-permute-start(f32[104,256]{1,0:T(8,128)S(1)} %pad_maximum_fusion.5.refs_5_), channel_id=1, source_target_pairs={{0,2},{1,3},{2,0},{3,1},{4,6},{5,7},{6,4},{7,5},{8,10},{9,11},{10,... | collective-permute-start | bytes 319496 | tf_op jit(solution)/shard_map/ppermute | solution.py:89
  81.9 7.1 %collective-permute-start.18 = (f32[136,256]{1,0:T(8,128)}, f32[136,256]{1,0:T(8,128)S(1)}, u32[]{:S(2)}, u32[]{:S(2)}) collective-permute-start(f32[136,256]{1,0:T(8,128)} %fusion), channel_id=1, source_target_pairs={{0,16},{4,12},{8,24},{12,4},{16,0},{20,28},{24,8},{28,20},{1,17},{... | collective-permute-start | bytes 417800 | tf_op jit(solution)/shard_map/ppermute | solution.py:99
  83.7 5.2 %collective-permute-start.19 = (f32[128,256]{1,0:T(8,128)}, f32[128,256]{1,0:T(8,128)S(1)}, u32[]{:S(2)}, u32[]{:S(2)}) collective-permute-start(f32[128,256]{1,0:T(8,128)} %fusion.3), channel_id=1, source_target_pairs={{0,16},{4,12},{8,24},{12,4},{16,0},{20,28},{24,8},{28,20},{1,17},{... | collective-permute-start | bytes 393224 | tf_op jit(solution)/shard_map/ppermute | solution.py:99
  90.5 4.8 %collective-permute-start.28 = (f32[104,256]{1,0:T(8,128)S(1)}, f32[104,256]{1,0:T(8,128)S(1)}, u32[]{:S(2)}, u32[]{:S(2)}) collective-permute-start(f32[104,256]{1,0:T(8,128)S(1)} %pad_maximum_fusion.6), channel_id=1, source_target_pairs={{0,1},{1,0},{2,3},{3,2},{4,5},{5,4},{6,7},{7,6},{8,9},{9,8},{10,11... | collective-permute-start | bytes 319496 | tf_op jit(solution)/shard_map/ppermute | solution.py:89
  90.6 7.0 %collective-permute-start.20 = (f32[128,256]{1,0:T(8,128)S(1)}, f32[128,256]{1,0:T(8,128)S(1)}, u32[]{:S(2)}, u32[]{:S(2)}) collective-permute-start(f32[128,256]{1,0:T(8,128)S(1)} %get-tuple-element.87), channel_id=1, source_target_pairs={{0,8},{4,12},{8,0},{12,4},{16,24},{20,28},{24,16},{28,20},{1,9},{5... | collective-permute-start | bytes 393224 | tf_op jit(solution)/shard_map/ppermute | solution.py:89
  92.6 5.1 %collective-permute-start.21 = (f32[128,256]{1,0:T(8,128)S(1)}, f32[128,256]{1,0:T(8,128)S(1)}, u32[]{:S(2)}, u32[]{:S(2)}) collective-permute-start(f32[128,256]{1,0:T(8,128)S(1)} %get-tuple-element.86), channel_id=1, source_target_pairs={{0,16},{4,20},{8,24},{12,28},{16,0},{20,4},{24,8},{28,12},{1,17},{... | collective-permute-start | bytes 393224 | tf_op jit(solution)/shard_map/ppermute | solution.py:89
  95.4 7.2 %collective-permute-start.29 = (f32[104,256]{1,0:T(8,128)S(1)}, f32[104,256]{1,0:T(8,128)S(1)}, u32[]{:S(2)}, u32[]{:S(2)}) collective-permute-start(f32[104,256]{1,0:T(8,128)S(1)} %pad_maximum_fusion.7), channel_id=1, source_target_pairs={{0,2},{1,3},{2,0},{3,1},{4,6},{5,7},{6,4},{7,5},{8,10},{9,11},{10,... | collective-permute-start | bytes 319496 | tf_op jit(solution)/shard_map/ppermute | solution.py:89
  97.7 7.0 %collective-permute-start.24 = (f32[128,256]{1,0:T(8,128)S(1)}, f32[128,256]{1,0:T(8,128)S(1)}, u32[]{:S(2)}, u32[]{:S(2)}) collective-permute-start(f32[128,256]{1,0:T(8,128)S(1)} %get-tuple-element.86), channel_id=1, source_target_pairs={{0,8},{4,12},{8,0},{12,4},{16,24},{20,28},{24,16},{28,20},{1,9},{5... | collective-permute-start | bytes 393224 | tf_op jit(solution)/shard_map/ppermute | solution.py:89
  100.4 5.8 %collective-permute-start.25 = (f32[128,256]{1,0:T(8,128)S(1)}, f32[128,256]{1,0:T(8,128)S(1)}, u32[]{:S(2)}, u32[]{:S(2)}) collective-permute-start(f32[128,256]{1,0:T(8,128)S(1)} %get-tuple-element.87), channel_id=1, source_target_pairs={{0,16},{4,20},{8,24},{12,28},{16,0},{20,4},{24,8},{28,12},{1,17},{... | collective-permute-start | bytes 393224 | tf_op jit(solution)/shard_map/ppermute | solution.py:89
  101.2 6.5 %collective-permute-start.22 = (f32[128,256]{1,0:T(8,128)S(1)}, f32[128,256]{1,0:T(8,128)S(1)}, u32[]{:S(2)}, u32[]{:S(2)}) collective-permute-start(f32[128,256]{1,0:T(8,128)S(1)} %collective-permute-done.21), channel_id=1, source_target_pairs={{0,8},{4,12},{8,0},{12,4},{16,24},{20,28},{24,16},{28,20},{1,9},{5... | collective-permute-start | bytes 393224 | tf_op jit(solution)/shard_map/ppermute | solution.py:89
  101.3 7.1 %collective-permute-start.23 = (f32[128,256]{1,0:T(8,128)S(1)}, f32[128,256]{1,0:T(8,128)S(1)}, u32[]{:S(2)}, u32[]{:S(2)}) collective-permute-start(f32[128,256]{1,0:T(8,128)S(1)} %collective-permute-done.20), channel_id=1, source_target_pairs={{0,16},{4,20},{8,24},{12,28},{16,0},{20,4},{24,8},{28,12},{1,17},{... | collective-permute-start | bytes 393224 | tf_op jit(solution)/shard_map/ppermute | solution.py:89
  102.6 5.9 %collective-permute-start.30 = (f32[72,256]{1,0:T(8,128)S(1)}, f32[72,256]{1,0:T(8,128)S(1)}, u32[]{:S(2)}, u32[]{:S(2)}) collective-permute-start(f32[72,256]{1,0:T(8,128)S(1)} %slice_add_fusion.11), channel_id=1, source_target_pairs={{0,8},{4,12},{8,0},{12,4},{16,24},{20,28},{24,16},{28,20},{1,9},{5... | collective-permute-start | bytes 221192 | tf_op jit(solution)/shard_map/ppermute | solution.py:89
  104.7 4.5 %collective-permute-start.31 = (f32[72,256]{1,0:T(8,128)S(1)}, f32[72,256]{1,0:T(8,128)S(1)}, u32[]{:S(2)}, u32[]{:S(2)}) collective-permute-start(f32[72,256]{1,0:T(8,128)S(1)} %slice_add_fusion.11), channel_id=1, source_target_pairs={{0,16},{4,20},{8,24},{12,28},{16,0},{20,4},{24,8},{28,12},{1,17},{... | collective-permute-start | bytes 221192 | tf_op jit(solution)/shard_map/ppermute | solution.py:89
  106.2 5.3 %collective-permute-start.32 = (f32[72,256]{1,0:T(8,128)S(1)}, f32[72,256]{1,0:T(8,128)S(1)}, u32[]{:S(2)}, u32[]{:S(2)}) collective-permute-start(f32[72,256]{1,0:T(8,128)S(1)} %slice_add_fusion.11), channel_id=1, source_target_pairs={{0,24},{4,28},{8,16},{12,20},{16,8},{20,12},{24,0},{28,4},{1,25},{... | collective-permute-start | bytes 221192 | tf_op jit(solution)/shard_map/ppermute | solution.py:89
  107.7 4.5 %collective-permute-start.27 = (f32[4,128,256]{2,1,0:T(8,128)S(1)}, f32[4,128,256]{2,1,0:T(8,128)S(1)}, u32[]{:S(2)}, u32[]{:S(2)}) collective-permute-start(f32[4,128,256]{2,1,0:T(8,128)S(1)} %pad_maximum_fusion.1.refs_1_), channel_id=1, source_target_pairs={{0,4},{4,0},{8,12},{12,8},{16,20},{20,16},{24,28},{28,24},{1,5},{5... | collective-permute-start | bytes 1572872 | tf_op jit(solution)/shard_map/ppermute | solution.py:89
  108.4 3.8 %collective-permute-start.26 = (f32[4,128,256]{2,1,0:T(8,128)S(1)}, f32[4,128,256]{2,1,0:T(8,128)S(1)}, u32[]{:S(2)}, u32[]{:S(2)}) collective-permute-start(f32[4,128,256]{2,1,0:T(8,128)S(1)} %pad_maximum_fusion.refs_0_), channel_id=1, source_target_pairs={{0,4},{4,0},{8,12},{12,8},{16,20},{20,16},{24,28},{28,24},{1,5},{5... | collective-permute-start | bytes 1572872 | tf_op jit(solution)/shard_map/ppermute | solution.py:89
  111.5 2.7 %collective-permute-start.33 = (f32[4,72,256]{2,1,0:T(8,128)S(1)}, f32[4,72,256]{2,1,0:T(8,128)S(1)}, u32[]{:S(2)}, u32[]{:S(2)}) collective-permute-start(f32[4,72,256]{2,1,0:T(8,128)S(1)} %pad_maximum_fusion.2.parts), channel_id=1, source_target_pairs={{0,4},{4,0},{8,12},{12,8},{16,20},{20,16},{24,28},{28,24},{1,5},{5... | collective-permute-start | bytes 884744 | tf_op jit(solution)/shard_map/ppermute | solution.py:89

commit v16 on v15

--- a/solution.py
+++ b/solution.py
@@ -463,22 +463,41 @@
 
 
 def place_body(info, *refs, flip):
-    fine_out, held, sems = refs[4:]
+    own, other = refs[:3], refs[3:6]
+    fine_out, coarse_out, fine_held, coarse_held, sems = refs[6:]
+    block_width = coarse_out.shape[1] // SLOTS
     rows = fine_out.shape[0] // 2
     mid = rows // 2
-    block_width = fine_out.shape[1] // SLOTS
-    sends = []
-    for at in range(2):
+    half = info[1] ^ flip
+
+    def column_of(slot, core):
+        start = block_of(info, slot, core) * block_width
+        return pl.ds(pl.multiple_of(start, block_width), block_width)
+
+    def put(at, *groups):
         for piece, (slot, is_low) in enumerate(PIECES):
-            block = refs[2 * at + piece // SLOTS][piece % SLOTS]
-            column = pl.multiple_of(block_of(info, slot, 0) * block_width, block_width)
-            held[at, is_low * mid : (is_low + 1) * mid, pl.ds(column, block_width)] = block
-        half = info[1] ^ flip ^ at
+            part = slice(is_low * mid, (is_low + 1) * mid)
+            fine_held[at, part, column_of(slot, 0)] = groups[piece // SLOTS][piece % SLOTS]
+
+    def send(at, half):
         span = pl.ds(pl.multiple_of(half * rows, rows), rows)
-        sends.append(pltpu.make_async_copy(held.at[at], fine_out.at[span], sems.at[at]))
-        sends[at].start()
-    for send in sends:
-        send.wait()
+        return pltpu.make_async_copy(fine_held.at[at], fine_out.at[span], sems.at[at])
+
+    put(0, *own[:2])
+    send(0, half).start()
+    put(1, *other[:2])
+    send(1, 1 - half).start()
+    parts, others = own[2], other[2]
+    weight = parts[0, NC:, :128] + others[0, NC:, :128]
+    weight = as_column(weight[:1], 128)[:NC, :1]
+    for slot in range(SLOTS):
+        total = parts[slot, :NC, :] + others[slot, :NC, :]
+        coarse_held[:, column_of(slot, 0)] = total / weight
+    send_coarse = pltpu.make_async_copy(coarse_held, coarse_out, sems.at[2])
+    send_coarse.start()
+    send(0, half).wait()
+    send(1, 1 - half).wait()
+    send_coarse.wait()
 
 
 def place(info, own, other, *, flip):
@@ -487,37 +506,20 @@
     args = [near_by(value) for value in (*own, *other)]
     return pl.pallas_call(
         functools.partial(place_body, flip=flip),
-        out_shape=jax.ShapeDtypeStruct((2 * rows, width), jnp.float32),
+        out_shape=[
+            jax.ShapeDtypeStruct((2 * rows, width), jnp.float32),
+            jax.ShapeDtypeStruct((NC, width), jnp.float32),
+        ],
         in_specs=[SCALARS] + [HERE] * len(args),
-        out_specs=AWAY,
+        out_specs=[AWAY, AWAY],
         scratch_shapes=[
             pltpu.VMEM((2, rows, width), jnp.float32),
-            pltpu.SemaphoreType.DMA((2,)),
+            pltpu.VMEM((NC, width), jnp.float32),
+            pltpu.SemaphoreType.DMA((3,)),
         ],
         compiler_params=pltpu.CompilerParams(vmem_limit_bytes=8 * 2**20),
-        name="place_fine",
+        name="place_blocks",
     )(info, *args)
-
-
-def place_coarse_body(info, parts, others, after, coarse_out):
-    block_width = parts.shape[2]
-    weight = parts[0, NC:, :128] + others[0, NC:, :128]
-    weight = as_column(weight[:1], 128)[:NC, :1]
-    for slot in range(SLOTS):
-        total = parts[slot, :NC, :] + others[slot, :NC, :]
-        column = pl.multiple_of(block_of(info, slot, 0) * block_width, block_width)
-        coarse_out[:, pl.ds(column, block_width)] = total / weight
-
-
-def place_coarse(info, parts, others, after):
-    return pl.pallas_call(
-        place_coarse_body,
-        out_shape=jax.ShapeDtypeStruct((NC, SLOTS * parts.shape[2]), jnp.float32),
-        in_specs=[SCALARS, HERE, HERE, AWAY],
-        out_specs=HERE,
-        compiler_params=pltpu.CompilerParams(vmem_limit_bytes=4 * 2**20),
-        name="place_coarse",
-    )(info, near_by(parts), near_by(others), far_off(after))
 
 
 def on_device_paired(points, fine_assign, fine_start, coarse_start, coarse_assign):
@@ -543,12 +545,13 @@
     own = jnp.stack(own)
     bits = range(lax.axis_size("cen").bit_length() - 1)
     folded = jnp.concatenate([part, seen_first.reshape(-1, block_width)], 0)
-    folded = over_cen(folded, fold, bits[:1])
-    own, folded = lax.optimization_barrier((own, folded))
+    paired = swap(folded, 1, "cen")
     other = swap(own, CORE)
 
     call = functools.partial(run_pass, info, pass_index=1, rows=rows)
     sent, seen = call(kept, fine_assign, own, squares, None, flip=0)
+    sent, paired = lax.optimization_barrier((sent, paired))
+    folded = fold(folded, paired)
     sibling = swap(sent, CORE)
     part = folded[: NC + TAIL]
     others_part = swap(part, CORE)
@@ -567,10 +570,8 @@
     own = gather_half(top, low, True)
     folded = over_cen(folded, fold)
     part, seen_second = folded[: NC + TAIL], folded[NC + TAIL :]
-    own = [jnp.stack(own[:4]), jnp.stack(own[4:])]
-    fine_now = place(info, own, [swap(group, CORE) for group in own], flip=1)
-    parts = jnp.stack(spread(part))
-    coarse_now = place_coarse(info, parts, swap(parts, CORE), fine_now)
+    blocks = [jnp.stack(own[:4]), jnp.stack(own[4:]), jnp.stack(spread(part))]
+    fine_now, coarse_now = place(info, blocks, [swap(block, CORE) for block in blocks], flip=1)
 
     seen = [each.reshape(2, -1) for each in (seen_first, seen_second)]
     gaps = jnp.stack([each[0] - each[1] for each in seen]) / math.sqrt(width)

time: 116 us -> 111 us (0.957)
  waiting for transfers between devices: 28.9 us -> 25.2 us
  starting transfers between devices: 37.1 us -> 38.8 us
  other arithmetic: 3.17 us -> 1.86 us
  Pallas kernels: 45.1 us -> 43.9 us
    ppermute x26, waiting for transfers between devices: 16.2 us -> 13.2 us  [swap(): return lax.ppermute(value, axis, [(i, i ^ bit) for i in range(size)])]
    ppermute x26, starting transfers between devices: 25.9 us -> 27.5 us  [swap(): return lax.ppermute(value, axis, [(i, i ^ bit) for i in range(size)])]
    add x4, other arithmetic: 2.07 us -> 0.76 us  [exchange(): held[2, rows] + sibling[2, rows] + arrived[1]]
    pallas_call x2 -> x1, Pallas kernels: 3.37 us -> 2.1 us  [place(): pl.pallas_call(functools.partial(place_body, flip=flip), out_shape=[jax.S...]
  transfers between devices with their start and end apart: 34 -> 34, of which waited for: 12 -> 12; matrix products, arithmetic and copies ran while one was open for 2% -> 2% of each run, Pallas kernels for 25% -> 24%
where the time goes in v16:
time: 111 us
  Pallas kernels  43.9 us (40%)
  starting transfers between devices  38.8 us (35%)
  waiting for transfers between devices  25.2 us (23%)
  other arithmetic  1.86 us (2%)
  between operations  1.21 us (1%)
    pallas_call x4, Pallas kernels, run_pass(): pl.pallas_call(body, out_shape=out_shape, in_specs=[SCALARS, *in_specs],...  35.2 us
    ppermute x26, starting transfers between devices, swap(): return lax.ppermute(value, axis, [(i, i ^ bit) for i in range(size)])  27.5 us
    ppermute x26, waiting for transfers between devices, swap(): return lax.ppermute(value, axis, [(i, i ^ bit) for i in range(size)])  13.2 us
    ppermute x4, waiting for transfers between devices, swap_second(): return lax.ppermute(value, 'pts', pairs)  6.79 us
    ppermute x4, starting transfers between devices, swap_second(): return lax.ppermute(value, 'pts', pairs)  6.62 us
    ppermute x4, waiting for transfers between devices, swap_first(): return lax.ppermute(value, 'pts', pairs)  5.22 us
    ppermute x4, starting transfers between devices, swap_first(): return lax.ppermute(value, 'pts', pairs)  4.64 us
    pallas_call x1, Pallas kernels, fetch(): pl.pallas_call(fetch_body, out_shape=pltpu.VMEM(points.shape, points.dtyp...  3.48 us
  transfers between devices with their start and end apart: 34, of which 12 were waited for; matrix products, arithmetic and copies ran while one was open for 2% of the time, Pallas kernels for 24%

profile of v16, /device:TPU:0, one launch (start us, length us, event | category | flops | bytes accessed | tf_op | source)
XLA Modules:
  0.0 111.2 jit_solution(3361141638350440343)
XLA Ops:
  0.6 0.1 pad_add_fusion.info
  0.7 12.2 %energies_and_sums_00.1 = (f32[4,264,256]{2,1,0:T(8,128)S(1)}, f32[2,4096]{1,0:T(2,128)S(1)}, f32[1,4096]{1,0:T(1,128)S(1)}, bf16[4096,1024]{1,0:T(8,128)(2,1)S(1)}) custom-call(s32[4]{0:T(128)S(1)} %pad_add_fusion.info, bf16[4096,1024]{1,0:T(8,128)(2,1)} %points.3, s32[2,4096]{1,0:T(2,128)} %assign.7, f32[512,1024]{1,0:T(8,128)} %fine.3), custom_call_target="tpu_custom_call" | custom-call | flops 4294967296 | bytes 8388608 | tf_op jit(solution)/shard_map/energies_and_sums_00/pallas_call | solution.py:341
  12.9 0.6 collective-permute-start
  13.5 7.6 %energies_and_sums_01.1 = (f32[4,264,256]{2,1,0:T(8,128)S(1)}, f32[2,4096]{1,0:T(2,128)S(1)}) custom-call(s32[4]{0:T(128)S(1)} %pad_add_fusion.info, bf16[4096,1024]{1,0:T(8,128)(2,1)S(1)} %get-tuple-element.48.points, s32[2,4096]{1,0:T(2,128)S(1)} %copy-done.3, f32[512,1024]{1,0:T(8,128)S(1)} %copy-done.2, f32[1,4096]{1,0:T(1,128)S(1)} %get-tuple-element.49.refs_0_, ...), custom_call_target="tpu_custom_call" | custom-call | flops 4294967296 | bytes 8388608 | tf_op jit(solution)/shard_map/energies_and_sums_01/pallas_call | solution.py:341
  21.2 0.0 copy-start
  21.3 0.0 copy-start.1
  21.3 2.5 %collective-permute-start.1 = (f32[2,136,256]{2,1,0:T(8,128)S(1)}, f32[2,136,256]{2,1,0:T(8,128)S(1)}, u32[]{:S(2)}, u32[]{:S(2)}) collective-permute-start(f32[2,136,256]{2,1,0:T(8,128)S(1)} %slice_add_fusion.1), channel_id=1, source_target_pairs={{0,8},{4,20},{8,0},{12,28},{16,24},{20,4},{24,16},{28,12},{1,9},{5... | collective-permute-start | bytes 835592 | tf_op jit(solution)/shard_map/ppermute | solution.py:94
  23.8 0.1 collective-permute-start.2
  23.9 4.4 %collective-permute-done.1.refs_0_ = f32[2,136,256]{2,1,0:T(8,128)S(1)} collective-permute-done((f32[2,136,256]{2,1,0:T(8,128)S(1)}, f32[2,136,256]{2,1,0:T(8,128)S(1)}, u32[]{:S(2)}, u32[]{:S(2)}) %collective-permute-start.1) | collective-permute-done | bytes 278560 | tf_op jit(solution)/shard_map/ppermute | solution.py:94
  28.3 2.1 %collective-permute-start.3 = (f32[136,256]{1,0:T(8,128)S(1)}, f32[136,256]{1,0:T(8,128)S(1)}, u32[]{:S(2)}, u32[]{:S(2)}) collective-permute-start(f32[136,256]{1,0:T(8,128)S(1)} %fusion.1), channel_id=1, source_target_pairs={{0,16},{4,12},{8,24},{12,4},{16,0},{20,28},{24,8},{28,20},{1,17},{... | collective-permute-start | bytes 417800 | tf_op jit(solution)/shard_map/ppermute | solution.py:99
  30.5 0.8 collective-permute-done.2.refs_1_
  31.3 2.4 %collective-permute-start.4 = (f32[128,256]{1,0:T(8,128)S(1)}, f32[128,256]{1,0:T(8,128)S(1)}, u32[]{:S(2)}, u32[]{:S(2)}) collective-permute-start(f32[128,256]{1,0:T(8,128)S(1)} %fusion.4), channel_id=1, source_target_pairs={{0,16},{4,12},{8,24},{12,4},{16,0},{20,28},{24,8},{28,20},{1,17},{... | collective-permute-start | bytes 393224 | tf_op jit(solution)/shard_map/ppermute | solution.py:99
  33.7 2.9 %collective-permute-done.4.refs_3_ = f32[128,256]{1,0:T(8,128)S(1)} collective-permute-done((f32[128,256]{1,0:T(8,128)S(1)}, f32[128,256]{1,0:T(8,128)S(1)}, u32[]{:S(2)}, u32[]{:S(2)}) %collective-permute-start.4) | collective-permute-done | bytes 131104 | tf_op jit(solution)/shard_map/ppermute | solution.py:99
  36.6 0.0 collective-permute-done.3.refs_2_
  36.6 1.5 %refine_half.2 = (f32[128,256]{1,0:T(8,128)S(1)}, f32[128,256]{1,0:T(8,128)S(1)}, f32[72,256]{1,0:T(8,128)S(1)}) custom-call(s32[4]{0:T(128)S(1)} %pad_add_fusion.info, f32[4,264,256]{2,1,0:T(8,128)S(1)} %get-tuple-element.51.own, f32[4,264,256]{2,1,0:T(8,128)S(1)} %collective-permute-done.sibling, f32[2,136,256]{2,1,0:T(8,128)S(1)} %collective-permute-done.1.refs_0_, ...), custom_call_target="tpu_custom_call" | custom-call | tf_op jit(solution)/shard_map/refine_half/pallas_call | solution.py:405
  38.1 2.0 %collective-permute-start.6 = (f32[128,256]{1,0:T(8,128)S(1)}, f32[128,256]{1,0:T(8,128)S(1)}, u32[]{:S(2)}, u32[]{:S(2)}) collective-permute-start(f32[128,256]{1,0:T(8,128)S(1)} %get-tuple-element.64), channel_id=1, source_target_pairs={{0,16},{4,20},{8,24},{12,28},{16,0},{20,4},{24,8},{28,12},{1,17},{... | collective-permute-start | bytes 393224 | tf_op jit(solution)/shard_map/ppermute | solution.py:89
  40.2 1.5 %collective-permute-start.5 = (f32[128,256]{1,0:T(8,128)S(1)}, f32[128,256]{1,0:T(8,128)S(1)}, u32[]{:S(2)}, u32[]{:S(2)}) collective-permute-start(f32[128,256]{1,0:T(8,128)S(1)} %get-tuple-element.65), channel_id=1, source_target_pairs={{0,8},{4,12},{8,0},{12,4},{16,24},{20,28},{24,16},{28,20},{1,9},{5... | collective-permute-start | bytes 393224 | tf_op jit(solution)/shard_map/ppermute | solution.py:89
  41.7 0.5 collective-permute-start.9
  42.2 0.1 collective-permute-start.10
  42.3 2.0 %collective-permute-done.6.refs_1_ = f32[128,256]{1,0:T(8,128)S(1)} collective-permute-done((f32[128,256]{1,0:T(8,128)S(1)}, f32[128,256]{1,0:T(8,128)S(1)}, u32[]{:S(2)}, u32[]{:S(2)}) %collective-permute-start.6) | collective-permute-done | bytes 131104 | tf_op jit(solution)/shard_map/ppermute | solution.py:89
  44.2 2.3 %collective-permute-start.7 = (f32[128,256]{1,0:T(8,128)S(1)}, f32[128,256]{1,0:T(8,128)S(1)}, u32[]{:S(2)}, u32[]{:S(2)}) collective-permute-start(f32[128,256]{1,0:T(8,128)S(1)} %collective-permute-done.6.refs_1_), channel_id=1, source_target_pairs={{0,8},{4,12},{8,0},{12,4},{16,24},{20,28},{24,16},{28,20},{1,9},{5... | collective-permute-start | bytes 393224 | tf_op jit(solution)/shard_map/ppermute | solution.py:89
  46.5 0.0 collective-permute-done.5.refs_0_
  46.5 0.7 collective-permute-start.8
  47.3 3.5 %fetch_points.1.points = bf16[4096,1024]{1,0:T(8,128)(2,1)S(1)} custom-call(bf16[4096,1024]{1,0:T(8,128)(2,1)} %points.3, f32[128,256]{1,0:T(8,128)S(1)} %collective-permute-done.5.refs_0_, f32[128,256]{1,0:T(8,128)S(1)} %collective-permute-done.6.refs_1_), custom_call_target="tpu_custom_call" | custom-call | bytes 16777216 | tf_op jit(solution)/shard_map/fetch_points/pallas_call | solution.py:280
  50.8 0.0 collective-permute-done.10
  50.8 0.0 collective-permute-done.7
  50.8 0.7 collective-permute-done.8
  51.6 0.1 collective-permute-start.11
  51.7 1.6 %collective-permute-start.12 = (f32[104,256]{1,0:T(8,128)S(1)}, f32[104,256]{1,0:T(8,128)S(1)}, u32[]{:S(2)}, u32[]{:S(2)}) collective-permute-start(f32[104,256]{1,0:T(8,128)S(1)} %pad_maximum_fusion.3), channel_id=1, source_target_pairs={{0,1},{1,0},{2,3},{3,2},{4,5},{5,4},{6,7},{7,6},{8,9},{9,8},{10,11... | collective-permute-start | bytes 319496 | tf_op jit(solution)/shard_map/ppermute | solution.py:89
  53.4 7.6 %energies_and_sums_10.1 = (f32[4,264,256]{2,1,0:T(8,128)S(1)}, f32[2,4096]{1,0:T(2,128)S(1)}) custom-call(s32[4]{0:T(128)S(1)} %pad_add_fusion.info, bf16[4096,1024]{1,0:T(8,128)(2,1)S(1)} %fetch_points.1.points, s32[2,4096]{1,0:T(2,128)S(1)} %copy-done.3, f32[8,128,256]{2,1,0:T(8,128)S(1)} %bitcast_dynamic-update-slice_fusion.fine, ...), custom_call_target="tpu_custom_call" | custom-call | flops 4294967296 | bytes 8388608 | tf_op jit(solution)/shard_map/energies_and_sums_10/pallas_call | solution.py:341
  61.0 0.3 collective-permute-start.14
  61.2 0.4 collective-permute-start.13
  61.6 7.8 %energies_and_sums_11.1 = (f32[4,264,256]{2,1,0:T(8,128)S(1)}, f32[2,4096]{1,0:T(2,128)S(1)}) custom-call(s32[4]{0:T(128)S(1)} %pad_add_fusion.info, bf16[4096,1024]{1,0:T(8,128)(2,1)S(1)} %fetch_points.1.points, s32[2,4096]{1,0:T(2,128)S(1)} %copy-done.3, f32[8,128,256]{2,1,0:T(8,128)S(1)} %collective-permute-done.11.fine, ...), custom_call_target="tpu_custom_call" | custom-call | flops 4294967296 | bytes 8388608 | tf_op jit(solution)/shard_map/energies_and_sums_11/pallas_call | solution.py:341
  69.6 1.2 %collective-permute-start.15 = (f32[2,136,256]{2,1,0:T(8,128)S(1)}, f32[2,136,256]{2,1,0:T(8,128)S(1)}, u32[]{:S(2)}, u32[]{:S(2)}) collective-permute-start(f32[2,136,256]{2,1,0:T(8,128)S(1)} %slice_add_fusion), channel_id=1, source_target_pairs={{0,8},{4,20},{8,0},{12,28},{16,24},{20,4},{24,16},{28,12},{1,9},{5... | collective-permute-start | bytes 835592 | tf_op jit(solution)/shard_map/ppermute | solution.py:94
  70.8 0.9 collective-permute-start.16
  71.7 2.6 %collective-permute-start.17 = (f32[104,256]{1,0:T(8,128)S(1)}, f32[104,256]{1,0:T(8,128)S(1)}, u32[]{:S(2)}, u32[]{:S(2)}) collective-permute-start(f32[104,256]{1,0:T(8,128)S(1)} %pad_maximum_fusion.4.refs_5_), channel_id=1, source_target_pairs={{0,2},{1,3},{2,0},{3,1},{4,6},{5,7},{6,4},{7,5},{8,10},{9,11},{10,... | collective-permute-start | bytes 319496 | tf_op jit(solution)/shard_map/ppermute | solution.py:89
  74.2 5.0 %collective-permute-done.17.refs_6_ = f32[104,256]{1,0:T(8,128)S(1)} collective-permute-done((f32[104,256]{1,0:T(8,128)S(1)}, f32[104,256]{1,0:T(8,128)S(1)}, u32[]{:S(2)}, u32[]{:S(2)}) %collective-permute-start.17) | collective-permute-done | bytes 106528 | tf_op jit(solution)/shard_map/ppermute | solution.py:89
  79.3 0.8 collective-permute-start.18
  80.1 0.7 fusion.3
  80.8 1.3 %collective-permute-start.19 = (f32[128,256]{1,0:T(8,128)}, f32[128,256]{1,0:T(8,128)S(1)}, u32[]{:S(2)}, u32[]{:S(2)}) collective-permute-start(f32[128,256]{1,0:T(8,128)} %fusion.3), channel_id=1, source_target_pairs={{0,16},{4,12},{8,24},{12,4},{16,0},{20,28},{24,8},{28,20},{1,17},{... | collective-permute-start | bytes 393224 | tf_op jit(solution)/shard_map/ppermute | solution.py:99
  82.1 3.8 %collective-permute-done.19.refs_3_ = f32[128,256]{1,0:T(8,128)S(1)} collective-permute-done((f32[128,256]{1,0:T(8,128)}, f32[128,256]{1,0:T(8,128)S(1)}, u32[]{:S(2)}, u32[]{:S(2)}) %collective-permute-start.19) | collective-permute-done | bytes 131104 | tf_op jit(solution)/shard_map/ppermute | solution.py:99
  86.0 1.6 %refine_half.3 = (f32[128,256]{1,0:T(8,128)S(1)}, f32[128,256]{1,0:T(8,128)S(1)}, f32[72,256]{1,0:T(8,128)S(1)}) custom-call(s32[4]{0:T(128)S(1)} %pad_add_fusion.info, f32[4,264,256]{2,1,0:T(8,128)S(1)} %get-tuple-element.72.own, f32[4,264,256]{2,1,0:T(8,128)S(1)} %collective-permute-done.14.sibling, f32[2,136,256]{2,1,0:T(8,128)S(1)} %collective-permute-done.15.refs_0_, ...), custom_call_target="tpu_custom_call" | custom-call | tf_op jit(solution)/shard_map/refine_half/pallas_call | solution.py:405
  87.6 0.2 collective-permute-start.26
  87.8 1.1 collective-permute-start.20
  88.9 1.4 %collective-permute-start.21 = (f32[128,256]{1,0:T(8,128)S(1)}, f32[128,256]{1,0:T(8,128)S(1)}, u32[]{:S(2)}, u32[]{:S(2)}) collective-permute-start(f32[128,256]{1,0:T(8,128)S(1)} %get-tuple-element.88), channel_id=1, source_target_pairs={{0,16},{4,20},{8,24},{12,28},{16,0},{20,4},{24,8},{28,12},{1,17},{... | collective-permute-start | bytes 393224 | tf_op jit(solution)/shard_map/ppermute | solution.py:89
  90.3 2.1 %collective-permute-done.26 = f32[104,256]{1,0:T(8,128)S(1)} collective-permute-done((f32[104,256]{1,0:T(8,128)S(1)}, f32[104,256]{1,0:T(8,128)S(1)}, u32[]{:S(2)}, u32[]{:S(2)}) %collective-permute-start.26) | collective-permute-done | bytes 106528 | tf_op jit(solution)/shard_map/ppermute | solution.py:89
  92.4 2.7 %collective-permute-start.27 = (f32[104,256]{1,0:T(8,128)S(1)}, f32[104,256]{1,0:T(8,128)S(1)}, u32[]{:S(2)}, u32[]{:S(2)}) collective-permute-start(f32[104,256]{1,0:T(8,128)S(1)} %pad_maximum_fusion.6), channel_id=1, source_target_pairs={{0,2},{1,3},{2,0},{3,1},{4,6},{5,7},{6,4},{7,5},{8,10},{9,11},{10,... | collective-permute-start | bytes 319496 | tf_op jit(solution)/shard_map/ppermute | solution.py:89
  95.1 2.0 %collective-permute-start.23 = (f32[128,256]{1,0:T(8,128)S(1)}, f32[128,256]{1,0:T(8,128)S(1)}, u32[]{:S(2)}, u32[]{:S(2)}) collective-permute-start(f32[128,256]{1,0:T(8,128)S(1)} %collective-permute-done.20), channel_id=1, source_target_pairs={{0,16},{4,20},{8,24},{12,28},{16,0},{20,4},{24,8},{28,12},{1,17},{... | collective-permute-start | bytes 393224 | tf_op jit(solution)/shard_map/ppermute | solution.py:89
  97.1 1.1 %collective-permute-start.22 = (f32[128,256]{1,0:T(8,128)S(1)}, f32[128,256]{1,0:T(8,128)S(1)}, u32[]{:S(2)}, u32[]{:S(2)}) collective-permute-start(f32[128,256]{1,0:T(8,128)S(1)} %collective-permute-done.21), channel_id=1, source_target_pairs={{0,8},{4,12},{8,0},{12,4},{16,24},{20,28},{24,16},{28,20},{1,9},{5... | collective-permute-start | bytes 393224 | tf_op jit(solution)/shard_map/ppermute | solution.py:89
  98.2 0.2 collective-permute-start.25
  98.5 0.8 collective-permute-start.24
  99.3 2.5 %collective-permute-start.30 = (f32[72,256]{1,0:T(8,128)S(1)}, f32[72,256]{1,0:T(8,128)S(1)}, u32[]{:S(2)}, u32[]{:S(2)}) collective-permute-start(f32[72,256]{1,0:T(8,128)S(1)} %slice_add_fusion.11), channel_id=1, source_target_pairs={{0,24},{4,28},{8,16},{12,20},{16,8},{20,12},{24,0},{28,4},{1,25},{... | collective-permute-start | bytes 221192 | tf_op jit(solution)/shard_map/ppermute | solution.py:89
  101.9 1.0 collective-permute-start.29
  102.9 1.1 %collective-permute-start.28 = (f32[72,256]{1,0:T(8,128)S(1)}, f32[72,256]{1,0:T(8,128)S(1)}, u32[]{:S(2)}, u32[]{:S(2)}) collective-permute-start(f32[72,256]{1,0:T(8,128)S(1)} %slice_add_fusion.11), channel_id=1, source_target_pairs={{0,8},{4,12},{8,0},{12,4},{16,24},{20,28},{24,16},{28,20},{1,9},{5... | collective-permute-start | bytes 221192 | tf_op jit(solution)/shard_map/ppermute | solution.py:89
  104.1 0.1 collective-permute-start.31
  104.1 0.0 collective-permute-done.24
  104.2 0.5 collective-permute-start.32
  104.7 0.7 collective-permute-done.30
  105.5 0.8 collective-permute-done.29
  106.3 0.9 collective-permute-done.28
  107.3 0.1 collective-permute-start.33
  107.3 0.7 maximum_multiply_fusion
  108.0 0.9 collective-permute-done.33.refs_5_
  108.9 2.1 %place_blocks.1 = (f32[512,1024]{1,0:T(8,128)}, f32[64,1024]{1,0:T(8,128)}) custom-call(s32[4]{0:T(128)S(1)} %pad_add_fusion.info, f32[4,128,256]{2,1,0:T(8,128)S(1)} %pad_maximum_fusion.refs_0_, f32[4,128,256]{2,1,0:T(8,128)S(1)} %pad_maximum_fusion.1.refs_1_, f32[4,72,256]{2,1,0:T(8,128)S(1)} %pad_maximum_fusion.2.refs_2_, ...), custom_call_target="tpu_custom_call" | custom-call | tf_op jit(solution)/shard_map/place_blocks/pallas_call | solution.py:507
  (59 shorter events, 0.7 us)
Async XLA Ops:
  0.7 12.8 %copy-start.2 = (f32[512,1024]{1,0:T(8,128)S(1)}, f32[512,1024]{1,0:T(8,128)}, u32[]{:S(2)}) copy-start(f32[512,1024]{1,0:T(8,128)} %fine.3) | copy-start | bytes 6291460
  0.7 12.8 %copy-start.3 = (s32[2,4096]{1,0:T(2,128)S(1)}, s32[2,4096]{1,0:T(2,128)}, u32[]{:S(2)}) copy-start(s32[2,4096]{1,0:T(2,128)} %assign.7) | copy-start | bytes 98308
  12.9 8.3 %collective-permute-start = (f32[4,264,256]{2,1,0:T(8,128)S(1)}, f32[4,264,256]{2,1,0:T(8,128)S(1)}, u32[]{:S(2)}, u32[]{:S(2)}) collective-permute-start(f32[4,264,256]{2,1,0:T(8,128)S(1)} %get-tuple-element.52), channel_id=1, source_target_pairs={{0,4},{4,0},{8,12},{12,8},{16,20},{20,16},{24,28},{28,24},{1,5},{5... | collective-permute-start | bytes 3244040 | tf_op jit(solution)/shard_map/ppermute | solution.py:89
  21.2 15.4 %copy-start = (f32[64,1024]{1,0:T(8,128)S(1)}, f32[64,1024]{1,0:T(8,128)}, u32[]{:S(2)}) copy-start(f32[64,1024]{1,0:T(8,128)} %refs_5_.1) | copy-start | bytes 786436
  21.3 15.4 %copy-start.1 = (s32[512]{0:T(512)S(1)}, s32[512]{0:T(512)}, u32[]{:S(2)}) copy-start(s32[512]{0:T(512)} %param.9) | copy-start | bytes 6148
  21.3 7.0 %collective-permute-start.1 = (f32[2,136,256]{2,1,0:T(8,128)S(1)}, f32[2,136,256]{2,1,0:T(8,128)S(1)}, u32[]{:S(2)}, u32[]{:S(2)}) collective-permute-start(f32[2,136,256]{2,1,0:T(8,128)S(1)} %slice_add_fusion.1), channel_id=1, source_target_pairs={{0,8},{4,20},{8,0},{12,28},{16,24},{20,4},{24,16},{28,12},{1,9},{5... | collective-permute-start | bytes 835592 | tf_op jit(solution)/shard_map/ppermute | solution.py:94
  23.8 7.4 %collective-permute-start.2 = (f32[2,128,256]{2,1,0:T(8,128)S(1)}, f32[2,128,256]{2,1,0:T(8,128)S(1)}, u32[]{:S(2)}, u32[]{:S(2)}) collective-permute-start(f32[2,128,256]{2,1,0:T(8,128)S(1)} %slice_add_fusion.3), channel_id=1, source_target_pairs={{0,8},{4,20},{8,0},{12,28},{16,24},{20,4},{24,16},{28,12},{1,9},{5... | collective-permute-start | bytes 786440 | tf_op jit(solution)/shard_map/ppermute | solution.py:94
  28.3 8.3 %collective-permute-start.3 = (f32[136,256]{1,0:T(8,128)S(1)}, f32[136,256]{1,0:T(8,128)S(1)}, u32[]{:S(2)}, u32[]{:S(2)}) collective-permute-start(f32[136,256]{1,0:T(8,128)S(1)} %fusion.1), channel_id=1, source_target_pairs={{0,16},{4,12},{8,24},{12,4},{16,0},{20,28},{24,8},{28,20},{1,17},{... | collective-permute-start | bytes 417800 | tf_op jit(solution)/shard_map/ppermute | solution.py:99
  31.3 5.4 %collective-permute-start.4 = (f32[128,256]{1,0:T(8,128)S(1)}, f32[128,256]{1,0:T(8,128)S(1)}, u32[]{:S(2)}, u32[]{:S(2)}) collective-permute-start(f32[128,256]{1,0:T(8,128)S(1)} %fusion.4), channel_id=1, source_target_pairs={{0,16},{4,12},{8,24},{12,4},{16,0},{20,28},{24,8},{28,20},{1,17},{... | collective-permute-start | bytes 393224 | tf_op jit(solution)/shard_map/ppermute | solution.py:99
  38.1 6.1 %collective-permute-start.6 = (f32[128,256]{1,0:T(8,128)S(1)}, f32[128,256]{1,0:T(8,128)S(1)}, u32[]{:S(2)}, u32[]{:S(2)}) collective-permute-start(f32[128,256]{1,0:T(8,128)S(1)} %get-tuple-element.64), channel_id=1, source_target_pairs={{0,16},{4,20},{8,24},{12,28},{16,0},{20,4},{24,8},{28,12},{1,17},{... | collective-permute-start | bytes 393224 | tf_op jit(solution)/shard_map/ppermute | solution.py:89
  40.2 6.4 %collective-permute-start.5 = (f32[128,256]{1,0:T(8,128)S(1)}, f32[128,256]{1,0:T(8,128)S(1)}, u32[]{:S(2)}, u32[]{:S(2)}) collective-permute-start(f32[128,256]{1,0:T(8,128)S(1)} %get-tuple-element.65), channel_id=1, source_target_pairs={{0,8},{4,12},{8,0},{12,4},{16,24},{20,28},{24,16},{28,20},{1,9},{5... | collective-permute-start | bytes 393224 | tf_op jit(solution)/shard_map/ppermute | solution.py:89
  41.7 9.1 %collective-permute-start.9 = (f32[128,256]{1,0:T(8,128)S(1)}, f32[128,256]{1,0:T(8,128)S(1)}, u32[]{:S(2)}, u32[]{:S(2)}) collective-permute-start(f32[128,256]{1,0:T(8,128)S(1)} %get-tuple-element.64), channel_id=1, source_target_pairs={{0,8},{4,12},{8,0},{12,4},{16,24},{20,28},{24,16},{28,20},{1,9},{5... | collective-permute-start | bytes 393224 | tf_op jit(solution)/shard_map/ppermute | solution.py:89
  42.2 8.6 %collective-permute-start.10 = (f32[128,256]{1,0:T(8,128)S(1)}, f32[128,256]{1,0:T(8,128)S(1)}, u32[]{:S(2)}, u32[]{:S(2)}) collective-permute-start(f32[128,256]{1,0:T(8,128)S(1)} %get-tuple-element.65), channel_id=1, source_target_pairs={{0,16},{4,20},{8,24},{12,28},{16,0},{20,4},{24,8},{28,12},{1,17},{... | collective-permute-start | bytes 393224 | tf_op jit(solution)/shard_map/ppermute | solution.py:89
  44.2 6.6 %collective-permute-start.7 = (f32[128,256]{1,0:T(8,128)S(1)}, f32[128,256]{1,0:T(8,128)S(1)}, u32[]{:S(2)}, u32[]{:S(2)}) collective-permute-start(f32[128,256]{1,0:T(8,128)S(1)} %collective-permute-done.6.refs_1_), channel_id=1, source_target_pairs={{0,8},{4,12},{8,0},{12,4},{16,24},{20,28},{24,16},{28,20},{1,9},{5... | collective-permute-start | bytes 393224 | tf_op jit(solution)/shard_map/ppermute | solution.py:89
  46.5 5.0 %collective-permute-start.8 = (f32[128,256]{1,0:T(8,128)S(1)}, f32[128,256]{1,0:T(8,128)S(1)}, u32[]{:S(2)}, u32[]{:S(2)}) collective-permute-start(f32[128,256]{1,0:T(8,128)S(1)} %collective-permute-done.5.refs_0_), channel_id=1, source_target_pairs={{0,16},{4,20},{8,24},{12,28},{16,0},{20,4},{24,8},{28,12},{1,17},{... | collective-permute-start | bytes 393224 | tf_op jit(solution)/shard_map/ppermute | solution.py:89
  51.6 10.0 %collective-permute-start.11 = (f32[8,128,256]{2,1,0:T(8,128)S(1)}, f32[8,128,256]{2,1,0:T(8,128)S(1)}, u32[]{:S(2)}, u32[]{:S(2)}) collective-permute-start(f32[8,128,256]{2,1,0:T(8,128)S(1)} %bitcast_dynamic-update-slice_fusion.fine), channel_id=1, source_target_pairs={{0,4},{4,0},{8,12},{12,8},{16,20},{20,16},{24,28},{28,24},{1,5},{5... | collective-permute-start | bytes 3145736 | tf_op jit(solution)/shard_map/ppermute | solution.py:89
  51.7 9.2 %collective-permute-start.12 = (f32[104,256]{1,0:T(8,128)S(1)}, f32[104,256]{1,0:T(8,128)S(1)}, u32[]{:S(2)}, u32[]{:S(2)}) collective-permute-start(f32[104,256]{1,0:T(8,128)S(1)} %pad_maximum_fusion.3), channel_id=1, source_target_pairs={{0,1},{1,0},{2,3},{3,2},{4,5},{5,4},{6,7},{7,6},{8,9},{9,8},{10,11... | collective-permute-start | bytes 319496 | tf_op jit(solution)/shard_map/ppermute | solution.py:89
  61.0 8.5 %collective-permute-start.14 = (f32[4,264,256]{2,1,0:T(8,128)S(1)}, f32[4,264,256]{2,1,0:T(8,128)S(1)}, u32[]{:S(2)}, u32[]{:S(2)}) collective-permute-start(f32[4,264,256]{2,1,0:T(8,128)S(1)} %get-tuple-element.73), channel_id=1, source_target_pairs={{0,4},{4,0},{8,12},{12,8},{16,20},{20,16},{24,28},{28,24},{1,5},{5... | collective-permute-start | bytes 3244040 | tf_op jit(solution)/shard_map/ppermute | solution.py:89
  61.2 8.2 %collective-permute-start.13 = (f32[72,256]{1,0:T(8,128)S(1)}, f32[72,256]{1,0:T(8,128)S(1)}, u32[]{:S(2)}, u32[]{:S(2)}) collective-permute-start(f32[72,256]{1,0:T(8,128)S(1)} %slice_add_fusion.13), channel_id=1, source_target_pairs={{0,4},{4,0},{8,12},{12,8},{16,20},{20,16},{24,28},{28,24},{1,5},{5... | collective-permute-start | bytes 221192 | tf_op jit(solution)/shard_map/ppermute | solution.py:89
  69.6 9.7 %collective-permute-start.15 = (f32[2,136,256]{2,1,0:T(8,128)S(1)}, f32[2,136,256]{2,1,0:T(8,128)S(1)}, u32[]{:S(2)}, u32[]{:S(2)}) collective-permute-start(f32[2,136,256]{2,1,0:T(8,128)S(1)} %slice_add_fusion), channel_id=1, source_target_pairs={{0,8},{4,20},{8,0},{12,28},{16,24},{20,4},{24,16},{28,12},{1,9},{5... | collective-permute-start | bytes 835592 | tf_op jit(solution)/shard_map/ppermute | solution.py:94
  70.8 8.5 %collective-permute-start.16 = (f32[2,128,256]{2,1,0:T(8,128)S(1)}, f32[2,128,256]{2,1,0:T(8,128)S(1)}, u32[]{:S(2)}, u32[]{:S(2)}) collective-permute-start(f32[2,128,256]{2,1,0:T(8,128)S(1)} %slice_add_fusion.2), channel_id=1, source_target_pairs={{0,8},{4,20},{8,0},{12,28},{16,24},{20,4},{24,16},{28,12},{1,9},{5... | collective-permute-start | bytes 786440 | tf_op jit(solution)/shard_map/ppermute | solution.py:94
  71.7 7.6 %collective-permute-start.17 = (f32[104,256]{1,0:T(8,128)S(1)}, f32[104,256]{1,0:T(8,128)S(1)}, u32[]{:S(2)}, u32[]{:S(2)}) collective-permute-start(f32[104,256]{1,0:T(8,128)S(1)} %pad_maximum_fusion.4.refs_5_), channel_id=1, source_target_pairs={{0,2},{1,3},{2,0},{3,1},{4,6},{5,7},{6,4},{7,5},{8,10},{9,11},{10,... | collective-permute-start | bytes 319496 | tf_op jit(solution)/shard_map/ppermute | solution.py:89
  79.3 6.6 %collective-permute-start.18 = (f32[136,256]{1,0:T(8,128)S(1)}, f32[136,256]{1,0:T(8,128)S(1)}, u32[]{:S(2)}, u32[]{:S(2)}) collective-permute-start(f32[136,256]{1,0:T(8,128)S(1)} %fusion), channel_id=1, source_target_pairs={{0,16},{4,12},{8,24},{12,4},{16,0},{20,28},{24,8},{28,20},{1,17},{... | collective-permute-start | bytes 417800 | tf_op jit(solution)/shard_map/ppermute | solution.py:99
  80.8 5.2 %collective-permute-start.19 = (f32[128,256]{1,0:T(8,128)}, f32[128,256]{1,0:T(8,128)S(1)}, u32[]{:S(2)}, u32[]{:S(2)}) collective-permute-start(f32[128,256]{1,0:T(8,128)} %fusion.3), channel_id=1, source_target_pairs={{0,16},{4,12},{8,24},{12,4},{16,0},{20,28},{24,8},{28,20},{1,17},{... | collective-permute-start | bytes 393224 | tf_op jit(solution)/shard_map/ppermute | solution.py:99
  87.6 4.8 %collective-permute-start.26 = (f32[104,256]{1,0:T(8,128)S(1)}, f32[104,256]{1,0:T(8,128)S(1)}, u32[]{:S(2)}, u32[]{:S(2)}) collective-permute-start(f32[104,256]{1,0:T(8,128)S(1)} %pad_maximum_fusion.5), channel_id=1, source_target_pairs={{0,1},{1,0},{2,3},{3,2},{4,5},{5,4},{6,7},{7,6},{8,9},{9,8},{10,11... | collective-permute-start | bytes 319496 | tf_op jit(solution)/shard_map/ppermute | solution.py:89
  87.8 7.3 %collective-permute-start.20 = (f32[128,256]{1,0:T(8,128)S(1)}, f32[128,256]{1,0:T(8,128)S(1)}, u32[]{:S(2)}, u32[]{:S(2)}) collective-permute-start(f32[128,256]{1,0:T(8,128)S(1)} %get-tuple-element.89), channel_id=1, source_target_pairs={{0,8},{4,12},{8,0},{12,4},{16,24},{20,28},{24,16},{28,20},{1,9},{5... | collective-permute-start | bytes 393224 | tf_op jit(solution)/shard_map/ppermute | solution.py:89
  88.9 6.3 %collective-permute-start.21 = (f32[128,256]{1,0:T(8,128)S(1)}, f32[128,256]{1,0:T(8,128)S(1)}, u32[]{:S(2)}, u32[]{:S(2)}) collective-permute-start(f32[128,256]{1,0:T(8,128)S(1)} %get-tuple-element.88), channel_id=1, source_target_pairs={{0,16},{4,20},{8,24},{12,28},{16,0},{20,4},{24,8},{28,12},{1,17},{... | collective-permute-start | bytes 393224 | tf_op jit(solution)/shard_map/ppermute | solution.py:89
  92.4 6.9 %collective-permute-start.27 = (f32[104,256]{1,0:T(8,128)S(1)}, f32[104,256]{1,0:T(8,128)S(1)}, u32[]{:S(2)}, u32[]{:S(2)}) collective-permute-start(f32[104,256]{1,0:T(8,128)S(1)} %pad_maximum_fusion.6), channel_id=1, source_target_pairs={{0,2},{1,3},{2,0},{3,1},{4,6},{5,7},{6,4},{7,5},{8,10},{9,11},{10,... | collective-permute-start | bytes 319496 | tf_op jit(solution)/shard_map/ppermute | solution.py:89
  95.1 6.7 %collective-permute-start.23 = (f32[128,256]{1,0:T(8,128)S(1)}, f32[128,256]{1,0:T(8,128)S(1)}, u32[]{:S(2)}, u32[]{:S(2)}) collective-permute-start(f32[128,256]{1,0:T(8,128)S(1)} %collective-permute-done.20), channel_id=1, source_target_pairs={{0,16},{4,20},{8,24},{12,28},{16,0},{20,4},{24,8},{28,12},{1,17},{... | collective-permute-start | bytes 393224 | tf_op jit(solution)/shard_map/ppermute | solution.py:89
  97.1 5.8 %collective-permute-start.22 = (f32[128,256]{1,0:T(8,128)S(1)}, f32[128,256]{1,0:T(8,128)S(1)}, u32[]{:S(2)}, u32[]{:S(2)}) collective-permute-start(f32[128,256]{1,0:T(8,128)S(1)} %collective-permute-done.21), channel_id=1, source_target_pairs={{0,8},{4,12},{8,0},{12,4},{16,24},{20,28},{24,16},{28,20},{1,9},{5... | collective-permute-start | bytes 393224 | tf_op jit(solution)/shard_map/ppermute | solution.py:89
  98.2 5.8 %collective-permute-start.25 = (f32[128,256]{1,0:T(8,128)S(1)}, f32[128,256]{1,0:T(8,128)S(1)}, u32[]{:S(2)}, u32[]{:S(2)}) collective-permute-start(f32[128,256]{1,0:T(8,128)S(1)} %get-tuple-element.89), channel_id=1, source_target_pairs={{0,16},{4,20},{8,24},{12,28},{16,0},{20,4},{24,8},{28,12},{1,17},{... | collective-permute-start | bytes 393224 | tf_op jit(solution)/shard_map/ppermute | solution.py:89
  98.5 5.7 %collective-permute-start.24 = (f32[128,256]{1,0:T(8,128)S(1)}, f32[128,256]{1,0:T(8,128)S(1)}, u32[]{:S(2)}, u32[]{:S(2)}) collective-permute-start(f32[128,256]{1,0:T(8,128)S(1)} %get-tuple-element.88), channel_id=1, source_target_pairs={{0,8},{4,12},{8,0},{12,4},{16,24},{20,28},{24,16},{28,20},{1,9},{5... | collective-permute-start | bytes 393224 | tf_op jit(solution)/shard_map/ppermute | solution.py:89
  99.3 6.2 %collective-permute-start.30 = (f32[72,256]{1,0:T(8,128)S(1)}, f32[72,256]{1,0:T(8,128)S(1)}, u32[]{:S(2)}, u32[]{:S(2)}) collective-permute-start(f32[72,256]{1,0:T(8,128)S(1)} %slice_add_fusion.11), channel_id=1, source_target_pairs={{0,24},{4,28},{8,16},{12,20},{16,8},{20,12},{24,0},{28,4},{1,25},{... | collective-permute-start | bytes 221192 | tf_op jit(solution)/shard_map/ppermute | solution.py:89
  101.9 4.4 %collective-permute-start.29 = (f32[72,256]{1,0:T(8,128)S(1)}, f32[72,256]{1,0:T(8,128)S(1)}, u32[]{:S(2)}, u32[]{:S(2)}) collective-permute-start(f32[72,256]{1,0:T(8,128)S(1)} %slice_add_fusion.11), channel_id=1, source_target_pairs={{0,16},{4,20},{8,24},{12,28},{16,0},{20,4},{24,8},{28,12},{1,17},{... | collective-permute-start | bytes 221192 | tf_op jit(solution)/shard_map/ppermute | solution.py:89
  102.9 4.4 %collective-permute-start.28 = (f32[72,256]{1,0:T(8,128)S(1)}, f32[72,256]{1,0:T(8,128)S(1)}, u32[]{:S(2)}, u32[]{:S(2)}) collective-permute-start(f32[72,256]{1,0:T(8,128)S(1)} %slice_add_fusion.11), channel_id=1, source_target_pairs={{0,8},{4,12},{8,0},{12,4},{16,24},{20,28},{24,16},{28,20},{1,9},{5... | collective-permute-start | bytes 221192 | tf_op jit(solution)/shard_map/ppermute | solution.py:89
  104.1 4.8 %collective-permute-start.31 = (f32[4,128,256]{2,1,0:T(8,128)S(1)}, f32[4,128,256]{2,1,0:T(8,128)S(1)}, u32[]{:S(2)}, u32[]{:S(2)}) collective-permute-start(f32[4,128,256]{2,1,0:T(8,128)S(1)} %pad_maximum_fusion.refs_0_), channel_id=1, source_target_pairs={{0,4},{4,0},{8,12},{12,8},{16,20},{20,16},{24,28},{28,24},{1,5},{5... | collective-permute-start | bytes 1572872 | tf_op jit(solution)/shard_map/ppermute | solution.py:89
  104.2 4.7 %collective-permute-start.32 = (f32[4,128,256]{2,1,0:T(8,128)S(1)}, f32[4,128,256]{2,1,0:T(8,128)S(1)}, u32[]{:S(2)}, u32[]{:S(2)}) collective-permute-start(f32[4,128,256]{2,1,0:T(8,128)S(1)} %pad_maximum_fusion.1.refs_1_), channel_id=1, source_target_pairs={{0,4},{4,0},{8,12},{12,8},{16,20},{20,16},{24,28},{28,24},{1,5},{5... | collective-permute-start | bytes 1572872 | tf_op jit(solution)/shard_map/ppermute | solution.py:89
  107.3 1.6 %collective-permute-start.33 = (f32[4,72,256]{2,1,0:T(8,128)S(1)}, f32[4,72,256]{2,1,0:T(8,128)S(1)}, u32[]{:S(2)}, u32[]{:S(2)}) collective-permute-start(f32[4,72,256]{2,1,0:T(8,128)S(1)} %pad_maximum_fusion.2.refs_2_), channel_id=1, source_target_pairs={{0,4},{4,0},{8,12},{12,8},{16,20},{20,16},{24,28},{28,24},{1,5},{5... | collective-permute-start | bytes 884744 | tf_op jit(solution)/shard_map/ppermute | solution.py:89

commit v17 on v16

--- a/solution.py
+++ b/solution.py
@@ -235,8 +235,15 @@
 
     if stream:
         load_assign.wait()
-    arrive(0, True)
-    multiply(0, even)
+        for half in range(2):
+            load(0, half).wait()
+            load(1, half).start()
+            part = slice(half * (tile // 2), (half + 1) * (tile // 2))
+            even[:, part] = lax.dot_general(
+                low[...], kept[part, :], (((1,), (1,)), ((), ())), preferred_element_type=jnp.float32
+            )
+    else:
+        multiply(0, even)
 
     @pl.loop(0, tiles // 2 - 1)
     def _(pair):
@@ -294,10 +301,10 @@
 def run_pass(info, points, fine_assign, fine, squares, seen, *, pass_index, flip, rows):
     count, width = points.shape
     block_width = width // SLOTS
-    tile = 1024
     initial = pass_index == 0
     chained = seen is not None
     stream = squares is None
+    tile = 1024 if stream or count % 4096 else 2048
     if stream:
         in_specs = [AWAY] * 3
         args = [far_off(points), far_off(fine_assign), far_off(fine)]
@@ -344,12 +351,24 @@
         in_specs=[SCALARS, *in_specs],
         out_specs=[HERE] * len(out_shape),
         scratch_shapes=scratch,
-        compiler_params=pltpu.CompilerParams(vmem_limit_bytes=20 * 2**20),
+        compiler_params=pltpu.CompilerParams(vmem_limit_bytes=24 * 2**20),
         cost_estimate=pl.CostEstimate(
             flops=4 * rows * count * width, bytes_accessed=2 * count * width, transcendentals=0
         ),
         name=f"energies_and_sums_{pass_index}{int(chained)}",
     )(info, *args)
+
+
+def one_hot_dot(table, value, dims):
+    table = table.astype(jnp.bfloat16)
+    total = 0.0
+    for _ in range(3):
+        term = value.astype(jnp.bfloat16)
+        value = value - term.astype(jnp.float32)
+        total = total + lax.dot_general(
+            table, term, dims, preferred_element_type=jnp.float32
+        )
+    return total
 
 
 def refine_body(info, own, sibling, *refs, flip):
@@ -373,28 +392,16 @@
     table = (
         lax.broadcasted_iota(jnp.int32, (NC, rows), 0) == owner
     ).astype(jnp.float32)
-    lookup = lax.dot_general(
-        table,
-        coarse,
-        (((0,), (0,)), ((), ())),
-        precision=HIGHEST,
-        preferred_element_type=jnp.float32,
-    )
+    lookup = one_hot_dot(table, coarse, (((0,), (0,)), ((), ())))
     new = (totals + prior_weight * lookup) / (counts + prior_weight)
     top[...] = new[:mid]
     low[...] = new[mid:]
     prior = jnp.where(info[3] == 0, prior_weight, 0.0)
-    part[:NC, :] = prior * coarse + jnp.dot(
-        table, counts * new, precision=HIGHEST, preferred_element_type=jnp.float32
-    )
+    part[:NC, :] = prior * coarse + one_hot_dot(table, counts * new, (((1,), (0,)), ((), ())))
     part[NC:, :] = jnp.zeros((TAIL, part.shape[1]), jnp.float32)
-    part[NC:, :NC] = prior + lax.dot_general(
-        counts_row,
-        table,
-        (((1,), (1,)), ((), ())),
-        precision=HIGHEST,
-        preferred_element_type=jnp.float32,
-    )
+    weight = jnp.sum(table * counts_row[:1], axis=1, keepdims=True)
+    weight = jnp.broadcast_to(weight, (NC, 128)).T[:TAIL]
+    part[NC:, :NC] = prior + weight
 
 
 def refine_half(info, own, sibling, incoming, owners, coarse, *, flip):

time: 111 us -> 111 us (level)
  no operation moved by 1% of the time
where the time goes in v17:
time: 111 us
  Pallas kernels  43.8 us (39%)
  starting transfers between devices  39 us (35%)
  waiting for transfers between devices  25.2 us (23%)
  other arithmetic  1.86 us (2%)
  between operations  1.22 us (1%)
    pallas_call x4, Pallas kernels, run_pass(): pl.pallas_call(body, out_shape=out_shape, in_specs=[SCALARS, *in_specs],...  35.9 us
    ppermute x26, starting transfers between devices, swap(): return lax.ppermute(value, axis, [(i, i ^ bit) for i in range(size)])  27.7 us
    ppermute x26, waiting for transfers between devices, swap(): return lax.ppermute(value, axis, [(i, i ^ bit) for i in range(size)])  13.2 us
    ppermute x4, waiting for transfers between devices, swap_second(): return lax.ppermute(value, 'pts', pairs)  6.8 us
    ppermute x4, starting transfers between devices, swap_second(): return lax.ppermute(value, 'pts', pairs)  6.66 us
    ppermute x4, waiting for transfers between devices, swap_first(): return lax.ppermute(value, 'pts', pairs)  5.21 us
    ppermute x4, starting transfers between devices, swap_first(): return lax.ppermute(value, 'pts', pairs)  4.63 us
    pallas_call x1, Pallas kernels, fetch(): pl.pallas_call(fetch_body, out_shape=pltpu.VMEM(points.shape, points.dtyp...  3.48 us
  transfers between devices with their start and end apart: 34, of which 12 were waited for; matrix products, arithmetic and copies ran while one was open for 2% of the time, Pallas kernels for 24%

profile of v17, /device:TPU:0, one launch (start us, length us, event | category | flops | bytes accessed | tf_op | source)
XLA Modules:
  0.0 111.3 jit_solution(7216882339157173541)
XLA Ops:
  0.6 0.1 pad_add_fusion.info
  0.7 12.4 %energies_and_sums_00.1 = (f32[4,264,256]{2,1,0:T(8,128)S(1)}, f32[2,4096]{1,0:T(2,128)S(1)}, f32[1,4096]{1,0:T(1,128)S(1)}, bf16[4096,1024]{1,0:T(8,128)(2,1)S(1)}) custom-call(s32[4]{0:T(128)S(1)} %pad_add_fusion.info, bf16[4096,1024]{1,0:T(8,128)(2,1)} %points.3, s32[2,4096]{1,0:T(2,128)} %assign.7, f32[512,1024]{1,0:T(8,128)} %fine.3), custom_call_target="tpu_custom_call" | custom-call | flops 4294967296 | bytes 8388608 | tf_op jit(solution)/shard_map/energies_and_sums_00/pallas_call | solution.py:348
  13.1 0.6 collective-permute-start
  13.8 7.8 %energies_and_sums_01.1 = (f32[4,264,256]{2,1,0:T(8,128)S(1)}, f32[2,4096]{1,0:T(2,128)S(1)}) custom-call(s32[4]{0:T(128)S(1)} %pad_add_fusion.info, bf16[4096,1024]{1,0:T(8,128)(2,1)S(1)} %get-tuple-element.48.points, s32[2,4096]{1,0:T(2,128)S(1)} %copy-done.3, f32[512,1024]{1,0:T(8,128)S(1)} %copy-done.2, f32[1,4096]{1,0:T(1,128)S(1)} %get-tuple-element.49.refs_0_, ...), custom_call_target="tpu_custom_call" | custom-call | flops 4294967296 | bytes 8388608 | tf_op jit(solution)/shard_map/energies_and_sums_01/pallas_call | solution.py:348
  21.7 0.0 copy-start
  21.7 0.0 copy-start.1
  21.7 2.5 %collective-permute-start.1 = (f32[2,136,256]{2,1,0:T(8,128)S(1)}, f32[2,136,256]{2,1,0:T(8,128)S(1)}, u32[]{:S(2)}, u32[]{:S(2)}) collective-permute-start(f32[2,136,256]{2,1,0:T(8,128)S(1)} %slice_add_fusion.1), channel_id=1, source_target_pairs={{0,8},{4,20},{8,0},{12,28},{16,24},{20,4},{24,16},{28,12},{1,9},{5... | collective-permute-start | bytes 835592 | tf_op jit(solution)/shard_map/ppermute | solution.py:94
  24.2 0.1 collective-permute-start.2
  24.3 4.4 %collective-permute-done.1.refs_0_ = f32[2,136,256]{2,1,0:T(8,128)S(1)} collective-permute-done((f32[2,136,256]{2,1,0:T(8,128)S(1)}, f32[2,136,256]{2,1,0:T(8,128)S(1)}, u32[]{:S(2)}, u32[]{:S(2)}) %collective-permute-start.1) | collective-permute-done | bytes 278560 | tf_op jit(solution)/shard_map/ppermute | solution.py:94
  28.8 2.1 %collective-permute-start.3 = (f32[136,256]{1,0:T(8,128)S(1)}, f32[136,256]{1,0:T(8,128)S(1)}, u32[]{:S(2)}, u32[]{:S(2)}) collective-permute-start(f32[136,256]{1,0:T(8,128)S(1)} %fusion.1), channel_id=1, source_target_pairs={{0,16},{4,12},{8,24},{12,4},{16,0},{20,28},{24,8},{28,20},{1,17},{... | collective-permute-start | bytes 417800 | tf_op jit(solution)/shard_map/ppermute | solution.py:99
  30.9 0.8 collective-permute-done.2.refs_1_
  31.7 2.4 %collective-permute-start.4 = (f32[128,256]{1,0:T(8,128)S(1)}, f32[128,256]{1,0:T(8,128)S(1)}, u32[]{:S(2)}, u32[]{:S(2)}) collective-permute-start(f32[128,256]{1,0:T(8,128)S(1)} %fusion.4), channel_id=1, source_target_pairs={{0,16},{4,12},{8,24},{12,4},{16,0},{20,28},{24,8},{28,20},{1,17},{... | collective-permute-start | bytes 393224 | tf_op jit(solution)/shard_map/ppermute | solution.py:99
  34.1 2.9 %collective-permute-done.4.refs_3_ = f32[128,256]{1,0:T(8,128)S(1)} collective-permute-done((f32[128,256]{1,0:T(8,128)S(1)}, f32[128,256]{1,0:T(8,128)S(1)}, u32[]{:S(2)}, u32[]{:S(2)}) %collective-permute-start.4) | collective-permute-done | bytes 131104 | tf_op jit(solution)/shard_map/ppermute | solution.py:99
  37.1 0.0 collective-permute-done.3.refs_2_
  37.1 1.1 refine_half.2
  38.2 2.1 %collective-permute-start.6 = (f32[128,256]{1,0:T(8,128)S(1)}, f32[128,256]{1,0:T(8,128)S(1)}, u32[]{:S(2)}, u32[]{:S(2)}) collective-permute-start(f32[128,256]{1,0:T(8,128)S(1)} %get-tuple-element.64), channel_id=1, source_target_pairs={{0,16},{4,20},{8,24},{12,28},{16,0},{20,4},{24,8},{28,12},{1,17},{... | collective-permute-start | bytes 393224 | tf_op jit(solution)/shard_map/ppermute | solution.py:89
  40.3 1.5 %collective-permute-start.5 = (f32[128,256]{1,0:T(8,128)S(1)}, f32[128,256]{1,0:T(8,128)S(1)}, u32[]{:S(2)}, u32[]{:S(2)}) collective-permute-start(f32[128,256]{1,0:T(8,128)S(1)} %get-tuple-element.65), channel_id=1, source_target_pairs={{0,8},{4,12},{8,0},{12,4},{16,24},{20,28},{24,16},{28,20},{1,9},{5... | collective-permute-start | bytes 393224 | tf_op jit(solution)/shard_map/ppermute | solution.py:89
  41.8 0.5 collective-permute-start.9
  42.3 0.1 collective-permute-start.10
  42.4 2.0 %collective-permute-done.6.refs_1_ = f32[128,256]{1,0:T(8,128)S(1)} collective-permute-done((f32[128,256]{1,0:T(8,128)S(1)}, f32[128,256]{1,0:T(8,128)S(1)}, u32[]{:S(2)}, u32[]{:S(2)}) %collective-permute-start.6) | collective-permute-done | bytes 131104 | tf_op jit(solution)/shard_map/ppermute | solution.py:89
  44.4 2.3 %collective-permute-start.7 = (f32[128,256]{1,0:T(8,128)S(1)}, f32[128,256]{1,0:T(8,128)S(1)}, u32[]{:S(2)}, u32[]{:S(2)}) collective-permute-start(f32[128,256]{1,0:T(8,128)S(1)} %collective-permute-done.6.refs_1_), channel_id=1, source_target_pairs={{0,8},{4,12},{8,0},{12,4},{16,24},{20,28},{24,16},{28,20},{1,9},{5... | collective-permute-start | bytes 393224 | tf_op jit(solution)/shard_map/ppermute | solution.py:89
  46.6 0.0 collective-permute-done.5.refs_0_
  46.6 0.7 collective-permute-start.8
  47.4 3.5 %fetch_points.1.points = bf16[4096,1024]{1,0:T(8,128)(2,1)S(1)} custom-call(bf16[4096,1024]{1,0:T(8,128)(2,1)} %points.3, f32[128,256]{1,0:T(8,128)S(1)} %collective-permute-done.5.refs_0_, f32[128,256]{1,0:T(8,128)S(1)} %collective-permute-done.6.refs_1_), custom_call_target="tpu_custom_call" | custom-call | bytes 16777216 | tf_op jit(solution)/shard_map/fetch_points/pallas_call | solution.py:287
  50.9 0.0 collective-permute-done.10
  50.9 0.0 collective-permute-done.7
  50.9 0.7 collective-permute-done.8
  51.7 0.1 collective-permute-start.11
  51.8 1.6 %collective-permute-start.12 = (f32[104,256]{1,0:T(8,128)S(1)}, f32[104,256]{1,0:T(8,128)S(1)}, u32[]{:S(2)}, u32[]{:S(2)}) collective-permute-start(f32[104,256]{1,0:T(8,128)S(1)} %pad_maximum_fusion.3), channel_id=1, source_target_pairs={{0,1},{1,0},{2,3},{3,2},{4,5},{5,4},{6,7},{7,6},{8,9},{9,8},{10,11... | collective-permute-start | bytes 319496 | tf_op jit(solution)/shard_map/ppermute | solution.py:89
  53.5 7.7 %energies_and_sums_10.1 = (f32[4,264,256]{2,1,0:T(8,128)S(1)}, f32[2,4096]{1,0:T(2,128)S(1)}) custom-call(s32[4]{0:T(128)S(1)} %pad_add_fusion.info, bf16[4096,1024]{1,0:T(8,128)(2,1)S(1)} %fetch_points.1.points, s32[2,4096]{1,0:T(2,128)S(1)} %copy-done.3, f32[8,128,256]{2,1,0:T(8,128)S(1)} %bitcast_dynamic-update-slice_fusion.fine, ...), custom_call_target="tpu_custom_call" | custom-call | flops 4294967296 | bytes 8388608 | tf_op jit(solution)/shard_map/energies_and_sums_10/pallas_call | solution.py:348
  61.2 0.3 collective-permute-start.14
  61.5 0.4 collective-permute-start.13
  61.9 8.0 %energies_and_sums_11.1 = (f32[4,264,256]{2,1,0:T(8,128)S(1)}, f32[2,4096]{1,0:T(2,128)S(1)}) custom-call(s32[4]{0:T(128)S(1)} %pad_add_fusion.info, bf16[4096,1024]{1,0:T(8,128)(2,1)S(1)} %fetch_points.1.points, s32[2,4096]{1,0:T(2,128)S(1)} %copy-done.3, f32[8,128,256]{2,1,0:T(8,128)S(1)} %collective-permute-done.11.fine, ...), custom_call_target="tpu_custom_call" | custom-call | flops 4294967296 | bytes 8388608 | tf_op jit(solution)/shard_map/energies_and_sums_11/pallas_call | solution.py:348
  70.0 1.2 %collective-permute-start.15 = (f32[2,136,256]{2,1,0:T(8,128)S(1)}, f32[2,136,256]{2,1,0:T(8,128)S(1)}, u32[]{:S(2)}, u32[]{:S(2)}) collective-permute-start(f32[2,136,256]{2,1,0:T(8,128)S(1)} %slice_add_fusion), channel_id=1, source_target_pairs={{0,8},{4,20},{8,0},{12,28},{16,24},{20,4},{24,16},{28,12},{1,9},{5... | collective-permute-start | bytes 835592 | tf_op jit(solution)/shard_map/ppermute | solution.py:94
  71.2 0.9 collective-permute-start.16
  72.1 2.6 %collective-permute-start.17 = (f32[104,256]{1,0:T(8,128)S(1)}, f32[104,256]{1,0:T(8,128)S(1)}, u32[]{:S(2)}, u32[]{:S(2)}) collective-permute-start(f32[104,256]{1,0:T(8,128)S(1)} %pad_maximum_fusion.4.refs_5_), channel_id=1, source_target_pairs={{0,2},{1,3},{2,0},{3,1},{4,6},{5,7},{6,4},{7,5},{8,10},{9,11},{10,... | collective-permute-start | bytes 319496 | tf_op jit(solution)/shard_map/ppermute | solution.py:89
  74.7 5.0 %collective-permute-done.17.refs_6_ = f32[104,256]{1,0:T(8,128)S(1)} collective-permute-done((f32[104,256]{1,0:T(8,128)S(1)}, f32[104,256]{1,0:T(8,128)S(1)}, u32[]{:S(2)}, u32[]{:S(2)}) %collective-permute-start.17) | collective-permute-done | bytes 106528 | tf_op jit(solution)/shard_map/ppermute | solution.py:89
  79.7 0.8 collective-permute-start.18
  80.5 0.7 fusion.3
  81.2 1.3 %collective-permute-start.19 = (f32[128,256]{1,0:T(8,128)}, f32[128,256]{1,0:T(8,128)S(1)}, u32[]{:S(2)}, u32[]{:S(2)}) collective-permute-start(f32[128,256]{1,0:T(8,128)} %fusion.3), channel_id=1, source_target_pairs={{0,16},{4,12},{8,24},{12,4},{16,0},{20,28},{24,8},{28,20},{1,17},{... | collective-permute-start | bytes 393224 | tf_op jit(solution)/shard_map/ppermute | solution.py:99
  82.5 3.8 %collective-permute-done.19.refs_3_ = f32[128,256]{1,0:T(8,128)S(1)} collective-permute-done((f32[128,256]{1,0:T(8,128)}, f32[128,256]{1,0:T(8,128)S(1)}, u32[]{:S(2)}, u32[]{:S(2)}) %collective-permute-start.19) | collective-permute-done | bytes 131104 | tf_op jit(solution)/shard_map/ppermute | solution.py:99
  86.4 1.2 %refine_half.3 = (f32[128,256]{1,0:T(8,128)S(1)}, f32[128,256]{1,0:T(8,128)S(1)}, f32[72,256]{1,0:T(8,128)S(1)}) custom-call(s32[4]{0:T(128)S(1)} %pad_add_fusion.info, f32[4,264,256]{2,1,0:T(8,128)S(1)} %get-tuple-element.72.own, f32[4,264,256]{2,1,0:T(8,128)S(1)} %collective-permute-done.14.sibling, f32[2,136,256]{2,1,0:T(8,128)S(1)} %collective-permute-done.15.refs_0_, ...), custom_call_target="tpu_custom_call" | custom-call | tf_op jit(solution)/shard_map/refine_half/pallas_call | solution.py:412
  87.6 0.2 collective-permute-start.26
  87.9 1.1 collective-permute-start.20
  88.9 1.4 %collective-permute-start.21 = (f32[128,256]{1,0:T(8,128)S(1)}, f32[128,256]{1,0:T(8,128)S(1)}, u32[]{:S(2)}, u32[]{:S(2)}) collective-permute-start(f32[128,256]{1,0:T(8,128)S(1)} %get-tuple-element.88), channel_id=1, source_target_pairs={{0,16},{4,20},{8,24},{12,28},{16,0},{20,4},{24,8},{28,12},{1,17},{... | collective-permute-start | bytes 393224 | tf_op jit(solution)/shard_map/ppermute | solution.py:89
  90.3 2.1 %collective-permute-done.26 = f32[104,256]{1,0:T(8,128)S(1)} collective-permute-done((f32[104,256]{1,0:T(8,128)S(1)}, f32[104,256]{1,0:T(8,128)S(1)}, u32[]{:S(2)}, u32[]{:S(2)}) %collective-permute-start.26) | collective-permute-done | bytes 106528 | tf_op jit(solution)/shard_map/ppermute | solution.py:89
  92.4 2.7 %collective-permute-start.27 = (f32[104,256]{1,0:T(8,128)S(1)}, f32[104,256]{1,0:T(8,128)S(1)}, u32[]{:S(2)}, u32[]{:S(2)}) collective-permute-start(f32[104,256]{1,0:T(8,128)S(1)} %pad_maximum_fusion.6), channel_id=1, source_target_pairs={{0,2},{1,3},{2,0},{3,1},{4,6},{5,7},{6,4},{7,5},{8,10},{9,11},{10,... | collective-permute-start | bytes 319496 | tf_op jit(solution)/shard_map/ppermute | solution.py:89
  95.2 2.0 %collective-permute-start.23 = (f32[128,256]{1,0:T(8,128)S(1)}, f32[128,256]{1,0:T(8,128)S(1)}, u32[]{:S(2)}, u32[]{:S(2)}) collective-permute-start(f32[128,256]{1,0:T(8,128)S(1)} %collective-permute-done.20), channel_id=1, source_target_pairs={{0,16},{4,20},{8,24},{12,28},{16,0},{20,4},{24,8},{28,12},{1,17},{... | collective-permute-start | bytes 393224 | tf_op jit(solution)/shard_map/ppermute | solution.py:89
  97.2 1.1 %collective-permute-start.22 = (f32[128,256]{1,0:T(8,128)S(1)}, f32[128,256]{1,0:T(8,128)S(1)}, u32[]{:S(2)}, u32[]{:S(2)}) collective-permute-start(f32[128,256]{1,0:T(8,128)S(1)} %collective-permute-done.21), channel_id=1, source_target_pairs={{0,8},{4,12},{8,0},{12,4},{16,24},{20,28},{24,16},{28,20},{1,9},{5... | collective-permute-start | bytes 393224 | tf_op jit(solution)/shard_map/ppermute | solution.py:89
  98.4 0.1 collective-permute-start.25
  98.4 0.9 collective-permute-start.24
  99.4 2.6 %collective-permute-start.30 = (f32[72,256]{1,0:T(8,128)S(1)}, f32[72,256]{1,0:T(8,128)S(1)}, u32[]{:S(2)}, u32[]{:S(2)}) collective-permute-start(f32[72,256]{1,0:T(8,128)S(1)} %slice_add_fusion.11), channel_id=1, source_target_pairs={{0,24},{4,28},{8,16},{12,20},{16,8},{20,12},{24,0},{28,4},{1,25},{... | collective-permute-start | bytes 221192 | tf_op jit(solution)/shard_map/ppermute | solution.py:89
  102.0 1.0 collective-permute-start.29
  103.0 1.1 %collective-permute-start.28 = (f32[72,256]{1,0:T(8,128)S(1)}, f32[72,256]{1,0:T(8,128)S(1)}, u32[]{:S(2)}, u32[]{:S(2)}) collective-permute-start(f32[72,256]{1,0:T(8,128)S(1)} %slice_add_fusion.11), channel_id=1, source_target_pairs={{0,8},{4,12},{8,0},{12,4},{16,24},{20,28},{24,16},{28,20},{1,9},{5... | collective-permute-start | bytes 221192 | tf_op jit(solution)/shard_map/ppermute | solution.py:89
  104.2 0.1 collective-permute-start.31
  104.3 0.0 collective-permute-done.24
  104.3 0.5 collective-permute-start.32
  104.9 0.7 collective-permute-done.30
  105.6 0.8 collective-permute-done.29
  106.4 0.9 collective-permute-done.28
  107.4 0.1 collective-permute-start.33
  107.4 0.7 maximum_multiply_fusion
  108.1 0.9 collective-permute-done.33.refs_5_
  109.0 2.1 %place_blocks.1 = (f32[512,1024]{1,0:T(8,128)}, f32[64,1024]{1,0:T(8,128)}) custom-call(s32[4]{0:T(128)S(1)} %pad_add_fusion.info, f32[4,128,256]{2,1,0:T(8,128)S(1)} %pad_maximum_fusion.refs_0_, f32[4,128,256]{2,1,0:T(8,128)S(1)} %pad_maximum_fusion.1.refs_1_, f32[4,72,256]{2,1,0:T(8,128)S(1)} %pad_maximum_fusion.2.refs_2_, ...), custom_call_target="tpu_custom_call" | custom-call | tf_op jit(solution)/shard_map/place_blocks/pallas_call | solution.py:514
  (59 shorter events, 0.7 us)
Async XLA Ops:
  0.7 13.1 %copy-start.2 = (f32[512,1024]{1,0:T(8,128)S(1)}, f32[512,1024]{1,0:T(8,128)}, u32[]{:S(2)}) copy-start(f32[512,1024]{1,0:T(8,128)} %fine.3) | copy-start | bytes 6291460
  0.7 13.1 %copy-start.3 = (s32[2,4096]{1,0:T(2,128)S(1)}, s32[2,4096]{1,0:T(2,128)}, u32[]{:S(2)}) copy-start(s32[2,4096]{1,0:T(2,128)} %assign.7) | copy-start | bytes 98308
  13.1 8.5 %collective-permute-start = (f32[4,264,256]{2,1,0:T(8,128)S(1)}, f32[4,264,256]{2,1,0:T(8,128)S(1)}, u32[]{:S(2)}, u32[]{:S(2)}) collective-permute-start(f32[4,264,256]{2,1,0:T(8,128)S(1)} %get-tuple-element.52), channel_id=1, source_target_pairs={{0,4},{4,0},{8,12},{12,8},{16,20},{20,16},{24,28},{28,24},{1,5},{5... | collective-permute-start | bytes 3244040 | tf_op jit(solution)/shard_map/ppermute | solution.py:89
  21.7 15.4 %copy-start = (f32[64,1024]{1,0:T(8,128)S(1)}, f32[64,1024]{1,0:T(8,128)}, u32[]{:S(2)}) copy-start(f32[64,1024]{1,0:T(8,128)} %refs_5_.1) | copy-start | bytes 786436
  21.7 15.4 %copy-start.1 = (s32[512]{0:T(512)S(1)}, s32[512]{0:T(512)}, u32[]{:S(2)}) copy-start(s32[512]{0:T(512)} %param.9) | copy-start | bytes 6148
  21.7 7.0 %collective-permute-start.1 = (f32[2,136,256]{2,1,0:T(8,128)S(1)}, f32[2,136,256]{2,1,0:T(8,128)S(1)}, u32[]{:S(2)}, u32[]{:S(2)}) collective-permute-start(f32[2,136,256]{2,1,0:T(8,128)S(1)} %slice_add_fusion.1), channel_id=1, source_target_pairs={{0,8},{4,20},{8,0},{12,28},{16,24},{20,4},{24,16},{28,12},{1,9},{5... | collective-permute-start | bytes 835592 | tf_op jit(solution)/shard_map/ppermute | solution.py:94
  24.2 7.4 %collective-permute-start.2 = (f32[2,128,256]{2,1,0:T(8,128)S(1)}, f32[2,128,256]{2,1,0:T(8,128)S(1)}, u32[]{:S(2)}, u32[]{:S(2)}) collective-permute-start(f32[2,128,256]{2,1,0:T(8,128)S(1)} %slice_add_fusion.3), channel_id=1, source_target_pairs={{0,8},{4,20},{8,0},{12,28},{16,24},{20,4},{24,16},{28,12},{1,9},{5... | collective-permute-start | bytes 786440 | tf_op jit(solution)/shard_map/ppermute | solution.py:94
  28.8 8.3 %collective-permute-start.3 = (f32[136,256]{1,0:T(8,128)S(1)}, f32[136,256]{1,0:T(8,128)S(1)}, u32[]{:S(2)}, u32[]{:S(2)}) collective-permute-start(f32[136,256]{1,0:T(8,128)S(1)} %fusion.1), channel_id=1, source_target_pairs={{0,16},{4,12},{8,24},{12,4},{16,0},{20,28},{24,8},{28,20},{1,17},{... | collective-permute-start | bytes 417800 | tf_op jit(solution)/shard_map/ppermute | solution.py:99
  31.7 5.4 %collective-permute-start.4 = (f32[128,256]{1,0:T(8,128)S(1)}, f32[128,256]{1,0:T(8,128)S(1)}, u32[]{:S(2)}, u32[]{:S(2)}) collective-permute-start(f32[128,256]{1,0:T(8,128)S(1)} %fusion.4), channel_id=1, source_target_pairs={{0,16},{4,12},{8,24},{12,4},{16,0},{20,28},{24,8},{28,20},{1,17},{... | collective-permute-start | bytes 393224 | tf_op jit(solution)/shard_map/ppermute | solution.py:99
  38.2 6.1 %collective-permute-start.6 = (f32[128,256]{1,0:T(8,128)S(1)}, f32[128,256]{1,0:T(8,128)S(1)}, u32[]{:S(2)}, u32[]{:S(2)}) collective-permute-start(f32[128,256]{1,0:T(8,128)S(1)} %get-tuple-element.64), channel_id=1, source_target_pairs={{0,16},{4,20},{8,24},{12,28},{16,0},{20,4},{24,8},{28,12},{1,17},{... | collective-permute-start | bytes 393224 | tf_op jit(solution)/shard_map/ppermute | solution.py:89
  40.3 6.3 %collective-permute-start.5 = (f32[128,256]{1,0:T(8,128)S(1)}, f32[128,256]{1,0:T(8,128)S(1)}, u32[]{:S(2)}, u32[]{:S(2)}) collective-permute-start(f32[128,256]{1,0:T(8,128)S(1)} %get-tuple-element.65), channel_id=1, source_target_pairs={{0,8},{4,12},{8,0},{12,4},{16,24},{20,28},{24,16},{28,20},{1,9},{5... | collective-permute-start | bytes 393224 | tf_op jit(solution)/shard_map/ppermute | solution.py:89
  41.8 9.1 %collective-permute-start.9 = (f32[128,256]{1,0:T(8,128)S(1)}, f32[128,256]{1,0:T(8,128)S(1)}, u32[]{:S(2)}, u32[]{:S(2)}) collective-permute-start(f32[128,256]{1,0:T(8,128)S(1)} %get-tuple-element.64), channel_id=1, source_target_pairs={{0,8},{4,12},{8,0},{12,4},{16,24},{20,28},{24,16},{28,20},{1,9},{5... | collective-permute-start | bytes 393224 | tf_op jit(solution)/shard_map/ppermute | solution.py:89
  42.3 8.5 %collective-permute-start.10 = (f32[128,256]{1,0:T(8,128)S(1)}, f32[128,256]{1,0:T(8,128)S(1)}, u32[]{:S(2)}, u32[]{:S(2)}) collective-permute-start(f32[128,256]{1,0:T(8,128)S(1)} %get-tuple-element.65), channel_id=1, source_target_pairs={{0,16},{4,20},{8,24},{12,28},{16,0},{20,4},{24,8},{28,12},{1,17},{... | collective-permute-start | bytes 393224 | tf_op jit(solution)/shard_map/ppermute | solution.py:89
  44.4 6.5 %collective-permute-start.7 = (f32[128,256]{1,0:T(8,128)S(1)}, f32[128,256]{1,0:T(8,128)S(1)}, u32[]{:S(2)}, u32[]{:S(2)}) collective-permute-start(f32[128,256]{1,0:T(8,128)S(1)} %collective-permute-done.6.refs_1_), channel_id=1, source_target_pairs={{0,8},{4,12},{8,0},{12,4},{16,24},{20,28},{24,16},{28,20},{1,9},{5... | collective-permute-start | bytes 393224 | tf_op jit(solution)/shard_map/ppermute | solution.py:89
  46.6 5.0 %collective-permute-start.8 = (f32[128,256]{1,0:T(8,128)S(1)}, f32[128,256]{1,0:T(8,128)S(1)}, u32[]{:S(2)}, u32[]{:S(2)}) collective-permute-start(f32[128,256]{1,0:T(8,128)S(1)} %collective-permute-done.5.refs_0_), channel_id=1, source_target_pairs={{0,16},{4,20},{8,24},{12,28},{16,0},{20,4},{24,8},{28,12},{1,17},{... | collective-permute-start | bytes 393224 | tf_op jit(solution)/shard_map/ppermute | solution.py:89
  51.7 10.1 %collective-permute-start.11 = (f32[8,128,256]{2,1,0:T(8,128)S(1)}, f32[8,128,256]{2,1,0:T(8,128)S(1)}, u32[]{:S(2)}, u32[]{:S(2)}) collective-permute-start(f32[8,128,256]{2,1,0:T(8,128)S(1)} %bitcast_dynamic-update-slice_fusion.fine), channel_id=1, source_target_pairs={{0,4},{4,0},{8,12},{12,8},{16,20},{20,16},{24,28},{28,24},{1,5},{5... | collective-permute-start | bytes 3145736 | tf_op jit(solution)/shard_map/ppermute | solution.py:89
  51.8 9.4 %collective-permute-start.12 = (f32[104,256]{1,0:T(8,128)S(1)}, f32[104,256]{1,0:T(8,128)S(1)}, u32[]{:S(2)}, u32[]{:S(2)}) collective-permute-start(f32[104,256]{1,0:T(8,128)S(1)} %pad_maximum_fusion.3), channel_id=1, source_target_pairs={{0,1},{1,0},{2,3},{3,2},{4,5},{5,4},{6,7},{7,6},{8,9},{9,8},{10,11... | collective-permute-start | bytes 319496 | tf_op jit(solution)/shard_map/ppermute | solution.py:89
  61.2 8.7 %collective-permute-start.14 = (f32[4,264,256]{2,1,0:T(8,128)S(1)}, f32[4,264,256]{2,1,0:T(8,128)S(1)}, u32[]{:S(2)}, u32[]{:S(2)}) collective-permute-start(f32[4,264,256]{2,1,0:T(8,128)S(1)} %get-tuple-element.73), channel_id=1, source_target_pairs={{0,4},{4,0},{8,12},{12,8},{16,20},{20,16},{24,28},{28,24},{1,5},{5... | collective-permute-start | bytes 3244040 | tf_op jit(solution)/shard_map/ppermute | solution.py:89
  61.5 8.3 %collective-permute-start.13 = (f32[72,256]{1,0:T(8,128)S(1)}, f32[72,256]{1,0:T(8,128)S(1)}, u32[]{:S(2)}, u32[]{:S(2)}) collective-permute-start(f32[72,256]{1,0:T(8,128)S(1)} %slice_add_fusion.13), channel_id=1, source_target_pairs={{0,4},{4,0},{8,12},{12,8},{16,20},{20,16},{24,28},{28,24},{1,5},{5... | collective-permute-start | bytes 221192 | tf_op jit(solution)/shard_map/ppermute | solution.py:89
  70.0 9.7 %collective-permute-start.15 = (f32[2,136,256]{2,1,0:T(8,128)S(1)}, f32[2,136,256]{2,1,0:T(8,128)S(1)}, u32[]{:S(2)}, u32[]{:S(2)}) collective-permute-start(f32[2,136,256]{2,1,0:T(8,128)S(1)} %slice_add_fusion), channel_id=1, source_target_pairs={{0,8},{4,20},{8,0},{12,28},{16,24},{20,4},{24,16},{28,12},{1,9},{5... | collective-permute-start | bytes 835592 | tf_op jit(solution)/shard_map/ppermute | solution.py:94
  71.2 8.5 %collective-permute-start.16 = (f32[2,128,256]{2,1,0:T(8,128)S(1)}, f32[2,128,256]{2,1,0:T(8,128)S(1)}, u32[]{:S(2)}, u32[]{:S(2)}) collective-permute-start(f32[2,128,256]{2,1,0:T(8,128)S(1)} %slice_add_fusion.2), channel_id=1, source_target_pairs={{0,8},{4,20},{8,0},{12,28},{16,24},{20,4},{24,16},{28,12},{1,9},{5... | collective-permute-start | bytes 786440 | tf_op jit(solution)/shard_map/ppermute | solution.py:94
  72.1 7.6 %collective-permute-start.17 = (f32[104,256]{1,0:T(8,128)S(1)}, f32[104,256]{1,0:T(8,128)S(1)}, u32[]{:S(2)}, u32[]{:S(2)}) collective-permute-start(f32[104,256]{1,0:T(8,128)S(1)} %pad_maximum_fusion.4.refs_5_), channel_id=1, source_target_pairs={{0,2},{1,3},{2,0},{3,1},{4,6},{5,7},{6,4},{7,5},{8,10},{9,11},{10,... | collective-permute-start | bytes 319496 | tf_op jit(solution)/shard_map/ppermute | solution.py:89
  79.7 6.7 %collective-permute-start.18 = (f32[136,256]{1,0:T(8,128)S(1)}, f32[136,256]{1,0:T(8,128)S(1)}, u32[]{:S(2)}, u32[]{:S(2)}) collective-permute-start(f32[136,256]{1,0:T(8,128)S(1)} %fusion), channel_id=1, source_target_pairs={{0,16},{4,12},{8,24},{12,4},{16,0},{20,28},{24,8},{28,20},{1,17},{... | collective-permute-start | bytes 417800 | tf_op jit(solution)/shard_map/ppermute | solution.py:99
  81.2 5.2 %collective-permute-start.19 = (f32[128,256]{1,0:T(8,128)}, f32[128,256]{1,0:T(8,128)S(1)}, u32[]{:S(2)}, u32[]{:S(2)}) collective-permute-start(f32[128,256]{1,0:T(8,128)} %fusion.3), channel_id=1, source_target_pairs={{0,16},{4,12},{8,24},{12,4},{16,0},{20,28},{24,8},{28,20},{1,17},{... | collective-permute-start | bytes 393224 | tf_op jit(solution)/shard_map/ppermute | solution.py:99
  87.6 4.8 %collective-permute-start.26 = (f32[104,256]{1,0:T(8,128)S(1)}, f32[104,256]{1,0:T(8,128)S(1)}, u32[]{:S(2)}, u32[]{:S(2)}) collective-permute-start(f32[104,256]{1,0:T(8,128)S(1)} %pad_maximum_fusion.5), channel_id=1, source_target_pairs={{0,1},{1,0},{2,3},{3,2},{4,5},{5,4},{6,7},{7,6},{8,9},{9,8},{10,11... | collective-permute-start | bytes 319496 | tf_op jit(solution)/shard_map/ppermute | solution.py:89
  87.9 7.3 %collective-permute-start.20 = (f32[128,256]{1,0:T(8,128)S(1)}, f32[128,256]{1,0:T(8,128)S(1)}, u32[]{:S(2)}, u32[]{:S(2)}) collective-permute-start(f32[128,256]{1,0:T(8,128)S(1)} %get-tuple-element.89), channel_id=1, source_target_pairs={{0,8},{4,12},{8,0},{12,4},{16,24},{20,28},{24,16},{28,20},{1,9},{5... | collective-permute-start | bytes 393224 | tf_op jit(solution)/shard_map/ppermute | solution.py:89
  88.9 6.3 %collective-permute-start.21 = (f32[128,256]{1,0:T(8,128)S(1)}, f32[128,256]{1,0:T(8,128)S(1)}, u32[]{:S(2)}, u32[]{:S(2)}) collective-permute-start(f32[128,256]{1,0:T(8,128)S(1)} %get-tuple-element.88), channel_id=1, source_target_pairs={{0,16},{4,20},{8,24},{12,28},{16,0},{20,4},{24,8},{28,12},{1,17},{... | collective-permute-start | bytes 393224 | tf_op jit(solution)/shard_map/ppermute | solution.py:89
  92.4 6.9 %collective-permute-start.27 = (f32[104,256]{1,0:T(8,128)S(1)}, f32[104,256]{1,0:T(8,128)S(1)}, u32[]{:S(2)}, u32[]{:S(2)}) collective-permute-start(f32[104,256]{1,0:T(8,128)S(1)} %pad_maximum_fusion.6), channel_id=1, source_target_pairs={{0,2},{1,3},{2,0},{3,1},{4,6},{5,7},{6,4},{7,5},{8,10},{9,11},{10,... | collective-permute-start | bytes 319496 | tf_op jit(solution)/shard_map/ppermute | solution.py:89
  95.2 6.7 %collective-permute-start.23 = (f32[128,256]{1,0:T(8,128)S(1)}, f32[128,256]{1,0:T(8,128)S(1)}, u32[]{:S(2)}, u32[]{:S(2)}) collective-permute-start(f32[128,256]{1,0:T(8,128)S(1)} %collective-permute-done.20), channel_id=1, source_target_pairs={{0,16},{4,20},{8,24},{12,28},{16,0},{20,4},{24,8},{28,12},{1,17},{... | collective-permute-start | bytes 393224 | tf_op jit(solution)/shard_map/ppermute | solution.py:89
  97.2 5.8 %collective-permute-start.22 = (f32[128,256]{1,0:T(8,128)S(1)}, f32[128,256]{1,0:T(8,128)S(1)}, u32[]{:S(2)}, u32[]{:S(2)}) collective-permute-start(f32[128,256]{1,0:T(8,128)S(1)} %collective-permute-done.21), channel_id=1, source_target_pairs={{0,8},{4,12},{8,0},{12,4},{16,24},{20,28},{24,16},{28,20},{1,9},{5... | collective-permute-start | bytes 393224 | tf_op jit(solution)/shard_map/ppermute | solution.py:89
  98.4 5.8 %collective-permute-start.25 = (f32[128,256]{1,0:T(8,128)S(1)}, f32[128,256]{1,0:T(8,128)S(1)}, u32[]{:S(2)}, u32[]{:S(2)}) collective-permute-start(f32[128,256]{1,0:T(8,128)S(1)} %get-tuple-element.89), channel_id=1, source_target_pairs={{0,16},{4,20},{8,24},{12,28},{16,0},{20,4},{24,8},{28,12},{1,17},{... | collective-permute-start | bytes 393224 | tf_op jit(solution)/shard_map/ppermute | solution.py:89
  98.4 5.8 %collective-permute-start.24 = (f32[128,256]{1,0:T(8,128)S(1)}, f32[128,256]{1,0:T(8,128)S(1)}, u32[]{:S(2)}, u32[]{:S(2)}) collective-permute-start(f32[128,256]{1,0:T(8,128)S(1)} %get-tuple-element.88), channel_id=1, source_target_pairs={{0,8},{4,12},{8,0},{12,4},{16,24},{20,28},{24,16},{28,20},{1,9},{5... | collective-permute-start | bytes 393224 | tf_op jit(solution)/shard_map/ppermute | solution.py:89
  99.4 6.2 %collective-permute-start.30 = (f32[72,256]{1,0:T(8,128)S(1)}, f32[72,256]{1,0:T(8,128)S(1)}, u32[]{:S(2)}, u32[]{:S(2)}) collective-permute-start(f32[72,256]{1,0:T(8,128)S(1)} %slice_add_fusion.11), channel_id=1, source_target_pairs={{0,24},{4,28},{8,16},{12,20},{16,8},{20,12},{24,0},{28,4},{1,25},{... | collective-permute-start | bytes 221192 | tf_op jit(solution)/shard_map/ppermute | solution.py:89
  102.0 4.4 %collective-permute-start.29 = (f32[72,256]{1,0:T(8,128)S(1)}, f32[72,256]{1,0:T(8,128)S(1)}, u32[]{:S(2)}, u32[]{:S(2)}) collective-permute-start(f32[72,256]{1,0:T(8,128)S(1)} %slice_add_fusion.11), channel_id=1, source_target_pairs={{0,16},{4,20},{8,24},{12,28},{16,0},{20,4},{24,8},{28,12},{1,17},{... | collective-permute-start | bytes 221192 | tf_op jit(solution)/shard_map/ppermute | solution.py:89
  103.0 4.4 %collective-permute-start.28 = (f32[72,256]{1,0:T(8,128)S(1)}, f32[72,256]{1,0:T(8,128)S(1)}, u32[]{:S(2)}, u32[]{:S(2)}) collective-permute-start(f32[72,256]{1,0:T(8,128)S(1)} %slice_add_fusion.11), channel_id=1, source_target_pairs={{0,8},{4,12},{8,0},{12,4},{16,24},{20,28},{24,16},{28,20},{1,9},{5... | collective-permute-start | bytes 221192 | tf_op jit(solution)/shard_map/ppermute | solution.py:89
  104.2 4.8 %collective-permute-start.31 = (f32[4,128,256]{2,1,0:T(8,128)S(1)}, f32[4,128,256]{2,1,0:T(8,128)S(1)}, u32[]{:S(2)}, u32[]{:S(2)}) collective-permute-start(f32[4,128,256]{2,1,0:T(8,128)S(1)} %pad_maximum_fusion.refs_0_), channel_id=1, source_target_pairs={{0,4},{4,0},{8,12},{12,8},{16,20},{20,16},{24,28},{28,24},{1,5},{5... | collective-permute-start | bytes 1572872 | tf_op jit(solution)/shard_map/ppermute | solution.py:89
  104.3 4.7 %collective-permute-start.32 = (f32[4,128,256]{2,1,0:T(8,128)S(1)}, f32[4,128,256]{2,1,0:T(8,128)S(1)}, u32[]{:S(2)}, u32[]{:S(2)}) collective-permute-start(f32[4,128,256]{2,1,0:T(8,128)S(1)} %pad_maximum_fusion.1.refs_1_), channel_id=1, source_target_pairs={{0,4},{4,0},{8,12},{12,8},{16,20},{20,16},{24,28},{28,24},{1,5},{5... | collective-permute-start | bytes 1572872 | tf_op jit(solution)/shard_map/ppermute | solution.py:89
  107.4 1.6 %collective-permute-start.33 = (f32[4,72,256]{2,1,0:T(8,128)S(1)}, f32[4,72,256]{2,1,0:T(8,128)S(1)}, u32[]{:S(2)}, u32[]{:S(2)}) collective-permute-start(f32[4,72,256]{2,1,0:T(8,128)S(1)} %pad_maximum_fusion.2.refs_2_), channel_id=1, source_target_pairs={{0,4},{4,0},{8,12},{12,8},{16,20},{20,16},{24,28},{28,24},{1,5},{5... | collective-permute-start | bytes 884744 | tf_op jit(solution)/shard_map/ppermute | solution.py:89

commit v18 on v17

--- a/solution.py
+++ b/solution.py
@@ -159,9 +159,14 @@
         load_start.start()
     if stream:
         load(0, 0).start()
-        load(0, 1).start()
         load_assign = pltpu.make_async_copy(assign, chosen_in, small_sems.at[0])
         load_assign.start()
+        load(0, 1).start()
+
+        @pl.loop(1, tiles)
+        def _(i):
+            load(i, 0).start()
+            load(i, 1).start()
 
     if initial:
         if first:
@@ -226,36 +231,27 @@
             preferred_element_type=jnp.float32,
         )
 
-    def arrive(i, more):
+    def arrive(i):
         for half in range(2):
             if stream:
                 load(i, half).wait()
-                if more:
-                    load(i + 1, half).start()
 
     if stream:
         load_assign.wait()
-        for half in range(2):
-            load(0, half).wait()
-            load(1, half).start()
-            part = slice(half * (tile // 2), (half + 1) * (tile // 2))
-            even[:, part] = lax.dot_general(
-                low[...], kept[part, :], (((1,), (1,)), ((), ())), preferred_element_type=jnp.float32
-            )
-    else:
-        multiply(0, even)
+    arrive(0)
+    multiply(0, even)
 
     @pl.loop(0, tiles // 2 - 1)
     def _(pair):
         i = 2 * pair
-        arrive(i + 1, True)
+        arrive(i + 1)
         multiply(i + 1, odd)
         collect(i, even)
-        arrive(i + 2, True)
+        arrive(i + 2)
         multiply(i + 2, even)
         collect(i + 1, odd)
 
-    arrive(tiles - 1, False)
+    arrive(tiles - 1)
     multiply(tiles - 1, odd)
     collect(tiles - 2, even)
     collect(tiles - 1, odd)
@@ -304,7 +300,7 @@
     initial = pass_index == 0
     chained = seen is not None
     stream = squares is None
-    tile = 1024 if stream or count % 4096 else 2048
+    tile = 1024
     if stream:
         in_specs = [AWAY] * 3
         args = [far_off(points), far_off(fine_assign), far_off(fine)]
@@ -351,7 +347,7 @@
         in_specs=[SCALARS, *in_specs],
         out_specs=[HERE] * len(out_shape),
         scratch_shapes=scratch,
-        compiler_params=pltpu.CompilerParams(vmem_limit_bytes=24 * 2**20),
+        compiler_params=pltpu.CompilerParams(vmem_limit_bytes=20 * 2**20),
         cost_estimate=pl.CostEstimate(
             flops=4 * rows * count * width, bytes_accessed=2 * count * width, transcendentals=0
         ),
@@ -548,11 +544,12 @@
         info, held, sibling, incoming, owners, [coarse_start], flip=0
     )
     own = gather_half(top, low)
-    own, kept = lax.optimization_barrier((own, fetch(points, own[:2])))
-    own = jnp.stack(own)
     bits = range(lax.axis_size("cen").bit_length() - 1)
     folded = jnp.concatenate([part, seen_first.reshape(-1, block_width)], 0)
     paired = swap(folded, 1, "cen")
+    kept = fetch(points, own[:2])
+    own, kept, paired = lax.optimization_barrier((own, kept, paired))
+    own = jnp.stack(own)
     other = swap(own, CORE)
 
     call = functools.partial(run_pass, info, pass_index=1, rows=rows)

time: 111 us -> 112 us (level)
  waiting for transfers between devices: 25.2 us -> 28.1 us
  Pallas kernels: 43.8 us -> 42.4 us
  starting transfers between devices: 39 us -> 37.6 us
    ppermute x26, waiting for transfers between devices: 13.2 us -> 15.9 us  [swap(): return lax.ppermute(value, axis, [(i, i ^ bit) for i in range(size)])]
    pallas_call x4, Pallas kernels: 35.9 us -> 34.5 us  [run_pass(): pl.pallas_call(body, out_shape=out_shape, in_specs=[SCALARS, *in_specs],...]
    ppermute x26, starting transfers between devices: 27.7 us -> 26.4 us  [swap(): return lax.ppermute(value, axis, [(i, i ^ bit) for i in range(size)])]
  transfers between devices with their start and end apart: 34 -> 34, of which waited for: 12 -> 13; matrix products, arithmetic and copies ran while one was open for 2% -> 2% of each run, Pallas kernels for 24% -> 24%
where the time goes in v18:
time: 112 us; the launch traced here: 111 us
  Pallas kernels  42.4 us (38%)
  starting transfers between devices  37.6 us (34%)
  waiting for transfers between devices  28.1 us (25%)
  other arithmetic  1.86 us (2%)
  between operations  1.24 us (1%)
    pallas_call x4, Pallas kernels, run_pass(): pl.pallas_call(body, out_shape=out_shape, in_specs=[SCALARS, *in_specs],...  34.5 us
    ppermute x26, starting transfers between devices, swap(): return lax.ppermute(value, axis, [(i, i ^ bit) for i in range(size)])  26.4 us
    ppermute x26, waiting for transfers between devices, swap(): return lax.ppermute(value, axis, [(i, i ^ bit) for i in range(size)])  15.9 us
    ppermute x4, waiting for transfers between devices, swap_second(): return lax.ppermute(value, 'pts', pairs)  6.99 us
    ppermute x4, starting transfers between devices, swap_second(): return lax.ppermute(value, 'pts', pairs)  6.61 us
    ppermute x4, waiting for transfers between devices, swap_first(): return lax.ppermute(value, 'pts', pairs)  5.27 us
    ppermute x4, starting transfers between devices, swap_first(): return lax.ppermute(value, 'pts', pairs)  4.56 us
    pallas_call x1, Pallas kernels, fetch(): pl.pallas_call(fetch_body, out_shape=pltpu.VMEM(points.shape, points.dtyp...  3.47 us
  transfers between devices with their start and end apart: 34, of which 13 were waited for; matrix products, arithmetic and copies ran while one was open for 2% of the time, Pallas kernels for 24%

profile of v18, /device:TPU:0, one launch (start us, length us, event | category | flops | bytes accessed | tf_op | source)
XLA Modules:
  0.0 111.4 jit_solution(13383819323406879337)
XLA Ops:
  0.6 0.1 pad_add_fusion.info
  0.7 11.5 %energies_and_sums_00.1 = (f32[4,264,256]{2,1,0:T(8,128)S(1)}, f32[2,4096]{1,0:T(2,128)S(1)}, f32[1,4096]{1,0:T(1,128)S(1)}, bf16[4096,1024]{1,0:T(8,128)(2,1)S(1)}) custom-call(s32[4]{0:T(128)S(1)} %pad_add_fusion.info, bf16[4096,1024]{1,0:T(8,128)(2,1)} %points.3, s32[2,4096]{1,0:T(2,128)} %assign.7, f32[512,1024]{1,0:T(8,128)} %fine.3), custom_call_target="tpu_custom_call" | custom-call | flops 4294967296 | bytes 8388608 | tf_op jit(solution)/shard_map/energies_and_sums_00/pallas_call | solution.py:344
  12.2 0.8 collective-permute-start
  13.0 7.6 %energies_and_sums_01.1 = (f32[4,264,256]{2,1,0:T(8,128)S(1)}, f32[2,4096]{1,0:T(2,128)S(1)}) custom-call(s32[4]{0:T(128)S(1)} %pad_add_fusion.info, bf16[4096,1024]{1,0:T(8,128)(2,1)S(1)} %get-tuple-element.49.points, s32[2,4096]{1,0:T(2,128)S(1)} %copy-done.3, f32[512,1024]{1,0:T(8,128)S(1)} %copy-done.2, f32[1,4096]{1,0:T(1,128)S(1)} %get-tuple-element.50.refs_0_, ...), custom_call_target="tpu_custom_call" | custom-call | flops 4294967296 | bytes 8388608 | tf_op jit(solution)/shard_map/energies_and_sums_01/pallas_call | solution.py:344
  20.6 0.0 collective-permute-done.sibling
  20.7 0.0 copy-start
  20.7 0.0 copy-start.1
  20.7 2.4 %collective-permute-start.1 = (f32[2,136,256]{2,1,0:T(8,128)S(1)}, f32[2,136,256]{2,1,0:T(8,128)S(1)}, u32[]{:S(2)}, u32[]{:S(2)}) collective-permute-start(f32[2,136,256]{2,1,0:T(8,128)S(1)} %slice_add_fusion.1), channel_id=1, source_target_pairs={{0,8},{4,20},{8,0},{12,28},{16,24},{20,4},{24,16},{28,12},{1,9},{5... | collective-permute-start | bytes 835592 | tf_op jit(solution)/shard_map/ppermute | solution.py:94
  23.1 0.1 collective-permute-start.2
  23.2 4.4 %collective-permute-done.1.refs_0_ = f32[2,136,256]{2,1,0:T(8,128)S(1)} collective-permute-done((f32[2,136,256]{2,1,0:T(8,128)S(1)}, f32[2,136,256]{2,1,0:T(8,128)S(1)}, u32[]{:S(2)}, u32[]{:S(2)}) %collective-permute-start.1) | collective-permute-done | bytes 278560 | tf_op jit(solution)/shard_map/ppermute | solution.py:94
  27.7 2.1 %collective-permute-start.3 = (f32[136,256]{1,0:T(8,128)S(1)}, f32[136,256]{1,0:T(8,128)S(1)}, u32[]{:S(2)}, u32[]{:S(2)}) collective-permute-start(f32[136,256]{1,0:T(8,128)S(1)} %fusion.1), channel_id=1, source_target_pairs={{0,16},{4,12},{8,24},{12,4},{16,0},{20,28},{24,8},{28,20},{1,17},{... | collective-permute-start | bytes 417800 | tf_op jit(solution)/shard_map/ppermute | solution.py:99
  29.8 0.8 collective-permute-done.2.refs_1_
  30.6 2.4 %collective-permute-start.4 = (f32[128,256]{1,0:T(8,128)S(1)}, f32[128,256]{1,0:T(8,128)S(1)}, u32[]{:S(2)}, u32[]{:S(2)}) collective-permute-start(f32[128,256]{1,0:T(8,128)S(1)} %fusion.4), channel_id=1, source_target_pairs={{0,16},{4,12},{8,24},{12,4},{16,0},{20,28},{24,8},{28,20},{1,17},{... | collective-permute-start | bytes 393224 | tf_op jit(solution)/shard_map/ppermute | solution.py:99
  33.1 2.9 %collective-permute-done.4.refs_3_ = f32[128,256]{1,0:T(8,128)S(1)} collective-permute-done((f32[128,256]{1,0:T(8,128)S(1)}, f32[128,256]{1,0:T(8,128)S(1)}, u32[]{:S(2)}, u32[]{:S(2)}) %collective-permute-start.4) | collective-permute-done | bytes 131104 | tf_op jit(solution)/shard_map/ppermute | solution.py:99
  36.0 0.0 collective-permute-done.3.refs_2_
  36.0 1.1 %refine_half.2 = (f32[128,256]{1,0:T(8,128)S(1)}, f32[128,256]{1,0:T(8,128)S(1)}, f32[72,256]{1,0:T(8,128)S(1)}) custom-call(s32[4]{0:T(128)S(1)} %pad_add_fusion.info, f32[4,264,256]{2,1,0:T(8,128)S(1)} %get-tuple-element.52.own, f32[4,264,256]{2,1,0:T(8,128)S(1)} %collective-permute-done.sibling, f32[2,136,256]{2,1,0:T(8,128)S(1)} %collective-permute-done.1.refs_0_, ...), custom_call_target="tpu_custom_call" | custom-call | tf_op jit(solution)/shard_map/refine_half/pallas_call | solution.py:408
  37.1 2.1 %collective-permute-start.5 = (f32[128,256]{1,0:T(8,128)S(1)}, f32[128,256]{1,0:T(8,128)S(1)}, u32[]{:S(2)}, u32[]{:S(2)}) collective-permute-start(f32[128,256]{1,0:T(8,128)S(1)} %get-tuple-element.68), channel_id=1, source_target_pairs={{0,8},{4,12},{8,0},{12,4},{16,24},{20,28},{24,16},{28,20},{1,9},{5... | collective-permute-start | bytes 393224 | tf_op jit(solution)/shard_map/ppermute | solution.py:89
  39.2 1.5 %collective-permute-start.6 = (f32[128,256]{1,0:T(8,128)S(1)}, f32[128,256]{1,0:T(8,128)S(1)}, u32[]{:S(2)}, u32[]{:S(2)}) collective-permute-start(f32[128,256]{1,0:T(8,128)S(1)} %get-tuple-element.67), channel_id=1, source_target_pairs={{0,16},{4,20},{8,24},{12,28},{16,0},{20,4},{24,8},{28,12},{1,17},{... | collective-permute-start | bytes 393224 | tf_op jit(solution)/shard_map/ppermute | solution.py:89
  40.8 0.6 collective-permute-start.10
  41.4 0.1 collective-permute-start.9
  41.4 1.9 %collective-permute-done.5.refs_0_ = f32[128,256]{1,0:T(8,128)S(1)} collective-permute-done((f32[128,256]{1,0:T(8,128)S(1)}, f32[128,256]{1,0:T(8,128)S(1)}, u32[]{:S(2)}, u32[]{:S(2)}) %collective-permute-start.5) | collective-permute-done | bytes 131104 | tf_op jit(solution)/shard_map/ppermute | solution.py:89
  43.3 2.3 %collective-permute-start.8 = (f32[128,256]{1,0:T(8,128)S(1)}, f32[128,256]{1,0:T(8,128)S(1)}, u32[]{:S(2)}, u32[]{:S(2)}) collective-permute-start(f32[128,256]{1,0:T(8,128)S(1)} %collective-permute-done.5.refs_0_), channel_id=1, source_target_pairs={{0,16},{4,20},{8,24},{12,28},{16,0},{20,4},{24,8},{28,12},{1,17},{... | collective-permute-start | bytes 393224 | tf_op jit(solution)/shard_map/ppermute | solution.py:89
  45.6 0.9 collective-permute-start.7
  46.5 1.6 %collective-permute-start.11 = (f32[104,256]{1,0:T(8,128)S(1)}, f32[104,256]{1,0:T(8,128)S(1)}, u32[]{:S(2)}, u32[]{:S(2)}) collective-permute-start(f32[104,256]{1,0:T(8,128)S(1)} %pad_maximum_fusion.3), channel_id=1, source_target_pairs={{0,1},{1,0},{2,3},{3,2},{4,5},{5,4},{6,7},{7,6},{8,9},{9,8},{10,11... | collective-permute-start | bytes 319496 | tf_op jit(solution)/shard_map/ppermute | solution.py:89
  48.1 3.5 %fetch_points.1.points = bf16[4096,1024]{1,0:T(8,128)(2,1)S(1)} custom-call(bf16[4096,1024]{1,0:T(8,128)(2,1)} %points.3, f32[128,256]{1,0:T(8,128)S(1)} %collective-permute-done.5.refs_0_, f32[128,256]{1,0:T(8,128)S(1)} %collective-permute-done.6.refs_1_), custom_call_target="tpu_custom_call" | custom-call | bytes 16777216 | tf_op jit(solution)/shard_map/fetch_points/pallas_call | solution.py:283
  51.6 0.0 collective-permute-done.11
  51.6 0.0 collective-permute-done.10
  51.8 0.1 collective-permute-start.12
  51.9 7.5 %energies_and_sums_10.1 = (f32[4,264,256]{2,1,0:T(8,128)S(1)}, f32[2,4096]{1,0:T(2,128)S(1)}) custom-call(s32[4]{0:T(128)S(1)} %pad_add_fusion.info, bf16[4096,1024]{1,0:T(8,128)(2,1)S(1)} %fetch_points.1.points, s32[2,4096]{1,0:T(2,128)S(1)} %copy-done.3, f32[8,128,256]{2,1,0:T(8,128)S(1)} %bitcast_dynamic-update-slice_fusion.fine, ...), custom_call_target="tpu_custom_call" | custom-call | flops 4294967296 | bytes 8388608 | tf_op jit(solution)/shard_map/energies_and_sums_10/pallas_call | solution.py:344
  59.4 0.6 collective-permute-start.14
  60.0 0.1 collective-permute-start.13
  60.1 7.8 %energies_and_sums_11.1 = (f32[4,264,256]{2,1,0:T(8,128)S(1)}, f32[2,4096]{1,0:T(2,128)S(1)}) custom-call(s32[4]{0:T(128)S(1)} %pad_add_fusion.info, bf16[4096,1024]{1,0:T(8,128)(2,1)S(1)} %fetch_points.1.points, s32[2,4096]{1,0:T(2,128)S(1)} %copy-done.3, f32[8,128,256]{2,1,0:T(8,128)S(1)} %collective-permute-done.12.fine, ...), custom_call_target="tpu_custom_call" | custom-call | flops 4294967296 | bytes 8388608 | tf_op jit(solution)/shard_map/energies_and_sums_11/pallas_call | solution.py:344
  68.1 1.2 %collective-permute-start.15 = (f32[2,136,256]{2,1,0:T(8,128)S(1)}, f32[2,136,256]{2,1,0:T(8,128)S(1)}, u32[]{:S(2)}, u32[]{:S(2)}) collective-permute-start(f32[2,136,256]{2,1,0:T(8,128)S(1)} %slice_add_fusion), channel_id=1, source_target_pairs={{0,8},{4,20},{8,0},{12,28},{16,24},{20,4},{24,16},{28,12},{1,9},{5... | collective-permute-start | bytes 835592 | tf_op jit(solution)/shard_map/ppermute | solution.py:94
  69.3 0.9 collective-permute-start.16
  70.2 2.6 %collective-permute-start.17 = (f32[104,256]{1,0:T(8,128)S(1)}, f32[104,256]{1,0:T(8,128)S(1)}, u32[]{:S(2)}, u32[]{:S(2)}) collective-permute-start(f32[104,256]{1,0:T(8,128)S(1)} %pad_maximum_fusion.4.refs_5_), channel_id=1, source_target_pairs={{0,2},{1,3},{2,0},{3,1},{4,6},{5,7},{6,4},{7,5},{8,10},{9,11},{10,... | collective-permute-start | bytes 319496 | tf_op jit(solution)/shard_map/ppermute | solution.py:89
  72.8 5.4 %collective-permute-done.17.refs_6_ = f32[104,256]{1,0:T(8,128)S(1)} collective-permute-done((f32[104,256]{1,0:T(8,128)S(1)}, f32[104,256]{1,0:T(8,128)S(1)}, u32[]{:S(2)}, u32[]{:S(2)}) %collective-permute-start.17) | collective-permute-done | bytes 106528 | tf_op jit(solution)/shard_map/ppermute | solution.py:89
  78.2 1.0 collective-permute-start.18
  79.2 0.7 fusion.3
  79.8 1.1 collective-permute-start.19
  81.0 4.0 %collective-permute-done.19.refs_3_ = f32[128,256]{1,0:T(8,128)S(1)} collective-permute-done((f32[128,256]{1,0:T(8,128)}, f32[128,256]{1,0:T(8,128)S(1)}, u32[]{:S(2)}, u32[]{:S(2)}) %collective-permute-start.19) | collective-permute-done | bytes 131104 | tf_op jit(solution)/shard_map/ppermute | solution.py:99
  85.0 1.2 %refine_half.3 = (f32[128,256]{1,0:T(8,128)S(1)}, f32[128,256]{1,0:T(8,128)S(1)}, f32[72,256]{1,0:T(8,128)S(1)}) custom-call(s32[4]{0:T(128)S(1)} %pad_add_fusion.info, f32[4,264,256]{2,1,0:T(8,128)S(1)} %get-tuple-element.74.own, f32[4,264,256]{2,1,0:T(8,128)S(1)} %collective-permute-done.14.sibling, f32[2,136,256]{2,1,0:T(8,128)S(1)} %collective-permute-done.15.refs_0_, ...), custom_call_target="tpu_custom_call" | custom-call | tf_op jit(solution)/shard_map/refine_half/pallas_call | solution.py:408
  86.3 0.6 collective-permute-start.26
  86.9 1.3 %collective-permute-start.20 = (f32[128,256]{1,0:T(8,128)S(1)}, f32[128,256]{1,0:T(8,128)S(1)}, u32[]{:S(2)}, u32[]{:S(2)}) collective-permute-start(f32[128,256]{1,0:T(8,128)S(1)} %get-tuple-element.91), channel_id=1, source_target_pairs={{0,8},{4,12},{8,0},{12,4},{16,24},{20,28},{24,16},{28,20},{1,9},{5... | collective-permute-start | bytes 393224 | tf_op jit(solution)/shard_map/ppermute | solution.py:89
  88.2 1.0 collective-permute-start.21
  89.2 1.8 %collective-permute-done.26 = f32[104,256]{1,0:T(8,128)S(1)} collective-permute-done((f32[104,256]{1,0:T(8,128)S(1)}, f32[104,256]{1,0:T(8,128)S(1)}, u32[]{:S(2)}, u32[]{:S(2)}) %collective-permute-start.26) | collective-permute-done | bytes 106528 | tf_op jit(solution)/shard_map/ppermute | solution.py:89
  91.1 2.0 %collective-permute-start.27 = (f32[104,256]{1,0:T(8,128)S(1)}, f32[104,256]{1,0:T(8,128)S(1)}, u32[]{:S(2)}, u32[]{:S(2)}) collective-permute-start(f32[104,256]{1,0:T(8,128)S(1)} %pad_maximum_fusion.6), channel_id=1, source_target_pairs={{0,2},{1,3},{2,0},{3,1},{4,6},{5,7},{6,4},{7,5},{8,10},{9,11},{10,... | collective-permute-start | bytes 319496 | tf_op jit(solution)/shard_map/ppermute | solution.py:89
  93.1 0.1 collective-permute-done.21
  93.2 1.4 %collective-permute-start.24 = (f32[128,256]{1,0:T(8,128)S(1)}, f32[128,256]{1,0:T(8,128)S(1)}, u32[]{:S(2)}, u32[]{:S(2)}) collective-permute-start(f32[128,256]{1,0:T(8,128)S(1)} %get-tuple-element.90), channel_id=1, source_target_pairs={{0,8},{4,12},{8,0},{12,4},{16,24},{20,28},{24,16},{28,20},{1,9},{5... | collective-permute-start | bytes 393224 | tf_op jit(solution)/shard_map/ppermute | solution.py:89
  94.6 1.0 collective-permute-start.25
  95.6 1.1 collective-permute-start.23
  96.6 0.6 collective-permute-start.22
  97.2 0.7 collective-permute-done.27
  98.0 1.8 %collective-permute-start.30 = (f32[72,256]{1,0:T(8,128)S(1)}, f32[72,256]{1,0:T(8,128)S(1)}, u32[]{:S(2)}, u32[]{:S(2)}) collective-permute-start(f32[72,256]{1,0:T(8,128)S(1)} %slice_add_fusion.11), channel_id=1, source_target_pairs={{0,24},{4,28},{8,16},{12,20},{16,8},{20,12},{24,0},{28,4},{1,25},{... | collective-permute-start | bytes 221192 | tf_op jit(solution)/shard_map/ppermute | solution.py:89
  99.7 2.5 %collective-permute-done.23 = f32[128,256]{1,0:T(8,128)S(1)} collective-permute-done((f32[128,256]{1,0:T(8,128)S(1)}, f32[128,256]{1,0:T(8,128)S(1)}, u32[]{:S(2)}, u32[]{:S(2)}) %collective-permute-start.23) | collective-permute-done | bytes 131104 | tf_op jit(solution)/shard_map/ppermute | solution.py:89
  102.3 0.8 collective-permute-start.29
  103.1 1.1 collective-permute-start.28
  104.2 0.1 collective-permute-start.31
  104.4 0.6 collective-permute-start.32
  104.9 1.7 %collective-permute-done.29 = f32[72,256]{1,0:T(8,128)S(1)} collective-permute-done((f32[72,256]{1,0:T(8,128)S(1)}, f32[72,256]{1,0:T(8,128)S(1)}, u32[]{:S(2)}, u32[]{:S(2)}) %collective-permute-start.29) | collective-permute-done | bytes 73760 | tf_op jit(solution)/shard_map/ppermute | solution.py:89
  106.6 0.8 collective-permute-done.28
  107.5 0.1 collective-permute-start.33
  107.6 0.7 maximum_multiply_fusion
  108.2 0.9 collective-permute-done.33.refs_5_
  109.1 2.1 %place_blocks.1 = (f32[512,1024]{1,0:T(8,128)}, f32[64,1024]{1,0:T(8,128)}) custom-call(s32[4]{0:T(128)S(1)} %pad_add_fusion.info, f32[4,128,256]{2,1,0:T(8,128)S(1)} %pad_maximum_fusion.refs_0_, f32[4,128,256]{2,1,0:T(8,128)S(1)} %pad_maximum_fusion.1.refs_1_, f32[4,72,256]{2,1,0:T(8,128)S(1)} %pad_maximum_fusion.2.refs_2_, ...), custom_call_target="tpu_custom_call" | custom-call | tf_op jit(solution)/shard_map/place_blocks/pallas_call | solution.py:510
  (59 shorter events, 0.7 us)
Async XLA Ops:
  0.7 12.3 %copy-start.2 = (f32[512,1024]{1,0:T(8,128)S(1)}, f32[512,1024]{1,0:T(8,128)}, u32[]{:S(2)}) copy-start(f32[512,1024]{1,0:T(8,128)} %fine.3) | copy-start | bytes 6291460
  0.7 12.3 %copy-start.3 = (s32[2,4096]{1,0:T(2,128)S(1)}, s32[2,4096]{1,0:T(2,128)}, u32[]{:S(2)}) copy-start(s32[2,4096]{1,0:T(2,128)} %assign.7) | copy-start | bytes 98308
  12.2 8.4 %collective-permute-start = (f32[4,264,256]{2,1,0:T(8,128)S(1)}, f32[4,264,256]{2,1,0:T(8,128)S(1)}, u32[]{:S(2)}, u32[]{:S(2)}) collective-permute-start(f32[4,264,256]{2,1,0:T(8,128)S(1)} %get-tuple-element.53), channel_id=1, source_target_pairs={{0,4},{4,0},{8,12},{12,8},{16,20},{20,16},{24,28},{28,24},{1,5},{5... | collective-permute-start | bytes 3244040 | tf_op jit(solution)/shard_map/ppermute | solution.py:89
  20.7 15.3 %copy-start = (f32[64,1024]{1,0:T(8,128)S(1)}, f32[64,1024]{1,0:T(8,128)}, u32[]{:S(2)}) copy-start(f32[64,1024]{1,0:T(8,128)} %refs_5_.1) | copy-start | bytes 786436
  20.7 15.3 %copy-start.1 = (s32[512]{0:T(512)S(1)}, s32[512]{0:T(512)}, u32[]{:S(2)}) copy-start(s32[512]{0:T(512)} %param.9) | copy-start | bytes 6148
  20.7 6.9 %collective-permute-start.1 = (f32[2,136,256]{2,1,0:T(8,128)S(1)}, f32[2,136,256]{2,1,0:T(8,128)S(1)}, u32[]{:S(2)}, u32[]{:S(2)}) collective-permute-start(f32[2,136,256]{2,1,0:T(8,128)S(1)} %slice_add_fusion.1), channel_id=1, source_target_pairs={{0,8},{4,20},{8,0},{12,28},{16,24},{20,4},{24,16},{28,12},{1,9},{5... | collective-permute-start | bytes 835592 | tf_op jit(solution)/shard_map/ppermute | solution.py:94
  23.1 7.5 %collective-permute-start.2 = (f32[2,128,256]{2,1,0:T(8,128)S(1)}, f32[2,128,256]{2,1,0:T(8,128)S(1)}, u32[]{:S(2)}, u32[]{:S(2)}) collective-permute-start(f32[2,128,256]{2,1,0:T(8,128)S(1)} %slice_add_fusion.3), channel_id=1, source_target_pairs={{0,8},{4,20},{8,0},{12,28},{16,24},{20,4},{24,16},{28,12},{1,9},{5... | collective-permute-start | bytes 786440 | tf_op jit(solution)/shard_map/ppermute | solution.py:94
  27.7 8.3 %collective-permute-start.3 = (f32[136,256]{1,0:T(8,128)S(1)}, f32[136,256]{1,0:T(8,128)S(1)}, u32[]{:S(2)}, u32[]{:S(2)}) collective-permute-start(f32[136,256]{1,0:T(8,128)S(1)} %fusion.1), channel_id=1, source_target_pairs={{0,16},{4,12},{8,24},{12,4},{16,0},{20,28},{24,8},{28,20},{1,17},{... | collective-permute-start | bytes 417800 | tf_op jit(solution)/shard_map/ppermute | solution.py:99
  30.6 5.4 %collective-permute-start.4 = (f32[128,256]{1,0:T(8,128)S(1)}, f32[128,256]{1,0:T(8,128)S(1)}, u32[]{:S(2)}, u32[]{:S(2)}) collective-permute-start(f32[128,256]{1,0:T(8,128)S(1)} %fusion.4), channel_id=1, source_target_pairs={{0,16},{4,12},{8,24},{12,4},{16,0},{20,28},{24,8},{28,20},{1,17},{... | collective-permute-start | bytes 393224 | tf_op jit(solution)/shard_map/ppermute | solution.py:99
  37.1 6.2 %collective-permute-start.5 = (f32[128,256]{1,0:T(8,128)S(1)}, f32[128,256]{1,0:T(8,128)S(1)}, u32[]{:S(2)}, u32[]{:S(2)}) collective-permute-start(f32[128,256]{1,0:T(8,128)S(1)} %get-tuple-element.68), channel_id=1, source_target_pairs={{0,8},{4,12},{8,0},{12,4},{16,24},{20,28},{24,16},{28,20},{1,9},{5... | collective-permute-start | bytes 393224 | tf_op jit(solution)/shard_map/ppermute | solution.py:89
  39.2 6.4 %collective-permute-start.6 = (f32[128,256]{1,0:T(8,128)S(1)}, f32[128,256]{1,0:T(8,128)S(1)}, u32[]{:S(2)}, u32[]{:S(2)}) collective-permute-start(f32[128,256]{1,0:T(8,128)S(1)} %get-tuple-element.67), channel_id=1, source_target_pairs={{0,16},{4,20},{8,24},{12,28},{16,0},{20,4},{24,8},{28,12},{1,17},{... | collective-permute-start | bytes 393224 | tf_op jit(solution)/shard_map/ppermute | solution.py:89
  40.8 10.9 %collective-permute-start.10 = (f32[128,256]{1,0:T(8,128)S(1)}, f32[128,256]{1,0:T(8,128)S(1)}, u32[]{:S(2)}, u32[]{:S(2)}) collective-permute-start(f32[128,256]{1,0:T(8,128)S(1)} %get-tuple-element.68), channel_id=1, source_target_pairs={{0,16},{4,20},{8,24},{12,28},{16,0},{20,4},{24,8},{28,12},{1,17},{... | collective-permute-start | bytes 393224 | tf_op jit(solution)/shard_map/ppermute | solution.py:89
  41.4 10.3 %collective-permute-start.9 = (f32[128,256]{1,0:T(8,128)S(1)}, f32[128,256]{1,0:T(8,128)S(1)}, u32[]{:S(2)}, u32[]{:S(2)}) collective-permute-start(f32[128,256]{1,0:T(8,128)S(1)} %get-tuple-element.67), channel_id=1, source_target_pairs={{0,8},{4,12},{8,0},{12,4},{16,24},{20,28},{24,16},{28,20},{1,9},{5... | collective-permute-start | bytes 393224 | tf_op jit(solution)/shard_map/ppermute | solution.py:89
  43.3 8.3 %collective-permute-start.8 = (f32[128,256]{1,0:T(8,128)S(1)}, f32[128,256]{1,0:T(8,128)S(1)}, u32[]{:S(2)}, u32[]{:S(2)}) collective-permute-start(f32[128,256]{1,0:T(8,128)S(1)} %collective-permute-done.5.refs_0_), channel_id=1, source_target_pairs={{0,16},{4,20},{8,24},{12,28},{16,0},{20,4},{24,8},{28,12},{1,17},{... | collective-permute-start | bytes 393224 | tf_op jit(solution)/shard_map/ppermute | solution.py:89
  45.6 6.0 %collective-permute-start.7 = (f32[128,256]{1,0:T(8,128)S(1)}, f32[128,256]{1,0:T(8,128)S(1)}, u32[]{:S(2)}, u32[]{:S(2)}) collective-permute-start(f32[128,256]{1,0:T(8,128)S(1)} %collective-permute-done.6.refs_1_), channel_id=1, source_target_pairs={{0,8},{4,12},{8,0},{12,4},{16,24},{20,28},{24,16},{28,20},{1,9},{5... | collective-permute-start | bytes 393224 | tf_op jit(solution)/shard_map/ppermute | solution.py:89
  46.5 5.1 %collective-permute-start.11 = (f32[104,256]{1,0:T(8,128)S(1)}, f32[104,256]{1,0:T(8,128)S(1)}, u32[]{:S(2)}, u32[]{:S(2)}) collective-permute-start(f32[104,256]{1,0:T(8,128)S(1)} %pad_maximum_fusion.3), channel_id=1, source_target_pairs={{0,1},{1,0},{2,3},{3,2},{4,5},{5,4},{6,7},{7,6},{8,9},{9,8},{10,11... | collective-permute-start | bytes 319496 | tf_op jit(solution)/shard_map/ppermute | solution.py:89
  51.8 8.3 %collective-permute-start.12 = (f32[8,128,256]{2,1,0:T(8,128)S(1)}, f32[8,128,256]{2,1,0:T(8,128)S(1)}, u32[]{:S(2)}, u32[]{:S(2)}) collective-permute-start(f32[8,128,256]{2,1,0:T(8,128)S(1)} %bitcast_dynamic-update-slice_fusion.fine), channel_id=1, source_target_pairs={{0,4},{4,0},{8,12},{12,8},{16,20},{20,16},{24,28},{28,24},{1,5},{5... | collective-permute-start | bytes 3145736 | tf_op jit(solution)/shard_map/ppermute | solution.py:89
  59.4 8.6 %collective-permute-start.14 = (f32[4,264,256]{2,1,0:T(8,128)S(1)}, f32[4,264,256]{2,1,0:T(8,128)S(1)}, u32[]{:S(2)}, u32[]{:S(2)}) collective-permute-start(f32[4,264,256]{2,1,0:T(8,128)S(1)} %get-tuple-element.75), channel_id=1, source_target_pairs={{0,4},{4,0},{8,12},{12,8},{16,20},{20,16},{24,28},{28,24},{1,5},{5... | collective-permute-start | bytes 3244040 | tf_op jit(solution)/shard_map/ppermute | solution.py:89
  60.0 7.9 %collective-permute-start.13 = (f32[72,256]{1,0:T(8,128)S(1)}, f32[72,256]{1,0:T(8,128)S(1)}, u32[]{:S(2)}, u32[]{:S(2)}) collective-permute-start(f32[72,256]{1,0:T(8,128)S(1)} %slice_add_fusion.13), channel_id=1, source_target_pairs={{0,4},{4,0},{8,12},{12,8},{16,20},{20,16},{24,28},{28,24},{1,5},{5... | collective-permute-start | bytes 221192 | tf_op jit(solution)/shard_map/ppermute | solution.py:89
  68.1 10.1 %collective-permute-start.15 = (f32[2,136,256]{2,1,0:T(8,128)S(1)}, f32[2,136,256]{2,1,0:T(8,128)S(1)}, u32[]{:S(2)}, u32[]{:S(2)}) collective-permute-start(f32[2,136,256]{2,1,0:T(8,128)S(1)} %slice_add_fusion), channel_id=1, source_target_pairs={{0,8},{4,20},{8,0},{12,28},{16,24},{20,4},{24,16},{28,12},{1,9},{5... | collective-permute-start | bytes 835592 | tf_op jit(solution)/shard_map/ppermute | solution.py:94
  69.3 8.8 %collective-permute-start.16 = (f32[2,128,256]{2,1,0:T(8,128)S(1)}, f32[2,128,256]{2,1,0:T(8,128)S(1)}, u32[]{:S(2)}, u32[]{:S(2)}) collective-permute-start(f32[2,128,256]{2,1,0:T(8,128)S(1)} %slice_add_fusion.2), channel_id=1, source_target_pairs={{0,8},{4,20},{8,0},{12,28},{16,24},{20,4},{24,16},{28,12},{1,9},{5... | collective-permute-start | bytes 786440 | tf_op jit(solution)/shard_map/ppermute | solution.py:94
  70.2 8.0 %collective-permute-start.17 = (f32[104,256]{1,0:T(8,128)S(1)}, f32[104,256]{1,0:T(8,128)S(1)}, u32[]{:S(2)}, u32[]{:S(2)}) collective-permute-start(f32[104,256]{1,0:T(8,128)S(1)} %pad_maximum_fusion.4.refs_5_), channel_id=1, source_target_pairs={{0,2},{1,3},{2,0},{3,1},{4,6},{5,7},{6,4},{7,5},{8,10},{9,11},{10,... | collective-permute-start | bytes 319496 | tf_op jit(solution)/shard_map/ppermute | solution.py:89
  78.2 6.8 %collective-permute-start.18 = (f32[136,256]{1,0:T(8,128)S(1)}, f32[136,256]{1,0:T(8,128)S(1)}, u32[]{:S(2)}, u32[]{:S(2)}) collective-permute-start(f32[136,256]{1,0:T(8,128)S(1)} %fusion), channel_id=1, source_target_pairs={{0,16},{4,12},{8,24},{12,4},{16,0},{20,28},{24,8},{28,20},{1,17},{... | collective-permute-start | bytes 417800 | tf_op jit(solution)/shard_map/ppermute | solution.py:99
  79.8 5.2 %collective-permute-start.19 = (f32[128,256]{1,0:T(8,128)}, f32[128,256]{1,0:T(8,128)S(1)}, u32[]{:S(2)}, u32[]{:S(2)}) collective-permute-start(f32[128,256]{1,0:T(8,128)} %fusion.3), channel_id=1, source_target_pairs={{0,16},{4,12},{8,24},{12,4},{16,0},{20,28},{24,8},{28,20},{1,17},{... | collective-permute-start | bytes 393224 | tf_op jit(solution)/shard_map/ppermute | solution.py:99
  86.3 4.8 %collective-permute-start.26 = (f32[104,256]{1,0:T(8,128)S(1)}, f32[104,256]{1,0:T(8,128)S(1)}, u32[]{:S(2)}, u32[]{:S(2)}) collective-permute-start(f32[104,256]{1,0:T(8,128)S(1)} %pad_maximum_fusion.5), channel_id=1, source_target_pairs={{0,1},{1,0},{2,3},{3,2},{4,5},{5,4},{6,7},{7,6},{8,9},{9,8},{10,11... | collective-permute-start | bytes 319496 | tf_op jit(solution)/shard_map/ppermute | solution.py:89
  86.9 6.2 %collective-permute-start.20 = (f32[128,256]{1,0:T(8,128)S(1)}, f32[128,256]{1,0:T(8,128)S(1)}, u32[]{:S(2)}, u32[]{:S(2)}) collective-permute-start(f32[128,256]{1,0:T(8,128)S(1)} %get-tuple-element.91), channel_id=1, source_target_pairs={{0,8},{4,12},{8,0},{12,4},{16,24},{20,28},{24,16},{28,20},{1,9},{5... | collective-permute-start | bytes 393224 | tf_op jit(solution)/shard_map/ppermute | solution.py:89
  88.2 5.0 %collective-permute-start.21 = (f32[128,256]{1,0:T(8,128)S(1)}, f32[128,256]{1,0:T(8,128)S(1)}, u32[]{:S(2)}, u32[]{:S(2)}) collective-permute-start(f32[128,256]{1,0:T(8,128)S(1)} %get-tuple-element.90), channel_id=1, source_target_pairs={{0,16},{4,20},{8,24},{12,28},{16,0},{20,4},{24,8},{28,12},{1,17},{... | collective-permute-start | bytes 393224 | tf_op jit(solution)/shard_map/ppermute | solution.py:89
  91.1 6.8 %collective-permute-start.27 = (f32[104,256]{1,0:T(8,128)S(1)}, f32[104,256]{1,0:T(8,128)S(1)}, u32[]{:S(2)}, u32[]{:S(2)}) collective-permute-start(f32[104,256]{1,0:T(8,128)S(1)} %pad_maximum_fusion.6), channel_id=1, source_target_pairs={{0,2},{1,3},{2,0},{3,1},{4,6},{5,7},{6,4},{7,5},{8,10},{9,11},{10,... | collective-permute-start | bytes 319496 | tf_op jit(solution)/shard_map/ppermute | solution.py:89
  93.2 11.1 %collective-permute-start.24 = (f32[128,256]{1,0:T(8,128)S(1)}, f32[128,256]{1,0:T(8,128)S(1)}, u32[]{:S(2)}, u32[]{:S(2)}) collective-permute-start(f32[128,256]{1,0:T(8,128)S(1)} %get-tuple-element.90), channel_id=1, source_target_pairs={{0,8},{4,12},{8,0},{12,4},{16,24},{20,28},{24,16},{28,20},{1,9},{5... | collective-permute-start | bytes 393224 | tf_op jit(solution)/shard_map/ppermute | solution.py:89
  94.6 9.7 %collective-permute-start.25 = (f32[128,256]{1,0:T(8,128)S(1)}, f32[128,256]{1,0:T(8,128)S(1)}, u32[]{:S(2)}, u32[]{:S(2)}) collective-permute-start(f32[128,256]{1,0:T(8,128)S(1)} %get-tuple-element.91), channel_id=1, source_target_pairs={{0,16},{4,20},{8,24},{12,28},{16,0},{20,4},{24,8},{28,12},{1,17},{... | collective-permute-start | bytes 393224 | tf_op jit(solution)/shard_map/ppermute | solution.py:89
  95.6 6.7 %collective-permute-start.23 = (f32[128,256]{1,0:T(8,128)S(1)}, f32[128,256]{1,0:T(8,128)S(1)}, u32[]{:S(2)}, u32[]{:S(2)}) collective-permute-start(f32[128,256]{1,0:T(8,128)S(1)} %collective-permute-done.20), channel_id=1, source_target_pairs={{0,16},{4,20},{8,24},{12,28},{16,0},{20,4},{24,8},{28,12},{1,17},{... | collective-permute-start | bytes 393224 | tf_op jit(solution)/shard_map/ppermute | solution.py:89
  96.6 6.5 %collective-permute-start.22 = (f32[128,256]{1,0:T(8,128)S(1)}, f32[128,256]{1,0:T(8,128)S(1)}, u32[]{:S(2)}, u32[]{:S(2)}) collective-permute-start(f32[128,256]{1,0:T(8,128)S(1)} %collective-permute-done.21), channel_id=1, source_target_pairs={{0,8},{4,12},{8,0},{12,4},{16,24},{20,28},{24,16},{28,20},{1,9},{5... | collective-permute-start | bytes 393224 | tf_op jit(solution)/shard_map/ppermute | solution.py:89
  98.0 7.0 %collective-permute-start.30 = (f32[72,256]{1,0:T(8,128)S(1)}, f32[72,256]{1,0:T(8,128)S(1)}, u32[]{:S(2)}, u32[]{:S(2)}) collective-permute-start(f32[72,256]{1,0:T(8,128)S(1)} %slice_add_fusion.11), channel_id=1, source_target_pairs={{0,24},{4,28},{8,16},{12,20},{16,8},{20,12},{24,0},{28,4},{1,25},{... | collective-permute-start | bytes 221192 | tf_op jit(solution)/shard_map/ppermute | solution.py:89
  102.3 4.4 %collective-permute-start.29 = (f32[72,256]{1,0:T(8,128)S(1)}, f32[72,256]{1,0:T(8,128)S(1)}, u32[]{:S(2)}, u32[]{:S(2)}) collective-permute-start(f32[72,256]{1,0:T(8,128)S(1)} %slice_add_fusion.11), channel_id=1, source_target_pairs={{0,16},{4,20},{8,24},{12,28},{16,0},{20,4},{24,8},{28,12},{1,17},{... | collective-permute-start | bytes 221192 | tf_op jit(solution)/shard_map/ppermute | solution.py:89
  103.1 4.4 %collective-permute-start.28 = (f32[72,256]{1,0:T(8,128)S(1)}, f32[72,256]{1,0:T(8,128)S(1)}, u32[]{:S(2)}, u32[]{:S(2)}) collective-permute-start(f32[72,256]{1,0:T(8,128)S(1)} %slice_add_fusion.11), channel_id=1, source_target_pairs={{0,8},{4,12},{8,0},{12,4},{16,24},{20,28},{24,16},{28,20},{1,9},{5... | collective-permute-start | bytes 221192 | tf_op jit(solution)/shard_map/ppermute | solution.py:89
  104.2 4.9 %collective-permute-start.31 = (f32[4,128,256]{2,1,0:T(8,128)S(1)}, f32[4,128,256]{2,1,0:T(8,128)S(1)}, u32[]{:S(2)}, u32[]{:S(2)}) collective-permute-start(f32[4,128,256]{2,1,0:T(8,128)S(1)} %pad_maximum_fusion.refs_0_), channel_id=1, source_target_pairs={{0,4},{4,0},{8,12},{12,8},{16,20},{20,16},{24,28},{28,24},{1,5},{5... | collective-permute-start | bytes 1572872 | tf_op jit(solution)/shard_map/ppermute | solution.py:89
  104.4 4.8 %collective-permute-start.32 = (f32[4,128,256]{2,1,0:T(8,128)S(1)}, f32[4,128,256]{2,1,0:T(8,128)S(1)}, u32[]{:S(2)}, u32[]{:S(2)}) collective-permute-start(f32[4,128,256]{2,1,0:T(8,128)S(1)} %pad_maximum_fusion.1.refs_1_), channel_id=1, source_target_pairs={{0,4},{4,0},{8,12},{12,8},{16,20},{20,16},{24,28},{28,24},{1,5},{5... | collective-permute-start | bytes 1572872 | tf_op jit(solution)/shard_map/ppermute | solution.py:89
  107.5 1.6 %collective-permute-start.33 = (f32[4,72,256]{2,1,0:T(8,128)S(1)}, f32[4,72,256]{2,1,0:T(8,128)S(1)}, u32[]{:S(2)}, u32[]{:S(2)}) collective-permute-start(f32[4,72,256]{2,1,0:T(8,128)S(1)} %pad_maximum_fusion.2.refs_2_), channel_id=1, source_target_pairs={{0,4},{4,0},{8,12},{12,8},{16,20},{20,16},{24,28},{28,24},{1,5},{5... | collective-permute-start | bytes 884744 | tf_op jit(solution)/shard_map/ppermute | solution.py:89

commit v19 on v18

--- a/solution.py
+++ b/solution.py
@@ -574,7 +574,9 @@
     own = gather_half(top, low, True)
     folded = over_cen(folded, fold)
     part, seen_second = folded[: NC + TAIL], folded[NC + TAIL :]
-    blocks = [jnp.stack(own[:4]), jnp.stack(own[4:]), jnp.stack(spread(part))]
+    parts = spread(part)
+    own[2], own[3], parts[1] = lax.optimization_barrier((own[2], own[3], parts[1]))
+    blocks = [jnp.stack(own[:4]), jnp.stack(own[4:]), jnp.stack(parts)]
     fine_now, coarse_now = place(info, blocks, [swap(block, CORE) for block in blocks], flip=1)
 
     seen = [each.reshape(2, -1) for each in (seen_first, seen_second)]

time: 112 us -> 110 us (0.982)
  waiting for transfers between devices: 28.1 us -> 26.4 us
    ppermute x26, waiting for transfers between devices: 15.9 us -> 14.2 us  [swap(): return lax.ppermute(value, axis, [(i, i ^ bit) for i in range(size)])]
  transfers between devices with their start and end apart: 34 -> 34, of which waited for: 13 -> 12; matrix products, arithmetic and copies ran while one was open for 2% -> 2% of each run, Pallas kernels for 24% -> 24%
where the time goes in v19:
time: 110 us
  Pallas kernels  42.4 us (39%)
  starting transfers between devices  37.8 us (34%)
  waiting for transfers between devices  26.4 us (24%)
  other arithmetic  1.85 us (2%)
  between operations  1.22 us (1%)
    pallas_call x4, Pallas kernels, run_pass(): pl.pallas_call(body, out_shape=out_shape, in_specs=[SCALARS, *in_specs],...  34.5 us
    ppermute x26, starting transfers between devices, swap(): return lax.ppermute(value, axis, [(i, i ^ bit) for i in range(size)])  26.6 us
    ppermute x26, waiting for transfers between devices, swap(): return lax.ppermute(value, axis, [(i, i ^ bit) for i in range(size)])  14.2 us
    ppermute x4, waiting for transfers between devices, swap_second(): return lax.ppermute(value, 'pts', pairs)  6.99 us
    ppermute x4, starting transfers between devices, swap_second(): return lax.ppermute(value, 'pts', pairs)  6.61 us
    ppermute x4, waiting for transfers between devices, swap_first(): return lax.ppermute(value, 'pts', pairs)  5.27 us
    ppermute x4, starting transfers between devices, swap_first(): return lax.ppermute(value, 'pts', pairs)  4.56 us
    pallas_call x1, Pallas kernels, fetch(): pl.pallas_call(fetch_body, out_shape=pltpu.VMEM(points.shape, points.dtyp...  3.47 us
  transfers between devices with their start and end apart: 34, of which 12 were waited for; matrix products, arithmetic and copies ran while one was open for 2% of the time, Pallas kernels for 24%

profile of v19, /device:TPU:0, one launch (start us, length us, event | category | flops | bytes accessed | tf_op | source)
XLA Modules:
  0.0 109.9 jit_solution(1324735307695581290)
XLA Ops:
  0.6 0.1 pad_add_fusion.info
  0.7 11.5 %energies_and_sums_00.1 = (f32[4,264,256]{2,1,0:T(8,128)S(1)}, f32[2,4096]{1,0:T(2,128)S(1)}, f32[1,4096]{1,0:T(1,128)S(1)}, bf16[4096,1024]{1,0:T(8,128)(2,1)S(1)}) custom-call(s32[4]{0:T(128)S(1)} %pad_add_fusion.info, bf16[4096,1024]{1,0:T(8,128)(2,1)} %points.3, s32[2,4096]{1,0:T(2,128)} %assign.7, f32[512,1024]{1,0:T(8,128)} %fine.3), custom_call_target="tpu_custom_call" | custom-call | flops 4294967296 | bytes 8388608 | tf_op jit(solution)/shard_map/energies_and_sums_00/pallas_call | solution.py:344
  12.2 0.8 collective-permute-start
  13.0 7.6 %energies_and_sums_01.1 = (f32[4,264,256]{2,1,0:T(8,128)S(1)}, f32[2,4096]{1,0:T(2,128)S(1)}) custom-call(s32[4]{0:T(128)S(1)} %pad_add_fusion.info, bf16[4096,1024]{1,0:T(8,128)(2,1)S(1)} %get-tuple-element.52.points, s32[2,4096]{1,0:T(2,128)S(1)} %copy-done.3, f32[512,1024]{1,0:T(8,128)S(1)} %copy-done.2, f32[1,4096]{1,0:T(1,128)S(1)} %get-tuple-element.53.refs_0_, ...), custom_call_target="tpu_custom_call" | custom-call | flops 4294967296 | bytes 8388608 | tf_op jit(solution)/shard_map/energies_and_sums_01/pallas_call | solution.py:344
  20.7 0.0 copy-start
  20.7 0.0 copy-start.1
  20.7 2.4 %collective-permute-start.1 = (f32[2,136,256]{2,1,0:T(8,128)S(1)}, f32[2,136,256]{2,1,0:T(8,128)S(1)}, u32[]{:S(2)}, u32[]{:S(2)}) collective-permute-start(f32[2,136,256]{2,1,0:T(8,128)S(1)} %slice_add_fusion.1), channel_id=1, source_target_pairs={{0,8},{4,20},{8,0},{12,28},{16,24},{20,4},{24,16},{28,12},{1,9},{5... | collective-permute-start | bytes 835592 | tf_op jit(solution)/shard_map/ppermute | solution.py:94
  23.1 0.1 collective-permute-start.2
  23.2 4.4 %collective-permute-done.1.refs_0_ = f32[2,136,256]{2,1,0:T(8,128)S(1)} collective-permute-done((f32[2,136,256]{2,1,0:T(8,128)S(1)}, f32[2,136,256]{2,1,0:T(8,128)S(1)}, u32[]{:S(2)}, u32[]{:S(2)}) %collective-permute-start.1) | collective-permute-done | bytes 278560 | tf_op jit(solution)/shard_map/ppermute | solution.py:94
  27.7 2.1 %collective-permute-start.3 = (f32[136,256]{1,0:T(8,128)S(1)}, f32[136,256]{1,0:T(8,128)S(1)}, u32[]{:S(2)}, u32[]{:S(2)}) collective-permute-start(f32[136,256]{1,0:T(8,128)S(1)} %fusion.1), channel_id=1, source_target_pairs={{0,16},{4,12},{8,24},{12,4},{16,0},{20,28},{24,8},{28,20},{1,17},{... | collective-permute-start | bytes 417800 | tf_op jit(solution)/shard_map/ppermute | solution.py:99
  29.8 0.8 collective-permute-done.2.refs_1_
  30.6 2.4 %collective-permute-start.4 = (f32[128,256]{1,0:T(8,128)S(1)}, f32[128,256]{1,0:T(8,128)S(1)}, u32[]{:S(2)}, u32[]{:S(2)}) collective-permute-start(f32[128,256]{1,0:T(8,128)S(1)} %fusion.4), channel_id=1, source_target_pairs={{0,16},{4,12},{8,24},{12,4},{16,0},{20,28},{24,8},{28,20},{1,17},{... | collective-permute-start | bytes 393224 | tf_op jit(solution)/shard_map/ppermute | solution.py:99
  33.1 2.9 %collective-permute-done.4.refs_3_ = f32[128,256]{1,0:T(8,128)S(1)} collective-permute-done((f32[128,256]{1,0:T(8,128)S(1)}, f32[128,256]{1,0:T(8,128)S(1)}, u32[]{:S(2)}, u32[]{:S(2)}) %collective-permute-start.4) | collective-permute-done | bytes 131104 | tf_op jit(solution)/shard_map/ppermute | solution.py:99
  36.0 0.0 collective-permute-done.3.refs_2_
  36.0 1.1 %refine_half.2 = (f32[128,256]{1,0:T(8,128)S(1)}, f32[128,256]{1,0:T(8,128)S(1)}, f32[72,256]{1,0:T(8,128)S(1)}) custom-call(s32[4]{0:T(128)S(1)} %pad_add_fusion.info, f32[4,264,256]{2,1,0:T(8,128)S(1)} %get-tuple-element.55.own, f32[4,264,256]{2,1,0:T(8,128)S(1)} %collective-permute-done.sibling, f32[2,136,256]{2,1,0:T(8,128)S(1)} %collective-permute-done.1.refs_0_, ...), custom_call_target="tpu_custom_call" | custom-call | tf_op jit(solution)/shard_map/refine_half/pallas_call | solution.py:408
  37.1 2.1 %collective-permute-start.5 = (f32[128,256]{1,0:T(8,128)S(1)}, f32[128,256]{1,0:T(8,128)S(1)}, u32[]{:S(2)}, u32[]{:S(2)}) collective-permute-start(f32[128,256]{1,0:T(8,128)S(1)} %get-tuple-element.71), channel_id=1, source_target_pairs={{0,8},{4,12},{8,0},{12,4},{16,24},{20,28},{24,16},{28,20},{1,9},{5... | collective-permute-start | bytes 393224 | tf_op jit(solution)/shard_map/ppermute | solution.py:89
  39.2 1.5 %collective-permute-start.6 = (f32[128,256]{1,0:T(8,128)S(1)}, f32[128,256]{1,0:T(8,128)S(1)}, u32[]{:S(2)}, u32[]{:S(2)}) collective-permute-start(f32[128,256]{1,0:T(8,128)S(1)} %get-tuple-element.70), channel_id=1, source_target_pairs={{0,16},{4,20},{8,24},{12,28},{16,0},{20,4},{24,8},{28,12},{1,17},{... | collective-permute-start | bytes 393224 | tf_op jit(solution)/shard_map/ppermute | solution.py:89
  40.8 0.6 collective-permute-start.10
  41.4 0.1 collective-permute-start.9
  41.4 1.9 %collective-permute-done.5.refs_0_ = f32[128,256]{1,0:T(8,128)S(1)} collective-permute-done((f32[128,256]{1,0:T(8,128)S(1)}, f32[128,256]{1,0:T(8,128)S(1)}, u32[]{:S(2)}, u32[]{:S(2)}) %collective-permute-start.5) | collective-permute-done | bytes 131104 | tf_op jit(solution)/shard_map/ppermute | solution.py:89
  43.3 2.3 %collective-permute-start.8 = (f32[128,256]{1,0:T(8,128)S(1)}, f32[128,256]{1,0:T(8,128)S(1)}, u32[]{:S(2)}, u32[]{:S(2)}) collective-permute-start(f32[128,256]{1,0:T(8,128)S(1)} %collective-permute-done.5.refs_0_), channel_id=1, source_target_pairs={{0,16},{4,20},{8,24},{12,28},{16,0},{20,4},{24,8},{28,12},{1,17},{... | collective-permute-start | bytes 393224 | tf_op jit(solution)/shard_map/ppermute | solution.py:89
  45.6 0.0 collective-permute-done.6.refs_1_
  45.6 0.9 collective-permute-start.7
  46.5 1.6 %collective-permute-start.11 = (f32[104,256]{1,0:T(8,128)S(1)}, f32[104,256]{1,0:T(8,128)S(1)}, u32[]{:S(2)}, u32[]{:S(2)}) collective-permute-start(f32[104,256]{1,0:T(8,128)S(1)} %pad_maximum_fusion.3), channel_id=1, source_target_pairs={{0,1},{1,0},{2,3},{3,2},{4,5},{5,4},{6,7},{7,6},{8,9},{9,8},{10,11... | collective-permute-start | bytes 319496 | tf_op jit(solution)/shard_map/ppermute | solution.py:89
  48.1 3.5 %fetch_points.1.points = bf16[4096,1024]{1,0:T(8,128)(2,1)S(1)} custom-call(bf16[4096,1024]{1,0:T(8,128)(2,1)} %points.3, f32[128,256]{1,0:T(8,128)S(1)} %collective-permute-done.5.refs_0_, f32[128,256]{1,0:T(8,128)S(1)} %collective-permute-done.6.refs_1_), custom_call_target="tpu_custom_call" | custom-call | bytes 16777216 | tf_op jit(solution)/shard_map/fetch_points/pallas_call | solution.py:283
  51.6 0.0 collective-permute-done.11
  51.6 0.0 collective-permute-done.9
  51.6 0.0 collective-permute-done.8
  51.8 0.1 collective-permute-start.12
  51.9 7.5 %energies_and_sums_10.1 = (f32[4,264,256]{2,1,0:T(8,128)S(1)}, f32[2,4096]{1,0:T(2,128)S(1)}) custom-call(s32[4]{0:T(128)S(1)} %pad_add_fusion.info, bf16[4096,1024]{1,0:T(8,128)(2,1)S(1)} %fetch_points.1.points, s32[2,4096]{1,0:T(2,128)S(1)} %copy-done.3, f32[8,128,256]{2,1,0:T(8,128)S(1)} %bitcast_dynamic-update-slice_fusion.fine, ...), custom_call_target="tpu_custom_call" | custom-call | flops 4294967296 | bytes 8388608 | tf_op jit(solution)/shard_map/energies_and_sums_10/pallas_call | solution.py:344
  59.4 0.6 collective-permute-start.14
  60.0 0.1 collective-permute-start.13
  60.1 7.8 %energies_and_sums_11.1 = (f32[4,264,256]{2,1,0:T(8,128)S(1)}, f32[2,4096]{1,0:T(2,128)S(1)}) custom-call(s32[4]{0:T(128)S(1)} %pad_add_fusion.info, bf16[4096,1024]{1,0:T(8,128)(2,1)S(1)} %fetch_points.1.points, s32[2,4096]{1,0:T(2,128)S(1)} %copy-done.3, f32[8,128,256]{2,1,0:T(8,128)S(1)} %collective-permute-done.12.fine, ...), custom_call_target="tpu_custom_call" | custom-call | flops 4294967296 | bytes 8388608 | tf_op jit(solution)/shard_map/energies_and_sums_11/pallas_call | solution.py:344
  68.0 0.0 collective-permute-done.13
  68.1 1.2 %collective-permute-start.15 = (f32[2,136,256]{2,1,0:T(8,128)S(1)}, f32[2,136,256]{2,1,0:T(8,128)S(1)}, u32[]{:S(2)}, u32[]{:S(2)}) collective-permute-start(f32[2,136,256]{2,1,0:T(8,128)S(1)} %slice_add_fusion), channel_id=1, source_target_pairs={{0,8},{4,20},{8,0},{12,28},{16,24},{20,4},{24,16},{28,12},{1,9},{5... | collective-permute-start | bytes 835592 | tf_op jit(solution)/shard_map/ppermute | solution.py:94
  69.3 0.9 collective-permute-start.16
  70.2 2.6 %collective-permute-start.17 = (f32[104,256]{1,0:T(8,128)S(1)}, f32[104,256]{1,0:T(8,128)S(1)}, u32[]{:S(2)}, u32[]{:S(2)}) collective-permute-start(f32[104,256]{1,0:T(8,128)S(1)} %pad_maximum_fusion.4.refs_5_), channel_id=1, source_target_pairs={{0,2},{1,3},{2,0},{3,1},{4,6},{5,7},{6,4},{7,5},{8,10},{9,11},{10,... | collective-permute-start | bytes 319496 | tf_op jit(solution)/shard_map/ppermute | solution.py:89
  72.8 5.4 %collective-permute-done.17.refs_6_ = f32[104,256]{1,0:T(8,128)S(1)} collective-permute-done((f32[104,256]{1,0:T(8,128)S(1)}, f32[104,256]{1,0:T(8,128)S(1)}, u32[]{:S(2)}, u32[]{:S(2)}) %collective-permute-start.17) | collective-permute-done | bytes 106528 | tf_op jit(solution)/shard_map/ppermute | solution.py:89
  78.2 1.0 collective-permute-start.18
  79.2 0.7 fusion.3
  79.8 1.1 %collective-permute-start.19 = (f32[128,256]{1,0:T(8,128)}, f32[128,256]{1,0:T(8,128)S(1)}, u32[]{:S(2)}, u32[]{:S(2)}) collective-permute-start(f32[128,256]{1,0:T(8,128)} %fusion.3), channel_id=1, source_target_pairs={{0,16},{4,12},{8,24},{12,4},{16,0},{20,28},{24,8},{28,20},{1,17},{... | collective-permute-start | bytes 393224 | tf_op jit(solution)/shard_map/ppermute | solution.py:99
  81.0 4.0 %collective-permute-done.19.refs_3_ = f32[128,256]{1,0:T(8,128)S(1)} collective-permute-done((f32[128,256]{1,0:T(8,128)}, f32[128,256]{1,0:T(8,128)S(1)}, u32[]{:S(2)}, u32[]{:S(2)}) %collective-permute-start.19) | collective-permute-done | bytes 131104 | tf_op jit(solution)/shard_map/ppermute | solution.py:99
  85.0 1.2 %refine_half.3 = (f32[128,256]{1,0:T(8,128)S(1)}, f32[128,256]{1,0:T(8,128)S(1)}, f32[72,256]{1,0:T(8,128)S(1)}) custom-call(s32[4]{0:T(128)S(1)} %pad_add_fusion.info, f32[4,264,256]{2,1,0:T(8,128)S(1)} %get-tuple-element.77.own, f32[4,264,256]{2,1,0:T(8,128)S(1)} %collective-permute-done.14.sibling, f32[2,136,256]{2,1,0:T(8,128)S(1)} %collective-permute-done.15.refs_0_, ...), custom_call_target="tpu_custom_call" | custom-call | tf_op jit(solution)/shard_map/refine_half/pallas_call | solution.py:408
  86.3 0.6 collective-permute-start.24
  86.9 1.3 %collective-permute-start.20 = (f32[128,256]{1,0:T(8,128)S(1)}, f32[128,256]{1,0:T(8,128)S(1)}, u32[]{:S(2)}, u32[]{:S(2)}) collective-permute-start(f32[128,256]{1,0:T(8,128)S(1)} %get-tuple-element.97), channel_id=1, source_target_pairs={{0,8},{4,12},{8,0},{12,4},{16,24},{20,28},{24,16},{28,20},{1,9},{5... | collective-permute-start | bytes 393224 | tf_op jit(solution)/shard_map/ppermute | solution.py:89
  88.2 1.0 collective-permute-start.21
  89.2 1.8 %collective-permute-done.24 = f32[104,256]{1,0:T(8,128)S(1)} collective-permute-done((f32[104,256]{1,0:T(8,128)S(1)}, f32[104,256]{1,0:T(8,128)S(1)}, u32[]{:S(2)}, u32[]{:S(2)}) %collective-permute-start.24) | collective-permute-done | bytes 106528 | tf_op jit(solution)/shard_map/ppermute | solution.py:89
  91.1 2.0 %collective-permute-start.25 = (f32[104,256]{1,0:T(8,128)S(1)}, f32[104,256]{1,0:T(8,128)S(1)}, u32[]{:S(2)}, u32[]{:S(2)}) collective-permute-start(f32[104,256]{1,0:T(8,128)S(1)} %pad_maximum_fusion.6), channel_id=1, source_target_pairs={{0,2},{1,3},{2,0},{3,1},{4,6},{5,7},{6,4},{7,5},{8,10},{9,11},{10,... | collective-permute-start | bytes 319496 | tf_op jit(solution)/shard_map/ppermute | solution.py:89
  93.1 0.1 collective-permute-done.21
  93.2 1.4 %collective-permute-start.27 = (f32[128,256]{1,0:T(8,128)S(1)}, f32[128,256]{1,0:T(8,128)S(1)}, u32[]{:S(2)}, u32[]{:S(2)}) collective-permute-start(f32[128,256]{1,0:T(8,128)S(1)} %get-tuple-element.96), channel_id=1, source_target_pairs={{0,8},{4,12},{8,0},{12,4},{16,24},{20,28},{24,16},{28,20},{1,9},{5... | collective-permute-start | bytes 393224 | tf_op jit(solution)/shard_map/ppermute | solution.py:89
  94.6 1.0 collective-permute-start.28
  95.6 1.1 collective-permute-start.23
  96.6 0.6 collective-permute-start.22
  97.2 0.7 collective-permute-done.25
  98.0 1.8 %collective-permute-start.30 = (f32[72,256]{1,0:T(8,128)S(1)}, f32[72,256]{1,0:T(8,128)S(1)}, u32[]{:S(2)}, u32[]{:S(2)}) collective-permute-start(f32[72,256]{1,0:T(8,128)S(1)} %slice_add_fusion.11), channel_id=1, source_target_pairs={{0,24},{4,28},{8,16},{12,20},{16,8},{20,12},{24,0},{28,4},{1,25},{... | collective-permute-start | bytes 221192 | tf_op jit(solution)/shard_map/ppermute | solution.py:89
  99.7 1.1 collective-permute-start.29
  100.8 1.1 %collective-permute-start.26 = (f32[72,256]{1,0:T(8,128)S(1)}, f32[72,256]{1,0:T(8,128)S(1)}, u32[]{:S(2)}, u32[]{:S(2)}) collective-permute-start(f32[72,256]{1,0:T(8,128)S(1)} %slice_add_fusion.11), channel_id=1, source_target_pairs={{0,8},{4,12},{8,0},{12,4},{16,24},{20,28},{24,16},{28,20},{1,9},{5... | collective-permute-start | bytes 221192 | tf_op jit(solution)/shard_map/ppermute | solution.py:89
  101.9 0.2 collective-permute-done.23
  102.2 3.0 %collective-permute-done.26 = f32[72,256]{1,0:T(8,128)S(1)} collective-permute-done((f32[72,256]{1,0:T(8,128)S(1)}, f32[72,256]{1,0:T(8,128)S(1)}, u32[]{:S(2)}, u32[]{:S(2)}) %collective-permute-start.26) | collective-permute-done | bytes 73760 | tf_op jit(solution)/shard_map/ppermute | solution.py:89
  105.2 0.1 collective-permute-start.31
  105.3 0.5 collective-permute-start.33
  105.9 0.6 maximum_multiply_fusion
  106.5 1.1 collective-permute-done.33.refs_5_
  107.6 2.1 %place_blocks.1 = (f32[512,1024]{1,0:T(8,128)}, f32[64,1024]{1,0:T(8,128)}) custom-call(s32[4]{0:T(128)S(1)} %pad_add_fusion.info, f32[4,128,256]{2,1,0:T(8,128)S(1)} %pad_maximum_fusion.refs_0_, f32[4,128,256]{2,1,0:T(8,128)S(1)} %pad_maximum_fusion.1.refs_1_, f32[4,72,256]{2,1,0:T(8,128)S(1)} %pad_maximum_fusion.2.refs_2_, ...), custom_call_target="tpu_custom_call" | custom-call | tf_op jit(solution)/shard_map/place_blocks/pallas_call | solution.py:510
  (59 shorter events, 0.7 us)
Async XLA Ops:
  0.7 12.3 %copy-start.2 = (f32[512,1024]{1,0:T(8,128)S(1)}, f32[512,1024]{1,0:T(8,128)}, u32[]{:S(2)}) copy-start(f32[512,1024]{1,0:T(8,128)} %fine.3) | copy-start | bytes 6291460
  0.7 12.3 %copy-start.3 = (s32[2,4096]{1,0:T(2,128)S(1)}, s32[2,4096]{1,0:T(2,128)}, u32[]{:S(2)}) copy-start(s32[2,4096]{1,0:T(2,128)} %assign.7) | copy-start | bytes 98308
  12.2 8.4 %collective-permute-start = (f32[4,264,256]{2,1,0:T(8,128)S(1)}, f32[4,264,256]{2,1,0:T(8,128)S(1)}, u32[]{:S(2)}, u32[]{:S(2)}) collective-permute-start(f32[4,264,256]{2,1,0:T(8,128)S(1)} %get-tuple-element.56), channel_id=1, source_target_pairs={{0,4},{4,0},{8,12},{12,8},{16,20},{20,16},{24,28},{28,24},{1,5},{5... | collective-permute-start | bytes 3244040 | tf_op jit(solution)/shard_map/ppermute | solution.py:89
  20.7 15.3 %copy-start = (f32[64,1024]{1,0:T(8,128)S(1)}, f32[64,1024]{1,0:T(8,128)}, u32[]{:S(2)}) copy-start(f32[64,1024]{1,0:T(8,128)} %refs_5_.1) | copy-start | bytes 786436
  20.7 15.3 %copy-start.1 = (s32[512]{0:T(512)S(1)}, s32[512]{0:T(512)}, u32[]{:S(2)}) copy-start(s32[512]{0:T(512)} %param.9) | copy-start | bytes 6148
  20.7 6.9 %collective-permute-start.1 = (f32[2,136,256]{2,1,0:T(8,128)S(1)}, f32[2,136,256]{2,1,0:T(8,128)S(1)}, u32[]{:S(2)}, u32[]{:S(2)}) collective-permute-start(f32[2,136,256]{2,1,0:T(8,128)S(1)} %slice_add_fusion.1), channel_id=1, source_target_pairs={{0,8},{4,20},{8,0},{12,28},{16,24},{20,4},{24,16},{28,12},{1,9},{5... | collective-permute-start | bytes 835592 | tf_op jit(solution)/shard_map/ppermute | solution.py:94
  23.1 7.5 %collective-permute-start.2 = (f32[2,128,256]{2,1,0:T(8,128)S(1)}, f32[2,128,256]{2,1,0:T(8,128)S(1)}, u32[]{:S(2)}, u32[]{:S(2)}) collective-permute-start(f32[2,128,256]{2,1,0:T(8,128)S(1)} %slice_add_fusion.3), channel_id=1, source_target_pairs={{0,8},{4,20},{8,0},{12,28},{16,24},{20,4},{24,16},{28,12},{1,9},{5... | collective-permute-start | bytes 786440 | tf_op jit(solution)/shard_map/ppermute | solution.py:94
  27.7 8.3 %collective-permute-start.3 = (f32[136,256]{1,0:T(8,128)S(1)}, f32[136,256]{1,0:T(8,128)S(1)}, u32[]{:S(2)}, u32[]{:S(2)}) collective-permute-start(f32[136,256]{1,0:T(8,128)S(1)} %fusion.1), channel_id=1, source_target_pairs={{0,16},{4,12},{8,24},{12,4},{16,0},{20,28},{24,8},{28,20},{1,17},{... | collective-permute-start | bytes 417800 | tf_op jit(solution)/shard_map/ppermute | solution.py:99
  30.6 5.4 %collective-permute-start.4 = (f32[128,256]{1,0:T(8,128)S(1)}, f32[128,256]{1,0:T(8,128)S(1)}, u32[]{:S(2)}, u32[]{:S(2)}) collective-permute-start(f32[128,256]{1,0:T(8,128)S(1)} %fusion.4), channel_id=1, source_target_pairs={{0,16},{4,12},{8,24},{12,4},{16,0},{20,28},{24,8},{28,20},{1,17},{... | collective-permute-start | bytes 393224 | tf_op jit(solution)/shard_map/ppermute | solution.py:99
  37.1 6.2 %collective-permute-start.5 = (f32[128,256]{1,0:T(8,128)S(1)}, f32[128,256]{1,0:T(8,128)S(1)}, u32[]{:S(2)}, u32[]{:S(2)}) collective-permute-start(f32[128,256]{1,0:T(8,128)S(1)} %get-tuple-element.71), channel_id=1, source_target_pairs={{0,8},{4,12},{8,0},{12,4},{16,24},{20,28},{24,16},{28,20},{1,9},{5... | collective-permute-start | bytes 393224 | tf_op jit(solution)/shard_map/ppermute | solution.py:89
  39.2 6.4 %collective-permute-start.6 = (f32[128,256]{1,0:T(8,128)S(1)}, f32[128,256]{1,0:T(8,128)S(1)}, u32[]{:S(2)}, u32[]{:S(2)}) collective-permute-start(f32[128,256]{1,0:T(8,128)S(1)} %get-tuple-element.70), channel_id=1, source_target_pairs={{0,16},{4,20},{8,24},{12,28},{16,0},{20,4},{24,8},{28,12},{1,17},{... | collective-permute-start | bytes 393224 | tf_op jit(solution)/shard_map/ppermute | solution.py:89
  40.8 10.9 %collective-permute-start.10 = (f32[128,256]{1,0:T(8,128)S(1)}, f32[128,256]{1,0:T(8,128)S(1)}, u32[]{:S(2)}, u32[]{:S(2)}) collective-permute-start(f32[128,256]{1,0:T(8,128)S(1)} %get-tuple-element.71), channel_id=1, source_target_pairs={{0,16},{4,20},{8,24},{12,28},{16,0},{20,4},{24,8},{28,12},{1,17},{... | collective-permute-start | bytes 393224 | tf_op jit(solution)/shard_map/ppermute | solution.py:89
  41.4 10.3 %collective-permute-start.9 = (f32[128,256]{1,0:T(8,128)S(1)}, f32[128,256]{1,0:T(8,128)S(1)}, u32[]{:S(2)}, u32[]{:S(2)}) collective-permute-start(f32[128,256]{1,0:T(8,128)S(1)} %get-tuple-element.70), channel_id=1, source_target_pairs={{0,8},{4,12},{8,0},{12,4},{16,24},{20,28},{24,16},{28,20},{1,9},{5... | collective-permute-start | bytes 393224 | tf_op jit(solution)/shard_map/ppermute | solution.py:89
  43.3 8.3 %collective-permute-start.8 = (f32[128,256]{1,0:T(8,128)S(1)}, f32[128,256]{1,0:T(8,128)S(1)}, u32[]{:S(2)}, u32[]{:S(2)}) collective-permute-start(f32[128,256]{1,0:T(8,128)S(1)} %collective-permute-done.5.refs_0_), channel_id=1, source_target_pairs={{0,16},{4,20},{8,24},{12,28},{16,0},{20,4},{24,8},{28,12},{1,17},{... | collective-permute-start | bytes 393224 | tf_op jit(solution)/shard_map/ppermute | solution.py:89
  45.6 6.0 %collective-permute-start.7 = (f32[128,256]{1,0:T(8,128)S(1)}, f32[128,256]{1,0:T(8,128)S(1)}, u32[]{:S(2)}, u32[]{:S(2)}) collective-permute-start(f32[128,256]{1,0:T(8,128)S(1)} %collective-permute-done.6.refs_1_), channel_id=1, source_target_pairs={{0,8},{4,12},{8,0},{12,4},{16,24},{20,28},{24,16},{28,20},{1,9},{5... | collective-permute-start | bytes 393224 | tf_op jit(solution)/shard_map/ppermute | solution.py:89
  46.5 5.1 %collective-permute-start.11 = (f32[104,256]{1,0:T(8,128)S(1)}, f32[104,256]{1,0:T(8,128)S(1)}, u32[]{:S(2)}, u32[]{:S(2)}) collective-permute-start(f32[104,256]{1,0:T(8,128)S(1)} %pad_maximum_fusion.3), channel_id=1, source_target_pairs={{0,1},{1,0},{2,3},{3,2},{4,5},{5,4},{6,7},{7,6},{8,9},{9,8},{10,11... | collective-permute-start | bytes 319496 | tf_op jit(solution)/shard_map/ppermute | solution.py:89
  51.8 8.3 %collective-permute-start.12 = (f32[8,128,256]{2,1,0:T(8,128)S(1)}, f32[8,128,256]{2,1,0:T(8,128)S(1)}, u32[]{:S(2)}, u32[]{:S(2)}) collective-permute-start(f32[8,128,256]{2,1,0:T(8,128)S(1)} %bitcast_dynamic-update-slice_fusion.fine), channel_id=1, source_target_pairs={{0,4},{4,0},{8,12},{12,8},{16,20},{20,16},{24,28},{28,24},{1,5},{5... | collective-permute-start | bytes 3145736 | tf_op jit(solution)/shard_map/ppermute | solution.py:89
  59.4 8.6 %collective-permute-start.14 = (f32[4,264,256]{2,1,0:T(8,128)S(1)}, f32[4,264,256]{2,1,0:T(8,128)S(1)}, u32[]{:S(2)}, u32[]{:S(2)}) collective-permute-start(f32[4,264,256]{2,1,0:T(8,128)S(1)} %get-tuple-element.78), channel_id=1, source_target_pairs={{0,4},{4,0},{8,12},{12,8},{16,20},{20,16},{24,28},{28,24},{1,5},{5... | collective-permute-start | bytes 3244040 | tf_op jit(solution)/shard_map/ppermute | solution.py:89
  60.0 7.9 %collective-permute-start.13 = (f32[72,256]{1,0:T(8,128)S(1)}, f32[72,256]{1,0:T(8,128)S(1)}, u32[]{:S(2)}, u32[]{:S(2)}) collective-permute-start(f32[72,256]{1,0:T(8,128)S(1)} %slice_add_fusion.13), channel_id=1, source_target_pairs={{0,4},{4,0},{8,12},{12,8},{16,20},{20,16},{24,28},{28,24},{1,5},{5... | collective-permute-start | bytes 221192 | tf_op jit(solution)/shard_map/ppermute | solution.py:89
  68.1 10.1 %collective-permute-start.15 = (f32[2,136,256]{2,1,0:T(8,128)S(1)}, f32[2,136,256]{2,1,0:T(8,128)S(1)}, u32[]{:S(2)}, u32[]{:S(2)}) collective-permute-start(f32[2,136,256]{2,1,0:T(8,128)S(1)} %slice_add_fusion), channel_id=1, source_target_pairs={{0,8},{4,20},{8,0},{12,28},{16,24},{20,4},{24,16},{28,12},{1,9},{5... | collective-permute-start | bytes 835592 | tf_op jit(solution)/shard_map/ppermute | solution.py:94
  69.3 8.8 %collective-permute-start.16 = (f32[2,128,256]{2,1,0:T(8,128)S(1)}, f32[2,128,256]{2,1,0:T(8,128)S(1)}, u32[]{:S(2)}, u32[]{:S(2)}) collective-permute-start(f32[2,128,256]{2,1,0:T(8,128)S(1)} %slice_add_fusion.2), channel_id=1, source_target_pairs={{0,8},{4,20},{8,0},{12,28},{16,24},{20,4},{24,16},{28,12},{1,9},{5... | collective-permute-start | bytes 786440 | tf_op jit(solution)/shard_map/ppermute | solution.py:94
  70.2 8.0 %collective-permute-start.17 = (f32[104,256]{1,0:T(8,128)S(1)}, f32[104,256]{1,0:T(8,128)S(1)}, u32[]{:S(2)}, u32[]{:S(2)}) collective-permute-start(f32[104,256]{1,0:T(8,128)S(1)} %pad_maximum_fusion.4.refs_5_), channel_id=1, source_target_pairs={{0,2},{1,3},{2,0},{3,1},{4,6},{5,7},{6,4},{7,5},{8,10},{9,11},{10,... | collective-permute-start | bytes 319496 | tf_op jit(solution)/shard_map/ppermute | solution.py:89
  78.2 6.8 %collective-permute-start.18 = (f32[136,256]{1,0:T(8,128)S(1)}, f32[136,256]{1,0:T(8,128)S(1)}, u32[]{:S(2)}, u32[]{:S(2)}) collective-permute-start(f32[136,256]{1,0:T(8,128)S(1)} %fusion), channel_id=1, source_target_pairs={{0,16},{4,12},{8,24},{12,4},{16,0},{20,28},{24,8},{28,20},{1,17},{... | collective-permute-start | bytes 417800 | tf_op jit(solution)/shard_map/ppermute | solution.py:99
  79.8 5.2 %collective-permute-start.19 = (f32[128,256]{1,0:T(8,128)}, f32[128,256]{1,0:T(8,128)S(1)}, u32[]{:S(2)}, u32[]{:S(2)}) collective-permute-start(f32[128,256]{1,0:T(8,128)} %fusion.3), channel_id=1, source_target_pairs={{0,16},{4,12},{8,24},{12,4},{16,0},{20,28},{24,8},{28,20},{1,17},{... | collective-permute-start | bytes 393224 | tf_op jit(solution)/shard_map/ppermute | solution.py:99
  86.3 4.8 %collective-permute-start.24 = (f32[104,256]{1,0:T(8,128)S(1)}, f32[104,256]{1,0:T(8,128)S(1)}, u32[]{:S(2)}, u32[]{:S(2)}) collective-permute-start(f32[104,256]{1,0:T(8,128)S(1)} %pad_maximum_fusion.5), channel_id=1, source_target_pairs={{0,1},{1,0},{2,3},{3,2},{4,5},{5,4},{6,7},{7,6},{8,9},{9,8},{10,11... | collective-permute-start | bytes 319496 | tf_op jit(solution)/shard_map/ppermute | solution.py:89
  86.9 6.2 %collective-permute-start.20 = (f32[128,256]{1,0:T(8,128)S(1)}, f32[128,256]{1,0:T(8,128)S(1)}, u32[]{:S(2)}, u32[]{:S(2)}) collective-permute-start(f32[128,256]{1,0:T(8,128)S(1)} %get-tuple-element.97), channel_id=1, source_target_pairs={{0,8},{4,12},{8,0},{12,4},{16,24},{20,28},{24,16},{28,20},{1,9},{5... | collective-permute-start | bytes 393224 | tf_op jit(solution)/shard_map/ppermute | solution.py:89
  88.2 5.0 %collective-permute-start.21 = (f32[128,256]{1,0:T(8,128)S(1)}, f32[128,256]{1,0:T(8,128)S(1)}, u32[]{:S(2)}, u32[]{:S(2)}) collective-permute-start(f32[128,256]{1,0:T(8,128)S(1)} %get-tuple-element.96), channel_id=1, source_target_pairs={{0,16},{4,20},{8,24},{12,28},{16,0},{20,4},{24,8},{28,12},{1,17},{... | collective-permute-start | bytes 393224 | tf_op jit(solution)/shard_map/ppermute | solution.py:89
  91.1 6.8 %collective-permute-start.25 = (f32[104,256]{1,0:T(8,128)S(1)}, f32[104,256]{1,0:T(8,128)S(1)}, u32[]{:S(2)}, u32[]{:S(2)}) collective-permute-start(f32[104,256]{1,0:T(8,128)S(1)} %pad_maximum_fusion.6), channel_id=1, source_target_pairs={{0,2},{1,3},{2,0},{3,1},{4,6},{5,7},{6,4},{7,5},{8,10},{9,11},{10,... | collective-permute-start | bytes 319496 | tf_op jit(solution)/shard_map/ppermute | solution.py:89
  93.2 6.6 %collective-permute-start.27 = (f32[128,256]{1,0:T(8,128)S(1)}, f32[128,256]{1,0:T(8,128)S(1)}, u32[]{:S(2)}, u32[]{:S(2)}) collective-permute-start(f32[128,256]{1,0:T(8,128)S(1)} %get-tuple-element.96), channel_id=1, source_target_pairs={{0,8},{4,12},{8,0},{12,4},{16,24},{20,28},{24,16},{28,20},{1,9},{5... | collective-permute-start | bytes 393224 | tf_op jit(solution)/shard_map/ppermute | solution.py:89
  94.6 6.2 %collective-permute-start.28 = (f32[128,256]{1,0:T(8,128)S(1)}, f32[128,256]{1,0:T(8,128)S(1)}, u32[]{:S(2)}, u32[]{:S(2)}) collective-permute-start(f32[128,256]{1,0:T(8,128)S(1)} %get-tuple-element.97), channel_id=1, source_target_pairs={{0,16},{4,20},{8,24},{12,28},{16,0},{20,4},{24,8},{28,12},{1,17},{... | collective-permute-start | bytes 393224 | tf_op jit(solution)/shard_map/ppermute | solution.py:89
  95.6 6.6 %collective-permute-start.23 = (f32[128,256]{1,0:T(8,128)S(1)}, f32[128,256]{1,0:T(8,128)S(1)}, u32[]{:S(2)}, u32[]{:S(2)}) collective-permute-start(f32[128,256]{1,0:T(8,128)S(1)} %collective-permute-done.20), channel_id=1, source_target_pairs={{0,16},{4,20},{8,24},{12,28},{16,0},{20,4},{24,8},{28,12},{1,17},{... | collective-permute-start | bytes 393224 | tf_op jit(solution)/shard_map/ppermute | solution.py:89
  96.6 5.5 %collective-permute-start.22 = (f32[128,256]{1,0:T(8,128)S(1)}, f32[128,256]{1,0:T(8,128)S(1)}, u32[]{:S(2)}, u32[]{:S(2)}) collective-permute-start(f32[128,256]{1,0:T(8,128)S(1)} %collective-permute-done.21), channel_id=1, source_target_pairs={{0,8},{4,12},{8,0},{12,4},{16,24},{20,28},{24,16},{28,20},{1,9},{5... | collective-permute-start | bytes 393224 | tf_op jit(solution)/shard_map/ppermute | solution.py:89
  98.0 7.3 %collective-permute-start.30 = (f32[72,256]{1,0:T(8,128)S(1)}, f32[72,256]{1,0:T(8,128)S(1)}, u32[]{:S(2)}, u32[]{:S(2)}) collective-permute-start(f32[72,256]{1,0:T(8,128)S(1)} %slice_add_fusion.11), channel_id=1, source_target_pairs={{0,24},{4,28},{8,16},{12,20},{16,8},{20,12},{24,0},{28,4},{1,25},{... | collective-permute-start | bytes 221192 | tf_op jit(solution)/shard_map/ppermute | solution.py:89
  99.7 5.5 %collective-permute-start.29 = (f32[72,256]{1,0:T(8,128)S(1)}, f32[72,256]{1,0:T(8,128)S(1)}, u32[]{:S(2)}, u32[]{:S(2)}) collective-permute-start(f32[72,256]{1,0:T(8,128)S(1)} %slice_add_fusion.11), channel_id=1, source_target_pairs={{0,16},{4,20},{8,24},{12,28},{16,0},{20,4},{24,8},{28,12},{1,17},{... | collective-permute-start | bytes 221192 | tf_op jit(solution)/shard_map/ppermute | solution.py:89
  100.8 4.4 %collective-permute-start.26 = (f32[72,256]{1,0:T(8,128)S(1)}, f32[72,256]{1,0:T(8,128)S(1)}, u32[]{:S(2)}, u32[]{:S(2)}) collective-permute-start(f32[72,256]{1,0:T(8,128)S(1)} %slice_add_fusion.11), channel_id=1, source_target_pairs={{0,8},{4,12},{8,0},{12,4},{16,24},{20,28},{24,16},{28,20},{1,9},{5... | collective-permute-start | bytes 221192 | tf_op jit(solution)/shard_map/ppermute | solution.py:89
  102.2 5.4 %collective-permute-start.32 = (f32[4,128,256]{2,1,0:T(8,128)S(1)}, f32[4,128,256]{2,1,0:T(8,128)S(1)}, u32[]{:S(2)}, u32[]{:S(2)}) collective-permute-start(f32[4,128,256]{2,1,0:T(8,128)S(1)} %pad_maximum_fusion.1.refs_1_), channel_id=1, source_target_pairs={{0,4},{4,0},{8,12},{12,8},{16,20},{20,16},{24,28},{28,24},{1,5},{5... | collective-permute-start | bytes 1572872 | tf_op jit(solution)/shard_map/ppermute | solution.py:89
  105.2 2.4 %collective-permute-start.31 = (f32[4,128,256]{2,1,0:T(8,128)S(1)}, f32[4,128,256]{2,1,0:T(8,128)S(1)}, u32[]{:S(2)}, u32[]{:S(2)}) collective-permute-start(f32[4,128,256]{2,1,0:T(8,128)S(1)} %pad_maximum_fusion.refs_0_), channel_id=1, source_target_pairs={{0,4},{4,0},{8,12},{12,8},{16,20},{20,16},{24,28},{28,24},{1,5},{5... | collective-permute-start | bytes 1572872 | tf_op jit(solution)/shard_map/ppermute | solution.py:89
  105.3 2.3 %collective-permute-start.33 = (f32[4,72,256]{2,1,0:T(8,128)S(1)}, f32[4,72,256]{2,1,0:T(8,128)S(1)}, u32[]{:S(2)}, u32[]{:S(2)}) collective-permute-start(f32[4,72,256]{2,1,0:T(8,128)S(1)} %pad_maximum_fusion.2.refs_2_), channel_id=1, source_target_pairs={{0,4},{4,0},{8,12},{12,8},{16,20},{20,16},{24,28},{28,24},{1,5},{5... | collective-permute-start | bytes 884744 | tf_op jit(solution)/shard_map/ppermute | solution.py:89

commit v20 on v19

--- a/solution.py
+++ b/solution.py
@@ -423,11 +423,12 @@
     first = [swap_first(chunk) for chunk in first]
     if folded is not None:
         folded = swap(folded, lax.axis_size("cen") // 2, "cen")
-        first[1], folded = lax.optimization_barrier((first[1], folded))
     second = [
-        swap_second(held[2, rows] + sibling[2, rows] + arrived[1])
-        for rows, arrived in zip(chunks, first)
+        held[2, rows] + sibling[2, rows] + arrived[1] for rows, arrived in zip(chunks, first)
     ]
+    if folded is not None:
+        second[1], folded = lax.optimization_barrier((second[1], folded))
+    second = [swap_second(chunk) for chunk in second]
     return [*first, *second], folded
 
 

time: 110 us -> 110 us (level)
  waiting for transfers between devices: 26.4 us -> 24.4 us
  starting transfers between devices: 37.8 us -> 39.4 us
    ppermute x26, waiting for transfers between devices: 14.2 us -> 7.72 us  [swap(): return lax.ppermute(value, axis, [(i, i ^ bit) for i in range(size)])]
    ppermute x4, waiting for transfers between devices: 5.27 us -> 9.45 us  [swap_first(): return lax.ppermute(value, 'pts', pairs)]
    ppermute x26, starting transfers between devices: 26.6 us -> 28.5 us  [swap(): return lax.ppermute(value, axis, [(i, i ^ bit) for i in range(size)])]
  transfers between devices with their start and end apart: 34 -> 34, of which waited for: 12 -> 11; matrix products, arithmetic and copies ran while one was open for 2% -> 2% of each run, Pallas kernels for 24% -> 24%
where the time goes in v20:
time: 110 us
  Pallas kernels  42.4 us (39%)
  starting transfers between devices  39.4 us (36%)
  waiting for transfers between devices  24.4 us (22%)
  other arithmetic  1.85 us (2%)
  between operations  1.24 us (1%)
    pallas_call x4, Pallas kernels, run_pass(): pl.pallas_call(body, out_shape=out_shape, in_specs=[SCALARS, *in_specs],...  34.5 us
    ppermute x26, starting transfers between devices, swap(): return lax.ppermute(value, axis, [(i, i ^ bit) for i in range(size)])  28.5 us
    ppermute x4, waiting for transfers between devices, swap_first(): return lax.ppermute(value, 'pts', pairs)  9.45 us
    ppermute x26, waiting for transfers between devices, swap(): return lax.ppermute(value, axis, [(i, i ^ bit) for i in range(size)])  7.72 us
    ppermute x4, waiting for transfers between devices, swap_second(): return lax.ppermute(value, 'pts', pairs)  7.21 us
    ppermute x4, starting transfers between devices, swap_second(): return lax.ppermute(value, 'pts', pairs)  6.38 us
    ppermute x4, starting transfers between devices, swap_first(): return lax.ppermute(value, 'pts', pairs)  4.56 us
    pallas_call x1, Pallas kernels, fetch(): pl.pallas_call(fetch_body, out_shape=pltpu.VMEM(points.shape, points.dtyp...  3.47 us
  transfers between devices with their start and end apart: 34, of which 11 were waited for; matrix products, arithmetic and copies ran while one was open for 2% of the time, Pallas kernels for 24%

profile of v20, /device:TPU:0, one launch (start us, length us, event | category | flops | bytes accessed | tf_op | source)
XLA Modules:
  0.0 109.5 jit_solution(12712887669726655041)
XLA Ops:
  0.6 0.1 pad_add_fusion.info
  0.7 11.5 %energies_and_sums_00.1 = (f32[4,264,256]{2,1,0:T(8,128)S(1)}, f32[2,4096]{1,0:T(2,128)S(1)}, f32[1,4096]{1,0:T(1,128)S(1)}, bf16[4096,1024]{1,0:T(8,128)(2,1)S(1)}) custom-call(s32[4]{0:T(128)S(1)} %pad_add_fusion.info, bf16[4096,1024]{1,0:T(8,128)(2,1)} %points.3, s32[2,4096]{1,0:T(2,128)} %assign.7, f32[512,1024]{1,0:T(8,128)} %fine.3), custom_call_target="tpu_custom_call" | custom-call | flops 4294967296 | bytes 8388608 | tf_op jit(solution)/shard_map/energies_and_sums_00/pallas_call | solution.py:344
  12.2 0.8 collective-permute-start
  13.0 7.6 %energies_and_sums_01.1 = (f32[4,264,256]{2,1,0:T(8,128)S(1)}, f32[2,4096]{1,0:T(2,128)S(1)}) custom-call(s32[4]{0:T(128)S(1)} %pad_add_fusion.info, bf16[4096,1024]{1,0:T(8,128)(2,1)S(1)} %get-tuple-element.52.points, s32[2,4096]{1,0:T(2,128)S(1)} %copy-done.3, f32[512,1024]{1,0:T(8,128)S(1)} %copy-done.2, f32[1,4096]{1,0:T(1,128)S(1)} %get-tuple-element.53.refs_0_, ...), custom_call_target="tpu_custom_call" | custom-call | flops 4294967296 | bytes 8388608 | tf_op jit(solution)/shard_map/energies_and_sums_01/pallas_call | solution.py:344
  20.7 0.0 copy-start
  20.7 0.0 copy-start.1
  20.7 2.4 %collective-permute-start.1 = (f32[2,136,256]{2,1,0:T(8,128)S(1)}, f32[2,136,256]{2,1,0:T(8,128)S(1)}, u32[]{:S(2)}, u32[]{:S(2)}) collective-permute-start(f32[2,136,256]{2,1,0:T(8,128)S(1)} %slice_add_fusion.1), channel_id=1, source_target_pairs={{0,8},{4,20},{8,0},{12,28},{16,24},{20,4},{24,16},{28,12},{1,9},{5... | collective-permute-start | bytes 835592 | tf_op jit(solution)/shard_map/ppermute | solution.py:94
  23.1 0.1 collective-permute-start.2
  23.2 4.4 %collective-permute-done.1.refs_0_ = f32[2,136,256]{2,1,0:T(8,128)S(1)} collective-permute-done((f32[2,136,256]{2,1,0:T(8,128)S(1)}, f32[2,136,256]{2,1,0:T(8,128)S(1)}, u32[]{:S(2)}, u32[]{:S(2)}) %collective-permute-start.1) | collective-permute-done | bytes 278560 | tf_op jit(solution)/shard_map/ppermute | solution.py:94
  27.7 2.1 %collective-permute-start.3 = (f32[136,256]{1,0:T(8,128)S(1)}, f32[136,256]{1,0:T(8,128)S(1)}, u32[]{:S(2)}, u32[]{:S(2)}) collective-permute-start(f32[136,256]{1,0:T(8,128)S(1)} %fusion.1), channel_id=1, source_target_pairs={{0,16},{4,12},{8,24},{12,4},{16,0},{20,28},{24,8},{28,20},{1,17},{... | collective-permute-start | bytes 417800 | tf_op jit(solution)/shard_map/ppermute | solution.py:99
  29.8 0.8 collective-permute-done.2.refs_1_
  30.6 2.4 %collective-permute-start.4 = (f32[128,256]{1,0:T(8,128)S(1)}, f32[128,256]{1,0:T(8,128)S(1)}, u32[]{:S(2)}, u32[]{:S(2)}) collective-permute-start(f32[128,256]{1,0:T(8,128)S(1)} %fusion.3), channel_id=1, source_target_pairs={{0,16},{4,12},{8,24},{12,4},{16,0},{20,28},{24,8},{28,20},{1,17},{... | collective-permute-start | bytes 393224 | tf_op jit(solution)/shard_map/ppermute | solution.py:99
  33.1 2.9 %collective-permute-done.4.refs_3_ = f32[128,256]{1,0:T(8,128)S(1)} collective-permute-done((f32[128,256]{1,0:T(8,128)S(1)}, f32[128,256]{1,0:T(8,128)S(1)}, u32[]{:S(2)}, u32[]{:S(2)}) %collective-permute-start.4) | collective-permute-done | bytes 131104 | tf_op jit(solution)/shard_map/ppermute | solution.py:99
  36.0 0.0 collective-permute-done.3.refs_2_
  36.0 1.1 %refine_half.2 = (f32[128,256]{1,0:T(8,128)S(1)}, f32[128,256]{1,0:T(8,128)S(1)}, f32[72,256]{1,0:T(8,128)S(1)}) custom-call(s32[4]{0:T(128)S(1)} %pad_add_fusion.info, f32[4,264,256]{2,1,0:T(8,128)S(1)} %get-tuple-element.55.own, f32[4,264,256]{2,1,0:T(8,128)S(1)} %collective-permute-done.sibling, f32[2,136,256]{2,1,0:T(8,128)S(1)} %collective-permute-done.1.refs_0_, ...), custom_call_target="tpu_custom_call" | custom-call | tf_op jit(solution)/shard_map/refine_half/pallas_call | solution.py:408
  37.1 2.1 %collective-permute-start.5 = (f32[128,256]{1,0:T(8,128)S(1)}, f32[128,256]{1,0:T(8,128)S(1)}, u32[]{:S(2)}, u32[]{:S(2)}) collective-permute-start(f32[128,256]{1,0:T(8,128)S(1)} %get-tuple-element.71), channel_id=1, source_target_pairs={{0,8},{4,12},{8,0},{12,4},{16,24},{20,28},{24,16},{28,20},{1,9},{5... | collective-permute-start | bytes 393224 | tf_op jit(solution)/shard_map/ppermute | solution.py:89
  39.2 1.5 %collective-permute-start.6 = (f32[128,256]{1,0:T(8,128)S(1)}, f32[128,256]{1,0:T(8,128)S(1)}, u32[]{:S(2)}, u32[]{:S(2)}) collective-permute-start(f32[128,256]{1,0:T(8,128)S(1)} %get-tuple-element.70), channel_id=1, source_target_pairs={{0,16},{4,20},{8,24},{12,28},{16,0},{20,4},{24,8},{28,12},{1,17},{... | collective-permute-start | bytes 393224 | tf_op jit(solution)/shard_map/ppermute | solution.py:89
  40.8 0.6 collective-permute-start.10
  41.4 0.1 collective-permute-start.9
  41.4 1.9 %collective-permute-done.5.refs_0_ = f32[128,256]{1,0:T(8,128)S(1)} collective-permute-done((f32[128,256]{1,0:T(8,128)S(1)}, f32[128,256]{1,0:T(8,128)S(1)}, u32[]{:S(2)}, u32[]{:S(2)}) %collective-permute-start.5) | collective-permute-done | bytes 131104 | tf_op jit(solution)/shard_map/ppermute | solution.py:89
  43.3 2.3 %collective-permute-start.8 = (f32[128,256]{1,0:T(8,128)S(1)}, f32[128,256]{1,0:T(8,128)S(1)}, u32[]{:S(2)}, u32[]{:S(2)}) collective-permute-start(f32[128,256]{1,0:T(8,128)S(1)} %collective-permute-done.5.refs_0_), channel_id=1, source_target_pairs={{0,16},{4,20},{8,24},{12,28},{16,0},{20,4},{24,8},{28,12},{1,17},{... | collective-permute-start | bytes 393224 | tf_op jit(solution)/shard_map/ppermute | solution.py:89
  45.6 0.0 collective-permute-done.6.refs_1_
  45.6 0.9 collective-permute-start.7
  46.5 1.6 %collective-permute-start.11 = (f32[104,256]{1,0:T(8,128)S(1)}, f32[104,256]{1,0:T(8,128)S(1)}, u32[]{:S(2)}, u32[]{:S(2)}) collective-permute-start(f32[104,256]{1,0:T(8,128)S(1)} %pad_maximum_fusion.3), channel_id=1, source_target_pairs={{0,1},{1,0},{2,3},{3,2},{4,5},{5,4},{6,7},{7,6},{8,9},{9,8},{10,11... | collective-permute-start | bytes 319496 | tf_op jit(solution)/shard_map/ppermute | solution.py:89
  48.1 3.5 %fetch_points.1.points = bf16[4096,1024]{1,0:T(8,128)(2,1)S(1)} custom-call(bf16[4096,1024]{1,0:T(8,128)(2,1)} %points.3, f32[128,256]{1,0:T(8,128)S(1)} %collective-permute-done.5.refs_0_, f32[128,256]{1,0:T(8,128)S(1)} %collective-permute-done.6.refs_1_), custom_call_target="tpu_custom_call" | custom-call | bytes 16777216 | tf_op jit(solution)/shard_map/fetch_points/pallas_call | solution.py:283
  51.6 0.0 collective-permute-done.11
  51.6 0.0 collective-permute-done.9
  51.6 0.0 collective-permute-done.8
  51.8 0.1 collective-permute-start.12
  51.9 7.5 %energies_and_sums_10.1 = (f32[4,264,256]{2,1,0:T(8,128)S(1)}, f32[2,4096]{1,0:T(2,128)S(1)}) custom-call(s32[4]{0:T(128)S(1)} %pad_add_fusion.info, bf16[4096,1024]{1,0:T(8,128)(2,1)S(1)} %fetch_points.1.points, s32[2,4096]{1,0:T(2,128)S(1)} %copy-done.3, f32[8,128,256]{2,1,0:T(8,128)S(1)} %bitcast_dynamic-update-slice_fusion.fine, ...), custom_call_target="tpu_custom_call" | custom-call | flops 4294967296 | bytes 8388608 | tf_op jit(solution)/shard_map/energies_and_sums_10/pallas_call | solution.py:344
  59.4 0.6 collective-permute-start.14
  60.0 0.1 collective-permute-start.13
  60.1 7.8 %energies_and_sums_11.1 = (f32[4,264,256]{2,1,0:T(8,128)S(1)}, f32[2,4096]{1,0:T(2,128)S(1)}) custom-call(s32[4]{0:T(128)S(1)} %pad_add_fusion.info, bf16[4096,1024]{1,0:T(8,128)(2,1)S(1)} %fetch_points.1.points, s32[2,4096]{1,0:T(2,128)S(1)} %copy-done.3, f32[8,128,256]{2,1,0:T(8,128)S(1)} %collective-permute-done.12.fine, ...), custom_call_target="tpu_custom_call" | custom-call | flops 4294967296 | bytes 8388608 | tf_op jit(solution)/shard_map/energies_and_sums_11/pallas_call | solution.py:344
  68.0 0.0 collective-permute-done.13
  68.1 1.2 %collective-permute-start.15 = (f32[2,136,256]{2,1,0:T(8,128)S(1)}, f32[2,136,256]{2,1,0:T(8,128)S(1)}, u32[]{:S(2)}, u32[]{:S(2)}) collective-permute-start(f32[2,136,256]{2,1,0:T(8,128)S(1)} %slice_add_fusion), channel_id=1, source_target_pairs={{0,8},{4,20},{8,0},{12,28},{16,24},{20,4},{24,16},{28,12},{1,9},{5... | collective-permute-start | bytes 835592 | tf_op jit(solution)/shard_map/ppermute | solution.py:94
  69.3 0.9 collective-permute-start.16
  70.2 2.6 %collective-permute-start.18 = (f32[104,256]{1,0:T(8,128)S(1)}, f32[104,256]{1,0:T(8,128)S(1)}, u32[]{:S(2)}, u32[]{:S(2)}) collective-permute-start(f32[104,256]{1,0:T(8,128)S(1)} %pad_maximum_fusion.4.refs_5_), channel_id=1, source_target_pairs={{0,2},{1,3},{2,0},{3,1},{4,6},{5,7},{6,4},{7,5},{8,10},{9,11},{10,... | collective-permute-start | bytes 319496 | tf_op jit(solution)/shard_map/ppermute | solution.py:89
  72.8 1.9 %collective-permute-done.15.refs_0_ = f32[2,136,256]{2,1,0:T(8,128)S(1)} collective-permute-done((f32[2,136,256]{2,1,0:T(8,128)S(1)}, f32[2,136,256]{2,1,0:T(8,128)S(1)}, u32[]{:S(2)}, u32[]{:S(2)}) %collective-permute-start.15) | collective-permute-done | bytes 278560 | tf_op jit(solution)/shard_map/ppermute | solution.py:94
  74.7 1.0 collective-permute-start.17
  75.7 2.3 %collective-permute-done.16.refs_1_ = f32[2,128,256]{2,1,0:T(8,128)S(1)} collective-permute-done((f32[2,128,256]{2,1,0:T(8,128)S(1)}, f32[2,128,256]{2,1,0:T(8,128)S(1)}, u32[]{:S(2)}, u32[]{:S(2)}) %collective-permute-start.16) | collective-permute-done | bytes 262176 | tf_op jit(solution)/shard_map/ppermute | solution.py:94
  78.0 0.7 fusion.2
  78.6 0.9 collective-permute-start.19
  79.6 4.3 %collective-permute-done.19.refs_3_ = f32[128,256]{1,0:T(8,128)S(1)} collective-permute-done((f32[128,256]{1,0:T(8,128)}, f32[128,256]{1,0:T(8,128)S(1)}, u32[]{:S(2)}, u32[]{:S(2)}) %collective-permute-start.19) | collective-permute-done | bytes 131104 | tf_op jit(solution)/shard_map/ppermute | solution.py:99
  83.8 1.2 %refine_half.3 = (f32[128,256]{1,0:T(8,128)S(1)}, f32[128,256]{1,0:T(8,128)S(1)}, f32[72,256]{1,0:T(8,128)S(1)}) custom-call(s32[4]{0:T(128)S(1)} %pad_add_fusion.info, f32[4,264,256]{2,1,0:T(8,128)S(1)} %get-tuple-element.77.own, f32[4,264,256]{2,1,0:T(8,128)S(1)} %collective-permute-done.14.sibling, f32[2,136,256]{2,1,0:T(8,128)S(1)} %collective-permute-done.15.refs_0_, ...), custom_call_target="tpu_custom_call" | custom-call | tf_op jit(solution)/shard_map/refine_half/pallas_call | solution.py:408
  85.1 1.3 %collective-permute-start.24 = (f32[104,256]{1,0:T(8,128)S(1)}, f32[104,256]{1,0:T(8,128)S(1)}, u32[]{:S(2)}, u32[]{:S(2)}) collective-permute-start(f32[104,256]{1,0:T(8,128)S(1)} %pad_maximum_fusion.5), channel_id=1, source_target_pairs={{0,1},{1,0},{2,3},{3,2},{4,5},{5,4},{6,7},{7,6},{8,9},{9,8},{10,11... | collective-permute-start | bytes 319496 | tf_op jit(solution)/shard_map/ppermute | solution.py:89
  86.4 1.2 %collective-permute-start.20 = (f32[128,256]{1,0:T(8,128)S(1)}, f32[128,256]{1,0:T(8,128)S(1)}, u32[]{:S(2)}, u32[]{:S(2)}) collective-permute-start(f32[128,256]{1,0:T(8,128)S(1)} %get-tuple-element.97), channel_id=1, source_target_pairs={{0,8},{4,12},{8,0},{12,4},{16,24},{20,28},{24,16},{28,20},{1,9},{5... | collective-permute-start | bytes 393224 | tf_op jit(solution)/shard_map/ppermute | solution.py:89
  87.5 1.0 collective-permute-start.21
  88.5 1.3 %collective-permute-done.24 = f32[104,256]{1,0:T(8,128)S(1)} collective-permute-done((f32[104,256]{1,0:T(8,128)S(1)}, f32[104,256]{1,0:T(8,128)S(1)}, u32[]{:S(2)}, u32[]{:S(2)}) %collective-permute-start.24) | collective-permute-done | bytes 106528 | tf_op jit(solution)/shard_map/ppermute | solution.py:89
  89.9 3.6 %collective-permute-start.25 = (f32[104,256]{1,0:T(8,128)S(1)}, f32[104,256]{1,0:T(8,128)S(1)}, u32[]{:S(2)}, u32[]{:S(2)}) collective-permute-start(f32[104,256]{1,0:T(8,128)S(1)} %pad_maximum_fusion.6), channel_id=1, source_target_pairs={{0,2},{1,3},{2,0},{3,1},{4,6},{5,7},{6,4},{7,5},{8,10},{9,11},{10,... | collective-permute-start | bytes 319496 | tf_op jit(solution)/shard_map/ppermute | solution.py:89
  93.5 1.3 %collective-permute-start.27 = (f32[128,256]{1,0:T(8,128)S(1)}, f32[128,256]{1,0:T(8,128)S(1)}, u32[]{:S(2)}, u32[]{:S(2)}) collective-permute-start(f32[128,256]{1,0:T(8,128)S(1)} %get-tuple-element.96), channel_id=1, source_target_pairs={{0,8},{4,12},{8,0},{12,4},{16,24},{20,28},{24,16},{28,20},{1,9},{5... | collective-permute-start | bytes 393224 | tf_op jit(solution)/shard_map/ppermute | solution.py:89
  94.8 1.0 collective-permute-start.28
  95.8 1.0 collective-permute-start.23
  96.8 0.8 collective-permute-start.22
  97.7 1.7 %collective-permute-start.30 = (f32[72,256]{1,0:T(8,128)S(1)}, f32[72,256]{1,0:T(8,128)S(1)}, u32[]{:S(2)}, u32[]{:S(2)}) collective-permute-start(f32[72,256]{1,0:T(8,128)S(1)} %slice_add_fusion.12), channel_id=1, source_target_pairs={{0,24},{4,28},{8,16},{12,20},{16,8},{20,12},{24,0},{28,4},{1,25},{... | collective-permute-start | bytes 221192 | tf_op jit(solution)/shard_map/ppermute | solution.py:89
  99.4 1.0 collective-permute-start.29
  100.4 0.8 collective-permute-start.26
  101.3 0.1 collective-permute-start.32
  101.4 0.4 collective-permute-done.22
  101.8 3.0 %collective-permute-done.26 = f32[72,256]{1,0:T(8,128)S(1)} collective-permute-done((f32[72,256]{1,0:T(8,128)S(1)}, f32[72,256]{1,0:T(8,128)S(1)}, u32[]{:S(2)}, u32[]{:S(2)}) %collective-permute-start.26) | collective-permute-done | bytes 73760 | tf_op jit(solution)/shard_map/ppermute | solution.py:89
  104.8 0.1 collective-permute-start.31
  104.9 0.5 collective-permute-start.33
  105.5 0.6 maximum_multiply_fusion
  106.1 1.1 collective-permute-done.33.refs_5_
  107.2 2.1 %place_blocks.1 = (f32[512,1024]{1,0:T(8,128)}, f32[64,1024]{1,0:T(8,128)}) custom-call(s32[4]{0:T(128)S(1)} %pad_add_fusion.info, f32[4,128,256]{2,1,0:T(8,128)S(1)} %pad_maximum_fusion.refs_0_, f32[4,128,256]{2,1,0:T(8,128)S(1)} %pad_maximum_fusion.1.refs_1_, f32[4,72,256]{2,1,0:T(8,128)S(1)} %pad_maximum_fusion.2.refs_2_, ...), custom_call_target="tpu_custom_call" | custom-call | tf_op jit(solution)/shard_map/place_blocks/pallas_call | solution.py:511
  (59 shorter events, 0.7 us)
Async XLA Ops:
  0.7 12.3 %copy-start.2 = (f32[512,1024]{1,0:T(8,128)S(1)}, f32[512,1024]{1,0:T(8,128)}, u32[]{:S(2)}) copy-start(f32[512,1024]{1,0:T(8,128)} %fine.3) | copy-start | bytes 6291460
  0.7 12.3 %copy-start.3 = (s32[2,4096]{1,0:T(2,128)S(1)}, s32[2,4096]{1,0:T(2,128)}, u32[]{:S(2)}) copy-start(s32[2,4096]{1,0:T(2,128)} %assign.7) | copy-start | bytes 98308
  12.2 8.4 %collective-permute-start = (f32[4,264,256]{2,1,0:T(8,128)S(1)}, f32[4,264,256]{2,1,0:T(8,128)S(1)}, u32[]{:S(2)}, u32[]{:S(2)}) collective-permute-start(f32[4,264,256]{2,1,0:T(8,128)S(1)} %get-tuple-element.56), channel_id=1, source_target_pairs={{0,4},{4,0},{8,12},{12,8},{16,20},{20,16},{24,28},{28,24},{1,5},{5... | collective-permute-start | bytes 3244040 | tf_op jit(solution)/shard_map/ppermute | solution.py:89
  20.7 15.3 %copy-start = (f32[64,1024]{1,0:T(8,128)S(1)}, f32[64,1024]{1,0:T(8,128)}, u32[]{:S(2)}) copy-start(f32[64,1024]{1,0:T(8,128)} %refs_5_.1) | copy-start | bytes 786436
  20.7 15.3 %copy-start.1 = (s32[512]{0:T(512)S(1)}, s32[512]{0:T(512)}, u32[]{:S(2)}) copy-start(s32[512]{0:T(512)} %param.9) | copy-start | bytes 6148
  20.7 6.9 %collective-permute-start.1 = (f32[2,136,256]{2,1,0:T(8,128)S(1)}, f32[2,136,256]{2,1,0:T(8,128)S(1)}, u32[]{:S(2)}, u32[]{:S(2)}) collective-permute-start(f32[2,136,256]{2,1,0:T(8,128)S(1)} %slice_add_fusion.1), channel_id=1, source_target_pairs={{0,8},{4,20},{8,0},{12,28},{16,24},{20,4},{24,16},{28,12},{1,9},{5... | collective-permute-start | bytes 835592 | tf_op jit(solution)/shard_map/ppermute | solution.py:94
  23.1 7.5 %collective-permute-start.2 = (f32[2,128,256]{2,1,0:T(8,128)S(1)}, f32[2,128,256]{2,1,0:T(8,128)S(1)}, u32[]{:S(2)}, u32[]{:S(2)}) collective-permute-start(f32[2,128,256]{2,1,0:T(8,128)S(1)} %slice_add_fusion.3), channel_id=1, source_target_pairs={{0,8},{4,20},{8,0},{12,28},{16,24},{20,4},{24,16},{28,12},{1,9},{5... | collective-permute-start | bytes 786440 | tf_op jit(solution)/shard_map/ppermute | solution.py:94
  27.7 8.3 %collective-permute-start.3 = (f32[136,256]{1,0:T(8,128)S(1)}, f32[136,256]{1,0:T(8,128)S(1)}, u32[]{:S(2)}, u32[]{:S(2)}) collective-permute-start(f32[136,256]{1,0:T(8,128)S(1)} %fusion.1), channel_id=1, source_target_pairs={{0,16},{4,12},{8,24},{12,4},{16,0},{20,28},{24,8},{28,20},{1,17},{... | collective-permute-start | bytes 417800 | tf_op jit(solution)/shard_map/ppermute | solution.py:99
  30.6 5.4 %collective-permute-start.4 = (f32[128,256]{1,0:T(8,128)S(1)}, f32[128,256]{1,0:T(8,128)S(1)}, u32[]{:S(2)}, u32[]{:S(2)}) collective-permute-start(f32[128,256]{1,0:T(8,128)S(1)} %fusion.3), channel_id=1, source_target_pairs={{0,16},{4,12},{8,24},{12,4},{16,0},{20,28},{24,8},{28,20},{1,17},{... | collective-permute-start | bytes 393224 | tf_op jit(solution)/shard_map/ppermute | solution.py:99
  37.1 6.2 %collective-permute-start.5 = (f32[128,256]{1,0:T(8,128)S(1)}, f32[128,256]{1,0:T(8,128)S(1)}, u32[]{:S(2)}, u32[]{:S(2)}) collective-permute-start(f32[128,256]{1,0:T(8,128)S(1)} %get-tuple-element.71), channel_id=1, source_target_pairs={{0,8},{4,12},{8,0},{12,4},{16,24},{20,28},{24,16},{28,20},{1,9},{5... | collective-permute-start | bytes 393224 | tf_op jit(solution)/shard_map/ppermute | solution.py:89
  39.2 6.4 %collective-permute-start.6 = (f32[128,256]{1,0:T(8,128)S(1)}, f32[128,256]{1,0:T(8,128)S(1)}, u32[]{:S(2)}, u32[]{:S(2)}) collective-permute-start(f32[128,256]{1,0:T(8,128)S(1)} %get-tuple-element.70), channel_id=1, source_target_pairs={{0,16},{4,20},{8,24},{12,28},{16,0},{20,4},{24,8},{28,12},{1,17},{... | collective-permute-start | bytes 393224 | tf_op jit(solution)/shard_map/ppermute | solution.py:89
  40.8 10.9 %collective-permute-start.10 = (f32[128,256]{1,0:T(8,128)S(1)}, f32[128,256]{1,0:T(8,128)S(1)}, u32[]{:S(2)}, u32[]{:S(2)}) collective-permute-start(f32[128,256]{1,0:T(8,128)S(1)} %get-tuple-element.71), channel_id=1, source_target_pairs={{0,16},{4,20},{8,24},{12,28},{16,0},{20,4},{24,8},{28,12},{1,17},{... | collective-permute-start | bytes 393224 | tf_op jit(solution)/shard_map/ppermute | solution.py:89
  41.4 10.3 %collective-permute-start.9 = (f32[128,256]{1,0:T(8,128)S(1)}, f32[128,256]{1,0:T(8,128)S(1)}, u32[]{:S(2)}, u32[]{:S(2)}) collective-permute-start(f32[128,256]{1,0:T(8,128)S(1)} %get-tuple-element.70), channel_id=1, source_target_pairs={{0,8},{4,12},{8,0},{12,4},{16,24},{20,28},{24,16},{28,20},{1,9},{5... | collective-permute-start | bytes 393224 | tf_op jit(solution)/shard_map/ppermute | solution.py:89
  43.3 8.3 %collective-permute-start.8 = (f32[128,256]{1,0:T(8,128)S(1)}, f32[128,256]{1,0:T(8,128)S(1)}, u32[]{:S(2)}, u32[]{:S(2)}) collective-permute-start(f32[128,256]{1,0:T(8,128)S(1)} %collective-permute-done.5.refs_0_), channel_id=1, source_target_pairs={{0,16},{4,20},{8,24},{12,28},{16,0},{20,4},{24,8},{28,12},{1,17},{... | collective-permute-start | bytes 393224 | tf_op jit(solution)/shard_map/ppermute | solution.py:89
  45.6 6.0 %collective-permute-start.7 = (f32[128,256]{1,0:T(8,128)S(1)}, f32[128,256]{1,0:T(8,128)S(1)}, u32[]{:S(2)}, u32[]{:S(2)}) collective-permute-start(f32[128,256]{1,0:T(8,128)S(1)} %collective-permute-done.6.refs_1_), channel_id=1, source_target_pairs={{0,8},{4,12},{8,0},{12,4},{16,24},{20,28},{24,16},{28,20},{1,9},{5... | collective-permute-start | bytes 393224 | tf_op jit(solution)/shard_map/ppermute | solution.py:89
  46.5 5.1 %collective-permute-start.11 = (f32[104,256]{1,0:T(8,128)S(1)}, f32[104,256]{1,0:T(8,128)S(1)}, u32[]{:S(2)}, u32[]{:S(2)}) collective-permute-start(f32[104,256]{1,0:T(8,128)S(1)} %pad_maximum_fusion.3), channel_id=1, source_target_pairs={{0,1},{1,0},{2,3},{3,2},{4,5},{5,4},{6,7},{7,6},{8,9},{9,8},{10,11... | collective-permute-start | bytes 319496 | tf_op jit(solution)/shard_map/ppermute | solution.py:89
  51.8 8.3 %collective-permute-start.12 = (f32[8,128,256]{2,1,0:T(8,128)S(1)}, f32[8,128,256]{2,1,0:T(8,128)S(1)}, u32[]{:S(2)}, u32[]{:S(2)}) collective-permute-start(f32[8,128,256]{2,1,0:T(8,128)S(1)} %bitcast_dynamic-update-slice_fusion.fine), channel_id=1, source_target_pairs={{0,4},{4,0},{8,12},{12,8},{16,20},{20,16},{24,28},{28,24},{1,5},{5... | collective-permute-start | bytes 3145736 | tf_op jit(solution)/shard_map/ppermute | solution.py:89
  59.4 8.6 %collective-permute-start.14 = (f32[4,264,256]{2,1,0:T(8,128)S(1)}, f32[4,264,256]{2,1,0:T(8,128)S(1)}, u32[]{:S(2)}, u32[]{:S(2)}) collective-permute-start(f32[4,264,256]{2,1,0:T(8,128)S(1)} %get-tuple-element.78), channel_id=1, source_target_pairs={{0,4},{4,0},{8,12},{12,8},{16,20},{20,16},{24,28},{28,24},{1,5},{5... | collective-permute-start | bytes 3244040 | tf_op jit(solution)/shard_map/ppermute | solution.py:89
  60.0 7.9 %collective-permute-start.13 = (f32[72,256]{1,0:T(8,128)S(1)}, f32[72,256]{1,0:T(8,128)S(1)}, u32[]{:S(2)}, u32[]{:S(2)}) collective-permute-start(f32[72,256]{1,0:T(8,128)S(1)} %slice_add_fusion.14), channel_id=1, source_target_pairs={{0,4},{4,0},{8,12},{12,8},{16,20},{20,16},{24,28},{28,24},{1,5},{5... | collective-permute-start | bytes 221192 | tf_op jit(solution)/shard_map/ppermute | solution.py:89
  68.1 6.6 %collective-permute-start.15 = (f32[2,136,256]{2,1,0:T(8,128)S(1)}, f32[2,136,256]{2,1,0:T(8,128)S(1)}, u32[]{:S(2)}, u32[]{:S(2)}) collective-permute-start(f32[2,136,256]{2,1,0:T(8,128)S(1)} %slice_add_fusion), channel_id=1, source_target_pairs={{0,8},{4,20},{8,0},{12,28},{16,24},{20,4},{24,16},{28,12},{1,9},{5... | collective-permute-start | bytes 835592 | tf_op jit(solution)/shard_map/ppermute | solution.py:94
  69.3 8.6 %collective-permute-start.16 = (f32[2,128,256]{2,1,0:T(8,128)S(1)}, f32[2,128,256]{2,1,0:T(8,128)S(1)}, u32[]{:S(2)}, u32[]{:S(2)}) collective-permute-start(f32[2,128,256]{2,1,0:T(8,128)S(1)} %slice_add_fusion.2), channel_id=1, source_target_pairs={{0,8},{4,20},{8,0},{12,28},{16,24},{20,4},{24,16},{28,12},{1,9},{5... | collective-permute-start | bytes 786440 | tf_op jit(solution)/shard_map/ppermute | solution.py:94
  70.2 8.5 %collective-permute-start.18 = (f32[104,256]{1,0:T(8,128)S(1)}, f32[104,256]{1,0:T(8,128)S(1)}, u32[]{:S(2)}, u32[]{:S(2)}) collective-permute-start(f32[104,256]{1,0:T(8,128)S(1)} %pad_maximum_fusion.4.refs_5_), channel_id=1, source_target_pairs={{0,2},{1,3},{2,0},{3,1},{4,6},{5,7},{6,4},{7,5},{8,10},{9,11},{10,... | collective-permute-start | bytes 319496 | tf_op jit(solution)/shard_map/ppermute | solution.py:89
  74.7 9.1 %collective-permute-start.17 = (f32[136,256]{1,0:T(8,128)S(1)}, f32[136,256]{1,0:T(8,128)S(1)}, u32[]{:S(2)}, u32[]{:S(2)}) collective-permute-start(f32[136,256]{1,0:T(8,128)S(1)} %fusion), channel_id=1, source_target_pairs={{0,16},{4,12},{8,24},{12,4},{16,0},{20,28},{24,8},{28,20},{1,17},{... | collective-permute-start | bytes 417800 | tf_op jit(solution)/shard_map/ppermute | solution.py:99
  78.6 5.2 %collective-permute-start.19 = (f32[128,256]{1,0:T(8,128)}, f32[128,256]{1,0:T(8,128)S(1)}, u32[]{:S(2)}, u32[]{:S(2)}) collective-permute-start(f32[128,256]{1,0:T(8,128)} %fusion.2), channel_id=1, source_target_pairs={{0,16},{4,12},{8,24},{12,4},{16,0},{20,28},{24,8},{28,20},{1,17},{... | collective-permute-start | bytes 393224 | tf_op jit(solution)/shard_map/ppermute | solution.py:99
  85.1 4.8 %collective-permute-start.24 = (f32[104,256]{1,0:T(8,128)S(1)}, f32[104,256]{1,0:T(8,128)S(1)}, u32[]{:S(2)}, u32[]{:S(2)}) collective-permute-start(f32[104,256]{1,0:T(8,128)S(1)} %pad_maximum_fusion.5), channel_id=1, source_target_pairs={{0,1},{1,0},{2,3},{3,2},{4,5},{5,4},{6,7},{7,6},{8,9},{9,8},{10,11... | collective-permute-start | bytes 319496 | tf_op jit(solution)/shard_map/ppermute | solution.py:89
  86.4 7.1 %collective-permute-start.20 = (f32[128,256]{1,0:T(8,128)S(1)}, f32[128,256]{1,0:T(8,128)S(1)}, u32[]{:S(2)}, u32[]{:S(2)}) collective-permute-start(f32[128,256]{1,0:T(8,128)S(1)} %get-tuple-element.97), channel_id=1, source_target_pairs={{0,8},{4,12},{8,0},{12,4},{16,24},{20,28},{24,16},{28,20},{1,9},{5... | collective-permute-start | bytes 393224 | tf_op jit(solution)/shard_map/ppermute | solution.py:89
  87.5 5.9 %collective-permute-start.21 = (f32[128,256]{1,0:T(8,128)S(1)}, f32[128,256]{1,0:T(8,128)S(1)}, u32[]{:S(2)}, u32[]{:S(2)}) collective-permute-start(f32[128,256]{1,0:T(8,128)S(1)} %get-tuple-element.96), channel_id=1, source_target_pairs={{0,16},{4,20},{8,24},{12,28},{16,0},{20,4},{24,8},{28,12},{1,17},{... | collective-permute-start | bytes 393224 | tf_op jit(solution)/shard_map/ppermute | solution.py:89
  89.9 7.7 %collective-permute-start.25 = (f32[104,256]{1,0:T(8,128)S(1)}, f32[104,256]{1,0:T(8,128)S(1)}, u32[]{:S(2)}, u32[]{:S(2)}) collective-permute-start(f32[104,256]{1,0:T(8,128)S(1)} %pad_maximum_fusion.6), channel_id=1, source_target_pairs={{0,2},{1,3},{2,0},{3,1},{4,6},{5,7},{6,4},{7,5},{8,10},{9,11},{10,... | collective-permute-start | bytes 319496 | tf_op jit(solution)/shard_map/ppermute | solution.py:89
  93.5 5.9 %collective-permute-start.27 = (f32[128,256]{1,0:T(8,128)S(1)}, f32[128,256]{1,0:T(8,128)S(1)}, u32[]{:S(2)}, u32[]{:S(2)}) collective-permute-start(f32[128,256]{1,0:T(8,128)S(1)} %get-tuple-element.96), channel_id=1, source_target_pairs={{0,8},{4,12},{8,0},{12,4},{16,24},{20,28},{24,16},{28,20},{1,9},{5... | collective-permute-start | bytes 393224 | tf_op jit(solution)/shard_map/ppermute | solution.py:89
  94.8 5.7 %collective-permute-start.28 = (f32[128,256]{1,0:T(8,128)S(1)}, f32[128,256]{1,0:T(8,128)S(1)}, u32[]{:S(2)}, u32[]{:S(2)}) collective-permute-start(f32[128,256]{1,0:T(8,128)S(1)} %get-tuple-element.97), channel_id=1, source_target_pairs={{0,16},{4,20},{8,24},{12,28},{16,0},{20,4},{24,8},{28,12},{1,17},{... | collective-permute-start | bytes 393224 | tf_op jit(solution)/shard_map/ppermute | solution.py:89
  95.8 5.5 %collective-permute-start.23 = (f32[128,256]{1,0:T(8,128)S(1)}, f32[128,256]{1,0:T(8,128)S(1)}, u32[]{:S(2)}, u32[]{:S(2)}) collective-permute-start(f32[128,256]{1,0:T(8,128)S(1)} %collective-permute-done.20), channel_id=1, source_target_pairs={{0,16},{4,20},{8,24},{12,28},{16,0},{20,4},{24,8},{28,12},{1,17},{... | collective-permute-start | bytes 393224 | tf_op jit(solution)/shard_map/ppermute | solution.py:89
  96.8 5.0 %collective-permute-start.22 = (f32[128,256]{1,0:T(8,128)S(1)}, f32[128,256]{1,0:T(8,128)S(1)}, u32[]{:S(2)}, u32[]{:S(2)}) collective-permute-start(f32[128,256]{1,0:T(8,128)S(1)} %collective-permute-done.21), channel_id=1, source_target_pairs={{0,8},{4,12},{8,0},{12,4},{16,24},{20,28},{24,16},{28,20},{1,9},{5... | collective-permute-start | bytes 393224 | tf_op jit(solution)/shard_map/ppermute | solution.py:89
  97.7 7.2 %collective-permute-start.30 = (f32[72,256]{1,0:T(8,128)S(1)}, f32[72,256]{1,0:T(8,128)S(1)}, u32[]{:S(2)}, u32[]{:S(2)}) collective-permute-start(f32[72,256]{1,0:T(8,128)S(1)} %slice_add_fusion.12), channel_id=1, source_target_pairs={{0,24},{4,28},{8,16},{12,20},{16,8},{20,12},{24,0},{28,4},{1,25},{... | collective-permute-start | bytes 221192 | tf_op jit(solution)/shard_map/ppermute | solution.py:89
  99.4 5.5 %collective-permute-start.29 = (f32[72,256]{1,0:T(8,128)S(1)}, f32[72,256]{1,0:T(8,128)S(1)}, u32[]{:S(2)}, u32[]{:S(2)}) collective-permute-start(f32[72,256]{1,0:T(8,128)S(1)} %slice_add_fusion.12), channel_id=1, source_target_pairs={{0,16},{4,20},{8,24},{12,28},{16,0},{20,4},{24,8},{28,12},{1,17},{... | collective-permute-start | bytes 221192 | tf_op jit(solution)/shard_map/ppermute | solution.py:89
  100.4 4.4 %collective-permute-start.26 = (f32[72,256]{1,0:T(8,128)S(1)}, f32[72,256]{1,0:T(8,128)S(1)}, u32[]{:S(2)}, u32[]{:S(2)}) collective-permute-start(f32[72,256]{1,0:T(8,128)S(1)} %slice_add_fusion.12), channel_id=1, source_target_pairs={{0,8},{4,12},{8,0},{12,4},{16,24},{20,28},{24,16},{28,20},{1,9},{5... | collective-permute-start | bytes 221192 | tf_op jit(solution)/shard_map/ppermute | solution.py:89
  101.3 5.9 %collective-permute-start.32 = (f32[4,128,256]{2,1,0:T(8,128)S(1)}, f32[4,128,256]{2,1,0:T(8,128)S(1)}, u32[]{:S(2)}, u32[]{:S(2)}) collective-permute-start(f32[4,128,256]{2,1,0:T(8,128)S(1)} %pad_maximum_fusion.1.refs_1_), channel_id=1, source_target_pairs={{0,4},{4,0},{8,12},{12,8},{16,20},{20,16},{24,28},{28,24},{1,5},{5... | collective-permute-start | bytes 1572872 | tf_op jit(solution)/shard_map/ppermute | solution.py:89
  104.8 2.4 %collective-permute-start.31 = (f32[4,128,256]{2,1,0:T(8,128)S(1)}, f32[4,128,256]{2,1,0:T(8,128)S(1)}, u32[]{:S(2)}, u32[]{:S(2)}) collective-permute-start(f32[4,128,256]{2,1,0:T(8,128)S(1)} %pad_maximum_fusion.refs_0_), channel_id=1, source_target_pairs={{0,4},{4,0},{8,12},{12,8},{16,20},{20,16},{24,28},{28,24},{1,5},{5... | collective-permute-start | bytes 1572872 | tf_op jit(solution)/shard_map/ppermute | solution.py:89
  104.9 2.3 %collective-permute-start.33 = (f32[4,72,256]{2,1,0:T(8,128)S(1)}, f32[4,72,256]{2,1,0:T(8,128)S(1)}, u32[]{:S(2)}, u32[]{:S(2)}) collective-permute-start(f32[4,72,256]{2,1,0:T(8,128)S(1)} %pad_maximum_fusion.2.refs_2_), channel_id=1, source_target_pairs={{0,4},{4,0},{8,12},{12,8},{16,20},{20,16},{24,28},{28,24},{1,5},{5... | collective-permute-start | bytes 884744 | tf_op jit(solution)/shard_map/ppermute | solution.py:89

commit v21 on v20

--- a/solution.py
+++ b/solution.py
@@ -130,10 +130,10 @@
     payload, seen = refs.pop(0), refs.pop(0)
     squares_out = refs.pop(0) if first else None
     kept = refs.pop(0) if stream else points
-    low, norms, tallies, sums, even, odd, scaled = refs[:7]
-    chosen_in = refs[7] if stream else assign
-    small_sems, point_sems = refs[8:10] if stream else (None, None)
-    start = refs[10] if first else None
+    low, norms, tallies, sums, even, odd, scaled, places = refs[:8]
+    chosen_in = refs[8] if stream else assign
+    small_sems, point_sems = refs[9:11] if stream else (None, None)
+    start = refs[11] if first else None
     rows, width = low.shape
     mid = rows // 2
     block_width = width // SLOTS
@@ -187,6 +187,7 @@
     norms[...] = jnp.broadcast_to(norm, norms.shape)
     tallies[...] = jnp.zeros_like(tallies)
     sums[...] = jnp.zeros_like(sums)
+    places[...] = lax.broadcasted_iota(jnp.int32, places.shape, 0).astype(jnp.int16)
 
     def multiply(i, target):
         target[...] = lax.dot_general(
@@ -225,11 +226,13 @@
         for lane in range(0, width, 128):
             values = kept[span(i), lane : lane + 128].astype(jnp.float32)
             scaled[:, lane : lane + 128] = (values * factor).astype(jnp.bfloat16)
-        sums[...] += jnp.dot(
-            member.astype(jnp.float32).astype(jnp.bfloat16),
-            scaled[...],
-            preferred_element_type=jnp.float32,
-        )
+        narrow = jnp.where(inside, chosen, -1).astype(jnp.int16)
+        table = jnp.where(
+            jnp.concatenate([places[...]] * (tile // 128), axis=1) == narrow,
+            jnp.ones((rows, tile), jnp.bfloat16),
+            jnp.zeros((rows, tile), jnp.bfloat16),
+        )
+        sums[...] += jnp.dot(table, scaled[...], preferred_element_type=jnp.float32)
 
     def arrive(i):
         for half in range(2):
@@ -323,6 +326,7 @@
         pltpu.VMEM((rows, tile), jnp.float32),
         pltpu.VMEM((rows, tile), jnp.float32),
         pltpu.VMEM((tile, width), jnp.bfloat16),
+        pltpu.VMEM((rows, 128), jnp.int16),
     ]
     if stream:
         scratch += [

time: 110 us -> 109 us (level)
  no operation moved by 1% of the time
where the time goes in v21:
time: 109 us
  Pallas kernels  42 us (39%)
  starting transfers between devices  39.3 us (36%)
  waiting for transfers between devices  24.4 us (22%)
  other arithmetic  1.85 us (2%)
  between operations  1.24 us (1%)
    pallas_call x4, Pallas kernels, run_pass(): pl.pallas_call(body, out_shape=out_shape, in_specs=[SCALARS, *in_specs],...  34.1 us
    ppermute x26, starting transfers between devices, swap(): return lax.ppermute(value, axis, [(i, i ^ bit) for i in range(size)])  28.4 us
    ppermute x4, waiting for transfers between devices, swap_first(): return lax.ppermute(value, 'pts', pairs)  9.48 us
    ppermute x26, waiting for transfers between devices, swap(): return lax.ppermute(value, axis, [(i, i ^ bit) for i in range(size)])  7.7 us
    ppermute x4, waiting for transfers between devices, swap_second(): return lax.ppermute(value, 'pts', pairs)  7.23 us
    ppermute x4, starting transfers between devices, swap_second(): return lax.ppermute(value, 'pts', pairs)  6.34 us
    ppermute x4, starting transfers between devices, swap_first(): return lax.ppermute(value, 'pts', pairs)  4.55 us
    pallas_call x1, Pallas kernels, fetch(): pl.pallas_call(fetch_body, out_shape=pltpu.VMEM(points.shape, points.dtyp...  3.47 us
  transfers between devices with their start and end apart: 34, of which 11 were waited for; matrix products, arithmetic and copies ran while one was open for 2% of the time, Pallas kernels for 24%

profile of v21, /device:TPU:0, one launch (start us, length us, event | category | flops | bytes accessed | tf_op | source)
XLA Modules:
  0.0 109.1 jit_solution(15552725064799047949)
XLA Ops:
  0.6 0.1 pad_add_fusion.info
  0.7 11.4 %energies_and_sums_00.1 = (f32[4,264,256]{2,1,0:T(8,128)S(1)}, f32[2,4096]{1,0:T(2,128)S(1)}, f32[1,4096]{1,0:T(1,128)S(1)}, bf16[4096,1024]{1,0:T(8,128)(2,1)S(1)}) custom-call(s32[4]{0:T(128)S(1)} %pad_add_fusion.info, bf16[4096,1024]{1,0:T(8,128)(2,1)} %points.3, s32[2,4096]{1,0:T(2,128)} %assign.7, f32[512,1024]{1,0:T(8,128)} %fine.3), custom_call_target="tpu_custom_call" | custom-call | flops 4294967296 | bytes 8388608 | tf_op jit(solution)/shard_map/energies_and_sums_00/pallas_call | solution.py:348
  12.1 0.8 collective-permute-start
  12.9 7.5 %energies_and_sums_01.1 = (f32[4,264,256]{2,1,0:T(8,128)S(1)}, f32[2,4096]{1,0:T(2,128)S(1)}) custom-call(s32[4]{0:T(128)S(1)} %pad_add_fusion.info, bf16[4096,1024]{1,0:T(8,128)(2,1)S(1)} %get-tuple-element.52.points, s32[2,4096]{1,0:T(2,128)S(1)} %copy-done.3, f32[512,1024]{1,0:T(8,128)S(1)} %copy-done.2, f32[1,4096]{1,0:T(1,128)S(1)} %get-tuple-element.53.refs_0_, ...), custom_call_target="tpu_custom_call" | custom-call | flops 4294967296 | bytes 8388608 | tf_op jit(solution)/shard_map/energies_and_sums_01/pallas_call | solution.py:348
  20.5 0.0 copy-start
  20.5 0.0 copy-start.1
  20.6 2.4 %collective-permute-start.1 = (f32[2,136,256]{2,1,0:T(8,128)S(1)}, f32[2,136,256]{2,1,0:T(8,128)S(1)}, u32[]{:S(2)}, u32[]{:S(2)}) collective-permute-start(f32[2,136,256]{2,1,0:T(8,128)S(1)} %slice_add_fusion.1), channel_id=1, source_target_pairs={{0,8},{4,20},{8,0},{12,28},{16,24},{20,4},{24,16},{28,12},{1,9},{5... | collective-permute-start | bytes 835592 | tf_op jit(solution)/shard_map/ppermute | solution.py:94
  23.0 0.1 collective-permute-start.2
  23.0 4.4 %collective-permute-done.1.refs_0_ = f32[2,136,256]{2,1,0:T(8,128)S(1)} collective-permute-done((f32[2,136,256]{2,1,0:T(8,128)S(1)}, f32[2,136,256]{2,1,0:T(8,128)S(1)}, u32[]{:S(2)}, u32[]{:S(2)}) %collective-permute-start.1) | collective-permute-done | bytes 278560 | tf_op jit(solution)/shard_map/ppermute | solution.py:94
  27.5 2.1 %collective-permute-start.3 = (f32[136,256]{1,0:T(8,128)S(1)}, f32[136,256]{1,0:T(8,128)S(1)}, u32[]{:S(2)}, u32[]{:S(2)}) collective-permute-start(f32[136,256]{1,0:T(8,128)S(1)} %fusion.1), channel_id=1, source_target_pairs={{0,16},{4,12},{8,24},{12,4},{16,0},{20,28},{24,8},{28,20},{1,17},{... | collective-permute-start | bytes 417800 | tf_op jit(solution)/shard_map/ppermute | solution.py:99
  29.6 0.8 collective-permute-done.2.refs_1_
  30.5 2.4 %collective-permute-start.4 = (f32[128,256]{1,0:T(8,128)S(1)}, f32[128,256]{1,0:T(8,128)S(1)}, u32[]{:S(2)}, u32[]{:S(2)}) collective-permute-start(f32[128,256]{1,0:T(8,128)S(1)} %fusion.3), channel_id=1, source_target_pairs={{0,16},{4,12},{8,24},{12,4},{16,0},{20,28},{24,8},{28,20},{1,17},{... | collective-permute-start | bytes 393224 | tf_op jit(solution)/shard_map/ppermute | solution.py:99
  32.9 2.9 %collective-permute-done.4.refs_3_ = f32[128,256]{1,0:T(8,128)S(1)} collective-permute-done((f32[128,256]{1,0:T(8,128)S(1)}, f32[128,256]{1,0:T(8,128)S(1)}, u32[]{:S(2)}, u32[]{:S(2)}) %collective-permute-start.4) | collective-permute-done | bytes 131104 | tf_op jit(solution)/shard_map/ppermute | solution.py:99
  35.9 0.0 collective-permute-done.3.refs_2_
  35.9 1.1 %refine_half.2 = (f32[128,256]{1,0:T(8,128)S(1)}, f32[128,256]{1,0:T(8,128)S(1)}, f32[72,256]{1,0:T(8,128)S(1)}) custom-call(s32[4]{0:T(128)S(1)} %pad_add_fusion.info, f32[4,264,256]{2,1,0:T(8,128)S(1)} %get-tuple-element.55.own, f32[4,264,256]{2,1,0:T(8,128)S(1)} %collective-permute-done.sibling, f32[2,136,256]{2,1,0:T(8,128)S(1)} %collective-permute-done.1.refs_0_, ...), custom_call_target="tpu_custom_call" | custom-call | tf_op jit(solution)/shard_map/refine_half/pallas_call | solution.py:412
  37.0 2.1 %collective-permute-start.5 = (f32[128,256]{1,0:T(8,128)S(1)}, f32[128,256]{1,0:T(8,128)S(1)}, u32[]{:S(2)}, u32[]{:S(2)}) collective-permute-start(f32[128,256]{1,0:T(8,128)S(1)} %get-tuple-element.71), channel_id=1, source_target_pairs={{0,8},{4,12},{8,0},{12,4},{16,24},{20,28},{24,16},{28,20},{1,9},{5... | collective-permute-start | bytes 393224 | tf_op jit(solution)/shard_map/ppermute | solution.py:89
  39.1 1.5 %collective-permute-start.6 = (f32[128,256]{1,0:T(8,128)S(1)}, f32[128,256]{1,0:T(8,128)S(1)}, u32[]{:S(2)}, u32[]{:S(2)}) collective-permute-start(f32[128,256]{1,0:T(8,128)S(1)} %get-tuple-element.70), channel_id=1, source_target_pairs={{0,16},{4,20},{8,24},{12,28},{16,0},{20,4},{24,8},{28,12},{1,17},{... | collective-permute-start | bytes 393224 | tf_op jit(solution)/shard_map/ppermute | solution.py:89
  40.6 0.6 collective-permute-start.10
  41.2 0.1 collective-permute-start.9
  41.3 1.9 %collective-permute-done.5.refs_0_ = f32[128,256]{1,0:T(8,128)S(1)} collective-permute-done((f32[128,256]{1,0:T(8,128)S(1)}, f32[128,256]{1,0:T(8,128)S(1)}, u32[]{:S(2)}, u32[]{:S(2)}) %collective-permute-start.5) | collective-permute-done | bytes 131104 | tf_op jit(solution)/shard_map/ppermute | solution.py:89
  43.2 2.3 %collective-permute-start.8 = (f32[128,256]{1,0:T(8,128)S(1)}, f32[128,256]{1,0:T(8,128)S(1)}, u32[]{:S(2)}, u32[]{:S(2)}) collective-permute-start(f32[128,256]{1,0:T(8,128)S(1)} %collective-permute-done.5.refs_0_), channel_id=1, source_target_pairs={{0,16},{4,20},{8,24},{12,28},{16,0},{20,4},{24,8},{28,12},{1,17},{... | collective-permute-start | bytes 393224 | tf_op jit(solution)/shard_map/ppermute | solution.py:89
  45.5 0.9 collective-permute-start.7
  46.3 1.6 %collective-permute-start.11 = (f32[104,256]{1,0:T(8,128)S(1)}, f32[104,256]{1,0:T(8,128)S(1)}, u32[]{:S(2)}, u32[]{:S(2)}) collective-permute-start(f32[104,256]{1,0:T(8,128)S(1)} %pad_maximum_fusion.3), channel_id=1, source_target_pairs={{0,1},{1,0},{2,3},{3,2},{4,5},{5,4},{6,7},{7,6},{8,9},{9,8},{10,11... | collective-permute-start | bytes 319496 | tf_op jit(solution)/shard_map/ppermute | solution.py:89
  48.0 3.5 %fetch_points.1.points = bf16[4096,1024]{1,0:T(8,128)(2,1)S(1)} custom-call(bf16[4096,1024]{1,0:T(8,128)(2,1)} %points.3, f32[128,256]{1,0:T(8,128)S(1)} %collective-permute-done.5.refs_0_, f32[128,256]{1,0:T(8,128)S(1)} %collective-permute-done.6.refs_1_), custom_call_target="tpu_custom_call" | custom-call | bytes 16777216 | tf_op jit(solution)/shard_map/fetch_points/pallas_call | solution.py:286
  51.4 0.0 collective-permute-done.11
  51.5 0.0 collective-permute-done.9
  51.5 0.0 collective-permute-done.8
  51.7 0.1 collective-permute-start.12
  51.7 7.5 %energies_and_sums_10.1 = (f32[4,264,256]{2,1,0:T(8,128)S(1)}, f32[2,4096]{1,0:T(2,128)S(1)}) custom-call(s32[4]{0:T(128)S(1)} %pad_add_fusion.info, bf16[4096,1024]{1,0:T(8,128)(2,1)S(1)} %fetch_points.1.points, s32[2,4096]{1,0:T(2,128)S(1)} %copy-done.3, f32[8,128,256]{2,1,0:T(8,128)S(1)} %bitcast_dynamic-update-slice_fusion.fine, ...), custom_call_target="tpu_custom_call" | custom-call | flops 4294967296 | bytes 8388608 | tf_op jit(solution)/shard_map/energies_and_sums_10/pallas_call | solution.py:348
  59.2 0.6 collective-permute-start.14
  59.8 0.1 collective-permute-start.13
  59.9 0.0 collective-permute-done.12.fine
  59.9 7.7 %energies_and_sums_11.1 = (f32[4,264,256]{2,1,0:T(8,128)S(1)}, f32[2,4096]{1,0:T(2,128)S(1)}) custom-call(s32[4]{0:T(128)S(1)} %pad_add_fusion.info, bf16[4096,1024]{1,0:T(8,128)(2,1)S(1)} %fetch_points.1.points, s32[2,4096]{1,0:T(2,128)S(1)} %copy-done.3, f32[8,128,256]{2,1,0:T(8,128)S(1)} %collective-permute-done.12.fine, ...), custom_call_target="tpu_custom_call" | custom-call | flops 4294967296 | bytes 8388608 | tf_op jit(solution)/shard_map/energies_and_sums_11/pallas_call | solution.py:348
  67.7 0.0 collective-permute-done.14.sibling
  67.8 1.2 %collective-permute-start.15 = (f32[2,136,256]{2,1,0:T(8,128)S(1)}, f32[2,136,256]{2,1,0:T(8,128)S(1)}, u32[]{:S(2)}, u32[]{:S(2)}) collective-permute-start(f32[2,136,256]{2,1,0:T(8,128)S(1)} %slice_add_fusion), channel_id=1, source_target_pairs={{0,8},{4,20},{8,0},{12,28},{16,24},{20,4},{24,16},{28,12},{1,9},{5... | collective-permute-start | bytes 835592 | tf_op jit(solution)/shard_map/ppermute | solution.py:94
  69.0 0.9 collective-permute-start.16
  69.9 2.6 %collective-permute-start.18 = (f32[104,256]{1,0:T(8,128)S(1)}, f32[104,256]{1,0:T(8,128)S(1)}, u32[]{:S(2)}, u32[]{:S(2)}) collective-permute-start(f32[104,256]{1,0:T(8,128)S(1)} %pad_maximum_fusion.4.refs_5_), channel_id=1, source_target_pairs={{0,2},{1,3},{2,0},{3,1},{4,6},{5,7},{6,4},{7,5},{8,10},{9,11},{10,... | collective-permute-start | bytes 319496 | tf_op jit(solution)/shard_map/ppermute | solution.py:89
  72.4 1.9 %collective-permute-done.15.refs_0_ = f32[2,136,256]{2,1,0:T(8,128)S(1)} collective-permute-done((f32[2,136,256]{2,1,0:T(8,128)S(1)}, f32[2,136,256]{2,1,0:T(8,128)S(1)}, u32[]{:S(2)}, u32[]{:S(2)}) %collective-permute-start.15) | collective-permute-done | bytes 278560 | tf_op jit(solution)/shard_map/ppermute | solution.py:94
  74.4 0.9 collective-permute-start.17
  75.3 2.3 %collective-permute-done.16.refs_1_ = f32[2,128,256]{2,1,0:T(8,128)S(1)} collective-permute-done((f32[2,128,256]{2,1,0:T(8,128)S(1)}, f32[2,128,256]{2,1,0:T(8,128)S(1)}, u32[]{:S(2)}, u32[]{:S(2)}) %collective-permute-start.16) | collective-permute-done | bytes 262176 | tf_op jit(solution)/shard_map/ppermute | solution.py:94
  77.6 0.7 fusion.2
  78.3 0.9 collective-permute-start.19
  79.2 4.3 %collective-permute-done.19.refs_3_ = f32[128,256]{1,0:T(8,128)S(1)} collective-permute-done((f32[128,256]{1,0:T(8,128)}, f32[128,256]{1,0:T(8,128)S(1)}, u32[]{:S(2)}, u32[]{:S(2)}) %collective-permute-start.19) | collective-permute-done | bytes 131104 | tf_op jit(solution)/shard_map/ppermute | solution.py:99
  83.5 1.2 %refine_half.3 = (f32[128,256]{1,0:T(8,128)S(1)}, f32[128,256]{1,0:T(8,128)S(1)}, f32[72,256]{1,0:T(8,128)S(1)}) custom-call(s32[4]{0:T(128)S(1)} %pad_add_fusion.info, f32[4,264,256]{2,1,0:T(8,128)S(1)} %get-tuple-element.77.own, f32[4,264,256]{2,1,0:T(8,128)S(1)} %collective-permute-done.14.sibling, f32[2,136,256]{2,1,0:T(8,128)S(1)} %collective-permute-done.15.refs_0_, ...), custom_call_target="tpu_custom_call" | custom-call | tf_op jit(solution)/shard_map/refine_half/pallas_call | solution.py:412
  84.7 1.3 %collective-permute-start.24 = (f32[104,256]{1,0:T(8,128)S(1)}, f32[104,256]{1,0:T(8,128)S(1)}, u32[]{:S(2)}, u32[]{:S(2)}) collective-permute-start(f32[104,256]{1,0:T(8,128)S(1)} %pad_maximum_fusion.5), channel_id=1, source_target_pairs={{0,1},{1,0},{2,3},{3,2},{4,5},{5,4},{6,7},{7,6},{8,9},{9,8},{10,11... | collective-permute-start | bytes 319496 | tf_op jit(solution)/shard_map/ppermute | solution.py:89
  86.0 1.1 %collective-permute-start.20 = (f32[128,256]{1,0:T(8,128)S(1)}, f32[128,256]{1,0:T(8,128)S(1)}, u32[]{:S(2)}, u32[]{:S(2)}) collective-permute-start(f32[128,256]{1,0:T(8,128)S(1)} %get-tuple-element.97), channel_id=1, source_target_pairs={{0,8},{4,12},{8,0},{12,4},{16,24},{20,28},{24,16},{28,20},{1,9},{5... | collective-permute-start | bytes 393224 | tf_op jit(solution)/shard_map/ppermute | solution.py:89
  87.1 1.0 collective-permute-start.21
  88.2 1.3 %collective-permute-done.24 = f32[104,256]{1,0:T(8,128)S(1)} collective-permute-done((f32[104,256]{1,0:T(8,128)S(1)}, f32[104,256]{1,0:T(8,128)S(1)}, u32[]{:S(2)}, u32[]{:S(2)}) %collective-permute-start.24) | collective-permute-done | bytes 106528 | tf_op jit(solution)/shard_map/ppermute | solution.py:89
  89.5 3.5 %collective-permute-start.25 = (f32[104,256]{1,0:T(8,128)S(1)}, f32[104,256]{1,0:T(8,128)S(1)}, u32[]{:S(2)}, u32[]{:S(2)}) collective-permute-start(f32[104,256]{1,0:T(8,128)S(1)} %pad_maximum_fusion.6), channel_id=1, source_target_pairs={{0,2},{1,3},{2,0},{3,1},{4,6},{5,7},{6,4},{7,5},{8,10},{9,11},{10,... | collective-permute-start | bytes 319496 | tf_op jit(solution)/shard_map/ppermute | solution.py:89
  93.1 1.2 %collective-permute-start.27 = (f32[128,256]{1,0:T(8,128)S(1)}, f32[128,256]{1,0:T(8,128)S(1)}, u32[]{:S(2)}, u32[]{:S(2)}) collective-permute-start(f32[128,256]{1,0:T(8,128)S(1)} %get-tuple-element.96), channel_id=1, source_target_pairs={{0,8},{4,12},{8,0},{12,4},{16,24},{20,28},{24,16},{28,20},{1,9},{5... | collective-permute-start | bytes 393224 | tf_op jit(solution)/shard_map/ppermute | solution.py:89
  94.3 0.9 collective-permute-start.28
  95.3 1.1 %collective-permute-start.23 = (f32[128,256]{1,0:T(8,128)S(1)}, f32[128,256]{1,0:T(8,128)S(1)}, u32[]{:S(2)}, u32[]{:S(2)}) collective-permute-start(f32[128,256]{1,0:T(8,128)S(1)} %collective-permute-done.20), channel_id=1, source_target_pairs={{0,16},{4,20},{8,24},{12,28},{16,0},{20,4},{24,8},{28,12},{1,17},{... | collective-permute-start | bytes 393224 | tf_op jit(solution)/shard_map/ppermute | solution.py:89
  96.4 0.9 collective-permute-start.22
  97.3 1.6 %collective-permute-start.30 = (f32[72,256]{1,0:T(8,128)S(1)}, f32[72,256]{1,0:T(8,128)S(1)}, u32[]{:S(2)}, u32[]{:S(2)}) collective-permute-start(f32[72,256]{1,0:T(8,128)S(1)} %slice_add_fusion.12), channel_id=1, source_target_pairs={{0,24},{4,28},{8,16},{12,20},{16,8},{20,12},{24,0},{28,4},{1,25},{... | collective-permute-start | bytes 221192 | tf_op jit(solution)/shard_map/ppermute | solution.py:89
  98.9 1.1 %collective-permute-start.29 = (f32[72,256]{1,0:T(8,128)S(1)}, f32[72,256]{1,0:T(8,128)S(1)}, u32[]{:S(2)}, u32[]{:S(2)}) collective-permute-start(f32[72,256]{1,0:T(8,128)S(1)} %slice_add_fusion.12), channel_id=1, source_target_pairs={{0,16},{4,20},{8,24},{12,28},{16,0},{20,4},{24,8},{28,12},{1,17},{... | collective-permute-start | bytes 221192 | tf_op jit(solution)/shard_map/ppermute | solution.py:89
  100.0 0.9 collective-permute-start.26
  100.9 0.1 collective-permute-start.32
  101.0 0.3 collective-permute-done.22
  101.3 3.0 %collective-permute-done.26 = f32[72,256]{1,0:T(8,128)S(1)} collective-permute-done((f32[72,256]{1,0:T(8,128)S(1)}, f32[72,256]{1,0:T(8,128)S(1)}, u32[]{:S(2)}, u32[]{:S(2)}) %collective-permute-start.26) | collective-permute-done | bytes 73760 | tf_op jit(solution)/shard_map/ppermute | solution.py:89
  104.4 0.1 collective-permute-start.31
  104.5 0.5 collective-permute-start.33
  105.1 0.6 maximum_multiply_fusion
  105.7 1.1 collective-permute-done.33.refs_5_
  106.8 2.1 %place_blocks.1 = (f32[512,1024]{1,0:T(8,128)}, f32[64,1024]{1,0:T(8,128)}) custom-call(s32[4]{0:T(128)S(1)} %pad_add_fusion.info, f32[4,128,256]{2,1,0:T(8,128)S(1)} %pad_maximum_fusion.refs_0_, f32[4,128,256]{2,1,0:T(8,128)S(1)} %pad_maximum_fusion.1.refs_1_, f32[4,72,256]{2,1,0:T(8,128)S(1)} %pad_maximum_fusion.2.refs_2_, ...), custom_call_target="tpu_custom_call" | custom-call | tf_op jit(solution)/shard_map/place_blocks/pallas_call | solution.py:515
  (59 shorter events, 0.7 us)
Async XLA Ops:
  0.7 12.2 %copy-start.2 = (f32[512,1024]{1,0:T(8,128)S(1)}, f32[512,1024]{1,0:T(8,128)}, u32[]{:S(2)}) copy-start(f32[512,1024]{1,0:T(8,128)} %fine.3) | copy-start | bytes 6291460
  0.7 12.2 %copy-start.3 = (s32[2,4096]{1,0:T(2,128)S(1)}, s32[2,4096]{1,0:T(2,128)}, u32[]{:S(2)}) copy-start(s32[2,4096]{1,0:T(2,128)} %assign.7) | copy-start | bytes 98308
  12.1 8.3 %collective-permute-start = (f32[4,264,256]{2,1,0:T(8,128)S(1)}, f32[4,264,256]{2,1,0:T(8,128)S(1)}, u32[]{:S(2)}, u32[]{:S(2)}) collective-permute-start(f32[4,264,256]{2,1,0:T(8,128)S(1)} %get-tuple-element.56), channel_id=1, source_target_pairs={{0,4},{4,0},{8,12},{12,8},{16,20},{20,16},{24,28},{28,24},{1,5},{5... | collective-permute-start | bytes 3244040 | tf_op jit(solution)/shard_map/ppermute | solution.py:89
  20.5 15.4 %copy-start = (f32[64,1024]{1,0:T(8,128)S(1)}, f32[64,1024]{1,0:T(8,128)}, u32[]{:S(2)}) copy-start(f32[64,1024]{1,0:T(8,128)} %refs_5_.1) | copy-start | bytes 786436
  20.5 15.3 %copy-start.1 = (s32[512]{0:T(512)S(1)}, s32[512]{0:T(512)}, u32[]{:S(2)}) copy-start(s32[512]{0:T(512)} %param.9) | copy-start | bytes 6148
  20.6 6.9 %collective-permute-start.1 = (f32[2,136,256]{2,1,0:T(8,128)S(1)}, f32[2,136,256]{2,1,0:T(8,128)S(1)}, u32[]{:S(2)}, u32[]{:S(2)}) collective-permute-start(f32[2,136,256]{2,1,0:T(8,128)S(1)} %slice_add_fusion.1), channel_id=1, source_target_pairs={{0,8},{4,20},{8,0},{12,28},{16,24},{20,4},{24,16},{28,12},{1,9},{5... | collective-permute-start | bytes 835592 | tf_op jit(solution)/shard_map/ppermute | solution.py:94
  23.0 7.5 %collective-permute-start.2 = (f32[2,128,256]{2,1,0:T(8,128)S(1)}, f32[2,128,256]{2,1,0:T(8,128)S(1)}, u32[]{:S(2)}, u32[]{:S(2)}) collective-permute-start(f32[2,128,256]{2,1,0:T(8,128)S(1)} %slice_add_fusion.3), channel_id=1, source_target_pairs={{0,8},{4,20},{8,0},{12,28},{16,24},{20,4},{24,16},{28,12},{1,9},{5... | collective-permute-start | bytes 786440 | tf_op jit(solution)/shard_map/ppermute | solution.py:94
  27.5 8.3 %collective-permute-start.3 = (f32[136,256]{1,0:T(8,128)S(1)}, f32[136,256]{1,0:T(8,128)S(1)}, u32[]{:S(2)}, u32[]{:S(2)}) collective-permute-start(f32[136,256]{1,0:T(8,128)S(1)} %fusion.1), channel_id=1, source_target_pairs={{0,16},{4,12},{8,24},{12,4},{16,0},{20,28},{24,8},{28,20},{1,17},{... | collective-permute-start | bytes 417800 | tf_op jit(solution)/shard_map/ppermute | solution.py:99
  30.5 5.4 %collective-permute-start.4 = (f32[128,256]{1,0:T(8,128)S(1)}, f32[128,256]{1,0:T(8,128)S(1)}, u32[]{:S(2)}, u32[]{:S(2)}) collective-permute-start(f32[128,256]{1,0:T(8,128)S(1)} %fusion.3), channel_id=1, source_target_pairs={{0,16},{4,12},{8,24},{12,4},{16,0},{20,28},{24,8},{28,20},{1,17},{... | collective-permute-start | bytes 393224 | tf_op jit(solution)/shard_map/ppermute | solution.py:99
  37.0 6.2 %collective-permute-start.5 = (f32[128,256]{1,0:T(8,128)S(1)}, f32[128,256]{1,0:T(8,128)S(1)}, u32[]{:S(2)}, u32[]{:S(2)}) collective-permute-start(f32[128,256]{1,0:T(8,128)S(1)} %get-tuple-element.71), channel_id=1, source_target_pairs={{0,8},{4,12},{8,0},{12,4},{16,24},{20,28},{24,16},{28,20},{1,9},{5... | collective-permute-start | bytes 393224 | tf_op jit(solution)/shard_map/ppermute | solution.py:89
  39.1 6.4 %collective-permute-start.6 = (f32[128,256]{1,0:T(8,128)S(1)}, f32[128,256]{1,0:T(8,128)S(1)}, u32[]{:S(2)}, u32[]{:S(2)}) collective-permute-start(f32[128,256]{1,0:T(8,128)S(1)} %get-tuple-element.70), channel_id=1, source_target_pairs={{0,16},{4,20},{8,24},{12,28},{16,0},{20,4},{24,8},{28,12},{1,17},{... | collective-permute-start | bytes 393224 | tf_op jit(solution)/shard_map/ppermute | solution.py:89
  40.6 10.8 %collective-permute-start.10 = (f32[128,256]{1,0:T(8,128)S(1)}, f32[128,256]{1,0:T(8,128)S(1)}, u32[]{:S(2)}, u32[]{:S(2)}) collective-permute-start(f32[128,256]{1,0:T(8,128)S(1)} %get-tuple-element.71), channel_id=1, source_target_pairs={{0,16},{4,20},{8,24},{12,28},{16,0},{20,4},{24,8},{28,12},{1,17},{... | collective-permute-start | bytes 393224 | tf_op jit(solution)/shard_map/ppermute | solution.py:89
  41.2 10.3 %collective-permute-start.9 = (f32[128,256]{1,0:T(8,128)S(1)}, f32[128,256]{1,0:T(8,128)S(1)}, u32[]{:S(2)}, u32[]{:S(2)}) collective-permute-start(f32[128,256]{1,0:T(8,128)S(1)} %get-tuple-element.70), channel_id=1, source_target_pairs={{0,8},{4,12},{8,0},{12,4},{16,24},{20,28},{24,16},{28,20},{1,9},{5... | collective-permute-start | bytes 393224 | tf_op jit(solution)/shard_map/ppermute | solution.py:89
  43.2 8.3 %collective-permute-start.8 = (f32[128,256]{1,0:T(8,128)S(1)}, f32[128,256]{1,0:T(8,128)S(1)}, u32[]{:S(2)}, u32[]{:S(2)}) collective-permute-start(f32[128,256]{1,0:T(8,128)S(1)} %collective-permute-done.5.refs_0_), channel_id=1, source_target_pairs={{0,16},{4,20},{8,24},{12,28},{16,0},{20,4},{24,8},{28,12},{1,17},{... | collective-permute-start | bytes 393224 | tf_op jit(solution)/shard_map/ppermute | solution.py:89
  45.5 6.0 %collective-permute-start.7 = (f32[128,256]{1,0:T(8,128)S(1)}, f32[128,256]{1,0:T(8,128)S(1)}, u32[]{:S(2)}, u32[]{:S(2)}) collective-permute-start(f32[128,256]{1,0:T(8,128)S(1)} %collective-permute-done.6.refs_1_), channel_id=1, source_target_pairs={{0,8},{4,12},{8,0},{12,4},{16,24},{20,28},{24,16},{28,20},{1,9},{5... | collective-permute-start | bytes 393224 | tf_op jit(solution)/shard_map/ppermute | solution.py:89
  46.3 5.1 %collective-permute-start.11 = (f32[104,256]{1,0:T(8,128)S(1)}, f32[104,256]{1,0:T(8,128)S(1)}, u32[]{:S(2)}, u32[]{:S(2)}) collective-permute-start(f32[104,256]{1,0:T(8,128)S(1)} %pad_maximum_fusion.3), channel_id=1, source_target_pairs={{0,1},{1,0},{2,3},{3,2},{4,5},{5,4},{6,7},{7,6},{8,9},{9,8},{10,11... | collective-permute-start | bytes 319496 | tf_op jit(solution)/shard_map/ppermute | solution.py:89
  51.7 8.2 %collective-permute-start.12 = (f32[8,128,256]{2,1,0:T(8,128)S(1)}, f32[8,128,256]{2,1,0:T(8,128)S(1)}, u32[]{:S(2)}, u32[]{:S(2)}) collective-permute-start(f32[8,128,256]{2,1,0:T(8,128)S(1)} %bitcast_dynamic-update-slice_fusion.fine), channel_id=1, source_target_pairs={{0,4},{4,0},{8,12},{12,8},{16,20},{20,16},{24,28},{28,24},{1,5},{5... | collective-permute-start | bytes 3145736 | tf_op jit(solution)/shard_map/ppermute | solution.py:89
  59.2 8.4 %collective-permute-start.14 = (f32[4,264,256]{2,1,0:T(8,128)S(1)}, f32[4,264,256]{2,1,0:T(8,128)S(1)}, u32[]{:S(2)}, u32[]{:S(2)}) collective-permute-start(f32[4,264,256]{2,1,0:T(8,128)S(1)} %get-tuple-element.78), channel_id=1, source_target_pairs={{0,4},{4,0},{8,12},{12,8},{16,20},{20,16},{24,28},{28,24},{1,5},{5... | collective-permute-start | bytes 3244040 | tf_op jit(solution)/shard_map/ppermute | solution.py:89
  59.8 7.8 %collective-permute-start.13 = (f32[72,256]{1,0:T(8,128)S(1)}, f32[72,256]{1,0:T(8,128)S(1)}, u32[]{:S(2)}, u32[]{:S(2)}) collective-permute-start(f32[72,256]{1,0:T(8,128)S(1)} %slice_add_fusion.14), channel_id=1, source_target_pairs={{0,4},{4,0},{8,12},{12,8},{16,20},{20,16},{24,28},{28,24},{1,5},{5... | collective-permute-start | bytes 221192 | tf_op jit(solution)/shard_map/ppermute | solution.py:89
  67.8 6.6 %collective-permute-start.15 = (f32[2,136,256]{2,1,0:T(8,128)S(1)}, f32[2,136,256]{2,1,0:T(8,128)S(1)}, u32[]{:S(2)}, u32[]{:S(2)}) collective-permute-start(f32[2,136,256]{2,1,0:T(8,128)S(1)} %slice_add_fusion), channel_id=1, source_target_pairs={{0,8},{4,20},{8,0},{12,28},{16,24},{20,4},{24,16},{28,12},{1,9},{5... | collective-permute-start | bytes 835592 | tf_op jit(solution)/shard_map/ppermute | solution.py:94
  69.0 8.6 %collective-permute-start.16 = (f32[2,128,256]{2,1,0:T(8,128)S(1)}, f32[2,128,256]{2,1,0:T(8,128)S(1)}, u32[]{:S(2)}, u32[]{:S(2)}) collective-permute-start(f32[2,128,256]{2,1,0:T(8,128)S(1)} %slice_add_fusion.2), channel_id=1, source_target_pairs={{0,8},{4,20},{8,0},{12,28},{16,24},{20,4},{24,16},{28,12},{1,9},{5... | collective-permute-start | bytes 786440 | tf_op jit(solution)/shard_map/ppermute | solution.py:94
  69.9 8.4 %collective-permute-start.18 = (f32[104,256]{1,0:T(8,128)S(1)}, f32[104,256]{1,0:T(8,128)S(1)}, u32[]{:S(2)}, u32[]{:S(2)}) collective-permute-start(f32[104,256]{1,0:T(8,128)S(1)} %pad_maximum_fusion.4.refs_5_), channel_id=1, source_target_pairs={{0,2},{1,3},{2,0},{3,1},{4,6},{5,7},{6,4},{7,5},{8,10},{9,11},{10,... | collective-permute-start | bytes 319496 | tf_op jit(solution)/shard_map/ppermute | solution.py:89
  74.4 9.1 %collective-permute-start.17 = (f32[136,256]{1,0:T(8,128)S(1)}, f32[136,256]{1,0:T(8,128)S(1)}, u32[]{:S(2)}, u32[]{:S(2)}) collective-permute-start(f32[136,256]{1,0:T(8,128)S(1)} %fusion), channel_id=1, source_target_pairs={{0,16},{4,12},{8,24},{12,4},{16,0},{20,28},{24,8},{28,20},{1,17},{... | collective-permute-start | bytes 417800 | tf_op jit(solution)/shard_map/ppermute | solution.py:99
  78.3 5.2 %collective-permute-start.19 = (f32[128,256]{1,0:T(8,128)}, f32[128,256]{1,0:T(8,128)S(1)}, u32[]{:S(2)}, u32[]{:S(2)}) collective-permute-start(f32[128,256]{1,0:T(8,128)} %fusion.2), channel_id=1, source_target_pairs={{0,16},{4,12},{8,24},{12,4},{16,0},{20,28},{24,8},{28,20},{1,17},{... | collective-permute-start | bytes 393224 | tf_op jit(solution)/shard_map/ppermute | solution.py:99
  84.7 4.8 %collective-permute-start.24 = (f32[104,256]{1,0:T(8,128)S(1)}, f32[104,256]{1,0:T(8,128)S(1)}, u32[]{:S(2)}, u32[]{:S(2)}) collective-permute-start(f32[104,256]{1,0:T(8,128)S(1)} %pad_maximum_fusion.5), channel_id=1, source_target_pairs={{0,1},{1,0},{2,3},{3,2},{4,5},{5,4},{6,7},{7,6},{8,9},{9,8},{10,11... | collective-permute-start | bytes 319496 | tf_op jit(solution)/shard_map/ppermute | solution.py:89
  86.0 7.1 %collective-permute-start.20 = (f32[128,256]{1,0:T(8,128)S(1)}, f32[128,256]{1,0:T(8,128)S(1)}, u32[]{:S(2)}, u32[]{:S(2)}) collective-permute-start(f32[128,256]{1,0:T(8,128)S(1)} %get-tuple-element.97), channel_id=1, source_target_pairs={{0,8},{4,12},{8,0},{12,4},{16,24},{20,28},{24,16},{28,20},{1,9},{5... | collective-permute-start | bytes 393224 | tf_op jit(solution)/shard_map/ppermute | solution.py:89
  87.1 6.0 %collective-permute-start.21 = (f32[128,256]{1,0:T(8,128)S(1)}, f32[128,256]{1,0:T(8,128)S(1)}, u32[]{:S(2)}, u32[]{:S(2)}) collective-permute-start(f32[128,256]{1,0:T(8,128)S(1)} %get-tuple-element.96), channel_id=1, source_target_pairs={{0,16},{4,20},{8,24},{12,28},{16,0},{20,4},{24,8},{28,12},{1,17},{... | collective-permute-start | bytes 393224 | tf_op jit(solution)/shard_map/ppermute | solution.py:89
  89.5 7.7 %collective-permute-start.25 = (f32[104,256]{1,0:T(8,128)S(1)}, f32[104,256]{1,0:T(8,128)S(1)}, u32[]{:S(2)}, u32[]{:S(2)}) collective-permute-start(f32[104,256]{1,0:T(8,128)S(1)} %pad_maximum_fusion.6), channel_id=1, source_target_pairs={{0,2},{1,3},{2,0},{3,1},{4,6},{5,7},{6,4},{7,5},{8,10},{9,11},{10,... | collective-permute-start | bytes 319496 | tf_op jit(solution)/shard_map/ppermute | solution.py:89
  93.1 5.8 %collective-permute-start.27 = (f32[128,256]{1,0:T(8,128)S(1)}, f32[128,256]{1,0:T(8,128)S(1)}, u32[]{:S(2)}, u32[]{:S(2)}) collective-permute-start(f32[128,256]{1,0:T(8,128)S(1)} %get-tuple-element.96), channel_id=1, source_target_pairs={{0,8},{4,12},{8,0},{12,4},{16,24},{20,28},{24,16},{28,20},{1,9},{5... | collective-permute-start | bytes 393224 | tf_op jit(solution)/shard_map/ppermute | solution.py:89
  94.3 5.7 %collective-permute-start.28 = (f32[128,256]{1,0:T(8,128)S(1)}, f32[128,256]{1,0:T(8,128)S(1)}, u32[]{:S(2)}, u32[]{:S(2)}) collective-permute-start(f32[128,256]{1,0:T(8,128)S(1)} %get-tuple-element.97), channel_id=1, source_target_pairs={{0,16},{4,20},{8,24},{12,28},{16,0},{20,4},{24,8},{28,12},{1,17},{... | collective-permute-start | bytes 393224 | tf_op jit(solution)/shard_map/ppermute | solution.py:89
  95.3 5.6 %collective-permute-start.23 = (f32[128,256]{1,0:T(8,128)S(1)}, f32[128,256]{1,0:T(8,128)S(1)}, u32[]{:S(2)}, u32[]{:S(2)}) collective-permute-start(f32[128,256]{1,0:T(8,128)S(1)} %collective-permute-done.20), channel_id=1, source_target_pairs={{0,16},{4,20},{8,24},{12,28},{16,0},{20,4},{24,8},{28,12},{1,17},{... | collective-permute-start | bytes 393224 | tf_op jit(solution)/shard_map/ppermute | solution.py:89
  96.4 5.0 %collective-permute-start.22 = (f32[128,256]{1,0:T(8,128)S(1)}, f32[128,256]{1,0:T(8,128)S(1)}, u32[]{:S(2)}, u32[]{:S(2)}) collective-permute-start(f32[128,256]{1,0:T(8,128)S(1)} %collective-permute-done.21), channel_id=1, source_target_pairs={{0,8},{4,12},{8,0},{12,4},{16,24},{20,28},{24,16},{28,20},{1,9},{5... | collective-permute-start | bytes 393224 | tf_op jit(solution)/shard_map/ppermute | solution.py:89
  97.3 7.2 %collective-permute-start.30 = (f32[72,256]{1,0:T(8,128)S(1)}, f32[72,256]{1,0:T(8,128)S(1)}, u32[]{:S(2)}, u32[]{:S(2)}) collective-permute-start(f32[72,256]{1,0:T(8,128)S(1)} %slice_add_fusion.12), channel_id=1, source_target_pairs={{0,24},{4,28},{8,16},{12,20},{16,8},{20,12},{24,0},{28,4},{1,25},{... | collective-permute-start | bytes 221192 | tf_op jit(solution)/shard_map/ppermute | solution.py:89
  98.9 5.6 %collective-permute-start.29 = (f32[72,256]{1,0:T(8,128)S(1)}, f32[72,256]{1,0:T(8,128)S(1)}, u32[]{:S(2)}, u32[]{:S(2)}) collective-permute-start(f32[72,256]{1,0:T(8,128)S(1)} %slice_add_fusion.12), channel_id=1, source_target_pairs={{0,16},{4,20},{8,24},{12,28},{16,0},{20,4},{24,8},{28,12},{1,17},{... | collective-permute-start | bytes 221192 | tf_op jit(solution)/shard_map/ppermute | solution.py:89
  100.0 4.4 %collective-permute-start.26 = (f32[72,256]{1,0:T(8,128)S(1)}, f32[72,256]{1,0:T(8,128)S(1)}, u32[]{:S(2)}, u32[]{:S(2)}) collective-permute-start(f32[72,256]{1,0:T(8,128)S(1)} %slice_add_fusion.12), channel_id=1, source_target_pairs={{0,8},{4,12},{8,0},{12,4},{16,24},{20,28},{24,16},{28,20},{1,9},{5... | collective-permute-start | bytes 221192 | tf_op jit(solution)/shard_map/ppermute | solution.py:89
  100.9 5.9 %collective-permute-start.32 = (f32[4,128,256]{2,1,0:T(8,128)S(1)}, f32[4,128,256]{2,1,0:T(8,128)S(1)}, u32[]{:S(2)}, u32[]{:S(2)}) collective-permute-start(f32[4,128,256]{2,1,0:T(8,128)S(1)} %pad_maximum_fusion.1.refs_1_), channel_id=1, source_target_pairs={{0,4},{4,0},{8,12},{12,8},{16,20},{20,16},{24,28},{28,24},{1,5},{5... | collective-permute-start | bytes 1572872 | tf_op jit(solution)/shard_map/ppermute | solution.py:89
  104.4 2.4 %collective-permute-start.31 = (f32[4,128,256]{2,1,0:T(8,128)S(1)}, f32[4,128,256]{2,1,0:T(8,128)S(1)}, u32[]{:S(2)}, u32[]{:S(2)}) collective-permute-start(f32[4,128,256]{2,1,0:T(8,128)S(1)} %pad_maximum_fusion.refs_0_), channel_id=1, source_target_pairs={{0,4},{4,0},{8,12},{12,8},{16,20},{20,16},{24,28},{28,24},{1,5},{5... | collective-permute-start | bytes 1572872 | tf_op jit(solution)/shard_map/ppermute | solution.py:89
  104.5 2.3 %collective-permute-start.33 = (f32[4,72,256]{2,1,0:T(8,128)S(1)}, f32[4,72,256]{2,1,0:T(8,128)S(1)}, u32[]{:S(2)}, u32[]{:S(2)}) collective-permute-start(f32[4,72,256]{2,1,0:T(8,128)S(1)} %pad_maximum_fusion.2.refs_2_), channel_id=1, source_target_pairs={{0,4},{4,0},{8,12},{12,8},{16,20},{20,16},{24,28},{28,24},{1,5},{5... | collective-permute-start | bytes 884744 | tf_op jit(solution)/shard_map/ppermute | solution.py:89

commit v22 on v21

--- a/solution.py
+++ b/solution.py
@@ -265,36 +265,6 @@
         payload[slot, :mid, :] = sums[:mid, columns]
         payload[slot, mid : mid + TAIL, :] = counts
         payload[slot, mid + TAIL :, :] = sums[mid:, columns]
-
-
-def fetch_body(points, *refs):
-    *_, kept, sems = refs
-    share = points.shape[0] // sems.shape[0]
-    copies = [
-        pltpu.make_async_copy(
-            points.at[i * share : (i + 1) * share], kept.at[i * share : (i + 1) * share], sems.at[i]
-        )
-        for i in range(sems.shape[0])
-    ]
-    for copy in copies:
-        copy.start()
-    for copy in copies:
-        copy.wait()
-
-
-def fetch(points, after):
-    return pl.pallas_call(
-        fetch_body,
-        out_shape=pltpu.VMEM(points.shape, points.dtype),
-        in_specs=[AWAY] + [HERE] * len(after),
-        out_specs=HERE,
-        scratch_shapes=[pltpu.SemaphoreType.DMA((8,))],
-        compiler_params=pltpu.CompilerParams(vmem_limit_bytes=2 * 2**20),
-        cost_estimate=pl.CostEstimate(
-            flops=0, bytes_accessed=4 * points.size, transcendentals=0
-        ),
-        name="fetch_points",
-    )(far_off(points), *[near_by(value) for value in after])
 
 
 def run_pass(info, points, fine_assign, fine, squares, seen, *, pass_index, flip, rows):
@@ -552,8 +522,7 @@
     bits = range(lax.axis_size("cen").bit_length() - 1)
     folded = jnp.concatenate([part, seen_first.reshape(-1, block_width)], 0)
     paired = swap(folded, 1, "cen")
-    kept = fetch(points, own[:2])
-    own, kept, paired = lax.optimization_barrier((own, kept, paired))
+    own, paired = lax.optimization_barrier((own, paired))
     own = jnp.stack(own)
     other = swap(own, CORE)
 

time: 109 us -> 112 us (1.028)
  Pallas kernels: 42 us -> 38.5 us
  local copies, waits for them, and re-layouts: 0.21 us -> 3.59 us
  waiting for transfers between devices: 24.4 us -> 26.8 us
    pallas_call x1 -> x0, Pallas kernels: 3.47 us -> none  [fetch(): pl.pallas_call(fetch_body, out_shape=pltpu.VMEM(points.shape, points.dtyp...]
    unnamed x17 -> x21, local copies, waits for them, and re-layouts: 0.14 us -> 3.52 us
    ppermute x26, waiting for transfers between devices: 7.7 us -> 9.97 us  [swap(): return lax.ppermute(value, axis, [(i, i ^ bit) for i in range(size)])]
  transfers between devices with their start and end apart: 34 -> 34, of which waited for: 11 -> 11; matrix products, arithmetic and copies ran while one was open for 2% -> 2% of each run, Pallas kernels for 24% -> 20%
where the time goes in v22:
time: 112 us; the launch traced here: 111 us
  starting transfers between devices  39.5 us (35%)
  Pallas kernels  38.5 us (34%)
  waiting for transfers between devices  26.8 us (24%)
  local copies, waits for them, and re-layouts  3.59 us (3%)
  other arithmetic  1.85 us (2%)
  between operations  1.24 us (1%)
    pallas_call x4, Pallas kernels, run_pass(): pl.pallas_call(body, out_shape=out_shape, in_specs=[SCALARS, *in_specs],...  34.1 us
    ppermute x26, starting transfers between devices, swap(): return lax.ppermute(value, axis, [(i, i ^ bit) for i in range(size)])  28.7 us
    ppermute x26, waiting for transfers between devices, swap(): return lax.ppermute(value, axis, [(i, i ^ bit) for i in range(size)])  9.97 us
    ppermute x4, waiting for transfers between devices, swap_first(): return lax.ppermute(value, 'pts', pairs)  9.49 us
    ppermute x4, waiting for transfers between devices, swap_second(): return lax.ppermute(value, 'pts', pairs)  7.3 us
    ppermute x4, starting transfers between devices, swap_second(): return lax.ppermute(value, 'pts', pairs)  6.13 us
    ppermute x4, starting transfers between devices, swap_first(): return lax.ppermute(value, 'pts', pairs)  4.62 us
    unnamed x21, local copies, waits for them, and re-layouts  3.52 us
  transfers between devices with their start and end apart: 34, of which 11 were waited for; matrix products, arithmetic and copies ran while one was open for 2% of the time, Pallas kernels for 20%

profile of v22, /device:TPU:0, one launch (start us, length us, event | category | flops | bytes accessed | tf_op | source)
XLA Modules:
  0.0 111.4 jit_solution(1163866867878848722)
XLA Ops:
  0.6 0.1 pad_add_fusion.info
  0.7 11.4 %energies_and_sums_00.1 = (f32[4,264,256]{2,1,0:T(8,128)S(1)}, f32[2,4096]{1,0:T(2,128)S(1)}, f32[1,4096]{1,0:T(1,128)S(1)}, bf16[4096,1024]{1,0:T(8,128)(2,1)S(1)}) custom-call(s32[4]{0:T(128)S(1)} %pad_add_fusion.info, bf16[4096,1024]{1,0:T(8,128)(2,1)} %points.1, s32[2,4096]{1,0:T(2,128)} %assign.7, f32[512,1024]{1,0:T(8,128)} %fine.3), custom_call_target="tpu_custom_call" | custom-call | flops 4294967296 | bytes 8388608 | tf_op jit(solution)/shard_map/energies_and_sums_00/pallas_call | solution.py:318
  12.1 0.7 collective-permute-start
  12.8 7.5 %energies_and_sums_01.1 = (f32[4,264,256]{2,1,0:T(8,128)S(1)}, f32[2,4096]{1,0:T(2,128)S(1)}) custom-call(s32[4]{0:T(128)S(1)} %pad_add_fusion.info, bf16[4096,1024]{1,0:T(8,128)(2,1)S(1)} %get-tuple-element.51.points, s32[2,4096]{1,0:T(2,128)S(1)} %copy-done.3, f32[512,1024]{1,0:T(8,128)S(1)} %copy-done.2, f32[1,4096]{1,0:T(1,128)S(1)} %get-tuple-element.52.refs_0_, ...), custom_call_target="tpu_custom_call" | custom-call | flops 4294967296 | bytes 8388608 | tf_op jit(solution)/shard_map/energies_and_sums_01/pallas_call | solution.py:318
  20.3 0.0 collective-permute-done.sibling
  20.4 0.0 copy-start
  20.4 0.0 copy-start.1
  20.5 2.4 %collective-permute-start.1 = (f32[2,136,256]{2,1,0:T(8,128)S(1)}, f32[2,136,256]{2,1,0:T(8,128)S(1)}, u32[]{:S(2)}, u32[]{:S(2)}) collective-permute-start(f32[2,136,256]{2,1,0:T(8,128)S(1)} %slice_add_fusion.1), channel_id=1, source_target_pairs={{0,8},{4,20},{8,0},{12,28},{16,24},{20,4},{24,16},{28,12},{1,9},{5... | collective-permute-start | bytes 835592 | tf_op jit(solution)/shard_map/ppermute | solution.py:94
  22.9 0.1 collective-permute-start.2
  23.0 4.4 %collective-permute-done.1.refs_0_ = f32[2,136,256]{2,1,0:T(8,128)S(1)} collective-permute-done((f32[2,136,256]{2,1,0:T(8,128)S(1)}, f32[2,136,256]{2,1,0:T(8,128)S(1)}, u32[]{:S(2)}, u32[]{:S(2)}) %collective-permute-start.1) | collective-permute-done | bytes 278560 | tf_op jit(solution)/shard_map/ppermute | solution.py:94
  27.5 2.1 %collective-permute-start.3 = (f32[136,256]{1,0:T(8,128)S(1)}, f32[136,256]{1,0:T(8,128)S(1)}, u32[]{:S(2)}, u32[]{:S(2)}) collective-permute-start(f32[136,256]{1,0:T(8,128)S(1)} %fusion.1), channel_id=1, source_target_pairs={{0,16},{4,12},{8,24},{12,4},{16,0},{20,28},{24,8},{28,20},{1,17},{... | collective-permute-start | bytes 417800 | tf_op jit(solution)/shard_map/ppermute | solution.py:99
  29.6 0.8 collective-permute-done.2.refs_1_
  30.4 2.4 %collective-permute-start.4 = (f32[128,256]{1,0:T(8,128)S(1)}, f32[128,256]{1,0:T(8,128)S(1)}, u32[]{:S(2)}, u32[]{:S(2)}) collective-permute-start(f32[128,256]{1,0:T(8,128)S(1)} %fusion.3), channel_id=1, source_target_pairs={{0,16},{4,12},{8,24},{12,4},{16,0},{20,28},{24,8},{28,20},{1,17},{... | collective-permute-start | bytes 393224 | tf_op jit(solution)/shard_map/ppermute | solution.py:99
  32.8 2.9 %collective-permute-done.4.refs_3_ = f32[128,256]{1,0:T(8,128)S(1)} collective-permute-done((f32[128,256]{1,0:T(8,128)S(1)}, f32[128,256]{1,0:T(8,128)S(1)}, u32[]{:S(2)}, u32[]{:S(2)}) %collective-permute-start.4) | collective-permute-done | bytes 131104 | tf_op jit(solution)/shard_map/ppermute | solution.py:99
  35.7 1.1 %refine_half.2 = (f32[128,256]{1,0:T(8,128)S(1)}, f32[128,256]{1,0:T(8,128)S(1)}, f32[72,256]{1,0:T(8,128)S(1)}) custom-call(s32[4]{0:T(128)S(1)} %pad_add_fusion.info, f32[4,264,256]{2,1,0:T(8,128)S(1)} %get-tuple-element.54.own, f32[4,264,256]{2,1,0:T(8,128)S(1)} %collective-permute-done.sibling, f32[2,136,256]{2,1,0:T(8,128)S(1)} %collective-permute-done.1.refs_0_, ...), custom_call_target="tpu_custom_call" | custom-call | tf_op jit(solution)/shard_map/refine_half/pallas_call | solution.py:382
  36.9 2.1 %collective-permute-start.5 = (f32[128,256]{1,0:T(8,128)S(1)}, f32[128,256]{1,0:T(8,128)S(1)}, u32[]{:S(2)}, u32[]{:S(2)}) collective-permute-start(f32[128,256]{1,0:T(8,128)S(1)} %get-tuple-element.69), channel_id=1, source_target_pairs={{0,8},{4,12},{8,0},{12,4},{16,24},{20,28},{24,16},{28,20},{1,9},{5... | collective-permute-start | bytes 393224 | tf_op jit(solution)/shard_map/ppermute | solution.py:89
  39.0 1.5 %collective-permute-start.6 = (f32[128,256]{1,0:T(8,128)S(1)}, f32[128,256]{1,0:T(8,128)S(1)}, u32[]{:S(2)}, u32[]{:S(2)}) collective-permute-start(f32[128,256]{1,0:T(8,128)S(1)} %get-tuple-element.68), channel_id=1, source_target_pairs={{0,16},{4,20},{8,24},{12,28},{16,0},{20,4},{24,8},{28,12},{1,17},{... | collective-permute-start | bytes 393224 | tf_op jit(solution)/shard_map/ppermute | solution.py:89
  40.5 0.6 collective-permute-start.10
  41.1 0.1 collective-permute-start.9
  41.2 1.8 %collective-permute-done.5 = f32[128,256]{1,0:T(8,128)S(1)} collective-permute-done((f32[128,256]{1,0:T(8,128)S(1)}, f32[128,256]{1,0:T(8,128)S(1)}, u32[]{:S(2)}, u32[]{:S(2)}) %collective-permute-start.5) | collective-permute-done | bytes 131104 | tf_op jit(solution)/shard_map/ppermute | solution.py:89
  43.0 2.3 %collective-permute-start.8 = (f32[128,256]{1,0:T(8,128)S(1)}, f32[128,256]{1,0:T(8,128)S(1)}, u32[]{:S(2)}, u32[]{:S(2)}) collective-permute-start(f32[128,256]{1,0:T(8,128)S(1)} %collective-permute-done.5), channel_id=1, source_target_pairs={{0,16},{4,20},{8,24},{12,28},{16,0},{20,4},{24,8},{28,12},{1,17},{... | collective-permute-start | bytes 393224 | tf_op jit(solution)/shard_map/ppermute | solution.py:89
  45.3 1.0 collective-permute-start.7
  46.3 1.7 %collective-permute-start.11 = (f32[104,256]{1,0:T(8,128)S(1)}, f32[104,256]{1,0:T(8,128)S(1)}, u32[]{:S(2)}, u32[]{:S(2)}) collective-permute-start(f32[104,256]{1,0:T(8,128)S(1)} %pad_maximum_fusion.3), channel_id=1, source_target_pairs={{0,1},{1,0},{2,3},{3,2},{4,5},{5,4},{6,7},{7,6},{8,9},{9,8},{10,11... | collective-permute-start | bytes 319496 | tf_op jit(solution)/shard_map/ppermute | solution.py:89
  47.9 3.1 %collective-permute-done.11 = f32[104,256]{1,0:T(8,128)S(1)} collective-permute-done((f32[104,256]{1,0:T(8,128)S(1)}, f32[104,256]{1,0:T(8,128)S(1)}, u32[]{:S(2)}, u32[]{:S(2)}) %collective-permute-start.11) | collective-permute-done | bytes 106528 | tf_op jit(solution)/shard_map/ppermute | solution.py:89
  51.1 0.0 collective-permute-done.10
  51.1 0.0 collective-permute-done.9
  51.1 0.0 collective-permute-done.8
  51.2 0.1 collective-permute-start.12
  51.3 3.4 %copy-done.5 = bf16[4096,1024]{1,0:T(8,128)(2,1)S(1)} copy-done((bf16[4096,1024]{1,0:T(8,128)(2,1)S(1)}, bf16[4096,1024]{1,0:T(8,128)(2,1)}, u32[]{:S(2)}) %copy-start.5) | copy-done | bytes 8388632
  54.7 7.5 %energies_and_sums_10.1 = (f32[4,264,256]{2,1,0:T(8,128)S(1)}, f32[2,4096]{1,0:T(2,128)S(1)}) custom-call(s32[4]{0:T(128)S(1)} %pad_add_fusion.info, bf16[4096,1024]{1,0:T(8,128)(2,1)S(1)} %copy-done.5, s32[2,4096]{1,0:T(2,128)S(1)} %copy-done.3, f32[8,128,256]{2,1,0:T(8,128)S(1)} %bitcast_dynamic-update-slice_fusion.fine, ...), custom_call_target="tpu_custom_call" | custom-call | flops 4294967296 | bytes 8388608 | tf_op jit(solution)/shard_map/energies_and_sums_10/pallas_call | solution.py:318
  62.2 0.6 collective-permute-start.14
  62.8 0.1 collective-permute-start.13
  62.9 7.7 %energies_and_sums_11.1 = (f32[4,264,256]{2,1,0:T(8,128)S(1)}, f32[2,4096]{1,0:T(2,128)S(1)}) custom-call(s32[4]{0:T(128)S(1)} %pad_add_fusion.info, bf16[4096,1024]{1,0:T(8,128)(2,1)S(1)} %copy-done.5, s32[2,4096]{1,0:T(2,128)S(1)} %copy-done.3, f32[8,128,256]{2,1,0:T(8,128)S(1)} %collective-permute-done.12.fine, f32[1,4096]{1,0:T(1,128)S(1)} %get-tuple-element.52.refs_0_, ...), custom_call_target="tpu_custom_call" | custom-call | flops 4294967296 | bytes 8388608 | tf_op jit(solution)/shard_map/energies_and_sums_11/pallas_call | solution.py:318
  70.6 0.0 collective-permute-done.14.sibling
  70.7 1.1 %collective-permute-start.15 = (f32[2,136,256]{2,1,0:T(8,128)S(1)}, f32[2,136,256]{2,1,0:T(8,128)S(1)}, u32[]{:S(2)}, u32[]{:S(2)}) collective-permute-start(f32[2,136,256]{2,1,0:T(8,128)S(1)} %slice_add_fusion), channel_id=1, source_target_pairs={{0,8},{4,20},{8,0},{12,28},{16,24},{20,4},{24,16},{28,12},{1,9},{5... | collective-permute-start | bytes 835592 | tf_op jit(solution)/shard_map/ppermute | solution.py:94
  71.9 0.9 collective-permute-start.16
  72.8 2.6 %collective-permute-start.18 = (f32[104,256]{1,0:T(8,128)S(1)}, f32[104,256]{1,0:T(8,128)S(1)}, u32[]{:S(2)}, u32[]{:S(2)}) collective-permute-start(f32[104,256]{1,0:T(8,128)S(1)} %pad_maximum_fusion.4.refs_5_), channel_id=1, source_target_pairs={{0,2},{1,3},{2,0},{3,1},{4,6},{5,7},{6,4},{7,5},{8,10},{9,11},{10,... | collective-permute-start | bytes 319496 | tf_op jit(solution)/shard_map/ppermute | solution.py:89
  75.4 1.9 %collective-permute-done.15.refs_0_ = f32[2,136,256]{2,1,0:T(8,128)S(1)} collective-permute-done((f32[2,136,256]{2,1,0:T(8,128)S(1)}, f32[2,136,256]{2,1,0:T(8,128)S(1)}, u32[]{:S(2)}, u32[]{:S(2)}) %collective-permute-start.15) | collective-permute-done | bytes 278560 | tf_op jit(solution)/shard_map/ppermute | solution.py:94
  77.4 0.8 collective-permute-start.17
  78.2 2.4 %collective-permute-done.16.refs_1_ = f32[2,128,256]{2,1,0:T(8,128)S(1)} collective-permute-done((f32[2,128,256]{2,1,0:T(8,128)S(1)}, f32[2,128,256]{2,1,0:T(8,128)S(1)}, u32[]{:S(2)}, u32[]{:S(2)}) %collective-permute-start.16) | collective-permute-done | bytes 262176 | tf_op jit(solution)/shard_map/ppermute | solution.py:94
  80.6 0.7 fusion.2
  81.3 0.8 collective-permute-start.19
  82.1 4.4 %collective-permute-done.19.refs_3_ = f32[128,256]{1,0:T(8,128)S(1)} collective-permute-done((f32[128,256]{1,0:T(8,128)}, f32[128,256]{1,0:T(8,128)S(1)}, u32[]{:S(2)}, u32[]{:S(2)}) %collective-permute-start.19) | collective-permute-done | bytes 131104 | tf_op jit(solution)/shard_map/ppermute | solution.py:99
  86.4 0.0 collective-permute-done.17.refs_2_
  86.4 1.2 %refine_half.3 = (f32[128,256]{1,0:T(8,128)S(1)}, f32[128,256]{1,0:T(8,128)S(1)}, f32[72,256]{1,0:T(8,128)S(1)}) custom-call(s32[4]{0:T(128)S(1)} %pad_add_fusion.info, f32[4,264,256]{2,1,0:T(8,128)S(1)} %get-tuple-element.75.own, f32[4,264,256]{2,1,0:T(8,128)S(1)} %collective-permute-done.14.sibling, f32[2,136,256]{2,1,0:T(8,128)S(1)} %collective-permute-done.15.refs_0_, ...), custom_call_target="tpu_custom_call" | custom-call | tf_op jit(solution)/shard_map/refine_half/pallas_call | solution.py:382
  87.7 1.7 %collective-permute-start.24 = (f32[104,256]{1,0:T(8,128)S(1)}, f32[104,256]{1,0:T(8,128)S(1)}, u32[]{:S(2)}, u32[]{:S(2)}) collective-permute-start(f32[104,256]{1,0:T(8,128)S(1)} %pad_maximum_fusion.5), channel_id=1, source_target_pairs={{0,1},{1,0},{2,3},{3,2},{4,5},{5,4},{6,7},{7,6},{8,9},{9,8},{10,11... | collective-permute-start | bytes 319496 | tf_op jit(solution)/shard_map/ppermute | solution.py:89
  89.3 1.1 collective-permute-start.20
  90.4 1.1 collective-permute-start.21
  91.5 0.9 collective-permute-done.24
  92.5 3.0 %collective-permute-start.25 = (f32[104,256]{1,0:T(8,128)S(1)}, f32[104,256]{1,0:T(8,128)S(1)}, u32[]{:S(2)}, u32[]{:S(2)}) collective-permute-start(f32[104,256]{1,0:T(8,128)S(1)} %pad_maximum_fusion.6), channel_id=1, source_target_pairs={{0,2},{1,3},{2,0},{3,1},{4,6},{5,7},{6,4},{7,5},{8,10},{9,11},{10,... | collective-permute-start | bytes 319496 | tf_op jit(solution)/shard_map/ppermute | solution.py:89
  95.5 1.1 %collective-permute-start.27 = (f32[128,256]{1,0:T(8,128)S(1)}, f32[128,256]{1,0:T(8,128)S(1)}, u32[]{:S(2)}, u32[]{:S(2)}) collective-permute-start(f32[128,256]{1,0:T(8,128)S(1)} %get-tuple-element.94), channel_id=1, source_target_pairs={{0,8},{4,12},{8,0},{12,4},{16,24},{20,28},{24,16},{28,20},{1,9},{5... | collective-permute-start | bytes 393224 | tf_op jit(solution)/shard_map/ppermute | solution.py:89
  96.7 1.1 %collective-permute-start.28 = (f32[128,256]{1,0:T(8,128)S(1)}, f32[128,256]{1,0:T(8,128)S(1)}, u32[]{:S(2)}, u32[]{:S(2)}) collective-permute-start(f32[128,256]{1,0:T(8,128)S(1)} %get-tuple-element.95), channel_id=1, source_target_pairs={{0,16},{4,20},{8,24},{12,28},{16,0},{20,4},{24,8},{28,12},{1,17},{... | collective-permute-start | bytes 393224 | tf_op jit(solution)/shard_map/ppermute | solution.py:89
  97.8 0.9 collective-permute-start.23
  98.7 0.9 collective-permute-start.22
  99.7 1.7 %collective-permute-start.30 = (f32[72,256]{1,0:T(8,128)S(1)}, f32[72,256]{1,0:T(8,128)S(1)}, u32[]{:S(2)}, u32[]{:S(2)}) collective-permute-start(f32[72,256]{1,0:T(8,128)S(1)} %slice_add_fusion.12), channel_id=1, source_target_pairs={{0,24},{4,28},{8,16},{12,20},{16,8},{20,12},{24,0},{28,4},{1,25},{... | collective-permute-start | bytes 221192 | tf_op jit(solution)/shard_map/ppermute | solution.py:89
  101.5 0.9 collective-permute-start.29
  102.3 1.2 %collective-permute-start.26 = (f32[72,256]{1,0:T(8,128)S(1)}, f32[72,256]{1,0:T(8,128)S(1)}, u32[]{:S(2)}, u32[]{:S(2)}) collective-permute-start(f32[72,256]{1,0:T(8,128)S(1)} %slice_add_fusion.12), channel_id=1, source_target_pairs={{0,8},{4,12},{8,0},{12,4},{16,24},{20,28},{24,16},{28,20},{1,9},{5... | collective-permute-start | bytes 221192 | tf_op jit(solution)/shard_map/ppermute | solution.py:89
  103.6 0.1 collective-permute-start.32
  103.7 3.0 %collective-permute-done.26 = f32[72,256]{1,0:T(8,128)S(1)} collective-permute-done((f32[72,256]{1,0:T(8,128)S(1)}, f32[72,256]{1,0:T(8,128)S(1)}, u32[]{:S(2)}, u32[]{:S(2)}) %collective-permute-start.26) | collective-permute-done | bytes 73760 | tf_op jit(solution)/shard_map/ppermute | solution.py:89
  106.7 0.1 collective-permute-start.31
  106.9 0.5 collective-permute-start.33
  107.4 0.6 maximum_multiply_fusion
  108.1 1.1 collective-permute-done.33.refs_5_
  109.1 2.1 %place_blocks.1 = (f32[512,1024]{1,0:T(8,128)}, f32[64,1024]{1,0:T(8,128)}) custom-call(s32[4]{0:T(128)S(1)} %pad_add_fusion.info, f32[4,128,256]{2,1,0:T(8,128)S(1)} %pad_maximum_fusion.refs_0_, f32[4,128,256]{2,1,0:T(8,128)S(1)} %pad_maximum_fusion.1.refs_1_, f32[4,72,256]{2,1,0:T(8,128)S(1)} %pad_maximum_fusion.2.refs_2_, ...), custom_call_target="tpu_custom_call" | custom-call | tf_op jit(solution)/shard_map/place_blocks/pallas_call | solution.py:485
  (62 shorter events, 0.7 us)
Async XLA Ops:
  0.7 12.1 %copy-start.2 = (f32[512,1024]{1,0:T(8,128)S(1)}, f32[512,1024]{1,0:T(8,128)}, u32[]{:S(2)}) copy-start(f32[512,1024]{1,0:T(8,128)} %fine.3) | copy-start | bytes 6291460
  0.7 12.1 %copy-start.3 = (s32[2,4096]{1,0:T(2,128)S(1)}, s32[2,4096]{1,0:T(2,128)}, u32[]{:S(2)}) copy-start(s32[2,4096]{1,0:T(2,128)} %assign.7) | copy-start | bytes 98308
  12.1 8.2 %copy-start.4 = (bf16[4096,1024]{1,0:T(8,128)(2,1)}, bf16[4096,1024]{1,0:T(8,128)(2,1)S(1)}, u32[]{:S(2)}) copy-start(bf16[4096,1024]{1,0:T(8,128)(2,1)S(1)} %get-tuple-element.51.points) | copy-start | bytes 25165828
  12.1 8.2 %collective-permute-start = (f32[4,264,256]{2,1,0:T(8,128)S(1)}, f32[4,264,256]{2,1,0:T(8,128)S(1)}, u32[]{:S(2)}, u32[]{:S(2)}) collective-permute-start(f32[4,264,256]{2,1,0:T(8,128)S(1)} %get-tuple-element.55), channel_id=1, source_target_pairs={{0,4},{4,0},{8,12},{12,8},{16,20},{20,16},{24,28},{28,24},{1,5},{5... | collective-permute-start | bytes 3244040 | tf_op jit(solution)/shard_map/ppermute | solution.py:89
  20.4 15.3 %copy-start = (f32[64,1024]{1,0:T(8,128)S(1)}, f32[64,1024]{1,0:T(8,128)}, u32[]{:S(2)}) copy-start(f32[64,1024]{1,0:T(8,128)} %refs_5_.1) | copy-start | bytes 786436
  20.4 15.3 %copy-start.1 = (s32[512]{0:T(512)S(1)}, s32[512]{0:T(512)}, u32[]{:S(2)}) copy-start(s32[512]{0:T(512)} %param.9) | copy-start | bytes 6148
  20.5 7.0 %collective-permute-start.1 = (f32[2,136,256]{2,1,0:T(8,128)S(1)}, f32[2,136,256]{2,1,0:T(8,128)S(1)}, u32[]{:S(2)}, u32[]{:S(2)}) collective-permute-start(f32[2,136,256]{2,1,0:T(8,128)S(1)} %slice_add_fusion.1), channel_id=1, source_target_pairs={{0,8},{4,20},{8,0},{12,28},{16,24},{20,4},{24,16},{28,12},{1,9},{5... | collective-permute-start | bytes 835592 | tf_op jit(solution)/shard_map/ppermute | solution.py:94
  22.9 7.4 %collective-permute-start.2 = (f32[2,128,256]{2,1,0:T(8,128)S(1)}, f32[2,128,256]{2,1,0:T(8,128)S(1)}, u32[]{:S(2)}, u32[]{:S(2)}) collective-permute-start(f32[2,128,256]{2,1,0:T(8,128)S(1)} %slice_add_fusion.3), channel_id=1, source_target_pairs={{0,8},{4,20},{8,0},{12,28},{16,24},{20,4},{24,16},{28,12},{1,9},{5... | collective-permute-start | bytes 786440 | tf_op jit(solution)/shard_map/ppermute | solution.py:94
  27.5 8.3 %collective-permute-start.3 = (f32[136,256]{1,0:T(8,128)S(1)}, f32[136,256]{1,0:T(8,128)S(1)}, u32[]{:S(2)}, u32[]{:S(2)}) collective-permute-start(f32[136,256]{1,0:T(8,128)S(1)} %fusion.1), channel_id=1, source_target_pairs={{0,16},{4,12},{8,24},{12,4},{16,0},{20,28},{24,8},{28,20},{1,17},{... | collective-permute-start | bytes 417800 | tf_op jit(solution)/shard_map/ppermute | solution.py:99
  30.4 5.3 %collective-permute-start.4 = (f32[128,256]{1,0:T(8,128)S(1)}, f32[128,256]{1,0:T(8,128)S(1)}, u32[]{:S(2)}, u32[]{:S(2)}) collective-permute-start(f32[128,256]{1,0:T(8,128)S(1)} %fusion.3), channel_id=1, source_target_pairs={{0,16},{4,12},{8,24},{12,4},{16,0},{20,28},{24,8},{28,20},{1,17},{... | collective-permute-start | bytes 393224 | tf_op jit(solution)/shard_map/ppermute | solution.py:99
  36.9 6.1 %collective-permute-start.5 = (f32[128,256]{1,0:T(8,128)S(1)}, f32[128,256]{1,0:T(8,128)S(1)}, u32[]{:S(2)}, u32[]{:S(2)}) collective-permute-start(f32[128,256]{1,0:T(8,128)S(1)} %get-tuple-element.69), channel_id=1, source_target_pairs={{0,8},{4,12},{8,0},{12,4},{16,24},{20,28},{24,16},{28,20},{1,9},{5... | collective-permute-start | bytes 393224 | tf_op jit(solution)/shard_map/ppermute | solution.py:89
  39.0 6.4 %collective-permute-start.6 = (f32[128,256]{1,0:T(8,128)S(1)}, f32[128,256]{1,0:T(8,128)S(1)}, u32[]{:S(2)}, u32[]{:S(2)}) collective-permute-start(f32[128,256]{1,0:T(8,128)S(1)} %get-tuple-element.68), channel_id=1, source_target_pairs={{0,16},{4,20},{8,24},{12,28},{16,0},{20,4},{24,8},{28,12},{1,17},{... | collective-permute-start | bytes 393224 | tf_op jit(solution)/shard_map/ppermute | solution.py:89
  40.5 10.6 %collective-permute-start.10 = (f32[128,256]{1,0:T(8,128)S(1)}, f32[128,256]{1,0:T(8,128)S(1)}, u32[]{:S(2)}, u32[]{:S(2)}) collective-permute-start(f32[128,256]{1,0:T(8,128)S(1)} %get-tuple-element.69), channel_id=1, source_target_pairs={{0,16},{4,20},{8,24},{12,28},{16,0},{20,4},{24,8},{28,12},{1,17},{... | collective-permute-start | bytes 393224 | tf_op jit(solution)/shard_map/ppermute | solution.py:89
  41.1 10.0 %collective-permute-start.9 = (f32[128,256]{1,0:T(8,128)S(1)}, f32[128,256]{1,0:T(8,128)S(1)}, u32[]{:S(2)}, u32[]{:S(2)}) collective-permute-start(f32[128,256]{1,0:T(8,128)S(1)} %get-tuple-element.68), channel_id=1, source_target_pairs={{0,8},{4,12},{8,0},{12,4},{16,24},{20,28},{24,16},{28,20},{1,9},{5... | collective-permute-start | bytes 393224 | tf_op jit(solution)/shard_map/ppermute | solution.py:89
  43.0 8.1 %collective-permute-start.8 = (f32[128,256]{1,0:T(8,128)S(1)}, f32[128,256]{1,0:T(8,128)S(1)}, u32[]{:S(2)}, u32[]{:S(2)}) collective-permute-start(f32[128,256]{1,0:T(8,128)S(1)} %collective-permute-done.5), channel_id=1, source_target_pairs={{0,16},{4,20},{8,24},{12,28},{16,0},{20,4},{24,8},{28,12},{1,17},{... | collective-permute-start | bytes 393224 | tf_op jit(solution)/shard_map/ppermute | solution.py:89
  45.3 5.8 %collective-permute-start.7 = (f32[128,256]{1,0:T(8,128)S(1)}, f32[128,256]{1,0:T(8,128)S(1)}, u32[]{:S(2)}, u32[]{:S(2)}) collective-permute-start(f32[128,256]{1,0:T(8,128)S(1)} %collective-permute-done.6), channel_id=1, source_target_pairs={{0,8},{4,12},{8,0},{12,4},{16,24},{20,28},{24,16},{28,20},{1,9},{5... | collective-permute-start | bytes 393224 | tf_op jit(solution)/shard_map/ppermute | solution.py:89
  46.3 4.8 %collective-permute-start.11 = (f32[104,256]{1,0:T(8,128)S(1)}, f32[104,256]{1,0:T(8,128)S(1)}, u32[]{:S(2)}, u32[]{:S(2)}) collective-permute-start(f32[104,256]{1,0:T(8,128)S(1)} %pad_maximum_fusion.3), channel_id=1, source_target_pairs={{0,1},{1,0},{2,3},{3,2},{4,5},{5,4},{6,7},{7,6},{8,9},{9,8},{10,11... | collective-permute-start | bytes 319496 | tf_op jit(solution)/shard_map/ppermute | solution.py:89
  51.2 11.6 %collective-permute-start.12 = (f32[8,128,256]{2,1,0:T(8,128)S(1)}, f32[8,128,256]{2,1,0:T(8,128)S(1)}, u32[]{:S(2)}, u32[]{:S(2)}) collective-permute-start(f32[8,128,256]{2,1,0:T(8,128)S(1)} %bitcast_dynamic-update-slice_fusion.fine), channel_id=1, source_target_pairs={{0,4},{4,0},{8,12},{12,8},{16,20},{20,16},{24,28},{28,24},{1,5},{5... | collective-permute-start | bytes 3145736 | tf_op jit(solution)/shard_map/ppermute | solution.py:89
  51.3 3.4 %copy-start.5 = (bf16[4096,1024]{1,0:T(8,128)(2,1)S(1)}, bf16[4096,1024]{1,0:T(8,128)(2,1)}, u32[]{:S(2)}) copy-start(bf16[4096,1024]{1,0:T(8,128)(2,1)} %copy-done.4) | copy-start | bytes 25165828
  62.2 8.4 %collective-permute-start.14 = (f32[4,264,256]{2,1,0:T(8,128)S(1)}, f32[4,264,256]{2,1,0:T(8,128)S(1)}, u32[]{:S(2)}, u32[]{:S(2)}) collective-permute-start(f32[4,264,256]{2,1,0:T(8,128)S(1)} %get-tuple-element.76), channel_id=1, source_target_pairs={{0,4},{4,0},{8,12},{12,8},{16,20},{20,16},{24,28},{28,24},{1,5},{5... | collective-permute-start | bytes 3244040 | tf_op jit(solution)/shard_map/ppermute | solution.py:89
  62.8 7.8 %collective-permute-start.13 = (f32[72,256]{1,0:T(8,128)S(1)}, f32[72,256]{1,0:T(8,128)S(1)}, u32[]{:S(2)}, u32[]{:S(2)}) collective-permute-start(f32[72,256]{1,0:T(8,128)S(1)} %slice_add_fusion.14), channel_id=1, source_target_pairs={{0,4},{4,0},{8,12},{12,8},{16,20},{20,16},{24,28},{28,24},{1,5},{5... | collective-permute-start | bytes 221192 | tf_op jit(solution)/shard_map/ppermute | solution.py:89
  70.7 6.6 %collective-permute-start.15 = (f32[2,136,256]{2,1,0:T(8,128)S(1)}, f32[2,136,256]{2,1,0:T(8,128)S(1)}, u32[]{:S(2)}, u32[]{:S(2)}) collective-permute-start(f32[2,136,256]{2,1,0:T(8,128)S(1)} %slice_add_fusion), channel_id=1, source_target_pairs={{0,8},{4,20},{8,0},{12,28},{16,24},{20,4},{24,16},{28,12},{1,9},{5... | collective-permute-start | bytes 835592 | tf_op jit(solution)/shard_map/ppermute | solution.py:94
  71.9 8.7 %collective-permute-start.16 = (f32[2,128,256]{2,1,0:T(8,128)S(1)}, f32[2,128,256]{2,1,0:T(8,128)S(1)}, u32[]{:S(2)}, u32[]{:S(2)}) collective-permute-start(f32[2,128,256]{2,1,0:T(8,128)S(1)} %slice_add_fusion.2), channel_id=1, source_target_pairs={{0,8},{4,20},{8,0},{12,28},{16,24},{20,4},{24,16},{28,12},{1,9},{5... | collective-permute-start | bytes 786440 | tf_op jit(solution)/shard_map/ppermute | solution.py:94
  72.8 8.4 %collective-permute-start.18 = (f32[104,256]{1,0:T(8,128)S(1)}, f32[104,256]{1,0:T(8,128)S(1)}, u32[]{:S(2)}, u32[]{:S(2)}) collective-permute-start(f32[104,256]{1,0:T(8,128)S(1)} %pad_maximum_fusion.4.refs_5_), channel_id=1, source_target_pairs={{0,2},{1,3},{2,0},{3,1},{4,6},{5,7},{6,4},{7,5},{8,10},{9,11},{10,... | collective-permute-start | bytes 319496 | tf_op jit(solution)/shard_map/ppermute | solution.py:89
  77.4 9.1 %collective-permute-start.17 = (f32[136,256]{1,0:T(8,128)S(1)}, f32[136,256]{1,0:T(8,128)S(1)}, u32[]{:S(2)}, u32[]{:S(2)}) collective-permute-start(f32[136,256]{1,0:T(8,128)S(1)} %fusion), channel_id=1, source_target_pairs={{0,16},{4,12},{8,24},{12,4},{16,0},{20,28},{24,8},{28,20},{1,17},{... | collective-permute-start | bytes 417800 | tf_op jit(solution)/shard_map/ppermute | solution.py:99
  81.3 5.2 %collective-permute-start.19 = (f32[128,256]{1,0:T(8,128)}, f32[128,256]{1,0:T(8,128)S(1)}, u32[]{:S(2)}, u32[]{:S(2)}) collective-permute-start(f32[128,256]{1,0:T(8,128)} %fusion.2), channel_id=1, source_target_pairs={{0,16},{4,12},{8,24},{12,4},{16,0},{20,28},{24,8},{28,20},{1,17},{... | collective-permute-start | bytes 393224 | tf_op jit(solution)/shard_map/ppermute | solution.py:99
  87.7 4.8 %collective-permute-start.24 = (f32[104,256]{1,0:T(8,128)S(1)}, f32[104,256]{1,0:T(8,128)S(1)}, u32[]{:S(2)}, u32[]{:S(2)}) collective-permute-start(f32[104,256]{1,0:T(8,128)S(1)} %pad_maximum_fusion.5), channel_id=1, source_target_pairs={{0,1},{1,0},{2,3},{3,2},{4,5},{5,4},{6,7},{7,6},{8,9},{9,8},{10,11... | collective-permute-start | bytes 319496 | tf_op jit(solution)/shard_map/ppermute | solution.py:89
  89.3 6.2 %collective-permute-start.20 = (f32[128,256]{1,0:T(8,128)S(1)}, f32[128,256]{1,0:T(8,128)S(1)}, u32[]{:S(2)}, u32[]{:S(2)}) collective-permute-start(f32[128,256]{1,0:T(8,128)S(1)} %get-tuple-element.95), channel_id=1, source_target_pairs={{0,8},{4,12},{8,0},{12,4},{16,24},{20,28},{24,16},{28,20},{1,9},{5... | collective-permute-start | bytes 393224 | tf_op jit(solution)/shard_map/ppermute | solution.py:89
  90.4 5.1 %collective-permute-start.21 = (f32[128,256]{1,0:T(8,128)S(1)}, f32[128,256]{1,0:T(8,128)S(1)}, u32[]{:S(2)}, u32[]{:S(2)}) collective-permute-start(f32[128,256]{1,0:T(8,128)S(1)} %get-tuple-element.94), channel_id=1, source_target_pairs={{0,16},{4,20},{8,24},{12,28},{16,0},{20,4},{24,8},{28,12},{1,17},{... | collective-permute-start | bytes 393224 | tf_op jit(solution)/shard_map/ppermute | solution.py:89
  92.5 7.2 %collective-permute-start.25 = (f32[104,256]{1,0:T(8,128)S(1)}, f32[104,256]{1,0:T(8,128)S(1)}, u32[]{:S(2)}, u32[]{:S(2)}) collective-permute-start(f32[104,256]{1,0:T(8,128)S(1)} %pad_maximum_fusion.6), channel_id=1, source_target_pairs={{0,2},{1,3},{2,0},{3,1},{4,6},{5,7},{6,4},{7,5},{8,10},{9,11},{10,... | collective-permute-start | bytes 319496 | tf_op jit(solution)/shard_map/ppermute | solution.py:89
  95.5 5.9 %collective-permute-start.27 = (f32[128,256]{1,0:T(8,128)S(1)}, f32[128,256]{1,0:T(8,128)S(1)}, u32[]{:S(2)}, u32[]{:S(2)}) collective-permute-start(f32[128,256]{1,0:T(8,128)S(1)} %get-tuple-element.94), channel_id=1, source_target_pairs={{0,8},{4,12},{8,0},{12,4},{16,24},{20,28},{24,16},{28,20},{1,9},{5... | collective-permute-start | bytes 393224 | tf_op jit(solution)/shard_map/ppermute | solution.py:89
  96.7 5.7 %collective-permute-start.28 = (f32[128,256]{1,0:T(8,128)S(1)}, f32[128,256]{1,0:T(8,128)S(1)}, u32[]{:S(2)}, u32[]{:S(2)}) collective-permute-start(f32[128,256]{1,0:T(8,128)S(1)} %get-tuple-element.95), channel_id=1, source_target_pairs={{0,16},{4,20},{8,24},{12,28},{16,0},{20,4},{24,8},{28,12},{1,17},{... | collective-permute-start | bytes 393224 | tf_op jit(solution)/shard_map/ppermute | solution.py:89
  97.8 5.8 %collective-permute-start.23 = (f32[128,256]{1,0:T(8,128)S(1)}, f32[128,256]{1,0:T(8,128)S(1)}, u32[]{:S(2)}, u32[]{:S(2)}) collective-permute-start(f32[128,256]{1,0:T(8,128)S(1)} %collective-permute-done.20), channel_id=1, source_target_pairs={{0,16},{4,20},{8,24},{12,28},{16,0},{20,4},{24,8},{28,12},{1,17},{... | collective-permute-start | bytes 393224 | tf_op jit(solution)/shard_map/ppermute | solution.py:89
  98.7 5.0 %collective-permute-start.22 = (f32[128,256]{1,0:T(8,128)S(1)}, f32[128,256]{1,0:T(8,128)S(1)}, u32[]{:S(2)}, u32[]{:S(2)}) collective-permute-start(f32[128,256]{1,0:T(8,128)S(1)} %collective-permute-done.21), channel_id=1, source_target_pairs={{0,8},{4,12},{8,0},{12,4},{16,24},{20,28},{24,16},{28,20},{1,9},{5... | collective-permute-start | bytes 393224 | tf_op jit(solution)/shard_map/ppermute | solution.py:89
  99.7 7.1 %collective-permute-start.30 = (f32[72,256]{1,0:T(8,128)S(1)}, f32[72,256]{1,0:T(8,128)S(1)}, u32[]{:S(2)}, u32[]{:S(2)}) collective-permute-start(f32[72,256]{1,0:T(8,128)S(1)} %slice_add_fusion.12), channel_id=1, source_target_pairs={{0,24},{4,28},{8,16},{12,20},{16,8},{20,12},{24,0},{28,4},{1,25},{... | collective-permute-start | bytes 221192 | tf_op jit(solution)/shard_map/ppermute | solution.py:89
  101.5 5.4 %collective-permute-start.29 = (f32[72,256]{1,0:T(8,128)S(1)}, f32[72,256]{1,0:T(8,128)S(1)}, u32[]{:S(2)}, u32[]{:S(2)}) collective-permute-start(f32[72,256]{1,0:T(8,128)S(1)} %slice_add_fusion.12), channel_id=1, source_target_pairs={{0,16},{4,20},{8,24},{12,28},{16,0},{20,4},{24,8},{28,12},{1,17},{... | collective-permute-start | bytes 221192 | tf_op jit(solution)/shard_map/ppermute | solution.py:89
  102.3 4.4 %collective-permute-start.26 = (f32[72,256]{1,0:T(8,128)S(1)}, f32[72,256]{1,0:T(8,128)S(1)}, u32[]{:S(2)}, u32[]{:S(2)}) collective-permute-start(f32[72,256]{1,0:T(8,128)S(1)} %slice_add_fusion.12), channel_id=1, source_target_pairs={{0,8},{4,12},{8,0},{12,4},{16,24},{20,28},{24,16},{28,20},{1,9},{5... | collective-permute-start | bytes 221192 | tf_op jit(solution)/shard_map/ppermute | solution.py:89
  103.6 5.5 %collective-permute-start.32 = (f32[4,128,256]{2,1,0:T(8,128)S(1)}, f32[4,128,256]{2,1,0:T(8,128)S(1)}, u32[]{:S(2)}, u32[]{:S(2)}) collective-permute-start(f32[4,128,256]{2,1,0:T(8,128)S(1)} %pad_maximum_fusion.1.refs_1_), channel_id=1, source_target_pairs={{0,4},{4,0},{8,12},{12,8},{16,20},{20,16},{24,28},{28,24},{1,5},{5... | collective-permute-start | bytes 1572872 | tf_op jit(solution)/shard_map/ppermute | solution.py:89
  106.7 2.4 %collective-permute-start.31 = (f32[4,128,256]{2,1,0:T(8,128)S(1)}, f32[4,128,256]{2,1,0:T(8,128)S(1)}, u32[]{:S(2)}, u32[]{:S(2)}) collective-permute-start(f32[4,128,256]{2,1,0:T(8,128)S(1)} %pad_maximum_fusion.refs_0_), channel_id=1, source_target_pairs={{0,4},{4,0},{8,12},{12,8},{16,20},{20,16},{24,28},{28,24},{1,5},{5... | collective-permute-start | bytes 1572872 | tf_op jit(solution)/shard_map/ppermute | solution.py:89
  106.9 2.3 %collective-permute-start.33 = (f32[4,72,256]{2,1,0:T(8,128)S(1)}, f32[4,72,256]{2,1,0:T(8,128)S(1)}, u32[]{:S(2)}, u32[]{:S(2)}) collective-permute-start(f32[4,72,256]{2,1,0:T(8,128)S(1)} %pad_maximum_fusion.2.refs_2_), channel_id=1, source_target_pairs={{0,4},{4,0},{8,12},{12,8},{16,20},{20,16},{24,28},{28,24},{1,5},{5... | collective-permute-start | bytes 884744 | tf_op jit(solution)/shard_map/ppermute | solution.py:89

commit v23 on v21

--- a/solution.py
+++ b/solution.py
@@ -163,10 +163,8 @@
         load_assign.start()
         load(0, 1).start()
 
-        @pl.loop(1, tiles)
-        def _(i):
-            load(i, 0).start()
-            load(i, 1).start()
+        load(1, 0).start()
+        load(1, 1).start()
 
     if initial:
         if first:
@@ -238,15 +236,15 @@
         for half in range(2):
             if stream:
                 load(i, half).wait()
+                if i + 2 < tiles:
+                    load(i + 2, half).start()
 
     if stream:
         load_assign.wait()
     arrive(0)
     multiply(0, even)
 
-    @pl.loop(0, tiles // 2 - 1)
-    def _(pair):
-        i = 2 * pair
+    for i in range(0, tiles - 2, 2):
         arrive(i + 1)
         multiply(i + 1, odd)
         collect(i, even)

time: 109 us -> 110 us (level)
  no operation moved by 1% of the time
where the time goes in v23:
time: 110 us; the launch traced here: 109 us
  Pallas kernels  42.4 us (39%)
  starting transfers between devices  39.4 us (36%)
  waiting for transfers between devices  24.3 us (22%)
  other arithmetic  1.85 us (2%)
  between operations  1.24 us (1%)
    pallas_call x4, Pallas kernels, run_pass(): pl.pallas_call(body, out_shape=out_shape, in_specs=[SCALARS, *in_specs],...  34.5 us
    ppermute x26, starting transfers between devices, swap(): return lax.ppermute(value, axis, [(i, i ^ bit) for i in range(size)])  28.5 us
    ppermute x4, waiting for transfers between devices, swap_first(): return lax.ppermute(value, 'pts', pairs)  9.46 us
    ppermute x26, waiting for transfers between devices, swap(): return lax.ppermute(value, axis, [(i, i ^ bit) for i in range(size)])  7.62 us
    ppermute x4, waiting for transfers between devices, swap_second(): return lax.ppermute(value, 'pts', pairs)  7.23 us
    ppermute x4, starting transfers between devices, swap_second(): return lax.ppermute(value, 'pts', pairs)  6.35 us
    ppermute x4, starting transfers between devices, swap_first(): return lax.ppermute(value, 'pts', pairs)  4.55 us
    pallas_call x1, Pallas kernels, fetch(): pl.pallas_call(fetch_body, out_shape=pltpu.VMEM(points.shape, points.dtyp...  3.47 us
  transfers between devices with their start and end apart: 34, of which 11 were waited for; matrix products, arithmetic and copies ran while one was open for 2% of the time, Pallas kernels for 24%

profile of v23, /device:TPU:0, one launch (start us, length us, event | category | flops | bytes accessed | tf_op | source)
XLA Modules:
  0.0 109.4 jit_solution(14426127649802937484)
XLA Ops:
  0.6 0.1 pad_add_fusion.info
  0.7 11.7 %energies_and_sums_00.1 = (f32[4,264,256]{2,1,0:T(8,128)S(1)}, f32[2,4096]{1,0:T(2,128)S(1)}, f32[1,4096]{1,0:T(1,128)S(1)}, bf16[4096,1024]{1,0:T(8,128)(2,1)S(1)}) custom-call(s32[4]{0:T(128)S(1)} %pad_add_fusion.info, bf16[4096,1024]{1,0:T(8,128)(2,1)} %points.3, s32[2,4096]{1,0:T(2,128)} %assign.7, f32[512,1024]{1,0:T(8,128)} %fine.3), custom_call_target="tpu_custom_call" | custom-call | flops 4294967296 | bytes 8388608 | tf_op jit(solution)/shard_map/energies_and_sums_00/pallas_call | solution.py:346
  12.4 0.8 collective-permute-start
  13.2 7.5 %energies_and_sums_01.1 = (f32[4,264,256]{2,1,0:T(8,128)S(1)}, f32[2,4096]{1,0:T(2,128)S(1)}) custom-call(s32[4]{0:T(128)S(1)} %pad_add_fusion.info, bf16[4096,1024]{1,0:T(8,128)(2,1)S(1)} %get-tuple-element.52.points, s32[2,4096]{1,0:T(2,128)S(1)} %copy-done.3, f32[512,1024]{1,0:T(8,128)S(1)} %copy-done.2, f32[1,4096]{1,0:T(1,128)S(1)} %get-tuple-element.53.refs_0_, ...), custom_call_target="tpu_custom_call" | custom-call | flops 4294967296 | bytes 8388608 | tf_op jit(solution)/shard_map/energies_and_sums_01/pallas_call | solution.py:346
  20.8 0.0 copy-start
  20.8 0.0 copy-start.1
  20.9 2.4 %collective-permute-start.1 = (f32[2,136,256]{2,1,0:T(8,128)S(1)}, f32[2,136,256]{2,1,0:T(8,128)S(1)}, u32[]{:S(2)}, u32[]{:S(2)}) collective-permute-start(f32[2,136,256]{2,1,0:T(8,128)S(1)} %slice_add_fusion.1), channel_id=1, source_target_pairs={{0,8},{4,20},{8,0},{12,28},{16,24},{20,4},{24,16},{28,12},{1,9},{5... | collective-permute-start | bytes 835592 | tf_op jit(solution)/shard_map/ppermute | solution.py:94
  23.2 0.1 collective-permute-start.2
  23.3 4.4 %collective-permute-done.1.refs_0_ = f32[2,136,256]{2,1,0:T(8,128)S(1)} collective-permute-done((f32[2,136,256]{2,1,0:T(8,128)S(1)}, f32[2,136,256]{2,1,0:T(8,128)S(1)}, u32[]{:S(2)}, u32[]{:S(2)}) %collective-permute-start.1) | collective-permute-done | bytes 278560 | tf_op jit(solution)/shard_map/ppermute | solution.py:94
  27.8 2.1 %collective-permute-start.3 = (f32[136,256]{1,0:T(8,128)S(1)}, f32[136,256]{1,0:T(8,128)S(1)}, u32[]{:S(2)}, u32[]{:S(2)}) collective-permute-start(f32[136,256]{1,0:T(8,128)S(1)} %fusion.1), channel_id=1, source_target_pairs={{0,16},{4,12},{8,24},{12,4},{16,0},{20,28},{24,8},{28,20},{1,17},{... | collective-permute-start | bytes 417800 | tf_op jit(solution)/shard_map/ppermute | solution.py:99
  29.9 0.8 collective-permute-done.2.refs_1_
  30.8 2.4 %collective-permute-start.4 = (f32[128,256]{1,0:T(8,128)S(1)}, f32[128,256]{1,0:T(8,128)S(1)}, u32[]{:S(2)}, u32[]{:S(2)}) collective-permute-start(f32[128,256]{1,0:T(8,128)S(1)} %fusion.3), channel_id=1, source_target_pairs={{0,16},{4,12},{8,24},{12,4},{16,0},{20,28},{24,8},{28,20},{1,17},{... | collective-permute-start | bytes 393224 | tf_op jit(solution)/shard_map/ppermute | solution.py:99
  33.2 2.9 %collective-permute-done.4.refs_3_ = f32[128,256]{1,0:T(8,128)S(1)} collective-permute-done((f32[128,256]{1,0:T(8,128)S(1)}, f32[128,256]{1,0:T(8,128)S(1)}, u32[]{:S(2)}, u32[]{:S(2)}) %collective-permute-start.4) | collective-permute-done | bytes 131104 | tf_op jit(solution)/shard_map/ppermute | solution.py:99
  36.1 0.0 collective-permute-done.3.refs_2_
  36.1 1.1 %refine_half.2 = (f32[128,256]{1,0:T(8,128)S(1)}, f32[128,256]{1,0:T(8,128)S(1)}, f32[72,256]{1,0:T(8,128)S(1)}) custom-call(s32[4]{0:T(128)S(1)} %pad_add_fusion.info, f32[4,264,256]{2,1,0:T(8,128)S(1)} %get-tuple-element.55.own, f32[4,264,256]{2,1,0:T(8,128)S(1)} %collective-permute-done.sibling, f32[2,136,256]{2,1,0:T(8,128)S(1)} %collective-permute-done.1.refs_0_, ...), custom_call_target="tpu_custom_call" | custom-call | tf_op jit(solution)/shard_map/refine_half/pallas_call | solution.py:410
  37.3 2.1 %collective-permute-start.5 = (f32[128,256]{1,0:T(8,128)S(1)}, f32[128,256]{1,0:T(8,128)S(1)}, u32[]{:S(2)}, u32[]{:S(2)}) collective-permute-start(f32[128,256]{1,0:T(8,128)S(1)} %get-tuple-element.71), channel_id=1, source_target_pairs={{0,8},{4,12},{8,0},{12,4},{16,24},{20,28},{24,16},{28,20},{1,9},{5... | collective-permute-start | bytes 393224 | tf_op jit(solution)/shard_map/ppermute | solution.py:89
  39.3 1.5 %collective-permute-start.6 = (f32[128,256]{1,0:T(8,128)S(1)}, f32[128,256]{1,0:T(8,128)S(1)}, u32[]{:S(2)}, u32[]{:S(2)}) collective-permute-start(f32[128,256]{1,0:T(8,128)S(1)} %get-tuple-element.70), channel_id=1, source_target_pairs={{0,16},{4,20},{8,24},{12,28},{16,0},{20,4},{24,8},{28,12},{1,17},{... | collective-permute-start | bytes 393224 | tf_op jit(solution)/shard_map/ppermute | solution.py:89
  40.9 0.6 collective-permute-start.10
  41.5 0.1 collective-permute-start.9
  41.6 1.9 %collective-permute-done.5.refs_0_ = f32[128,256]{1,0:T(8,128)S(1)} collective-permute-done((f32[128,256]{1,0:T(8,128)S(1)}, f32[128,256]{1,0:T(8,128)S(1)}, u32[]{:S(2)}, u32[]{:S(2)}) %collective-permute-start.5) | collective-permute-done | bytes 131104 | tf_op jit(solution)/shard_map/ppermute | solution.py:89
  43.4 2.3 %collective-permute-start.8 = (f32[128,256]{1,0:T(8,128)S(1)}, f32[128,256]{1,0:T(8,128)S(1)}, u32[]{:S(2)}, u32[]{:S(2)}) collective-permute-start(f32[128,256]{1,0:T(8,128)S(1)} %collective-permute-done.5.refs_0_), channel_id=1, source_target_pairs={{0,16},{4,20},{8,24},{12,28},{16,0},{20,4},{24,8},{28,12},{1,17},{... | collective-permute-start | bytes 393224 | tf_op jit(solution)/shard_map/ppermute | solution.py:89
  45.7 0.9 collective-permute-start.7
  46.6 1.6 %collective-permute-start.11 = (f32[104,256]{1,0:T(8,128)S(1)}, f32[104,256]{1,0:T(8,128)S(1)}, u32[]{:S(2)}, u32[]{:S(2)}) collective-permute-start(f32[104,256]{1,0:T(8,128)S(1)} %pad_maximum_fusion.3), channel_id=1, source_target_pairs={{0,1},{1,0},{2,3},{3,2},{4,5},{5,4},{6,7},{7,6},{8,9},{9,8},{10,11... | collective-permute-start | bytes 319496 | tf_op jit(solution)/shard_map/ppermute | solution.py:89
  48.2 3.5 %fetch_points.1.points = bf16[4096,1024]{1,0:T(8,128)(2,1)S(1)} custom-call(bf16[4096,1024]{1,0:T(8,128)(2,1)} %points.3, f32[128,256]{1,0:T(8,128)S(1)} %collective-permute-done.5.refs_0_, f32[128,256]{1,0:T(8,128)S(1)} %collective-permute-done.6.refs_1_), custom_call_target="tpu_custom_call" | custom-call | bytes 16777216 | tf_op jit(solution)/shard_map/fetch_points/pallas_call | solution.py:284
  51.7 0.0 collective-permute-done.10
  51.7 0.0 collective-permute-done.9
  51.8 0.0 collective-permute-done.7
  51.9 0.1 collective-permute-start.12
  52.0 7.5 %energies_and_sums_10.1 = (f32[4,264,256]{2,1,0:T(8,128)S(1)}, f32[2,4096]{1,0:T(2,128)S(1)}) custom-call(s32[4]{0:T(128)S(1)} %pad_add_fusion.info, bf16[4096,1024]{1,0:T(8,128)(2,1)S(1)} %fetch_points.1.points, s32[2,4096]{1,0:T(2,128)S(1)} %copy-done.3, f32[8,128,256]{2,1,0:T(8,128)S(1)} %bitcast_dynamic-update-slice_fusion.fine, ...), custom_call_target="tpu_custom_call" | custom-call | flops 4294967296 | bytes 8388608 | tf_op jit(solution)/shard_map/energies_and_sums_10/pallas_call | solution.py:346
  59.5 0.5 collective-permute-start.14
  60.1 0.1 collective-permute-start.13
  60.2 7.7 %energies_and_sums_11.1 = (f32[4,264,256]{2,1,0:T(8,128)S(1)}, f32[2,4096]{1,0:T(2,128)S(1)}) custom-call(s32[4]{0:T(128)S(1)} %pad_add_fusion.info, bf16[4096,1024]{1,0:T(8,128)(2,1)S(1)} %fetch_points.1.points, s32[2,4096]{1,0:T(2,128)S(1)} %copy-done.3, f32[8,128,256]{2,1,0:T(8,128)S(1)} %collective-permute-done.12.fine, ...), custom_call_target="tpu_custom_call" | custom-call | flops 4294967296 | bytes 8388608 | tf_op jit(solution)/shard_map/energies_and_sums_11/pallas_call | solution.py:346
  68.0 0.0 collective-permute-done.14.sibling
  68.1 1.2 %collective-permute-start.15 = (f32[2,136,256]{2,1,0:T(8,128)S(1)}, f32[2,136,256]{2,1,0:T(8,128)S(1)}, u32[]{:S(2)}, u32[]{:S(2)}) collective-permute-start(f32[2,136,256]{2,1,0:T(8,128)S(1)} %slice_add_fusion), channel_id=1, source_target_pairs={{0,8},{4,20},{8,0},{12,28},{16,24},{20,4},{24,16},{28,12},{1,9},{5... | collective-permute-start | bytes 835592 | tf_op jit(solution)/shard_map/ppermute | solution.py:94
  69.3 0.9 collective-permute-start.16
  70.2 2.6 %collective-permute-start.18 = (f32[104,256]{1,0:T(8,128)S(1)}, f32[104,256]{1,0:T(8,128)S(1)}, u32[]{:S(2)}, u32[]{:S(2)}) collective-permute-start(f32[104,256]{1,0:T(8,128)S(1)} %pad_maximum_fusion.4.refs_5_), channel_id=1, source_target_pairs={{0,2},{1,3},{2,0},{3,1},{4,6},{5,7},{6,4},{7,5},{8,10},{9,11},{10,... | collective-permute-start | bytes 319496 | tf_op jit(solution)/shard_map/ppermute | solution.py:89
  72.7 1.9 %collective-permute-done.15.refs_0_ = f32[2,136,256]{2,1,0:T(8,128)S(1)} collective-permute-done((f32[2,136,256]{2,1,0:T(8,128)S(1)}, f32[2,136,256]{2,1,0:T(8,128)S(1)}, u32[]{:S(2)}, u32[]{:S(2)}) %collective-permute-start.15) | collective-permute-done | bytes 278560 | tf_op jit(solution)/shard_map/ppermute | solution.py:94
  74.7 0.9 collective-permute-start.17
  75.6 2.3 %collective-permute-done.16.refs_1_ = f32[2,128,256]{2,1,0:T(8,128)S(1)} collective-permute-done((f32[2,128,256]{2,1,0:T(8,128)S(1)}, f32[2,128,256]{2,1,0:T(8,128)S(1)}, u32[]{:S(2)}, u32[]{:S(2)}) %collective-permute-start.16) | collective-permute-done | bytes 262176 | tf_op jit(solution)/shard_map/ppermute | solution.py:94
  77.9 0.7 fusion.2
  78.6 0.0 collective-permute-done.18.refs_6_
  78.6 0.9 collective-permute-start.19
  79.5 4.3 %collective-permute-done.19.refs_3_ = f32[128,256]{1,0:T(8,128)S(1)} collective-permute-done((f32[128,256]{1,0:T(8,128)}, f32[128,256]{1,0:T(8,128)S(1)}, u32[]{:S(2)}, u32[]{:S(2)}) %collective-permute-start.19) | collective-permute-done | bytes 131104 | tf_op jit(solution)/shard_map/ppermute | solution.py:99
  83.8 1.2 %refine_half.3 = (f32[128,256]{1,0:T(8,128)S(1)}, f32[128,256]{1,0:T(8,128)S(1)}, f32[72,256]{1,0:T(8,128)S(1)}) custom-call(s32[4]{0:T(128)S(1)} %pad_add_fusion.info, f32[4,264,256]{2,1,0:T(8,128)S(1)} %get-tuple-element.77.own, f32[4,264,256]{2,1,0:T(8,128)S(1)} %collective-permute-done.14.sibling, f32[2,136,256]{2,1,0:T(8,128)S(1)} %collective-permute-done.15.refs_0_, ...), custom_call_target="tpu_custom_call" | custom-call | tf_op jit(solution)/shard_map/refine_half/pallas_call | solution.py:410
  85.0 1.2 %collective-permute-start.24 = (f32[104,256]{1,0:T(8,128)S(1)}, f32[104,256]{1,0:T(8,128)S(1)}, u32[]{:S(2)}, u32[]{:S(2)}) collective-permute-start(f32[104,256]{1,0:T(8,128)S(1)} %pad_maximum_fusion.5), channel_id=1, source_target_pairs={{0,1},{1,0},{2,3},{3,2},{4,5},{5,4},{6,7},{7,6},{8,9},{9,8},{10,11... | collective-permute-start | bytes 319496 | tf_op jit(solution)/shard_map/ppermute | solution.py:89
  86.3 1.2 %collective-permute-start.20 = (f32[128,256]{1,0:T(8,128)S(1)}, f32[128,256]{1,0:T(8,128)S(1)}, u32[]{:S(2)}, u32[]{:S(2)}) collective-permute-start(f32[128,256]{1,0:T(8,128)S(1)} %get-tuple-element.97), channel_id=1, source_target_pairs={{0,8},{4,12},{8,0},{12,4},{16,24},{20,28},{24,16},{28,20},{1,9},{5... | collective-permute-start | bytes 393224 | tf_op jit(solution)/shard_map/ppermute | solution.py:89
  87.4 1.0 collective-permute-start.21
  88.4 1.4 %collective-permute-done.24 = f32[104,256]{1,0:T(8,128)S(1)} collective-permute-done((f32[104,256]{1,0:T(8,128)S(1)}, f32[104,256]{1,0:T(8,128)S(1)}, u32[]{:S(2)}, u32[]{:S(2)}) %collective-permute-start.24) | collective-permute-done | bytes 106528 | tf_op jit(solution)/shard_map/ppermute | solution.py:89
  89.8 3.6 %collective-permute-start.25 = (f32[104,256]{1,0:T(8,128)S(1)}, f32[104,256]{1,0:T(8,128)S(1)}, u32[]{:S(2)}, u32[]{:S(2)}) collective-permute-start(f32[104,256]{1,0:T(8,128)S(1)} %pad_maximum_fusion.6), channel_id=1, source_target_pairs={{0,2},{1,3},{2,0},{3,1},{4,6},{5,7},{6,4},{7,5},{8,10},{9,11},{10,... | collective-permute-start | bytes 319496 | tf_op jit(solution)/shard_map/ppermute | solution.py:89
  93.5 1.1 %collective-permute-start.27 = (f32[128,256]{1,0:T(8,128)S(1)}, f32[128,256]{1,0:T(8,128)S(1)}, u32[]{:S(2)}, u32[]{:S(2)}) collective-permute-start(f32[128,256]{1,0:T(8,128)S(1)} %get-tuple-element.96), channel_id=1, source_target_pairs={{0,8},{4,12},{8,0},{12,4},{16,24},{20,28},{24,16},{28,20},{1,9},{5... | collective-permute-start | bytes 393224 | tf_op jit(solution)/shard_map/ppermute | solution.py:89
  94.6 1.0 collective-permute-start.28
  95.6 1.1 collective-permute-start.23
  96.6 1.0 collective-permute-start.22
  97.7 1.5 %collective-permute-start.30 = (f32[72,256]{1,0:T(8,128)S(1)}, f32[72,256]{1,0:T(8,128)S(1)}, u32[]{:S(2)}, u32[]{:S(2)}) collective-permute-start(f32[72,256]{1,0:T(8,128)S(1)} %slice_add_fusion.12), channel_id=1, source_target_pairs={{0,24},{4,28},{8,16},{12,20},{16,8},{20,12},{24,0},{28,4},{1,25},{... | collective-permute-start | bytes 221192 | tf_op jit(solution)/shard_map/ppermute | solution.py:89
  99.2 1.1 collective-permute-start.29
  100.3 1.0 collective-permute-start.26
  101.3 0.1 collective-permute-start.32
  101.4 0.2 collective-permute-done.22
  101.6 3.0 %collective-permute-done.26 = f32[72,256]{1,0:T(8,128)S(1)} collective-permute-done((f32[72,256]{1,0:T(8,128)S(1)}, f32[72,256]{1,0:T(8,128)S(1)}, u32[]{:S(2)}, u32[]{:S(2)}) %collective-permute-start.26) | collective-permute-done | bytes 73760 | tf_op jit(solution)/shard_map/ppermute | solution.py:89
  104.7 0.1 collective-permute-start.31
  104.8 0.5 collective-permute-start.33
  105.3 0.6 maximum_multiply_fusion
  106.0 1.1 collective-permute-done.33.refs_5_
  107.1 2.1 %place_blocks.1 = (f32[512,1024]{1,0:T(8,128)}, f32[64,1024]{1,0:T(8,128)}) custom-call(s32[4]{0:T(128)S(1)} %pad_add_fusion.info, f32[4,128,256]{2,1,0:T(8,128)S(1)} %pad_maximum_fusion.refs_0_, f32[4,128,256]{2,1,0:T(8,128)S(1)} %pad_maximum_fusion.1.refs_1_, f32[4,72,256]{2,1,0:T(8,128)S(1)} %pad_maximum_fusion.2.refs_2_, ...), custom_call_target="tpu_custom_call" | custom-call | tf_op jit(solution)/shard_map/place_blocks/pallas_call | solution.py:513
  (59 shorter events, 0.7 us)
Async XLA Ops:
  0.7 12.5 %copy-start.2 = (f32[512,1024]{1,0:T(8,128)S(1)}, f32[512,1024]{1,0:T(8,128)}, u32[]{:S(2)}) copy-start(f32[512,1024]{1,0:T(8,128)} %fine.3) | copy-start | bytes 6291460
  0.7 12.5 %copy-start.3 = (s32[2,4096]{1,0:T(2,128)S(1)}, s32[2,4096]{1,0:T(2,128)}, u32[]{:S(2)}) copy-start(s32[2,4096]{1,0:T(2,128)} %assign.7) | copy-start | bytes 98308
  12.4 8.3 %collective-permute-start = (f32[4,264,256]{2,1,0:T(8,128)S(1)}, f32[4,264,256]{2,1,0:T(8,128)S(1)}, u32[]{:S(2)}, u32[]{:S(2)}) collective-permute-start(f32[4,264,256]{2,1,0:T(8,128)S(1)} %get-tuple-element.56), channel_id=1, source_target_pairs={{0,4},{4,0},{8,12},{12,8},{16,20},{20,16},{24,28},{28,24},{1,5},{5... | collective-permute-start | bytes 3244040 | tf_op jit(solution)/shard_map/ppermute | solution.py:89
  20.8 15.3 %copy-start = (f32[64,1024]{1,0:T(8,128)S(1)}, f32[64,1024]{1,0:T(8,128)}, u32[]{:S(2)}) copy-start(f32[64,1024]{1,0:T(8,128)} %refs_5_.1) | copy-start | bytes 786436
  20.8 15.3 %copy-start.1 = (s32[512]{0:T(512)S(1)}, s32[512]{0:T(512)}, u32[]{:S(2)}) copy-start(s32[512]{0:T(512)} %param.9) | copy-start | bytes 6148
  20.9 6.9 %collective-permute-start.1 = (f32[2,136,256]{2,1,0:T(8,128)S(1)}, f32[2,136,256]{2,1,0:T(8,128)S(1)}, u32[]{:S(2)}, u32[]{:S(2)}) collective-permute-start(f32[2,136,256]{2,1,0:T(8,128)S(1)} %slice_add_fusion.1), channel_id=1, source_target_pairs={{0,8},{4,20},{8,0},{12,28},{16,24},{20,4},{24,16},{28,12},{1,9},{5... | collective-permute-start | bytes 835592 | tf_op jit(solution)/shard_map/ppermute | solution.py:94
  23.2 7.5 %collective-permute-start.2 = (f32[2,128,256]{2,1,0:T(8,128)S(1)}, f32[2,128,256]{2,1,0:T(8,128)S(1)}, u32[]{:S(2)}, u32[]{:S(2)}) collective-permute-start(f32[2,128,256]{2,1,0:T(8,128)S(1)} %slice_add_fusion.3), channel_id=1, source_target_pairs={{0,8},{4,20},{8,0},{12,28},{16,24},{20,4},{24,16},{28,12},{1,9},{5... | collective-permute-start | bytes 786440 | tf_op jit(solution)/shard_map/ppermute | solution.py:94
  27.8 8.3 %collective-permute-start.3 = (f32[136,256]{1,0:T(8,128)S(1)}, f32[136,256]{1,0:T(8,128)S(1)}, u32[]{:S(2)}, u32[]{:S(2)}) collective-permute-start(f32[136,256]{1,0:T(8,128)S(1)} %fusion.1), channel_id=1, source_target_pairs={{0,16},{4,12},{8,24},{12,4},{16,0},{20,28},{24,8},{28,20},{1,17},{... | collective-permute-start | bytes 417800 | tf_op jit(solution)/shard_map/ppermute | solution.py:99
  30.8 5.4 %collective-permute-start.4 = (f32[128,256]{1,0:T(8,128)S(1)}, f32[128,256]{1,0:T(8,128)S(1)}, u32[]{:S(2)}, u32[]{:S(2)}) collective-permute-start(f32[128,256]{1,0:T(8,128)S(1)} %fusion.3), channel_id=1, source_target_pairs={{0,16},{4,12},{8,24},{12,4},{16,0},{20,28},{24,8},{28,20},{1,17},{... | collective-permute-start | bytes 393224 | tf_op jit(solution)/shard_map/ppermute | solution.py:99
  37.3 6.2 %collective-permute-start.5 = (f32[128,256]{1,0:T(8,128)S(1)}, f32[128,256]{1,0:T(8,128)S(1)}, u32[]{:S(2)}, u32[]{:S(2)}) collective-permute-start(f32[128,256]{1,0:T(8,128)S(1)} %get-tuple-element.71), channel_id=1, source_target_pairs={{0,8},{4,12},{8,0},{12,4},{16,24},{20,28},{24,16},{28,20},{1,9},{5... | collective-permute-start | bytes 393224 | tf_op jit(solution)/shard_map/ppermute | solution.py:89
  39.3 6.4 %collective-permute-start.6 = (f32[128,256]{1,0:T(8,128)S(1)}, f32[128,256]{1,0:T(8,128)S(1)}, u32[]{:S(2)}, u32[]{:S(2)}) collective-permute-start(f32[128,256]{1,0:T(8,128)S(1)} %get-tuple-element.70), channel_id=1, source_target_pairs={{0,16},{4,20},{8,24},{12,28},{16,0},{20,4},{24,8},{28,12},{1,17},{... | collective-permute-start | bytes 393224 | tf_op jit(solution)/shard_map/ppermute | solution.py:89
  40.9 10.9 %collective-permute-start.10 = (f32[128,256]{1,0:T(8,128)S(1)}, f32[128,256]{1,0:T(8,128)S(1)}, u32[]{:S(2)}, u32[]{:S(2)}) collective-permute-start(f32[128,256]{1,0:T(8,128)S(1)} %get-tuple-element.71), channel_id=1, source_target_pairs={{0,16},{4,20},{8,24},{12,28},{16,0},{20,4},{24,8},{28,12},{1,17},{... | collective-permute-start | bytes 393224 | tf_op jit(solution)/shard_map/ppermute | solution.py:89
  41.5 10.3 %collective-permute-start.9 = (f32[128,256]{1,0:T(8,128)S(1)}, f32[128,256]{1,0:T(8,128)S(1)}, u32[]{:S(2)}, u32[]{:S(2)}) collective-permute-start(f32[128,256]{1,0:T(8,128)S(1)} %get-tuple-element.70), channel_id=1, source_target_pairs={{0,8},{4,12},{8,0},{12,4},{16,24},{20,28},{24,16},{28,20},{1,9},{5... | collective-permute-start | bytes 393224 | tf_op jit(solution)/shard_map/ppermute | solution.py:89
  43.4 8.3 %collective-permute-start.8 = (f32[128,256]{1,0:T(8,128)S(1)}, f32[128,256]{1,0:T(8,128)S(1)}, u32[]{:S(2)}, u32[]{:S(2)}) collective-permute-start(f32[128,256]{1,0:T(8,128)S(1)} %collective-permute-done.5.refs_0_), channel_id=1, source_target_pairs={{0,16},{4,20},{8,24},{12,28},{16,0},{20,4},{24,8},{28,12},{1,17},{... | collective-permute-start | bytes 393224 | tf_op jit(solution)/shard_map/ppermute | solution.py:89
  45.7 6.0 %collective-permute-start.7 = (f32[128,256]{1,0:T(8,128)S(1)}, f32[128,256]{1,0:T(8,128)S(1)}, u32[]{:S(2)}, u32[]{:S(2)}) collective-permute-start(f32[128,256]{1,0:T(8,128)S(1)} %collective-permute-done.6.refs_1_), channel_id=1, source_target_pairs={{0,8},{4,12},{8,0},{12,4},{16,24},{20,28},{24,16},{28,20},{1,9},{5... | collective-permute-start | bytes 393224 | tf_op jit(solution)/shard_map/ppermute | solution.py:89
  46.6 5.1 %collective-permute-start.11 = (f32[104,256]{1,0:T(8,128)S(1)}, f32[104,256]{1,0:T(8,128)S(1)}, u32[]{:S(2)}, u32[]{:S(2)}) collective-permute-start(f32[104,256]{1,0:T(8,128)S(1)} %pad_maximum_fusion.3), channel_id=1, source_target_pairs={{0,1},{1,0},{2,3},{3,2},{4,5},{5,4},{6,7},{7,6},{8,9},{9,8},{10,11... | collective-permute-start | bytes 319496 | tf_op jit(solution)/shard_map/ppermute | solution.py:89
  51.9 8.3 %collective-permute-start.12 = (f32[8,128,256]{2,1,0:T(8,128)S(1)}, f32[8,128,256]{2,1,0:T(8,128)S(1)}, u32[]{:S(2)}, u32[]{:S(2)}) collective-permute-start(f32[8,128,256]{2,1,0:T(8,128)S(1)} %bitcast_dynamic-update-slice_fusion.fine), channel_id=1, source_target_pairs={{0,4},{4,0},{8,12},{12,8},{16,20},{20,16},{24,28},{28,24},{1,5},{5... | collective-permute-start | bytes 3145736 | tf_op jit(solution)/shard_map/ppermute | solution.py:89
  59.5 8.4 %collective-permute-start.14 = (f32[4,264,256]{2,1,0:T(8,128)S(1)}, f32[4,264,256]{2,1,0:T(8,128)S(1)}, u32[]{:S(2)}, u32[]{:S(2)}) collective-permute-start(f32[4,264,256]{2,1,0:T(8,128)S(1)} %get-tuple-element.78), channel_id=1, source_target_pairs={{0,4},{4,0},{8,12},{12,8},{16,20},{20,16},{24,28},{28,24},{1,5},{5... | collective-permute-start | bytes 3244040 | tf_op jit(solution)/shard_map/ppermute | solution.py:89
  60.1 7.8 %collective-permute-start.13 = (f32[72,256]{1,0:T(8,128)S(1)}, f32[72,256]{1,0:T(8,128)S(1)}, u32[]{:S(2)}, u32[]{:S(2)}) collective-permute-start(f32[72,256]{1,0:T(8,128)S(1)} %slice_add_fusion.14), channel_id=1, source_target_pairs={{0,4},{4,0},{8,12},{12,8},{16,20},{20,16},{24,28},{28,24},{1,5},{5... | collective-permute-start | bytes 221192 | tf_op jit(solution)/shard_map/ppermute | solution.py:89
  68.1 6.6 %collective-permute-start.15 = (f32[2,136,256]{2,1,0:T(8,128)S(1)}, f32[2,136,256]{2,1,0:T(8,128)S(1)}, u32[]{:S(2)}, u32[]{:S(2)}) collective-permute-start(f32[2,136,256]{2,1,0:T(8,128)S(1)} %slice_add_fusion), channel_id=1, source_target_pairs={{0,8},{4,20},{8,0},{12,28},{16,24},{20,4},{24,16},{28,12},{1,9},{5... | collective-permute-start | bytes 835592 | tf_op jit(solution)/shard_map/ppermute | solution.py:94
  69.3 8.6 %collective-permute-start.16 = (f32[2,128,256]{2,1,0:T(8,128)S(1)}, f32[2,128,256]{2,1,0:T(8,128)S(1)}, u32[]{:S(2)}, u32[]{:S(2)}) collective-permute-start(f32[2,128,256]{2,1,0:T(8,128)S(1)} %slice_add_fusion.2), channel_id=1, source_target_pairs={{0,8},{4,20},{8,0},{12,28},{16,24},{20,4},{24,16},{28,12},{1,9},{5... | collective-permute-start | bytes 786440 | tf_op jit(solution)/shard_map/ppermute | solution.py:94
  70.2 8.5 %collective-permute-start.18 = (f32[104,256]{1,0:T(8,128)S(1)}, f32[104,256]{1,0:T(8,128)S(1)}, u32[]{:S(2)}, u32[]{:S(2)}) collective-permute-start(f32[104,256]{1,0:T(8,128)S(1)} %pad_maximum_fusion.4.refs_5_), channel_id=1, source_target_pairs={{0,2},{1,3},{2,0},{3,1},{4,6},{5,7},{6,4},{7,5},{8,10},{9,11},{10,... | collective-permute-start | bytes 319496 | tf_op jit(solution)/shard_map/ppermute | solution.py:89
  74.7 9.1 %collective-permute-start.17 = (f32[136,256]{1,0:T(8,128)S(1)}, f32[136,256]{1,0:T(8,128)S(1)}, u32[]{:S(2)}, u32[]{:S(2)}) collective-permute-start(f32[136,256]{1,0:T(8,128)S(1)} %fusion), channel_id=1, source_target_pairs={{0,16},{4,12},{8,24},{12,4},{16,0},{20,28},{24,8},{28,20},{1,17},{... | collective-permute-start | bytes 417800 | tf_op jit(solution)/shard_map/ppermute | solution.py:99
  78.6 5.2 %collective-permute-start.19 = (f32[128,256]{1,0:T(8,128)}, f32[128,256]{1,0:T(8,128)S(1)}, u32[]{:S(2)}, u32[]{:S(2)}) collective-permute-start(f32[128,256]{1,0:T(8,128)} %fusion.2), channel_id=1, source_target_pairs={{0,16},{4,12},{8,24},{12,4},{16,0},{20,28},{24,8},{28,20},{1,17},{... | collective-permute-start | bytes 393224 | tf_op jit(solution)/shard_map/ppermute | solution.py:99
  85.0 4.8 %collective-permute-start.24 = (f32[104,256]{1,0:T(8,128)S(1)}, f32[104,256]{1,0:T(8,128)S(1)}, u32[]{:S(2)}, u32[]{:S(2)}) collective-permute-start(f32[104,256]{1,0:T(8,128)S(1)} %pad_maximum_fusion.5), channel_id=1, source_target_pairs={{0,1},{1,0},{2,3},{3,2},{4,5},{5,4},{6,7},{7,6},{8,9},{9,8},{10,11... | collective-permute-start | bytes 319496 | tf_op jit(solution)/shard_map/ppermute | solution.py:89
  86.3 7.2 %collective-permute-start.20 = (f32[128,256]{1,0:T(8,128)S(1)}, f32[128,256]{1,0:T(8,128)S(1)}, u32[]{:S(2)}, u32[]{:S(2)}) collective-permute-start(f32[128,256]{1,0:T(8,128)S(1)} %get-tuple-element.97), channel_id=1, source_target_pairs={{0,8},{4,12},{8,0},{12,4},{16,24},{20,28},{24,16},{28,20},{1,9},{5... | collective-permute-start | bytes 393224 | tf_op jit(solution)/shard_map/ppermute | solution.py:89
  87.4 6.0 %collective-permute-start.21 = (f32[128,256]{1,0:T(8,128)S(1)}, f32[128,256]{1,0:T(8,128)S(1)}, u32[]{:S(2)}, u32[]{:S(2)}) collective-permute-start(f32[128,256]{1,0:T(8,128)S(1)} %get-tuple-element.96), channel_id=1, source_target_pairs={{0,16},{4,20},{8,24},{12,28},{16,0},{20,4},{24,8},{28,12},{1,17},{... | collective-permute-start | bytes 393224 | tf_op jit(solution)/shard_map/ppermute | solution.py:89
  89.8 7.8 %collective-permute-start.25 = (f32[104,256]{1,0:T(8,128)S(1)}, f32[104,256]{1,0:T(8,128)S(1)}, u32[]{:S(2)}, u32[]{:S(2)}) collective-permute-start(f32[104,256]{1,0:T(8,128)S(1)} %pad_maximum_fusion.6), channel_id=1, source_target_pairs={{0,2},{1,3},{2,0},{3,1},{4,6},{5,7},{6,4},{7,5},{8,10},{9,11},{10,... | collective-permute-start | bytes 319496 | tf_op jit(solution)/shard_map/ppermute | solution.py:89
  93.5 5.7 %collective-permute-start.27 = (f32[128,256]{1,0:T(8,128)S(1)}, f32[128,256]{1,0:T(8,128)S(1)}, u32[]{:S(2)}, u32[]{:S(2)}) collective-permute-start(f32[128,256]{1,0:T(8,128)S(1)} %get-tuple-element.96), channel_id=1, source_target_pairs={{0,8},{4,12},{8,0},{12,4},{16,24},{20,28},{24,16},{28,20},{1,9},{5... | collective-permute-start | bytes 393224 | tf_op jit(solution)/shard_map/ppermute | solution.py:89
  94.6 5.7 %collective-permute-start.28 = (f32[128,256]{1,0:T(8,128)S(1)}, f32[128,256]{1,0:T(8,128)S(1)}, u32[]{:S(2)}, u32[]{:S(2)}) collective-permute-start(f32[128,256]{1,0:T(8,128)S(1)} %get-tuple-element.97), channel_id=1, source_target_pairs={{0,16},{4,20},{8,24},{12,28},{16,0},{20,4},{24,8},{28,12},{1,17},{... | collective-permute-start | bytes 393224 | tf_op jit(solution)/shard_map/ppermute | solution.py:89
  95.6 5.7 %collective-permute-start.23 = (f32[128,256]{1,0:T(8,128)S(1)}, f32[128,256]{1,0:T(8,128)S(1)}, u32[]{:S(2)}, u32[]{:S(2)}) collective-permute-start(f32[128,256]{1,0:T(8,128)S(1)} %collective-permute-done.20), channel_id=1, source_target_pairs={{0,16},{4,20},{8,24},{12,28},{16,0},{20,4},{24,8},{28,12},{1,17},{... | collective-permute-start | bytes 393224 | tf_op jit(solution)/shard_map/ppermute | solution.py:89
  96.6 5.0 %collective-permute-start.22 = (f32[128,256]{1,0:T(8,128)S(1)}, f32[128,256]{1,0:T(8,128)S(1)}, u32[]{:S(2)}, u32[]{:S(2)}) collective-permute-start(f32[128,256]{1,0:T(8,128)S(1)} %collective-permute-done.21), channel_id=1, source_target_pairs={{0,8},{4,12},{8,0},{12,4},{16,24},{20,28},{24,16},{28,20},{1,9},{5... | collective-permute-start | bytes 393224 | tf_op jit(solution)/shard_map/ppermute | solution.py:89
  97.7 7.1 %collective-permute-start.30 = (f32[72,256]{1,0:T(8,128)S(1)}, f32[72,256]{1,0:T(8,128)S(1)}, u32[]{:S(2)}, u32[]{:S(2)}) collective-permute-start(f32[72,256]{1,0:T(8,128)S(1)} %slice_add_fusion.12), channel_id=1, source_target_pairs={{0,24},{4,28},{8,16},{12,20},{16,8},{20,12},{24,0},{28,4},{1,25},{... | collective-permute-start | bytes 221192 | tf_op jit(solution)/shard_map/ppermute | solution.py:89
  99.2 5.5 %collective-permute-start.29 = (f32[72,256]{1,0:T(8,128)S(1)}, f32[72,256]{1,0:T(8,128)S(1)}, u32[]{:S(2)}, u32[]{:S(2)}) collective-permute-start(f32[72,256]{1,0:T(8,128)S(1)} %slice_add_fusion.12), channel_id=1, source_target_pairs={{0,16},{4,20},{8,24},{12,28},{16,0},{20,4},{24,8},{28,12},{1,17},{... | collective-permute-start | bytes 221192 | tf_op jit(solution)/shard_map/ppermute | solution.py:89
  100.3 4.4 %collective-permute-start.26 = (f32[72,256]{1,0:T(8,128)S(1)}, f32[72,256]{1,0:T(8,128)S(1)}, u32[]{:S(2)}, u32[]{:S(2)}) collective-permute-start(f32[72,256]{1,0:T(8,128)S(1)} %slice_add_fusion.12), channel_id=1, source_target_pairs={{0,8},{4,12},{8,0},{12,4},{16,24},{20,28},{24,16},{28,20},{1,9},{5... | collective-permute-start | bytes 221192 | tf_op jit(solution)/shard_map/ppermute | solution.py:89
  101.3 5.8 %collective-permute-start.32 = (f32[4,128,256]{2,1,0:T(8,128)S(1)}, f32[4,128,256]{2,1,0:T(8,128)S(1)}, u32[]{:S(2)}, u32[]{:S(2)}) collective-permute-start(f32[4,128,256]{2,1,0:T(8,128)S(1)} %pad_maximum_fusion.1.refs_1_), channel_id=1, source_target_pairs={{0,4},{4,0},{8,12},{12,8},{16,20},{20,16},{24,28},{28,24},{1,5},{5... | collective-permute-start | bytes 1572872 | tf_op jit(solution)/shard_map/ppermute | solution.py:89
  104.7 2.4 %collective-permute-start.31 = (f32[4,128,256]{2,1,0:T(8,128)S(1)}, f32[4,128,256]{2,1,0:T(8,128)S(1)}, u32[]{:S(2)}, u32[]{:S(2)}) collective-permute-start(f32[4,128,256]{2,1,0:T(8,128)S(1)} %pad_maximum_fusion.refs_0_), channel_id=1, source_target_pairs={{0,4},{4,0},{8,12},{12,8},{16,20},{20,16},{24,28},{28,24},{1,5},{5... | collective-permute-start | bytes 1572872 | tf_op jit(solution)/shard_map/ppermute | solution.py:89
  104.8 2.3 %collective-permute-start.33 = (f32[4,72,256]{2,1,0:T(8,128)S(1)}, f32[4,72,256]{2,1,0:T(8,128)S(1)}, u32[]{:S(2)}, u32[]{:S(2)}) collective-permute-start(f32[4,72,256]{2,1,0:T(8,128)S(1)} %pad_maximum_fusion.2.refs_2_), channel_id=1, source_target_pairs={{0,4},{4,0},{8,12},{12,8},{16,20},{20,16},{24,28},{28,24},{1,5},{5... | collective-permute-start | bytes 884744 | tf_op jit(solution)/shard_map/ppermute | solution.py:89
